TPU v7x, 32 devices: a whole 2x2x4 slice. The times are simulated.
32 devices in a mesh: groups: 1, layer: 32 (over z, y, x, core).
Axes of the slice: x: 2, y: 2, z: 4, core: 2. Of those that a mesh axis runs over, the one named last changes fastest.
Arguments:
- resid: bfloat16 [32, 8, 8192], P('layer', 'groups'), may hold values from -6 to 6
- enc_weight: bfloat16 [32, 8192, 256], P('layer'), may hold values from -0.0625 to 0.0625
- enc_bias: bfloat16 [32, 256], P('layer'), may hold values from -0.5 to 0.5
- active: int32 [32, 2, 2], P('layer', 'groups'), may hold values from 0 to 1, as said below
- dec_weight: bfloat16 [32, 2, 256, 8192], P('layer'), may hold values from -0.125 to 0.125
- target: bfloat16 [32, 8, 8192], P('layer', 'groups'), may hold values from -5 to 5
Outputs:
- error: bfloat16 [32, 8, 8192], P('layer', 'groups')
- grad_codes: float32 [32, 64, 256], P('layer', 'groups')
Inputs may be any that keep to these rules, and one draw needn't show every extreme that they name: `active`: in every slab exactly 3 of the 2 x 2 (token tile, feature block) pairs are 1.
All inputs are finite; a program needn't handle non-finite values.
Results may differ from a plain program's by a relative error of at most 0.0041.
Values may be sent and summed in bfloat16 or wider, within the bound.
No kernel may reach another device: no remote copies, remote signals or barrier semaphores. Data moves between devices by JAX's collectives and lax.ppermute only.
A program may use at most 128 MiB of HBM per device.

v0:
```python
import jax
import jax.numpy as jnp
from jax import lax
from jax.sharding import PartitionSpec as P

BLOCK = 128
LAYERS = 4
TILE = 32


def from_partner(value, axis, apart):
    mask = 2**apart
    pairs = [(source, source ^ mask) for source in range(lax.axis_size(axis))]
    return lax.ppermute(value, axis, pairs)


def shifted(block, axis, distance):
    devices = range(lax.axis_size(axis))
    route = [(i - distance, i) for i in devices if i - distance in devices]
    return lax.ppermute(block, axis, route)


def transposed(left, weight):
    return lax.dot_general(
        left, weight, (((1,), (1,)), ((), ())), preferred_element_type=jnp.float32
    )


def joined(upper, mine, other):
    return jnp.where(
        upper, jnp.concatenate([other, mine], axis=0), jnp.concatenate([mine, other], axis=0)
    )


def halves(whole, upper):
    half = whole.shape[0] // 2
    lower_rows = whole[:half]
    upper_rows = whole[half:]
    return (jnp.where(upper, upper_rows, lower_rows), jnp.where(upper, lower_rows, upper_rows))


def on_device(resid, enc_weight, enc_bias, active, dec_weight, target):
    group = lax.axis_size("layer") // LAYERS
    levels = group.bit_length() - 1
    place = lax.axis_index("layer") % group
    rows = resid[0]
    for level in range(levels):
        got = from_partner(rows, "layer", level)
        rows = joined(place >> level & 1 == 1, rows, got)
    pre = (
        jnp.dot(rows, enc_weight[0], preferred_element_type=jnp.float32)
        + enc_bias[0].astype(jnp.float32)[None, :]
    )
    gate = jnp.repeat(jnp.repeat(active[0], TILE, axis=0), BLOCK, axis=1).astype(jnp.float32)
    codes = (jax.nn.relu(pre) * gate).astype(jnp.bfloat16)
    own_dec = dec_weight[0, 0]
    next_dec = dec_weight[0, 1]
    wanted = target[0].astype(jnp.float32)
    own_part = jnp.dot(codes, own_dec, preferred_element_type=jnp.float32)
    next_part = jnp.dot(codes, next_dec, preferred_element_type=jnp.float32)
    for level in reversed(range(levels)):
        upper = place >> level & 1 == 1
        keep_own, send_own = halves(own_part, upper)
        keep_next, send_next = halves(next_part, upper)
        got_own, got_next = from_partner((send_own, send_next), "layer", level)
        own_part = keep_own + got_own
        next_part = keep_next + got_next
    recon = own_part + shifted(next_part, "layer", group)
    error = (recon - wanted).astype(jnp.bfloat16)
    later = shifted(error, "layer", -group)
    here_rows, after_rows = (error, later)
    for level in range(levels):
        got_here, got_after = from_partner((here_rows, after_rows), "layer", level)
        upper = place >> level & 1 == 1
        here_rows = joined(upper, here_rows, got_here)
        after_rows = joined(upper, after_rows, got_after)
    grad = transposed(here_rows, own_dec) + transposed(after_rows, next_dec)
    return (error[None], grad[None])


def solution(mesh):
    return jax.shard_map(
        on_device,
        mesh=mesh,
        in_specs=(
            P("layer", "groups", None),
            P("layer", None, None),
            P("layer", None),
            P("layer", "groups", None),
            P("layer", None, None, None),
            P("layer", "groups", None),
        ),
        out_specs=(P("layer", "groups", None), P("layer", "groups", None)),
        check_vma=False,
    )
```

profile of v0, /device:TPU:0, one launch (start us, length us, event | category | flops | bytes accessed | tf_op | source)
XLA Modules:
  0.0 146.1 jit_solution(9828516602899074804)
XLA Ops:
  0.6 0.5 collective-permute-start
  1.1 1.2 collective-permute-done
  2.3 1.0 maximum_select_fusion.9
  3.4 2.9 %collective-permute-start.1 = (bf16[16,8192]{1,0:T(8,128)(2,1)S(1)}, bf16[16,8192]{1,0:T(8,128)(2,1)S(1)}, u32[]{:S(2)}, u32[]{:S(2)}) collective-permute-start(bf16[16,8192]{1,0:T(8,128)(2,1)S(1)} %maximum_select_fusion.9), channel_id=1, source_target_pairs={{0,2},{1,3},{2,0},{3,1},{4,6},{5,7},{6,4},{7,5},{8,10},{9,11},{10,... | collective-permute-start | bytes 786440 | tf_op jit(solution)/shard_map/ppermute | solution.py:14
  6.3 6.6 %collective-permute-done.1 = bf16[16,8192]{1,0:T(8,128)(2,1)S(1)} collective-permute-done((bf16[16,8192]{1,0:T(8,128)(2,1)S(1)}, bf16[16,8192]{1,0:T(8,128)(2,1)S(1)}, u32[]{:S(2)}, u32[]{:S(2)}) %collective-permute-start.1) | collective-permute-done | bytes 262176 | tf_op jit(solution)/shard_map/ppermute | solution.py:14
  12.9 0.1 maximum_select_fusion.6
  13.0 1.8 %collective-permute-start.2 = (bf16[32,8192]{1,0:T(8,128)(2,1)S(1)}, bf16[32,8192]{1,0:T(8,128)(2,1)S(1)}, u32[]{:S(2)}, u32[]{:S(2)}) collective-permute-start(bf16[32,8192]{1,0:T(8,128)(2,1)S(1)} %maximum_select_fusion.6), channel_id=1, source_target_pairs={{0,4},{1,5},{2,6},{3,7},{4,0},{5,1},{6,2},{7,3},{8,12},{9,13},{10,... | collective-permute-start | bytes 1572872 | tf_op jit(solution)/shard_map/ppermute | solution.py:14
  14.8 0.7 add.54
  15.5 0.7 convert_bitcast_fusion
  16.2 10.3 %collective-permute-done.2 = bf16[32,8192]{1,0:T(8,128)(2,1)S(1)} collective-permute-done((bf16[32,8192]{1,0:T(8,128)(2,1)S(1)}, bf16[32,8192]{1,0:T(8,128)(2,1)S(1)}, u32[]{:S(2)}, u32[]{:S(2)}) %collective-permute-start.2) | collective-permute-done | bytes 524320 | tf_op jit(solution)/shard_map/ppermute | solution.py:14
  26.5 0.1 broadcast_in_dim.14
  26.7 0.0 copy-start
  26.7 3.2 %fusion.29 = bf16[64,256]{1,0:T(8,128)(2,1)S(1)} fusion(bf16[1,8192,256]{2,1,0:T(8,128)(2,1)} %param.7, bf16[32,8192]{1,0:T(8,128)(2,1)S(1)} %maximum_select_fusion.6, bf16[32,8192]{1,0:T(8,128)(2,1)S(1)} %collective-permute-done.2, pred[]{:T(512)S(6)} %eq.10, f32[8,8,2,128]{3,2,1,0:T(2,128)S(1)} %bitcast.45, f32[256]{0:T(256)S(1)} %bitcast.46), kind=kOutput, calls=%fused_computation.19 | convolution fusion | flops 273219584 | bytes 5342209 | tf_op jit(solution)/shard_map/dot_general | solution.py:51
  29.9 3.5 %fusion.2 = f32[64,8192]{1,0:T(8,128)S(1)} fusion(bf16[64,256]{1,0:T(8,128)(2,1)S(1)} %fusion.29, bf16[1,2,256,8192]{3,2,1,0:T(8,128)(2,1)} %param.10), kind=kOutput, calls=%fused_computation.2 | convolution fusion | flops 268435456 | bytes 6324224 | tf_op jit(solution)/shard_map/dot_general | solution.py:60
  33.4 0.0 copy-done
  33.4 0.9 fusion.6
  34.2 0.1 slice_select_fusion
  34.3 1.5 %collective-permute-start.6 = (f32[32,8192]{1,0:T(8,128)S(1)}, f32[32,8192]{1,0:T(8,128)S(1)}, u32[]{:S(2)}, u32[]{:S(2)}) collective-permute-start(f32[32,8192]{1,0:T(8,128)S(1)} %slice_select_fusion), channel_id=1, source_target_pairs={{0,4},{1,5},{2,6},{3,7},{4,0},{5,1},{6,2},{7,3},{8,12},{9,13},{10,... | collective-permute-start | bytes 3145736 | tf_op jit(solution)/shard_map/ppermute | solution.py:14
  35.9 0.1 slice_select_fusion.1
  36.0 0.6 collective-permute-start.3
  36.6 23.9 %collective-permute-done.6 = f32[32,8192]{1,0:T(8,128)S(1)} collective-permute-done((f32[32,8192]{1,0:T(8,128)S(1)}, f32[32,8192]{1,0:T(8,128)S(1)}, u32[]{:S(2)}, u32[]{:S(2)}) %collective-permute-start.6) | collective-permute-done | bytes 1048608 | tf_op jit(solution)/shard_map/ppermute | solution.py:14
  60.5 0.2 select_add_fusion
  60.7 0.1 slice_select_fusion.2
  60.8 1.5 %collective-permute-start.7 = (f32[16,8192]{1,0:T(8,128)S(1)}, f32[16,8192]{1,0:T(8,128)S(1)}, u32[]{:S(2)}, u32[]{:S(2)}) collective-permute-start(f32[16,8192]{1,0:T(8,128)S(1)} %slice_select_fusion.2), channel_id=1, source_target_pairs={{0,2},{1,3},{2,0},{3,1},{4,6},{5,7},{6,4},{7,5},{8,10},{9,11},{10,... | collective-permute-start | bytes 1572872 | tf_op jit(solution)/shard_map/ppermute | solution.py:14
  62.3 18.4 %collective-permute-done.3 = f32[32,8192]{1,0:T(8,128)S(1)} collective-permute-done((f32[32,8192]{1,0:T(8,128)S(1)}, f32[32,8192]{1,0:T(8,128)S(1)}, u32[]{:S(2)}, u32[]{:S(2)}) %collective-permute-start.3) | collective-permute-done | bytes 1048608 | tf_op jit(solution)/shard_map/ppermute | solution.py:14
  80.7 0.1 select_add_fusion.1
  80.8 0.1 slice_select_fusion.3
  80.9 1.1 collective-permute-start.4
  82.0 0.0 collective-permute-done.7
  82.0 0.1 select_add_fusion.2
  82.2 0.0 copy-start.2
  82.2 0.1 collective-permute-start.8
  82.3 10.3 %collective-permute-done.4 = f32[16,8192]{1,0:T(8,128)S(1)} collective-permute-done((f32[16,8192]{1,0:T(8,128)S(1)}, f32[16,8192]{1,0:T(8,128)S(1)}, u32[]{:S(2)}, u32[]{:S(2)}) %collective-permute-start.4) | collective-permute-done | bytes 524320 | tf_op jit(solution)/shard_map/ppermute | solution.py:14
  92.6 0.1 select_add_fusion.3
  92.8 0.1 collective-permute-start.5
  92.9 0.0 collective-permute-done.8
  92.9 2.7 %collective-permute-start.9 = (f32[8,8192]{1,0:T(8,128)S(1)}, f32[8,8192]{1,0:T(8,128)S(1)}, u32[]{:S(2)}, u32[]{:S(2)}) collective-permute-start(f32[8,8192]{1,0:T(8,128)S(1)} %select_add_fusion.4), channel_id=1, source_target_pairs={{0,8},{1,9},{2,10},{3,11},{4,12},{5,13},{6,14},{7,15},{8,16},{9,17... | collective-permute-start | bytes 786440 | tf_op jit(solution)/shard_map/ppermute | solution.py:20
  95.7 0.0 collective-permute-done.5
  95.7 6.2 %collective-permute-done.9 = f32[8,8192]{1,0:T(8,128)S(1)} collective-permute-done((f32[8,8192]{1,0:T(8,128)S(1)}, f32[8,8192]{1,0:T(8,128)S(1)}, u32[]{:S(2)}, u32[]{:S(2)}) %collective-permute-start.9) | collective-permute-done | bytes 262176 | tf_op jit(solution)/shard_map/ppermute | solution.py:20
  101.8 0.0 copy-done.2
  101.8 0.1 fusion.50
  101.9 0.0 copy-start.1
  101.9 1.3 collective-permute-start.13
  103.2 6.4 %collective-permute-done.13 = bf16[8,8192]{1,0:T(8,128)(2,1)S(1)} collective-permute-done((bf16[8,8192]{1,0:T(8,128)(2,1)S(1)}, bf16[8,8192]{1,0:T(8,128)(2,1)S(1)}, u32[]{:S(2)}, u32[]{:S(2)}) %collective-permute-start.13) | collective-permute-done | bytes 131104 | tf_op jit(solution)/shard_map/ppermute | solution.py:20
  109.7 0.0 collective-permute-start.14
  109.7 0.5 collective-permute-start.10
  110.2 0.8 collective-permute-done.14
  111.1 1.6 %collective-permute-start.15 = (bf16[16,8192]{1,0:T(8,128)(2,1)S(1)}, bf16[16,8192]{1,0:T(8,128)(2,1)S(1)}, u32[]{:S(2)}, u32[]{:S(2)}) collective-permute-start(bf16[16,8192]{1,0:T(8,128)(2,1)S(1)} %maximum_select_fusion.11), channel_id=1, source_target_pairs={{0,2},{1,3},{2,0},{3,1},{4,6},{5,7},{6,4},{7,5},{8,10},{9,11},{10,... | collective-permute-start | bytes 786440 | tf_op jit(solution)/shard_map/ppermute | solution.py:14
  112.6 0.0 collective-permute-done.10
  112.7 0.6 collective-permute-start.11
  113.3 7.0 %collective-permute-done.15 = bf16[16,8192]{1,0:T(8,128)(2,1)S(1)} collective-permute-done((bf16[16,8192]{1,0:T(8,128)(2,1)S(1)}, bf16[16,8192]{1,0:T(8,128)(2,1)S(1)}, u32[]{:S(2)}, u32[]{:S(2)}) %collective-permute-start.15) | collective-permute-done | bytes 262176 | tf_op jit(solution)/shard_map/ppermute | solution.py:14
  120.3 0.1 maximum_select_fusion.8
  120.4 1.6 %collective-permute-start.16 = (bf16[32,8192]{1,0:T(8,128)(2,1)S(1)}, bf16[32,8192]{1,0:T(8,128)(2,1)S(1)}, u32[]{:S(2)}, u32[]{:S(2)}) collective-permute-start(bf16[32,8192]{1,0:T(8,128)(2,1)S(1)} %maximum_select_fusion.8), channel_id=1, source_target_pairs={{0,4},{1,5},{2,6},{3,7},{4,0},{5,1},{6,2},{7,3},{8,12},{9,13},{10,... | collective-permute-start | bytes 1572872 | tf_op jit(solution)/shard_map/ppermute | solution.py:14
  122.0 3.2 %collective-permute-done.11 = bf16[16,8192]{1,0:T(8,128)(2,1)S(1)} collective-permute-done((bf16[16,8192]{1,0:T(8,128)(2,1)S(1)}, bf16[16,8192]{1,0:T(8,128)(2,1)S(1)}, u32[]{:S(2)}, u32[]{:S(2)}) %collective-permute-start.11) | collective-permute-done | bytes 262176 | tf_op jit(solution)/shard_map/ppermute | solution.py:14
  125.1 0.1 maximum_select_fusion.7
  125.2 1.6 %collective-permute-start.12 = (bf16[32,8192]{1,0:T(8,128)(2,1)S(1)}, bf16[32,8192]{1,0:T(8,128)(2,1)S(1)}, u32[]{:S(2)}, u32[]{:S(2)}) collective-permute-start(bf16[32,8192]{1,0:T(8,128)(2,1)S(1)} %maximum_select_fusion.7), channel_id=1, source_target_pairs={{0,4},{1,5},{2,6},{3,7},{4,0},{5,1},{6,2},{7,3},{8,12},{9,13},{10,... | collective-permute-start | bytes 1572872 | tf_op jit(solution)/shard_map/ppermute | solution.py:14
  126.8 8.5 %collective-permute-done.16 = bf16[32,8192]{1,0:T(8,128)(2,1)S(1)} collective-permute-done((bf16[32,8192]{1,0:T(8,128)(2,1)S(1)}, bf16[32,8192]{1,0:T(8,128)(2,1)S(1)}, u32[]{:S(2)}, u32[]{:S(2)}) %collective-permute-start.16) | collective-permute-done | bytes 524320 | tf_op jit(solution)/shard_map/ppermute | solution.py:14
  135.3 1.4 fusion
  136.7 0.0 copy-done.1
  136.7 7.3 %collective-permute-done.12 = bf16[32,8192]{1,0:T(8,128)(2,1)S(1)} collective-permute-done((bf16[32,8192]{1,0:T(8,128)(2,1)S(1)}, bf16[32,8192]{1,0:T(8,128)(2,1)S(1)}, u32[]{:S(2)}, u32[]{:S(2)}) %collective-permute-start.12) | collective-permute-done | bytes 524320 | tf_op jit(solution)/shard_map/ppermute | solution.py:14
  144.0 2.0 %fusion.26 = f32[1,64,256]{2,1,0:T(8,128)} fusion(f32[64,256]{1,0:T(8,128)S(1)} %fusion, bf16[1,2,256,8192]{3,2,1,0:T(8,128)(2,1)S(1)} %copy-done, bf16[32,8192]{1,0:T(8,128)(2,1)S(1)} %maximum_select_fusion.7, bf16[32,8192]{1,0:T(8,128)(2,1)S(1)} %collective-permute-done.12, pred[]{:T(512)S(6)} %eq.10), kind=kOutput, calls=%fused_computation.18 | convolution fusion | flops 273170432 | bytes 5373953 | tf_op jit(solution)/shard_map/dot_general | solution.py:24
  (6 shorter events, 0.2 us)
Async XLA Ops:
  0.6 1.7 %collective-permute-start = (bf16[8,8192]{1,0:T(8,128)(2,1)}, bf16[8,8192]{1,0:T(8,128)(2,1)S(1)}, u32[]{:S(2)}, u32[]{:S(2)}) collective-permute-start(bf16[8,8192]{1,0:T(8,128)(2,1)} %bitcast.42), channel_id=1, source_target_pairs={{0,1},{1,0},{2,3},{3,2},{4,5},{5,4},{6,7},{7,6},{8,9},{9,8},{10,11... | collective-permute-start | bytes 393224 | tf_op jit(solution)/shard_map/ppermute | solution.py:14
  3.4 9.5 %collective-permute-start.1 = (bf16[16,8192]{1,0:T(8,128)(2,1)S(1)}, bf16[16,8192]{1,0:T(8,128)(2,1)S(1)}, u32[]{:S(2)}, u32[]{:S(2)}) collective-permute-start(bf16[16,8192]{1,0:T(8,128)(2,1)S(1)} %maximum_select_fusion.9), channel_id=1, source_target_pairs={{0,2},{1,3},{2,0},{3,1},{4,6},{5,7},{6,4},{7,5},{8,10},{9,11},{10,... | collective-permute-start | bytes 786440 | tf_op jit(solution)/shard_map/ppermute | solution.py:14
  13.0 13.5 %collective-permute-start.2 = (bf16[32,8192]{1,0:T(8,128)(2,1)S(1)}, bf16[32,8192]{1,0:T(8,128)(2,1)S(1)}, u32[]{:S(2)}, u32[]{:S(2)}) collective-permute-start(bf16[32,8192]{1,0:T(8,128)(2,1)S(1)} %maximum_select_fusion.6), channel_id=1, source_target_pairs={{0,4},{1,5},{2,6},{3,7},{4,0},{5,1},{6,2},{7,3},{8,12},{9,13},{10,... | collective-permute-start | bytes 1572872 | tf_op jit(solution)/shard_map/ppermute | solution.py:14
  26.7 6.7 %copy-start = (bf16[1,2,256,8192]{3,2,1,0:T(8,128)(2,1)S(1)}, bf16[1,2,256,8192]{3,2,1,0:T(8,128)(2,1)}, u32[]{:S(2)}) copy-start(bf16[1,2,256,8192]{3,2,1,0:T(8,128)(2,1)} %param.10) | copy-start | bytes 25165828
  34.3 26.2 %collective-permute-start.6 = (f32[32,8192]{1,0:T(8,128)S(1)}, f32[32,8192]{1,0:T(8,128)S(1)}, u32[]{:S(2)}, u32[]{:S(2)}) collective-permute-start(f32[32,8192]{1,0:T(8,128)S(1)} %slice_select_fusion), channel_id=1, source_target_pairs={{0,4},{1,5},{2,6},{3,7},{4,0},{5,1},{6,2},{7,3},{8,12},{9,13},{10,... | collective-permute-start | bytes 3145736 | tf_op jit(solution)/shard_map/ppermute | solution.py:14
  36.0 44.7 %collective-permute-start.3 = (f32[32,8192]{1,0:T(8,128)S(1)}, f32[32,8192]{1,0:T(8,128)S(1)}, u32[]{:S(2)}, u32[]{:S(2)}) collective-permute-start(f32[32,8192]{1,0:T(8,128)S(1)} %slice_select_fusion.1), channel_id=1, source_target_pairs={{0,4},{1,5},{2,6},{3,7},{4,0},{5,1},{6,2},{7,3},{8,12},{9,13},{10,... | collective-permute-start | bytes 3145736 | tf_op jit(solution)/shard_map/ppermute | solution.py:14
  60.8 21.3 %collective-permute-start.7 = (f32[16,8192]{1,0:T(8,128)S(1)}, f32[16,8192]{1,0:T(8,128)S(1)}, u32[]{:S(2)}, u32[]{:S(2)}) collective-permute-start(f32[16,8192]{1,0:T(8,128)S(1)} %slice_select_fusion.2), channel_id=1, source_target_pairs={{0,2},{1,3},{2,0},{3,1},{4,6},{5,7},{6,4},{7,5},{8,10},{9,11},{10,... | collective-permute-start | bytes 1572872 | tf_op jit(solution)/shard_map/ppermute | solution.py:14
  80.9 11.7 %collective-permute-start.4 = (f32[16,8192]{1,0:T(8,128)S(1)}, f32[16,8192]{1,0:T(8,128)S(1)}, u32[]{:S(2)}, u32[]{:S(2)}) collective-permute-start(f32[16,8192]{1,0:T(8,128)S(1)} %slice_select_fusion.3), channel_id=1, source_target_pairs={{0,2},{1,3},{2,0},{3,1},{4,6},{5,7},{6,4},{7,5},{8,10},{9,11},{10,... | collective-permute-start | bytes 1572872 | tf_op jit(solution)/shard_map/ppermute | solution.py:14
  82.2 19.7 %copy-start.2 = (bf16[1,8,8192]{2,1,0:T(8,128)(2,1)S(1)}, bf16[1,8,8192]{2,1,0:T(8,128)(2,1)}, u32[]{:S(2)}) copy-start(bf16[1,8,8192]{2,1,0:T(8,128)(2,1)} %param.11) | copy-start | bytes 393220
  82.2 10.7 %collective-permute-start.8 = (f32[8,8192]{1,0:T(8,128)S(1)}, f32[8,8192]{1,0:T(8,128)S(1)}, u32[]{:S(2)}, u32[]{:S(2)}) collective-permute-start(f32[8,8192]{1,0:T(8,128)S(1)} %slice_select_fusion.4), channel_id=1, source_target_pairs={{0,1},{1,0},{2,3},{3,2},{4,5},{5,4},{6,7},{7,6},{8,9},{9,8},{10,11... | collective-permute-start | bytes 786440 | tf_op jit(solution)/shard_map/ppermute | solution.py:14
  92.8 2.9 %collective-permute-start.5 = (f32[8,8192]{1,0:T(8,128)S(1)}, f32[8,8192]{1,0:T(8,128)S(1)}, u32[]{:S(2)}, u32[]{:S(2)}) collective-permute-start(f32[8,8192]{1,0:T(8,128)S(1)} %slice_select_fusion.5), channel_id=1, source_target_pairs={{0,1},{1,0},{2,3},{3,2},{4,5},{5,4},{6,7},{7,6},{8,9},{9,8},{10,11... | collective-permute-start | bytes 786440 | tf_op jit(solution)/shard_map/ppermute | solution.py:14
  92.9 8.9 %collective-permute-start.9 = (f32[8,8192]{1,0:T(8,128)S(1)}, f32[8,8192]{1,0:T(8,128)S(1)}, u32[]{:S(2)}, u32[]{:S(2)}) collective-permute-start(f32[8,8192]{1,0:T(8,128)S(1)} %select_add_fusion.4), channel_id=1, source_target_pairs={{0,8},{1,9},{2,10},{3,11},{4,12},{5,13},{6,14},{7,15},{8,16},{9,17... | collective-permute-start | bytes 786440 | tf_op jit(solution)/shard_map/ppermute | solution.py:20
  101.9 34.8 %copy-start.1 = (bf16[8,8192]{1,0:T(8,128)(2,1)}, bf16[8,8192]{1,0:T(8,128)(2,1)S(1)}, u32[]{:S(2)}) copy-start(bf16[8,8192]{1,0:T(8,128)(2,1)S(1)} %fusion.50) | copy-start | bytes 393220
  101.9 7.7 %collective-permute-start.13 = (bf16[8,8192]{1,0:T(8,128)(2,1)S(1)}, bf16[8,8192]{1,0:T(8,128)(2,1)S(1)}, u32[]{:S(2)}, u32[]{:S(2)}) collective-permute-start(bf16[8,8192]{1,0:T(8,128)(2,1)S(1)} %fusion.50), channel_id=1, source_target_pairs={{8,0},{9,1},{10,2},{11,3},{12,4},{13,5},{14,6},{15,7},{16,8},{17,9... | collective-permute-start | bytes 393224 | tf_op jit(solution)/shard_map/ppermute | solution.py:20
  109.7 1.3 collective-permute-start.14
  109.7 3.0 %collective-permute-start.10 = (bf16[8,8192]{1,0:T(8,128)(2,1)S(1)}, bf16[8,8192]{1,0:T(8,128)(2,1)S(1)}, u32[]{:S(2)}, u32[]{:S(2)}) collective-permute-start(bf16[8,8192]{1,0:T(8,128)(2,1)S(1)} %fusion.50), channel_id=1, source_target_pairs={{0,1},{1,0},{2,3},{3,2},{4,5},{5,4},{6,7},{7,6},{8,9},{9,8},{10,11... | collective-permute-start | bytes 393224 | tf_op jit(solution)/shard_map/ppermute | solution.py:14
  111.1 9.2 %collective-permute-start.15 = (bf16[16,8192]{1,0:T(8,128)(2,1)S(1)}, bf16[16,8192]{1,0:T(8,128)(2,1)S(1)}, u32[]{:S(2)}, u32[]{:S(2)}) collective-permute-start(bf16[16,8192]{1,0:T(8,128)(2,1)S(1)} %maximum_select_fusion.11), channel_id=1, source_target_pairs={{0,2},{1,3},{2,0},{3,1},{4,6},{5,7},{6,4},{7,5},{8,10},{9,11},{10,... | collective-permute-start | bytes 786440 | tf_op jit(solution)/shard_map/ppermute | solution.py:14
  112.7 12.4 %collective-permute-start.11 = (bf16[16,8192]{1,0:T(8,128)(2,1)S(1)}, bf16[16,8192]{1,0:T(8,128)(2,1)S(1)}, u32[]{:S(2)}, u32[]{:S(2)}) collective-permute-start(bf16[16,8192]{1,0:T(8,128)(2,1)S(1)} %maximum_select_fusion.10), channel_id=1, source_target_pairs={{0,2},{1,3},{2,0},{3,1},{4,6},{5,7},{6,4},{7,5},{8,10},{9,11},{10,... | collective-permute-start | bytes 786440 | tf_op jit(solution)/shard_map/ppermute | solution.py:14
  120.4 14.9 %collective-permute-start.16 = (bf16[32,8192]{1,0:T(8,128)(2,1)S(1)}, bf16[32,8192]{1,0:T(8,128)(2,1)S(1)}, u32[]{:S(2)}, u32[]{:S(2)}) collective-permute-start(bf16[32,8192]{1,0:T(8,128)(2,1)S(1)} %maximum_select_fusion.8), channel_id=1, source_target_pairs={{0,4},{1,5},{2,6},{3,7},{4,0},{5,1},{6,2},{7,3},{8,12},{9,13},{10,... | collective-permute-start | bytes 1572872 | tf_op jit(solution)/shard_map/ppermute | solution.py:14
  125.2 18.8 %collective-permute-start.12 = (bf16[32,8192]{1,0:T(8,128)(2,1)S(1)}, bf16[32,8192]{1,0:T(8,128)(2,1)S(1)}, u32[]{:S(2)}, u32[]{:S(2)}) collective-permute-start(bf16[32,8192]{1,0:T(8,128)(2,1)S(1)} %maximum_select_fusion.7), channel_id=1, source_target_pairs={{0,4},{1,5},{2,6},{3,7},{4,0},{5,1},{6,2},{7,3},{8,12},{9,13},{10,... | collective-permute-start | bytes 1572872 | tf_op jit(solution)/shard_map/ppermute | solution.py:14
where the time goes:
time: 146 us
  waiting for transfers between devices  110 us (75%)
  starting transfers between devices  20.1 us (14%)
  matrix products  10.9 us (7%)
  other arithmetic  3.83 us (3%)
    ppermute x15, waiting for transfers between devices, from_partner(): return lax.ppermute(value, axis, pairs)  97.6 us
    ppermute x15, starting transfers between devices, from_partner(): return lax.ppermute(value, axis, pairs)  16 us
    ppermute x2, waiting for transfers between devices, shifted(): return lax.ppermute(block, axis, route)  12.6 us
    ppermute x2, starting transfers between devices, shifted(): return lax.ppermute(block, axis, route)  4.03 us
    dot_general x1, matrix products, on_device(): next_part = jnp.dot(codes, next_dec, preferred_element_type=jnp.float32)  3.51 us
    dot_general x2, matrix products, transposed(): lax.dot_general(left, weight, (((1,), (1,)), ((), ())), preferred_element...  3.43 us
    dot_general x1, matrix products, on_device(): jnp.dot(rows, enc_weight[0], preferred_element_type=jnp.float32)  3.16 us
  transfers between devices with their start and end apart: 17, of which 13 were waited for; matrix products, arithmetic and copies ran while one was open for 3% of the time, Pallas kernels for 0%

commit v1 on v0

v1 whole, which is shorter than its diff:
```python
import jax
import jax.numpy as jnp
from jax import lax
from jax.sharding import PartitionSpec as P

BLOCK = 128
LAYERS = 4
TILE = 32
CORES = 2
AXIS = "layer"


def swap(value, mask):
    pairs = [(source, source ^ mask) for source in range(lax.axis_size(AXIS))]
    return lax.ppermute(value, AXIS, pairs)


def shifted(block, distance):
    devices = range(lax.axis_size(AXIS))
    route = [(i - distance, i) for i in devices if i - distance in devices]
    return lax.ppermute(block, AXIS, route)


def transposed(left, weight):
    return lax.dot_general(
        left, weight, (((1,), (1,)), ((), ())), preferred_element_type=jnp.float32
    )


def gathered(slab, chips):
    near = [slab] + [swap(slab, CORES * chip) for chip in range(1, chips)]
    far = [swap(piece, 1) for piece in near]
    return jnp.concatenate(near + far, axis=0)


def scattered(part, chips):
    half = part.shape[0] // CORES
    rows = half // chips
    got = swap(part[half:].astype(jnp.bfloat16), 1)
    total = part[:half] + got.astype(jnp.float32)
    sends = [total[chip * rows : (chip + 1) * rows].astype(jnp.bfloat16) for chip in range(1, chips)]
    came = [swap(sends[chip - 1], CORES * chip) for chip in range(1, chips)]
    out = total[:rows]
    for block in came:
        out = out + block.astype(jnp.float32)
    return out


def on_device(resid, enc_weight, enc_bias, active, dec_weight, target):
    group = lax.axis_size(AXIS) // LAYERS
    chips = group // CORES
    bits = chips.bit_length() - 1
    place = lax.axis_index(AXIS) % group
    tokens = resid.shape[1]
    x = gathered(resid[0], chips)
    pre = (
        jnp.dot(x, enc_weight[0], preferred_element_type=jnp.float32)
        + enc_bias[0].astype(jnp.float32)[None, :]
    )
    order = jnp.array(
        [CORES * chip + core for core in range(CORES) for chip in range(chips)], dtype=jnp.int32
    )
    slab = jnp.bitwise_xor(order, place)
    tile = (slab * tokens) // TILE
    pick = (tile[:, None] == jnp.arange(active.shape[1], dtype=jnp.int32)[None, :]).astype(jnp.int32)
    live = jnp.sum(pick[:, :, None] * active[0][None, :, :], axis=1)
    gate = jnp.repeat(jnp.repeat(live, tokens, axis=0), BLOCK, axis=1).astype(jnp.float32)
    codes = (jax.nn.relu(pre) * gate).astype(jnp.bfloat16)
    own_dec = dec_weight[0, 0]
    next_dec = dec_weight[0, 1]
    wanted = target[0].astype(jnp.float32)
    next_part = jnp.dot(codes, next_dec, preferred_element_type=jnp.float32)
    own_part = jnp.dot(codes, own_dec, preferred_element_type=jnp.float32)
    next_sum = scattered(next_part, chips).astype(jnp.bfloat16)
    from_before = shifted(next_sum, group).astype(jnp.float32)
    own_sum = scattered(own_part, chips)
    error = (own_sum + from_before - wanted).astype(jnp.bfloat16)
    later = shifted(error, -group)
    here_rows = gathered(error, chips)
    after_rows = gathered(later, chips)
    grad = transposed(here_rows, own_dec) + transposed(after_rows, next_dec)
    features = grad.shape[1]
    grad = grad.reshape((2,) * (bits + 1) + (tokens, features))
    for axis in range(bits + 1):
        bit = 0 if axis == 0 else bits + 1 - axis
        grad = jnp.where((place >> bit) & 1 == 1, jnp.flip(grad, axis), grad)
    grad = jnp.moveaxis(grad, 0, bits).reshape(group * tokens, features)
    return (error[None], grad[None])


def solution(mesh):
    return jax.shard_map(
        on_device,
        mesh=mesh,
        in_specs=(
            P("layer", "groups", None),
            P("layer", None, None),
            P("layer", None),
            P("layer", "groups", None),
            P("layer", None, None, None),
            P("layer", "groups", None),
        ),
        out_specs=(P("layer", "groups", None), P("layer", "groups", None)),
        check_vma=False,
    )
```

time: 146 us -> 68.8 us (0.47)
  waiting for transfers between devices: 110 us -> 20.5 us
  starting transfers between devices: 20.1 us -> 26.6 us
  matrix products: 10.9 us -> 14.7 us
  local copies, waits for them, and re-layouts: 0.15 us -> 2.2 us
    ppermute x17 -> x31, waiting for transfers between devices: 110 us -> 20.5 us  [the longest x29 16.9 us: swap(): return lax.ppermute(value, AXIS, pairs)]
    ppermute x17 -> x31, starting transfers between devices: 20.1 us -> 26.6 us  [the longest x29 21.8 us: swap(): return lax.ppermute(value, AXIS, pairs)]
    dot_general x2, matrix products: 3.43 us -> 7.17 us  [transposed(): lax.dot_general(left, weight, (((1,), (1,)), ((), ())), preferred_element...]
  transfers between devices with their start and end apart: 17 -> 31, of which waited for: 13 -> 15; matrix products, arithmetic and copies ran while one was open for 3% -> 12% of each run, Pallas kernels for 0% -> 0%
where the time goes in v1:
time: 68.8 us; the launch traced here: 67.5 us
  starting transfers between devices  26.6 us (39%)
  waiting for transfers between devices  20.5 us (30%)
  matrix products  14.7 us (21%)
  other arithmetic  2.54 us (4%)
  local copies, waits for them, and re-layouts  2.2 us (3%)
  between operations  1.04 us (2%)
    ppermute x29, starting transfers between devices, swap(): return lax.ppermute(value, AXIS, pairs)  21.8 us
    ppermute x29, waiting for transfers between devices, swap(): return lax.ppermute(value, AXIS, pairs)  16.9 us
    dot_general x2, matrix products, transposed(): lax.dot_general(left, weight, (((1,), (1,)), ((), ())), preferred_element...  7.17 us
    ppermute x2, starting transfers between devices, shifted(): return lax.ppermute(block, AXIS, route)  4.78 us
    ppermute x2, waiting for transfers between devices, shifted(): return lax.ppermute(block, AXIS, route)  3.62 us
    dot_general x1, matrix products, on_device(): next_part = jnp.dot(codes, next_dec, preferred_element_type=jnp.float32)  3.53 us
    dot_general x1, matrix products, on_device(): jnp.dot(x, enc_weight[0], preferred_element_type=jnp.float32)  3.14 us
  transfers between devices with their start and end apart: 31, of which 15 were waited for; matrix products, arithmetic and copies ran while one was open for 12% of the time, Pallas kernels for 0%

profile of v1, /device:TPU:0, one launch (start us, length us, event | category | flops | bytes accessed | tf_op | source)
XLA Modules:
  0.0 67.5 jit_solution(535174505998367100)
XLA Ops:
  0.6 3.0 %collective-permute-start = (bf16[8,8192]{1,0:T(8,128)(2,1)}, bf16[8,8192]{1,0:T(8,128)(2,1)S(1)}, u32[]{:S(2)}, u32[]{:S(2)}) collective-permute-start(bf16[8,8192]{1,0:T(8,128)(2,1)} %bitcast.48), channel_id=1, source_target_pairs={{0,2},{1,3},{2,0},{3,1},{4,6},{5,7},{6,4},{7,5},{8,10},{9,11},{10,... | collective-permute-start | bytes 393224 | tf_op jit(solution)/shard_map/ppermute | solution.py:15
  3.6 1.5 %collective-permute-start.1 = (bf16[8,8192]{1,0:T(8,128)(2,1)}, bf16[8,8192]{1,0:T(8,128)(2,1)S(1)}, u32[]{:S(2)}, u32[]{:S(2)}) collective-permute-start(bf16[8,8192]{1,0:T(8,128)(2,1)} %bitcast.49), channel_id=1, source_target_pairs={{0,4},{1,5},{2,6},{3,7},{4,0},{5,1},{6,2},{7,3},{8,12},{9,13},{10,... | collective-permute-start | bytes 393224 | tf_op jit(solution)/shard_map/ppermute | solution.py:15
  5.2 0.0 collective-permute-start.2
  5.2 0.0 collective-permute-start.3
  5.2 1.0 %constant_dynamic-update-slice_fusion.7 = bf16[64,8192]{1,0:T(8,128)(2,1)S(1)} fusion(bf16[1,8,8192]{2,1,0:T(8,128)(2,1)} %param.7), kind=kLoop, calls=%fused_computation.44 | loop fusion | bytes 262144
  6.1 0.7 and_select_fusion
  6.8 0.8 %multiply_reduce_fusion = s32[8,2]{0,1:T(2,128)S(1)} fusion(s32[2,2]{1,0:T(2,128)} %bitcast.55, s32[8,2]{0,1:T(2,128)S(1)} %compare_convert_fusion), kind=kLoop, calls=%fused_computation.62 | loop fusion | flops 48 | bytes 144 | tf_op jit(solution)/shard_map/reduce_sum | solution.py:66
  7.6 0.1 copy.14
  7.7 0.7 %add.63 = f32[1,256]{1,0:T(1,128)S(1)} convert(bf16[1,256]{1,0:T(2,128)(2,1)} %param.9) | non-fusion elementwise | flops 256 | bytes 1536 | tf_op jit(solution)/shard_map/add | solution.py:57
  8.4 0.5 collective-permute-start.4
  8.9 2.7 %collective-permute-done.1 = bf16[8,8192]{1,0:T(8,128)(2,1)S(1)} collective-permute-done((bf16[8,8192]{1,0:T(8,128)(2,1)}, bf16[8,8192]{1,0:T(8,128)(2,1)S(1)}, u32[]{:S(2)}, u32[]{:S(2)}) %collective-permute-start.1) | collective-permute-done | bytes 131104 | tf_op jit(solution)/shard_map/ppermute | solution.py:15
  11.6 0.0 collective-permute-start.5
  11.6 0.6 collective-permute-start.6
  12.3 0.7 %collective-permute-done.5 = bf16[8,8192]{1,0:T(8,128)(2,1)S(1)} collective-permute-done((bf16[8,8192]{1,0:T(8,128)(2,1)S(1)}, bf16[8,8192]{1,0:T(8,128)(2,1)S(1)}, u32[]{:S(2)}, u32[]{:S(2)}) %collective-permute-start.5) | collective-permute-done | bytes 131104 | tf_op jit(solution)/shard_map/ppermute | solution.py:15
  13.0 0.2 collective-permute-done.6
  13.2 0.1 broadcast_in_dim.14
  13.3 0.0 copy-start
  13.4 3.1 %fusion.26 = bf16[64,256]{1,0:T(8,128)(2,1)S(1)} fusion(bf16[64,8192]{1,0:T(8,128)(2,1)S(1)} %constant_dynamic-update-slice_fusion, bf16[1,8192,256]{2,1,0:T(8,128)(2,1)} %param.8, f32[8,8,2,128]{3,2,1,0:T(2,128)S(1)} %bitcast.46, f32[256]{0:T(256)S(1)} %bitcast.54), kind=kOutput, calls=%fused_computation.18 | convolution fusion | flops 268500992 | bytes 5342208 | tf_op jit(solution)/shard_map/dot_general | solution.py:57
  16.5 3.5 %fusion.2 = f32[64,8192]{1,0:T(8,128)S(1)} fusion(bf16[64,256]{1,0:T(8,128)(2,1)S(1)} %fusion.26, bf16[1,2,256,8192]{3,2,1,0:T(8,128)(2,1)} %param.11), kind=kOutput, calls=%fused_computation.2 | convolution fusion | flops 268435456 | bytes 6324224 | tf_op jit(solution)/shard_map/dot_general | solution.py:72
  20.0 0.1 slice.116
  20.1 0.4 collective-permute-start.11
  20.5 0.8 %fusion.6 = f32[64,8192]{1,0:T(8,128)S(1)} fusion(bf16[64,256]{1,0:T(8,128)(2,1)S(1)} %fusion.26, bf16[1,2,256,8192]{3,2,1,0:T(8,128)(2,1)S(1)} %copy-done), kind=kOutput, calls=%fused_computation.6 | convolution fusion | flops 268435456 | bytes 6324224 | tf_op jit(solution)/shard_map/dot_general | solution.py:73
  21.4 0.1 slice.117
  21.4 0.0 copy-start.1
  21.5 0.2 collective-permute-start.7
  21.7 0.4 collective-permute-done.11
  22.1 0.1 fusion.40
  22.2 1.6 %collective-permute-start.14 = (bf16[8,8192]{1,0:T(8,128)(2,1)S(1)}, bf16[8,8192]{1,0:T(8,128)(2,1)S(1)}, u32[]{:S(2)}, u32[]{:S(2)}) collective-permute-start(bf16[8,8192]{1,0:T(8,128)(2,1)S(1)} %get-tuple-element.12), channel_id=1, source_target_pairs={{0,6},{1,7},{2,4},{3,5},{4,2},{5,3},{6,0},{7,1},{8,14},{9,15},{10,... | collective-permute-start | bytes 393224 | tf_op jit(solution)/shard_map/ppermute | solution.py:15
  23.8 1.0 %collective-permute-start.13 = (bf16[8,8192]{1,0:T(8,128)(2,1)S(1)}, bf16[8,8192]{1,0:T(8,128)(2,1)S(1)}, u32[]{:S(2)}, u32[]{:S(2)}) collective-permute-start(bf16[8,8192]{1,0:T(8,128)(2,1)S(1)} %get-tuple-element.13), channel_id=1, source_target_pairs={{0,4},{1,5},{2,6},{3,7},{4,0},{5,1},{6,2},{7,3},{8,12},{9,13},{10,... | collective-permute-start | bytes 393224 | tf_op jit(solution)/shard_map/ppermute | solution.py:15
  24.8 1.1 %collective-permute-start.12 = (bf16[8,8192]{1,0:T(8,128)(2,1)S(1)}, bf16[8,8192]{1,0:T(8,128)(2,1)S(1)}, u32[]{:S(2)}, u32[]{:S(2)}) collective-permute-start(bf16[8,8192]{1,0:T(8,128)(2,1)S(1)} %get-tuple-element.11), channel_id=1, source_target_pairs={{0,2},{1,3},{2,0},{3,1},{4,6},{5,7},{6,4},{7,5},{8,10},{9,11},{10,... | collective-permute-start | bytes 393224 | tf_op jit(solution)/shard_map/ppermute | solution.py:15
  25.8 0.1 fusion.39
  26.0 1.5 %collective-permute-start.10 = (bf16[8,8192]{1,0:T(8,128)(2,1)S(1)}, bf16[8,8192]{1,0:T(8,128)(2,1)S(1)}, u32[]{:S(2)}, u32[]{:S(2)}) collective-permute-start(bf16[8,8192]{1,0:T(8,128)(2,1)S(1)} %get-tuple-element.9), channel_id=1, source_target_pairs={{0,6},{1,7},{2,4},{3,5},{4,2},{5,3},{6,0},{7,1},{8,14},{9,15},{10,... | collective-permute-start | bytes 393224 | tf_op jit(solution)/shard_map/ppermute | solution.py:15
  27.5 1.0 %collective-permute-start.9 = (bf16[8,8192]{1,0:T(8,128)(2,1)S(1)}, bf16[8,8192]{1,0:T(8,128)(2,1)S(1)}, u32[]{:S(2)}, u32[]{:S(2)}) collective-permute-start(bf16[8,8192]{1,0:T(8,128)(2,1)S(1)} %get-tuple-element.10), channel_id=1, source_target_pairs={{0,4},{1,5},{2,6},{3,7},{4,0},{5,1},{6,2},{7,3},{8,12},{9,13},{10,... | collective-permute-start | bytes 393224 | tf_op jit(solution)/shard_map/ppermute | solution.py:15
  28.5 1.1 %collective-permute-done.14 = bf16[8,8192]{1,0:T(8,128)(2,1)S(1)} collective-permute-done((bf16[8,8192]{1,0:T(8,128)(2,1)S(1)}, bf16[8,8192]{1,0:T(8,128)(2,1)S(1)}, u32[]{:S(2)}, u32[]{:S(2)}) %collective-permute-start.14) | collective-permute-done | bytes 131104 | tf_op jit(solution)/shard_map/ppermute | solution.py:15
  29.6 0.7 %collective-permute-start.8 = (bf16[8,8192]{1,0:T(8,128)(2,1)S(1)}, bf16[8,8192]{1,0:T(8,128)(2,1)S(1)}, u32[]{:S(2)}, u32[]{:S(2)}) collective-permute-start(bf16[8,8192]{1,0:T(8,128)(2,1)S(1)} %get-tuple-element.8), channel_id=1, source_target_pairs={{0,2},{1,3},{2,0},{3,1},{4,6},{5,7},{6,4},{7,5},{8,10},{9,11},{10,... | collective-permute-start | bytes 393224 | tf_op jit(solution)/shard_map/ppermute | solution.py:15
  30.3 2.1 %collective-permute-done.13 = bf16[8,8192]{1,0:T(8,128)(2,1)S(1)} collective-permute-done((bf16[8,8192]{1,0:T(8,128)(2,1)S(1)}, bf16[8,8192]{1,0:T(8,128)(2,1)S(1)}, u32[]{:S(2)}, u32[]{:S(2)}) %collective-permute-start.13) | collective-permute-done | bytes 131104 | tf_op jit(solution)/shard_map/ppermute | solution.py:15
  32.4 0.1 fusion.31
  32.5 3.5 %collective-permute-start.15 = (bf16[8,8192]{1,0:T(8,128)(2,1)S(1)}, bf16[8,8192]{1,0:T(8,128)(2,1)S(1)}, u32[]{:S(2)}, u32[]{:S(2)}) collective-permute-start(bf16[8,8192]{1,0:T(8,128)(2,1)S(1)} %fusion.31), channel_id=1, source_target_pairs={{0,8},{1,9},{2,10},{3,11},{4,12},{5,13},{6,14},{7,15},{8,16},{9,17... | collective-permute-start | bytes 393224 | tf_op jit(solution)/shard_map/ppermute | solution.py:21
  36.0 1.4 %collective-permute-done.9 = bf16[8,8192]{1,0:T(8,128)(2,1)S(1)} collective-permute-done((bf16[8,8192]{1,0:T(8,128)(2,1)S(1)}, bf16[8,8192]{1,0:T(8,128)(2,1)S(1)}, u32[]{:S(2)}, u32[]{:S(2)}) %collective-permute-start.9) | collective-permute-done | bytes 131104 | tf_op jit(solution)/shard_map/ppermute | solution.py:15
  37.4 0.1 collective-permute-done.8
  37.5 1.2 %collective-permute-done.15 = bf16[8,8192]{1,0:T(8,128)(2,1)S(1)} collective-permute-done((bf16[8,8192]{1,0:T(8,128)(2,1)S(1)}, bf16[8,8192]{1,0:T(8,128)(2,1)S(1)}, u32[]{:S(2)}, u32[]{:S(2)}) %collective-permute-start.15) | collective-permute-done | bytes 131104 | tf_op jit(solution)/shard_map/ppermute | solution.py:21
  38.7 0.1 constant_dynamic-update-slice_fusion.15
  38.8 0.0 copy-start.2
  38.8 1.3 %collective-permute-start.23 = (bf16[8,8192]{1,0:T(8,128)(2,1)S(1)}, bf16[8,8192]{1,0:T(8,128)(2,1)S(1)}, u32[]{:S(2)}, u32[]{:S(2)}) collective-permute-start(bf16[8,8192]{1,0:T(8,128)(2,1)S(1)} %get-tuple-element.3), channel_id=1, source_target_pairs={{8,0},{9,1},{10,2},{11,3},{12,4},{13,5},{14,6},{15,7},{16,8},{17,9... | collective-permute-start | bytes 393224 | tf_op jit(solution)/shard_map/ppermute | solution.py:21
  40.1 0.9 %collective-permute-start.16 = (bf16[8,8192]{1,0:T(8,128)(2,1)S(1)}, bf16[8,8192]{1,0:T(8,128)(2,1)S(1)}, u32[]{:S(2)}, u32[]{:S(2)}) collective-permute-start(bf16[8,8192]{1,0:T(8,128)(2,1)S(1)} %get-tuple-element.3), channel_id=1, source_target_pairs={{0,2},{1,3},{2,0},{3,1},{4,6},{5,7},{6,4},{7,5},{8,10},{9,11},{10,... | collective-permute-start | bytes 393224 | tf_op jit(solution)/shard_map/ppermute | solution.py:15
  41.0 1.2 %collective-permute-start.17 = (bf16[8,8192]{1,0:T(8,128)(2,1)S(1)}, bf16[8,8192]{1,0:T(8,128)(2,1)S(1)}, u32[]{:S(2)}, u32[]{:S(2)}) collective-permute-start(bf16[8,8192]{1,0:T(8,128)(2,1)S(1)} %get-tuple-element.3), channel_id=1, source_target_pairs={{0,4},{1,5},{2,6},{3,7},{4,0},{5,1},{6,2},{7,3},{8,12},{9,13},{10,... | collective-permute-start | bytes 393224 | tf_op jit(solution)/shard_map/ppermute | solution.py:15
  42.2 1.4 %collective-permute-start.18 = (bf16[8,8192]{1,0:T(8,128)(2,1)S(1)}, bf16[8,8192]{1,0:T(8,128)(2,1)S(1)}, u32[]{:S(2)}, u32[]{:S(2)}) collective-permute-start(bf16[8,8192]{1,0:T(8,128)(2,1)S(1)} %get-tuple-element.3), channel_id=1, source_target_pairs={{0,6},{1,7},{2,4},{3,5},{4,2},{5,3},{6,0},{7,1},{8,14},{9,15},{10,... | collective-permute-start | bytes 393224 | tf_op jit(solution)/shard_map/ppermute | solution.py:15
  43.7 2.5 %collective-permute-done.23 = bf16[8,8192]{1,0:T(8,128)(2,1)S(1)} collective-permute-done((bf16[8,8192]{1,0:T(8,128)(2,1)S(1)}, bf16[8,8192]{1,0:T(8,128)(2,1)S(1)}, u32[]{:S(2)}, u32[]{:S(2)}) %collective-permute-start.23) | collective-permute-done | bytes 131104 | tf_op jit(solution)/shard_map/ppermute | solution.py:21
  46.1 0.9 %collective-permute-start.24 = (bf16[8,8192]{1,0:T(8,128)(2,1)S(1)}, bf16[8,8192]{1,0:T(8,128)(2,1)S(1)}, u32[]{:S(2)}, u32[]{:S(2)}) collective-permute-start(bf16[8,8192]{1,0:T(8,128)(2,1)S(1)} %collective-permute-done.23), channel_id=1, source_target_pairs={{0,2},{1,3},{2,0},{3,1},{4,6},{5,7},{6,4},{7,5},{8,10},{9,11},{10,... | collective-permute-start | bytes 393224 | tf_op jit(solution)/shard_map/ppermute | solution.py:15
  47.1 0.6 collective-permute-start.21
  47.7 1.2 %collective-permute-done.18 = bf16[8,8192]{1,0:T(8,128)(2,1)S(1)} collective-permute-done((bf16[8,8192]{1,0:T(8,128)(2,1)S(1)}, bf16[8,8192]{1,0:T(8,128)(2,1)S(1)}, u32[]{:S(2)}, u32[]{:S(2)}) %collective-permute-start.18) | collective-permute-done | bytes 131104 | tf_op jit(solution)/shard_map/ppermute | solution.py:15
  48.9 1.0 %collective-permute-start.25 = (bf16[8,8192]{1,0:T(8,128)(2,1)S(1)}, bf16[8,8192]{1,0:T(8,128)(2,1)S(1)}, u32[]{:S(2)}, u32[]{:S(2)}) collective-permute-start(bf16[8,8192]{1,0:T(8,128)(2,1)S(1)} %collective-permute-done.23), channel_id=1, source_target_pairs={{0,4},{1,5},{2,6},{3,7},{4,0},{5,1},{6,2},{7,3},{8,12},{9,13},{10,... | collective-permute-start | bytes 393224 | tf_op jit(solution)/shard_map/ppermute | solution.py:15
  50.0 1.9 %collective-permute-start.26 = (bf16[8,8192]{1,0:T(8,128)(2,1)S(1)}, bf16[8,8192]{1,0:T(8,128)(2,1)S(1)}, u32[]{:S(2)}, u32[]{:S(2)}) collective-permute-start(bf16[8,8192]{1,0:T(8,128)(2,1)S(1)} %collective-permute-done.23), channel_id=1, source_target_pairs={{0,6},{1,7},{2,4},{3,5},{4,2},{5,3},{6,0},{7,1},{8,14},{9,15},{10,... | collective-permute-start | bytes 393224 | tf_op jit(solution)/shard_map/ppermute | solution.py:15
  51.9 0.1 collective-permute-start.27
  52.1 5.6 %collective-permute-done.25 = bf16[8,8192]{1,0:T(8,128)(2,1)S(1)} collective-permute-done((bf16[8,8192]{1,0:T(8,128)(2,1)S(1)}, bf16[8,8192]{1,0:T(8,128)(2,1)S(1)}, u32[]{:S(2)}, u32[]{:S(2)}) %collective-permute-start.25) | collective-permute-done | bytes 131104 | tf_op jit(solution)/shard_map/ppermute | solution.py:15
  57.7 3.6 %fusion.4 = f32[64,256]{1,0:T(8,128)S(1)} fusion(bf16[64,8192]{1,0:T(8,128)(2,1)S(1)} %constant_dynamic-update-slice_fusion.8, bf16[1,2,256,8192]{3,2,1,0:T(8,128)(2,1)} %param.11), kind=kOutput, calls=%fused_computation.4 | convolution fusion | flops 268435456 | bytes 5308416 | tf_op jit(solution)/shard_map/dot_general | solution.py:25
  61.3 0.1 collective-permute-start.28
  61.4 0.5 collective-permute-start.29
  61.9 0.1 collective-permute-start.30
  62.0 0.7 %collective-permute-done.28 = bf16[8,8192]{1,0:T(8,128)(2,1)S(1)} collective-permute-done((bf16[8,8192]{1,0:T(8,128)(2,1)S(1)}, bf16[8,8192]{1,0:T(8,128)(2,1)S(1)}, u32[]{:S(2)}, u32[]{:S(2)}) %collective-permute-start.28) | collective-permute-done | bytes 131104 | tf_op jit(solution)/shard_map/ppermute | solution.py:15
  62.7 0.2 collective-permute-done.29
  62.9 0.3 collective-permute-done.30
  63.2 3.6 %fusion.23 = f32[64,256]{1,0:T(8,128)S(1)} fusion(f32[64,256]{1,0:T(8,128)S(1)} %fusion.4, bf16[64,8192]{1,0:T(8,128)(2,1)S(1)} %constant_dynamic-update-slice_fusion.16, bf16[1,2,256,8192]{3,2,1,0:T(8,128)(2,1)} %param.11), kind=kOutput, calls=%fused_computation.17 | convolution fusion | flops 268451840 | bytes 5373952 | tf_op jit(solution)/shard_map/dot_general | solution.py:25
  66.9 0.6 copy.12
  (52 shorter events, 0.4 us)
Async XLA Ops:
  0.6 7.7 %collective-permute-start = (bf16[8,8192]{1,0:T(8,128)(2,1)}, bf16[8,8192]{1,0:T(8,128)(2,1)S(1)}, u32[]{:S(2)}, u32[]{:S(2)}) collective-permute-start(bf16[8,8192]{1,0:T(8,128)(2,1)} %bitcast.48), channel_id=1, source_target_pairs={{0,2},{1,3},{2,0},{3,1},{4,6},{5,7},{6,4},{7,5},{8,10},{9,11},{10,... | collective-permute-start | bytes 393224 | tf_op jit(solution)/shard_map/ppermute | solution.py:15
  3.6 8.0 %collective-permute-start.1 = (bf16[8,8192]{1,0:T(8,128)(2,1)}, bf16[8,8192]{1,0:T(8,128)(2,1)S(1)}, u32[]{:S(2)}, u32[]{:S(2)}) collective-permute-start(bf16[8,8192]{1,0:T(8,128)(2,1)} %bitcast.49), channel_id=1, source_target_pairs={{0,4},{1,5},{2,6},{3,7},{4,0},{5,1},{6,2},{7,3},{8,12},{9,13},{10,... | collective-permute-start | bytes 393224 | tf_op jit(solution)/shard_map/ppermute | solution.py:15
  5.2 6.5 %collective-permute-start.2 = (bf16[8,8192]{1,0:T(8,128)(2,1)}, bf16[8,8192]{1,0:T(8,128)(2,1)S(1)}, u32[]{:S(2)}, u32[]{:S(2)}) collective-permute-start(bf16[8,8192]{1,0:T(8,128)(2,1)} %bitcast.50), channel_id=1, source_target_pairs={{0,6},{1,7},{2,4},{3,5},{4,2},{5,3},{6,0},{7,1},{8,14},{9,15},{10,... | collective-permute-start | bytes 393224 | tf_op jit(solution)/shard_map/ppermute | solution.py:15
  5.2 7.1 %collective-permute-start.3 = (bf16[8,8192]{1,0:T(8,128)(2,1)}, bf16[8,8192]{1,0:T(8,128)(2,1)S(1)}, u32[]{:S(2)}, u32[]{:S(2)}) collective-permute-start(bf16[8,8192]{1,0:T(8,128)(2,1)} %bitcast.51), channel_id=1, source_target_pairs={{0,1},{1,0},{2,3},{3,2},{4,5},{5,4},{6,7},{7,6},{8,9},{9,8},{10,11... | collective-permute-start | bytes 393224 | tf_op jit(solution)/shard_map/ppermute | solution.py:15
  8.4 3.9 %collective-permute-start.4 = (bf16[8,8192]{1,0:T(8,128)(2,1)S(1)}, bf16[8,8192]{1,0:T(8,128)(2,1)S(1)}, u32[]{:S(2)}, u32[]{:S(2)}) collective-permute-start(bf16[8,8192]{1,0:T(8,128)(2,1)S(1)} %collective-permute-done), channel_id=1, source_target_pairs={{0,1},{1,0},{2,3},{3,2},{4,5},{5,4},{6,7},{7,6},{8,9},{9,8},{10,11... | collective-permute-start | bytes 393224 | tf_op jit(solution)/shard_map/ppermute | solution.py:15
  11.6 1.3 %collective-permute-start.5 = (bf16[8,8192]{1,0:T(8,128)(2,1)S(1)}, bf16[8,8192]{1,0:T(8,128)(2,1)S(1)}, u32[]{:S(2)}, u32[]{:S(2)}) collective-permute-start(bf16[8,8192]{1,0:T(8,128)(2,1)S(1)} %collective-permute-done.1), channel_id=1, source_target_pairs={{0,1},{1,0},{2,3},{3,2},{4,5},{5,4},{6,7},{7,6},{8,9},{9,8},{10,11... | collective-permute-start | bytes 393224 | tf_op jit(solution)/shard_map/ppermute | solution.py:15
  11.6 1.6 %collective-permute-start.6 = (bf16[8,8192]{1,0:T(8,128)(2,1)S(1)}, bf16[8,8192]{1,0:T(8,128)(2,1)S(1)}, u32[]{:S(2)}, u32[]{:S(2)}) collective-permute-start(bf16[8,8192]{1,0:T(8,128)(2,1)S(1)} %collective-permute-done.2), channel_id=1, source_target_pairs={{0,1},{1,0},{2,3},{3,2},{4,5},{5,4},{6,7},{7,6},{8,9},{9,8},{10,11... | collective-permute-start | bytes 393224 | tf_op jit(solution)/shard_map/ppermute | solution.py:15
  13.3 7.2 %copy-start = (bf16[1,2,256,8192]{3,2,1,0:T(8,128)(2,1)S(1)}, bf16[1,2,256,8192]{3,2,1,0:T(8,128)(2,1)}, u32[]{:S(2)}) copy-start(bf16[1,2,256,8192]{3,2,1,0:T(8,128)(2,1)} %param.11) | copy-start | bytes 25165828
  20.1 2.0 %collective-permute-start.11 = (bf16[32,8192]{1,0:T(8,128)(2,1)S(1)}, bf16[32,8192]{1,0:T(8,128)(2,1)S(1)}, u32[]{:S(2)}, u32[]{:S(2)}) collective-permute-start(bf16[32,8192]{1,0:T(8,128)(2,1)S(1)} %slice.116), channel_id=1, source_target_pairs={{0,1},{1,0},{2,3},{3,2},{4,5},{5,4},{6,7},{7,6},{8,9},{9,8},{10,11... | collective-permute-start | bytes 1572872 | tf_op jit(solution)/shard_map/ppermute | solution.py:15
  21.4 17.2 %copy-start.1 = (bf16[1,8,8192]{2,1,0:T(8,128)(2,1)S(1)}, bf16[1,8,8192]{2,1,0:T(8,128)(2,1)}, u32[]{:S(2)}) copy-start(bf16[1,8,8192]{2,1,0:T(8,128)(2,1)} %param.12) | copy-start | bytes 393220
  21.5 4.3 %collective-permute-start.7 = (bf16[32,8192]{1,0:T(8,128)(2,1)S(1)}, bf16[32,8192]{1,0:T(8,128)(2,1)S(1)}, u32[]{:S(2)}, u32[]{:S(2)}) collective-permute-start(bf16[32,8192]{1,0:T(8,128)(2,1)S(1)} %slice.117), channel_id=1, source_target_pairs={{0,1},{1,0},{2,3},{3,2},{4,5},{5,4},{6,7},{7,6},{8,9},{9,8},{10,11... | collective-permute-start | bytes 1572872 | tf_op jit(solution)/shard_map/ppermute | solution.py:15
  22.2 7.3 %collective-permute-start.14 = (bf16[8,8192]{1,0:T(8,128)(2,1)S(1)}, bf16[8,8192]{1,0:T(8,128)(2,1)S(1)}, u32[]{:S(2)}, u32[]{:S(2)}) collective-permute-start(bf16[8,8192]{1,0:T(8,128)(2,1)S(1)} %get-tuple-element.12), channel_id=1, source_target_pairs={{0,6},{1,7},{2,4},{3,5},{4,2},{5,3},{6,0},{7,1},{8,14},{9,15},{10,... | collective-permute-start | bytes 393224 | tf_op jit(solution)/shard_map/ppermute | solution.py:15
  23.8 8.6 %collective-permute-start.13 = (bf16[8,8192]{1,0:T(8,128)(2,1)S(1)}, bf16[8,8192]{1,0:T(8,128)(2,1)S(1)}, u32[]{:S(2)}, u32[]{:S(2)}) collective-permute-start(bf16[8,8192]{1,0:T(8,128)(2,1)S(1)} %get-tuple-element.13), channel_id=1, source_target_pairs={{0,4},{1,5},{2,6},{3,7},{4,0},{5,1},{6,2},{7,3},{8,12},{9,13},{10,... | collective-permute-start | bytes 393224 | tf_op jit(solution)/shard_map/ppermute | solution.py:15
  24.8 7.7 %collective-permute-start.12 = (bf16[8,8192]{1,0:T(8,128)(2,1)S(1)}, bf16[8,8192]{1,0:T(8,128)(2,1)S(1)}, u32[]{:S(2)}, u32[]{:S(2)}) collective-permute-start(bf16[8,8192]{1,0:T(8,128)(2,1)S(1)} %get-tuple-element.11), channel_id=1, source_target_pairs={{0,2},{1,3},{2,0},{3,1},{4,6},{5,7},{6,4},{7,5},{8,10},{9,11},{10,... | collective-permute-start | bytes 393224 | tf_op jit(solution)/shard_map/ppermute | solution.py:15
  26.0 10.0 %collective-permute-start.10 = (bf16[8,8192]{1,0:T(8,128)(2,1)S(1)}, bf16[8,8192]{1,0:T(8,128)(2,1)S(1)}, u32[]{:S(2)}, u32[]{:S(2)}) collective-permute-start(bf16[8,8192]{1,0:T(8,128)(2,1)S(1)} %get-tuple-element.9), channel_id=1, source_target_pairs={{0,6},{1,7},{2,4},{3,5},{4,2},{5,3},{6,0},{7,1},{8,14},{9,15},{10,... | collective-permute-start | bytes 393224 | tf_op jit(solution)/shard_map/ppermute | solution.py:15
  27.5 9.9 %collective-permute-start.9 = (bf16[8,8192]{1,0:T(8,128)(2,1)S(1)}, bf16[8,8192]{1,0:T(8,128)(2,1)S(1)}, u32[]{:S(2)}, u32[]{:S(2)}) collective-permute-start(bf16[8,8192]{1,0:T(8,128)(2,1)S(1)} %get-tuple-element.10), channel_id=1, source_target_pairs={{0,4},{1,5},{2,6},{3,7},{4,0},{5,1},{6,2},{7,3},{8,12},{9,13},{10,... | collective-permute-start | bytes 393224 | tf_op jit(solution)/shard_map/ppermute | solution.py:15
  29.6 8.0 %collective-permute-start.8 = (bf16[8,8192]{1,0:T(8,128)(2,1)S(1)}, bf16[8,8192]{1,0:T(8,128)(2,1)S(1)}, u32[]{:S(2)}, u32[]{:S(2)}) collective-permute-start(bf16[8,8192]{1,0:T(8,128)(2,1)S(1)} %get-tuple-element.8), channel_id=1, source_target_pairs={{0,2},{1,3},{2,0},{3,1},{4,6},{5,7},{6,4},{7,5},{8,10},{9,11},{10,... | collective-permute-start | bytes 393224 | tf_op jit(solution)/shard_map/ppermute | solution.py:15
  32.5 6.2 %collective-permute-start.15 = (bf16[8,8192]{1,0:T(8,128)(2,1)S(1)}, bf16[8,8192]{1,0:T(8,128)(2,1)S(1)}, u32[]{:S(2)}, u32[]{:S(2)}) collective-permute-start(bf16[8,8192]{1,0:T(8,128)(2,1)S(1)} %fusion.31), channel_id=1, source_target_pairs={{0,8},{1,9},{2,10},{3,11},{4,12},{5,13},{6,14},{7,15},{8,16},{9,17... | collective-permute-start | bytes 393224 | tf_op jit(solution)/shard_map/ppermute | solution.py:21
  38.8 23.2 %copy-start.2 = (bf16[8,8192]{1,0:T(8,128)(2,1)}, bf16[8,8192]{1,0:T(8,128)(2,1)S(1)}, u32[]{:S(2)}) copy-start(bf16[8,8192]{1,0:T(8,128)(2,1)S(1)} %get-tuple-element.3) | copy-start | bytes 393220
  38.8 7.3 %collective-permute-start.23 = (bf16[8,8192]{1,0:T(8,128)(2,1)S(1)}, bf16[8,8192]{1,0:T(8,128)(2,1)S(1)}, u32[]{:S(2)}, u32[]{:S(2)}) collective-permute-start(bf16[8,8192]{1,0:T(8,128)(2,1)S(1)} %get-tuple-element.3), channel_id=1, source_target_pairs={{8,0},{9,1},{10,2},{11,3},{12,4},{13,5},{14,6},{15,7},{16,8},{17,9... | collective-permute-start | bytes 393224 | tf_op jit(solution)/shard_map/ppermute | solution.py:21
  40.1 7.0 %collective-permute-start.16 = (bf16[8,8192]{1,0:T(8,128)(2,1)S(1)}, bf16[8,8192]{1,0:T(8,128)(2,1)S(1)}, u32[]{:S(2)}, u32[]{:S(2)}) collective-permute-start(bf16[8,8192]{1,0:T(8,128)(2,1)S(1)} %get-tuple-element.3), channel_id=1, source_target_pairs={{0,2},{1,3},{2,0},{3,1},{4,6},{5,7},{6,4},{7,5},{8,10},{9,11},{10,... | collective-permute-start | bytes 393224 | tf_op jit(solution)/shard_map/ppermute | solution.py:15
  41.0 6.1 %collective-permute-start.17 = (bf16[8,8192]{1,0:T(8,128)(2,1)S(1)}, bf16[8,8192]{1,0:T(8,128)(2,1)S(1)}, u32[]{:S(2)}, u32[]{:S(2)}) collective-permute-start(bf16[8,8192]{1,0:T(8,128)(2,1)S(1)} %get-tuple-element.3), channel_id=1, source_target_pairs={{0,4},{1,5},{2,6},{3,7},{4,0},{5,1},{6,2},{7,3},{8,12},{9,13},{10,... | collective-permute-start | bytes 393224 | tf_op jit(solution)/shard_map/ppermute | solution.py:15
  42.2 6.7 %collective-permute-start.18 = (bf16[8,8192]{1,0:T(8,128)(2,1)S(1)}, bf16[8,8192]{1,0:T(8,128)(2,1)S(1)}, u32[]{:S(2)}, u32[]{:S(2)}) collective-permute-start(bf16[8,8192]{1,0:T(8,128)(2,1)S(1)} %get-tuple-element.3), channel_id=1, source_target_pairs={{0,6},{1,7},{2,4},{3,5},{4,2},{5,3},{6,0},{7,1},{8,14},{9,15},{10,... | collective-permute-start | bytes 393224 | tf_op jit(solution)/shard_map/ppermute | solution.py:15
  43.7 5.2 %collective-permute-start.19 = (bf16[8,8192]{1,0:T(8,128)(2,1)S(1)}, bf16[8,8192]{1,0:T(8,128)(2,1)S(1)}, u32[]{:S(2)}, u32[]{:S(2)}) collective-permute-start(bf16[8,8192]{1,0:T(8,128)(2,1)S(1)} %get-tuple-element.3), channel_id=1, source_target_pairs={{0,1},{1,0},{2,3},{3,2},{4,5},{5,4},{6,7},{7,6},{8,9},{9,8},{10,11... | collective-permute-start | bytes 393224 | tf_op jit(solution)/shard_map/ppermute | solution.py:15
  46.1 5.9 %collective-permute-start.24 = (bf16[8,8192]{1,0:T(8,128)(2,1)S(1)}, bf16[8,8192]{1,0:T(8,128)(2,1)S(1)}, u32[]{:S(2)}, u32[]{:S(2)}) collective-permute-start(bf16[8,8192]{1,0:T(8,128)(2,1)S(1)} %collective-permute-done.23), channel_id=1, source_target_pairs={{0,2},{1,3},{2,0},{3,1},{4,6},{5,7},{6,4},{7,5},{8,10},{9,11},{10,... | collective-permute-start | bytes 393224 | tf_op jit(solution)/shard_map/ppermute | solution.py:15
  47.1 2.9 %collective-permute-start.20 = (bf16[8,8192]{1,0:T(8,128)(2,1)S(1)}, bf16[8,8192]{1,0:T(8,128)(2,1)S(1)}, u32[]{:S(2)}, u32[]{:S(2)}) collective-permute-start(bf16[8,8192]{1,0:T(8,128)(2,1)S(1)} %collective-permute-done.16), channel_id=1, source_target_pairs={{0,1},{1,0},{2,3},{3,2},{4,5},{5,4},{6,7},{7,6},{8,9},{9,8},{10,11... | collective-permute-start | bytes 393224 | tf_op jit(solution)/shard_map/ppermute | solution.py:15
  47.1 4.8 %collective-permute-start.21 = (bf16[8,8192]{1,0:T(8,128)(2,1)S(1)}, bf16[8,8192]{1,0:T(8,128)(2,1)S(1)}, u32[]{:S(2)}, u32[]{:S(2)}) collective-permute-start(bf16[8,8192]{1,0:T(8,128)(2,1)S(1)} %collective-permute-done.17), channel_id=1, source_target_pairs={{0,1},{1,0},{2,3},{3,2},{4,5},{5,4},{6,7},{7,6},{8,9},{9,8},{10,11... | collective-permute-start | bytes 393224 | tf_op jit(solution)/shard_map/ppermute | solution.py:15
  48.9 3.1 %collective-permute-start.22 = (bf16[8,8192]{1,0:T(8,128)(2,1)S(1)}, bf16[8,8192]{1,0:T(8,128)(2,1)S(1)}, u32[]{:S(2)}, u32[]{:S(2)}) collective-permute-start(bf16[8,8192]{1,0:T(8,128)(2,1)S(1)} %collective-permute-done.18), channel_id=1, source_target_pairs={{0,1},{1,0},{2,3},{3,2},{4,5},{5,4},{6,7},{7,6},{8,9},{9,8},{10,11... | collective-permute-start | bytes 393224 | tf_op jit(solution)/shard_map/ppermute | solution.py:15
  48.9 8.8 %collective-permute-start.25 = (bf16[8,8192]{1,0:T(8,128)(2,1)S(1)}, bf16[8,8192]{1,0:T(8,128)(2,1)S(1)}, u32[]{:S(2)}, u32[]{:S(2)}) collective-permute-start(bf16[8,8192]{1,0:T(8,128)(2,1)S(1)} %collective-permute-done.23), channel_id=1, source_target_pairs={{0,4},{1,5},{2,6},{3,7},{4,0},{5,1},{6,2},{7,3},{8,12},{9,13},{10,... | collective-permute-start | bytes 393224 | tf_op jit(solution)/shard_map/ppermute | solution.py:15
  50.0 11.9 %collective-permute-start.26 = (bf16[8,8192]{1,0:T(8,128)(2,1)S(1)}, bf16[8,8192]{1,0:T(8,128)(2,1)S(1)}, u32[]{:S(2)}, u32[]{:S(2)}) collective-permute-start(bf16[8,8192]{1,0:T(8,128)(2,1)S(1)} %collective-permute-done.23), channel_id=1, source_target_pairs={{0,6},{1,7},{2,4},{3,5},{4,2},{5,3},{6,0},{7,1},{8,14},{9,15},{10,... | collective-permute-start | bytes 393224 | tf_op jit(solution)/shard_map/ppermute | solution.py:15
  51.9 10.1 %collective-permute-start.27 = (bf16[8,8192]{1,0:T(8,128)(2,1)S(1)}, bf16[8,8192]{1,0:T(8,128)(2,1)S(1)}, u32[]{:S(2)}, u32[]{:S(2)}) collective-permute-start(bf16[8,8192]{1,0:T(8,128)(2,1)S(1)} %collective-permute-done.23), channel_id=1, source_target_pairs={{0,1},{1,0},{2,3},{3,2},{4,5},{5,4},{6,7},{7,6},{8,9},{9,8},{10,11... | collective-permute-start | bytes 393224 | tf_op jit(solution)/shard_map/ppermute | solution.py:15
  61.3 1.4 %collective-permute-start.28 = (bf16[8,8192]{1,0:T(8,128)(2,1)S(1)}, bf16[8,8192]{1,0:T(8,128)(2,1)S(1)}, u32[]{:S(2)}, u32[]{:S(2)}) collective-permute-start(bf16[8,8192]{1,0:T(8,128)(2,1)S(1)} %collective-permute-done.24), channel_id=1, source_target_pairs={{0,1},{1,0},{2,3},{3,2},{4,5},{5,4},{6,7},{7,6},{8,9},{9,8},{10,11... | collective-permute-start | bytes 393224 | tf_op jit(solution)/shard_map/ppermute | solution.py:15
  61.4 1.5 %collective-permute-start.29 = (bf16[8,8192]{1,0:T(8,128)(2,1)S(1)}, bf16[8,8192]{1,0:T(8,128)(2,1)S(1)}, u32[]{:S(2)}, u32[]{:S(2)}) collective-permute-start(bf16[8,8192]{1,0:T(8,128)(2,1)S(1)} %collective-permute-done.25), channel_id=1, source_target_pairs={{0,1},{1,0},{2,3},{3,2},{4,5},{5,4},{6,7},{7,6},{8,9},{9,8},{10,11... | collective-permute-start | bytes 393224 | tf_op jit(solution)/shard_map/ppermute | solution.py:15
  61.9 1.3 %collective-permute-start.30 = (bf16[8,8192]{1,0:T(8,128)(2,1)S(1)}, bf16[8,8192]{1,0:T(8,128)(2,1)S(1)}, u32[]{:S(2)}, u32[]{:S(2)}) collective-permute-start(bf16[8,8192]{1,0:T(8,128)(2,1)S(1)} %collective-permute-done.26), channel_id=1, source_target_pairs={{0,1},{1,0},{2,3},{3,2},{4,5},{5,4},{6,7},{7,6},{8,9},{9,8},{10,11... | collective-permute-start | bytes 393224 | tf_op jit(solution)/shard_map/ppermute | solution.py:15

commit v2 on v1

v2 whole, which is shorter than its diff:
```python
import jax
import jax.numpy as jnp
from jax import lax
from jax.sharding import PartitionSpec as P

BLOCK = 128
LAYERS = 4
TILE = 32
CORES = 2
AXIS = "layer"


def swap(value, mask):
    pairs = [(source, source ^ mask) for source in range(lax.axis_size(AXIS))]
    return lax.ppermute(value, AXIS, pairs)


def shifted(block, distance):
    devices = range(lax.axis_size(AXIS))
    route = [(i - distance, i) for i in devices if i - distance in devices]
    return lax.ppermute(block, AXIS, route)


def transposed(left, weight):
    return lax.dot_general(
        left, weight, (((1,), (1,)), ((), ())), preferred_element_type=jnp.float32
    )


def chip_sets(group):
    size = lax.axis_size(AXIS)
    return [
        [start + CORES * chip + core for chip in range(group // CORES)]
        for start in range(0, size, group)
        for core in range(CORES)
    ]


def gathered(slab, group):
    near = lax.all_gather(slab, AXIS, axis_index_groups=chip_sets(group), tiled=True)
    return jnp.concatenate([near, swap(near, 1)], axis=0)


def scattered(part, group):
    half = part.shape[0] // CORES
    got = swap(part[half:].astype(jnp.bfloat16), 1)
    total = (part[:half] + got.astype(jnp.float32)).astype(jnp.bfloat16)
    blocks = total.reshape(group // CORES, -1, part.shape[1])
    came = lax.all_to_all(blocks, AXIS, 0, 0, axis_index_groups=chip_sets(group))
    return jnp.sum(came.astype(jnp.float32), axis=0)


def on_device(resid, enc_weight, enc_bias, active, dec_weight, target):
    group = lax.axis_size(AXIS) // LAYERS
    chips = group // CORES
    place = lax.axis_index(AXIS) % group
    tokens = resid.shape[1]
    x = gathered(resid[0], group)
    pre = (
        jnp.dot(x, enc_weight[0], preferred_element_type=jnp.float32)
        + enc_bias[0].astype(jnp.float32)[None, :]
    )
    slab = jnp.arange(group, dtype=jnp.int32) % chips * CORES + (
        (place % CORES) ^ (jnp.arange(group, dtype=jnp.int32) // chips)
    )
    tile = (slab * tokens) // TILE
    pick = (tile[:, None] == jnp.arange(active.shape[1], dtype=jnp.int32)[None, :]).astype(jnp.int32)
    live = jnp.sum(pick[:, :, None] * active[0][None, :, :], axis=1)
    gate = jnp.repeat(jnp.repeat(live, tokens, axis=0), BLOCK, axis=1).astype(jnp.float32)
    codes = (jax.nn.relu(pre) * gate).astype(jnp.bfloat16)
    own_dec = dec_weight[0, 0]
    next_dec = dec_weight[0, 1]
    wanted = target[0].astype(jnp.float32)
    next_part = jnp.dot(codes, next_dec, preferred_element_type=jnp.float32)
    own_part = jnp.dot(codes, own_dec, preferred_element_type=jnp.float32)
    next_sum = scattered(next_part, group).astype(jnp.bfloat16)
    from_before = shifted(next_sum, group).astype(jnp.float32)
    own_sum = scattered(own_part, group)
    error = (own_sum + from_before - wanted).astype(jnp.bfloat16)
    later = shifted(error, -group)
    here_rows = gathered(error, group)
    after_rows = gathered(later, group)
    grad = transposed(here_rows, own_dec) + transposed(after_rows, next_dec)
    features = grad.shape[1]
    grad = grad.reshape(CORES, chips, tokens, features)
    grad = jnp.where(place % CORES == 1, jnp.flip(grad, 0), grad)
    grad = jnp.swapaxes(grad, 0, 1).reshape(group * tokens, features)
    return (error[None], grad[None])


def solution(mesh):
    return jax.shard_map(
        on_device,
        mesh=mesh,
        in_specs=(
            P("layer", "groups", None),
            P("layer", None, None),
            P("layer", None),
            P("layer", "groups", None),
            P("layer", None, None, None),
            P("layer", "groups", None),
        ),
        out_specs=(P("layer", "groups", None), P("layer", "groups", None)),
        check_vma=False,
    )
```

time: 68.8 us -> 83.2 us (1.21)
  blocking collectives: 0 us -> 32.2 us
  starting transfers between devices: 26.6 us -> 12.4 us
  waiting for transfers between devices: 20.5 us -> 17.1 us
  other arithmetic: 2.54 us -> 4.5 us
  local copies, waits for them, and re-layouts: 2.2 us -> 0.97 us
    all_gather x0 -> x3, blocking collectives: none -> 32.2 us  [gathered(): lax.all_gather(slab, AXIS, axis_index_groups=chip_sets(group), tiled=True)]
    ppermute x29 -> x5, starting transfers between devices: 21.8 us -> 0.65 us  [swap(): return lax.ppermute(value, AXIS, pairs)]
    ppermute x29 -> x5, waiting for transfers between devices: 16.9 us -> 0.73 us  [swap(): return lax.ppermute(value, AXIS, pairs)]
    all_to_all x0 -> x2, waiting for transfers between devices: none -> 10.8 us  [scattered(): lax.all_to_all(blocks, AXIS, 0, 0, axis_index_groups=chip_sets(group))]
    all_to_all x0 -> x2, starting transfers between devices: none -> 6.94 us  [scattered(): lax.all_to_all(blocks, AXIS, 0, 0, axis_index_groups=chip_sets(group))]
    reshape x0 -> x2, other arithmetic: none -> 2.82 us  [scattered(): blocks = total.reshape(group // CORES, -1, part.shape[1])]
    ppermute x2, waiting for transfers between devices: 3.62 us -> 5.56 us  [shifted(): return lax.ppermute(block, AXIS, route)]
    unnamed x27 -> x7, local copies, waits for them, and re-layouts: 1.25 us -> 0.1 us
  transfers between devices with their start and end apart: 31 -> 9, of which waited for: 15 -> 5; matrix products, arithmetic and copies ran while one was open for 12% -> 11% of each run, Pallas kernels for 0% -> 0%
where the time goes in v2:
time: 83.2 us; the launch traced here: 82.7 us
  blocking collectives  32.2 us (39%)
  waiting for transfers between devices  17.1 us (21%)
  matrix products  14.7 us (18%)
  starting transfers between devices  12.4 us (15%)
  other arithmetic  4.5 us (5%)
  local copies, waits for them, and re-layouts  0.97 us (1%)
  between operations  0.85 us (1%)
    all_gather x3, blocking collectives, gathered(): lax.all_gather(slab, AXIS, axis_index_groups=chip_sets(group), tiled=True)  32.2 us
    all_to_all x2, waiting for transfers between devices, scattered(): lax.all_to_all(blocks, AXIS, 0, 0, axis_index_groups=chip_sets(group))  10.8 us
    dot_general x2, matrix products, transposed(): lax.dot_general(left, weight, (((1,), (1,)), ((), ())), preferred_element...  7.17 us
    all_to_all x2, starting transfers between devices, scattered(): lax.all_to_all(blocks, AXIS, 0, 0, axis_index_groups=chip_sets(group))  6.94 us
    ppermute x2, waiting for transfers between devices, shifted(): return lax.ppermute(block, AXIS, route)  5.56 us
    ppermute x2, starting transfers between devices, shifted(): return lax.ppermute(block, AXIS, route)  4.78 us
    dot_general x1, matrix products, on_device(): next_part = jnp.dot(codes, next_dec, preferred_element_type=jnp.float32)  3.53 us
    dot_general x1, matrix products, on_device(): jnp.dot(x, enc_weight[0], preferred_element_type=jnp.float32)  3.14 us
  transfers between devices with their start and end apart: 9, of which 5 were waited for; matrix products, arithmetic and copies ran while one was open for 11% of the time, Pallas kernels for 0%

profile of v2, /device:TPU:0, one launch (start us, length us, event | category | flops | bytes accessed | tf_op | source)
XLA Modules:
  0.0 82.7 jit_solution(7059775932420007245)
XLA Ops:
  0.6 11.8 %all-gather = bf16[1,32,8192]{2,1,0:T(8,128)(2,1)S(1)} all-gather(bf16[1,8,8192]{2,1,0:T(8,128)(2,1)} %param.6), channel_id=2, replica_groups={{0,2,4,6},{1,3,5,7},{8,10,12,14},{9,11,13,15},{16,18,20,22},{17,19,21,2..., dimensions={1}, use_global_device_ids=true | all-gather | bytes 655360 | tf_op jit(solution)/shard_map/all_gather | solution.py:40
  12.5 0.0 collective-permute-start
  12.5 0.8 multiply_reduce_fusion
  13.3 0.7 add.72
  14.0 0.1 copy.13
  14.1 0.3 collective-permute-done
  14.4 0.1 broadcast_in_dim.14
  14.5 0.0 copy-start
  14.5 3.1 %fusion.26 = bf16[64,256]{1,0:T(8,128)(2,1)S(1)} fusion(bf16[1,8192,256]{2,1,0:T(8,128)(2,1)} %param.7, bf16[32,8192]{1,0:T(8,128)(2,1)S(1)} %collective-permute-done, bf16[32,8192]{1,0:T(8,128)(2,1)S(1)} %bitcast.46, f32[8,8,2,128]{3,2,1,0:T(2,128)S(1)} %bitcast.48, f32[256]{0:T(256)S(1)} %bitcast.51), kind=kOutput, calls=%fused_computation.18 | convolution fusion | flops 270598144 | bytes 5342208 | tf_op jit(solution)/shard_map/dot_general | solution.py:60
  17.7 3.5 %fusion.2 = f32[64,8192]{1,0:T(8,128)S(1)} fusion(bf16[64,256]{1,0:T(8,128)(2,1)S(1)} %fusion.26, bf16[1,2,256,8192]{3,2,1,0:T(8,128)(2,1)} %param.10), kind=kOutput, calls=%fused_computation.2 | convolution fusion | flops 268435456 | bytes 6324224 | tf_op jit(solution)/shard_map/dot_general | solution.py:74
  21.2 0.1 slice.60
  21.3 0.2 collective-permute-start.2
  21.5 0.0 copy-done
  21.5 0.8 %fusion.6 = f32[64,8192]{1,0:T(8,128)S(1)} fusion(bf16[64,256]{1,0:T(8,128)(2,1)S(1)} %fusion.26, bf16[1,2,256,8192]{3,2,1,0:T(8,128)(2,1)S(1)} %copy-done), kind=kOutput, calls=%fused_computation.6 | convolution fusion | flops 268435456 | bytes 6324224 | tf_op jit(solution)/shard_map/dot_general | solution.py:75
  22.4 0.0 copy-start.2
  22.4 0.1 slice.61
  22.4 0.4 collective-permute-start.1
  22.8 0.4 collective-permute-done.2
  23.2 0.9 %fusion.41 = bf16[4,8,8192]{2,1,0:T(8,128)(2,1)} fusion(bf16[32,8192]{1,0:T(8,128)(2,1)S(1)} %collective-permute-done.2, f32[64,8192]{1,0:T(8,128)S(1)} %fusion.2), kind=kLoop, calls=%fused_computation.36 | loop fusion | flops 786432 | bytes 2097152 | tf_op jit(solution)/shard_map/reshape | solution.py:48
  24.1 3.5 %all-to-all-start.1 = ((bf16[4,8,8192]{2,1,0:T(8,128)(2,1)}), bf16[4,8,8192]{2,1,0:T(8,128)(2,1)S(1)}, u32[]{:S(2)}, u32[]{:S(2)}) async-start(bf16[4,8,8192]{2,1,0:T(8,128)(2,1)} %fusion.41), calls=%async_computation.1 | async-start | bytes 1048576 | tf_op jit(solution)/shard_map/all_to_all | solution.py:49
  27.6 0.0 collective-permute-done.1
  27.6 1.9 %fusion.40 = bf16[4,8,8192]{2,1,0:T(8,128)(2,1)} fusion(bf16[32,8192]{1,0:T(8,128)(2,1)} %collective-permute-done.1, f32[64,8192]{1,0:T(8,128)S(1)} %fusion.6), kind=kLoop, calls=%fused_computation.35 | loop fusion | flops 786432 | bytes 2097152 | tf_op jit(solution)/shard_map/reshape | solution.py:48
  29.6 6.7 %all-to-all-done.1 = bf16[4,8,8192]{2,1,0:T(8,128)(2,1)S(1)} async-done(((bf16[4,8,8192]{2,1,0:T(8,128)(2,1)}), bf16[4,8,8192]{2,1,0:T(8,128)(2,1)S(1)}, u32[]{:S(2)}, u32[]{:S(2)}) %all-to-all-start.1) | async-done | bytes 524320 | tf_op jit(solution)/shard_map/all_to_all | solution.py:49
  36.2 3.5 %all-to-all-start = ((bf16[4,8,8192]{2,1,0:T(8,128)(2,1)}), bf16[4,8,8192]{2,1,0:T(8,128)(2,1)S(1)}, u32[]{:S(2)}, u32[]{:S(2)}) async-start(bf16[4,8,8192]{2,1,0:T(8,128)(2,1)} %fusion.40), calls=%async_computation | async-start | bytes 1048576 | tf_op jit(solution)/shard_map/all_to_all | solution.py:49
  39.7 0.1 reduce_sum.32
  39.8 3.5 %collective-permute-start.3 = (bf16[8,8192]{1,0:T(8,128)(2,1)S(1)}, bf16[8,8192]{1,0:T(8,128)(2,1)S(1)}, u32[]{:S(2)}, u32[]{:S(2)}) collective-permute-start(bf16[8,8192]{1,0:T(8,128)(2,1)S(1)} %reduce_sum.32), channel_id=1, source_target_pairs={{0,8},{1,9},{2,10},{3,11},{4,12},{5,13},{6,14},{7,15},{8,16},{9,17... | collective-permute-start | bytes 393224 | tf_op jit(solution)/shard_map/ppermute | solution.py:21
  43.3 4.2 %all-to-all-done = bf16[4,8,8192]{2,1,0:T(8,128)(2,1)S(1)} async-done(((bf16[4,8,8192]{2,1,0:T(8,128)(2,1)}), bf16[4,8,8192]{2,1,0:T(8,128)(2,1)S(1)}, u32[]{:S(2)}, u32[]{:S(2)}) %all-to-all-start) | async-done | bytes 524320 | tf_op jit(solution)/shard_map/all_to_all | solution.py:49
  47.5 0.1 convert_reduce_fusion
  47.5 0.0 collective-permute-done.3
  47.5 0.0 copy-done.2
  47.5 0.1 fusion.42
  47.6 0.0 copy-start.1
  47.6 1.3 %collective-permute-start.5 = (bf16[8,8192]{1,0:T(8,128)(2,1)S(1)}, bf16[8,8192]{1,0:T(8,128)(2,1)S(1)}, u32[]{:S(2)}, u32[]{:S(2)}) collective-permute-start(bf16[8,8192]{1,0:T(8,128)(2,1)S(1)} %fusion.42), channel_id=1, source_target_pairs={{8,0},{9,1},{10,2},{11,3},{12,4},{13,5},{14,6},{15,7},{16,8},{17,9... | collective-permute-start | bytes 393224 | tf_op jit(solution)/shard_map/ppermute | solution.py:21
  48.9 5.6 %collective-permute-done.5 = bf16[8,8192]{1,0:T(8,128)(2,1)S(1)} collective-permute-done((bf16[8,8192]{1,0:T(8,128)(2,1)S(1)}, bf16[8,8192]{1,0:T(8,128)(2,1)S(1)}, u32[]{:S(2)}, u32[]{:S(2)}) %collective-permute-start.5) | collective-permute-done | bytes 131104 | tf_op jit(solution)/shard_map/ppermute | solution.py:21
  54.5 10.0 %all_gather.11 = bf16[32,8192]{1,0:T(8,128)(2,1)S(1)} all-gather(bf16[8,8192]{1,0:T(8,128)(2,1)S(1)} %collective-permute-done.5), channel_id=1, replica_groups={{0,2,4,6},{1,3,5,7},{8,10,12,14},{9,11,13,15},{16,18,20,22},{17,19,21,2..., dimensions={0}, use_global_device_ids=true | all-gather | bytes 655360 | tf_op jit(solution)/shard_map/all_gather | solution.py:40
  64.5 0.0 collective-permute-start.6
  64.5 10.3 %all_gather.10 = bf16[32,8192]{1,0:T(8,128)(2,1)S(1)} all-gather(bf16[8,8192]{1,0:T(8,128)(2,1)S(1)} %fusion.42), channel_id=1, replica_groups={{0,2,4,6},{1,3,5,7},{8,10,12,14},{9,11,13,15},{16,18,20,22},{17,19,21,2..., dimensions={0}, use_global_device_ids=true | all-gather | bytes 655360 | tf_op jit(solution)/shard_map/all_gather | solution.py:40
  74.8 0.0 collective-permute-start.4
  74.8 0.0 collective-permute-done.6
  74.8 3.6 %fusion = f32[64,256]{1,0:T(8,128)S(1)} fusion(bf16[1,2,256,8192]{3,2,1,0:T(8,128)(2,1)} %param.10, bf16[32,8192]{1,0:T(8,128)(2,1)S(1)} %collective-permute-done.6, bf16[32,8192]{1,0:T(8,128)(2,1)S(1)} %all_gather.11), kind=kOutput, calls=%fused_computation | convolution fusion | flops 270532608 | bytes 5308416 | tf_op jit(solution)/shard_map/dot_general | solution.py:25
  78.4 0.0 collective-permute-done.4
  78.4 3.6 %fusion.23 = f32[64,256]{1,0:T(8,128)S(1)} fusion(f32[64,256]{1,0:T(8,128)S(1)} %fusion, bf16[1,2,256,8192]{3,2,1,0:T(8,128)(2,1)} %param.10, bf16[32,8192]{1,0:T(8,128)(2,1)S(1)} %collective-permute-done.4, bf16[32,8192]{1,0:T(8,128)(2,1)S(1)} %all_gather.10), kind=kOutput, calls=%fused_computation.17 | convolution fusion | flops 270548992 | bytes 5373952 | tf_op jit(solution)/shard_map/dot_general | solution.py:25
  82.0 0.0 copy-done.1
  82.0 0.6 copy.11
  (5 shorter events, 0.0 us)
Async XLA Ops:
  12.5 1.9 %collective-permute-start = (bf16[32,8192]{1,0:T(8,128)(2,1)S(1)}, bf16[32,8192]{1,0:T(8,128)(2,1)S(1)}, u32[]{:S(2)}, u32[]{:S(2)}) collective-permute-start(bf16[32,8192]{1,0:T(8,128)(2,1)S(1)} %bitcast.45), channel_id=1, source_target_pairs={{0,1},{1,0},{2,3},{3,2},{4,5},{5,4},{6,7},{7,6},{8,9},{9,8},{10,11... | collective-permute-start | bytes 1572872 | tf_op jit(solution)/shard_map/ppermute | solution.py:15
  14.5 7.0 %copy-start = (bf16[1,2,256,8192]{3,2,1,0:T(8,128)(2,1)S(1)}, bf16[1,2,256,8192]{3,2,1,0:T(8,128)(2,1)}, u32[]{:S(2)}) copy-start(bf16[1,2,256,8192]{3,2,1,0:T(8,128)(2,1)} %param.10) | copy-start | bytes 25165828
  21.3 2.0 %collective-permute-start.2 = (bf16[32,8192]{1,0:T(8,128)(2,1)S(1)}, bf16[32,8192]{1,0:T(8,128)(2,1)S(1)}, u32[]{:S(2)}, u32[]{:S(2)}) collective-permute-start(bf16[32,8192]{1,0:T(8,128)(2,1)S(1)} %slice.60), channel_id=1, source_target_pairs={{0,1},{1,0},{2,3},{3,2},{4,5},{5,4},{6,7},{7,6},{8,9},{9,8},{10,11... | collective-permute-start | bytes 1572872 | tf_op jit(solution)/shard_map/ppermute | solution.py:15
  22.4 25.2 %copy-start.2 = (bf16[1,8,8192]{2,1,0:T(8,128)(2,1)S(1)}, bf16[1,8,8192]{2,1,0:T(8,128)(2,1)}, u32[]{:S(2)}) copy-start(bf16[1,8,8192]{2,1,0:T(8,128)(2,1)} %param.11) | copy-start | bytes 393220
  22.4 5.2 %collective-permute-start.1 = (bf16[32,8192]{1,0:T(8,128)(2,1)S(1)}, bf16[32,8192]{1,0:T(8,128)(2,1)}, u32[]{:S(2)}, u32[]{:S(2)}) collective-permute-start(bf16[32,8192]{1,0:T(8,128)(2,1)S(1)} %slice.61), channel_id=1, source_target_pairs={{0,1},{1,0},{2,3},{3,2},{4,5},{5,4},{6,7},{7,6},{8,9},{9,8},{10,11... | collective-permute-start | bytes 1572872 | tf_op jit(solution)/shard_map/ppermute | solution.py:15
  24.1 12.1 %all-to-all-start.1 = ((bf16[4,8,8192]{2,1,0:T(8,128)(2,1)}), bf16[4,8,8192]{2,1,0:T(8,128)(2,1)S(1)}, u32[]{:S(2)}, u32[]{:S(2)}) async-start(bf16[4,8,8192]{2,1,0:T(8,128)(2,1)} %fusion.41), calls=%async_computation.1 | async-start | bytes 1048576 | tf_op jit(solution)/shard_map/all_to_all | solution.py:49
  36.2 11.2 %all-to-all-start = ((bf16[4,8,8192]{2,1,0:T(8,128)(2,1)}), bf16[4,8,8192]{2,1,0:T(8,128)(2,1)S(1)}, u32[]{:S(2)}, u32[]{:S(2)}) async-start(bf16[4,8,8192]{2,1,0:T(8,128)(2,1)} %fusion.40), calls=%async_computation | async-start | bytes 1048576 | tf_op jit(solution)/shard_map/all_to_all | solution.py:49
  39.8 7.7 %collective-permute-start.3 = (bf16[8,8192]{1,0:T(8,128)(2,1)S(1)}, bf16[8,8192]{1,0:T(8,128)(2,1)S(1)}, u32[]{:S(2)}, u32[]{:S(2)}) collective-permute-start(bf16[8,8192]{1,0:T(8,128)(2,1)S(1)} %reduce_sum.32), channel_id=1, source_target_pairs={{0,8},{1,9},{2,10},{3,11},{4,12},{5,13},{6,14},{7,15},{8,16},{9,17... | collective-permute-start | bytes 393224 | tf_op jit(solution)/shard_map/ppermute | solution.py:21
  47.6 34.4 %copy-start.1 = (bf16[8,8192]{1,0:T(8,128)(2,1)}, bf16[8,8192]{1,0:T(8,128)(2,1)S(1)}, u32[]{:S(2)}) copy-start(bf16[8,8192]{1,0:T(8,128)(2,1)S(1)} %fusion.42) | copy-start | bytes 393220
  47.6 6.9 %collective-permute-start.5 = (bf16[8,8192]{1,0:T(8,128)(2,1)S(1)}, bf16[8,8192]{1,0:T(8,128)(2,1)S(1)}, u32[]{:S(2)}, u32[]{:S(2)}) collective-permute-start(bf16[8,8192]{1,0:T(8,128)(2,1)S(1)} %fusion.42), channel_id=1, source_target_pairs={{8,0},{9,1},{10,2},{11,3},{12,4},{13,5},{14,6},{15,7},{16,8},{17,9... | collective-permute-start | bytes 393224 | tf_op jit(solution)/shard_map/ppermute | solution.py:21
  64.5 10.4 %collective-permute-start.6 = (bf16[32,8192]{1,0:T(8,128)(2,1)S(1)}, bf16[32,8192]{1,0:T(8,128)(2,1)S(1)}, u32[]{:S(2)}, u32[]{:S(2)}) collective-permute-start(bf16[32,8192]{1,0:T(8,128)(2,1)S(1)} %all_gather.11), channel_id=1, source_target_pairs={{0,1},{1,0},{2,3},{3,2},{4,5},{5,4},{6,7},{7,6},{8,9},{9,8},{10,11... | collective-permute-start | bytes 1572872 | tf_op jit(solution)/shard_map/ppermute | solution.py:15
  74.8 3.6 %collective-permute-start.4 = (bf16[32,8192]{1,0:T(8,128)(2,1)S(1)}, bf16[32,8192]{1,0:T(8,128)(2,1)S(1)}, u32[]{:S(2)}, u32[]{:S(2)}) collective-permute-start(bf16[32,8192]{1,0:T(8,128)(2,1)S(1)} %all_gather.10), channel_id=1, source_target_pairs={{0,1},{1,0},{2,3},{3,2},{4,5},{5,4},{6,7},{7,6},{8,9},{9,8},{10,11... | collective-permute-start | bytes 1572872 | tf_op jit(solution)/shard_map/ppermute | solution.py:15

commit v3 on v1

--- a/solution.py
+++ b/solution.py
@@ -1,6 +1,8 @@
 import jax
 import jax.numpy as jnp
 from jax import lax
+from jax.experimental import pallas as pl
+from jax.experimental.pallas import tpu as pltpu
 from jax.sharding import PartitionSpec as P
 
 BLOCK = 128
@@ -46,15 +48,43 @@
     return out
 
 
+def load_kernel(*refs):
+    count = len(refs) // 2
+    sources, held, sems = refs[:count], refs[count : 2 * count], refs[-1]
+    copies = [
+        pltpu.make_async_copy(source, target, sems.at[i])
+        for i, (source, target) in enumerate(zip(sources, held))
+    ]
+    for copy in copies:
+        copy.start()
+    for copy in copies:
+        copy.wait()
+
+
+def loaded(*weights):
+    size = sum(w.size * w.dtype.itemsize for w in weights)
+    return pl.pallas_call(
+        load_kernel,
+        out_shape=[pltpu.VMEM(w.shape, w.dtype) for w in weights],
+        in_specs=[pl.BlockSpec(memory_space=pl.ANY)] * len(weights),
+        out_specs=[pl.BlockSpec(memory_space=pltpu.VMEM)] * len(weights),
+        scratch_shapes=[pltpu.SemaphoreType.DMA((len(weights),))],
+        compiler_params=pltpu.CompilerParams(vmem_limit_bytes=1 << 20),
+        cost_estimate=pl.CostEstimate(flops=0, bytes_accessed=2 * size, transcendentals=0),
+        name="load_weights",
+    )(*[pltpu.with_memory_space_constraint(w, pltpu.HBM) for w in weights])
+
+
 def on_device(resid, enc_weight, enc_bias, active, dec_weight, target):
     group = lax.axis_size(AXIS) // LAYERS
     chips = group // CORES
     bits = chips.bit_length() - 1
     place = lax.axis_index(AXIS) % group
     tokens = resid.shape[1]
+    enc, dec = loaded(enc_weight, dec_weight)
     x = gathered(resid[0], chips)
     pre = (
-        jnp.dot(x, enc_weight[0], preferred_element_type=jnp.float32)
+        jnp.dot(x, enc[0], preferred_element_type=jnp.float32)
         + enc_bias[0].astype(jnp.float32)[None, :]
     )
     order = jnp.array(
@@ -66,8 +96,8 @@
     live = jnp.sum(pick[:, :, None] * active[0][None, :, :], axis=1)
     gate = jnp.repeat(jnp.repeat(live, tokens, axis=0), BLOCK, axis=1).astype(jnp.float32)
     codes = (jax.nn.relu(pre) * gate).astype(jnp.bfloat16)
-    own_dec = dec_weight[0, 0]
-    next_dec = dec_weight[0, 1]
+    own_dec = dec[0, 0]
+    next_dec = dec[0, 1]
     wanted = target[0].astype(jnp.float32)
     next_part = jnp.dot(codes, next_dec, preferred_element_type=jnp.float32)
     own_part = jnp.dot(codes, own_dec, preferred_element_type=jnp.float32)

time: 68.8 us -> 67.2 us (0.977)
  the two profiles are of different devices: /device:TPU:0 before, /device:TPU:17 now
where the time goes in v3:
time: 67.2 us; the launch traced here: 66.9 us
  starting transfers between devices  31.7 us (47%)
  waiting for transfers between devices  15.1 us (22%)
  matrix products  9.68 us (14%)
  Pallas kernels  4.68 us (7%)
  other arithmetic  2.54 us (4%)
  local copies, waits for them, and re-layouts  2.15 us (3%)
  between operations  1.04 us (2%)
    ppermute x29, starting transfers between devices, swap(): return lax.ppermute(value, AXIS, pairs)  26.5 us
    ppermute x29, waiting for transfers between devices, swap(): return lax.ppermute(value, AXIS, pairs)  13.6 us
    dot_general x2, matrix products, transposed(): lax.dot_general(left, weight, (((1,), (1,)), ((), ())), preferred_element...  7.17 us
    ppermute x2, starting transfers between devices, shifted(): return lax.ppermute(block, AXIS, route)  5.28 us
    pallas_call x1, Pallas kernels, loaded(): pl.pallas_call(load_kernel, out_shape=[pltpu.VMEM(w.shape, w.dtype) for w...  4.68 us
    ppermute x2, waiting for transfers between devices, shifted(): return lax.ppermute(block, AXIS, route)  1.48 us
  transfers between devices with their start and end apart: 31, of which 12 were waited for; matrix products, arithmetic and copies ran while one was open for 12% of the time, Pallas kernels for 7%

profile of v3, /device:TPU:17, one launch (start us, length us, event | category | flops | bytes accessed | tf_op | source)
XLA Modules:
  0.0 66.9 jit_solution(13322628068492229443)
XLA Ops:
  0.6 1.3 %collective-permute-start = (bf16[8,8192]{1,0:T(8,128)(2,1)}, bf16[8,8192]{1,0:T(8,128)(2,1)S(1)}, u32[]{:S(2)}, u32[]{:S(2)}) collective-permute-start(bf16[8,8192]{1,0:T(8,128)(2,1)} %bitcast.48), channel_id=1, source_target_pairs={{0,2},{1,3},{2,0},{3,1},{4,6},{5,7},{6,4},{7,5},{8,10},{9,11},{10,... | collective-permute-start | bytes 393224 | tf_op jit(solution)/shard_map/ppermute | solution.py:17
  1.9 1.2 %collective-permute-start.1 = (bf16[8,8192]{1,0:T(8,128)(2,1)}, bf16[8,8192]{1,0:T(8,128)(2,1)S(1)}, u32[]{:S(2)}, u32[]{:S(2)}) collective-permute-start(bf16[8,8192]{1,0:T(8,128)(2,1)} %bitcast.49), channel_id=1, source_target_pairs={{0,4},{1,5},{2,6},{3,7},{4,0},{5,1},{6,2},{7,3},{8,12},{9,13},{10,... | collective-permute-start | bytes 393224 | tf_op jit(solution)/shard_map/ppermute | solution.py:17
  3.1 0.2 collective-permute-start.2
  3.3 1.5 %collective-permute-start.3 = (bf16[8,8192]{1,0:T(8,128)(2,1)}, bf16[8,8192]{1,0:T(8,128)(2,1)S(1)}, u32[]{:S(2)}, u32[]{:S(2)}) collective-permute-start(bf16[8,8192]{1,0:T(8,128)(2,1)} %bitcast.51), channel_id=1, source_target_pairs={{0,1},{1,0},{2,3},{3,2},{4,5},{5,4},{6,7},{7,6},{8,9},{9,8},{10,11... | collective-permute-start | bytes 393224 | tf_op jit(solution)/shard_map/ppermute | solution.py:17
  4.9 0.9 %constant_dynamic-update-slice_fusion.7 = bf16[64,8192]{1,0:T(8,128)(2,1)S(1)} fusion(bf16[1,8,8192]{2,1,0:T(8,128)(2,1)} %param.7), kind=kLoop, calls=%fused_computation.44 | loop fusion | bytes 262144
  5.8 0.7 %and_select_fusion = s32[8]{0:T(128)S(1)} fusion(s32[8]{0:T(128)} %constant.42.clone, s32[]{:T(128)S(6)} %select_n.32), kind=kLoop, calls=%fused_computation.64 | loop fusion | flops 136 | bytes 68 | tf_op jit(solution)/shard_map/jit(floor_divide)/jit(_where)/select_n | solution.py:94
  6.5 0.8 %multiply_reduce_fusion = s32[8,2]{0,1:T(2,128)S(1)} fusion(s32[2,2]{1,0:T(2,128)} %bitcast.55, s32[8,2]{0,1:T(2,128)S(1)} %compare_convert_fusion), kind=kLoop, calls=%fused_computation.62 | loop fusion | flops 48 | bytes 144 | tf_op jit(solution)/shard_map/reduce_sum | solution.py:96
  7.2 0.1 copy.14
  7.3 0.7 %add.63 = f32[1,256]{1,0:T(1,128)S(1)} convert(bf16[1,256]{1,0:T(2,128)(2,1)} %param.9) | non-fusion elementwise | flops 256 | bytes 1536 | tf_op jit(solution)/shard_map/add | solution.py:87
  8.0 4.7 %load_weights.1 = (bf16[1,8192,256]{2,1,0:T(8,128)(2,1)S(1)}, bf16[1,2,256,8192]{3,2,1,0:T(8,128)(2,1)S(1)}) custom-call(bf16[1,8192,256]{2,1,0:T(8,128)(2,1)} %refs_0_.1, bf16[1,2,256,8192]{3,2,1,0:T(8,128)(2,1)} %refs_1_.1), custom_call_target="tpu_custom_call" | custom-call | bytes 25165824 | tf_op jit(solution)/shard_map/load_weights/pallas_call | solution.py:66
  12.7 0.1 collective-permute-start.4
  12.8 0.5 collective-permute-start.5
  13.4 0.1 collective-permute-start.6
  13.5 0.6 collective-permute-done.4
  14.1 0.2 collective-permute-done.5
  14.4 0.4 collective-permute-done.6
  14.8 0.1 broadcast_in_dim.14
  15.0 0.8 %fusion.26 = bf16[64,256]{1,0:T(8,128)(2,1)S(1)} fusion(bf16[64,8192]{1,0:T(8,128)(2,1)S(1)} %constant_dynamic-update-slice_fusion, bf16[1,8192,256]{2,1,0:T(8,128)(2,1)S(1)} %get-tuple-element.4, f32[8,8,2,128]{3,2,1,0:T(2,128)S(1)} %bitcast.46, f32[256]{0:T(256)S(1)} %bitcast.54), kind=kOutput, calls=%fused_computation.18 | convolution fusion | flops 268500992 | bytes 5342208 | tf_op jit(solution)/shard_map/dot_general | solution.py:87
  15.8 0.8 %fusion.2 = f32[64,8192]{1,0:T(8,128)S(1)} fusion(bf16[64,256]{1,0:T(8,128)(2,1)S(1)} %fusion.26, bf16[1,2,256,8192]{3,2,1,0:T(8,128)(2,1)S(1)} %get-tuple-element.5), kind=kOutput, calls=%fused_computation.2 | convolution fusion | flops 268435456 | bytes 6324224 | tf_op jit(solution)/shard_map/dot_general | solution.py:102
  16.6 0.1 slice.116
  16.7 0.2 collective-permute-start.11
  16.9 0.8 %fusion.6 = f32[64,8192]{1,0:T(8,128)S(1)} fusion(bf16[64,256]{1,0:T(8,128)(2,1)S(1)} %fusion.26, bf16[1,2,256,8192]{3,2,1,0:T(8,128)(2,1)S(1)} %get-tuple-element.5), kind=kOutput, calls=%fused_computation.6 | convolution fusion | flops 268435456 | bytes 6324224 | tf_op jit(solution)/shard_map/dot_general | solution.py:103
  17.8 0.1 slice.117
  17.8 0.0 copy-start.1
  17.8 0.4 collective-permute-start.7
  18.3 0.4 collective-permute-done.11
  18.7 0.1 fusion.40
  18.8 2.2 %collective-permute-start.14 = (bf16[8,8192]{1,0:T(8,128)(2,1)S(1)}, bf16[8,8192]{1,0:T(8,128)(2,1)S(1)}, u32[]{:S(2)}, u32[]{:S(2)}) collective-permute-start(bf16[8,8192]{1,0:T(8,128)(2,1)S(1)} %get-tuple-element.16), channel_id=1, source_target_pairs={{0,6},{1,7},{2,4},{3,5},{4,2},{5,3},{6,0},{7,1},{8,14},{9,15},{10,... | collective-permute-start | bytes 393224 | tf_op jit(solution)/shard_map/ppermute | solution.py:17
  21.1 0.2 collective-permute-start.13
  21.3 0.3 collective-permute-start.12
  21.6 0.1 fusion.39
  21.7 2.2 %collective-permute-start.10 = (bf16[8,8192]{1,0:T(8,128)(2,1)S(1)}, bf16[8,8192]{1,0:T(8,128)(2,1)S(1)}, u32[]{:S(2)}, u32[]{:S(2)}) collective-permute-start(bf16[8,8192]{1,0:T(8,128)(2,1)S(1)} %get-tuple-element.13), channel_id=1, source_target_pairs={{0,6},{1,7},{2,4},{3,5},{4,2},{5,3},{6,0},{7,1},{8,14},{9,15},{10,... | collective-permute-start | bytes 393224 | tf_op jit(solution)/shard_map/ppermute | solution.py:17
  23.9 0.2 collective-permute-start.9
  24.2 0.6 collective-permute-done.14
  24.8 1.2 %collective-permute-start.8 = (bf16[8,8192]{1,0:T(8,128)(2,1)S(1)}, bf16[8,8192]{1,0:T(8,128)(2,1)S(1)}, u32[]{:S(2)}, u32[]{:S(2)}) collective-permute-start(bf16[8,8192]{1,0:T(8,128)(2,1)S(1)} %get-tuple-element.12), channel_id=1, source_target_pairs={{0,2},{1,3},{2,0},{3,1},{4,6},{5,7},{6,4},{7,5},{8,10},{9,11},{10,... | collective-permute-start | bytes 393224 | tf_op jit(solution)/shard_map/ppermute | solution.py:17
  26.0 2.8 %collective-permute-done.13 = bf16[8,8192]{1,0:T(8,128)(2,1)S(1)} collective-permute-done((bf16[8,8192]{1,0:T(8,128)(2,1)S(1)}, bf16[8,8192]{1,0:T(8,128)(2,1)S(1)}, u32[]{:S(2)}, u32[]{:S(2)}) %collective-permute-start.13) | collective-permute-done | bytes 131104 | tf_op jit(solution)/shard_map/ppermute | solution.py:17
  28.8 0.1 fusion.31
  28.9 3.2 %collective-permute-start.15 = (bf16[8,8192]{1,0:T(8,128)(2,1)S(1)}, bf16[8,8192]{1,0:T(8,128)(2,1)S(1)}, u32[]{:S(2)}, u32[]{:S(2)}) collective-permute-start(bf16[8,8192]{1,0:T(8,128)(2,1)S(1)} %fusion.31), channel_id=1, source_target_pairs={{0,8},{1,9},{2,10},{3,11},{4,12},{5,13},{6,14},{7,15},{8,16},{9,17... | collective-permute-start | bytes 393224 | tf_op jit(solution)/shard_map/ppermute | solution.py:23
  32.1 1.6 %collective-permute-done.9 = bf16[8,8192]{1,0:T(8,128)(2,1)S(1)} collective-permute-done((bf16[8,8192]{1,0:T(8,128)(2,1)S(1)}, bf16[8,8192]{1,0:T(8,128)(2,1)S(1)}, u32[]{:S(2)}, u32[]{:S(2)}) %collective-permute-start.9) | collective-permute-done | bytes 131104 | tf_op jit(solution)/shard_map/ppermute | solution.py:17
  33.7 1.5 %collective-permute-done.15 = bf16[8,8192]{1,0:T(8,128)(2,1)S(1)} collective-permute-done((bf16[8,8192]{1,0:T(8,128)(2,1)S(1)}, bf16[8,8192]{1,0:T(8,128)(2,1)S(1)}, u32[]{:S(2)}, u32[]{:S(2)}) %collective-permute-start.15) | collective-permute-done | bytes 131104 | tf_op jit(solution)/shard_map/ppermute | solution.py:23
  35.1 0.1 constant_dynamic-update-slice_fusion.15
  35.2 0.0 copy-start.2
  35.2 2.1 %collective-permute-start.23 = (bf16[8,8192]{1,0:T(8,128)(2,1)S(1)}, bf16[8,8192]{1,0:T(8,128)(2,1)S(1)}, u32[]{:S(2)}, u32[]{:S(2)}) collective-permute-start(bf16[8,8192]{1,0:T(8,128)(2,1)S(1)} %get-tuple-element.7), channel_id=1, source_target_pairs={{8,0},{9,1},{10,2},{11,3},{12,4},{13,5},{14,6},{15,7},{16,8},{17,9... | collective-permute-start | bytes 393224 | tf_op jit(solution)/shard_map/ppermute | solution.py:23
  37.3 0.9 %collective-permute-start.16 = (bf16[8,8192]{1,0:T(8,128)(2,1)S(1)}, bf16[8,8192]{1,0:T(8,128)(2,1)S(1)}, u32[]{:S(2)}, u32[]{:S(2)}) collective-permute-start(bf16[8,8192]{1,0:T(8,128)(2,1)S(1)} %get-tuple-element.7), channel_id=1, source_target_pairs={{0,2},{1,3},{2,0},{3,1},{4,6},{5,7},{6,4},{7,5},{8,10},{9,11},{10,... | collective-permute-start | bytes 393224 | tf_op jit(solution)/shard_map/ppermute | solution.py:17
  38.2 0.1 collective-permute-start.17
  38.3 1.7 %collective-permute-start.18 = (bf16[8,8192]{1,0:T(8,128)(2,1)S(1)}, bf16[8,8192]{1,0:T(8,128)(2,1)S(1)}, u32[]{:S(2)}, u32[]{:S(2)}) collective-permute-start(bf16[8,8192]{1,0:T(8,128)(2,1)S(1)} %get-tuple-element.7), channel_id=1, source_target_pairs={{0,6},{1,7},{2,4},{3,5},{4,2},{5,3},{6,0},{7,1},{8,14},{9,15},{10,... | collective-permute-start | bytes 393224 | tf_op jit(solution)/shard_map/ppermute | solution.py:17
  40.1 2.7 %collective-permute-start.19 = (bf16[8,8192]{1,0:T(8,128)(2,1)S(1)}, bf16[8,8192]{1,0:T(8,128)(2,1)S(1)}, u32[]{:S(2)}, u32[]{:S(2)}) collective-permute-start(bf16[8,8192]{1,0:T(8,128)(2,1)S(1)} %get-tuple-element.7), channel_id=1, source_target_pairs={{0,1},{1,0},{2,3},{3,2},{4,5},{5,4},{6,7},{7,6},{8,9},{9,8},{10,11... | collective-permute-start | bytes 393224 | tf_op jit(solution)/shard_map/ppermute | solution.py:17
  42.7 1.0 %collective-permute-start.24 = (bf16[8,8192]{1,0:T(8,128)(2,1)S(1)}, bf16[8,8192]{1,0:T(8,128)(2,1)S(1)}, u32[]{:S(2)}, u32[]{:S(2)}) collective-permute-start(bf16[8,8192]{1,0:T(8,128)(2,1)S(1)} %collective-permute-done.23), channel_id=1, source_target_pairs={{0,2},{1,3},{2,0},{3,1},{4,6},{5,7},{6,4},{7,5},{8,10},{9,11},{10,... | collective-permute-start | bytes 393224 | tf_op jit(solution)/shard_map/ppermute | solution.py:17
  43.7 1.6 %collective-permute-start.20 = (bf16[8,8192]{1,0:T(8,128)(2,1)S(1)}, bf16[8,8192]{1,0:T(8,128)(2,1)S(1)}, u32[]{:S(2)}, u32[]{:S(2)}) collective-permute-start(bf16[8,8192]{1,0:T(8,128)(2,1)S(1)} %collective-permute-done.16), channel_id=1, source_target_pairs={{0,1},{1,0},{2,3},{3,2},{4,5},{5,4},{6,7},{7,6},{8,9},{9,8},{10,11... | collective-permute-start | bytes 393224 | tf_op jit(solution)/shard_map/ppermute | solution.py:17
  45.3 0.2 collective-permute-start.21
  45.6 3.1 %collective-permute-start.22 = (bf16[8,8192]{1,0:T(8,128)(2,1)S(1)}, bf16[8,8192]{1,0:T(8,128)(2,1)S(1)}, u32[]{:S(2)}, u32[]{:S(2)}) collective-permute-start(bf16[8,8192]{1,0:T(8,128)(2,1)S(1)} %collective-permute-done.18), channel_id=1, source_target_pairs={{0,1},{1,0},{2,3},{3,2},{4,5},{5,4},{6,7},{7,6},{8,9},{9,8},{10,11... | collective-permute-start | bytes 393224 | tf_op jit(solution)/shard_map/ppermute | solution.py:17
  48.7 0.4 collective-permute-start.25
  49.1 0.8 %collective-permute-start.26 = (bf16[8,8192]{1,0:T(8,128)(2,1)S(1)}, bf16[8,8192]{1,0:T(8,128)(2,1)S(1)}, u32[]{:S(2)}, u32[]{:S(2)}) collective-permute-start(bf16[8,8192]{1,0:T(8,128)(2,1)S(1)} %collective-permute-done.23), channel_id=1, source_target_pairs={{0,6},{1,7},{2,4},{3,5},{4,2},{5,3},{6,0},{7,1},{8,14},{9,15},{10,... | collective-permute-start | bytes 393224 | tf_op jit(solution)/shard_map/ppermute | solution.py:17
  49.9 0.6 collective-permute-start.27
  50.6 6.0 %collective-permute-done.25 = bf16[8,8192]{1,0:T(8,128)(2,1)S(1)} collective-permute-done((bf16[8,8192]{1,0:T(8,128)(2,1)S(1)}, bf16[8,8192]{1,0:T(8,128)(2,1)S(1)}, u32[]{:S(2)}, u32[]{:S(2)}) %collective-permute-start.25) | collective-permute-done | bytes 131104 | tf_op jit(solution)/shard_map/ppermute | solution.py:17
  56.7 3.6 %fusion.4 = f32[64,256]{1,0:T(8,128)S(1)} fusion(bf16[64,8192]{1,0:T(8,128)(2,1)S(1)} %constant_dynamic-update-slice_fusion.8, bf16[1,2,256,8192]{3,2,1,0:T(8,128)(2,1)} %copy-done), kind=kOutput, calls=%fused_computation.4 | convolution fusion | flops 268435456 | bytes 5308416 | tf_op jit(solution)/shard_map/dot_general | solution.py:27
  60.3 0.8 %collective-permute-start.28 = (bf16[8,8192]{1,0:T(8,128)(2,1)S(1)}, bf16[8,8192]{1,0:T(8,128)(2,1)S(1)}, u32[]{:S(2)}, u32[]{:S(2)}) collective-permute-start(bf16[8,8192]{1,0:T(8,128)(2,1)S(1)} %collective-permute-done.24), channel_id=1, source_target_pairs={{0,1},{1,0},{2,3},{3,2},{4,5},{5,4},{6,7},{7,6},{8,9},{9,8},{10,11... | collective-permute-start | bytes 393224 | tf_op jit(solution)/shard_map/ppermute | solution.py:17
  61.1 0.1 collective-permute-start.29
  61.2 0.4 collective-permute-start.30
  61.7 0.4 collective-permute-done.28
  62.1 0.3 collective-permute-done.29
  62.5 0.2 collective-permute-done.30
  62.7 3.6 %fusion.23 = f32[64,256]{1,0:T(8,128)S(1)} fusion(f32[64,256]{1,0:T(8,128)S(1)} %fusion.4, bf16[64,8192]{1,0:T(8,128)(2,1)S(1)} %constant_dynamic-update-slice_fusion.16, bf16[1,2,256,8192]{3,2,1,0:T(8,128)(2,1)} %copy-done), kind=kOutput, calls=%fused_computation.17 | convolution fusion | flops 268451840 | bytes 5373952 | tf_op jit(solution)/shard_map/dot_general | solution.py:27
  66.3 0.6 copy.12
  (53 shorter events, 0.4 us)
Async XLA Ops:
  0.6 12.1 %collective-permute-start = (bf16[8,8192]{1,0:T(8,128)(2,1)}, bf16[8,8192]{1,0:T(8,128)(2,1)S(1)}, u32[]{:S(2)}, u32[]{:S(2)}) collective-permute-start(bf16[8,8192]{1,0:T(8,128)(2,1)} %bitcast.48), channel_id=1, source_target_pairs={{0,2},{1,3},{2,0},{3,1},{4,6},{5,7},{6,4},{7,5},{8,10},{9,11},{10,... | collective-permute-start | bytes 393224 | tf_op jit(solution)/shard_map/ppermute | solution.py:17
  1.9 10.9 %collective-permute-start.1 = (bf16[8,8192]{1,0:T(8,128)(2,1)}, bf16[8,8192]{1,0:T(8,128)(2,1)S(1)}, u32[]{:S(2)}, u32[]{:S(2)}) collective-permute-start(bf16[8,8192]{1,0:T(8,128)(2,1)} %bitcast.49), channel_id=1, source_target_pairs={{0,4},{1,5},{2,6},{3,7},{4,0},{5,1},{6,2},{7,3},{8,12},{9,13},{10,... | collective-permute-start | bytes 393224 | tf_op jit(solution)/shard_map/ppermute | solution.py:17
  3.1 10.2 %collective-permute-start.2 = (bf16[8,8192]{1,0:T(8,128)(2,1)}, bf16[8,8192]{1,0:T(8,128)(2,1)S(1)}, u32[]{:S(2)}, u32[]{:S(2)}) collective-permute-start(bf16[8,8192]{1,0:T(8,128)(2,1)} %bitcast.50), channel_id=1, source_target_pairs={{0,6},{1,7},{2,4},{3,5},{4,2},{5,3},{6,0},{7,1},{8,14},{9,15},{10,... | collective-permute-start | bytes 393224 | tf_op jit(solution)/shard_map/ppermute | solution.py:17
  3.3 10.2 %collective-permute-start.3 = (bf16[8,8192]{1,0:T(8,128)(2,1)}, bf16[8,8192]{1,0:T(8,128)(2,1)S(1)}, u32[]{:S(2)}, u32[]{:S(2)}) collective-permute-start(bf16[8,8192]{1,0:T(8,128)(2,1)} %bitcast.51), channel_id=1, source_target_pairs={{0,1},{1,0},{2,3},{3,2},{4,5},{5,4},{6,7},{7,6},{8,9},{9,8},{10,11... | collective-permute-start | bytes 393224 | tf_op jit(solution)/shard_map/ppermute | solution.py:17
  12.7 4.2 %copy-start = (bf16[1,2,256,8192]{3,2,1,0:T(8,128)(2,1)}, bf16[1,2,256,8192]{3,2,1,0:T(8,128)(2,1)S(1)}, u32[]{:S(2)}) copy-start(bf16[1,2,256,8192]{3,2,1,0:T(8,128)(2,1)S(1)} %get-tuple-element.5) | copy-start | bytes 25165828
  12.7 1.4 %collective-permute-start.4 = (bf16[8,8192]{1,0:T(8,128)(2,1)S(1)}, bf16[8,8192]{1,0:T(8,128)(2,1)S(1)}, u32[]{:S(2)}, u32[]{:S(2)}) collective-permute-start(bf16[8,8192]{1,0:T(8,128)(2,1)S(1)} %collective-permute-done), channel_id=1, source_target_pairs={{0,1},{1,0},{2,3},{3,2},{4,5},{5,4},{6,7},{7,6},{8,9},{9,8},{10,11... | collective-permute-start | bytes 393224 | tf_op jit(solution)/shard_map/ppermute | solution.py:17
  12.8 1.5 %collective-permute-start.5 = (bf16[8,8192]{1,0:T(8,128)(2,1)S(1)}, bf16[8,8192]{1,0:T(8,128)(2,1)S(1)}, u32[]{:S(2)}, u32[]{:S(2)}) collective-permute-start(bf16[8,8192]{1,0:T(8,128)(2,1)S(1)} %collective-permute-done.1), channel_id=1, source_target_pairs={{0,1},{1,0},{2,3},{3,2},{4,5},{5,4},{6,7},{7,6},{8,9},{9,8},{10,11... | collective-permute-start | bytes 393224 | tf_op jit(solution)/shard_map/ppermute | solution.py:17
  13.4 1.4 %collective-permute-start.6 = (bf16[8,8192]{1,0:T(8,128)(2,1)S(1)}, bf16[8,8192]{1,0:T(8,128)(2,1)S(1)}, u32[]{:S(2)}, u32[]{:S(2)}) collective-permute-start(bf16[8,8192]{1,0:T(8,128)(2,1)S(1)} %collective-permute-done.2), channel_id=1, source_target_pairs={{0,1},{1,0},{2,3},{3,2},{4,5},{5,4},{6,7},{7,6},{8,9},{9,8},{10,11... | collective-permute-start | bytes 393224 | tf_op jit(solution)/shard_map/ppermute | solution.py:17
  16.7 2.0 %collective-permute-start.11 = (bf16[32,8192]{1,0:T(8,128)(2,1)S(1)}, bf16[32,8192]{1,0:T(8,128)(2,1)S(1)}, u32[]{:S(2)}, u32[]{:S(2)}) collective-permute-start(bf16[32,8192]{1,0:T(8,128)(2,1)S(1)} %slice.116), channel_id=1, source_target_pairs={{0,1},{1,0},{2,3},{3,2},{4,5},{5,4},{6,7},{7,6},{8,9},{9,8},{10,11... | collective-permute-start | bytes 1572872 | tf_op jit(solution)/shard_map/ppermute | solution.py:17
  17.8 17.3 %copy-start.1 = (bf16[1,8,8192]{2,1,0:T(8,128)(2,1)S(1)}, bf16[1,8,8192]{2,1,0:T(8,128)(2,1)}, u32[]{:S(2)}) copy-start(bf16[1,8,8192]{2,1,0:T(8,128)(2,1)} %param.12) | copy-start | bytes 393220
  17.8 3.7 %collective-permute-start.7 = (bf16[32,8192]{1,0:T(8,128)(2,1)S(1)}, bf16[32,8192]{1,0:T(8,128)(2,1)S(1)}, u32[]{:S(2)}, u32[]{:S(2)}) collective-permute-start(bf16[32,8192]{1,0:T(8,128)(2,1)S(1)} %slice.117), channel_id=1, source_target_pairs={{0,1},{1,0},{2,3},{3,2},{4,5},{5,4},{6,7},{7,6},{8,9},{9,8},{10,11... | collective-permute-start | bytes 1572872 | tf_op jit(solution)/shard_map/ppermute | solution.py:17
  18.8 5.9 %collective-permute-start.14 = (bf16[8,8192]{1,0:T(8,128)(2,1)S(1)}, bf16[8,8192]{1,0:T(8,128)(2,1)S(1)}, u32[]{:S(2)}, u32[]{:S(2)}) collective-permute-start(bf16[8,8192]{1,0:T(8,128)(2,1)S(1)} %get-tuple-element.16), channel_id=1, source_target_pairs={{0,6},{1,7},{2,4},{3,5},{4,2},{5,3},{6,0},{7,1},{8,14},{9,15},{10,... | collective-permute-start | bytes 393224 | tf_op jit(solution)/shard_map/ppermute | solution.py:17
  21.1 7.7 %collective-permute-start.13 = (bf16[8,8192]{1,0:T(8,128)(2,1)S(1)}, bf16[8,8192]{1,0:T(8,128)(2,1)S(1)}, u32[]{:S(2)}, u32[]{:S(2)}) collective-permute-start(bf16[8,8192]{1,0:T(8,128)(2,1)S(1)} %get-tuple-element.17), channel_id=1, source_target_pairs={{0,4},{1,5},{2,6},{3,7},{4,0},{5,1},{6,2},{7,3},{8,12},{9,13},{10,... | collective-permute-start | bytes 393224 | tf_op jit(solution)/shard_map/ppermute | solution.py:17
  21.3 7.5 %collective-permute-start.12 = (bf16[8,8192]{1,0:T(8,128)(2,1)S(1)}, bf16[8,8192]{1,0:T(8,128)(2,1)S(1)}, u32[]{:S(2)}, u32[]{:S(2)}) collective-permute-start(bf16[8,8192]{1,0:T(8,128)(2,1)S(1)} %get-tuple-element.15), channel_id=1, source_target_pairs={{0,2},{1,3},{2,0},{3,1},{4,6},{5,7},{6,4},{7,5},{8,10},{9,11},{10,... | collective-permute-start | bytes 393224 | tf_op jit(solution)/shard_map/ppermute | solution.py:17
  21.7 10.4 %collective-permute-start.10 = (bf16[8,8192]{1,0:T(8,128)(2,1)S(1)}, bf16[8,8192]{1,0:T(8,128)(2,1)S(1)}, u32[]{:S(2)}, u32[]{:S(2)}) collective-permute-start(bf16[8,8192]{1,0:T(8,128)(2,1)S(1)} %get-tuple-element.13), channel_id=1, source_target_pairs={{0,6},{1,7},{2,4},{3,5},{4,2},{5,3},{6,0},{7,1},{8,14},{9,15},{10,... | collective-permute-start | bytes 393224 | tf_op jit(solution)/shard_map/ppermute | solution.py:17
  23.9 9.7 %collective-permute-start.9 = (bf16[8,8192]{1,0:T(8,128)(2,1)S(1)}, bf16[8,8192]{1,0:T(8,128)(2,1)S(1)}, u32[]{:S(2)}, u32[]{:S(2)}) collective-permute-start(bf16[8,8192]{1,0:T(8,128)(2,1)S(1)} %get-tuple-element.14), channel_id=1, source_target_pairs={{0,4},{1,5},{2,6},{3,7},{4,0},{5,1},{6,2},{7,3},{8,12},{9,13},{10,... | collective-permute-start | bytes 393224 | tf_op jit(solution)/shard_map/ppermute | solution.py:17
  24.8 8.9 %collective-permute-start.8 = (bf16[8,8192]{1,0:T(8,128)(2,1)S(1)}, bf16[8,8192]{1,0:T(8,128)(2,1)S(1)}, u32[]{:S(2)}, u32[]{:S(2)}) collective-permute-start(bf16[8,8192]{1,0:T(8,128)(2,1)S(1)} %get-tuple-element.12), channel_id=1, source_target_pairs={{0,2},{1,3},{2,0},{3,1},{4,6},{5,7},{6,4},{7,5},{8,10},{9,11},{10,... | collective-permute-start | bytes 393224 | tf_op jit(solution)/shard_map/ppermute | solution.py:17
  28.9 6.3 %collective-permute-start.15 = (bf16[8,8192]{1,0:T(8,128)(2,1)S(1)}, bf16[8,8192]{1,0:T(8,128)(2,1)S(1)}, u32[]{:S(2)}, u32[]{:S(2)}) collective-permute-start(bf16[8,8192]{1,0:T(8,128)(2,1)S(1)} %fusion.31), channel_id=1, source_target_pairs={{0,8},{1,9},{2,10},{3,11},{4,12},{5,13},{6,14},{7,15},{8,16},{9,17... | collective-permute-start | bytes 393224 | tf_op jit(solution)/shard_map/ppermute | solution.py:23
  35.2 26.4 %copy-start.2 = (bf16[8,8192]{1,0:T(8,128)(2,1)}, bf16[8,8192]{1,0:T(8,128)(2,1)S(1)}, u32[]{:S(2)}) copy-start(bf16[8,8192]{1,0:T(8,128)(2,1)S(1)} %get-tuple-element.7) | copy-start | bytes 393220
  35.2 7.5 %collective-permute-start.23 = (bf16[8,8192]{1,0:T(8,128)(2,1)S(1)}, bf16[8,8192]{1,0:T(8,128)(2,1)S(1)}, u32[]{:S(2)}, u32[]{:S(2)}) collective-permute-start(bf16[8,8192]{1,0:T(8,128)(2,1)S(1)} %get-tuple-element.7), channel_id=1, source_target_pairs={{8,0},{9,1},{10,2},{11,3},{12,4},{13,5},{14,6},{15,7},{16,8},{17,9... | collective-permute-start | bytes 393224 | tf_op jit(solution)/shard_map/ppermute | solution.py:23
  37.3 6.3 %collective-permute-start.16 = (bf16[8,8192]{1,0:T(8,128)(2,1)S(1)}, bf16[8,8192]{1,0:T(8,128)(2,1)S(1)}, u32[]{:S(2)}, u32[]{:S(2)}) collective-permute-start(bf16[8,8192]{1,0:T(8,128)(2,1)S(1)} %get-tuple-element.7), channel_id=1, source_target_pairs={{0,2},{1,3},{2,0},{3,1},{4,6},{5,7},{6,4},{7,5},{8,10},{9,11},{10,... | collective-permute-start | bytes 393224 | tf_op jit(solution)/shard_map/ppermute | solution.py:17
  38.2 7.1 %collective-permute-start.17 = (bf16[8,8192]{1,0:T(8,128)(2,1)S(1)}, bf16[8,8192]{1,0:T(8,128)(2,1)S(1)}, u32[]{:S(2)}, u32[]{:S(2)}) collective-permute-start(bf16[8,8192]{1,0:T(8,128)(2,1)S(1)} %get-tuple-element.7), channel_id=1, source_target_pairs={{0,4},{1,5},{2,6},{3,7},{4,0},{5,1},{6,2},{7,3},{8,12},{9,13},{10,... | collective-permute-start | bytes 393224 | tf_op jit(solution)/shard_map/ppermute | solution.py:17
  38.3 7.2 %collective-permute-start.18 = (bf16[8,8192]{1,0:T(8,128)(2,1)S(1)}, bf16[8,8192]{1,0:T(8,128)(2,1)S(1)}, u32[]{:S(2)}, u32[]{:S(2)}) collective-permute-start(bf16[8,8192]{1,0:T(8,128)(2,1)S(1)} %get-tuple-element.7), channel_id=1, source_target_pairs={{0,6},{1,7},{2,4},{3,5},{4,2},{5,3},{6,0},{7,1},{8,14},{9,15},{10,... | collective-permute-start | bytes 393224 | tf_op jit(solution)/shard_map/ppermute | solution.py:17
  40.1 8.6 %collective-permute-start.19 = (bf16[8,8192]{1,0:T(8,128)(2,1)S(1)}, bf16[8,8192]{1,0:T(8,128)(2,1)S(1)}, u32[]{:S(2)}, u32[]{:S(2)}) collective-permute-start(bf16[8,8192]{1,0:T(8,128)(2,1)S(1)} %get-tuple-element.7), channel_id=1, source_target_pairs={{0,1},{1,0},{2,3},{3,2},{4,5},{5,4},{6,7},{7,6},{8,9},{9,8},{10,11... | collective-permute-start | bytes 393224 | tf_op jit(solution)/shard_map/ppermute | solution.py:17
  42.7 7.9 %collective-permute-start.24 = (bf16[8,8192]{1,0:T(8,128)(2,1)S(1)}, bf16[8,8192]{1,0:T(8,128)(2,1)S(1)}, u32[]{:S(2)}, u32[]{:S(2)}) collective-permute-start(bf16[8,8192]{1,0:T(8,128)(2,1)S(1)} %collective-permute-done.23), channel_id=1, source_target_pairs={{0,2},{1,3},{2,0},{3,1},{4,6},{5,7},{6,4},{7,5},{8,10},{9,11},{10,... | collective-permute-start | bytes 393224 | tf_op jit(solution)/shard_map/ppermute | solution.py:17
  43.7 5.4 %collective-permute-start.20 = (bf16[8,8192]{1,0:T(8,128)(2,1)S(1)}, bf16[8,8192]{1,0:T(8,128)(2,1)S(1)}, u32[]{:S(2)}, u32[]{:S(2)}) collective-permute-start(bf16[8,8192]{1,0:T(8,128)(2,1)S(1)} %collective-permute-done.16), channel_id=1, source_target_pairs={{0,1},{1,0},{2,3},{3,2},{4,5},{5,4},{6,7},{7,6},{8,9},{9,8},{10,11... | collective-permute-start | bytes 393224 | tf_op jit(solution)/shard_map/ppermute | solution.py:17
  45.3 4.6 %collective-permute-start.21 = (bf16[8,8192]{1,0:T(8,128)(2,1)S(1)}, bf16[8,8192]{1,0:T(8,128)(2,1)S(1)}, u32[]{:S(2)}, u32[]{:S(2)}) collective-permute-start(bf16[8,8192]{1,0:T(8,128)(2,1)S(1)} %collective-permute-done.17), channel_id=1, source_target_pairs={{0,1},{1,0},{2,3},{3,2},{4,5},{5,4},{6,7},{7,6},{8,9},{9,8},{10,11... | collective-permute-start | bytes 393224 | tf_op jit(solution)/shard_map/ppermute | solution.py:17
  45.6 5.0 %collective-permute-start.22 = (bf16[8,8192]{1,0:T(8,128)(2,1)S(1)}, bf16[8,8192]{1,0:T(8,128)(2,1)S(1)}, u32[]{:S(2)}, u32[]{:S(2)}) collective-permute-start(bf16[8,8192]{1,0:T(8,128)(2,1)S(1)} %collective-permute-done.18), channel_id=1, source_target_pairs={{0,1},{1,0},{2,3},{3,2},{4,5},{5,4},{6,7},{7,6},{8,9},{9,8},{10,11... | collective-permute-start | bytes 393224 | tf_op jit(solution)/shard_map/ppermute | solution.py:17
  48.7 8.0 %collective-permute-start.25 = (bf16[8,8192]{1,0:T(8,128)(2,1)S(1)}, bf16[8,8192]{1,0:T(8,128)(2,1)S(1)}, u32[]{:S(2)}, u32[]{:S(2)}) collective-permute-start(bf16[8,8192]{1,0:T(8,128)(2,1)S(1)} %collective-permute-done.23), channel_id=1, source_target_pairs={{0,4},{1,5},{2,6},{3,7},{4,0},{5,1},{6,2},{7,3},{8,12},{9,13},{10,... | collective-permute-start | bytes 393224 | tf_op jit(solution)/shard_map/ppermute | solution.py:17
  49.1 12.1 %collective-permute-start.26 = (bf16[8,8192]{1,0:T(8,128)(2,1)S(1)}, bf16[8,8192]{1,0:T(8,128)(2,1)S(1)}, u32[]{:S(2)}, u32[]{:S(2)}) collective-permute-start(bf16[8,8192]{1,0:T(8,128)(2,1)S(1)} %collective-permute-done.23), channel_id=1, source_target_pairs={{0,6},{1,7},{2,4},{3,5},{4,2},{5,3},{6,0},{7,1},{8,14},{9,15},{10,... | collective-permute-start | bytes 393224 | tf_op jit(solution)/shard_map/ppermute | solution.py:17
  49.9 11.7 %collective-permute-start.27 = (bf16[8,8192]{1,0:T(8,128)(2,1)S(1)}, bf16[8,8192]{1,0:T(8,128)(2,1)S(1)}, u32[]{:S(2)}, u32[]{:S(2)}) collective-permute-start(bf16[8,8192]{1,0:T(8,128)(2,1)S(1)} %collective-permute-done.23), channel_id=1, source_target_pairs={{0,1},{1,0},{2,3},{3,2},{4,5},{5,4},{6,7},{7,6},{8,9},{9,8},{10,11... | collective-permute-start | bytes 393224 | tf_op jit(solution)/shard_map/ppermute | solution.py:17
  60.3 1.8 %collective-permute-start.28 = (bf16[8,8192]{1,0:T(8,128)(2,1)S(1)}, bf16[8,8192]{1,0:T(8,128)(2,1)S(1)}, u32[]{:S(2)}, u32[]{:S(2)}) collective-permute-start(bf16[8,8192]{1,0:T(8,128)(2,1)S(1)} %collective-permute-done.24), channel_id=1, source_target_pairs={{0,1},{1,0},{2,3},{3,2},{4,5},{5,4},{6,7},{7,6},{8,9},{9,8},{10,11... | collective-permute-start | bytes 393224 | tf_op jit(solution)/shard_map/ppermute | solution.py:17
  61.1 1.3 %collective-permute-start.29 = (bf16[8,8192]{1,0:T(8,128)(2,1)S(1)}, bf16[8,8192]{1,0:T(8,128)(2,1)S(1)}, u32[]{:S(2)}, u32[]{:S(2)}) collective-permute-start(bf16[8,8192]{1,0:T(8,128)(2,1)S(1)} %collective-permute-done.25), channel_id=1, source_target_pairs={{0,1},{1,0},{2,3},{3,2},{4,5},{5,4},{6,7},{7,6},{8,9},{9,8},{10,11... | collective-permute-start | bytes 393224 | tf_op jit(solution)/shard_map/ppermute | solution.py:17
  61.2 1.5 %collective-permute-start.30 = (bf16[8,8192]{1,0:T(8,128)(2,1)S(1)}, bf16[8,8192]{1,0:T(8,128)(2,1)S(1)}, u32[]{:S(2)}, u32[]{:S(2)}) collective-permute-start(bf16[8,8192]{1,0:T(8,128)(2,1)S(1)} %collective-permute-done.26), channel_id=1, source_target_pairs={{0,1},{1,0},{2,3},{3,2},{4,5},{5,4},{6,7},{7,6},{8,9},{9,8},{10,11... | collective-permute-start | bytes 393224 | tf_op jit(solution)/shard_map/ppermute | solution.py:17

commit v4 on v3

v4 whole, which is shorter than its diff:
```python
import functools

import jax
import jax.numpy as jnp
from jax import lax
from jax.experimental import pallas as pl
from jax.experimental.pallas import tpu as pltpu
from jax.sharding import PartitionSpec as P

BLOCK = 128
LAYERS = 4
TILE = 32
CORES = 2
AXIS = "layer"
CHUNK = 1024
LIMIT = 4 << 20


def swap(value, mask):
    pairs = [(source, source ^ mask) for source in range(lax.axis_size(AXIS))]
    return lax.ppermute(value, AXIS, pairs)


def shifted(block, distance):
    devices = range(lax.axis_size(AXIS))
    route = [(i - distance, i) for i in devices if i - distance in devices]
    return lax.ppermute(block, AXIS, route)


def in_vmem(*arrays):
    return [pltpu.with_memory_space_constraint(a, pltpu.VMEM) for a in arrays]


VMEM_SPEC = pl.BlockSpec(memory_space=pltpu.VMEM)
SMEM_SPEC = pl.BlockSpec(memory_space=pltpu.SMEM)


def gathered(slab, chips):
    near = [slab] + [swap(slab, CORES * chip) for chip in range(1, chips)]
    far = [swap(piece, 1) for piece in near]
    return jnp.concatenate(near + far, axis=0)


def scattered(near, far, chips):
    rows = near.shape[0] // chips
    total = near + swap(far, 1).astype(jnp.float32)
    sends = [total[chip * rows : (chip + 1) * rows].astype(jnp.bfloat16) for chip in range(1, chips)]
    came = [swap(sends[chip - 1], CORES * chip) for chip in range(1, chips)]
    out = total[:rows]
    for block in came:
        out = out + block.astype(jnp.float32)
    return out


def load_kernel(*refs):
    count = len(refs) // 2
    sources, held, sems = refs[:count], refs[count : 2 * count], refs[-1]
    copies = [
        pltpu.make_async_copy(source, target, sems.at[i])
        for i, (source, target) in enumerate(zip(sources, held))
    ]
    for copy in copies:
        copy.start()
    for copy in copies:
        copy.wait()


def loaded(*weights):
    size = sum(w.size * w.dtype.itemsize for w in weights)
    return pl.pallas_call(
        load_kernel,
        out_shape=[pltpu.VMEM(w.shape, w.dtype) for w in weights],
        in_specs=[pl.BlockSpec(memory_space=pl.ANY)] * len(weights),
        out_specs=[pl.BlockSpec(memory_space=pltpu.VMEM)] * len(weights),
        scratch_shapes=[pltpu.SemaphoreType.DMA((len(weights),))],
        compiler_params=pltpu.CompilerParams(vmem_limit_bytes=1 << 20),
        cost_estimate=pl.CostEstimate(flops=0, bytes_accessed=2 * size, transcendentals=0),
        name="load_weights",
    )(*[pltpu.with_memory_space_constraint(w, pltpu.HBM) for w in weights])


def decode(codes, dec_ref, reach, near_ref, far_ref):
    half, width = near_ref.shape

    @pl.loop(0, width // CHUNK)
    def _(step):
        columns = pl.ds(pl.multiple_of(step * CHUNK, CHUNK), CHUNK)
        part = jnp.dot(codes, dec_ref[0, reach, :, columns], preferred_element_type=jnp.float32)
        near_ref[:, columns] = part[:half]
        far_ref[:, columns] = part[half:].astype(jnp.bfloat16)


def encode_kernel(tokens, place_ref, active_ref, x_ref, enc_ref, bias_ref, dec_ref, codes_ref, near_ref, far_ref, held):
    rows, depth = x_ref.shape
    group = rows // tokens
    chips = group // CORES

    def step(i, total):
        part = pl.ds(pl.multiple_of(i * CHUNK, CHUNK), CHUNK)
        return total + jnp.dot(x_ref[:, part], enc_ref[0, part, :], preferred_element_type=jnp.float32)

    pre = lax.fori_loop(0, depth // CHUNK, step, jnp.zeros((rows, enc_ref.shape[2]), jnp.float32))
    held[...] = jnp.maximum(pre + bias_ref[...].astype(jnp.float32), 0.0)
    for block in range(group):
        core, chip = block // chips, block % chips
        tile = ((place_ref[0] ^ (CORES * chip + core)) * tokens) // TILE
        for part in range(active_ref.shape[1]):
            where = (pl.ds(block * tokens, tokens), pl.ds(part * BLOCK, BLOCK))
            held[where] = held[where] * active_ref[tile, part].astype(jnp.float32)
    codes_ref[...] = held[...].astype(jnp.bfloat16)
    decode(codes_ref[...], dec_ref, 1, near_ref, far_ref)


def decode_kernel(codes_ref, dec_ref, near_ref, far_ref):
    decode(codes_ref[...], dec_ref, 0, near_ref, far_ref)


def halves_of(rows, width):
    return [pltpu.VMEM((rows // CORES, width), jnp.float32), pltpu.VMEM((rows // CORES, width), jnp.bfloat16)]


def encoded(place, active, x, enc, bias, dec, tokens):
    rows, depth = x.shape
    features = enc.shape[2]
    return pl.pallas_call(
        functools.partial(encode_kernel, tokens),
        out_shape=[pltpu.VMEM((rows, features), jnp.bfloat16)] + halves_of(rows, depth),
        in_specs=[SMEM_SPEC, SMEM_SPEC] + [VMEM_SPEC] * 4,
        out_specs=[VMEM_SPEC] * 3,
        scratch_shapes=[pltpu.VMEM((rows, features), jnp.float32)],
        compiler_params=pltpu.CompilerParams(vmem_limit_bytes=LIMIT),
        cost_estimate=pl.CostEstimate(flops=4 * rows * depth * features, bytes_accessed=4 * depth * features, transcendentals=0),
        name="encode",
    )(place, active, *in_vmem(x, enc, bias, dec))


def decoded(codes, dec):
    rows, features = codes.shape
    width = dec.shape[3]
    return pl.pallas_call(
        decode_kernel,
        out_shape=halves_of(rows, width),
        in_specs=[VMEM_SPEC] * 2,
        out_specs=[VMEM_SPEC] * 2,
        compiler_params=pltpu.CompilerParams(vmem_limit_bytes=LIMIT),
        cost_estimate=pl.CostEstimate(flops=2 * rows * width * features, bytes_accessed=2 * width * features, transcendentals=0),
        name="decode_own",
    )(*in_vmem(codes, dec))


def back(rows_ref, dec_ref, reach, total):
    def step(i, total):
        part = pl.ds(pl.multiple_of(i * CHUNK, CHUNK), CHUNK)
        return total + lax.dot_general(
            rows_ref[:, part], dec_ref[0, reach, :, part], (((1,), (1,)), ((), ())), preferred_element_type=jnp.float32
        )

    return lax.fori_loop(0, rows_ref.shape[1] // CHUNK, step, total)


def grad_own_kernel(rows_ref, dec_ref, out_ref):
    out_ref[...] = back(rows_ref, dec_ref, 0, jnp.zeros(out_ref.shape, jnp.float32))


def grad_kernel(tokens, place_ref, rows_ref, dec_ref, own_ref, out_ref):
    total = back(rows_ref, dec_ref, 1, own_ref[...])
    group = rows_ref.shape[0] // tokens
    chips = group // CORES
    for block in range(group):
        slab = place_ref[0] ^ (CORES * (block % chips) + block // chips)
        out_ref[0, pl.ds(pl.multiple_of(slab * tokens, tokens), tokens), :] = total[block * tokens : (block + 1) * tokens]


def grad_own(rows, dec):
    shape = (rows.shape[0], dec.shape[2])
    return pl.pallas_call(
        grad_own_kernel,
        out_shape=pltpu.VMEM(shape, jnp.float32),
        in_specs=[VMEM_SPEC] * 2,
        out_specs=VMEM_SPEC,
        compiler_params=pltpu.CompilerParams(vmem_limit_bytes=LIMIT),
        cost_estimate=pl.CostEstimate(flops=2 * rows.size * shape[1], bytes_accessed=dec.size, transcendentals=0),
        name="grad_own",
    )(*in_vmem(rows, dec))


def grad_all(place, rows, dec, own, tokens):
    return pl.pallas_call(
        functools.partial(grad_kernel, tokens),
        out_shape=jax.ShapeDtypeStruct((1,) + own.shape, jnp.float32),
        in_specs=[SMEM_SPEC] + [VMEM_SPEC] * 3,
        out_specs=VMEM_SPEC,
        compiler_params=pltpu.CompilerParams(vmem_limit_bytes=LIMIT),
        cost_estimate=pl.CostEstimate(flops=2 * rows.size * own.shape[1], bytes_accessed=dec.size, transcendentals=0),
        name="grad_all",
    )(place, *in_vmem(rows, dec, own))


def on_device(resid, enc_weight, enc_bias, active, dec_weight, target):
    group = lax.axis_size(AXIS) // LAYERS
    chips = group // CORES
    place = (lax.axis_index(AXIS) % group).astype(jnp.int32).reshape(1)
    tokens = resid.shape[1]
    enc, dec = loaded(enc_weight, dec_weight)
    x = gathered(resid[0], chips)
    codes, next_near, next_far = encoded(place, active[0], x, enc, enc_bias, dec, tokens)
    own_near, own_far = decoded(codes, dec)
    next_sum = scattered(next_near, next_far, chips).astype(jnp.bfloat16)
    from_before = shifted(next_sum, group).astype(jnp.float32)
    own_sum = scattered(own_near, own_far, chips)
    error = (own_sum + from_before - target[0].astype(jnp.float32)).astype(jnp.bfloat16)

    later = shifted(error, -group)
    here = [error] + [swap(error, CORES * chip) for chip in range(1, chips)]
    after = [later] + [swap(later, CORES * chip) for chip in range(1, chips - 1)]
    last = shifted(here[-1], -group)
    here_near = jnp.concatenate(here, axis=0)
    here_rows = jnp.concatenate([here_near, swap(here_near, 1)], axis=0)
    after_most = jnp.concatenate(after, axis=0)
    after_rows = jnp.concatenate([after_most, last, swap(after_most, 1), swap(last, 1)], axis=0)
    grad = grad_all(place, after_rows, dec, grad_own(here_rows, dec), tokens)
    return (error[None], grad)


def solution(mesh):
    return jax.shard_map(
        on_device,
        mesh=mesh,
        in_specs=(
            P("layer", "groups", None),
            P("layer", None, None),
            P("layer", None),
            P("layer", "groups", None),
            P("layer", None, None, None),
            P("layer", "groups", None),
        ),
        out_specs=(P("layer", "groups", None), P("layer", "groups", None)),
        check_vma=False,
    )
```

time: 67.2 us -> 62.6 us (0.932)
  the two profiles are of different devices: /device:TPU:17 before, /device:TPU:0 now
where the time goes in v4:
time: 62.6 us; the launch traced here: 61.9 us
  starting transfers between devices  25.7 us (41%)
  waiting for transfers between devices  18.1 us (29%)
  Pallas kernels  15.5 us (25%)
  local copies, waits for them, and re-layouts  1.24 us (2%)
  between operations  1 us (2%)
    ppermute x23, starting transfers between devices, swap(): return lax.ppermute(value, AXIS, pairs)  19.6 us
    ppermute x23, waiting for transfers between devices, swap(): return lax.ppermute(value, AXIS, pairs)  14.9 us
    ppermute x3, starting transfers between devices, shifted(): return lax.ppermute(block, AXIS, route)  6.07 us
    pallas_call x1, Pallas kernels, loaded(): pl.pallas_call(load_kernel, out_shape=[pltpu.VMEM(w.shape, w.dtype) for w...  4.68 us
    pallas_call x1, Pallas kernels, encoded(): pl.pallas_call(functools.partial(encode_kernel, tokens), out_shape=[pltpu...  4 us
    ppermute x3, waiting for transfers between devices, shifted(): return lax.ppermute(block, AXIS, route)  3.21 us
    pallas_call x1, Pallas kernels, grad_all(): pl.pallas_call(functools.partial(grad_kernel, tokens), out_shape=jax.Shap...  2.87 us
    pallas_call x1, Pallas kernels, grad_own(): pl.pallas_call(grad_own_kernel, out_shape=pltpu.VMEM(shape, jnp.float32),...  2.23 us
  transfers between devices with their start and end apart: 26, of which 14 were waited for; matrix products, arithmetic and copies ran while one was open for 3% of the time, Pallas kernels for 14%

profile of v4, /device:TPU:0, one launch (start us, length us, event | category | flops | bytes accessed | tf_op | source)
XLA Modules:
  0.0 61.9 jit_solution(13516733287867158231)
XLA Ops:
  0.6 0.0 copy-start
  0.6 0.5 collective-permute-start.3
  1.2 3.5 %collective-permute-start.2 = (bf16[8,8192]{1,0:T(8,128)(2,1)}, bf16[8,8192]{1,0:T(8,128)(2,1)S(1)}, u32[]{:S(2)}, u32[]{:S(2)}) collective-permute-start(bf16[8,8192]{1,0:T(8,128)(2,1)} %bitcast.12), channel_id=1, source_target_pairs={{0,6},{1,7},{2,4},{3,5},{4,2},{5,3},{6,0},{7,1},{8,14},{9,15},{10,... | collective-permute-start | bytes 393224 | tf_op jit(solution)/shard_map/ppermute | solution.py:21
  4.7 0.5 collective-permute-start.1
  5.2 0.1 collective-permute-start
  5.3 0.9 %constant_dynamic-update-slice_fusion.7 = bf16[64,8192]{1,0:T(8,128)(2,1)S(1)} fusion(bf16[1,8,8192]{2,1,0:T(8,128)(2,1)} %param.6), kind=kLoop, calls=%fused_computation.21 | loop fusion | bytes 262144
  6.3 4.7 %load_weights.1 = (bf16[1,8192,256]{2,1,0:T(8,128)(2,1)S(1)}, bf16[1,2,256,8192]{3,2,1,0:T(8,128)(2,1)S(1)}) custom-call(bf16[1,8192,256]{2,1,0:T(8,128)(2,1)} %refs_0_.1, bf16[1,2,256,8192]{3,2,1,0:T(8,128)(2,1)} %refs_1_.1), custom_call_target="tpu_custom_call" | custom-call | bytes 25165824 | tf_op jit(solution)/shard_map/load_weights/pallas_call | solution.py:70
  11.0 0.0 collective-permute-done.2
  11.0 0.1 collective-permute-start.6
  11.1 0.7 %collective-permute-done.1 = bf16[8,8192]{1,0:T(8,128)(2,1)S(1)} collective-permute-done((bf16[8,8192]{1,0:T(8,128)(2,1)}, bf16[8,8192]{1,0:T(8,128)(2,1)S(1)}, u32[]{:S(2)}, u32[]{:S(2)}) %collective-permute-start.1) | collective-permute-done | bytes 131104 | tf_op jit(solution)/shard_map/ppermute | solution.py:21
  11.8 0.0 collective-permute-start.5
  11.8 0.3 collective-permute-done
  12.1 0.2 collective-permute-start.4
  12.4 0.0 collective-permute-done.3
  12.4 1.1 %collective-permute-done.4 = bf16[8,8192]{1,0:T(8,128)(2,1)S(1)} collective-permute-done((bf16[8,8192]{1,0:T(8,128)(2,1)S(1)}, bf16[8,8192]{1,0:T(8,128)(2,1)S(1)}, u32[]{:S(2)}, u32[]{:S(2)}) %collective-permute-start.4) | collective-permute-done | bytes 131104 | tf_op jit(solution)/shard_map/ppermute | solution.py:21
  13.5 0.0 collective-permute-done.5
  13.5 0.0 collective-permute-done.6
  13.5 4.0 %encode.1 = (bf16[64,256]{1,0:T(8,128)(2,1)S(1)}, f32[32,8192]{1,0:T(8,128)S(1)}, bf16[32,8192]{1,0:T(8,128)(2,1)S(1)}) custom-call(s32[1]{0:T(128)} %bitcast.place_ref, s32[2,2]{1,0:T(2,128)S(1)} %bitcast.9, bf16[64,8192]{1,0:T(8,128)(2,1)S(1)} %constant_dynamic-update-slice_fusion.x_ref, bf16[1,8192,256]{2,1,0:T(8,128)(2,1)S(1)} %get-tuple-element.9.enc_ref, ...), custom_call_target="tpu_custom_call" | custom-call | flops 536870912 | bytes 8388608 | tf_op jit(solution)/shard_map/encode/pallas_call | solution.py:125
  17.6 0.3 collective-permute-start.11
  17.8 1.7 %decode_own.1 = (f32[32,8192]{1,0:T(8,128)S(1)}, bf16[32,8192]{1,0:T(8,128)(2,1)S(1)}) custom-call(bf16[64,256]{1,0:T(8,128)(2,1)S(1)} %get-tuple-element.11.codes_ref, bf16[1,2,256,8192]{3,2,1,0:T(8,128)(2,1)S(1)} %get-tuple-element.10.dec_ref), custom_call_target="tpu_custom_call" | custom-call | flops 268435456 | bytes 4194304 | tf_op jit(solution)/shard_map/decode_own/pallas_call | solution.py:140
  19.5 0.4 collective-permute-start.7
  19.9 0.0 collective-permute-done.11
  19.9 0.1 fusion.10
  20.0 1.6 %collective-permute-start.12 = (bf16[8,8192]{1,0:T(8,128)(2,1)S(1)}, bf16[8,8192]{1,0:T(8,128)(2,1)S(1)}, u32[]{:S(2)}, u32[]{:S(2)}) collective-permute-start(bf16[8,8192]{1,0:T(8,128)(2,1)S(1)} %get-tuple-element.25), channel_id=1, source_target_pairs={{0,2},{1,3},{2,0},{3,1},{4,6},{5,7},{6,4},{7,5},{8,10},{9,11},{10,... | collective-permute-start | bytes 393224 | tf_op jit(solution)/shard_map/ppermute | solution.py:21
  21.7 1.5 %collective-permute-start.14 = (bf16[8,8192]{1,0:T(8,128)(2,1)S(1)}, bf16[8,8192]{1,0:T(8,128)(2,1)S(1)}, u32[]{:S(2)}, u32[]{:S(2)}) collective-permute-start(bf16[8,8192]{1,0:T(8,128)(2,1)S(1)} %get-tuple-element.26), channel_id=1, source_target_pairs={{0,6},{1,7},{2,4},{3,5},{4,2},{5,3},{6,0},{7,1},{8,14},{9,15},{10,... | collective-permute-start | bytes 393224 | tf_op jit(solution)/shard_map/ppermute | solution.py:21
  23.2 0.4 collective-permute-start.13
  23.6 0.0 collective-permute-done.7
  23.6 0.1 fusion.9
  23.8 1.6 %collective-permute-start.8 = (bf16[8,8192]{1,0:T(8,128)(2,1)S(1)}, bf16[8,8192]{1,0:T(8,128)(2,1)S(1)}, u32[]{:S(2)}, u32[]{:S(2)}) collective-permute-start(bf16[8,8192]{1,0:T(8,128)(2,1)S(1)} %get-tuple-element.22), channel_id=1, source_target_pairs={{0,2},{1,3},{2,0},{3,1},{4,6},{5,7},{6,4},{7,5},{8,10},{9,11},{10,... | collective-permute-start | bytes 393224 | tf_op jit(solution)/shard_map/ppermute | solution.py:21
  25.4 1.5 %collective-permute-start.10 = (bf16[8,8192]{1,0:T(8,128)(2,1)S(1)}, bf16[8,8192]{1,0:T(8,128)(2,1)S(1)}, u32[]{:S(2)}, u32[]{:S(2)}) collective-permute-start(bf16[8,8192]{1,0:T(8,128)(2,1)S(1)} %get-tuple-element.23), channel_id=1, source_target_pairs={{0,6},{1,7},{2,4},{3,5},{4,2},{5,3},{6,0},{7,1},{8,14},{9,15},{10,... | collective-permute-start | bytes 393224 | tf_op jit(solution)/shard_map/ppermute | solution.py:21
  26.9 0.0 collective-permute-done.12
  26.9 1.1 %collective-permute-start.9 = (bf16[8,8192]{1,0:T(8,128)(2,1)S(1)}, bf16[8,8192]{1,0:T(8,128)(2,1)S(1)}, u32[]{:S(2)}, u32[]{:S(2)}) collective-permute-start(bf16[8,8192]{1,0:T(8,128)(2,1)S(1)} %get-tuple-element.24), channel_id=1, source_target_pairs={{0,4},{1,5},{2,6},{3,7},{4,0},{5,1},{6,2},{7,3},{8,12},{9,13},{10,... | collective-permute-start | bytes 393224 | tf_op jit(solution)/shard_map/ppermute | solution.py:21
  28.0 2.3 %collective-permute-done.14 = bf16[8,8192]{1,0:T(8,128)(2,1)S(1)} collective-permute-done((bf16[8,8192]{1,0:T(8,128)(2,1)S(1)}, bf16[8,8192]{1,0:T(8,128)(2,1)S(1)}, u32[]{:S(2)}, u32[]{:S(2)}) %collective-permute-start.14) | collective-permute-done | bytes 131104 | tf_op jit(solution)/shard_map/ppermute | solution.py:21
  30.3 2.0 %collective-permute-done.13 = bf16[8,8192]{1,0:T(8,128)(2,1)S(1)} collective-permute-done((bf16[8,8192]{1,0:T(8,128)(2,1)S(1)}, bf16[8,8192]{1,0:T(8,128)(2,1)S(1)}, u32[]{:S(2)}, u32[]{:S(2)}) %collective-permute-start.13) | collective-permute-done | bytes 131104 | tf_op jit(solution)/shard_map/ppermute | solution.py:21
  32.4 0.1 fusion.2
  32.4 3.5 %collective-permute-start.15 = (bf16[8,8192]{1,0:T(8,128)(2,1)S(1)}, bf16[8,8192]{1,0:T(8,128)(2,1)S(1)}, u32[]{:S(2)}, u32[]{:S(2)}) collective-permute-start(bf16[8,8192]{1,0:T(8,128)(2,1)S(1)} %fusion.2), channel_id=1, source_target_pairs={{0,8},{1,9},{2,10},{3,11},{4,12},{5,13},{6,14},{7,15},{8,16},{9,17... | collective-permute-start | bytes 393224 | tf_op jit(solution)/shard_map/ppermute | solution.py:27
  35.9 0.0 collective-permute-done.8
  35.9 0.0 collective-permute-done.10
  36.0 0.8 %collective-permute-done.9 = bf16[8,8192]{1,0:T(8,128)(2,1)S(1)} collective-permute-done((bf16[8,8192]{1,0:T(8,128)(2,1)S(1)}, bf16[8,8192]{1,0:T(8,128)(2,1)S(1)}, u32[]{:S(2)}, u32[]{:S(2)}) %collective-permute-start.9) | collective-permute-done | bytes 131104 | tf_op jit(solution)/shard_map/ppermute | solution.py:21
  36.8 1.7 %collective-permute-done.15 = bf16[8,8192]{1,0:T(8,128)(2,1)S(1)} collective-permute-done((bf16[8,8192]{1,0:T(8,128)(2,1)S(1)}, bf16[8,8192]{1,0:T(8,128)(2,1)S(1)}, u32[]{:S(2)}, u32[]{:S(2)}) %collective-permute-start.15) | collective-permute-done | bytes 131104 | tf_op jit(solution)/shard_map/ppermute | solution.py:27
  38.4 0.1 constant_dynamic-update-slice_fusion.18
  38.5 0.0 copy-start.2
  38.6 0.6 collective-permute-start.24
  39.1 1.5 %collective-permute-start.23 = (bf16[8,8192]{1,0:T(8,128)(2,1)S(1)}, bf16[8,8192]{1,0:T(8,128)(2,1)S(1)}, u32[]{:S(2)}, u32[]{:S(2)}) collective-permute-start(bf16[8,8192]{1,0:T(8,128)(2,1)S(1)} %get-tuple-element.17), channel_id=1, source_target_pairs={{0,2},{1,3},{2,0},{3,1},{4,6},{5,7},{6,4},{7,5},{8,10},{9,11},{10,... | collective-permute-start | bytes 393224 | tf_op jit(solution)/shard_map/ppermute | solution.py:21
  40.6 1.5 %collective-permute-start.19 = (bf16[8,8192]{1,0:T(8,128)(2,1)S(1)}, bf16[8,8192]{1,0:T(8,128)(2,1)S(1)}, u32[]{:S(2)}, u32[]{:S(2)}) collective-permute-start(bf16[8,8192]{1,0:T(8,128)(2,1)S(1)} %get-tuple-element.17), channel_id=1, source_target_pairs={{0,6},{1,7},{2,4},{3,5},{4,2},{5,3},{6,0},{7,1},{8,14},{9,15},{10,... | collective-permute-start | bytes 393224 | tf_op jit(solution)/shard_map/ppermute | solution.py:21
  42.1 1.3 %collective-permute-start.16 = (bf16[8,8192]{1,0:T(8,128)(2,1)S(1)}, bf16[8,8192]{1,0:T(8,128)(2,1)S(1)}, u32[]{:S(2)}, u32[]{:S(2)}) collective-permute-start(bf16[8,8192]{1,0:T(8,128)(2,1)S(1)} %get-tuple-element.17), channel_id=1, source_target_pairs={{8,0},{9,1},{10,2},{11,3},{12,4},{13,5},{14,6},{15,7},{16,8},{17,9... | collective-permute-start | bytes 393224 | tf_op jit(solution)/shard_map/ppermute | solution.py:27
  43.4 0.7 %collective-permute-done.24 = bf16[8,8192]{1,0:T(8,128)(2,1)S(1)} collective-permute-done((bf16[8,8192]{1,0:T(8,128)(2,1)S(1)}, bf16[8,8192]{1,0:T(8,128)(2,1)S(1)}, u32[]{:S(2)}, u32[]{:S(2)}) %collective-permute-start.24) | collective-permute-done | bytes 131104 | tf_op jit(solution)/shard_map/ppermute | solution.py:21
  44.1 0.0 collective-permute-done.23
  44.1 2.4 %collective-permute-done.19 = bf16[8,8192]{1,0:T(8,128)(2,1)S(1)} collective-permute-done((bf16[8,8192]{1,0:T(8,128)(2,1)S(1)}, bf16[8,8192]{1,0:T(8,128)(2,1)S(1)}, u32[]{:S(2)}, u32[]{:S(2)}) %collective-permute-start.19) | collective-permute-done | bytes 131104 | tf_op jit(solution)/shard_map/ppermute | solution.py:21
  46.5 0.1 collective-permute-start.25
  46.6 1.3 %collective-permute-start.20 = (bf16[8,8192]{1,0:T(8,128)(2,1)S(1)}, bf16[8,8192]{1,0:T(8,128)(2,1)S(1)}, u32[]{:S(2)}, u32[]{:S(2)}) collective-permute-start(bf16[8,8192]{1,0:T(8,128)(2,1)S(1)} %collective-permute-done.19), channel_id=1, source_target_pairs={{8,0},{9,1},{10,2},{11,3},{12,4},{13,5},{14,6},{15,7},{16,8},{17,9... | collective-permute-start | bytes 393224 | tf_op jit(solution)/shard_map/ppermute | solution.py:27
  47.9 1.5 %collective-permute-done.16 = bf16[8,8192]{1,0:T(8,128)(2,1)S(1)} collective-permute-done((bf16[8,8192]{1,0:T(8,128)(2,1)S(1)}, bf16[8,8192]{1,0:T(8,128)(2,1)S(1)}, u32[]{:S(2)}, u32[]{:S(2)}) %collective-permute-start.16) | collective-permute-done | bytes 131104 | tf_op jit(solution)/shard_map/ppermute | solution.py:27
  49.4 0.5 collective-permute-start.18
  49.9 1.5 %collective-permute-start.17 = (bf16[8,8192]{1,0:T(8,128)(2,1)S(1)}, bf16[8,8192]{1,0:T(8,128)(2,1)S(1)}, u32[]{:S(2)}, u32[]{:S(2)}) collective-permute-start(bf16[8,8192]{1,0:T(8,128)(2,1)S(1)} %collective-permute-done.16), channel_id=1, source_target_pairs={{0,2},{1,3},{2,0},{3,1},{4,6},{5,7},{6,4},{7,5},{8,10},{9,11},{10,... | collective-permute-start | bytes 393224 | tf_op jit(solution)/shard_map/ppermute | solution.py:21
  51.5 2.9 %collective-permute-done.18 = bf16[8,8192]{1,0:T(8,128)(2,1)S(1)} collective-permute-done((bf16[8,8192]{1,0:T(8,128)(2,1)S(1)}, bf16[8,8192]{1,0:T(8,128)(2,1)S(1)}, u32[]{:S(2)}, u32[]{:S(2)}) %collective-permute-start.18) | collective-permute-done | bytes 131104 | tf_op jit(solution)/shard_map/ppermute | solution.py:21
  54.4 0.6 collective-permute-done.17
  55.0 0.1 collective-permute-start.21
  55.0 0.1 collective-permute-done.20
  55.1 0.4 collective-permute-start.22
  55.6 0.0 collective-permute-done.25
  55.6 1.1 %collective-permute-done.21 = bf16[24,8192]{1,0:T(8,128)(2,1)S(1)} collective-permute-done((bf16[24,8192]{1,0:T(8,128)(2,1)S(1)}, bf16[24,8192]{1,0:T(8,128)(2,1)S(1)}, u32[]{:S(2)}, u32[]{:S(2)}) %collective-permute-start.21) | collective-permute-done | bytes 393248 | tf_op jit(solution)/shard_map/ppermute | solution.py:21
  56.8 2.2 %grad_own.1.own_ref = f32[64,256]{1,0:T(8,128)S(1)} custom-call(bf16[64,8192]{1,0:T(8,128)(2,1)S(1)} %constant_dynamic-update-slice_fusion.14.rows_ref, bf16[1,2,256,8192]{3,2,1,0:T(8,128)(2,1)S(1)} %get-tuple-element.10.dec_ref), custom_call_target="tpu_custom_call" | custom-call | flops 268435456 | bytes 4194304 | tf_op jit(solution)/shard_map/grad_own/pallas_call | solution.py:176
  59.0 0.0 collective-permute-done.22
  59.0 2.9 %grad_all.1 = f32[1,64,256]{2,1,0:T(8,128)} custom-call(s32[1]{0:T(128)} %bitcast.place_ref, bf16[64,8192]{1,0:T(8,128)(2,1)S(1)} %constant_dynamic-update-slice_fusion.8.rows_ref, bf16[1,2,256,8192]{3,2,1,0:T(8,128)(2,1)S(1)} %get-tuple-element.10.dec_ref, f32[64,256]{1,0:T(8,128)S(1)} %grad_own.1.own_ref), custom_call_target="tpu_custom_call" | custom-call | flops 268435456 | bytes 4194304 | tf_op jit(solution)/shard_map/grad_all/pallas_call | solution.py:188
  (27 shorter events, 0.4 us)
Async XLA Ops:
  0.6 12.9 %copy-start = (s32[1,2,2]{2,1,0:T(2,128)S(1)}, s32[1,2,2]{2,1,0:T(2,128)}, u32[]{:S(2)}) copy-start(s32[1,2,2]{2,1,0:T(2,128)} %param.9) | copy-start | bytes 52
  0.6 12.9 %copy-start.1 = (bf16[1,256]{1,0:T(2,128)(2,1)S(1)}, bf16[1,256]{1,0:T(2,128)(2,1)}, u32[]{:S(2)}) copy-start(bf16[1,256]{1,0:T(2,128)(2,1)} %bias_ref.1) | copy-start | bytes 1540
  0.6 11.7 %collective-permute-start.3 = (bf16[8,8192]{1,0:T(8,128)(2,1)}, bf16[8,8192]{1,0:T(8,128)(2,1)S(1)}, u32[]{:S(2)}, u32[]{:S(2)}) collective-permute-start(bf16[8,8192]{1,0:T(8,128)(2,1)} %bitcast.11), channel_id=1, source_target_pairs={{0,1},{1,0},{2,3},{3,2},{4,5},{5,4},{6,7},{7,6},{8,9},{9,8},{10,11... | collective-permute-start | bytes 393224 | tf_op jit(solution)/shard_map/ppermute | solution.py:21
  1.2 9.8 %collective-permute-start.2 = (bf16[8,8192]{1,0:T(8,128)(2,1)}, bf16[8,8192]{1,0:T(8,128)(2,1)S(1)}, u32[]{:S(2)}, u32[]{:S(2)}) collective-permute-start(bf16[8,8192]{1,0:T(8,128)(2,1)} %bitcast.12), channel_id=1, source_target_pairs={{0,6},{1,7},{2,4},{3,5},{4,2},{5,3},{6,0},{7,1},{8,14},{9,15},{10,... | collective-permute-start | bytes 393224 | tf_op jit(solution)/shard_map/ppermute | solution.py:21
  4.7 7.1 %collective-permute-start.1 = (bf16[8,8192]{1,0:T(8,128)(2,1)}, bf16[8,8192]{1,0:T(8,128)(2,1)S(1)}, u32[]{:S(2)}, u32[]{:S(2)}) collective-permute-start(bf16[8,8192]{1,0:T(8,128)(2,1)} %bitcast.13), channel_id=1, source_target_pairs={{0,4},{1,5},{2,6},{3,7},{4,0},{5,1},{6,2},{7,3},{8,12},{9,13},{10,... | collective-permute-start | bytes 393224 | tf_op jit(solution)/shard_map/ppermute | solution.py:21
  5.2 6.9 %collective-permute-start = (bf16[8,8192]{1,0:T(8,128)(2,1)}, bf16[8,8192]{1,0:T(8,128)(2,1)S(1)}, u32[]{:S(2)}, u32[]{:S(2)}) collective-permute-start(bf16[8,8192]{1,0:T(8,128)(2,1)} %bitcast.14), channel_id=1, source_target_pairs={{0,2},{1,3},{2,0},{3,1},{4,6},{5,7},{6,4},{7,5},{8,10},{9,11},{10,... | collective-permute-start | bytes 393224 | tf_op jit(solution)/shard_map/ppermute | solution.py:21
  11.0 2.5 %collective-permute-start.6 = (bf16[8,8192]{1,0:T(8,128)(2,1)S(1)}, bf16[8,8192]{1,0:T(8,128)(2,1)S(1)}, u32[]{:S(2)}, u32[]{:S(2)}) collective-permute-start(bf16[8,8192]{1,0:T(8,128)(2,1)S(1)} %collective-permute-done.2), channel_id=1, source_target_pairs={{0,1},{1,0},{2,3},{3,2},{4,5},{5,4},{6,7},{7,6},{8,9},{9,8},{10,11... | collective-permute-start | bytes 393224 | tf_op jit(solution)/shard_map/ppermute | solution.py:21
  11.8 1.7 %collective-permute-start.5 = (bf16[8,8192]{1,0:T(8,128)(2,1)S(1)}, bf16[8,8192]{1,0:T(8,128)(2,1)S(1)}, u32[]{:S(2)}, u32[]{:S(2)}) collective-permute-start(bf16[8,8192]{1,0:T(8,128)(2,1)S(1)} %collective-permute-done.1), channel_id=1, source_target_pairs={{0,1},{1,0},{2,3},{3,2},{4,5},{5,4},{6,7},{7,6},{8,9},{9,8},{10,11... | collective-permute-start | bytes 393224 | tf_op jit(solution)/shard_map/ppermute | solution.py:21
  12.1 1.3 %collective-permute-start.4 = (bf16[8,8192]{1,0:T(8,128)(2,1)S(1)}, bf16[8,8192]{1,0:T(8,128)(2,1)S(1)}, u32[]{:S(2)}, u32[]{:S(2)}) collective-permute-start(bf16[8,8192]{1,0:T(8,128)(2,1)S(1)} %collective-permute-done), channel_id=1, source_target_pairs={{0,1},{1,0},{2,3},{3,2},{4,5},{5,4},{6,7},{7,6},{8,9},{9,8},{10,11... | collective-permute-start | bytes 393224 | tf_op jit(solution)/shard_map/ppermute | solution.py:21
  17.6 2.3 %collective-permute-start.11 = (bf16[32,8192]{1,0:T(8,128)(2,1)S(1)}, bf16[32,8192]{1,0:T(8,128)(2,1)S(1)}, u32[]{:S(2)}, u32[]{:S(2)}) collective-permute-start(bf16[32,8192]{1,0:T(8,128)(2,1)S(1)} %get-tuple-element.15), channel_id=1, source_target_pairs={{0,1},{1,0},{2,3},{3,2},{4,5},{5,4},{6,7},{7,6},{8,9},{9,8},{10,11... | collective-permute-start | bytes 1572872 | tf_op jit(solution)/shard_map/ppermute | solution.py:21
  17.8 20.6 %copy-start.3 = (bf16[1,8,8192]{2,1,0:T(8,128)(2,1)S(1)}, bf16[1,8,8192]{2,1,0:T(8,128)(2,1)}, u32[]{:S(2)}) copy-start(bf16[1,8,8192]{2,1,0:T(8,128)(2,1)} %param.11) | copy-start | bytes 393220
  19.5 4.1 %collective-permute-start.7 = (bf16[32,8192]{1,0:T(8,128)(2,1)S(1)}, bf16[32,8192]{1,0:T(8,128)(2,1)S(1)}, u32[]{:S(2)}, u32[]{:S(2)}) collective-permute-start(bf16[32,8192]{1,0:T(8,128)(2,1)S(1)} %get-tuple-element.13), channel_id=1, source_target_pairs={{0,1},{1,0},{2,3},{3,2},{4,5},{5,4},{6,7},{7,6},{8,9},{9,8},{10,11... | collective-permute-start | bytes 1572872 | tf_op jit(solution)/shard_map/ppermute | solution.py:21
  20.0 6.9 %collective-permute-start.12 = (bf16[8,8192]{1,0:T(8,128)(2,1)S(1)}, bf16[8,8192]{1,0:T(8,128)(2,1)S(1)}, u32[]{:S(2)}, u32[]{:S(2)}) collective-permute-start(bf16[8,8192]{1,0:T(8,128)(2,1)S(1)} %get-tuple-element.25), channel_id=1, source_target_pairs={{0,2},{1,3},{2,0},{3,1},{4,6},{5,7},{6,4},{7,5},{8,10},{9,11},{10,... | collective-permute-start | bytes 393224 | tf_op jit(solution)/shard_map/ppermute | solution.py:21
  21.7 8.6 %collective-permute-start.14 = (bf16[8,8192]{1,0:T(8,128)(2,1)S(1)}, bf16[8,8192]{1,0:T(8,128)(2,1)S(1)}, u32[]{:S(2)}, u32[]{:S(2)}) collective-permute-start(bf16[8,8192]{1,0:T(8,128)(2,1)S(1)} %get-tuple-element.26), channel_id=1, source_target_pairs={{0,6},{1,7},{2,4},{3,5},{4,2},{5,3},{6,0},{7,1},{8,14},{9,15},{10,... | collective-permute-start | bytes 393224 | tf_op jit(solution)/shard_map/ppermute | solution.py:21
  23.2 9.2 %collective-permute-start.13 = (bf16[8,8192]{1,0:T(8,128)(2,1)S(1)}, bf16[8,8192]{1,0:T(8,128)(2,1)S(1)}, u32[]{:S(2)}, u32[]{:S(2)}) collective-permute-start(bf16[8,8192]{1,0:T(8,128)(2,1)S(1)} %get-tuple-element.27), channel_id=1, source_target_pairs={{0,4},{1,5},{2,6},{3,7},{4,0},{5,1},{6,2},{7,3},{8,12},{9,13},{10,... | collective-permute-start | bytes 393224 | tf_op jit(solution)/shard_map/ppermute | solution.py:21
  23.8 12.2 %collective-permute-start.8 = (bf16[8,8192]{1,0:T(8,128)(2,1)S(1)}, bf16[8,8192]{1,0:T(8,128)(2,1)S(1)}, u32[]{:S(2)}, u32[]{:S(2)}) collective-permute-start(bf16[8,8192]{1,0:T(8,128)(2,1)S(1)} %get-tuple-element.22), channel_id=1, source_target_pairs={{0,2},{1,3},{2,0},{3,1},{4,6},{5,7},{6,4},{7,5},{8,10},{9,11},{10,... | collective-permute-start | bytes 393224 | tf_op jit(solution)/shard_map/ppermute | solution.py:21
  25.4 10.5 %collective-permute-start.10 = (bf16[8,8192]{1,0:T(8,128)(2,1)S(1)}, bf16[8,8192]{1,0:T(8,128)(2,1)S(1)}, u32[]{:S(2)}, u32[]{:S(2)}) collective-permute-start(bf16[8,8192]{1,0:T(8,128)(2,1)S(1)} %get-tuple-element.23), channel_id=1, source_target_pairs={{0,6},{1,7},{2,4},{3,5},{4,2},{5,3},{6,0},{7,1},{8,14},{9,15},{10,... | collective-permute-start | bytes 393224 | tf_op jit(solution)/shard_map/ppermute | solution.py:21
  26.9 9.9 %collective-permute-start.9 = (bf16[8,8192]{1,0:T(8,128)(2,1)S(1)}, bf16[8,8192]{1,0:T(8,128)(2,1)S(1)}, u32[]{:S(2)}, u32[]{:S(2)}) collective-permute-start(bf16[8,8192]{1,0:T(8,128)(2,1)S(1)} %get-tuple-element.24), channel_id=1, source_target_pairs={{0,4},{1,5},{2,6},{3,7},{4,0},{5,1},{6,2},{7,3},{8,12},{9,13},{10,... | collective-permute-start | bytes 393224 | tf_op jit(solution)/shard_map/ppermute | solution.py:21
  32.4 6.0 %collective-permute-start.15 = (bf16[8,8192]{1,0:T(8,128)(2,1)S(1)}, bf16[8,8192]{1,0:T(8,128)(2,1)S(1)}, u32[]{:S(2)}, u32[]{:S(2)}) collective-permute-start(bf16[8,8192]{1,0:T(8,128)(2,1)S(1)} %fusion.2), channel_id=1, source_target_pairs={{0,8},{1,9},{2,10},{3,11},{4,12},{5,13},{6,14},{7,15},{8,16},{9,17... | collective-permute-start | bytes 393224 | tf_op jit(solution)/shard_map/ppermute | solution.py:27
  38.5 23.4 %copy-start.2 = (bf16[8,8192]{1,0:T(8,128)(2,1)}, bf16[8,8192]{1,0:T(8,128)(2,1)S(1)}, u32[]{:S(2)}) copy-start(bf16[8,8192]{1,0:T(8,128)(2,1)S(1)} %get-tuple-element.17) | copy-start | bytes 393220
  38.6 5.5 %collective-permute-start.24 = (bf16[8,8192]{1,0:T(8,128)(2,1)S(1)}, bf16[8,8192]{1,0:T(8,128)(2,1)S(1)}, u32[]{:S(2)}, u32[]{:S(2)}) collective-permute-start(bf16[8,8192]{1,0:T(8,128)(2,1)S(1)} %get-tuple-element.17), channel_id=1, source_target_pairs={{0,4},{1,5},{2,6},{3,7},{4,0},{5,1},{6,2},{7,3},{8,12},{9,13},{10,... | collective-permute-start | bytes 393224 | tf_op jit(solution)/shard_map/ppermute | solution.py:21
  39.1 5.0 %collective-permute-start.23 = (bf16[8,8192]{1,0:T(8,128)(2,1)S(1)}, bf16[8,8192]{1,0:T(8,128)(2,1)S(1)}, u32[]{:S(2)}, u32[]{:S(2)}) collective-permute-start(bf16[8,8192]{1,0:T(8,128)(2,1)S(1)} %get-tuple-element.17), channel_id=1, source_target_pairs={{0,2},{1,3},{2,0},{3,1},{4,6},{5,7},{6,4},{7,5},{8,10},{9,11},{10,... | collective-permute-start | bytes 393224 | tf_op jit(solution)/shard_map/ppermute | solution.py:21
  40.6 5.9 %collective-permute-start.19 = (bf16[8,8192]{1,0:T(8,128)(2,1)S(1)}, bf16[8,8192]{1,0:T(8,128)(2,1)S(1)}, u32[]{:S(2)}, u32[]{:S(2)}) collective-permute-start(bf16[8,8192]{1,0:T(8,128)(2,1)S(1)} %get-tuple-element.17), channel_id=1, source_target_pairs={{0,6},{1,7},{2,4},{3,5},{4,2},{5,3},{6,0},{7,1},{8,14},{9,15},{10,... | collective-permute-start | bytes 393224 | tf_op jit(solution)/shard_map/ppermute | solution.py:21
  42.1 7.3 %collective-permute-start.16 = (bf16[8,8192]{1,0:T(8,128)(2,1)S(1)}, bf16[8,8192]{1,0:T(8,128)(2,1)S(1)}, u32[]{:S(2)}, u32[]{:S(2)}) collective-permute-start(bf16[8,8192]{1,0:T(8,128)(2,1)S(1)} %get-tuple-element.17), channel_id=1, source_target_pairs={{8,0},{9,1},{10,2},{11,3},{12,4},{13,5},{14,6},{15,7},{16,8},{17,9... | collective-permute-start | bytes 393224 | tf_op jit(solution)/shard_map/ppermute | solution.py:27
  46.5 9.1 %collective-permute-start.25 = (bf16[32,8192]{1,0:T(8,128)(2,1)S(1)}, bf16[32,8192]{1,0:T(8,128)(2,1)S(1)}, u32[]{:S(2)}, u32[]{:S(2)}) collective-permute-start(bf16[32,8192]{1,0:T(8,128)(2,1)S(1)} %pad_maximum_fusion), channel_id=1, source_target_pairs={{0,1},{1,0},{2,3},{3,2},{4,5},{5,4},{6,7},{7,6},{8,9},{9,8},{10,11... | collective-permute-start | bytes 1572872 | tf_op jit(solution)/shard_map/ppermute | solution.py:21
  46.6 8.5 %collective-permute-start.20 = (bf16[8,8192]{1,0:T(8,128)(2,1)S(1)}, bf16[8,8192]{1,0:T(8,128)(2,1)S(1)}, u32[]{:S(2)}, u32[]{:S(2)}) collective-permute-start(bf16[8,8192]{1,0:T(8,128)(2,1)S(1)} %collective-permute-done.19), channel_id=1, source_target_pairs={{8,0},{9,1},{10,2},{11,3},{12,4},{13,5},{14,6},{15,7},{16,8},{17,9... | collective-permute-start | bytes 393224 | tf_op jit(solution)/shard_map/ppermute | solution.py:27
  49.4 5.0 %collective-permute-start.18 = (bf16[8,8192]{1,0:T(8,128)(2,1)S(1)}, bf16[8,8192]{1,0:T(8,128)(2,1)S(1)}, u32[]{:S(2)}, u32[]{:S(2)}) collective-permute-start(bf16[8,8192]{1,0:T(8,128)(2,1)S(1)} %collective-permute-done.16), channel_id=1, source_target_pairs={{0,4},{1,5},{2,6},{3,7},{4,0},{5,1},{6,2},{7,3},{8,12},{9,13},{10,... | collective-permute-start | bytes 393224 | tf_op jit(solution)/shard_map/ppermute | solution.py:21
  49.9 5.0 %collective-permute-start.17 = (bf16[8,8192]{1,0:T(8,128)(2,1)S(1)}, bf16[8,8192]{1,0:T(8,128)(2,1)S(1)}, u32[]{:S(2)}, u32[]{:S(2)}) collective-permute-start(bf16[8,8192]{1,0:T(8,128)(2,1)S(1)} %collective-permute-done.16), channel_id=1, source_target_pairs={{0,2},{1,3},{2,0},{3,1},{4,6},{5,7},{6,4},{7,5},{8,10},{9,11},{10,... | collective-permute-start | bytes 393224 | tf_op jit(solution)/shard_map/ppermute | solution.py:21
  55.0 1.8 %collective-permute-start.21 = (bf16[24,8192]{1,0:T(8,128)(2,1)S(1)}, bf16[24,8192]{1,0:T(8,128)(2,1)S(1)}, u32[]{:S(2)}, u32[]{:S(2)}) collective-permute-start(bf16[24,8192]{1,0:T(8,128)(2,1)S(1)} %pad_maximum_fusion.1), channel_id=1, source_target_pairs={{0,1},{1,0},{2,3},{3,2},{4,5},{5,4},{6,7},{7,6},{8,9},{9,8},{10,11... | collective-permute-start | bytes 1179656 | tf_op jit(solution)/shard_map/ppermute | solution.py:21
  55.1 3.9 %collective-permute-start.22 = (bf16[8,8192]{1,0:T(8,128)(2,1)S(1)}, bf16[8,8192]{1,0:T(8,128)(2,1)S(1)}, u32[]{:S(2)}, u32[]{:S(2)}) collective-permute-start(bf16[8,8192]{1,0:T(8,128)(2,1)S(1)} %collective-permute-done.20), channel_id=1, source_target_pairs={{0,1},{1,0},{2,3},{3,2},{4,5},{5,4},{6,7},{7,6},{8,9},{9,8},{10,11... | collective-permute-start | bytes 393224 | tf_op jit(solution)/shard_map/ppermute | solution.py:21

commit v5 on v4

--- a/solution.py
+++ b/solution.py
@@ -41,15 +41,17 @@
     return jnp.concatenate(near + far, axis=0)
 
 
-def scattered(near, far, chips):
+def blocks_of(near, far, chips):
     rows = near.shape[0] // chips
     total = near + swap(far, 1).astype(jnp.float32)
-    sends = [total[chip * rows : (chip + 1) * rows].astype(jnp.bfloat16) for chip in range(1, chips)]
-    came = [swap(sends[chip - 1], CORES * chip) for chip in range(1, chips)]
-    out = total[:rows]
-    for block in came:
-        out = out + block.astype(jnp.float32)
-    return out
+    return [total[chip * rows : (chip + 1) * rows] for chip in range(chips)]
+
+
+def summed(blocks, sent):
+    total = blocks[0]
+    for came in [swap(blocks[chip].astype(jnp.bfloat16), CORES * chip) for chip in sent]:
+        total = total + came.astype(jnp.float32)
+    return total
 
 
 def load_kernel(*refs):
@@ -82,9 +84,8 @@
 def decode(codes, dec_ref, reach, near_ref, far_ref):
     half, width = near_ref.shape
 
-    @pl.loop(0, width // CHUNK)
-    def _(step):
-        columns = pl.ds(pl.multiple_of(step * CHUNK, CHUNK), CHUNK)
+    for step in range(width // CHUNK):
+        columns = pl.ds(step * CHUNK, CHUNK)
         part = jnp.dot(codes, dec_ref[0, reach, :, columns], preferred_element_type=jnp.float32)
         near_ref[:, columns] = part[:half]
         far_ref[:, columns] = part[half:].astype(jnp.bfloat16)
@@ -95,11 +96,7 @@
     group = rows // tokens
     chips = group // CORES
 
-    def step(i, total):
-        part = pl.ds(pl.multiple_of(i * CHUNK, CHUNK), CHUNK)
-        return total + jnp.dot(x_ref[:, part], enc_ref[0, part, :], preferred_element_type=jnp.float32)
-
-    pre = lax.fori_loop(0, depth // CHUNK, step, jnp.zeros((rows, enc_ref.shape[2]), jnp.float32))
+    pre = jnp.dot(x_ref[...], enc_ref[0], preferred_element_type=jnp.float32)
     held[...] = jnp.maximum(pre + bias_ref[...].astype(jnp.float32), 0.0)
     for block in range(group):
         core, chip = block // chips, block % chips
@@ -149,13 +146,9 @@
 
 
 def back(rows_ref, dec_ref, reach, total):
-    def step(i, total):
-        part = pl.ds(pl.multiple_of(i * CHUNK, CHUNK), CHUNK)
-        return total + lax.dot_general(
-            rows_ref[:, part], dec_ref[0, reach, :, part], (((1,), (1,)), ((), ())), preferred_element_type=jnp.float32
-        )
-
-    return lax.fori_loop(0, rows_ref.shape[1] // CHUNK, step, total)
+    return total + lax.dot_general(
+        rows_ref[...], dec_ref[0, reach], (((1,), (1,)), ((), ())), preferred_element_type=jnp.float32
+    )
 
 
 def grad_own_kernel(rows_ref, dec_ref, out_ref):
@@ -201,22 +194,28 @@
     chips = group // CORES
     place = (lax.axis_index(AXIS) % group).astype(jnp.int32).reshape(1)
     tokens = resid.shape[1]
-    enc, dec = loaded(enc_weight, dec_weight)
+    (enc,), (dec,) = loaded(enc_weight), loaded(dec_weight)
     x = gathered(resid[0], chips)
     codes, next_near, next_far = encoded(place, active[0], x, enc, enc_bias, dec, tokens)
     own_near, own_far = decoded(codes, dec)
-    next_sum = scattered(next_near, next_far, chips).astype(jnp.bfloat16)
+    nexts = blocks_of(next_near, next_far, chips)
+    owns = blocks_of(own_near, own_far, chips)
+    risen = shifted(nexts[-1].astype(jnp.bfloat16), group)
+    next_sum = summed(nexts, range(1, chips - 1)).astype(jnp.bfloat16)
+    owns[-1] = owns[-1] + risen.astype(jnp.float32)
     from_before = shifted(next_sum, group).astype(jnp.float32)
-    own_sum = scattered(own_near, own_far, chips)
+    own_sum = summed(owns, range(1, chips))
     error = (own_sum + from_before - target[0].astype(jnp.float32)).astype(jnp.bfloat16)
 
     later = shifted(error, -group)
     here = [error] + [swap(error, CORES * chip) for chip in range(1, chips)]
     after = [later] + [swap(later, CORES * chip) for chip in range(1, chips - 1)]
+    here[-1], _ = lax.optimization_barrier((here[-1], later))
     last = shifted(here[-1], -group)
     here_near = jnp.concatenate(here, axis=0)
-    here_rows = jnp.concatenate([here_near, swap(here_near, 1)], axis=0)
-    after_most = jnp.concatenate(after, axis=0)
+    here_far = swap(here_near, 1)
+    here_rows = jnp.concatenate([here_near, here_far], axis=0)
+    after_most, _ = lax.optimization_barrier((jnp.concatenate(after, axis=0), here_far))
     after_rows = jnp.concatenate([after_most, last, swap(after_most, 1), swap(last, 1)], axis=0)
     grad = grad_all(place, after_rows, dec, grad_own(here_rows, dec), tokens)
     return (error[None], grad)

time: 62.6 us -> 73.9 us (1.18)
  local copies, waits for them, and re-layouts: 1.24 us -> 12 us
  Pallas kernels: 15.5 us -> 13 us
  starting transfers between devices: 25.7 us -> 27.6 us
  waiting for transfers between devices: 18.1 us -> 19.3 us
    unnamed x23 -> x28, local copies, waits for them, and re-layouts: 1.13 us -> 11.9 us
    ppermute x3 -> x4, waiting for transfers between devices: 3.21 us -> 7.57 us  [shifted(): return lax.ppermute(block, AXIS, route)]
    ppermute x3 -> x4, starting transfers between devices: 6.07 us -> 9.92 us  [shifted(): return lax.ppermute(block, AXIS, route)]
    ppermute x23 -> x22, waiting for transfers between devices: 14.9 us -> 11.7 us  [swap(): return lax.ppermute(value, AXIS, pairs)]
    ppermute x23 -> x22, starting transfers between devices: 19.6 us -> 17.7 us  [swap(): return lax.ppermute(value, AXIS, pairs)]
    pallas_call x1 -> x2, Pallas kernels: 4.68 us -> 5.62 us  [loaded(): pl.pallas_call(load_kernel, out_shape=[pltpu.VMEM(w.shape, w.dtype) for w...]
    pallas_call x1, Pallas kernels: 4 us -> 3.14 us  [encoded(): pl.pallas_call(functools.partial(encode_kernel, tokens), out_shape=[pltpu...]
    pallas_call x1, Pallas kernels: 1.69 us -> 0.84 us  [decoded(): pl.pallas_call(decode_kernel, out_shape=halves_of(rows, width), in_specs=...]
  transfers between devices with their start and end apart: 26 -> 26, of which waited for: 14 -> 11; matrix products, arithmetic and copies ran while one was open for 3% -> 2% of each run, Pallas kernels for 14% -> 11%
where the time goes in v5:
time: 73.9 us; the launch traced here: 73.4 us
  starting transfers between devices  27.6 us (37%)
  waiting for transfers between devices  19.3 us (26%)
  Pallas kernels  13 us (18%)
  local copies, waits for them, and re-layouts  12 us (16%)
  between operations  0.98 us (1%)
    ppermute x22, starting transfers between devices, swap(): return lax.ppermute(value, AXIS, pairs)  17.7 us
    unnamed x28, local copies, waits for them, and re-layouts  11.9 us
    ppermute x22, waiting for transfers between devices, swap(): return lax.ppermute(value, AXIS, pairs)  11.7 us
    ppermute x4, starting transfers between devices, shifted(): return lax.ppermute(block, AXIS, route)  9.92 us
    ppermute x4, waiting for transfers between devices, shifted(): return lax.ppermute(block, AXIS, route)  7.57 us
    pallas_call x2, Pallas kernels, loaded(): pl.pallas_call(load_kernel, out_shape=[pltpu.VMEM(w.shape, w.dtype) for w...  5.62 us
    pallas_call x1, Pallas kernels, encoded(): pl.pallas_call(functools.partial(encode_kernel, tokens), out_shape=[pltpu...  3.14 us
    pallas_call x1, Pallas kernels, grad_all(): pl.pallas_call(functools.partial(grad_kernel, tokens), out_shape=jax.Shap...  2.03 us
  transfers between devices with their start and end apart: 26, of which 11 were waited for; matrix products, arithmetic and copies ran while one was open for 2% of the time, Pallas kernels for 11%

profile of v5, /device:TPU:0, one launch (start us, length us, event | category | flops | bytes accessed | tf_op | source)
XLA Modules:
  0.0 73.4 jit_solution(7282368335820698103)
XLA Ops:
  0.6 0.5 collective-permute-start.3
  1.1 3.5 %collective-permute-start.2 = (bf16[8,8192]{1,0:T(8,128)(2,1)}, bf16[8,8192]{1,0:T(8,128)(2,1)S(1)}, u32[]{:S(2)}, u32[]{:S(2)}) collective-permute-start(bf16[8,8192]{1,0:T(8,128)(2,1)} %bitcast.12), channel_id=1, source_target_pairs={{0,6},{1,7},{2,4},{3,5},{4,2},{5,3},{6,0},{7,1},{8,14},{9,15},{10,... | collective-permute-start | bytes 393224 | tf_op jit(solution)/shard_map/ppermute | solution.py:21
  4.7 0.5 collective-permute-start.1
  5.2 0.1 collective-permute-start
  5.3 0.9 %constant_dynamic-update-slice_fusion.7 = bf16[64,8192]{1,0:T(8,128)(2,1)S(1)} fusion(bf16[1,8,8192]{2,1,0:T(8,128)(2,1)} %param.6), kind=kLoop, calls=%fused_computation.23 | loop fusion | bytes 262144
  6.3 2.2 %load_weights.2.enc_ref = bf16[1,8192,256]{2,1,0:T(8,128)(2,1)S(1)} custom-call(bf16[1,8192,256]{2,1,0:T(8,128)(2,1)} %refs_0_.2), custom_call_target="tpu_custom_call" | custom-call | bytes 8388608 | tf_op jit(solution)/shard_map/load_weights/pallas_call | solution.py:72
  8.5 2.0 %copy-done.3 = bf16[1,8192,256]{2,1,0:T(8,128)(2,1)} copy-done((bf16[1,8192,256]{2,1,0:T(8,128)(2,1)}, bf16[1,8192,256]{2,1,0:T(8,128)(2,1)S(1)}, u32[]{:S(2)}) %copy-start.3) | copy-done | bytes 4194328
  10.5 3.4 %load_weights.3.dec_ref = bf16[1,2,256,8192]{3,2,1,0:T(8,128)(2,1)S(1)} custom-call(bf16[1,2,256,8192]{3,2,1,0:T(8,128)(2,1)} %refs_0_.3), custom_call_target="tpu_custom_call" | custom-call | bytes 16777216 | tf_op jit(solution)/shard_map/load_weights/pallas_call | solution.py:72
  13.9 3.3 %copy-done = bf16[1,2,256,8192]{3,2,1,0:T(8,128)(2,1)} copy-done((bf16[1,2,256,8192]{3,2,1,0:T(8,128)(2,1)}, bf16[1,2,256,8192]{3,2,1,0:T(8,128)(2,1)S(1)}, u32[]{:S(2)}) %copy-start) | copy-done | bytes 8388632
  17.2 0.0 collective-permute-done.2
  17.2 0.0 collective-permute-start.6
  17.2 0.0 collective-permute-done.1
  17.2 0.5 collective-permute-start.5
  17.7 0.0 collective-permute-done
  17.8 0.1 collective-permute-start.4
  17.9 0.0 collective-permute-done.3
  17.9 1.2 %collective-permute-done.4 = bf16[8,8192]{1,0:T(8,128)(2,1)S(1)} collective-permute-done((bf16[8,8192]{1,0:T(8,128)(2,1)S(1)}, bf16[8,8192]{1,0:T(8,128)(2,1)S(1)}, u32[]{:S(2)}, u32[]{:S(2)}) %collective-permute-start.4) | collective-permute-done | bytes 131104 | tf_op jit(solution)/shard_map/ppermute | solution.py:21
  19.1 0.0 collective-permute-done.5
  19.1 0.0 collective-permute-done.6
  19.2 3.4 %copy-done.1 = bf16[1,2,256,8192]{3,2,1,0:T(8,128)(2,1)S(1)} copy-done((bf16[1,2,256,8192]{3,2,1,0:T(8,128)(2,1)S(1)}, bf16[1,2,256,8192]{3,2,1,0:T(8,128)(2,1)}, u32[]{:S(2)}) %copy-start.1) | copy-done | bytes 8388632
  22.6 2.2 %copy-done.4 = bf16[1,8192,256]{2,1,0:T(8,128)(2,1)S(1)} copy-done((bf16[1,8192,256]{2,1,0:T(8,128)(2,1)S(1)}, bf16[1,8192,256]{2,1,0:T(8,128)(2,1)}, u32[]{:S(2)}) %copy-start.4) | copy-done | bytes 4194328
  24.8 3.1 %encode.1 = (bf16[64,256]{1,0:T(8,128)(2,1)S(1)}, f32[32,8192]{1,0:T(8,128)S(1)}, bf16[32,8192]{1,0:T(8,128)(2,1)S(1)}) custom-call(s32[1]{0:T(128)} %bitcast.place_ref, s32[2,2]{1,0:T(2,128)S(1)} %bitcast.9, bf16[64,8192]{1,0:T(8,128)(2,1)S(1)} %constant_dynamic-update-slice_fusion.x_ref, bf16[1,8192,256]{2,1,0:T(8,128)(2,1)S(1)} %copy-done.4, ...), custom_call_target="tpu_custom_call" | custom-call | flops 536870912 | bytes 8388608 | tf_op jit(solution)/shard_map/encode/pallas_call | solution.py:122
  27.9 0.2 collective-permute-start.10
  28.2 0.8 %decode_own.1 = (f32[32,8192]{1,0:T(8,128)S(1)}, bf16[32,8192]{1,0:T(8,128)(2,1)S(1)}) custom-call(bf16[64,256]{1,0:T(8,128)(2,1)S(1)} %get-tuple-element.9.codes_ref, bf16[1,2,256,8192]{3,2,1,0:T(8,128)(2,1)S(1)} %copy-done.2), custom_call_target="tpu_custom_call" | custom-call | flops 268435456 | bytes 4194304 | tf_op jit(solution)/shard_map/decode_own/pallas_call | solution.py:137
  29.0 0.4 collective-permute-start.7
  29.4 0.5 collective-permute-done.10
  29.9 0.1 fusion.10
  30.0 3.9 %collective-permute-start.11 = (bf16[8,8192]{1,0:T(8,128)(2,1)S(1)}, bf16[8,8192]{1,0:T(8,128)(2,1)S(1)}, u32[]{:S(2)}, u32[]{:S(2)}) collective-permute-start(bf16[8,8192]{1,0:T(8,128)(2,1)S(1)} %get-tuple-element.24), channel_id=1, source_target_pairs={{0,8},{1,9},{2,10},{3,11},{4,12},{5,13},{6,14},{7,15},{8,16},{9,17... | collective-permute-start | bytes 393224 | tf_op jit(solution)/shard_map/ppermute | solution.py:27
  33.9 1.6 %collective-permute-start.14 = (bf16[8,8192]{1,0:T(8,128)(2,1)S(1)}, bf16[8,8192]{1,0:T(8,128)(2,1)S(1)}, u32[]{:S(2)}, u32[]{:S(2)}) collective-permute-start(bf16[8,8192]{1,0:T(8,128)(2,1)S(1)} %get-tuple-element.25), channel_id=1, source_target_pairs={{0,4},{1,5},{2,6},{3,7},{4,0},{5,1},{6,2},{7,3},{8,12},{9,13},{10,... | collective-permute-start | bytes 393224 | tf_op jit(solution)/shard_map/ppermute | solution.py:21
  35.5 1.5 %collective-permute-start.13 = (bf16[8,8192]{1,0:T(8,128)(2,1)S(1)}, bf16[8,8192]{1,0:T(8,128)(2,1)S(1)}, u32[]{:S(2)}, u32[]{:S(2)}) collective-permute-start(bf16[8,8192]{1,0:T(8,128)(2,1)S(1)} %get-tuple-element.26), channel_id=1, source_target_pairs={{0,2},{1,3},{2,0},{3,1},{4,6},{5,7},{6,4},{7,5},{8,10},{9,11},{10,... | collective-permute-start | bytes 393224 | tf_op jit(solution)/shard_map/ppermute | solution.py:21
  37.0 0.0 collective-permute-done.7
  37.0 0.1 fusion.9
  37.2 0.6 collective-permute-start.8
  37.8 0.5 collective-permute-start.9
  38.3 1.0 %collective-permute-done.14 = bf16[8,8192]{1,0:T(8,128)(2,1)S(1)} collective-permute-done((bf16[8,8192]{1,0:T(8,128)(2,1)S(1)}, bf16[8,8192]{1,0:T(8,128)(2,1)S(1)}, u32[]{:S(2)}, u32[]{:S(2)}) %collective-permute-start.14) | collective-permute-done | bytes 131104 | tf_op jit(solution)/shard_map/ppermute | solution.py:21
  39.3 2.6 %collective-permute-done.13 = bf16[8,8192]{1,0:T(8,128)(2,1)S(1)} collective-permute-done((bf16[8,8192]{1,0:T(8,128)(2,1)S(1)}, bf16[8,8192]{1,0:T(8,128)(2,1)S(1)}, u32[]{:S(2)}, u32[]{:S(2)}) %collective-permute-start.13) | collective-permute-done | bytes 131104 | tf_op jit(solution)/shard_map/ppermute | solution.py:21
  42.0 3.5 %collective-permute-start.15 = (bf16[8,8192]{1,0:T(8,128)(2,1)S(1)}, bf16[8,8192]{1,0:T(8,128)(2,1)S(1)}, u32[]{:S(2)}, u32[]{:S(2)}) collective-permute-start(bf16[8,8192]{1,0:T(8,128)(2,1)S(1)} %fusion.1), channel_id=1, source_target_pairs={{0,8},{1,9},{2,10},{3,11},{4,12},{5,13},{6,14},{7,15},{8,16},{9,17... | collective-permute-start | bytes 393224 | tf_op jit(solution)/shard_map/ppermute | solution.py:27
  45.4 0.0 collective-permute-done.11
  45.5 1.5 %collective-permute-start.12 = (bf16[8,8192]{1,0:T(8,128)(2,1)S(1)}, bf16[8,8192]{1,0:T(8,128)(2,1)S(1)}, u32[]{:S(2)}, u32[]{:S(2)}) collective-permute-start(bf16[8,8192]{1,0:T(8,128)(2,1)S(1)} %fusion.2), channel_id=1, source_target_pairs={{0,6},{1,7},{2,4},{3,5},{4,2},{5,3},{6,0},{7,1},{8,14},{9,15},{10,... | collective-permute-start | bytes 393224 | tf_op jit(solution)/shard_map/ppermute | solution.py:21
  47.0 0.0 collective-permute-done.8
  47.0 0.9 %collective-permute-done.15 = bf16[8,8192]{1,0:T(8,128)(2,1)S(1)} collective-permute-done((bf16[8,8192]{1,0:T(8,128)(2,1)S(1)}, bf16[8,8192]{1,0:T(8,128)(2,1)S(1)}, u32[]{:S(2)}, u32[]{:S(2)}) %collective-permute-start.15) | collective-permute-done | bytes 131104 | tf_op jit(solution)/shard_map/ppermute | solution.py:27
  47.9 3.9 %collective-permute-done.12 = bf16[8,8192]{1,0:T(8,128)(2,1)S(1)} collective-permute-done((bf16[8,8192]{1,0:T(8,128)(2,1)S(1)}, bf16[8,8192]{1,0:T(8,128)(2,1)S(1)}, u32[]{:S(2)}, u32[]{:S(2)}) %collective-permute-start.12) | collective-permute-done | bytes 131104 | tf_op jit(solution)/shard_map/ppermute | solution.py:21
  51.8 0.1 constant_dynamic-update-slice_fusion.12
  51.9 0.0 copy-start.7
  51.9 1.4 %collective-permute-start.21 = (bf16[8,8192]{1,0:T(8,128)(2,1)S(1)}, bf16[8,8192]{1,0:T(8,128)(2,1)S(1)}, u32[]{:S(2)}, u32[]{:S(2)}) collective-permute-start(bf16[8,8192]{1,0:T(8,128)(2,1)S(1)} %get-tuple-element.17), channel_id=1, source_target_pairs={{0,6},{1,7},{2,4},{3,5},{4,2},{5,3},{6,0},{7,1},{8,14},{9,15},{10,... | collective-permute-start | bytes 393224 | tf_op jit(solution)/shard_map/ppermute | solution.py:21
  53.4 1.3 %collective-permute-start.16 = (bf16[8,8192]{1,0:T(8,128)(2,1)S(1)}, bf16[8,8192]{1,0:T(8,128)(2,1)S(1)}, u32[]{:S(2)}, u32[]{:S(2)}) collective-permute-start(bf16[8,8192]{1,0:T(8,128)(2,1)S(1)} %get-tuple-element.17), channel_id=1, source_target_pairs={{8,0},{9,1},{10,2},{11,3},{12,4},{13,5},{14,6},{15,7},{16,8},{17,9... | collective-permute-start | bytes 393224 | tf_op jit(solution)/shard_map/ppermute | solution.py:27
  54.7 0.6 collective-permute-start.19
  55.2 1.6 %collective-permute-start.20 = (bf16[8,8192]{1,0:T(8,128)(2,1)S(1)}, bf16[8,8192]{1,0:T(8,128)(2,1)S(1)}, u32[]{:S(2)}, u32[]{:S(2)}) collective-permute-start(bf16[8,8192]{1,0:T(8,128)(2,1)S(1)} %get-tuple-element.17), channel_id=1, source_target_pairs={{0,4},{1,5},{2,6},{3,7},{4,0},{5,1},{6,2},{7,3},{8,12},{9,13},{10,... | collective-permute-start | bytes 393224 | tf_op jit(solution)/shard_map/ppermute | solution.py:21
  56.8 1.0 %collective-permute-done.21 = bf16[8,8192]{1,0:T(8,128)(2,1)S(1)} collective-permute-done((bf16[8,8192]{1,0:T(8,128)(2,1)S(1)}, bf16[8,8192]{1,0:T(8,128)(2,1)S(1)}, u32[]{:S(2)}, u32[]{:S(2)}) %collective-permute-start.21) | collective-permute-done | bytes 131104 | tf_op jit(solution)/shard_map/ppermute | solution.py:21
  57.9 3.6 %collective-permute-done.16 = bf16[8,8192]{1,0:T(8,128)(2,1)S(1)} collective-permute-done((bf16[8,8192]{1,0:T(8,128)(2,1)S(1)}, bf16[8,8192]{1,0:T(8,128)(2,1)S(1)}, u32[]{:S(2)}, u32[]{:S(2)}) %collective-permute-start.16) | collective-permute-done | bytes 131104 | tf_op jit(solution)/shard_map/ppermute | solution.py:27
  61.5 1.3 %collective-permute-start.23 = (bf16[8,8192]{1,0:T(8,128)(2,1)S(1)}, bf16[8,8192]{1,0:T(8,128)(2,1)S(1)}, u32[]{:S(2)}, u32[]{:S(2)}) collective-permute-start(bf16[8,8192]{1,0:T(8,128)(2,1)S(1)} %collective-permute-done.21), channel_id=1, source_target_pairs={{8,0},{9,1},{10,2},{11,3},{12,4},{13,5},{14,6},{15,7},{16,8},{17,9... | collective-permute-start | bytes 393224 | tf_op jit(solution)/shard_map/ppermute | solution.py:27
  62.8 1.8 %collective-permute-start.18 = (bf16[8,8192]{1,0:T(8,128)(2,1)S(1)}, bf16[8,8192]{1,0:T(8,128)(2,1)S(1)}, u32[]{:S(2)}, u32[]{:S(2)}) collective-permute-start(bf16[8,8192]{1,0:T(8,128)(2,1)S(1)} %collective-permute-done.16), channel_id=1, source_target_pairs={{0,4},{1,5},{2,6},{3,7},{4,0},{5,1},{6,2},{7,3},{8,12},{9,13},{10,... | collective-permute-start | bytes 393224 | tf_op jit(solution)/shard_map/ppermute | solution.py:21
  64.5 0.5 collective-permute-start.17
  65.1 0.0 collective-permute-done.19
  65.2 0.1 collective-permute-start.22
  65.3 3.0 %collective-permute-done.23 = bf16[8,8192]{1,0:T(8,128)(2,1)S(1)} collective-permute-done((bf16[8,8192]{1,0:T(8,128)(2,1)S(1)}, bf16[8,8192]{1,0:T(8,128)(2,1)S(1)}, u32[]{:S(2)}, u32[]{:S(2)}) %collective-permute-start.23) | collective-permute-done | bytes 131104 | tf_op jit(solution)/shard_map/ppermute | solution.py:27
  68.3 1.2 %collective-permute-done.17 = bf16[8,8192]{1,0:T(8,128)(2,1)S(1)} collective-permute-done((bf16[8,8192]{1,0:T(8,128)(2,1)S(1)}, bf16[8,8192]{1,0:T(8,128)(2,1)S(1)}, u32[]{:S(2)}, u32[]{:S(2)}) %collective-permute-start.17) | collective-permute-done | bytes 131104 | tf_op jit(solution)/shard_map/ppermute | solution.py:21
  69.5 0.0 collective-permute-done.22
  69.6 0.1 collective-permute-start.24
  69.7 1.4 %grad_own.1.own_ref = f32[64,256]{1,0:T(8,128)S(1)} custom-call(bf16[64,8192]{1,0:T(8,128)(2,1)S(1)} %constant_dynamic-update-slice_fusion.8.rows_ref, bf16[1,2,256,8192]{3,2,1,0:T(8,128)(2,1)S(1)} %copy-done.2), custom_call_target="tpu_custom_call" | custom-call | flops 268435456 | bytes 4194304 | tf_op jit(solution)/shard_map/grad_own/pallas_call | solution.py:169
  71.1 0.0 collective-permute-done.25
  71.1 0.2 collective-permute-done.24
  71.3 0.1 pad_maximum_fusion.rows_ref
  71.4 2.0 %grad_all.1 = f32[1,64,256]{2,1,0:T(8,128)} custom-call(s32[1]{0:T(128)} %bitcast.place_ref, bf16[64,8192]{1,0:T(8,128)(2,1)S(1)} %pad_maximum_fusion.rows_ref, bf16[1,2,256,8192]{3,2,1,0:T(8,128)(2,1)S(1)} %copy-done.2, f32[64,256]{1,0:T(8,128)S(1)} %grad_own.1.own_ref), custom_call_target="tpu_custom_call" | custom-call | flops 268435456 | bytes 4194304 | tf_op jit(solution)/shard_map/grad_all/pallas_call | solution.py:181
  (34 shorter events, 0.4 us)
Async XLA Ops:
  0.6 17.2 %collective-permute-start.3 = (bf16[8,8192]{1,0:T(8,128)(2,1)}, bf16[8,8192]{1,0:T(8,128)(2,1)S(1)}, u32[]{:S(2)}, u32[]{:S(2)}) collective-permute-start(bf16[8,8192]{1,0:T(8,128)(2,1)} %bitcast.11), channel_id=1, source_target_pairs={{0,1},{1,0},{2,3},{3,2},{4,5},{5,4},{6,7},{7,6},{8,9},{9,8},{10,11... | collective-permute-start | bytes 393224 | tf_op jit(solution)/shard_map/ppermute | solution.py:21
  1.1 16.1 %collective-permute-start.2 = (bf16[8,8192]{1,0:T(8,128)(2,1)}, bf16[8,8192]{1,0:T(8,128)(2,1)S(1)}, u32[]{:S(2)}, u32[]{:S(2)}) collective-permute-start(bf16[8,8192]{1,0:T(8,128)(2,1)} %bitcast.12), channel_id=1, source_target_pairs={{0,6},{1,7},{2,4},{3,5},{4,2},{5,3},{6,0},{7,1},{8,14},{9,15},{10,... | collective-permute-start | bytes 393224 | tf_op jit(solution)/shard_map/ppermute | solution.py:21
  4.7 12.6 %collective-permute-start.1 = (bf16[8,8192]{1,0:T(8,128)(2,1)}, bf16[8,8192]{1,0:T(8,128)(2,1)S(1)}, u32[]{:S(2)}, u32[]{:S(2)}) collective-permute-start(bf16[8,8192]{1,0:T(8,128)(2,1)} %bitcast.13), channel_id=1, source_target_pairs={{0,4},{1,5},{2,6},{3,7},{4,0},{5,1},{6,2},{7,3},{8,12},{9,13},{10,... | collective-permute-start | bytes 393224 | tf_op jit(solution)/shard_map/ppermute | solution.py:21
  5.2 12.6 %collective-permute-start = (bf16[8,8192]{1,0:T(8,128)(2,1)}, bf16[8,8192]{1,0:T(8,128)(2,1)S(1)}, u32[]{:S(2)}, u32[]{:S(2)}) collective-permute-start(bf16[8,8192]{1,0:T(8,128)(2,1)} %bitcast.14), channel_id=1, source_target_pairs={{0,2},{1,3},{2,0},{3,1},{4,6},{5,7},{6,4},{7,5},{8,10},{9,11},{10,... | collective-permute-start | bytes 393224 | tf_op jit(solution)/shard_map/ppermute | solution.py:21
  8.5 2.0 %copy-start.3 = (bf16[1,8192,256]{2,1,0:T(8,128)(2,1)}, bf16[1,8192,256]{2,1,0:T(8,128)(2,1)S(1)}, u32[]{:S(2)}) copy-start(bf16[1,8192,256]{2,1,0:T(8,128)(2,1)S(1)} %load_weights.2.enc_ref) | copy-start | bytes 12582916
  10.5 8.7 %copy-start.5 = (s32[1,2,2]{2,1,0:T(2,128)S(1)}, s32[1,2,2]{2,1,0:T(2,128)}, u32[]{:S(2)}) copy-start(s32[1,2,2]{2,1,0:T(2,128)} %param.9) | copy-start | bytes 52
  10.5 8.7 %copy-start.6 = (bf16[1,256]{1,0:T(2,128)(2,1)S(1)}, bf16[1,256]{1,0:T(2,128)(2,1)}, u32[]{:S(2)}) copy-start(bf16[1,256]{1,0:T(2,128)(2,1)} %bias_ref.1) | copy-start | bytes 1540
  13.9 3.3 %copy-start = (bf16[1,2,256,8192]{3,2,1,0:T(8,128)(2,1)}, bf16[1,2,256,8192]{3,2,1,0:T(8,128)(2,1)S(1)}, u32[]{:S(2)}) copy-start(bf16[1,2,256,8192]{3,2,1,0:T(8,128)(2,1)S(1)} %load_weights.3.dec_ref) | copy-start | bytes 25165828
  17.2 1.9 %collective-permute-start.6 = (bf16[8,8192]{1,0:T(8,128)(2,1)S(1)}, bf16[8,8192]{1,0:T(8,128)(2,1)S(1)}, u32[]{:S(2)}, u32[]{:S(2)}) collective-permute-start(bf16[8,8192]{1,0:T(8,128)(2,1)S(1)} %collective-permute-done.2), channel_id=1, source_target_pairs={{0,1},{1,0},{2,3},{3,2},{4,5},{5,4},{6,7},{7,6},{8,9},{9,8},{10,11... | collective-permute-start | bytes 393224 | tf_op jit(solution)/shard_map/ppermute | solution.py:21
  17.2 1.9 %collective-permute-start.5 = (bf16[8,8192]{1,0:T(8,128)(2,1)S(1)}, bf16[8,8192]{1,0:T(8,128)(2,1)S(1)}, u32[]{:S(2)}, u32[]{:S(2)}) collective-permute-start(bf16[8,8192]{1,0:T(8,128)(2,1)S(1)} %collective-permute-done.1), channel_id=1, source_target_pairs={{0,1},{1,0},{2,3},{3,2},{4,5},{5,4},{6,7},{7,6},{8,9},{9,8},{10,11... | collective-permute-start | bytes 393224 | tf_op jit(solution)/shard_map/ppermute | solution.py:21
  17.8 1.3 %collective-permute-start.4 = (bf16[8,8192]{1,0:T(8,128)(2,1)S(1)}, bf16[8,8192]{1,0:T(8,128)(2,1)S(1)}, u32[]{:S(2)}, u32[]{:S(2)}) collective-permute-start(bf16[8,8192]{1,0:T(8,128)(2,1)S(1)} %collective-permute-done), channel_id=1, source_target_pairs={{0,1},{1,0},{2,3},{3,2},{4,5},{5,4},{6,7},{7,6},{8,9},{9,8},{10,11... | collective-permute-start | bytes 393224 | tf_op jit(solution)/shard_map/ppermute | solution.py:21
  19.2 3.4 %copy-start.1 = (bf16[1,2,256,8192]{3,2,1,0:T(8,128)(2,1)S(1)}, bf16[1,2,256,8192]{3,2,1,0:T(8,128)(2,1)}, u32[]{:S(2)}) copy-start(bf16[1,2,256,8192]{3,2,1,0:T(8,128)(2,1)} %copy-done) | copy-start | bytes 25165828
  22.6 2.2 %copy-start.4 = (bf16[1,8192,256]{2,1,0:T(8,128)(2,1)S(1)}, bf16[1,8192,256]{2,1,0:T(8,128)(2,1)}, u32[]{:S(2)}) copy-start(bf16[1,8192,256]{2,1,0:T(8,128)(2,1)} %copy-done.3) | copy-start | bytes 12582916
  24.8 3.4 %copy-start.2 = (bf16[1,2,256,8192]{3,2,1,0:T(8,128)(2,1)S(1)}, bf16[1,2,256,8192]{3,2,1,0:T(8,128)(2,1)}, u32[]{:S(2)}) copy-start(bf16[1,2,256,8192]{3,2,1,0:T(8,128)(2,1)} %copy-done) | copy-start | bytes 25165828
  27.9 2.0 %collective-permute-start.10 = (bf16[32,8192]{1,0:T(8,128)(2,1)S(1)}, bf16[32,8192]{1,0:T(8,128)(2,1)S(1)}, u32[]{:S(2)}, u32[]{:S(2)}) collective-permute-start(bf16[32,8192]{1,0:T(8,128)(2,1)S(1)} %get-tuple-element.13), channel_id=1, source_target_pairs={{0,1},{1,0},{2,3},{3,2},{4,5},{5,4},{6,7},{7,6},{8,9},{9,8},{10,11... | collective-permute-start | bytes 1572872 | tf_op jit(solution)/shard_map/ppermute | solution.py:21
  29.0 8.0 %collective-permute-start.7 = (bf16[32,8192]{1,0:T(8,128)(2,1)S(1)}, bf16[32,8192]{1,0:T(8,128)(2,1)S(1)}, u32[]{:S(2)}, u32[]{:S(2)}) collective-permute-start(bf16[32,8192]{1,0:T(8,128)(2,1)S(1)} %get-tuple-element.11), channel_id=1, source_target_pairs={{0,1},{1,0},{2,3},{3,2},{4,5},{5,4},{6,7},{7,6},{8,9},{9,8},{10,11... | collective-permute-start | bytes 1572872 | tf_op jit(solution)/shard_map/ppermute | solution.py:21
  30.0 15.4 %collective-permute-start.11 = (bf16[8,8192]{1,0:T(8,128)(2,1)S(1)}, bf16[8,8192]{1,0:T(8,128)(2,1)S(1)}, u32[]{:S(2)}, u32[]{:S(2)}) collective-permute-start(bf16[8,8192]{1,0:T(8,128)(2,1)S(1)} %get-tuple-element.24), channel_id=1, source_target_pairs={{0,8},{1,9},{2,10},{3,11},{4,12},{5,13},{6,14},{7,15},{8,16},{9,17... | collective-permute-start | bytes 393224 | tf_op jit(solution)/shard_map/ppermute | solution.py:27
  33.9 5.4 %collective-permute-start.14 = (bf16[8,8192]{1,0:T(8,128)(2,1)S(1)}, bf16[8,8192]{1,0:T(8,128)(2,1)S(1)}, u32[]{:S(2)}, u32[]{:S(2)}) collective-permute-start(bf16[8,8192]{1,0:T(8,128)(2,1)S(1)} %get-tuple-element.25), channel_id=1, source_target_pairs={{0,4},{1,5},{2,6},{3,7},{4,0},{5,1},{6,2},{7,3},{8,12},{9,13},{10,... | collective-permute-start | bytes 393224 | tf_op jit(solution)/shard_map/ppermute | solution.py:21
  35.5 6.4 %collective-permute-start.13 = (bf16[8,8192]{1,0:T(8,128)(2,1)S(1)}, bf16[8,8192]{1,0:T(8,128)(2,1)S(1)}, u32[]{:S(2)}, u32[]{:S(2)}) collective-permute-start(bf16[8,8192]{1,0:T(8,128)(2,1)S(1)} %get-tuple-element.26), channel_id=1, source_target_pairs={{0,2},{1,3},{2,0},{3,1},{4,6},{5,7},{6,4},{7,5},{8,10},{9,11},{10,... | collective-permute-start | bytes 393224 | tf_op jit(solution)/shard_map/ppermute | solution.py:21
  37.0 14.8 %copy-start.8 = (bf16[1,8,8192]{2,1,0:T(8,128)(2,1)S(1)}, bf16[1,8,8192]{2,1,0:T(8,128)(2,1)}, u32[]{:S(2)}) copy-start(bf16[1,8,8192]{2,1,0:T(8,128)(2,1)} %param.11) | copy-start | bytes 393220
  37.2 9.9 %collective-permute-start.8 = (bf16[8,8192]{1,0:T(8,128)(2,1)S(1)}, bf16[8,8192]{1,0:T(8,128)(2,1)S(1)}, u32[]{:S(2)}, u32[]{:S(2)}) collective-permute-start(bf16[8,8192]{1,0:T(8,128)(2,1)S(1)} %get-tuple-element.22), channel_id=1, source_target_pairs={{0,2},{1,3},{2,0},{3,1},{4,6},{5,7},{6,4},{7,5},{8,10},{9,11},{10,... | collective-permute-start | bytes 393224 | tf_op jit(solution)/shard_map/ppermute | solution.py:21
  37.8 9.3 %collective-permute-start.9 = (bf16[8,8192]{1,0:T(8,128)(2,1)S(1)}, bf16[8,8192]{1,0:T(8,128)(2,1)S(1)}, u32[]{:S(2)}, u32[]{:S(2)}) collective-permute-start(bf16[8,8192]{1,0:T(8,128)(2,1)S(1)} %get-tuple-element.23), channel_id=1, source_target_pairs={{0,4},{1,5},{2,6},{3,7},{4,0},{5,1},{6,2},{7,3},{8,12},{9,13},{10,... | collective-permute-start | bytes 393224 | tf_op jit(solution)/shard_map/ppermute | solution.py:21
  42.0 6.0 %collective-permute-start.15 = (bf16[8,8192]{1,0:T(8,128)(2,1)S(1)}, bf16[8,8192]{1,0:T(8,128)(2,1)S(1)}, u32[]{:S(2)}, u32[]{:S(2)}) collective-permute-start(bf16[8,8192]{1,0:T(8,128)(2,1)S(1)} %fusion.1), channel_id=1, source_target_pairs={{0,8},{1,9},{2,10},{3,11},{4,12},{5,13},{6,14},{7,15},{8,16},{9,17... | collective-permute-start | bytes 393224 | tf_op jit(solution)/shard_map/ppermute | solution.py:27
  45.5 6.3 %collective-permute-start.12 = (bf16[8,8192]{1,0:T(8,128)(2,1)S(1)}, bf16[8,8192]{1,0:T(8,128)(2,1)S(1)}, u32[]{:S(2)}, u32[]{:S(2)}) collective-permute-start(bf16[8,8192]{1,0:T(8,128)(2,1)S(1)} %fusion.2), channel_id=1, source_target_pairs={{0,6},{1,7},{2,4},{3,5},{4,2},{5,3},{6,0},{7,1},{8,14},{9,15},{10,... | collective-permute-start | bytes 393224 | tf_op jit(solution)/shard_map/ppermute | solution.py:21
  51.9 19.2 %copy-start.7 = (bf16[8,8192]{1,0:T(8,128)(2,1)}, bf16[8,8192]{1,0:T(8,128)(2,1)S(1)}, u32[]{:S(2)}) copy-start(bf16[8,8192]{1,0:T(8,128)(2,1)S(1)} %get-tuple-element.17) | copy-start | bytes 393220
  51.9 5.9 %collective-permute-start.21 = (bf16[8,8192]{1,0:T(8,128)(2,1)S(1)}, bf16[8,8192]{1,0:T(8,128)(2,1)S(1)}, u32[]{:S(2)}, u32[]{:S(2)}) collective-permute-start(bf16[8,8192]{1,0:T(8,128)(2,1)S(1)} %get-tuple-element.17), channel_id=1, source_target_pairs={{0,6},{1,7},{2,4},{3,5},{4,2},{5,3},{6,0},{7,1},{8,14},{9,15},{10,... | collective-permute-start | bytes 393224 | tf_op jit(solution)/shard_map/ppermute | solution.py:21
  53.4 8.1 %collective-permute-start.16 = (bf16[8,8192]{1,0:T(8,128)(2,1)S(1)}, bf16[8,8192]{1,0:T(8,128)(2,1)S(1)}, u32[]{:S(2)}, u32[]{:S(2)}) collective-permute-start(bf16[8,8192]{1,0:T(8,128)(2,1)S(1)} %get-tuple-element.17), channel_id=1, source_target_pairs={{8,0},{9,1},{10,2},{11,3},{12,4},{13,5},{14,6},{15,7},{16,8},{17,9... | collective-permute-start | bytes 393224 | tf_op jit(solution)/shard_map/ppermute | solution.py:27
  54.7 10.4 %collective-permute-start.19 = (bf16[8,8192]{1,0:T(8,128)(2,1)S(1)}, bf16[8,8192]{1,0:T(8,128)(2,1)S(1)}, u32[]{:S(2)}, u32[]{:S(2)}) collective-permute-start(bf16[8,8192]{1,0:T(8,128)(2,1)S(1)} %get-tuple-element.17), channel_id=1, source_target_pairs={{0,2},{1,3},{2,0},{3,1},{4,6},{5,7},{6,4},{7,5},{8,10},{9,11},{10,... | collective-permute-start | bytes 393224 | tf_op jit(solution)/shard_map/ppermute | solution.py:21
  55.2 9.9 %collective-permute-start.20 = (bf16[8,8192]{1,0:T(8,128)(2,1)S(1)}, bf16[8,8192]{1,0:T(8,128)(2,1)S(1)}, u32[]{:S(2)}, u32[]{:S(2)}) collective-permute-start(bf16[8,8192]{1,0:T(8,128)(2,1)S(1)} %get-tuple-element.17), channel_id=1, source_target_pairs={{0,4},{1,5},{2,6},{3,7},{4,0},{5,1},{6,2},{7,3},{8,12},{9,13},{10,... | collective-permute-start | bytes 393224 | tf_op jit(solution)/shard_map/ppermute | solution.py:21
  61.5 6.8 %collective-permute-start.23 = (bf16[8,8192]{1,0:T(8,128)(2,1)S(1)}, bf16[8,8192]{1,0:T(8,128)(2,1)S(1)}, u32[]{:S(2)}, u32[]{:S(2)}) collective-permute-start(bf16[8,8192]{1,0:T(8,128)(2,1)S(1)} %collective-permute-done.21), channel_id=1, source_target_pairs={{8,0},{9,1},{10,2},{11,3},{12,4},{13,5},{14,6},{15,7},{16,8},{17,9... | collective-permute-start | bytes 393224 | tf_op jit(solution)/shard_map/ppermute | solution.py:27
  62.8 5.6 %collective-permute-start.18 = (bf16[8,8192]{1,0:T(8,128)(2,1)S(1)}, bf16[8,8192]{1,0:T(8,128)(2,1)S(1)}, u32[]{:S(2)}, u32[]{:S(2)}) collective-permute-start(bf16[8,8192]{1,0:T(8,128)(2,1)S(1)} %collective-permute-done.16), channel_id=1, source_target_pairs={{0,4},{1,5},{2,6},{3,7},{4,0},{5,1},{6,2},{7,3},{8,12},{9,13},{10,... | collective-permute-start | bytes 393224 | tf_op jit(solution)/shard_map/ppermute | solution.py:21
  64.5 5.0 %collective-permute-start.17 = (bf16[8,8192]{1,0:T(8,128)(2,1)S(1)}, bf16[8,8192]{1,0:T(8,128)(2,1)S(1)}, u32[]{:S(2)}, u32[]{:S(2)}) collective-permute-start(bf16[8,8192]{1,0:T(8,128)(2,1)S(1)} %collective-permute-done.16), channel_id=1, source_target_pairs={{0,2},{1,3},{2,0},{3,1},{4,6},{5,7},{6,4},{7,5},{8,10},{9,11},{10,... | collective-permute-start | bytes 393224 | tf_op jit(solution)/shard_map/ppermute | solution.py:21
  65.2 4.4 %collective-permute-start.22 = (bf16[32,8192]{1,0:T(8,128)(2,1)S(1)}, bf16[32,8192]{1,0:T(8,128)(2,1)S(1)}, u32[]{:S(2)}, u32[]{:S(2)}) collective-permute-start(bf16[32,8192]{1,0:T(8,128)(2,1)S(1)} %pad_maximum_fusion.1), channel_id=1, source_target_pairs={{0,1},{1,0},{2,3},{3,2},{4,5},{5,4},{6,7},{7,6},{8,9},{9,8},{10,11... | collective-permute-start | bytes 1572872 | tf_op jit(solution)/shard_map/ppermute | solution.py:21
  68.3 2.8 %collective-permute-start.25 = (bf16[8,8192]{1,0:T(8,128)(2,1)S(1)}, bf16[8,8192]{1,0:T(8,128)(2,1)S(1)}, u32[]{:S(2)}, u32[]{:S(2)}) collective-permute-start(bf16[8,8192]{1,0:T(8,128)(2,1)S(1)} %collective-permute-done.23), channel_id=1, source_target_pairs={{0,1},{1,0},{2,3},{3,2},{4,5},{5,4},{6,7},{7,6},{8,9},{9,8},{10,11... | collective-permute-start | bytes 393224 | tf_op jit(solution)/shard_map/ppermute | solution.py:21
  69.6 1.8 %collective-permute-start.24 = (bf16[24,8192]{1,0:T(8,128)(2,1)S(1)}, bf16[24,8192]{1,0:T(8,128)(2,1)S(1)}, u32[]{:S(2)}, u32[]{:S(2)}) collective-permute-start(bf16[24,8192]{1,0:T(8,128)(2,1)S(1)} %pad_maximum_fusion.2), channel_id=1, source_target_pairs={{0,1},{1,0},{2,3},{3,2},{4,5},{5,4},{6,7},{7,6},{8,9},{9,8},{10,11... | collective-permute-start | bytes 1179656 | tf_op jit(solution)/shard_map/ppermute | solution.py:21

commit v6 on v1

v6 whole, which is shorter than its diff:
```python
import functools

import jax
import jax.numpy as jnp
from jax import lax
from jax.experimental import pallas as pl
from jax.experimental.pallas import tpu as pltpu
from jax.sharding import PartitionSpec as P

BLOCK = 128
LAYERS = 4
TILE = 32
CORES = 2
PARTS = 2
CHUNK = 1024
LIMIT = 20 << 20
AXIS = "layer"

ANY_SPEC = pl.BlockSpec(memory_space=pl.ANY)
VMEM_SPEC = pl.BlockSpec(memory_space=pltpu.VMEM)
SMEM_SPEC = pl.BlockSpec(memory_space=pltpu.SMEM)


def swap(value, mask):
    pairs = [(source, source ^ mask) for source in range(lax.axis_size(AXIS))]
    return lax.ppermute(value, AXIS, pairs)


def swap_inner(value, group):
    pairs = []
    for low in range(1, LAYERS - 1, 2):
        for i in range(low * group, (low + 1) * group):
            pairs += [(i, i + group), (i + group, i)]
    return lax.ppermute(value, AXIS, pairs)


def in_vmem(*arrays):
    return [pltpu.with_memory_space_constraint(a, pltpu.VMEM) for a in arrays]


def in_hbm(*arrays):
    return [pltpu.with_memory_space_constraint(a, pltpu.HBM) for a in arrays]


def slab_of(place_ref, block, chips):
    return place_ref[0] ^ (CORES * (block % chips) + block // chips)


def load_kernel(tokens, place_ref, active_ref, enc_hbm, dec_hbm, gate_ref, enc_ref, *rest):
    dec_refs, sems = rest[:-1], rest[-1]
    width = dec_refs[0].shape[2]
    copies = [pltpu.make_async_copy(enc_hbm.at[0], enc_ref, sems.at[0])]
    for i, dec_ref in enumerate(dec_refs):
        source = dec_hbm.at[0, :, :, pl.ds(i * width, width)]
        copies.append(pltpu.make_async_copy(source, dec_ref, sems.at[i + 1]))
    for copy in copies:
        copy.start()
    group = gate_ref.shape[0] // tokens
    for block in range(group):
        tile = (slab_of(place_ref, block, group // CORES) * tokens) // TILE
        for part in range(active_ref.shape[1]):
            live = active_ref[tile, part].astype(jnp.float32)
            gate_ref[pl.ds(block * tokens, tokens), pl.ds(part * BLOCK, BLOCK)] = jnp.full((tokens, BLOCK), live)
    for copy in copies:
        copy.wait()


def loaded(place, active, enc, dec, tokens, group):
    _, depth, features = enc.shape
    _, reach, _, width = dec.shape
    dtype = enc.dtype
    return pl.pallas_call(
        functools.partial(load_kernel, tokens),
        out_shape=[pltpu.VMEM((group * tokens, features), jnp.float32), pltpu.VMEM((depth, features), dtype)]
        + [pltpu.VMEM((reach, features, width // PARTS), dtype)] * PARTS,
        in_specs=[SMEM_SPEC] * 2 + [ANY_SPEC] * 2,
        out_specs=[VMEM_SPEC] * (PARTS + 2),
        scratch_shapes=[pltpu.SemaphoreType.DMA((PARTS + 1,))],
        compiler_params=pltpu.CompilerParams(vmem_limit_bytes=1 << 20),
        cost_estimate=pl.CostEstimate(flops=0, bytes_accessed=4 * (enc.size + dec.size), transcendentals=0),
        name="load_weights",
    )(place, active, *in_hbm(enc, dec))


def decode_kernel(tokens, codes_ref, dec_ref, near_ref, far_ref):
    half = near_ref.shape[0]
    for step in range(near_ref.shape[1] // CHUNK):
        columns = pl.ds(step * CHUNK, CHUNK)
        own, later = [
            jnp.dot(codes_ref[...], dec_ref[reach, :, columns], preferred_element_type=jnp.float32)
            for reach in range(2)
        ]
        mixed = []
        for row in range(0, own.shape[0], tokens):
            mixed += [later[row : row + tokens], own[row : row + tokens]]
        mixed = jnp.concatenate(mixed, axis=0)
        near_ref[:, columns] = mixed[:half]
        far_ref[:, columns] = mixed[half:].astype(jnp.bfloat16)


def decoded(codes, dec, tokens):
    rows, features = codes.shape
    reach, _, width = dec.shape
    half = reach * rows // CORES
    return pl.pallas_call(
        functools.partial(decode_kernel, tokens),
        out_shape=[pltpu.VMEM((half, width), jnp.float32), pltpu.VMEM((half, width), jnp.bfloat16)],
        in_specs=[VMEM_SPEC] * 2,
        out_specs=[VMEM_SPEC] * 2,
        compiler_params=pltpu.CompilerParams(vmem_limit_bytes=LIMIT),
        cost_estimate=pl.CostEstimate(flops=4 * rows * width * features, bytes_accessed=2 * dec.size, transcendentals=0),
        name="decode",
    )(*in_vmem(codes, dec))


def grad_part(tokens, near_ref, far_ref, dec_ref, blocks):
    out = []
    for rows_ref in (near_ref, far_ref):
        here, after = [
            lax.dot_general(
                rows_ref[...], dec_ref[reach], (((1,), (1,)), ((), ())), preferred_element_type=jnp.float32
            )
            for reach in range(2)
        ]
        for row in range(0, here.shape[0], 2 * tokens):
            out.append(here[row : row + tokens] + after[row + tokens : row + 2 * tokens])
    return out if blocks is None else [a + b for a, b in zip(blocks, out)]


def grad_first_kernel(tokens, near_ref, far_ref, dec_ref, out_ref, used_ref):
    blocks = grad_part(tokens, near_ref, far_ref, dec_ref, None)
    for i, block in enumerate(blocks):
        out_ref[pl.ds(i * tokens, tokens), :] = block
    used_ref[...] = jnp.zeros(used_ref.shape, jnp.float32)


def grad_last_kernel(tokens, place_ref, near_ref, far_ref, dec_ref, so_far_ref, out_ref):
    group = so_far_ref.shape[0] // tokens
    so_far = [so_far_ref[pl.ds(i * tokens, tokens), :] for i in range(group)]
    blocks = grad_part(tokens, near_ref, far_ref, dec_ref, so_far)
    for i, block in enumerate(blocks):
        slab = slab_of(place_ref, i, group // CORES)
        out_ref[0, pl.ds(pl.multiple_of(slab * tokens, tokens), tokens), :] = block


def grad_cost(near, dec):
    return pl.CostEstimate(flops=4 * near.size * dec.shape[1], bytes_accessed=2 * dec.size, transcendentals=0)


def grad_first(near, far, dec, tokens):
    return pl.pallas_call(
        functools.partial(grad_first_kernel, tokens),
        out_shape=[pltpu.VMEM((near.shape[0], dec.shape[1]), jnp.float32), pltpu.VMEM((8, 128), jnp.float32)],
        in_specs=[VMEM_SPEC] * 3,
        out_specs=[VMEM_SPEC] * 2,
        compiler_params=pltpu.CompilerParams(vmem_limit_bytes=LIMIT),
        cost_estimate=grad_cost(near, dec),
        name="grad_first",
    )(*in_vmem(near, far, dec))[0]


def grad_last(place, near, far, dec, so_far, tokens):
    return pl.pallas_call(
        functools.partial(grad_last_kernel, tokens),
        out_shape=jax.ShapeDtypeStruct((1,) + so_far.shape, jnp.float32),
        in_specs=[SMEM_SPEC] + [VMEM_SPEC] * 4,
        out_specs=VMEM_SPEC,
        compiler_params=pltpu.CompilerParams(vmem_limit_bytes=LIMIT),
        cost_estimate=grad_cost(near, dec),
        name="grad_last",
    )(place, *in_vmem(near, far, dec, so_far))


def reduced(near, far, chips):
    rows = near.shape[0] // chips
    total = near + swap(far, 1).astype(jnp.float32)
    sent = [total[chip * rows : (chip + 1) * rows].astype(jnp.bfloat16) for chip in range(chips)]
    came = [swap(sent[chip], CORES * chip) for chip in range(1, chips)]
    out = total[:rows]
    for block in came:
        out = out + block.astype(jnp.float32)
    return out


def exchanged(later_sum, own_less, layer, group):
    even = layer % 2 == 0
    up, down = later_sum.astype(jnp.bfloat16), own_less.astype(jnp.bfloat16)
    outer = swap(jnp.where(even, up, down), group)
    inner = swap_inner(jnp.where(even, down, up), group)
    below = jnp.where(even, inner, outer).astype(jnp.float32)
    above = jnp.where(even, outer, inner).astype(jnp.float32)
    here = (own_less + below).astype(jnp.bfloat16)
    after = jnp.where(layer == LAYERS - 1, 0.0, later_sum + above).astype(jnp.bfloat16)
    return here, after


def on_device(resid, enc_weight, enc_bias, active, dec_weight, target):
    group = lax.axis_size(AXIS) // LAYERS
    chips = group // CORES
    index = lax.axis_index(AXIS)
    layer = index // group
    place = (index % group).astype(jnp.int32).reshape(1)
    tokens = resid.shape[1]
    gate, enc, *decs = loaded(place, active[0], enc_weight, dec_weight, tokens, group)
    near = [resid[0]] + [swap(resid[0], CORES * chip) for chip in range(1, chips)]
    others = jnp.concatenate(near[1:], axis=0)
    x = jnp.concatenate(near + [swap(near[0], 1), swap(others, 1)], axis=0)
    pre = jnp.dot(x, enc, preferred_element_type=jnp.float32) + enc_bias.astype(jnp.float32)
    codes = (jax.nn.relu(pre) * gate).astype(jnp.bfloat16)

    width = decs[0].shape[2]
    parts = [decoded(codes, dec, tokens) for dec in decs]
    sums = [reduced(*part, chips) for part in parts]
    errors, grad = [], None
    for i, total in enumerate(sums):
        wanted = target[0, :, i * width : (i + 1) * width].astype(jnp.float32)
        here, after = exchanged(total[:tokens], total[tokens:] - wanted, layer, group)
        errors.append(here)
        both = jnp.concatenate([here, after], axis=0)
        near = jnp.concatenate([both] + [swap(both, CORES * chip) for chip in range(1, chips)], axis=0)
        far = swap(near, 1)
        if i < PARTS - 1:
            grad = grad_first(near, far, decs[i], tokens)
        else:
            grad = grad_last(place, near, far, decs[i], grad, tokens)
    return (jnp.concatenate(errors, axis=1)[None], grad)


def solution(mesh):
    return jax.shard_map(
        on_device,
        mesh=mesh,
        in_specs=(
            P("layer", "groups", None),
            P("layer", None, None),
            P("layer", None),
            P("layer", "groups", None),
            P("layer", None, None, None),
            P("layer", "groups", None),
        ),
        out_specs=(P("layer", "groups", None), P("layer", "groups", None)),
        check_vma=False,
    )
```

time: 68.8 us -> 68.4 us (level); the launches traced: 67.5 us -> 68.2 us
  matrix products: 14.7 us -> 0.8 us
  Pallas kernels: 0 us -> 13.2 us
  waiting for transfers between devices: 20.5 us -> 12.9 us
  starting transfers between devices: 26.6 us -> 32.3 us
  local copies, waits for them, and re-layouts: 2.2 us -> 5.98 us
    dot_general x5 -> x1, matrix products: 14.7 us -> 0.8 us  [on_device(): jnp.dot(x, enc, preferred_element_type=jnp.float32)]
    pallas_call x0 -> x5, Pallas kernels: none -> 13.2 us  [the longest x1 5.23 us: loaded(): pl.pallas_call(functools.partial(load_kernel, tokens), out_shape=[pltpu.V...]
    ppermute x29 -> x23, starting transfers between devices: 21.8 us -> 31 us  [swap(): return lax.ppermute(value, AXIS, pairs)]
    unnamed x27 -> x23, local copies, waits for them, and re-layouts: 1.25 us -> 5.88 us
    ppermute x29 -> x23, waiting for transfers between devices: 16.9 us -> 12.9 us  [swap(): return lax.ppermute(value, AXIS, pairs)]
    ppermute x2, waiting for transfers between devices: 3.62 us -> 0.01 us  [swap_inner(): return lax.ppermute(value, AXIS, pairs)]
    ppermute x2, starting transfers between devices: 4.78 us -> 1.32 us  [swap_inner(): return lax.ppermute(value, AXIS, pairs)]
    reduce_sum x1 -> x0, other arithmetic: 0.76 us -> none  [on_device(): live = jnp.sum(pick[:, :, None] * active[0][None, :, :], axis=1)]
  transfers between devices with their start and end apart: 31 -> 25, of which waited for: 15 -> 8; matrix products, arithmetic and copies ran while one was open for 12% -> 4% of each run, Pallas kernels for 0% -> 13%
where the time goes in v6:
time: 68.4 us; the launch traced here: 68.2 us
  starting transfers between devices  32.3 us (47%)
  Pallas kernels  13.2 us (19%)
  waiting for transfers between devices  12.9 us (19%)
  local copies, waits for them, and re-layouts  5.98 us (9%)
  other arithmetic  1.93 us (3%)
  between operations  1 us (1%)
  matrix products  0.8 us (1%)
    ppermute x23, starting transfers between devices, swap(): return lax.ppermute(value, AXIS, pairs)  31 us
    ppermute x23, waiting for transfers between devices, swap(): return lax.ppermute(value, AXIS, pairs)  12.9 us
    unnamed x23, local copies, waits for them, and re-layouts  5.88 us
    pallas_call x1, Pallas kernels, loaded(): pl.pallas_call(functools.partial(load_kernel, tokens), out_shape=[pltpu.V...  5.23 us
    pallas_call x1, Pallas kernels, grad_last(): pl.pallas_call(functools.partial(grad_last_kernel, tokens), out_shape=jax...  3.28 us
    pallas_call x1, Pallas kernels, grad_first(): pl.pallas_call(functools.partial(grad_first_kernel, tokens), out_shape=[p...  3.04 us
    pallas_call x2, Pallas kernels, decoded(): pl.pallas_call(functools.partial(decode_kernel, tokens), out_shape=[pltpu...  1.68 us
  transfers between devices with their start and end apart: 25, of which 8 were waited for; matrix products, arithmetic and copies ran while one was open for 4% of the time, Pallas kernels for 13%

profile of v6, /device:TPU:0, one launch (start us, length us, event | category | flops | bytes accessed | tf_op | source)
XLA Modules:
  0.0 68.2 jit_solution(2644557898296134466)
XLA Ops:
  0.6 0.5 collective-permute-start.3
  1.1 3.5 %collective-permute-start.2 = (bf16[8,8192]{1,0:T(8,128)(2,1)}, bf16[8,8192]{1,0:T(8,128)(2,1)S(1)}, u32[]{:S(2)}, u32[]{:S(2)}) collective-permute-start(bf16[8,8192]{1,0:T(8,128)(2,1)} %bitcast.29), channel_id=1, source_target_pairs={{0,6},{1,7},{2,4},{3,5},{4,2},{5,3},{6,0},{7,1},{8,14},{9,15},{10,... | collective-permute-start | bytes 393224 | tf_op jit(solution)/shard_map/ppermute | solution.py:26
  4.7 0.5 collective-permute-start.1
  5.2 0.1 collective-permute-start
  5.3 0.9 %constant_dynamic-update-slice_fusion.5 = bf16[64,8192]{1,0:T(8,128)(2,1)S(1)} fusion(bf16[1,8,8192]{2,1,0:T(8,128)(2,1)} %param.6), kind=kLoop, calls=%fused_computation.35 | loop fusion | bytes 262144
  6.3 0.7 %add.76 = f32[1,256]{1,0:T(1,128)S(1)} convert(bf16[1,256]{1,0:T(2,128)(2,1)} %param.8) | non-fusion elementwise | flops 256 | bytes 1536 | tf_op jit(solution)/shard_map/add | solution.py:208
  7.0 0.7 copy-done.5
  7.6 5.2 %load_weights.1 = (f32[64,256]{1,0:T(8,128)S(1)}, bf16[8192,256]{1,0:T(8,128)(2,1)S(1)}, bf16[2,256,4096]{2,1,0:T(8,128)(2,1)S(1)}, bf16[2,256,4096]{2,1,0:T(8,128)(2,1)S(1)}) custom-call(s32[1]{0:T(128)} %bitcast.1.place_ref, s32[2,2]{1,0:T(2,128)S(1)} %bitcast.27, bf16[1,8192,256]{2,1,0:T(8,128)(2,1)} %enc_hbm.1, bf16[1,2,256,8192]{3,2,1,0:T(8,128)(2,1)} %dec_hbm.1), custom_call_target="tpu_custom_call" | custom-call | bytes 25165824 | tf_op jit(solution)/shard_map/load_weights/pallas_call | solution.py:72
  12.9 2.0 %copy-done.2 = bf16[2,256,4096]{2,1,0:T(8,128)(2,1)} copy-done((bf16[2,256,4096]{2,1,0:T(8,128)(2,1)}, bf16[2,256,4096]{2,1,0:T(8,128)(2,1)S(1)}, u32[]{:S(2)}) %copy-start.2) | copy-done | bytes 4194328
  14.9 0.0 collective-permute-done.2
  14.9 0.0 collective-permute-done.1
  14.9 0.0 collective-permute-done
  14.9 0.1 collective-permute-start.4
  15.1 0.0 collective-permute-done.3
  15.1 1.6 %collective-permute-done.4 = bf16[24,8192]{1,0:T(8,128)(2,1)S(1)} collective-permute-done((bf16[24,8192]{1,0:T(8,128)(2,1)S(1)}, bf16[24,8192]{1,0:T(8,128)(2,1)S(1)}, u32[]{:S(2)}, u32[]{:S(2)}) %collective-permute-start.4) | collective-permute-done | bytes 393248 | tf_op jit(solution)/shard_map/ppermute | solution.py:26
  16.7 0.8 %fusion.2.codes_ref = bf16[64,256]{1,0:T(8,128)(2,1)S(1)} fusion(f32[64,256]{1,0:T(8,128)S(1)} %get-tuple-element.12, bf16[64,8192]{1,0:T(8,128)(2,1)S(1)} %constant_dynamic-update-slice_fusion, bf16[8192,256]{1,0:T(8,128)(2,1)S(1)} %get-tuple-element.11, f32[256]{0:T(256)S(1)} %bitcast.32), kind=kOutput, calls=%fused_computation.3 | convolution fusion | flops 268500992 | bytes 5342208 | tf_op jit(solution)/shard_map/dot_general | solution.py:208
  17.5 0.8 %decode.2 = (f32[64,4096]{1,0:T(8,128)S(1)}, bf16[64,4096]{1,0:T(8,128)(2,1)S(1)}) custom-call(bf16[64,256]{1,0:T(8,128)(2,1)S(1)} %fusion.2.codes_ref, bf16[2,256,4096]{2,1,0:T(8,128)(2,1)S(1)} %get-tuple-element.13.dec_ref), custom_call_target="tpu_custom_call" | custom-call | flops 268435456 | bytes 4194304 | tf_op jit(solution)/shard_map/decode/pallas_call | solution.py:105
  18.4 0.2 collective-permute-start.5
  18.6 2.2 %copy-done.3 = bf16[2,256,4096]{2,1,0:T(8,128)(2,1)S(1)} copy-done((bf16[2,256,4096]{2,1,0:T(8,128)(2,1)S(1)}, bf16[2,256,4096]{2,1,0:T(8,128)(2,1)}, u32[]{:S(2)}) %copy-start.3) | copy-done | bytes 4194328
  20.8 0.8 %decode.3 = (f32[64,4096]{1,0:T(8,128)S(1)}, bf16[64,4096]{1,0:T(8,128)(2,1)S(1)}) custom-call(bf16[64,256]{1,0:T(8,128)(2,1)S(1)} %fusion.2.codes_ref, bf16[2,256,4096]{2,1,0:T(8,128)(2,1)S(1)} %copy-done.3), custom_call_target="tpu_custom_call" | custom-call | flops 268435456 | bytes 4194304 | tf_op jit(solution)/shard_map/decode/pallas_call | solution.py:105
  21.6 0.4 collective-permute-start.11
  22.1 0.0 collective-permute-done.5
  22.1 0.1 fusion.9
  22.3 1.9 %collective-permute-start.6 = (bf16[16,4096]{1,0:T(8,128)(2,1)S(1)}, bf16[16,4096]{1,0:T(8,128)(2,1)S(1)}, u32[]{:S(2)}, u32[]{:S(2)}) collective-permute-start(bf16[16,4096]{1,0:T(8,128)(2,1)S(1)} %get-tuple-element.32), channel_id=1, source_target_pairs={{0,2},{1,3},{2,0},{3,1},{4,6},{5,7},{6,4},{7,5},{8,10},{9,11},{10,... | collective-permute-start | bytes 393224 | tf_op jit(solution)/shard_map/ppermute | solution.py:26
  24.2 1.5 %collective-permute-start.8 = (bf16[16,4096]{1,0:T(8,128)(2,1)S(1)}, bf16[16,4096]{1,0:T(8,128)(2,1)S(1)}, u32[]{:S(2)}, u32[]{:S(2)}) collective-permute-start(bf16[16,4096]{1,0:T(8,128)(2,1)S(1)} %get-tuple-element.33), channel_id=1, source_target_pairs={{0,6},{1,7},{2,4},{3,5},{4,2},{5,3},{6,0},{7,1},{8,14},{9,15},{10,... | collective-permute-start | bytes 393224 | tf_op jit(solution)/shard_map/ppermute | solution.py:26
  25.7 0.1 collective-permute-start.7
  25.8 0.0 collective-permute-done.11
  25.8 0.1 fusion.10
  26.0 1.9 %collective-permute-start.12 = (bf16[16,4096]{1,0:T(8,128)(2,1)S(1)}, bf16[16,4096]{1,0:T(8,128)(2,1)S(1)}, u32[]{:S(2)}, u32[]{:S(2)}) collective-permute-start(bf16[16,4096]{1,0:T(8,128)(2,1)S(1)} %get-tuple-element.35), channel_id=1, source_target_pairs={{0,2},{1,3},{2,0},{3,1},{4,6},{5,7},{6,4},{7,5},{8,10},{9,11},{10,... | collective-permute-start | bytes 393224 | tf_op jit(solution)/shard_map/ppermute | solution.py:26
  27.9 1.5 %collective-permute-start.14 = (bf16[16,4096]{1,0:T(8,128)(2,1)S(1)}, bf16[16,4096]{1,0:T(8,128)(2,1)S(1)}, u32[]{:S(2)}, u32[]{:S(2)}) collective-permute-start(bf16[16,4096]{1,0:T(8,128)(2,1)S(1)} %get-tuple-element.36), channel_id=1, source_target_pairs={{0,6},{1,7},{2,4},{3,5},{4,2},{5,3},{6,0},{7,1},{8,14},{9,15},{10,... | collective-permute-start | bytes 393224 | tf_op jit(solution)/shard_map/ppermute | solution.py:26
  29.4 0.0 collective-permute-done.6
  29.4 1.1 %collective-permute-start.13 = (bf16[16,4096]{1,0:T(8,128)(2,1)S(1)}, bf16[16,4096]{1,0:T(8,128)(2,1)S(1)}, u32[]{:S(2)}, u32[]{:S(2)}) collective-permute-start(bf16[16,4096]{1,0:T(8,128)(2,1)S(1)} %get-tuple-element.37), channel_id=1, source_target_pairs={{0,4},{1,5},{2,6},{3,7},{4,0},{5,1},{6,2},{7,3},{8,12},{9,13},{10,... | collective-permute-start | bytes 393224 | tf_op jit(solution)/shard_map/ppermute | solution.py:26
  30.6 2.3 %collective-permute-done.8 = bf16[16,4096]{1,0:T(8,128)(2,1)S(1)} collective-permute-done((bf16[16,4096]{1,0:T(8,128)(2,1)S(1)}, bf16[16,4096]{1,0:T(8,128)(2,1)S(1)}, u32[]{:S(2)}, u32[]{:S(2)}) %collective-permute-start.8) | collective-permute-done | bytes 131104 | tf_op jit(solution)/shard_map/ppermute | solution.py:26
  32.9 2.1 %collective-permute-done.7 = bf16[16,4096]{1,0:T(8,128)(2,1)S(1)} collective-permute-done((bf16[16,4096]{1,0:T(8,128)(2,1)S(1)}, bf16[16,4096]{1,0:T(8,128)(2,1)S(1)}, u32[]{:S(2)}, u32[]{:S(2)}) %collective-permute-start.7) | collective-permute-done | bytes 131104 | tf_op jit(solution)/shard_map/ppermute | solution.py:26
  34.9 0.1 fusion.6
  35.0 1.6 %collective-permute-start.10 = (bf16[8,4096]{1,0:T(8,128)(2,1)S(1)}, bf16[8,4096]{1,0:T(8,128)(2,1)S(1)}, u32[]{:S(2)}, u32[]{:S(2)}) collective-permute-start(bf16[8,4096]{1,0:T(8,128)(2,1)S(1)} %get-tuple-element.38), channel_id=1, source_target_pairs={{0,8},{1,9},{2,10},{3,11},{4,12},{5,13},{6,14},{7,15},{8,0},{9,1},... | collective-permute-start | bytes 196616 | tf_op jit(solution)/shard_map/ppermute | solution.py:26
  36.7 0.7 collective-permute-start.9
  37.3 0.0 collective-permute-done.12
  37.3 0.4 collective-permute-done.14
  37.8 1.3 %collective-permute-done.13 = bf16[16,4096]{1,0:T(8,128)(2,1)S(1)} collective-permute-done((bf16[16,4096]{1,0:T(8,128)(2,1)S(1)}, bf16[16,4096]{1,0:T(8,128)(2,1)S(1)}, u32[]{:S(2)}, u32[]{:S(2)}) %collective-permute-start.13) | collective-permute-done | bytes 131104 | tf_op jit(solution)/shard_map/ppermute | solution.py:26
  39.1 0.1 fusion.4
  39.1 0.2 collective-permute-done.10
  39.4 0.0 collective-permute-done.9
  39.4 0.1 constant_dynamic-update-slice_fusion.15
  39.4 0.7 collective-permute-start.15
  40.1 7.9 %collective-permute-start.16 = (bf16[8,4096]{1,0:T(8,128)(2,1)S(1)}, bf16[8,4096]{1,0:T(8,128)(2,1)S(1)}, u32[]{:S(2)}, u32[]{:S(2)}) collective-permute-start(bf16[8,4096]{1,0:T(8,128)(2,1)S(1)} %get-tuple-element.43), channel_id=1, source_target_pairs={{0,8},{1,9},{2,10},{3,11},{4,12},{5,13},{6,14},{7,15},{8,0},{9,1},... | collective-permute-start | bytes 196616 | tf_op jit(solution)/shard_map/ppermute | solution.py:26
  48.0 1.5 %collective-permute-start.23 = (bf16[16,4096]{1,0:T(8,128)(2,1)S(1)}, bf16[16,4096]{1,0:T(8,128)(2,1)S(1)}, u32[]{:S(2)}, u32[]{:S(2)}) collective-permute-start(bf16[16,4096]{1,0:T(8,128)(2,1)S(1)} %pad_maximum_fusion.2), channel_id=1, source_target_pairs={{0,6},{1,7},{2,4},{3,5},{4,2},{5,3},{6,0},{7,1},{8,14},{9,15},{10,... | collective-permute-start | bytes 393224 | tf_op jit(solution)/shard_map/ppermute | solution.py:26
  49.5 1.5 %collective-permute-start.22 = (bf16[16,4096]{1,0:T(8,128)(2,1)S(1)}, bf16[16,4096]{1,0:T(8,128)(2,1)S(1)}, u32[]{:S(2)}, u32[]{:S(2)}) collective-permute-start(bf16[16,4096]{1,0:T(8,128)(2,1)S(1)} %pad_maximum_fusion.2), channel_id=1, source_target_pairs={{0,4},{1,5},{2,6},{3,7},{4,0},{5,1},{6,2},{7,3},{8,12},{9,13},{10,... | collective-permute-start | bytes 393224 | tf_op jit(solution)/shard_map/ppermute | solution.py:26
  51.1 0.5 collective-permute-start.21
  51.6 0.0 collective-permute-done.15
  51.6 0.0 collective-permute-done.16
  51.7 1.5 %collective-permute-start.19 = (bf16[16,4096]{1,0:T(8,128)(2,1)S(1)}, bf16[16,4096]{1,0:T(8,128)(2,1)S(1)}, u32[]{:S(2)}, u32[]{:S(2)}) collective-permute-start(bf16[16,4096]{1,0:T(8,128)(2,1)S(1)} %pad_maximum_fusion.1), channel_id=1, source_target_pairs={{0,6},{1,7},{2,4},{3,5},{4,2},{5,3},{6,0},{7,1},{8,14},{9,15},{10,... | collective-permute-start | bytes 393224 | tf_op jit(solution)/shard_map/ppermute | solution.py:26
  53.2 1.5 %collective-permute-start.18 = (bf16[16,4096]{1,0:T(8,128)(2,1)S(1)}, bf16[16,4096]{1,0:T(8,128)(2,1)S(1)}, u32[]{:S(2)}, u32[]{:S(2)}) collective-permute-start(bf16[16,4096]{1,0:T(8,128)(2,1)S(1)} %pad_maximum_fusion.1), channel_id=1, source_target_pairs={{0,4},{1,5},{2,6},{3,7},{4,0},{5,1},{6,2},{7,3},{8,12},{9,13},{10,... | collective-permute-start | bytes 393224 | tf_op jit(solution)/shard_map/ppermute | solution.py:26
  54.7 1.3 %collective-permute-done.21 = bf16[16,4096]{1,0:T(8,128)(2,1)S(1)} collective-permute-done((bf16[16,4096]{1,0:T(8,128)(2,1)S(1)}, bf16[16,4096]{1,0:T(8,128)(2,1)S(1)}, u32[]{:S(2)}, u32[]{:S(2)}) %collective-permute-start.21) | collective-permute-done | bytes 131104 | tf_op jit(solution)/shard_map/ppermute | solution.py:26
  56.0 1.2 %collective-permute-start.17 = (bf16[16,4096]{1,0:T(8,128)(2,1)S(1)}, bf16[16,4096]{1,0:T(8,128)(2,1)S(1)}, u32[]{:S(2)}, u32[]{:S(2)}) collective-permute-start(bf16[16,4096]{1,0:T(8,128)(2,1)S(1)} %pad_maximum_fusion.1), channel_id=1, source_target_pairs={{0,2},{1,3},{2,0},{3,1},{4,6},{5,7},{6,4},{7,5},{8,10},{9,11},{10,... | collective-permute-start | bytes 393224 | tf_op jit(solution)/shard_map/ppermute | solution.py:26
  57.3 0.0 collective-permute-done.22
  57.3 0.1 collective-permute-start.24
  57.4 3.6 %collective-permute-done.17 = bf16[16,4096]{1,0:T(8,128)(2,1)S(1)} collective-permute-done((bf16[16,4096]{1,0:T(8,128)(2,1)S(1)}, bf16[16,4096]{1,0:T(8,128)(2,1)S(1)}, u32[]{:S(2)}, u32[]{:S(2)}) %collective-permute-start.17) | collective-permute-done | bytes 131104 | tf_op jit(solution)/shard_map/ppermute | solution.py:26
  61.0 0.0 collective-permute-done.18
  61.1 0.0 collective-permute-done.19
  61.1 0.1 collective-permute-start.20
  61.2 0.7 maximum_bitcast_fusion
  61.8 3.0 %grad_first.1 = (f32[64,256]{1,0:T(8,128)S(1)}, f32[8,128]{1,0:T(8,128)}) custom-call(bf16[64,4096]{1,0:T(8,128)(2,1)S(1)} %constant_dynamic-update-slice_fusion.11.near_ref, bf16[64,4096]{1,0:T(8,128)(2,1)S(1)} %collective-permute-done.24.far_ref, bf16[2,256,4096]{2,1,0:T(8,128)(2,1)S(1)} %copy-done.1), custom_call_target="tpu_custom_call" | custom-call | flops 268435456 | bytes 4194304 | tf_op jit(solution)/shard_map/grad_first/pallas_call | solution.py:151
  64.9 3.3 %grad_last.1 = f32[1,64,256]{2,1,0:T(8,128)} custom-call(s32[1]{0:T(128)} %bitcast.1.place_ref, bf16[64,4096]{1,0:T(8,128)(2,1)S(1)} %constant_dynamic-update-slice_fusion.6.near_ref, bf16[64,4096]{1,0:T(8,128)(2,1)S(1)} %collective-permute-done.20.far_ref, bf16[2,256,4096]{2,1,0:T(8,128)(2,1)S(1)} %copy-done.4, f32[64,256]{1,0:T(8,128)S(1)} %get-tuple-element.19.so_far_ref), custom_call_target="tpu_custom_call" | custom-call | flops 268435456 | bytes 4194304 | tf_op jit(solution)/shard_map/grad_last/pallas_call | solution.py:163
  (34 shorter events, 0.4 us)
Async XLA Ops:
  0.6 14.4 %collective-permute-start.3 = (bf16[8,8192]{1,0:T(8,128)(2,1)}, bf16[8,8192]{1,0:T(8,128)(2,1)S(1)}, u32[]{:S(2)}, u32[]{:S(2)}) collective-permute-start(bf16[8,8192]{1,0:T(8,128)(2,1)} %bitcast.28), channel_id=1, source_target_pairs={{0,1},{1,0},{2,3},{3,2},{4,5},{5,4},{6,7},{7,6},{8,9},{9,8},{10,11... | collective-permute-start | bytes 393224 | tf_op jit(solution)/shard_map/ppermute | solution.py:26
  1.1 13.7 %collective-permute-start.2 = (bf16[8,8192]{1,0:T(8,128)(2,1)}, bf16[8,8192]{1,0:T(8,128)(2,1)S(1)}, u32[]{:S(2)}, u32[]{:S(2)}) collective-permute-start(bf16[8,8192]{1,0:T(8,128)(2,1)} %bitcast.29), channel_id=1, source_target_pairs={{0,6},{1,7},{2,4},{3,5},{4,2},{5,3},{6,0},{7,1},{8,14},{9,15},{10,... | collective-permute-start | bytes 393224 | tf_op jit(solution)/shard_map/ppermute | solution.py:26
  4.7 10.2 %collective-permute-start.1 = (bf16[8,8192]{1,0:T(8,128)(2,1)}, bf16[8,8192]{1,0:T(8,128)(2,1)S(1)}, u32[]{:S(2)}, u32[]{:S(2)}) collective-permute-start(bf16[8,8192]{1,0:T(8,128)(2,1)} %bitcast.30), channel_id=1, source_target_pairs={{0,4},{1,5},{2,6},{3,7},{4,0},{5,1},{6,2},{7,3},{8,12},{9,13},{10,... | collective-permute-start | bytes 393224 | tf_op jit(solution)/shard_map/ppermute | solution.py:26
  5.2 9.7 %collective-permute-start = (bf16[8,8192]{1,0:T(8,128)(2,1)}, bf16[8,8192]{1,0:T(8,128)(2,1)S(1)}, u32[]{:S(2)}, u32[]{:S(2)}) collective-permute-start(bf16[8,8192]{1,0:T(8,128)(2,1)} %bitcast.31), channel_id=1, source_target_pairs={{0,2},{1,3},{2,0},{3,1},{4,6},{5,7},{6,4},{7,5},{8,10},{9,11},{10,... | collective-permute-start | bytes 393224 | tf_op jit(solution)/shard_map/ppermute | solution.py:26
  7.0 0.7 copy-start.5
  12.9 2.0 %copy-start.2 = (bf16[2,256,4096]{2,1,0:T(8,128)(2,1)}, bf16[2,256,4096]{2,1,0:T(8,128)(2,1)S(1)}, u32[]{:S(2)}) copy-start(bf16[2,256,4096]{2,1,0:T(8,128)(2,1)S(1)} %get-tuple-element.16.dec_ref) | copy-start | bytes 12582916
  14.9 3.5 %copy-start = (bf16[2,256,4096]{2,1,0:T(8,128)(2,1)}, bf16[2,256,4096]{2,1,0:T(8,128)(2,1)S(1)}, u32[]{:S(2)}) copy-start(bf16[2,256,4096]{2,1,0:T(8,128)(2,1)S(1)} %get-tuple-element.13.dec_ref) | copy-start | bytes 12582916
  14.9 1.8 %collective-permute-start.4 = (bf16[24,8192]{1,0:T(8,128)(2,1)S(1)}, bf16[24,8192]{1,0:T(8,128)(2,1)S(1)}, u32[]{:S(2)}, u32[]{:S(2)}) collective-permute-start(bf16[24,8192]{1,0:T(8,128)(2,1)S(1)} %pad_maximum_fusion), channel_id=1, source_target_pairs={{0,1},{1,0},{2,3},{3,2},{4,5},{5,4},{6,7},{7,6},{8,9},{9,8},{10,11... | collective-permute-start | bytes 1179656 | tf_op jit(solution)/shard_map/ppermute | solution.py:26
  18.4 3.7 %collective-permute-start.5 = (bf16[64,4096]{1,0:T(8,128)(2,1)S(1)}, bf16[64,4096]{1,0:T(8,128)(2,1)S(1)}, u32[]{:S(2)}, u32[]{:S(2)}) collective-permute-start(bf16[64,4096]{1,0:T(8,128)(2,1)S(1)} %get-tuple-element.15), channel_id=1, source_target_pairs={{0,1},{1,0},{2,3},{3,2},{4,5},{5,4},{6,7},{7,6},{8,9},{9,8},{10,11... | collective-permute-start | bytes 1572872 | tf_op jit(solution)/shard_map/ppermute | solution.py:26
  18.6 2.2 %copy-start.3 = (bf16[2,256,4096]{2,1,0:T(8,128)(2,1)S(1)}, bf16[2,256,4096]{2,1,0:T(8,128)(2,1)}, u32[]{:S(2)}) copy-start(bf16[2,256,4096]{2,1,0:T(8,128)(2,1)} %copy-done.2) | copy-start | bytes 12582916
  21.6 4.2 %collective-permute-start.11 = (bf16[64,4096]{1,0:T(8,128)(2,1)S(1)}, bf16[64,4096]{1,0:T(8,128)(2,1)S(1)}, u32[]{:S(2)}, u32[]{:S(2)}) collective-permute-start(bf16[64,4096]{1,0:T(8,128)(2,1)S(1)} %get-tuple-element.18), channel_id=1, source_target_pairs={{0,1},{1,0},{2,3},{3,2},{4,5},{5,4},{6,7},{7,6},{8,9},{9,8},{10,11... | collective-permute-start | bytes 1572872 | tf_op jit(solution)/shard_map/ppermute | solution.py:26
  22.1 12.9 %copy-start.6 = (bf16[1,8,8192]{2,1,0:T(8,128)(2,1)S(1)}, bf16[1,8,8192]{2,1,0:T(8,128)(2,1)}, u32[]{:S(2)}) copy-start(bf16[1,8,8192]{2,1,0:T(8,128)(2,1)} %param.11) | copy-start | bytes 393220
  22.3 7.2 %collective-permute-start.6 = (bf16[16,4096]{1,0:T(8,128)(2,1)S(1)}, bf16[16,4096]{1,0:T(8,128)(2,1)S(1)}, u32[]{:S(2)}, u32[]{:S(2)}) collective-permute-start(bf16[16,4096]{1,0:T(8,128)(2,1)S(1)} %get-tuple-element.32), channel_id=1, source_target_pairs={{0,2},{1,3},{2,0},{3,1},{4,6},{5,7},{6,4},{7,5},{8,10},{9,11},{10,... | collective-permute-start | bytes 393224 | tf_op jit(solution)/shard_map/ppermute | solution.py:26
  24.2 8.7 %collective-permute-start.8 = (bf16[16,4096]{1,0:T(8,128)(2,1)S(1)}, bf16[16,4096]{1,0:T(8,128)(2,1)S(1)}, u32[]{:S(2)}, u32[]{:S(2)}) collective-permute-start(bf16[16,4096]{1,0:T(8,128)(2,1)S(1)} %get-tuple-element.33), channel_id=1, source_target_pairs={{0,6},{1,7},{2,4},{3,5},{4,2},{5,3},{6,0},{7,1},{8,14},{9,15},{10,... | collective-permute-start | bytes 393224 | tf_op jit(solution)/shard_map/ppermute | solution.py:26
  25.7 9.2 %collective-permute-start.7 = (bf16[16,4096]{1,0:T(8,128)(2,1)S(1)}, bf16[16,4096]{1,0:T(8,128)(2,1)S(1)}, u32[]{:S(2)}, u32[]{:S(2)}) collective-permute-start(bf16[16,4096]{1,0:T(8,128)(2,1)S(1)} %get-tuple-element.34), channel_id=1, source_target_pairs={{0,4},{1,5},{2,6},{3,7},{4,0},{5,1},{6,2},{7,3},{8,12},{9,13},{10,... | collective-permute-start | bytes 393224 | tf_op jit(solution)/shard_map/ppermute | solution.py:26
  25.9 35.9 %copy-start.1 = (bf16[2,256,4096]{2,1,0:T(8,128)(2,1)S(1)}, bf16[2,256,4096]{2,1,0:T(8,128)(2,1)}, u32[]{:S(2)}) copy-start(bf16[2,256,4096]{2,1,0:T(8,128)(2,1)} %copy-done) | copy-start | bytes 12582916
  26.0 11.3 %collective-permute-start.12 = (bf16[16,4096]{1,0:T(8,128)(2,1)S(1)}, bf16[16,4096]{1,0:T(8,128)(2,1)S(1)}, u32[]{:S(2)}, u32[]{:S(2)}) collective-permute-start(bf16[16,4096]{1,0:T(8,128)(2,1)S(1)} %get-tuple-element.35), channel_id=1, source_target_pairs={{0,2},{1,3},{2,0},{3,1},{4,6},{5,7},{6,4},{7,5},{8,10},{9,11},{10,... | collective-permute-start | bytes 393224 | tf_op jit(solution)/shard_map/ppermute | solution.py:26
  27.9 9.8 %collective-permute-start.14 = (bf16[16,4096]{1,0:T(8,128)(2,1)S(1)}, bf16[16,4096]{1,0:T(8,128)(2,1)S(1)}, u32[]{:S(2)}, u32[]{:S(2)}) collective-permute-start(bf16[16,4096]{1,0:T(8,128)(2,1)S(1)} %get-tuple-element.36), channel_id=1, source_target_pairs={{0,6},{1,7},{2,4},{3,5},{4,2},{5,3},{6,0},{7,1},{8,14},{9,15},{10,... | collective-permute-start | bytes 393224 | tf_op jit(solution)/shard_map/ppermute | solution.py:26
  29.4 9.7 %collective-permute-start.13 = (bf16[16,4096]{1,0:T(8,128)(2,1)S(1)}, bf16[16,4096]{1,0:T(8,128)(2,1)S(1)}, u32[]{:S(2)}, u32[]{:S(2)}) collective-permute-start(bf16[16,4096]{1,0:T(8,128)(2,1)S(1)} %get-tuple-element.37), channel_id=1, source_target_pairs={{0,4},{1,5},{2,6},{3,7},{4,0},{5,1},{6,2},{7,3},{8,12},{9,13},{10,... | collective-permute-start | bytes 393224 | tf_op jit(solution)/shard_map/ppermute | solution.py:26
  35.0 4.3 %collective-permute-start.10 = (bf16[8,4096]{1,0:T(8,128)(2,1)S(1)}, bf16[8,4096]{1,0:T(8,128)(2,1)S(1)}, u32[]{:S(2)}, u32[]{:S(2)}) collective-permute-start(bf16[8,4096]{1,0:T(8,128)(2,1)S(1)} %get-tuple-element.38), channel_id=1, source_target_pairs={{0,8},{1,9},{2,10},{3,11},{4,12},{5,13},{6,14},{7,15},{8,0},{9,1},... | collective-permute-start | bytes 196616 | tf_op jit(solution)/shard_map/ppermute | solution.py:26
  36.7 2.7 %collective-permute-start.9 = (bf16[8,4096]{1,0:T(8,128)(2,1)S(1)}, bf16[8,4096]{1,0:T(8,128)(2,1)S(1)}, u32[]{:S(2)}, u32[]{:S(2)}) collective-permute-start(bf16[8,4096]{1,0:T(8,128)(2,1)S(1)} %get-tuple-element.39), channel_id=1, source_target_pairs={{8,16},{16,8},{9,17},{17,9},{10,18},{18,10},{11,19},{19,11},{12,20... | collective-permute-start | bytes 196616 | tf_op jit(solution)/shard_map/ppermute | solution.py:34
  39.4 12.2 %collective-permute-start.15 = (bf16[8,4096]{1,0:T(8,128)(2,1)S(1)}, bf16[8,4096]{1,0:T(8,128)(2,1)S(1)}, u32[]{:S(2)}, u32[]{:S(2)}) collective-permute-start(bf16[8,4096]{1,0:T(8,128)(2,1)S(1)} %get-tuple-element.42), channel_id=1, source_target_pairs={{8,16},{16,8},{9,17},{17,9},{10,18},{18,10},{11,19},{19,11},{12,20... | collective-permute-start | bytes 196616 | tf_op jit(solution)/shard_map/ppermute | solution.py:34
  40.1 11.5 %collective-permute-start.16 = (bf16[8,4096]{1,0:T(8,128)(2,1)S(1)}, bf16[8,4096]{1,0:T(8,128)(2,1)S(1)}, u32[]{:S(2)}, u32[]{:S(2)}) collective-permute-start(bf16[8,4096]{1,0:T(8,128)(2,1)S(1)} %get-tuple-element.43), channel_id=1, source_target_pairs={{0,8},{1,9},{2,10},{3,11},{4,12},{5,13},{6,14},{7,15},{8,0},{9,1},... | collective-permute-start | bytes 196616 | tf_op jit(solution)/shard_map/ppermute | solution.py:26
  48.0 16.9 %copy-start.4 = (bf16[2,256,4096]{2,1,0:T(8,128)(2,1)S(1)}, bf16[2,256,4096]{2,1,0:T(8,128)(2,1)}, u32[]{:S(2)}) copy-start(bf16[2,256,4096]{2,1,0:T(8,128)(2,1)} %copy-done.2) | copy-start | bytes 12582916
  48.0 9.3 %collective-permute-start.23 = (bf16[16,4096]{1,0:T(8,128)(2,1)S(1)}, bf16[16,4096]{1,0:T(8,128)(2,1)S(1)}, u32[]{:S(2)}, u32[]{:S(2)}) collective-permute-start(bf16[16,4096]{1,0:T(8,128)(2,1)S(1)} %pad_maximum_fusion.2), channel_id=1, source_target_pairs={{0,6},{1,7},{2,4},{3,5},{4,2},{5,3},{6,0},{7,1},{8,14},{9,15},{10,... | collective-permute-start | bytes 393224 | tf_op jit(solution)/shard_map/ppermute | solution.py:26
  49.5 7.7 %collective-permute-start.22 = (bf16[16,4096]{1,0:T(8,128)(2,1)S(1)}, bf16[16,4096]{1,0:T(8,128)(2,1)S(1)}, u32[]{:S(2)}, u32[]{:S(2)}) collective-permute-start(bf16[16,4096]{1,0:T(8,128)(2,1)S(1)} %pad_maximum_fusion.2), channel_id=1, source_target_pairs={{0,4},{1,5},{2,6},{3,7},{4,0},{5,1},{6,2},{7,3},{8,12},{9,13},{10,... | collective-permute-start | bytes 393224 | tf_op jit(solution)/shard_map/ppermute | solution.py:26
  51.1 5.0 %collective-permute-start.21 = (bf16[16,4096]{1,0:T(8,128)(2,1)S(1)}, bf16[16,4096]{1,0:T(8,128)(2,1)S(1)}, u32[]{:S(2)}, u32[]{:S(2)}) collective-permute-start(bf16[16,4096]{1,0:T(8,128)(2,1)S(1)} %pad_maximum_fusion.2), channel_id=1, source_target_pairs={{0,2},{1,3},{2,0},{3,1},{4,6},{5,7},{6,4},{7,5},{8,10},{9,11},{10,... | collective-permute-start | bytes 393224 | tf_op jit(solution)/shard_map/ppermute | solution.py:26
  51.7 9.4 %collective-permute-start.19 = (bf16[16,4096]{1,0:T(8,128)(2,1)S(1)}, bf16[16,4096]{1,0:T(8,128)(2,1)S(1)}, u32[]{:S(2)}, u32[]{:S(2)}) collective-permute-start(bf16[16,4096]{1,0:T(8,128)(2,1)S(1)} %pad_maximum_fusion.1), channel_id=1, source_target_pairs={{0,6},{1,7},{2,4},{3,5},{4,2},{5,3},{6,0},{7,1},{8,14},{9,15},{10,... | collective-permute-start | bytes 393224 | tf_op jit(solution)/shard_map/ppermute | solution.py:26
  53.2 7.8 %collective-permute-start.18 = (bf16[16,4096]{1,0:T(8,128)(2,1)S(1)}, bf16[16,4096]{1,0:T(8,128)(2,1)S(1)}, u32[]{:S(2)}, u32[]{:S(2)}) collective-permute-start(bf16[16,4096]{1,0:T(8,128)(2,1)S(1)} %pad_maximum_fusion.1), channel_id=1, source_target_pairs={{0,4},{1,5},{2,6},{3,7},{4,0},{5,1},{6,2},{7,3},{8,12},{9,13},{10,... | collective-permute-start | bytes 393224 | tf_op jit(solution)/shard_map/ppermute | solution.py:26
  56.0 5.0 %collective-permute-start.17 = (bf16[16,4096]{1,0:T(8,128)(2,1)S(1)}, bf16[16,4096]{1,0:T(8,128)(2,1)S(1)}, u32[]{:S(2)}, u32[]{:S(2)}) collective-permute-start(bf16[16,4096]{1,0:T(8,128)(2,1)S(1)} %pad_maximum_fusion.1), channel_id=1, source_target_pairs={{0,2},{1,3},{2,0},{3,1},{4,6},{5,7},{6,4},{7,5},{8,10},{9,11},{10,... | collective-permute-start | bytes 393224 | tf_op jit(solution)/shard_map/ppermute | solution.py:26
  57.3 4.5 %collective-permute-start.24 = (bf16[64,4096]{1,0:T(8,128)(2,1)S(1)}, bf16[64,4096]{1,0:T(8,128)(2,1)S(1)}, u32[]{:S(2)}, u32[]{:S(2)}) collective-permute-start(bf16[64,4096]{1,0:T(8,128)(2,1)S(1)} %constant_dynamic-update-slice_fusion.11.near_ref), channel_id=1, source_target_pairs={{0,1},{1,0},{2,3},{3,2},{4,5},{5,4},{6,7},{7,6},{8,9},{9,8},{10,11... | collective-permute-start | bytes 1572872 | tf_op jit(solution)/shard_map/ppermute | solution.py:26
  61.1 3.8 %collective-permute-start.20 = (bf16[64,4096]{1,0:T(8,128)(2,1)S(1)}, bf16[64,4096]{1,0:T(8,128)(2,1)S(1)}, u32[]{:S(2)}, u32[]{:S(2)}) collective-permute-start(bf16[64,4096]{1,0:T(8,128)(2,1)S(1)} %constant_dynamic-update-slice_fusion.6.near_ref), channel_id=1, source_target_pairs={{0,1},{1,0},{2,3},{3,2},{4,5},{5,4},{6,7},{7,6},{8,9},{9,8},{10,11... | collective-permute-start | bytes 1572872 | tf_op jit(solution)/shard_map/ppermute | solution.py:26

commit v7 on v2

v7 whole, which is shorter than its diff:
```python
import functools

import jax
import jax.numpy as jnp
from jax import lax
from jax.experimental import pallas as pl
from jax.experimental.pallas import tpu as pltpu
from jax.sharding import PartitionSpec as P

BLOCK = 128
LAYERS = 4
TILE = 32
CORES = 2
PARTS = 2
CHUNK = 1024
LIMIT = 10 << 20
AXIS = "layer"

ANY_SPEC = pl.BlockSpec(memory_space=pl.ANY)
VMEM_SPEC = pl.BlockSpec(memory_space=pltpu.VMEM)
SMEM_SPEC = pl.BlockSpec(memory_space=pltpu.SMEM)


def swap(value, mask):
    pairs = [(source, source ^ mask) for source in range(lax.axis_size(AXIS))]
    return lax.ppermute(value, AXIS, pairs)


def raised(value, layer, group):
    size = lax.axis_size(AXIS)
    came = lax.ppermute(value, AXIS, [(i, (i + group) % size) for i in range(size)])
    return jnp.where(layer == 0, jnp.zeros_like(came), came)


def lowered(value, layer, group):
    inner = []
    for low in range(LAYERS):
        away = 0 if low in (0, LAYERS - 1) else group if low % 2 == 1 else -group
        inner += [(i, i + away) for i in range(low * group, (low + 1) * group)]
    first = swap(value, group)
    second = lax.ppermute(value, AXIS, inner)
    came = jnp.where(layer % 2 == 0, first, second)
    return jnp.where(layer == LAYERS - 1, jnp.zeros_like(came), came)


def after(values, done):
    return lax.optimization_barrier((values, done))[0]


def bit_of(part, step, bits):
    return step if part % 2 == 0 else bits - 1 - step


def bits_left(part, step, bits):
    return sorted(set(range(bits)) - {bit_of(part, s, bits) for s in range(step)})[::-1]


def halve(parts, step, bits):
    out = []
    for i, part in enumerate(parts):
        bit = bit_of(i, step, bits)
        at = bits_left(i, step, bits).index(bit)
        sent = lax.index_in_dim(part, 1, at, keepdims=False).astype(jnp.bfloat16)
        kept = lax.index_in_dim(part, 0, at, keepdims=False)
        out.append(kept + swap(sent, CORES << bit).astype(jnp.float32))
    return out


def double(parts, step, bits):
    out = []
    for i, part in enumerate(parts):
        bit = bit_of(i, step, bits)
        had = {bit_of(i, s, bits) for s in range(step + 1)}
        at = sorted(had)[::-1].index(bit)
        out.append(jnp.stack([part, swap(part, CORES << bit)], axis=at))
    return out


def by_rows(parts):
    return [part.reshape(-1, part.shape[-1]) for part in parts]


def by_bits(total, bits):
    rows, width = total.shape[0] >> bits, total.shape[1] // PARTS
    return [total[:, i * width : (i + 1) * width].reshape((2,) * bits + (rows, width)) for i in range(PARTS)]


def split(slab):
    width = slab.shape[1] // PARTS
    return [slab[:, i * width : (i + 1) * width] for i in range(PARTS)]


def in_vmem(*arrays):
    return [pltpu.with_memory_space_constraint(a, pltpu.VMEM) for a in arrays]


def slab_of(place_ref, block, chips):
    return place_ref[0] ^ (CORES * (block % chips) + block // chips)


def kernel_params():
    return pltpu.CompilerParams(vmem_limit_bytes=LIMIT)


def load_kernel(pieces, weight_ref, *rest):
    held, sems = rest[:-1], rest[-1]
    copies = [
        pltpu.make_async_copy(weight_ref.at[piece], target, sems.at[i])
        for i, (piece, target) in enumerate(zip(pieces, held))
    ]
    for copy in copies:
        copy.start()
    for copy in copies:
        copy.wait()


def loaded(weight, pieces, shape):
    return pl.pallas_call(
        functools.partial(load_kernel, pieces),
        out_shape=[pltpu.VMEM(shape, weight.dtype)] * len(pieces),
        in_specs=[ANY_SPEC],
        out_specs=[VMEM_SPEC] * len(pieces),
        scratch_shapes=[pltpu.SemaphoreType.DMA((len(pieces),))],
        compiler_params=pltpu.CompilerParams(vmem_limit_bytes=1 << 20),
        cost_estimate=pl.CostEstimate(flops=0, bytes_accessed=4 * weight.size, transcendentals=0),
        name="load_weights",
    )(pltpu.with_memory_space_constraint(weight, pltpu.HBM))


def decode(codes, dec_ref, near_ref, far_ref):
    half, width = near_ref.shape
    for step in range(width // CHUNK):
        columns = pl.ds(step * CHUNK, CHUNK)
        part = jnp.dot(codes, dec_ref[:, columns], preferred_element_type=jnp.float32)
        near_ref[:, columns] = part[:half]
        far_ref[:, columns] = part[half:].astype(jnp.bfloat16)


def joined(refs):
    return [
        jnp.concatenate([near[...], far[...]], axis=0) for near, far in zip(refs[:PARTS], refs[PARTS:])
    ]


def encode_kernel(tokens, place_ref, active_ref, *refs):
    row_refs, enc_refs = refs[: 2 * PARTS], refs[2 * PARTS : 3 * PARTS]
    bias_ref, dec_hbm, codes_ref, near_ref, far_ref, own_ref, held, next_ref, sems = refs[3 * PARTS :]
    load_next = pltpu.make_async_copy(dec_hbm.at[0, 1], next_ref, sems.at[1])
    load_own = pltpu.make_async_copy(dec_hbm.at[0, 0], own_ref, sems.at[0])
    load_next.start()
    group = held.shape[0] // tokens
    pre = bias_ref[...].astype(jnp.float32)
    for rows, enc_ref in zip(joined(row_refs), enc_refs):
        pre = pre + jnp.dot(rows, enc_ref[...], preferred_element_type=jnp.float32)
    held[...] = jnp.maximum(pre, 0.0)
    for block in range(group):
        tile = (slab_of(place_ref, block, group // CORES) * tokens) // TILE
        for part in range(active_ref.shape[1]):
            where = (pl.ds(block * tokens, tokens), pl.ds(part * BLOCK, BLOCK))
            held[where] = held[where] * active_ref[tile, part].astype(jnp.float32)
    codes_ref[...] = held[...].astype(jnp.bfloat16)
    load_own.start()
    load_next.wait()
    decode(codes_ref[...], next_ref, near_ref, far_ref)
    load_own.wait()


def decode_kernel(codes_ref, dec_ref, near_ref, far_ref):
    decode(codes_ref[...], dec_ref, near_ref, far_ref)


def halves_of(rows, width):
    return [pltpu.VMEM((rows // CORES, width), jnp.float32), pltpu.VMEM((rows // CORES, width), jnp.bfloat16)]


def encoded(place, active, near, far, enc, bias, dec, tokens):
    rows = CORES * near[0].shape[0]
    features, depth = dec.shape[2:]
    return pl.pallas_call(
        functools.partial(encode_kernel, tokens),
        out_shape=[pltpu.VMEM((rows, features), jnp.bfloat16)] + halves_of(rows, depth) + [pltpu.VMEM((features, depth), dec.dtype)],
        in_specs=[SMEM_SPEC, SMEM_SPEC] + [VMEM_SPEC] * (3 * PARTS + 1) + [ANY_SPEC],
        out_specs=[VMEM_SPEC] * 4,
        scratch_shapes=[
            pltpu.VMEM((rows, features), jnp.float32),
            pltpu.VMEM((features, depth), dec.dtype),
            pltpu.SemaphoreType.DMA((2,)),
        ],
        compiler_params=kernel_params(),
        cost_estimate=pl.CostEstimate(flops=4 * rows * depth * features, bytes_accessed=4 * depth * features, transcendentals=0),
        name="encode",
    )(place, active, *in_vmem(*near, *far, *enc, bias), pltpu.with_memory_space_constraint(dec, pltpu.HBM))


def decoded(codes, dec):
    rows, features = codes.shape
    width = dec.shape[1]
    return pl.pallas_call(
        decode_kernel,
        out_shape=halves_of(rows, width),
        in_specs=[VMEM_SPEC] * 2,
        out_specs=[VMEM_SPEC] * 2,
        compiler_params=kernel_params(),
        cost_estimate=pl.CostEstimate(flops=2 * rows * width * features, bytes_accessed=2 * width * features, transcendentals=0),
        name="decode_own",
    )(*in_vmem(codes, dec))


def back(row_refs, dec_ref, reach):
    total = None
    for i, rows in enumerate(joined(row_refs)):
        width = rows.shape[1]
        part = lax.dot_general(
            rows,
            dec_ref[0, reach, :, pl.ds(i * width, width)],
            (((1,), (1,)), ((), ())),
            preferred_element_type=jnp.float32,
        )
        total = part if total is None else total + part
    return total


def grad_own_kernel(*refs):
    row_refs, (dec_ref, out_ref, _) = refs[: 2 * PARTS], refs[2 * PARTS :]
    out_ref[...] = back(row_refs, dec_ref, 0)


def grad_all_kernel(tokens, place_ref, *refs):
    row_refs, (dec_ref, own_ref, out_ref) = refs[: 2 * PARTS], refs[2 * PARTS :]
    total = own_ref[...] + back(row_refs, dec_ref, 1)
    group = total.shape[0] // tokens
    for block in range(group):
        slab = slab_of(place_ref, block, group // CORES)
        where = pl.ds(pl.multiple_of(slab * tokens, tokens), tokens)
        out_ref[0, where, :] = total[block * tokens : (block + 1) * tokens]


def grad_cost(near, dec):
    size = 2 * sum(part.size for part in near)
    return pl.CostEstimate(flops=2 * size * dec.shape[2], bytes_accessed=dec.size, transcendentals=0)


def grad_own(near, far, dec):
    shape = (CORES * near[0].shape[0], dec.shape[2])
    return pl.pallas_call(
        grad_own_kernel,
        out_shape=[pltpu.VMEM(shape, jnp.float32), pltpu.VMEM((8, 128), jnp.float32)],
        in_specs=[VMEM_SPEC] * (2 * PARTS + 1),
        out_specs=[VMEM_SPEC] * 2,
        compiler_params=kernel_params(),
        cost_estimate=grad_cost(near, dec),
        name="grad_own",
    )(*in_vmem(*near, *far, dec))[0]


def grad_all(place, near, far, dec, own, tokens):
    return pl.pallas_call(
        functools.partial(grad_all_kernel, tokens),
        out_shape=jax.ShapeDtypeStruct((1,) + own.shape, jnp.float32),
        in_specs=[SMEM_SPEC] + [VMEM_SPEC] * (2 * PARTS + 2),
        out_specs=VMEM_SPEC,
        compiler_params=kernel_params(),
        cost_estimate=grad_cost(near, dec),
        name="grad_all",
    )(place, *in_vmem(*near, *far, dec, own))


def on_device(resid, enc_weight, enc_bias, active, dec_weight, target):
    group = lax.axis_size(AXIS) // LAYERS
    chips = group // CORES
    bits = chips.bit_length() - 1
    index = lax.axis_index(AXIS)
    layer = index // group
    place = (index % group).astype(jnp.int32).reshape(1)
    tokens = resid.shape[1]
    _, depth, features = enc_weight.shape
    depth = depth // PARTS
    enc = loaded(enc_weight, [(0, pl.ds(i * depth, depth)) for i in range(PARTS)], (depth, features))
    near = split(resid[0])
    for step in range(bits):
        near = double(near if step == 0 else after(near, enc), step, bits)
    near = by_rows(near)
    far = [swap(part, 1) for part in near]
    codes, next_near, next_far, own_dec = encoded(place, active[0], near, far, enc, enc_bias, dec_weight, tokens)

    next_far = swap(next_far, 1)
    own_near, own_far = decoded(after(codes, next_far), own_dec)
    nexts = [by_bits(next_near + next_far.astype(jnp.float32), bits)]
    owns = by_bits(own_near + swap(own_far, 1).astype(jnp.float32), bits)
    for step in range(bits):
        nexts.append(halve(nexts[-1] if step == 0 else after(nexts[-1], owns), step, bits))
    for step in range(bits):
        owns = halve(after(owns, nexts[step + 1]), step, bits)
    next_sum = jnp.concatenate([part.astype(jnp.bfloat16) for part in nexts[-1]], axis=1)
    from_before = raised(next_sum, layer, group).astype(jnp.float32)
    own_sum = jnp.concatenate(owns, axis=1)
    error = (own_sum + from_before - target[0].astype(jnp.float32)).astype(jnp.bfloat16)

    later = lowered(error, layer, group)
    heres = [split(error)]
    for step in range(bits):
        heres.append(double(heres[-1], step, bits))
    here_near = by_rows(heres[-1])
    here_far = [swap(part, 1) for part in here_near]
    afters = split(later)
    for step in range(bits):
        afters = double(after(afters, heres[step + 1]), step, bits)
    after_near = after(by_rows(afters), here_far)
    after_far = [swap(part, 1) for part in after_near]
    own_grad = grad_own(here_near, here_far, dec_weight)
    grad = grad_all(place, after_near, after_far, dec_weight, own_grad, tokens)
    return (error[None], grad)


def solution(mesh):
    return jax.shard_map(
        on_device,
        mesh=mesh,
        in_specs=(
            P("layer", "groups", None),
            P("layer", None, None),
            P("layer", None),
            P("layer", "groups", None),
            P("layer", None, None, None),
            P("layer", "groups", None),
        ),
        out_specs=(P("layer", "groups", None), P("layer", "groups", None)),
        check_vma=False,
    )
```

time: 83.2 us -> 86.7 us (1.042)
  blocking collectives: 32.2 us -> 0 us
  starting transfers between devices: 12.4 us -> 31.4 us
  matrix products: 14.7 us -> 0 us
  Pallas kernels: 0 us -> 13 us
  local copies, waits for them, and re-layouts: 0.97 us -> 13.9 us
  waiting for transfers between devices: 17.1 us -> 25.2 us
  other arithmetic: 4.5 us -> 1.91 us
    all_gather x3 -> x0, blocking collectives: 32.2 us -> none  [gathered(): lax.all_gather(slab, AXIS, axis_index_groups=chip_sets(group), tiled=True)]
    ppermute x5 -> x29, starting transfers between devices: 0.65 us -> 29.1 us  [swap(): return lax.ppermute(value, AXIS, pairs)]
    ppermute x5 -> x29, waiting for transfers between devices: 0.73 us -> 25.2 us  [swap(): return lax.ppermute(value, AXIS, pairs)]
    dot_general x5 -> x0, matrix products: 14.7 us -> none  [the longest x2 7.17 us: transposed(): lax.dot_general(left, weight, (((1,), (1,)), ((), ())), preferred_element...]
    pallas_call x0 -> x5, Pallas kernels: none -> 13 us  [the longest x1 6.04 us: encoded(): pl.pallas_call(functools.partial(encode_kernel, tokens), out_shape=[pltpu...]
    unnamed x7 -> x22, local copies, waits for them, and re-layouts: 0.1 us -> 12.7 us
    all_to_all x2 -> x0, waiting for transfers between devices: 10.8 us -> none  [scattered(): lax.all_to_all(blocks, AXIS, 0, 0, axis_index_groups=chip_sets(group))]
    all_to_all x2 -> x0, starting transfers between devices: 6.94 us -> none  [scattered(): lax.all_to_all(blocks, AXIS, 0, 0, axis_index_groups=chip_sets(group))]
  transfers between devices with their start and end apart: 9 -> 31, of which waited for: 5 -> 18; matrix products, arithmetic and copies ran while one was open for 11% -> 1% of each run, Pallas kernels for 0% -> 6%
where the time goes in v7:
time: 86.7 us; the launch traced here: 86.4 us
  starting transfers between devices  31.4 us (36%)
  waiting for transfers between devices  25.2 us (29%)
  local copies, waits for them, and re-layouts  13.9 us (16%)
  Pallas kernels  13 us (15%)
  other arithmetic  1.91 us (2%)
  between operations  1.06 us (1%)
    ppermute x29, starting transfers between devices, swap(): return lax.ppermute(value, AXIS, pairs)  29.1 us
    ppermute x29, waiting for transfers between devices, swap(): return lax.ppermute(value, AXIS, pairs)  25.2 us
    unnamed x22, local copies, waits for them, and re-layouts  12.7 us
    pallas_call x1, Pallas kernels, encoded(): pl.pallas_call(functools.partial(encode_kernel, tokens), out_shape=[pltpu...  6.04 us
    pallas_call x1, Pallas kernels, loaded(): pl.pallas_call(functools.partial(load_kernel, pieces), out_shape=[pltpu.V...  2.24 us
    pallas_call x1, Pallas kernels, grad_all(): pl.pallas_call(functools.partial(grad_all_kernel, tokens), out_shape=jax....  2.03 us
    pallas_call x1, Pallas kernels, grad_own(): pl.pallas_call(grad_own_kernel, out_shape=[pltpu.VMEM(shape, jnp.float32)...  1.85 us
  transfers between devices with their start and end apart: 31, of which 18 were waited for; matrix products, arithmetic and copies ran while one was open for 1% of the time, Pallas kernels for 6%

profile of v7, /device:TPU:0, one launch (start us, length us, event | category | flops | bytes accessed | tf_op | source)
XLA Modules:
  0.0 86.4 jit_solution(4917567461389061539)
XLA Ops:
  0.6 0.9 %slice_bitcast_fusion.4 = (bf16[1,8,4096]{2,1,0:T(8,128)(2,1)S(1)}, bf16[1,8,4096]{2,1,0:T(8,128)(2,1)S(1)}, bf16[8,4096]{1,0:T(8,128)(2,1)S(1)}, bf16[8,4096]{1,0:T(8,128)(2,1)S(1)}) fusion(bf16[8,8192]{1,0:T(8,128)(2,1)} %bitcast.110), kind=kLoop, calls=%fused_computation.48 | loop fusion | bytes 393216 | tf_op jit(solution)/shard_map/stack | solution.py:75
  1.6 3.0 %collective-permute-start.1 = (bf16[8,4096]{1,0:T(8,128)(2,1)S(1)}, bf16[8,4096]{1,0:T(8,128)(2,1)S(1)}, u32[]{:S(2)}, u32[]{:S(2)}) collective-permute-start(bf16[8,4096]{1,0:T(8,128)(2,1)S(1)} %get-tuple-element.64), channel_id=1, source_target_pairs={{0,4},{1,5},{2,6},{3,7},{4,0},{5,1},{6,2},{7,3},{8,12},{9,13},{10,... | collective-permute-start | bytes 196616 | tf_op jit(solution)/shard_map/ppermute | solution.py:26
  4.6 1.5 %collective-permute-start = (bf16[8,4096]{1,0:T(8,128)(2,1)S(1)}, bf16[8,4096]{1,0:T(8,128)(2,1)S(1)}, u32[]{:S(2)}, u32[]{:S(2)}) collective-permute-start(bf16[8,4096]{1,0:T(8,128)(2,1)S(1)} %get-tuple-element.65), channel_id=1, source_target_pairs={{0,2},{1,3},{2,0},{3,1},{4,6},{5,7},{6,4},{7,5},{8,10},{9,11},{10,... | collective-permute-start | bytes 196616 | tf_op jit(solution)/shard_map/ppermute | solution.py:26
  6.1 2.2 %load_weights.1 = (bf16[4096,256]{1,0:T(8,128)(2,1)S(1)}, bf16[4096,256]{1,0:T(8,128)(2,1)S(1)}) custom-call(bf16[1,8192,256]{2,1,0:T(8,128)(2,1)} %weight_ref.1), custom_call_target="tpu_custom_call" | custom-call | bytes 8388608 | tf_op jit(solution)/shard_map/load_weights/pallas_call | solution.py:118
  8.3 1.3 %copy-done.4 = bf16[4096,256]{1,0:T(8,128)(2,1)} copy-done((bf16[4096,256]{1,0:T(8,128)(2,1)}, bf16[4096,256]{1,0:T(8,128)(2,1)S(1)}, u32[]{:S(2)}) %copy-start.4) | copy-done | bytes 2097176
  9.7 0.7 collective-permute-start.3
  10.4 0.5 collective-permute-start.2
  10.9 3.8 %collective-permute-done.3 = bf16[2,8,4096]{2,1,0:T(8,128)(2,1)S(1)} collective-permute-done((bf16[2,8,4096]{2,1,0:T(8,128)(2,1)S(1)}, bf16[2,8,4096]{2,1,0:T(8,128)(2,1)S(1)}, u32[]{:S(2)}, u32[]{:S(2)}) %collective-permute-start.3) | collective-permute-done | bytes 131104 | tf_op jit(solution)/shard_map/ppermute | solution.py:26
  14.8 0.1 collective-permute-start.5
  14.9 0.5 collective-permute-done.2
  15.4 0.1 collective-permute-start.4
  15.5 0.9 %collective-permute-done.5.refs_3_ = bf16[32,4096]{1,0:T(8,128)(2,1)S(1)} collective-permute-done((bf16[32,4096]{1,0:T(8,128)(2,1)S(1)}, bf16[32,4096]{1,0:T(8,128)(2,1)S(1)}, u32[]{:S(2)}, u32[]{:S(2)}) %collective-permute-start.5) | collective-permute-done | bytes 262176 | tf_op jit(solution)/shard_map/ppermute | solution.py:26
  16.4 0.6 collective-permute-done.4.refs_2_
  17.0 1.6 %copy-done.5 = bf16[4096,256]{1,0:T(8,128)(2,1)S(1)} copy-done((bf16[4096,256]{1,0:T(8,128)(2,1)S(1)}, bf16[4096,256]{1,0:T(8,128)(2,1)}, u32[]{:S(2)}) %copy-start.5) | copy-done | bytes 2097176
  18.6 6.0 %encode.1 = (bf16[64,256]{1,0:T(8,128)(2,1)S(1)}, f32[32,8192]{1,0:T(8,128)S(1)}, bf16[32,8192]{1,0:T(8,128)(2,1)}, bf16[256,8192]{1,0:T(8,128)(2,1)S(1)}) custom-call(s32[1]{0:T(128)} %bitcast.place_ref, s32[2,2]{1,0:T(2,128)S(1)} %bitcast.96, bf16[32,4096]{1,0:T(8,128)(2,1)S(1)} %bitcast.89, bf16[32,4096]{1,0:T(8,128)(2,1)S(1)} %bitcast.85, ...), custom_call_target="tpu_custom_call" | custom-call | flops 536870912 | bytes 8388608 | tf_op jit(solution)/shard_map/encode/pallas_call | solution.py:179
  24.7 2.0 %copy-done.2 = bf16[256,8192]{1,0:T(8,128)(2,1)} copy-done((bf16[256,8192]{1,0:T(8,128)(2,1)}, bf16[256,8192]{1,0:T(8,128)(2,1)S(1)}, u32[]{:S(2)}) %copy-start.2) | copy-done | bytes 4194328
  26.6 1.0 %copy-done.6 = f32[32,8192]{1,0:T(8,128)} copy-done((f32[32,8192]{1,0:T(8,128)}, f32[32,8192]{1,0:T(8,128)S(1)}, u32[]{:S(2)}) %copy-start.6) | copy-done | bytes 1048600
  27.6 0.1 collective-permute-start.6
  27.8 2.0 %collective-permute-done.6 = bf16[32,8192]{1,0:T(8,128)(2,1)S(1)} collective-permute-done((bf16[32,8192]{1,0:T(8,128)(2,1)}, bf16[32,8192]{1,0:T(8,128)(2,1)S(1)}, u32[]{:S(2)}, u32[]{:S(2)}) %collective-permute-start.6) | collective-permute-done | bytes 524320 | tf_op jit(solution)/shard_map/ppermute | solution.py:26
  29.8 1.3 %convert_add_fusion = f32[32,8192]{1,0:T(8,128)S(1)} fusion(f32[32,8192]{1,0:T(8,128)} %copy-done.6, bf16[32,8192]{1,0:T(8,128)(2,1)S(1)} %collective-permute-done.6), kind=kLoop, calls=%fused_computation | loop fusion | flops 524288 | bytes 2621440 | tf_op jit(solution)/shard_map/add | solution.py:288
  31.1 0.6 collective-permute-start.9
  31.7 1.5 %collective-permute-start.8 = (bf16[2,8,4096]{2,1,0:T(8,128)(2,1)S(1)}, bf16[2,8,4096]{2,1,0:T(8,128)(2,1)S(1)}, u32[]{:S(2)}, u32[]{:S(2)}) collective-permute-start(bf16[2,8,4096]{2,1,0:T(8,128)(2,1)S(1)} %fusion.8), channel_id=1, source_target_pairs={{0,2},{1,3},{2,0},{3,1},{4,6},{5,7},{6,4},{7,5},{8,10},{9,11},{10,... | collective-permute-start | bytes 393224 | tf_op jit(solution)/shard_map/ppermute | solution.py:26
  33.2 0.8 decode_own.1
  34.0 0.1 collective-permute-start.7
  34.1 2.6 %collective-permute-done.9 = bf16[2,8,4096]{2,1,0:T(8,128)(2,1)S(1)} collective-permute-done((bf16[2,8,4096]{2,1,0:T(8,128)(2,1)S(1)}, bf16[2,8,4096]{2,1,0:T(8,128)(2,1)S(1)}, u32[]{:S(2)}, u32[]{:S(2)}) %collective-permute-start.9) | collective-permute-done | bytes 131104 | tf_op jit(solution)/shard_map/ppermute | solution.py:26
  36.8 0.3 collective-permute-done.8
  37.1 0.1 convert_add_fusion.1
  37.2 0.1 fusion.15
  37.3 1.4 %collective-permute-start.13 = (bf16[8,4096]{1,0:T(8,128)(2,1)S(1)}, bf16[8,4096]{1,0:T(8,128)(2,1)S(1)}, u32[]{:S(2)}, u32[]{:S(2)}) collective-permute-start(bf16[8,4096]{1,0:T(8,128)(2,1)S(1)} %fusion.10), channel_id=1, source_target_pairs={{0,2},{1,3},{2,0},{3,1},{4,6},{5,7},{6,4},{7,5},{8,10},{9,11},{10,... | collective-permute-start | bytes 196616 | tf_op jit(solution)/shard_map/ppermute | solution.py:26
  38.8 1.5 %collective-permute-start.12 = (bf16[8,4096]{1,0:T(8,128)(2,1)S(1)}, bf16[8,4096]{1,0:T(8,128)(2,1)S(1)}, u32[]{:S(2)}, u32[]{:S(2)}) collective-permute-start(bf16[8,4096]{1,0:T(8,128)(2,1)S(1)} %fusion.9), channel_id=1, source_target_pairs={{0,4},{1,5},{2,6},{3,7},{4,0},{5,1},{6,2},{7,3},{8,12},{9,13},{10,... | collective-permute-start | bytes 196616 | tf_op jit(solution)/shard_map/ppermute | solution.py:26
  40.3 0.6 collective-permute-start.11
  40.9 0.6 collective-permute-start.10
  41.5 0.1 collective-permute-done.13
  41.7 1.9 %collective-permute-done.12 = bf16[8,4096]{1,0:T(8,128)(2,1)S(1)} collective-permute-done((bf16[8,4096]{1,0:T(8,128)(2,1)S(1)}, bf16[8,4096]{1,0:T(8,128)(2,1)S(1)}, u32[]{:S(2)}, u32[]{:S(2)}) %collective-permute-start.12) | collective-permute-done | bytes 65568 | tf_op jit(solution)/shard_map/ppermute | solution.py:26
  43.6 1.6 %collective-permute-start.16 = (bf16[8,8192]{1,0:T(8,128)(2,1)S(1)}, bf16[8,8192]{1,0:T(8,128)(2,1)S(1)}, u32[]{:S(2)}, u32[]{:S(2)}) collective-permute-start(bf16[8,8192]{1,0:T(8,128)(2,1)S(1)} %pad_maximum_fusion.8), channel_id=1, source_target_pairs={{0,8},{1,9},{2,10},{3,11},{4,12},{5,13},{6,14},{7,15},{8,16},{9,17... | collective-permute-start | bytes 393224 | tf_op jit(solution)/shard_map/ppermute | solution.py:31
  45.2 0.2 collective-permute-done.11
  45.4 0.5 collective-permute-done.10
  45.9 0.7 collective-permute-start.15
  46.6 1.6 %collective-permute-start.14 = (bf16[8,4096]{1,0:T(8,128)(2,1)S(1)}, bf16[8,4096]{1,0:T(8,128)(2,1)S(1)}, u32[]{:S(2)}, u32[]{:S(2)}) collective-permute-start(bf16[8,4096]{1,0:T(8,128)(2,1)S(1)} %fusion.11), channel_id=1, source_target_pairs={{0,4},{1,5},{2,6},{3,7},{4,0},{5,1},{6,2},{7,3},{8,12},{9,13},{10,... | collective-permute-start | bytes 196616 | tf_op jit(solution)/shard_map/ppermute | solution.py:26
  48.2 2.0 %collective-permute-done.15 = bf16[8,4096]{1,0:T(8,128)(2,1)S(1)} collective-permute-done((bf16[8,4096]{1,0:T(8,128)(2,1)S(1)}, bf16[8,4096]{1,0:T(8,128)(2,1)S(1)}, u32[]{:S(2)}, u32[]{:S(2)}) %collective-permute-start.15) | collective-permute-done | bytes 65568 | tf_op jit(solution)/shard_map/ppermute | solution.py:26
  50.3 1.3 %collective-permute-done.14 = bf16[8,4096]{1,0:T(8,128)(2,1)S(1)} collective-permute-done((bf16[8,4096]{1,0:T(8,128)(2,1)S(1)}, bf16[8,4096]{1,0:T(8,128)(2,1)S(1)}, u32[]{:S(2)}, u32[]{:S(2)}) %collective-permute-start.14) | collective-permute-done | bytes 65568 | tf_op jit(solution)/shard_map/ppermute | solution.py:26
  51.6 0.1 fusion.4
  51.7 1.6 %collective-permute-start.20 = (bf16[8,4096]{1,0:T(8,128)(2,1)S(1)}, bf16[8,4096]{1,0:T(8,128)(2,1)S(1)}, u32[]{:S(2)}, u32[]{:S(2)}) collective-permute-start(bf16[8,4096]{1,0:T(8,128)(2,1)S(1)} %get-tuple-element.58), channel_id=1, source_target_pairs={{0,4},{1,5},{2,6},{3,7},{4,0},{5,1},{6,2},{7,3},{8,12},{9,13},{10,... | collective-permute-start | bytes 196616 | tf_op jit(solution)/shard_map/ppermute | solution.py:26
  53.3 0.7 collective-permute-start.18
  53.9 4.2 %collective-permute-start.17 = (bf16[8,8192]{1,0:T(8,128)(2,1)S(1)}, bf16[8,8192]{1,0:T(8,128)(2,1)S(1)}, u32[]{:S(2)}, u32[]{:S(2)}) collective-permute-start(bf16[8,8192]{1,0:T(8,128)(2,1)S(1)} %fusion.4), channel_id=1, source_target_pairs={{0,8},{1,9},{2,10},{3,11},{4,12},{5,13},{6,14},{7,15},{8,0},{9,1},... | collective-permute-start | bytes 393224 | tf_op jit(solution)/shard_map/ppermute | solution.py:26
  58.2 1.4 %collective-permute-start.19 = (bf16[8,4096]{1,0:T(8,128)(2,1)S(1)}, bf16[8,4096]{1,0:T(8,128)(2,1)S(1)}, u32[]{:S(2)}, u32[]{:S(2)}) collective-permute-start(bf16[8,4096]{1,0:T(8,128)(2,1)S(1)} %get-tuple-element.59), channel_id=1, source_target_pairs={{0,2},{1,3},{2,0},{3,1},{4,6},{5,7},{6,4},{7,5},{8,10},{9,11},{10,... | collective-permute-start | bytes 196616 | tf_op jit(solution)/shard_map/ppermute | solution.py:26
  59.6 0.7 collective-permute-start.24
  60.3 2.1 %collective-permute-done.19 = bf16[8,4096]{1,0:T(8,128)(2,1)S(1)} collective-permute-done((bf16[8,4096]{1,0:T(8,128)(2,1)S(1)}, bf16[8,4096]{1,0:T(8,128)(2,1)S(1)}, u32[]{:S(2)}, u32[]{:S(2)}) %collective-permute-start.19) | collective-permute-done | bytes 65568 | tf_op jit(solution)/shard_map/ppermute | solution.py:26
  62.5 0.7 collective-permute-start.23
  63.2 1.6 %collective-permute-start.21 = (bf16[8,4096]{1,0:T(8,128)(2,1)S(1)}, bf16[8,4096]{1,0:T(8,128)(2,1)S(1)}, u32[]{:S(2)}, u32[]{:S(2)}) collective-permute-start(bf16[8,4096]{1,0:T(8,128)(2,1)S(1)} %get-tuple-element.43), channel_id=1, source_target_pairs={{0,2},{1,3},{2,0},{3,1},{4,6},{5,7},{6,4},{7,5},{8,10},{9,11},{10,... | collective-permute-start | bytes 196616 | tf_op jit(solution)/shard_map/ppermute | solution.py:26
  64.8 1.2 %collective-permute-start.22 = (bf16[8,4096]{1,0:T(8,128)(2,1)S(1)}, bf16[8,4096]{1,0:T(8,128)(2,1)S(1)}, u32[]{:S(2)}, u32[]{:S(2)}) collective-permute-start(bf16[8,4096]{1,0:T(8,128)(2,1)S(1)} %get-tuple-element.44), channel_id=1, source_target_pairs={{0,4},{1,5},{2,6},{3,7},{4,0},{5,1},{6,2},{7,3},{8,12},{9,13},{10,... | collective-permute-start | bytes 196616 | tf_op jit(solution)/shard_map/ppermute | solution.py:26
  66.1 1.5 %collective-permute-done.21 = bf16[8,4096]{1,0:T(8,128)(2,1)S(1)} collective-permute-done((bf16[8,4096]{1,0:T(8,128)(2,1)S(1)}, bf16[8,4096]{1,0:T(8,128)(2,1)S(1)}, u32[]{:S(2)}, u32[]{:S(2)}) %collective-permute-start.21) | collective-permute-done | bytes 65568 | tf_op jit(solution)/shard_map/ppermute | solution.py:26
  67.6 1.5 %collective-permute-done.22 = bf16[8,4096]{1,0:T(8,128)(2,1)S(1)} collective-permute-done((bf16[8,4096]{1,0:T(8,128)(2,1)S(1)}, bf16[8,4096]{1,0:T(8,128)(2,1)S(1)}, u32[]{:S(2)}, u32[]{:S(2)}) %collective-permute-start.22) | collective-permute-done | bytes 65568 | tf_op jit(solution)/shard_map/ppermute | solution.py:26
  69.2 0.9 %collective-permute-start.26 = (bf16[2,8,4096]{2,1,0:T(8,128)(2,1)S(1)}, bf16[2,8,4096]{2,1,0:T(8,128)(2,1)S(1)}, u32[]{:S(2)}, u32[]{:S(2)}) collective-permute-start(bf16[2,8,4096]{2,1,0:T(8,128)(2,1)S(1)} %pad_maximum_fusion.12), channel_id=1, source_target_pairs={{0,2},{1,3},{2,0},{3,1},{4,6},{5,7},{6,4},{7,5},{8,10},{9,11},{10,... | collective-permute-start | bytes 393224 | tf_op jit(solution)/shard_map/ppermute | solution.py:26
  70.1 1.1 %collective-permute-start.25 = (bf16[2,8,4096]{2,1,0:T(8,128)(2,1)S(1)}, bf16[2,8,4096]{2,1,0:T(8,128)(2,1)S(1)}, u32[]{:S(2)}, u32[]{:S(2)}) collective-permute-start(bf16[2,8,4096]{2,1,0:T(8,128)(2,1)S(1)} %pad_maximum_fusion.11), channel_id=1, source_target_pairs={{0,4},{1,5},{2,6},{3,7},{4,0},{5,1},{6,2},{7,3},{8,12},{9,13},{10,... | collective-permute-start | bytes 393224 | tf_op jit(solution)/shard_map/ppermute | solution.py:26
  71.2 0.5 collective-permute-start.27
  71.7 2.5 %collective-permute-done.26 = bf16[2,8,4096]{2,1,0:T(8,128)(2,1)S(1)} collective-permute-done((bf16[2,8,4096]{2,1,0:T(8,128)(2,1)S(1)}, bf16[2,8,4096]{2,1,0:T(8,128)(2,1)S(1)}, u32[]{:S(2)}, u32[]{:S(2)}) %collective-permute-start.26) | collective-permute-done | bytes 131104 | tf_op jit(solution)/shard_map/ppermute | solution.py:26
  74.3 0.9 %collective-permute-done.25 = bf16[2,8,4096]{2,1,0:T(8,128)(2,1)S(1)} collective-permute-done((bf16[2,8,4096]{2,1,0:T(8,128)(2,1)S(1)}, bf16[2,8,4096]{2,1,0:T(8,128)(2,1)S(1)}, u32[]{:S(2)}, u32[]{:S(2)}) %collective-permute-start.25) | collective-permute-done | bytes 131104 | tf_op jit(solution)/shard_map/ppermute | solution.py:26
  75.2 0.1 collective-permute-start.29
  75.3 0.5 collective-permute-start.30
  75.8 3.4 %copy-done = bf16[1,2,256,8192]{3,2,1,0:T(8,128)(2,1)S(1)} copy-done((bf16[1,2,256,8192]{3,2,1,0:T(8,128)(2,1)S(1)}, bf16[1,2,256,8192]{3,2,1,0:T(8,128)(2,1)}, u32[]{:S(2)}) %copy-start) | copy-done | bytes 8388632
  79.2 1.9 %grad_own.1 = (f32[64,256]{1,0:T(8,128)S(1)}, f32[8,128]{1,0:T(8,128)}) custom-call(bf16[32,4096]{1,0:T(8,128)(2,1)S(1)} %bitcast.87, bf16[32,4096]{1,0:T(8,128)(2,1)S(1)} %bitcast.91, bf16[32,4096]{1,0:T(8,128)(2,1)S(1)} %collective-permute-done.27.refs_2_, bf16[32,4096]{1,0:T(8,128)(2,1)S(1)} %collective-permute-done.28.refs_3_, ...), custom_call_target="tpu_custom_call" | custom-call | flops 268435456 | bytes 4194304 | tf_op jit(solution)/shard_map/grad_own/pallas_call | solution.py:245
  81.0 3.4 %copy-done.1 = bf16[1,2,256,8192]{3,2,1,0:T(8,128)(2,1)S(1)} copy-done((bf16[1,2,256,8192]{3,2,1,0:T(8,128)(2,1)S(1)}, bf16[1,2,256,8192]{3,2,1,0:T(8,128)(2,1)}, u32[]{:S(2)}) %copy-start.1) | copy-done | bytes 8388632
  84.4 2.0 %grad_all.1 = f32[1,64,256]{2,1,0:T(8,128)} custom-call(s32[1]{0:T(128)} %bitcast.place_ref, bf16[32,4096]{1,0:T(8,128)(2,1)S(1)} %bitcast.95, bf16[32,4096]{1,0:T(8,128)(2,1)S(1)} %bitcast.93, bf16[32,4096]{1,0:T(8,128)(2,1)S(1)} %collective-permute-done.29.refs_2_, bf16[32,4096]{1,0:T(8,128)(2,1)S(1)} %collective-permute-done.30.refs_3_, ...), custom_call_target="tpu_custom_call" | custom-call | flops 268435456 | bytes 4194304 | tf_op jit(solution)/shard_map/grad_all/pallas_call | solution.py:257
  (66 shorter events, 0.7 us)
Async XLA Ops:
  0.6 16.4 %copy-start.7 = (s32[1,2,2]{2,1,0:T(2,128)S(1)}, s32[1,2,2]{2,1,0:T(2,128)}, u32[]{:S(2)}) copy-start(s32[1,2,2]{2,1,0:T(2,128)} %param.9) | copy-start | bytes 52
  0.6 16.4 %copy-start.8 = (bf16[1,256]{1,0:T(2,128)(2,1)S(1)}, bf16[1,256]{1,0:T(2,128)(2,1)}, u32[]{:S(2)}) copy-start(bf16[1,256]{1,0:T(2,128)(2,1)} %refs_6_.1) | copy-start | bytes 1540
  1.6 8.1 %collective-permute-start.1 = (bf16[8,4096]{1,0:T(8,128)(2,1)S(1)}, bf16[8,4096]{1,0:T(8,128)(2,1)S(1)}, u32[]{:S(2)}, u32[]{:S(2)}) collective-permute-start(bf16[8,4096]{1,0:T(8,128)(2,1)S(1)} %get-tuple-element.64), channel_id=1, source_target_pairs={{0,4},{1,5},{2,6},{3,7},{4,0},{5,1},{6,2},{7,3},{8,12},{9,13},{10,... | collective-permute-start | bytes 196616 | tf_op jit(solution)/shard_map/ppermute | solution.py:26
  4.6 5.1 %collective-permute-start = (bf16[8,4096]{1,0:T(8,128)(2,1)S(1)}, bf16[8,4096]{1,0:T(8,128)(2,1)S(1)}, u32[]{:S(2)}, u32[]{:S(2)}) collective-permute-start(bf16[8,4096]{1,0:T(8,128)(2,1)S(1)} %get-tuple-element.65), channel_id=1, source_target_pairs={{0,2},{1,3},{2,0},{3,1},{4,6},{5,7},{6,4},{7,5},{8,10},{9,11},{10,... | collective-permute-start | bytes 196616 | tf_op jit(solution)/shard_map/ppermute | solution.py:26
  8.3 1.3 %copy-start.4 = (bf16[4096,256]{1,0:T(8,128)(2,1)}, bf16[4096,256]{1,0:T(8,128)(2,1)S(1)}, u32[]{:S(2)}) copy-start(bf16[4096,256]{1,0:T(8,128)(2,1)S(1)} %get-tuple-element.27.refs_5_) | copy-start | bytes 6291460
  9.7 5.0 %collective-permute-start.3 = (bf16[2,8,4096]{2,1,0:T(8,128)(2,1)S(1)}, bf16[2,8,4096]{2,1,0:T(8,128)(2,1)S(1)}, u32[]{:S(2)}, u32[]{:S(2)}) collective-permute-start(bf16[2,8,4096]{2,1,0:T(8,128)(2,1)S(1)} %pad_maximum_fusion.7), channel_id=1, source_target_pairs={{0,2},{1,3},{2,0},{3,1},{4,6},{5,7},{6,4},{7,5},{8,10},{9,11},{10,... | collective-permute-start | bytes 393224 | tf_op jit(solution)/shard_map/ppermute | solution.py:26
  10.4 5.0 %collective-permute-start.2 = (bf16[2,8,4096]{2,1,0:T(8,128)(2,1)S(1)}, bf16[2,8,4096]{2,1,0:T(8,128)(2,1)S(1)}, u32[]{:S(2)}, u32[]{:S(2)}) collective-permute-start(bf16[2,8,4096]{2,1,0:T(8,128)(2,1)S(1)} %pad_maximum_fusion.6), channel_id=1, source_target_pairs={{0,4},{1,5},{2,6},{3,7},{4,0},{5,1},{6,2},{7,3},{8,12},{9,13},{10,... | collective-permute-start | bytes 393224 | tf_op jit(solution)/shard_map/ppermute | solution.py:26
  14.8 1.6 %collective-permute-start.5 = (bf16[32,4096]{1,0:T(8,128)(2,1)S(1)}, bf16[32,4096]{1,0:T(8,128)(2,1)S(1)}, u32[]{:S(2)}, u32[]{:S(2)}) collective-permute-start(bf16[32,4096]{1,0:T(8,128)(2,1)S(1)} %bitcast.84), channel_id=1, source_target_pairs={{0,1},{1,0},{2,3},{3,2},{4,5},{5,4},{6,7},{7,6},{8,9},{9,8},{10,11... | collective-permute-start | bytes 786440 | tf_op jit(solution)/shard_map/ppermute | solution.py:26
  15.4 1.6 %collective-permute-start.4 = (bf16[32,4096]{1,0:T(8,128)(2,1)S(1)}, bf16[32,4096]{1,0:T(8,128)(2,1)S(1)}, u32[]{:S(2)}, u32[]{:S(2)}) collective-permute-start(bf16[32,4096]{1,0:T(8,128)(2,1)S(1)} %bitcast.88), channel_id=1, source_target_pairs={{0,1},{1,0},{2,3},{3,2},{4,5},{5,4},{6,7},{7,6},{8,9},{9,8},{10,11... | collective-permute-start | bytes 786440 | tf_op jit(solution)/shard_map/ppermute | solution.py:26
  17.0 1.6 %copy-start.5 = (bf16[4096,256]{1,0:T(8,128)(2,1)S(1)}, bf16[4096,256]{1,0:T(8,128)(2,1)}, u32[]{:S(2)}) copy-start(bf16[4096,256]{1,0:T(8,128)(2,1)} %copy-done.4) | copy-start | bytes 6291460
  24.7 2.0 %copy-start.2 = (bf16[256,8192]{1,0:T(8,128)(2,1)}, bf16[256,8192]{1,0:T(8,128)(2,1)S(1)}, u32[]{:S(2)}) copy-start(bf16[256,8192]{1,0:T(8,128)(2,1)S(1)} %get-tuple-element.33.dec_ref) | copy-start | bytes 12582916
  26.6 1.0 %copy-start.6 = (f32[32,8192]{1,0:T(8,128)}, f32[32,8192]{1,0:T(8,128)S(1)}, u32[]{:S(2)}) copy-start(f32[32,8192]{1,0:T(8,128)S(1)} %get-tuple-element.36) | copy-start | bytes 3145732
  27.6 2.1 %collective-permute-start.6 = (bf16[32,8192]{1,0:T(8,128)(2,1)}, bf16[32,8192]{1,0:T(8,128)(2,1)S(1)}, u32[]{:S(2)}, u32[]{:S(2)}) collective-permute-start(bf16[32,8192]{1,0:T(8,128)(2,1)} %get-tuple-element.31), channel_id=1, source_target_pairs={{0,1},{1,0},{2,3},{3,2},{4,5},{5,4},{6,7},{7,6},{8,9},{9,8},{10,11... | collective-permute-start | bytes 1572872 | tf_op jit(solution)/shard_map/ppermute | solution.py:26
  27.8 5.4 %copy-start.3 = (bf16[256,8192]{1,0:T(8,128)(2,1)S(1)}, bf16[256,8192]{1,0:T(8,128)(2,1)}, u32[]{:S(2)}) copy-start(bf16[256,8192]{1,0:T(8,128)(2,1)} %copy-done.2) | copy-start | bytes 12582916
  31.1 5.6 %collective-permute-start.9 = (bf16[2,8,4096]{2,1,0:T(8,128)(2,1)S(1)}, bf16[2,8,4096]{2,1,0:T(8,128)(2,1)S(1)}, u32[]{:S(2)}, u32[]{:S(2)}) collective-permute-start(bf16[2,8,4096]{2,1,0:T(8,128)(2,1)S(1)} %fusion.5), channel_id=1, source_target_pairs={{0,4},{1,5},{2,6},{3,7},{4,0},{5,1},{6,2},{7,3},{8,12},{9,13},{10,... | collective-permute-start | bytes 393224 | tf_op jit(solution)/shard_map/ppermute | solution.py:26
  31.7 5.3 %collective-permute-start.8 = (bf16[2,8,4096]{2,1,0:T(8,128)(2,1)S(1)}, bf16[2,8,4096]{2,1,0:T(8,128)(2,1)S(1)}, u32[]{:S(2)}, u32[]{:S(2)}) collective-permute-start(bf16[2,8,4096]{2,1,0:T(8,128)(2,1)S(1)} %fusion.8), channel_id=1, source_target_pairs={{0,2},{1,3},{2,0},{3,1},{4,6},{5,7},{6,4},{7,5},{8,10},{9,11},{10,... | collective-permute-start | bytes 393224 | tf_op jit(solution)/shard_map/ppermute | solution.py:26
  34.0 3.1 %collective-permute-start.7 = (bf16[32,8192]{1,0:T(8,128)(2,1)S(1)}, bf16[32,8192]{1,0:T(8,128)(2,1)S(1)}, u32[]{:S(2)}, u32[]{:S(2)}) collective-permute-start(bf16[32,8192]{1,0:T(8,128)(2,1)S(1)} %get-tuple-element.35), channel_id=1, source_target_pairs={{0,1},{1,0},{2,3},{3,2},{4,5},{5,4},{6,7},{7,6},{8,9},{9,8},{10,11... | collective-permute-start | bytes 1572872 | tf_op jit(solution)/shard_map/ppermute | solution.py:26
  37.1 14.5 %copy-start.10 = (bf16[1,8,8192]{2,1,0:T(8,128)(2,1)S(1)}, bf16[1,8,8192]{2,1,0:T(8,128)(2,1)}, u32[]{:S(2)}) copy-start(bf16[1,8,8192]{2,1,0:T(8,128)(2,1)} %param.11) | copy-start | bytes 393220
  37.3 4.3 %collective-permute-start.13 = (bf16[8,4096]{1,0:T(8,128)(2,1)S(1)}, bf16[8,4096]{1,0:T(8,128)(2,1)S(1)}, u32[]{:S(2)}, u32[]{:S(2)}) collective-permute-start(bf16[8,4096]{1,0:T(8,128)(2,1)S(1)} %fusion.10), channel_id=1, source_target_pairs={{0,2},{1,3},{2,0},{3,1},{4,6},{5,7},{6,4},{7,5},{8,10},{9,11},{10,... | collective-permute-start | bytes 196616 | tf_op jit(solution)/shard_map/ppermute | solution.py:26
  38.8 4.8 %collective-permute-start.12 = (bf16[8,4096]{1,0:T(8,128)(2,1)S(1)}, bf16[8,4096]{1,0:T(8,128)(2,1)S(1)}, u32[]{:S(2)}, u32[]{:S(2)}) collective-permute-start(bf16[8,4096]{1,0:T(8,128)(2,1)S(1)} %fusion.9), channel_id=1, source_target_pairs={{0,4},{1,5},{2,6},{3,7},{4,0},{5,1},{6,2},{7,3},{8,12},{9,13},{10,... | collective-permute-start | bytes 196616 | tf_op jit(solution)/shard_map/ppermute | solution.py:26
  40.3 5.0 %collective-permute-start.11 = (bf16[2,8,4096]{2,1,0:T(8,128)(2,1)S(1)}, bf16[2,8,4096]{2,1,0:T(8,128)(2,1)S(1)}, u32[]{:S(2)}, u32[]{:S(2)}) collective-permute-start(bf16[2,8,4096]{2,1,0:T(8,128)(2,1)S(1)} %fusion.7), channel_id=1, source_target_pairs={{0,4},{1,5},{2,6},{3,7},{4,0},{5,1},{6,2},{7,3},{8,12},{9,13},{10,... | collective-permute-start | bytes 393224 | tf_op jit(solution)/shard_map/ppermute | solution.py:26
  40.9 5.0 %collective-permute-start.10 = (bf16[2,8,4096]{2,1,0:T(8,128)(2,1)S(1)}, bf16[2,8,4096]{2,1,0:T(8,128)(2,1)S(1)}, u32[]{:S(2)}, u32[]{:S(2)}) collective-permute-start(bf16[2,8,4096]{2,1,0:T(8,128)(2,1)S(1)} %fusion.6), channel_id=1, source_target_pairs={{0,2},{1,3},{2,0},{3,1},{4,6},{5,7},{6,4},{7,5},{8,10},{9,11},{10,... | collective-permute-start | bytes 393224 | tf_op jit(solution)/shard_map/ppermute | solution.py:26
  43.6 8.0 %collective-permute-start.16 = (bf16[8,8192]{1,0:T(8,128)(2,1)S(1)}, bf16[8,8192]{1,0:T(8,128)(2,1)S(1)}, u32[]{:S(2)}, u32[]{:S(2)}) collective-permute-start(bf16[8,8192]{1,0:T(8,128)(2,1)S(1)} %pad_maximum_fusion.8), channel_id=1, source_target_pairs={{0,8},{1,9},{2,10},{3,11},{4,12},{5,13},{6,14},{7,15},{8,16},{9,17... | collective-permute-start | bytes 393224 | tf_op jit(solution)/shard_map/ppermute | solution.py:31
  45.9 4.3 %collective-permute-start.15 = (bf16[8,4096]{1,0:T(8,128)(2,1)S(1)}, bf16[8,4096]{1,0:T(8,128)(2,1)S(1)}, u32[]{:S(2)}, u32[]{:S(2)}) collective-permute-start(bf16[8,4096]{1,0:T(8,128)(2,1)S(1)} %fusion.12), channel_id=1, source_target_pairs={{0,2},{1,3},{2,0},{3,1},{4,6},{5,7},{6,4},{7,5},{8,10},{9,11},{10,... | collective-permute-start | bytes 196616 | tf_op jit(solution)/shard_map/ppermute | solution.py:26
  46.6 4.9 %collective-permute-start.14 = (bf16[8,4096]{1,0:T(8,128)(2,1)S(1)}, bf16[8,4096]{1,0:T(8,128)(2,1)S(1)}, u32[]{:S(2)}, u32[]{:S(2)}) collective-permute-start(bf16[8,4096]{1,0:T(8,128)(2,1)S(1)} %fusion.11), channel_id=1, source_target_pairs={{0,4},{1,5},{2,6},{3,7},{4,0},{5,1},{6,2},{7,3},{8,12},{9,13},{10,... | collective-permute-start | bytes 196616 | tf_op jit(solution)/shard_map/ppermute | solution.py:26
  51.7 29.4 %copy-start.9 = (bf16[8,8192]{1,0:T(8,128)(2,1)}, bf16[8,8192]{1,0:T(8,128)(2,1)S(1)}, u32[]{:S(2)}) copy-start(bf16[8,8192]{1,0:T(8,128)(2,1)S(1)} %fusion.4) | copy-start | bytes 393220
  51.7 7.9 %collective-permute-start.20 = (bf16[8,4096]{1,0:T(8,128)(2,1)S(1)}, bf16[8,4096]{1,0:T(8,128)(2,1)S(1)}, u32[]{:S(2)}, u32[]{:S(2)}) collective-permute-start(bf16[8,4096]{1,0:T(8,128)(2,1)S(1)} %get-tuple-element.58), channel_id=1, source_target_pairs={{0,4},{1,5},{2,6},{3,7},{4,0},{5,1},{6,2},{7,3},{8,12},{9,13},{10,... | collective-permute-start | bytes 196616 | tf_op jit(solution)/shard_map/ppermute | solution.py:26
  53.3 9.9 %collective-permute-start.18 = (bf16[8,8192]{1,0:T(8,128)(2,1)S(1)}, bf16[8,8192]{1,0:T(8,128)(2,1)S(1)}, u32[]{:S(2)}, u32[]{:S(2)}) collective-permute-start(bf16[8,8192]{1,0:T(8,128)(2,1)S(1)} %fusion.4), channel_id=1, source_target_pairs={{0,0},{1,1},{2,2},{3,3},{4,4},{5,5},{6,6},{7,7},{8,16},{9,17},{10,... | collective-permute-start | bytes 393224 | tf_op jit(solution)/shard_map/ppermute | solution.py:41
  53.9 9.3 %collective-permute-start.17 = (bf16[8,8192]{1,0:T(8,128)(2,1)S(1)}, bf16[8,8192]{1,0:T(8,128)(2,1)S(1)}, u32[]{:S(2)}, u32[]{:S(2)}) collective-permute-start(bf16[8,8192]{1,0:T(8,128)(2,1)S(1)} %fusion.4), channel_id=1, source_target_pairs={{0,8},{1,9},{2,10},{3,11},{4,12},{5,13},{6,14},{7,15},{8,0},{9,1},... | collective-permute-start | bytes 393224 | tf_op jit(solution)/shard_map/ppermute | solution.py:26
  58.2 4.3 %collective-permute-start.19 = (bf16[8,4096]{1,0:T(8,128)(2,1)S(1)}, bf16[8,4096]{1,0:T(8,128)(2,1)S(1)}, u32[]{:S(2)}, u32[]{:S(2)}) collective-permute-start(bf16[8,4096]{1,0:T(8,128)(2,1)S(1)} %get-tuple-element.59), channel_id=1, source_target_pairs={{0,2},{1,3},{2,0},{3,1},{4,6},{5,7},{6,4},{7,5},{8,10},{9,11},{10,... | collective-permute-start | bytes 196616 | tf_op jit(solution)/shard_map/ppermute | solution.py:26
  59.6 6.5 %collective-permute-start.24 = (bf16[2,8,4096]{2,1,0:T(8,128)(2,1)S(1)}, bf16[2,8,4096]{2,1,0:T(8,128)(2,1)S(1)}, u32[]{:S(2)}, u32[]{:S(2)}) collective-permute-start(bf16[2,8,4096]{2,1,0:T(8,128)(2,1)S(1)} %get-tuple-element.53), channel_id=1, source_target_pairs={{0,2},{1,3},{2,0},{3,1},{4,6},{5,7},{6,4},{7,5},{8,10},{9,11},{10,... | collective-permute-start | bytes 393224 | tf_op jit(solution)/shard_map/ppermute | solution.py:26
  62.5 6.6 %collective-permute-start.23 = (bf16[2,8,4096]{2,1,0:T(8,128)(2,1)S(1)}, bf16[2,8,4096]{2,1,0:T(8,128)(2,1)S(1)}, u32[]{:S(2)}, u32[]{:S(2)}) collective-permute-start(bf16[2,8,4096]{2,1,0:T(8,128)(2,1)S(1)} %get-tuple-element.55), channel_id=1, source_target_pairs={{0,4},{1,5},{2,6},{3,7},{4,0},{5,1},{6,2},{7,3},{8,12},{9,13},{10,... | collective-permute-start | bytes 393224 | tf_op jit(solution)/shard_map/ppermute | solution.py:26
  63.2 4.3 %collective-permute-start.21 = (bf16[8,4096]{1,0:T(8,128)(2,1)S(1)}, bf16[8,4096]{1,0:T(8,128)(2,1)S(1)}, u32[]{:S(2)}, u32[]{:S(2)}) collective-permute-start(bf16[8,4096]{1,0:T(8,128)(2,1)S(1)} %get-tuple-element.43), channel_id=1, source_target_pairs={{0,2},{1,3},{2,0},{3,1},{4,6},{5,7},{6,4},{7,5},{8,10},{9,11},{10,... | collective-permute-start | bytes 196616 | tf_op jit(solution)/shard_map/ppermute | solution.py:26
  64.8 4.3 %collective-permute-start.22 = (bf16[8,4096]{1,0:T(8,128)(2,1)S(1)}, bf16[8,4096]{1,0:T(8,128)(2,1)S(1)}, u32[]{:S(2)}, u32[]{:S(2)}) collective-permute-start(bf16[8,4096]{1,0:T(8,128)(2,1)S(1)} %get-tuple-element.44), channel_id=1, source_target_pairs={{0,4},{1,5},{2,6},{3,7},{4,0},{5,1},{6,2},{7,3},{8,12},{9,13},{10,... | collective-permute-start | bytes 196616 | tf_op jit(solution)/shard_map/ppermute | solution.py:26
  69.2 5.0 %collective-permute-start.26 = (bf16[2,8,4096]{2,1,0:T(8,128)(2,1)S(1)}, bf16[2,8,4096]{2,1,0:T(8,128)(2,1)S(1)}, u32[]{:S(2)}, u32[]{:S(2)}) collective-permute-start(bf16[2,8,4096]{2,1,0:T(8,128)(2,1)S(1)} %pad_maximum_fusion.12), channel_id=1, source_target_pairs={{0,2},{1,3},{2,0},{3,1},{4,6},{5,7},{6,4},{7,5},{8,10},{9,11},{10,... | collective-permute-start | bytes 393224 | tf_op jit(solution)/shard_map/ppermute | solution.py:26
  70.1 5.0 %collective-permute-start.25 = (bf16[2,8,4096]{2,1,0:T(8,128)(2,1)S(1)}, bf16[2,8,4096]{2,1,0:T(8,128)(2,1)S(1)}, u32[]{:S(2)}, u32[]{:S(2)}) collective-permute-start(bf16[2,8,4096]{2,1,0:T(8,128)(2,1)S(1)} %pad_maximum_fusion.11), channel_id=1, source_target_pairs={{0,4},{1,5},{2,6},{3,7},{4,0},{5,1},{6,2},{7,3},{8,12},{9,13},{10,... | collective-permute-start | bytes 393224 | tf_op jit(solution)/shard_map/ppermute | solution.py:26
  71.2 4.0 %collective-permute-start.28 = (bf16[32,4096]{1,0:T(8,128)(2,1)S(1)}, bf16[32,4096]{1,0:T(8,128)(2,1)S(1)}, u32[]{:S(2)}, u32[]{:S(2)}) collective-permute-start(bf16[32,4096]{1,0:T(8,128)(2,1)S(1)} %bitcast.90), channel_id=1, source_target_pairs={{0,1},{1,0},{2,3},{3,2},{4,5},{5,4},{6,7},{7,6},{8,9},{9,8},{10,11... | collective-permute-start | bytes 786440 | tf_op jit(solution)/shard_map/ppermute | solution.py:26
  71.2 4.0 %collective-permute-start.27 = (bf16[32,4096]{1,0:T(8,128)(2,1)S(1)}, bf16[32,4096]{1,0:T(8,128)(2,1)S(1)}, u32[]{:S(2)}, u32[]{:S(2)}) collective-permute-start(bf16[32,4096]{1,0:T(8,128)(2,1)S(1)} %bitcast.86), channel_id=1, source_target_pairs={{0,1},{1,0},{2,3},{3,2},{4,5},{5,4},{6,7},{7,6},{8,9},{9,8},{10,11... | collective-permute-start | bytes 786440 | tf_op jit(solution)/shard_map/ppermute | solution.py:26
  75.2 5.8 %collective-permute-start.29 = (bf16[32,4096]{1,0:T(8,128)(2,1)S(1)}, bf16[32,4096]{1,0:T(8,128)(2,1)S(1)}, u32[]{:S(2)}, u32[]{:S(2)}) collective-permute-start(bf16[32,4096]{1,0:T(8,128)(2,1)S(1)} %bitcast.94), channel_id=1, source_target_pairs={{0,1},{1,0},{2,3},{3,2},{4,5},{5,4},{6,7},{7,6},{8,9},{9,8},{10,11... | collective-permute-start | bytes 786440 | tf_op jit(solution)/shard_map/ppermute | solution.py:26
  75.3 5.7 %collective-permute-start.30 = (bf16[32,4096]{1,0:T(8,128)(2,1)S(1)}, bf16[32,4096]{1,0:T(8,128)(2,1)S(1)}, u32[]{:S(2)}, u32[]{:S(2)}) collective-permute-start(bf16[32,4096]{1,0:T(8,128)(2,1)S(1)} %bitcast.92), channel_id=1, source_target_pairs={{0,1},{1,0},{2,3},{3,2},{4,5},{5,4},{6,7},{7,6},{8,9},{9,8},{10,11... | collective-permute-start | bytes 786440 | tf_op jit(solution)/shard_map/ppermute | solution.py:26
  75.8 3.4 %copy-start = (bf16[1,2,256,8192]{3,2,1,0:T(8,128)(2,1)S(1)}, bf16[1,2,256,8192]{3,2,1,0:T(8,128)(2,1)}, u32[]{:S(2)}) copy-start(bf16[1,2,256,8192]{3,2,1,0:T(8,128)(2,1)} %refs_4_.3) | copy-start | bytes 25165828
  81.0 3.4 %copy-start.1 = (bf16[1,2,256,8192]{3,2,1,0:T(8,128)(2,1)S(1)}, bf16[1,2,256,8192]{3,2,1,0:T(8,128)(2,1)}, u32[]{:S(2)}) copy-start(bf16[1,2,256,8192]{3,2,1,0:T(8,128)(2,1)} %refs_4_.3) | copy-start | bytes 25165828

commit v8 on v5

--- a/solution.py
+++ b/solution.py
@@ -21,10 +21,16 @@
     return lax.ppermute(value, AXIS, pairs)
 
 
-def shifted(block, distance):
-    devices = range(lax.axis_size(AXIS))
-    route = [(i - distance, i) for i in devices if i - distance in devices]
-    return lax.ppermute(block, AXIS, route)
+def raised(value, layer, group):
+    size = lax.axis_size(AXIS)
+    came = lax.ppermute(value, AXIS, [(i, (i + group) % size) for i in range(size)])
+    return jnp.where(layer == 0, jnp.zeros_like(came), came)
+
+
+def lowered(value, layer, group):
+    size = lax.axis_size(AXIS)
+    came = lax.ppermute(value, AXIS, [((i + group) % size, i) for i in range(size)])
+    return jnp.where(layer == LAYERS - 1, jnp.zeros_like(came), came)
 
 
 def in_vmem(*arrays):
@@ -96,7 +102,11 @@
     group = rows // tokens
     chips = group // CORES
 
-    pre = jnp.dot(x_ref[...], enc_ref[0], preferred_element_type=jnp.float32)
+    half = depth // 2
+    pre = sum(
+        jnp.dot(x_ref[:, part], enc_ref[0, part, :], preferred_element_type=jnp.float32)
+        for part in (pl.ds(0, half), pl.ds(half, half))
+    )
     held[...] = jnp.maximum(pre + bias_ref[...].astype(jnp.float32), 0.0)
     for block in range(group):
         core, chip = block // chips, block % chips
@@ -146,9 +156,12 @@
 
 
 def back(rows_ref, dec_ref, reach, total):
-    return total + lax.dot_general(
-        rows_ref[...], dec_ref[0, reach], (((1,), (1,)), ((), ())), preferred_element_type=jnp.float32
-    )
+    half = rows_ref.shape[1] // 2
+    for part in (pl.ds(0, half), pl.ds(half, half)):
+        total = total + lax.dot_general(
+            rows_ref[:, part], dec_ref[0, reach, :, part], (((1,), (1,)), ((), ())), preferred_element_type=jnp.float32
+        )
+    return total
 
 
 def grad_own_kernel(rows_ref, dec_ref, out_ref):
@@ -192,26 +205,28 @@
 def on_device(resid, enc_weight, enc_bias, active, dec_weight, target):
     group = lax.axis_size(AXIS) // LAYERS
     chips = group // CORES
-    place = (lax.axis_index(AXIS) % group).astype(jnp.int32).reshape(1)
+    index = lax.axis_index(AXIS)
+    layer = index // group
+    place = (index % group).astype(jnp.int32).reshape(1)
     tokens = resid.shape[1]
-    (enc,), (dec,) = loaded(enc_weight), loaded(dec_weight)
+    enc, dec = loaded(enc_weight, dec_weight)
     x = gathered(resid[0], chips)
     codes, next_near, next_far = encoded(place, active[0], x, enc, enc_bias, dec, tokens)
     own_near, own_far = decoded(codes, dec)
     nexts = blocks_of(next_near, next_far, chips)
     owns = blocks_of(own_near, own_far, chips)
-    risen = shifted(nexts[-1].astype(jnp.bfloat16), group)
+    risen = raised(nexts[-1].astype(jnp.bfloat16), layer, group)
     next_sum = summed(nexts, range(1, chips - 1)).astype(jnp.bfloat16)
     owns[-1] = owns[-1] + risen.astype(jnp.float32)
-    from_before = shifted(next_sum, group).astype(jnp.float32)
+    from_before = raised(next_sum, layer, group).astype(jnp.float32)
     own_sum = summed(owns, range(1, chips))
     error = (own_sum + from_before - target[0].astype(jnp.float32)).astype(jnp.bfloat16)
 
-    later = shifted(error, -group)
+    later = lowered(error, layer, group)
     here = [error] + [swap(error, CORES * chip) for chip in range(1, chips)]
     after = [later] + [swap(later, CORES * chip) for chip in range(1, chips - 1)]
     here[-1], _ = lax.optimization_barrier((here[-1], later))
-    last = shifted(here[-1], -group)
+    last = lowered(here[-1], layer, group)
     here_near = jnp.concatenate(here, axis=0)
     here_far = swap(here_near, 1)
     here_rows = jnp.concatenate([here_near, here_far], axis=0)

time: 73.9 us -> 64.1 us (0.87)
  waiting for transfers between devices: 19.3 us -> 12.8 us
  starting transfers between devices: 27.6 us -> 26 us
  Pallas kernels: 13 us -> 12.1 us
    ppermute x22, waiting for transfers between devices: 11.7 us -> 6.84 us  [swap(): return lax.ppermute(value, AXIS, pairs)]
    ppermute x4, waiting for transfers between devices: 7.57 us -> 6 us  [the longest x2 3.67 us: raised(): lax.ppermute(value, AXIS, [(i, (i + group) % size) for i in range(size)])]
    ppermute x4, starting transfers between devices: 9.92 us -> 8.54 us  [the longest x2 5.19 us: lowered(): lax.ppermute(value, AXIS, [((i + group) % size, i) for i in range(size)])]
    pallas_call x2 -> x1, Pallas kernels: 5.62 us -> 4.69 us  [loaded(): pl.pallas_call(load_kernel, out_shape=[pltpu.VMEM(w.shape, w.dtype) for w...]
    unnamed x28 -> x26, local copies, waits for them, and re-layouts: 11.9 us -> 11.2 us
  transfers between devices with their start and end apart: 26 -> 26, of which waited for: 11 -> 9; matrix products, arithmetic and copies ran while one was open for 2% -> 2% of each run, Pallas kernels for 11% -> 11%
where the time goes in v8:
time: 64.1 us; the launch traced here: 63.8 us
  starting transfers between devices  26 us (41%)
  waiting for transfers between devices  12.8 us (20%)
  Pallas kernels  12.1 us (19%)
  local copies, waits for them, and re-layouts  11.3 us (18%)
  between operations  1.01 us (2%)
    ppermute x22, starting transfers between devices, swap(): return lax.ppermute(value, AXIS, pairs)  17.5 us
    unnamed x26, local copies, waits for them, and re-layouts  11.2 us
    ppermute x22, waiting for transfers between devices, swap(): return lax.ppermute(value, AXIS, pairs)  6.84 us
    ppermute x2, starting transfers between devices, lowered(): lax.ppermute(value, AXIS, [((i + group) % size, i) for i in range(size)])  5.19 us
    pallas_call x1, Pallas kernels, loaded(): pl.pallas_call(load_kernel, out_shape=[pltpu.VMEM(w.shape, w.dtype) for w...  4.69 us
    ppermute x2, waiting for transfers between devices, raised(): lax.ppermute(value, AXIS, [(i, (i + group) % size) for i in range(size)])  3.67 us
    ppermute x2, starting transfers between devices, raised(): lax.ppermute(value, AXIS, [(i, (i + group) % size) for i in range(size)])  3.35 us
    pallas_call x1, Pallas kernels, encoded(): pl.pallas_call(functools.partial(encode_kernel, tokens), out_shape=[pltpu...  3.14 us
  transfers between devices with their start and end apart: 26, of which 9 were waited for; matrix products, arithmetic and copies ran while one was open for 2% of the time, Pallas kernels for 11%

profile of v8, /device:TPU:0, one launch (start us, length us, event | category | flops | bytes accessed | tf_op | source)
XLA Modules:
  0.0 63.8 jit_solution(5651084286861269714)
XLA Ops:
  0.6 0.5 collective-permute-start.3
  1.1 3.5 %collective-permute-start.2 = (bf16[8,8192]{1,0:T(8,128)(2,1)}, bf16[8,8192]{1,0:T(8,128)(2,1)S(1)}, u32[]{:S(2)}, u32[]{:S(2)}) collective-permute-start(bf16[8,8192]{1,0:T(8,128)(2,1)} %bitcast.12), channel_id=1, source_target_pairs={{0,6},{1,7},{2,4},{3,5},{4,2},{5,3},{6,0},{7,1},{8,14},{9,15},{10,... | collective-permute-start | bytes 393224 | tf_op jit(solution)/shard_map/ppermute | solution.py:21
  4.7 0.5 collective-permute-start.1
  5.2 0.1 collective-permute-start
  5.3 0.9 %constant_dynamic-update-slice_fusion.7 = bf16[64,8192]{1,0:T(8,128)(2,1)S(1)} fusion(bf16[1,8,8192]{2,1,0:T(8,128)(2,1)} %param.6), kind=kLoop, calls=%fused_computation.25 | loop fusion | bytes 262144
  6.3 0.0 copy-start.4
  6.3 0.0 copy-start.5
  6.3 4.7 %load_weights.1 = (bf16[1,8192,256]{2,1,0:T(8,128)(2,1)S(1)}, bf16[1,2,256,8192]{3,2,1,0:T(8,128)(2,1)S(1)}) custom-call(bf16[1,8192,256]{2,1,0:T(8,128)(2,1)} %refs_0_.1, bf16[1,2,256,8192]{3,2,1,0:T(8,128)(2,1)} %refs_1_.1), custom_call_target="tpu_custom_call" | custom-call | bytes 25165824 | tf_op jit(solution)/shard_map/load_weights/pallas_call | solution.py:78
  11.0 0.0 collective-permute-done.2
  11.0 0.1 collective-permute-start.6
  11.1 0.7 %collective-permute-done.1 = bf16[8,8192]{1,0:T(8,128)(2,1)S(1)} collective-permute-done((bf16[8,8192]{1,0:T(8,128)(2,1)}, bf16[8,8192]{1,0:T(8,128)(2,1)S(1)}, u32[]{:S(2)}, u32[]{:S(2)}) %collective-permute-start.1) | collective-permute-done | bytes 131104 | tf_op jit(solution)/shard_map/ppermute | solution.py:21
  11.8 0.0 collective-permute-start.5
  11.8 0.3 collective-permute-done
  12.1 0.2 collective-permute-start.4
  12.4 1.1 %collective-permute-done.4 = bf16[8,8192]{1,0:T(8,128)(2,1)S(1)} collective-permute-done((bf16[8,8192]{1,0:T(8,128)(2,1)S(1)}, bf16[8,8192]{1,0:T(8,128)(2,1)S(1)}, u32[]{:S(2)}, u32[]{:S(2)}) %collective-permute-start.4) | collective-permute-done | bytes 131104 | tf_op jit(solution)/shard_map/ppermute | solution.py:21
  13.4 0.0 collective-permute-done.5
  13.5 3.1 %encode.1 = (bf16[64,256]{1,0:T(8,128)(2,1)S(1)}, f32[32,8192]{1,0:T(8,128)S(1)}, bf16[32,8192]{1,0:T(8,128)(2,1)S(1)}) custom-call(s32[1]{0:T(128)} %bitcast.place_ref, s32[2,2]{1,0:T(2,128)S(1)} %bitcast.9, bf16[64,8192]{1,0:T(8,128)(2,1)S(1)} %constant_dynamic-update-slice_fusion.x_ref, bf16[1,8192,256]{2,1,0:T(8,128)(2,1)S(1)} %get-tuple-element.11.enc_ref, ...), custom_call_target="tpu_custom_call" | custom-call | flops 536870912 | bytes 8388608 | tf_op jit(solution)/shard_map/encode/pallas_call | solution.py:132
  16.7 0.3 collective-permute-start.10
  17.0 3.4 %copy-done.1 = bf16[1,2,256,8192]{3,2,1,0:T(8,128)(2,1)S(1)} copy-done((bf16[1,2,256,8192]{3,2,1,0:T(8,128)(2,1)S(1)}, bf16[1,2,256,8192]{3,2,1,0:T(8,128)(2,1)}, u32[]{:S(2)}) %copy-start.1) | copy-done | bytes 8388632
  20.3 0.8 %decode_own.1 = (f32[32,8192]{1,0:T(8,128)S(1)}, bf16[32,8192]{1,0:T(8,128)(2,1)S(1)}) custom-call(bf16[64,256]{1,0:T(8,128)(2,1)S(1)} %get-tuple-element.13.codes_ref, bf16[1,2,256,8192]{3,2,1,0:T(8,128)(2,1)S(1)} %copy-done.1), custom_call_target="tpu_custom_call" | custom-call | flops 268435456 | bytes 4194304 | tf_op jit(solution)/shard_map/decode_own/pallas_call | solution.py:147
  21.2 0.4 collective-permute-start.7
  21.6 0.1 fusion.10
  21.7 1.7 %collective-permute-start.11 = (bf16[8,8192]{1,0:T(8,128)(2,1)S(1)}, bf16[8,8192]{1,0:T(8,128)(2,1)S(1)}, u32[]{:S(2)}, u32[]{:S(2)}) collective-permute-start(bf16[8,8192]{1,0:T(8,128)(2,1)S(1)} %get-tuple-element.28), channel_id=1, source_target_pairs={{0,8},{1,9},{2,10},{3,11},{4,12},{5,13},{6,14},{7,15},{8,16},{9,17... | collective-permute-start | bytes 393224 | tf_op jit(solution)/shard_map/ppermute | solution.py:26
  23.4 1.5 %collective-permute-start.14 = (bf16[8,8192]{1,0:T(8,128)(2,1)S(1)}, bf16[8,8192]{1,0:T(8,128)(2,1)S(1)}, u32[]{:S(2)}, u32[]{:S(2)}) collective-permute-start(bf16[8,8192]{1,0:T(8,128)(2,1)S(1)} %get-tuple-element.29), channel_id=1, source_target_pairs={{0,4},{1,5},{2,6},{3,7},{4,0},{5,1},{6,2},{7,3},{8,12},{9,13},{10,... | collective-permute-start | bytes 393224 | tf_op jit(solution)/shard_map/ppermute | solution.py:21
  24.9 1.3 %collective-permute-start.13 = (bf16[8,8192]{1,0:T(8,128)(2,1)S(1)}, bf16[8,8192]{1,0:T(8,128)(2,1)S(1)}, u32[]{:S(2)}, u32[]{:S(2)}) collective-permute-start(bf16[8,8192]{1,0:T(8,128)(2,1)S(1)} %get-tuple-element.30), channel_id=1, source_target_pairs={{0,2},{1,3},{2,0},{3,1},{4,6},{5,7},{6,4},{7,5},{8,10},{9,11},{10,... | collective-permute-start | bytes 393224 | tf_op jit(solution)/shard_map/ppermute | solution.py:21
  26.3 0.0 collective-permute-done.7
  26.3 0.1 fusion.9
  26.4 0.8 %collective-permute-start.8 = (bf16[8,8192]{1,0:T(8,128)(2,1)S(1)}, bf16[8,8192]{1,0:T(8,128)(2,1)S(1)}, u32[]{:S(2)}, u32[]{:S(2)}) collective-permute-start(bf16[8,8192]{1,0:T(8,128)(2,1)S(1)} %get-tuple-element.26), channel_id=1, source_target_pairs={{0,2},{1,3},{2,0},{3,1},{4,6},{5,7},{6,4},{7,5},{8,10},{9,11},{10,... | collective-permute-start | bytes 393224 | tf_op jit(solution)/shard_map/ppermute | solution.py:21
  27.2 0.5 collective-permute-start.9
  27.7 1.2 %collective-permute-done.14 = bf16[8,8192]{1,0:T(8,128)(2,1)S(1)} collective-permute-done((bf16[8,8192]{1,0:T(8,128)(2,1)S(1)}, bf16[8,8192]{1,0:T(8,128)(2,1)S(1)}, u32[]{:S(2)}, u32[]{:S(2)}) %collective-permute-start.14) | collective-permute-done | bytes 131104 | tf_op jit(solution)/shard_map/ppermute | solution.py:21
  28.9 2.5 %collective-permute-done.13 = bf16[8,8192]{1,0:T(8,128)(2,1)S(1)} collective-permute-done((bf16[8,8192]{1,0:T(8,128)(2,1)S(1)}, bf16[8,8192]{1,0:T(8,128)(2,1)S(1)}, u32[]{:S(2)}, u32[]{:S(2)}) %collective-permute-start.13) | collective-permute-done | bytes 131104 | tf_op jit(solution)/shard_map/ppermute | solution.py:21
  31.4 1.6 %collective-permute-start.15 = (bf16[8,8192]{1,0:T(8,128)(2,1)S(1)}, bf16[8,8192]{1,0:T(8,128)(2,1)S(1)}, u32[]{:S(2)}, u32[]{:S(2)}) collective-permute-start(bf16[8,8192]{1,0:T(8,128)(2,1)S(1)} %fusion.1), channel_id=1, source_target_pairs={{0,8},{1,9},{2,10},{3,11},{4,12},{5,13},{6,14},{7,15},{8,16},{9,17... | collective-permute-start | bytes 393224 | tf_op jit(solution)/shard_map/ppermute | solution.py:26
  33.1 1.5 %collective-permute-start.12 = (bf16[8,8192]{1,0:T(8,128)(2,1)S(1)}, bf16[8,8192]{1,0:T(8,128)(2,1)S(1)}, u32[]{:S(2)}, u32[]{:S(2)}) collective-permute-start(bf16[8,8192]{1,0:T(8,128)(2,1)S(1)} %fusion.2), channel_id=1, source_target_pairs={{0,6},{1,7},{2,4},{3,5},{4,2},{5,3},{6,0},{7,1},{8,14},{9,15},{10,... | collective-permute-start | bytes 393224 | tf_op jit(solution)/shard_map/ppermute | solution.py:21
  34.6 0.0 collective-permute-done.8
  34.6 0.0 collective-permute-done.9
  34.6 3.7 %collective-permute-done.15 = bf16[8,8192]{1,0:T(8,128)(2,1)S(1)} collective-permute-done((bf16[8,8192]{1,0:T(8,128)(2,1)S(1)}, bf16[8,8192]{1,0:T(8,128)(2,1)S(1)}, u32[]{:S(2)}, u32[]{:S(2)}) %collective-permute-start.15) | collective-permute-done | bytes 131104 | tf_op jit(solution)/shard_map/ppermute | solution.py:26
  38.2 0.8 %collective-permute-done.12 = bf16[8,8192]{1,0:T(8,128)(2,1)S(1)} collective-permute-done((bf16[8,8192]{1,0:T(8,128)(2,1)S(1)}, bf16[8,8192]{1,0:T(8,128)(2,1)S(1)}, u32[]{:S(2)}, u32[]{:S(2)}) %collective-permute-start.12) | collective-permute-done | bytes 131104 | tf_op jit(solution)/shard_map/ppermute | solution.py:21
  39.0 0.1 constant_dynamic-update-slice_fusion.12
  39.1 0.0 copy-start.6
  39.1 2.3 %collective-permute-start.16 = (bf16[8,8192]{1,0:T(8,128)(2,1)S(1)}, bf16[8,8192]{1,0:T(8,128)(2,1)S(1)}, u32[]{:S(2)}, u32[]{:S(2)}) collective-permute-start(bf16[8,8192]{1,0:T(8,128)(2,1)S(1)} %get-tuple-element.21), channel_id=1, source_target_pairs={{8,0},{9,1},{10,2},{11,3},{12,4},{13,5},{14,6},{15,7},{16,8},{17,9... | collective-permute-start | bytes 393224 | tf_op jit(solution)/shard_map/ppermute | solution.py:32
  41.4 1.4 %collective-permute-start.21 = (bf16[8,8192]{1,0:T(8,128)(2,1)S(1)}, bf16[8,8192]{1,0:T(8,128)(2,1)S(1)}, u32[]{:S(2)}, u32[]{:S(2)}) collective-permute-start(bf16[8,8192]{1,0:T(8,128)(2,1)S(1)} %get-tuple-element.21), channel_id=1, source_target_pairs={{0,6},{1,7},{2,4},{3,5},{4,2},{5,3},{6,0},{7,1},{8,14},{9,15},{10,... | collective-permute-start | bytes 393224 | tf_op jit(solution)/shard_map/ppermute | solution.py:21
  42.9 1.4 %collective-permute-start.20 = (bf16[8,8192]{1,0:T(8,128)(2,1)S(1)}, bf16[8,8192]{1,0:T(8,128)(2,1)S(1)}, u32[]{:S(2)}, u32[]{:S(2)}) collective-permute-start(bf16[8,8192]{1,0:T(8,128)(2,1)S(1)} %get-tuple-element.21), channel_id=1, source_target_pairs={{0,4},{1,5},{2,6},{3,7},{4,0},{5,1},{6,2},{7,3},{8,12},{9,13},{10,... | collective-permute-start | bytes 393224 | tf_op jit(solution)/shard_map/ppermute | solution.py:21
  44.2 0.7 %collective-permute-start.19 = (bf16[8,8192]{1,0:T(8,128)(2,1)S(1)}, bf16[8,8192]{1,0:T(8,128)(2,1)S(1)}, u32[]{:S(2)}, u32[]{:S(2)}) collective-permute-start(bf16[8,8192]{1,0:T(8,128)(2,1)S(1)} %get-tuple-element.21), channel_id=1, source_target_pairs={{0,2},{1,3},{2,0},{3,1},{4,6},{5,7},{6,4},{7,5},{8,10},{9,11},{10,... | collective-permute-start | bytes 393224 | tf_op jit(solution)/shard_map/ppermute | solution.py:21
  44.9 0.0 collective-permute-done.16
  44.9 0.6 collective-permute-start.18
  45.5 1.5 %collective-permute-start.17 = (bf16[8,8192]{1,0:T(8,128)(2,1)S(1)}, bf16[8,8192]{1,0:T(8,128)(2,1)S(1)}, u32[]{:S(2)}, u32[]{:S(2)}) collective-permute-start(bf16[8,8192]{1,0:T(8,128)(2,1)S(1)} %broadcast_select_fusion.1), channel_id=1, source_target_pairs={{0,2},{1,3},{2,0},{3,1},{4,6},{5,7},{6,4},{7,5},{8,10},{9,11},{10,... | collective-permute-start | bytes 393224 | tf_op jit(solution)/shard_map/ppermute | solution.py:21
  47.0 0.4 collective-permute-done.21
  47.4 2.9 %collective-permute-start.23 = (bf16[8,8192]{1,0:T(8,128)(2,1)S(1)}, bf16[8,8192]{1,0:T(8,128)(2,1)S(1)}, u32[]{:S(2)}, u32[]{:S(2)}) collective-permute-start(bf16[8,8192]{1,0:T(8,128)(2,1)S(1)} %collective-permute-done.21), channel_id=1, source_target_pairs={{8,0},{9,1},{10,2},{11,3},{12,4},{13,5},{14,6},{15,7},{16,8},{17,9... | collective-permute-start | bytes 393224 | tf_op jit(solution)/shard_map/ppermute | solution.py:32
  50.3 0.0 collective-permute-done.19
  50.3 0.0 collective-permute-done.20
  50.3 0.1 pad_maximum_fusion.1
  50.4 0.1 collective-permute-start.22
  50.5 2.3 %collective-permute-done.23 = bf16[8,8192]{1,0:T(8,128)(2,1)S(1)} collective-permute-done((bf16[8,8192]{1,0:T(8,128)(2,1)S(1)}, bf16[8,8192]{1,0:T(8,128)(2,1)S(1)}, u32[]{:S(2)}, u32[]{:S(2)}) %collective-permute-start.23) | collective-permute-done | bytes 131104 | tf_op jit(solution)/shard_map/ppermute | solution.py:32
  52.8 0.1 collective-permute-start.25
  52.9 0.0 collective-permute-done.18
  52.9 0.0 collective-permute-done.17
  52.9 0.0 collective-permute-done.22
  53.0 0.5 collective-permute-start.24
  53.6 3.4 %copy-done.2 = bf16[1,2,256,8192]{3,2,1,0:T(8,128)(2,1)S(1)} copy-done((bf16[1,2,256,8192]{3,2,1,0:T(8,128)(2,1)S(1)}, bf16[1,2,256,8192]{3,2,1,0:T(8,128)(2,1)}, u32[]{:S(2)}) %copy-start.2) | copy-done | bytes 8388632
  56.9 1.4 %grad_own.1.own_ref = f32[64,256]{1,0:T(8,128)S(1)} custom-call(bf16[64,8192]{1,0:T(8,128)(2,1)S(1)} %constant_dynamic-update-slice_fusion.8.rows_ref, bf16[1,2,256,8192]{3,2,1,0:T(8,128)(2,1)S(1)} %copy-done.2), custom_call_target="tpu_custom_call" | custom-call | flops 268435456 | bytes 4194304 | tf_op jit(solution)/shard_map/grad_own/pallas_call | solution.py:182
  58.3 0.0 collective-permute-done.24
  58.3 0.1 pad_maximum_fusion.rows_ref
  58.4 3.4 %copy-done.3 = bf16[1,2,256,8192]{3,2,1,0:T(8,128)(2,1)S(1)} copy-done((bf16[1,2,256,8192]{3,2,1,0:T(8,128)(2,1)S(1)}, bf16[1,2,256,8192]{3,2,1,0:T(8,128)(2,1)}, u32[]{:S(2)}) %copy-start.3) | copy-done | bytes 8388632
  61.8 2.0 %grad_all.1 = f32[1,64,256]{2,1,0:T(8,128)} custom-call(s32[1]{0:T(128)} %bitcast.place_ref, bf16[64,8192]{1,0:T(8,128)(2,1)S(1)} %pad_maximum_fusion.rows_ref, bf16[1,2,256,8192]{3,2,1,0:T(8,128)(2,1)S(1)} %copy-done.3, f32[64,256]{1,0:T(8,128)S(1)} %grad_own.1.own_ref), custom_call_target="tpu_custom_call" | custom-call | flops 268435456 | bytes 4194304 | tf_op jit(solution)/shard_map/grad_all/pallas_call | solution.py:194
  (33 shorter events, 0.4 us)
Async XLA Ops:
  0.6 11.7 %collective-permute-start.3 = (bf16[8,8192]{1,0:T(8,128)(2,1)}, bf16[8,8192]{1,0:T(8,128)(2,1)S(1)}, u32[]{:S(2)}, u32[]{:S(2)}) collective-permute-start(bf16[8,8192]{1,0:T(8,128)(2,1)} %bitcast.11), channel_id=1, source_target_pairs={{0,1},{1,0},{2,3},{3,2},{4,5},{5,4},{6,7},{7,6},{8,9},{9,8},{10,11... | collective-permute-start | bytes 393224 | tf_op jit(solution)/shard_map/ppermute | solution.py:21
  1.1 9.9 %collective-permute-start.2 = (bf16[8,8192]{1,0:T(8,128)(2,1)}, bf16[8,8192]{1,0:T(8,128)(2,1)S(1)}, u32[]{:S(2)}, u32[]{:S(2)}) collective-permute-start(bf16[8,8192]{1,0:T(8,128)(2,1)} %bitcast.12), channel_id=1, source_target_pairs={{0,6},{1,7},{2,4},{3,5},{4,2},{5,3},{6,0},{7,1},{8,14},{9,15},{10,... | collective-permute-start | bytes 393224 | tf_op jit(solution)/shard_map/ppermute | solution.py:21
  4.7 7.1 %collective-permute-start.1 = (bf16[8,8192]{1,0:T(8,128)(2,1)}, bf16[8,8192]{1,0:T(8,128)(2,1)S(1)}, u32[]{:S(2)}, u32[]{:S(2)}) collective-permute-start(bf16[8,8192]{1,0:T(8,128)(2,1)} %bitcast.13), channel_id=1, source_target_pairs={{0,4},{1,5},{2,6},{3,7},{4,0},{5,1},{6,2},{7,3},{8,12},{9,13},{10,... | collective-permute-start | bytes 393224 | tf_op jit(solution)/shard_map/ppermute | solution.py:21
  5.2 6.9 %collective-permute-start = (bf16[8,8192]{1,0:T(8,128)(2,1)}, bf16[8,8192]{1,0:T(8,128)(2,1)S(1)}, u32[]{:S(2)}, u32[]{:S(2)}) collective-permute-start(bf16[8,8192]{1,0:T(8,128)(2,1)} %bitcast.14), channel_id=1, source_target_pairs={{0,2},{1,3},{2,0},{3,1},{4,6},{5,7},{6,4},{7,5},{8,10},{9,11},{10,... | collective-permute-start | bytes 393224 | tf_op jit(solution)/shard_map/ppermute | solution.py:21
  6.3 7.2 %copy-start.4 = (s32[1,2,2]{2,1,0:T(2,128)S(1)}, s32[1,2,2]{2,1,0:T(2,128)}, u32[]{:S(2)}) copy-start(s32[1,2,2]{2,1,0:T(2,128)} %param.9) | copy-start | bytes 52
  6.3 7.2 %copy-start.5 = (bf16[1,256]{1,0:T(2,128)(2,1)S(1)}, bf16[1,256]{1,0:T(2,128)(2,1)}, u32[]{:S(2)}) copy-start(bf16[1,256]{1,0:T(2,128)(2,1)} %bias_ref.1) | copy-start | bytes 1540
  11.0 5.7 %copy-start = (bf16[1,2,256,8192]{3,2,1,0:T(8,128)(2,1)}, bf16[1,2,256,8192]{3,2,1,0:T(8,128)(2,1)S(1)}, u32[]{:S(2)}) copy-start(bf16[1,2,256,8192]{3,2,1,0:T(8,128)(2,1)S(1)} %get-tuple-element.12.dec_ref) | copy-start | bytes 25165828
  11.0 2.5 %collective-permute-start.6 = (bf16[8,8192]{1,0:T(8,128)(2,1)S(1)}, bf16[8,8192]{1,0:T(8,128)(2,1)S(1)}, u32[]{:S(2)}, u32[]{:S(2)}) collective-permute-start(bf16[8,8192]{1,0:T(8,128)(2,1)S(1)} %collective-permute-done.2), channel_id=1, source_target_pairs={{0,1},{1,0},{2,3},{3,2},{4,5},{5,4},{6,7},{7,6},{8,9},{9,8},{10,11... | collective-permute-start | bytes 393224 | tf_op jit(solution)/shard_map/ppermute | solution.py:21
  11.8 1.7 %collective-permute-start.5 = (bf16[8,8192]{1,0:T(8,128)(2,1)S(1)}, bf16[8,8192]{1,0:T(8,128)(2,1)S(1)}, u32[]{:S(2)}, u32[]{:S(2)}) collective-permute-start(bf16[8,8192]{1,0:T(8,128)(2,1)S(1)} %collective-permute-done.1), channel_id=1, source_target_pairs={{0,1},{1,0},{2,3},{3,2},{4,5},{5,4},{6,7},{7,6},{8,9},{9,8},{10,11... | collective-permute-start | bytes 393224 | tf_op jit(solution)/shard_map/ppermute | solution.py:21
  12.1 1.3 %collective-permute-start.4 = (bf16[8,8192]{1,0:T(8,128)(2,1)S(1)}, bf16[8,8192]{1,0:T(8,128)(2,1)S(1)}, u32[]{:S(2)}, u32[]{:S(2)}) collective-permute-start(bf16[8,8192]{1,0:T(8,128)(2,1)S(1)} %collective-permute-done), channel_id=1, source_target_pairs={{0,1},{1,0},{2,3},{3,2},{4,5},{5,4},{6,7},{7,6},{8,9},{9,8},{10,11... | collective-permute-start | bytes 393224 | tf_op jit(solution)/shard_map/ppermute | solution.py:21
  16.7 4.9 %collective-permute-start.10 = (bf16[32,8192]{1,0:T(8,128)(2,1)S(1)}, bf16[32,8192]{1,0:T(8,128)(2,1)S(1)}, u32[]{:S(2)}, u32[]{:S(2)}) collective-permute-start(bf16[32,8192]{1,0:T(8,128)(2,1)S(1)} %get-tuple-element.17), channel_id=1, source_target_pairs={{0,1},{1,0},{2,3},{3,2},{4,5},{5,4},{6,7},{7,6},{8,9},{9,8},{10,11... | collective-permute-start | bytes 1572872 | tf_op jit(solution)/shard_map/ppermute | solution.py:21
  17.0 3.4 %copy-start.1 = (bf16[1,2,256,8192]{3,2,1,0:T(8,128)(2,1)S(1)}, bf16[1,2,256,8192]{3,2,1,0:T(8,128)(2,1)}, u32[]{:S(2)}) copy-start(bf16[1,2,256,8192]{3,2,1,0:T(8,128)(2,1)} %copy-done) | copy-start | bytes 25165828
  21.2 5.1 %collective-permute-start.7 = (bf16[32,8192]{1,0:T(8,128)(2,1)S(1)}, bf16[32,8192]{1,0:T(8,128)(2,1)S(1)}, u32[]{:S(2)}, u32[]{:S(2)}) collective-permute-start(bf16[32,8192]{1,0:T(8,128)(2,1)S(1)} %get-tuple-element.15), channel_id=1, source_target_pairs={{0,1},{1,0},{2,3},{3,2},{4,5},{5,4},{6,7},{7,6},{8,9},{9,8},{10,11... | collective-permute-start | bytes 1572872 | tf_op jit(solution)/shard_map/ppermute | solution.py:21
  21.7 11.3 %collective-permute-start.11 = (bf16[8,8192]{1,0:T(8,128)(2,1)S(1)}, bf16[8,8192]{1,0:T(8,128)(2,1)S(1)}, u32[]{:S(2)}, u32[]{:S(2)}) collective-permute-start(bf16[8,8192]{1,0:T(8,128)(2,1)S(1)} %get-tuple-element.28), channel_id=1, source_target_pairs={{0,8},{1,9},{2,10},{3,11},{4,12},{5,13},{6,14},{7,15},{8,16},{9,17... | collective-permute-start | bytes 393224 | tf_op jit(solution)/shard_map/ppermute | solution.py:26
  23.4 5.5 %collective-permute-start.14 = (bf16[8,8192]{1,0:T(8,128)(2,1)S(1)}, bf16[8,8192]{1,0:T(8,128)(2,1)S(1)}, u32[]{:S(2)}, u32[]{:S(2)}) collective-permute-start(bf16[8,8192]{1,0:T(8,128)(2,1)S(1)} %get-tuple-element.29), channel_id=1, source_target_pairs={{0,4},{1,5},{2,6},{3,7},{4,0},{5,1},{6,2},{7,3},{8,12},{9,13},{10,... | collective-permute-start | bytes 393224 | tf_op jit(solution)/shard_map/ppermute | solution.py:21
  24.9 6.4 %collective-permute-start.13 = (bf16[8,8192]{1,0:T(8,128)(2,1)S(1)}, bf16[8,8192]{1,0:T(8,128)(2,1)S(1)}, u32[]{:S(2)}, u32[]{:S(2)}) collective-permute-start(bf16[8,8192]{1,0:T(8,128)(2,1)S(1)} %get-tuple-element.30), channel_id=1, source_target_pairs={{0,2},{1,3},{2,0},{3,1},{4,6},{5,7},{6,4},{7,5},{8,10},{9,11},{10,... | collective-permute-start | bytes 393224 | tf_op jit(solution)/shard_map/ppermute | solution.py:21
  26.3 12.7 %copy-start.7 = (bf16[1,8,8192]{2,1,0:T(8,128)(2,1)S(1)}, bf16[1,8,8192]{2,1,0:T(8,128)(2,1)}, u32[]{:S(2)}) copy-start(bf16[1,8,8192]{2,1,0:T(8,128)(2,1)} %param.11) | copy-start | bytes 393220
  26.4 8.2 %collective-permute-start.8 = (bf16[8,8192]{1,0:T(8,128)(2,1)S(1)}, bf16[8,8192]{1,0:T(8,128)(2,1)S(1)}, u32[]{:S(2)}, u32[]{:S(2)}) collective-permute-start(bf16[8,8192]{1,0:T(8,128)(2,1)S(1)} %get-tuple-element.26), channel_id=1, source_target_pairs={{0,2},{1,3},{2,0},{3,1},{4,6},{5,7},{6,4},{7,5},{8,10},{9,11},{10,... | collective-permute-start | bytes 393224 | tf_op jit(solution)/shard_map/ppermute | solution.py:21
  27.2 7.4 %collective-permute-start.9 = (bf16[8,8192]{1,0:T(8,128)(2,1)S(1)}, bf16[8,8192]{1,0:T(8,128)(2,1)S(1)}, u32[]{:S(2)}, u32[]{:S(2)}) collective-permute-start(bf16[8,8192]{1,0:T(8,128)(2,1)S(1)} %get-tuple-element.27), channel_id=1, source_target_pairs={{0,4},{1,5},{2,6},{3,7},{4,0},{5,1},{6,2},{7,3},{8,12},{9,13},{10,... | collective-permute-start | bytes 393224 | tf_op jit(solution)/shard_map/ppermute | solution.py:21
  31.4 6.8 %collective-permute-start.15 = (bf16[8,8192]{1,0:T(8,128)(2,1)S(1)}, bf16[8,8192]{1,0:T(8,128)(2,1)S(1)}, u32[]{:S(2)}, u32[]{:S(2)}) collective-permute-start(bf16[8,8192]{1,0:T(8,128)(2,1)S(1)} %fusion.1), channel_id=1, source_target_pairs={{0,8},{1,9},{2,10},{3,11},{4,12},{5,13},{6,14},{7,15},{8,16},{9,17... | collective-permute-start | bytes 393224 | tf_op jit(solution)/shard_map/ppermute | solution.py:26
  33.1 5.9 %collective-permute-start.12 = (bf16[8,8192]{1,0:T(8,128)(2,1)S(1)}, bf16[8,8192]{1,0:T(8,128)(2,1)S(1)}, u32[]{:S(2)}, u32[]{:S(2)}) collective-permute-start(bf16[8,8192]{1,0:T(8,128)(2,1)S(1)} %fusion.2), channel_id=1, source_target_pairs={{0,6},{1,7},{2,4},{3,5},{4,2},{5,3},{6,0},{7,1},{8,14},{9,15},{10,... | collective-permute-start | bytes 393224 | tf_op jit(solution)/shard_map/ppermute | solution.py:21
  39.1 14.4 %copy-start.6 = (bf16[8,8192]{1,0:T(8,128)(2,1)}, bf16[8,8192]{1,0:T(8,128)(2,1)S(1)}, u32[]{:S(2)}) copy-start(bf16[8,8192]{1,0:T(8,128)(2,1)S(1)} %get-tuple-element.21) | copy-start | bytes 393220
  39.1 5.8 %collective-permute-start.16 = (bf16[8,8192]{1,0:T(8,128)(2,1)S(1)}, bf16[8,8192]{1,0:T(8,128)(2,1)S(1)}, u32[]{:S(2)}, u32[]{:S(2)}) collective-permute-start(bf16[8,8192]{1,0:T(8,128)(2,1)S(1)} %get-tuple-element.21), channel_id=1, source_target_pairs={{8,0},{9,1},{10,2},{11,3},{12,4},{13,5},{14,6},{15,7},{16,8},{17,9... | collective-permute-start | bytes 393224 | tf_op jit(solution)/shard_map/ppermute | solution.py:32
  41.4 6.0 %collective-permute-start.21 = (bf16[8,8192]{1,0:T(8,128)(2,1)S(1)}, bf16[8,8192]{1,0:T(8,128)(2,1)S(1)}, u32[]{:S(2)}, u32[]{:S(2)}) collective-permute-start(bf16[8,8192]{1,0:T(8,128)(2,1)S(1)} %get-tuple-element.21), channel_id=1, source_target_pairs={{0,6},{1,7},{2,4},{3,5},{4,2},{5,3},{6,0},{7,1},{8,14},{9,15},{10,... | collective-permute-start | bytes 393224 | tf_op jit(solution)/shard_map/ppermute | solution.py:21
  42.9 7.4 %collective-permute-start.20 = (bf16[8,8192]{1,0:T(8,128)(2,1)S(1)}, bf16[8,8192]{1,0:T(8,128)(2,1)S(1)}, u32[]{:S(2)}, u32[]{:S(2)}) collective-permute-start(bf16[8,8192]{1,0:T(8,128)(2,1)S(1)} %get-tuple-element.21), channel_id=1, source_target_pairs={{0,4},{1,5},{2,6},{3,7},{4,0},{5,1},{6,2},{7,3},{8,12},{9,13},{10,... | collective-permute-start | bytes 393224 | tf_op jit(solution)/shard_map/ppermute | solution.py:21
  44.2 6.1 %collective-permute-start.19 = (bf16[8,8192]{1,0:T(8,128)(2,1)S(1)}, bf16[8,8192]{1,0:T(8,128)(2,1)S(1)}, u32[]{:S(2)}, u32[]{:S(2)}) collective-permute-start(bf16[8,8192]{1,0:T(8,128)(2,1)S(1)} %get-tuple-element.21), channel_id=1, source_target_pairs={{0,2},{1,3},{2,0},{3,1},{4,6},{5,7},{6,4},{7,5},{8,10},{9,11},{10,... | collective-permute-start | bytes 393224 | tf_op jit(solution)/shard_map/ppermute | solution.py:21
  44.9 8.0 %collective-permute-start.18 = (bf16[8,8192]{1,0:T(8,128)(2,1)S(1)}, bf16[8,8192]{1,0:T(8,128)(2,1)S(1)}, u32[]{:S(2)}, u32[]{:S(2)}) collective-permute-start(bf16[8,8192]{1,0:T(8,128)(2,1)S(1)} %broadcast_select_fusion.1), channel_id=1, source_target_pairs={{0,4},{1,5},{2,6},{3,7},{4,0},{5,1},{6,2},{7,3},{8,12},{9,13},{10,... | collective-permute-start | bytes 393224 | tf_op jit(solution)/shard_map/ppermute | solution.py:21
  45.5 7.4 %collective-permute-start.17 = (bf16[8,8192]{1,0:T(8,128)(2,1)S(1)}, bf16[8,8192]{1,0:T(8,128)(2,1)S(1)}, u32[]{:S(2)}, u32[]{:S(2)}) collective-permute-start(bf16[8,8192]{1,0:T(8,128)(2,1)S(1)} %broadcast_select_fusion.1), channel_id=1, source_target_pairs={{0,2},{1,3},{2,0},{3,1},{4,6},{5,7},{6,4},{7,5},{8,10},{9,11},{10,... | collective-permute-start | bytes 393224 | tf_op jit(solution)/shard_map/ppermute | solution.py:21
  47.4 5.4 %collective-permute-start.23 = (bf16[8,8192]{1,0:T(8,128)(2,1)S(1)}, bf16[8,8192]{1,0:T(8,128)(2,1)S(1)}, u32[]{:S(2)}, u32[]{:S(2)}) collective-permute-start(bf16[8,8192]{1,0:T(8,128)(2,1)S(1)} %collective-permute-done.21), channel_id=1, source_target_pairs={{8,0},{9,1},{10,2},{11,3},{12,4},{13,5},{14,6},{15,7},{16,8},{17,9... | collective-permute-start | bytes 393224 | tf_op jit(solution)/shard_map/ppermute | solution.py:32
  50.4 2.6 %collective-permute-start.22 = (bf16[32,8192]{1,0:T(8,128)(2,1)S(1)}, bf16[32,8192]{1,0:T(8,128)(2,1)S(1)}, u32[]{:S(2)}, u32[]{:S(2)}) collective-permute-start(bf16[32,8192]{1,0:T(8,128)(2,1)S(1)} %pad_maximum_fusion.1), channel_id=1, source_target_pairs={{0,1},{1,0},{2,3},{3,2},{4,5},{5,4},{6,7},{7,6},{8,9},{9,8},{10,11... | collective-permute-start | bytes 1572872 | tf_op jit(solution)/shard_map/ppermute | solution.py:21
  52.8 5.5 %collective-permute-start.25 = (bf16[8,8192]{1,0:T(8,128)(2,1)S(1)}, bf16[8,8192]{1,0:T(8,128)(2,1)S(1)}, u32[]{:S(2)}, u32[]{:S(2)}) collective-permute-start(bf16[8,8192]{1,0:T(8,128)(2,1)S(1)} %broadcast_select_fusion), channel_id=1, source_target_pairs={{0,1},{1,0},{2,3},{3,2},{4,5},{5,4},{6,7},{7,6},{8,9},{9,8},{10,11... | collective-permute-start | bytes 393224 | tf_op jit(solution)/shard_map/ppermute | solution.py:21
  53.0 5.4 %collective-permute-start.24 = (bf16[24,8192]{1,0:T(8,128)(2,1)S(1)}, bf16[24,8192]{1,0:T(8,128)(2,1)S(1)}, u32[]{:S(2)}, u32[]{:S(2)}) collective-permute-start(bf16[24,8192]{1,0:T(8,128)(2,1)S(1)} %pad_maximum_fusion.2), channel_id=1, source_target_pairs={{0,1},{1,0},{2,3},{3,2},{4,5},{5,4},{6,7},{7,6},{8,9},{9,8},{10,11... | collective-permute-start | bytes 1179656 | tf_op jit(solution)/shard_map/ppermute | solution.py:21
  53.5 3.4 %copy-start.2 = (bf16[1,2,256,8192]{3,2,1,0:T(8,128)(2,1)S(1)}, bf16[1,2,256,8192]{3,2,1,0:T(8,128)(2,1)}, u32[]{:S(2)}) copy-start(bf16[1,2,256,8192]{3,2,1,0:T(8,128)(2,1)} %copy-done) | copy-start | bytes 25165828
  58.4 3.4 %copy-start.3 = (bf16[1,2,256,8192]{3,2,1,0:T(8,128)(2,1)S(1)}, bf16[1,2,256,8192]{3,2,1,0:T(8,128)(2,1)}, u32[]{:S(2)}) copy-start(bf16[1,2,256,8192]{3,2,1,0:T(8,128)(2,1)} %copy-done) | copy-start | bytes 25165828

commit v9 on v8

v9 whole, which is shorter than its diff:
```python
import functools

import jax
import jax.numpy as jnp
from jax import lax
from jax.experimental import pallas as pl
from jax.experimental.pallas import tpu as pltpu
from jax.sharding import PartitionSpec as P

BLOCK = 128
LAYERS = 4
TILE = 32
CORES = 2
CHUNK = 1024
LIMIT = 4 << 20
AXIS = "layer"

ANY_SPEC = pl.BlockSpec(memory_space=pl.ANY)
VMEM_SPEC = pl.BlockSpec(memory_space=pltpu.VMEM)
SMEM_SPEC = pl.BlockSpec(memory_space=pltpu.SMEM)


def turned(chip, chips):
    bits = chips.bit_length() - 1
    return sum(((chip >> bit) & 1) << (bits - 1 - bit) for bit in range(bits))


def across(value, chip, chips):
    masks = (CORES * chip, CORES * turned(chip, chips))
    pairs = [(i, i ^ masks[i % CORES]) for i in range(lax.axis_size(AXIS))]
    return lax.ppermute(value, AXIS, pairs)


def other_core(value):
    return lax.ppermute(value, AXIS, [(i, i ^ 1) for i in range(lax.axis_size(AXIS))])


def raised(value, layer, group):
    size = lax.axis_size(AXIS)
    came = lax.ppermute(value, AXIS, [(i, (i + group) % size) for i in range(size)])
    return jnp.where(layer == 0, jnp.zeros_like(came), came)


def lowered(value, layer, group):
    size = lax.axis_size(AXIS)
    came = lax.ppermute(value, AXIS, [((i + group) % size, i) for i in range(size)])
    return jnp.where(layer == LAYERS - 1, jnp.zeros_like(came), came)


def after(values, done):
    return lax.optimization_barrier((values, done))[0]


def slab_of(place, block, chips):
    far, chip = block // chips, block % chips
    odd = (place & 1) ^ far
    return place ^ (far + CORES * (chip * (1 - odd) + turned(chip, chips) * odd))


def in_vmem(*arrays):
    return [pltpu.with_memory_space_constraint(a, pltpu.VMEM) for a in arrays]


def in_hbm(*arrays):
    return [pltpu.with_memory_space_constraint(a, pltpu.HBM) for a in arrays]


def kernel_params(limit=LIMIT):
    return pltpu.CompilerParams(vmem_limit_bytes=limit)


def load_kernel(enc_hbm, dec_hbm, enc_ref, dec_ref, sems):
    copies = [
        pltpu.make_async_copy(enc_hbm, enc_ref, sems.at[0]),
        pltpu.make_async_copy(dec_hbm.at[0, 1], dec_ref, sems.at[1]),
    ]
    for copy in copies:
        copy.start()
    for copy in copies:
        copy.wait()


def loaded(enc, dec):
    return pl.pallas_call(
        load_kernel,
        out_shape=[pltpu.VMEM(enc.shape, enc.dtype), pltpu.VMEM(dec.shape[2:], dec.dtype)],
        in_specs=[ANY_SPEC] * 2,
        out_specs=[VMEM_SPEC] * 2,
        scratch_shapes=[pltpu.SemaphoreType.DMA((2,))],
        compiler_params=kernel_params(1 << 20),
        cost_estimate=pl.CostEstimate(flops=0, bytes_accessed=4 * (enc.size + dec.size), transcendentals=0),
        name="load_weights",
    )(*in_hbm(enc, dec))


def fetches(dec_hbm, reach, held, sems):
    return [
        pltpu.make_async_copy(
            dec_hbm.at[0, reach, :, pl.ds(step * CHUNK, CHUNK)], held.at[:, pl.ds(step * CHUNK, CHUNK)], sems.at[step]
        )
        for step in range(held.shape[1] // CHUNK)
    ]


def decode(codes, dec_ref, near_ref, far_ref, copies=None):
    half, width = near_ref.shape
    for step in range(width // CHUNK):
        if copies is not None:
            copies[step].wait()
        columns = pl.ds(step * CHUNK, CHUNK)
        part = jnp.dot(codes, dec_ref[:, columns], preferred_element_type=jnp.float32)
        near_ref[:, columns] = part[:half]
        far_ref[:, columns] = part[half:].astype(jnp.bfloat16)


def encode_kernel(tokens, place_ref, active_ref, x_ref, enc_ref, bias_ref, dec_ref, codes_ref, near_ref, far_ref, held):
    rows, depth = x_ref.shape
    group = rows // tokens
    half = depth // 2
    pre = bias_ref[...].astype(jnp.float32) + sum(
        jnp.dot(x_ref[:, part], enc_ref[0, part, :], preferred_element_type=jnp.float32)
        for part in (pl.ds(0, half), pl.ds(half, half))
    )
    held[...] = jnp.maximum(pre, 0.0)
    for block in range(group):
        tile = (slab_of(place_ref[0], block, group // CORES) * tokens) // TILE
        for part in range(active_ref.shape[1]):
            where = (pl.ds(block * tokens, tokens), pl.ds(part * BLOCK, BLOCK))
            held[where] = held[where] * active_ref[tile, part].astype(jnp.float32)
    codes_ref[...] = held[...].astype(jnp.bfloat16)
    decode(codes_ref[...], dec_ref, near_ref, far_ref)


def decode_kernel(codes_ref, dec_hbm, near_ref, far_ref, held, sems):
    copies = fetches(dec_hbm, 0, held, sems)
    for copy in copies:
        copy.start()
    decode(codes_ref[...], held, near_ref, far_ref, copies)


def halves_of(rows, width):
    return [pltpu.VMEM((rows // CORES, width), jnp.float32), pltpu.VMEM((rows // CORES, width), jnp.bfloat16)]


def encoded(place, active, x, enc, bias, dec, tokens):
    rows, depth = x.shape
    features = enc.shape[2]
    return pl.pallas_call(
        functools.partial(encode_kernel, tokens),
        out_shape=[pltpu.VMEM((rows, features), jnp.bfloat16)] + halves_of(rows, depth),
        in_specs=[SMEM_SPEC, SMEM_SPEC] + [VMEM_SPEC] * 4,
        out_specs=[VMEM_SPEC] * 3,
        scratch_shapes=[pltpu.VMEM((rows, features), jnp.float32)],
        compiler_params=kernel_params(),
        cost_estimate=pl.CostEstimate(flops=4 * rows * depth * features, bytes_accessed=4 * depth * features, transcendentals=0),
        name="encode",
    )(place, active, *in_vmem(x, enc, bias, dec))


def decoded(codes, dec):
    rows, features = codes.shape
    width = dec.shape[3]
    return pl.pallas_call(
        decode_kernel,
        out_shape=halves_of(rows, width),
        in_specs=[VMEM_SPEC, ANY_SPEC],
        out_specs=[VMEM_SPEC] * 2,
        scratch_shapes=[pltpu.VMEM((features, width), dec.dtype), pltpu.SemaphoreType.DMA((width // CHUNK,))],
        compiler_params=kernel_params(2 * LIMIT),
        cost_estimate=pl.CostEstimate(flops=2 * rows * width * features, bytes_accessed=2 * width * features, transcendentals=0),
        name="decode_own",
    )(*in_vmem(codes), *in_hbm(dec))


def back(rows_ref, dec_ref, copies=None):
    sums = [None, None]
    steps = rows_ref.shape[1] // CHUNK
    for step in range(steps):
        if copies is not None:
            copies[step].wait()
        columns = pl.ds(step * CHUNK, CHUNK)
        part = lax.dot_general(
            rows_ref[:, columns], dec_ref[:, columns], (((1,), (1,)), ((), ())), preferred_element_type=jnp.float32
        )
        which = step * len(sums) // steps
        sums[which] = part if sums[which] is None else sums[which] + part
    return sums[0] + sums[1]


def grad_own_kernel(rows_ref, dec_hbm, out_ref, next_ref, held, sems, next_sem):
    copies = fetches(dec_hbm, 0, held, sems)
    load_next = pltpu.make_async_copy(dec_hbm.at[0, 1], next_ref, next_sem)
    for copy in copies:
        copy.start()
    load_next.start()
    out_ref[...] = back(rows_ref, held, copies)
    load_next.wait()


def grad_all_kernel(tokens, place_ref, rows_ref, dec_ref, own_ref, out_ref):
    total = own_ref[...] + back(rows_ref, dec_ref)
    group = total.shape[0] // tokens
    for block in range(group):
        slab = slab_of(place_ref[0], block, group // CORES)
        where = pl.ds(pl.multiple_of(slab * tokens, tokens), tokens)
        out_ref[0, where, :] = total[block * tokens : (block + 1) * tokens]


def grad_own(rows, dec):
    _, _, features, width = dec.shape
    return pl.pallas_call(
        grad_own_kernel,
        out_shape=[pltpu.VMEM((rows.shape[0], features), jnp.float32), pltpu.VMEM((features, width), dec.dtype)],
        in_specs=[VMEM_SPEC, ANY_SPEC],
        out_specs=[VMEM_SPEC] * 2,
        scratch_shapes=[
            pltpu.VMEM((features, width), dec.dtype),
            pltpu.SemaphoreType.DMA((width // CHUNK,)),
            pltpu.SemaphoreType.DMA(()),
        ],
        compiler_params=kernel_params(2 * LIMIT),
        cost_estimate=pl.CostEstimate(flops=2 * rows.size * features, bytes_accessed=2 * dec.size, transcendentals=0),
        name="grad_own",
    )(*in_vmem(rows), *in_hbm(dec))


def grad_all(place, rows, dec, own, tokens):
    return pl.pallas_call(
        functools.partial(grad_all_kernel, tokens),
        out_shape=jax.ShapeDtypeStruct((1,) + own.shape, jnp.float32),
        in_specs=[SMEM_SPEC] + [VMEM_SPEC] * 3,
        out_specs=VMEM_SPEC,
        compiler_params=kernel_params(),
        cost_estimate=pl.CostEstimate(flops=2 * rows.size * own.shape[1], bytes_accessed=2 * dec.size, transcendentals=0),
        name="grad_all",
    )(place, *in_vmem(rows, dec, own))


def blocks_of(near, far, chips):
    rows = near.shape[0] // chips
    total = near + other_core(far).astype(jnp.float32)
    return [total[chip * rows : (chip + 1) * rows] for chip in range(chips)]


def summed(blocks, sent):
    total = blocks[0]
    for came in [across(blocks[chip].astype(jnp.bfloat16), chip, len(blocks)) for chip in sent]:
        total = total + came.astype(jnp.float32)
    return total


def on_device(resid, enc_weight, enc_bias, active, dec_weight, target):
    group = lax.axis_size(AXIS) // LAYERS
    chips = group // CORES
    index = lax.axis_index(AXIS)
    layer = index // group
    place = (index % group).astype(jnp.int32).reshape(1)
    tokens = resid.shape[1]
    enc, next_dec = loaded(enc_weight, dec_weight)
    near = [resid[0]] + [across(resid[0], chip, chips) for chip in range(1, chips)]
    x = jnp.concatenate(near + [other_core(piece) for piece in near], axis=0)
    codes, next_near, next_far = encoded(place, active[0], x, enc, enc_bias, next_dec, tokens)
    own_near, own_far = decoded(codes, dec_weight)

    nexts = blocks_of(next_near, next_far, chips)
    owns = blocks_of(own_near, own_far, chips)
    risen = raised(nexts[-1].astype(jnp.bfloat16), layer, group)
    next_sum = summed(nexts, range(1, chips - 1)).astype(jnp.bfloat16)
    owns[-1] = owns[-1] + risen.astype(jnp.float32)
    from_before = raised(next_sum, layer, group).astype(jnp.float32)
    own_sum = summed(owns, range(1, chips))
    error = (own_sum + from_before - target[0].astype(jnp.float32)).astype(jnp.bfloat16)

    later = lowered(error, layer, group)
    heres = [error] + [across(error, chip, chips) for chip in range(1, chips)]
    afters = [later] + [across(later, chip, chips) for chip in range(1, chips - 1)]
    last = lowered(after(heres[-1], later), layer, group)
    here_near = jnp.concatenate(heres, axis=0)
    here_far = other_core(here_near)
    here_rows = jnp.concatenate([here_near, here_far], axis=0)
    most = after(jnp.concatenate(afters, axis=0), here_far)
    after_rows = jnp.concatenate([most, last, other_core(most), other_core(last)], axis=0)
    own_grad, next_dec = grad_own(here_rows, dec_weight)
    grad = grad_all(place, after_rows, next_dec, own_grad, tokens)
    return (error[None], grad)


def solution(mesh):
    return jax.shard_map(
        on_device,
        mesh=mesh,
        in_specs=(
            P("layer", "groups", None),
            P("layer", None, None),
            P("layer", None),
            P("layer", "groups", None),
            P("layer", None, None, None),
            P("layer", "groups", None),
        ),
        out_specs=(P("layer", "groups", None), P("layer", "groups", None)),
        check_vma=False,
    )
```

time: 64.1 us -> 58.7 us (0.916)
  local copies, waits for them, and re-layouts: 11.3 us -> 1.16 us
  waiting for transfers between devices: 12.8 us -> 16.4 us
  Pallas kernels: 12.1 us -> 15.3 us
  starting transfers between devices: 26 us -> 24.1 us
    unnamed x26 -> x18, local copies, waits for them, and re-layouts: 11.2 us -> 1.07 us
    ppermute x22, waiting for transfers between devices: 6.84 us -> 9.22 us  [the longest x13 8.14 us: across(): return lax.ppermute(value, AXIS, pairs)]
    pallas_call x1, Pallas kernels: 0.84 us -> 2.8 us  [decoded(): pl.pallas_call(decode_kernel, out_shape=halves_of(rows, width), in_specs=...]
    ppermute x2, starting transfers between devices: 5.19 us -> 3.73 us  [lowered(): lax.ppermute(value, AXIS, [((i + group) % size, i) for i in range(size)])]
    pallas_call x3, Pallas kernels: 8.11 us -> 9.38 us  [the longest x1 3.85 us: grad_own(): pl.pallas_call(grad_own_kernel, out_shape=[pltpu.VMEM((rows.shape[0], fea...]
    ppermute x2, waiting for transfers between devices: 2.33 us -> 3.34 us  [lowered(): lax.ppermute(value, AXIS, [((i + group) % size, i) for i in range(size)])]
  transfers between devices with their start and end apart: 26 -> 26, of which waited for: 9 -> 9; matrix products, arithmetic and copies ran while one was open for 2% -> 3% of each run, Pallas kernels for 11% -> 17%
where the time goes in v9:
time: 58.7 us; the launch traced here: 58.6 us
  starting transfers between devices  24.1 us (41%)
  waiting for transfers between devices  16.4 us (28%)
  Pallas kernels  15.3 us (26%)
  local copies, waits for them, and re-layouts  1.16 us (2%)
  between operations  0.98 us (2%)
    ppermute x13, starting transfers between devices, across(): return lax.ppermute(value, AXIS, pairs)  14.9 us
    ppermute x13, waiting for transfers between devices, across(): return lax.ppermute(value, AXIS, pairs)  8.14 us
    pallas_call x1, Pallas kernels, grad_own(): pl.pallas_call(grad_own_kernel, out_shape=[pltpu.VMEM((rows.shape[0], fea...  3.85 us
    ppermute x2, waiting for transfers between devices, raised(): lax.ppermute(value, AXIS, [(i, (i + group) % size) for i in range(size)])  3.84 us
    ppermute x2, starting transfers between devices, lowered(): lax.ppermute(value, AXIS, [((i + group) % size, i) for i in range(size)])  3.73 us
    pallas_call x1, Pallas kernels, loaded(): pl.pallas_call(load_kernel, out_shape=[pltpu.VMEM(enc.shape, enc.dtype),...  3.49 us
    ppermute x2, starting transfers between devices, raised(): lax.ppermute(value, AXIS, [(i, (i + group) % size) for i in range(size)])  3.34 us
    ppermute x2, waiting for transfers between devices, lowered(): lax.ppermute(value, AXIS, [((i + group) % size, i) for i in range(size)])  3.34 us
  transfers between devices with their start and end apart: 26, of which 9 were waited for; matrix products, arithmetic and copies ran while one was open for 3% of the time, Pallas kernels for 17%

profile of v9, /device:TPU:0, one launch (start us, length us, event | category | flops | bytes accessed | tf_op | source)
XLA Modules:
  0.0 58.6 jit_solution(1409086801796303112)
XLA Ops:
  0.6 0.5 collective-permute-start.3
  1.1 3.5 %collective-permute-start.2 = (bf16[8,8192]{1,0:T(8,128)(2,1)}, bf16[8,8192]{1,0:T(8,128)(2,1)S(1)}, u32[]{:S(2)}, u32[]{:S(2)}) collective-permute-start(bf16[8,8192]{1,0:T(8,128)(2,1)} %bitcast.12), channel_id=1, source_target_pairs={{0,6},{1,7},{2,4},{3,5},{4,2},{5,3},{6,0},{7,1},{8,14},{9,15},{10,... | collective-permute-start | bytes 393224 | tf_op jit(solution)/shard_map/ppermute | solution.py:31
  4.7 0.5 collective-permute-start.1
  5.2 0.1 collective-permute-start
  5.3 0.9 %constant_dynamic-update-slice_fusion.7 = bf16[64,8192]{1,0:T(8,128)(2,1)S(1)} fusion(bf16[1,8,8192]{2,1,0:T(8,128)(2,1)} %param.6), kind=kLoop, calls=%fused_computation.25 | loop fusion | bytes 262144
  6.3 0.0 copy-start
  6.3 0.0 copy-start.1
  6.3 3.5 %load_weights.1 = (bf16[1,8192,256]{2,1,0:T(8,128)(2,1)S(1)}, bf16[256,8192]{1,0:T(8,128)(2,1)S(1)}) custom-call(bf16[1,8192,256]{2,1,0:T(8,128)(2,1)} %enc_hbm.1, bf16[1,2,256,8192]{3,2,1,0:T(8,128)(2,1)} %dec_hbm.5), custom_call_target="tpu_custom_call" | custom-call | bytes 25165824 | tf_op jit(solution)/shard_map/load_weights/pallas_call | solution.py:84
  9.8 0.0 collective-permute-done.2
  9.8 0.1 collective-permute-start.6
  9.9 1.9 %collective-permute-done.1 = bf16[8,8192]{1,0:T(8,128)(2,1)S(1)} collective-permute-done((bf16[8,8192]{1,0:T(8,128)(2,1)}, bf16[8,8192]{1,0:T(8,128)(2,1)S(1)}, u32[]{:S(2)}, u32[]{:S(2)}) %collective-permute-start.1) | collective-permute-done | bytes 131104 | tf_op jit(solution)/shard_map/ppermute | solution.py:31
  11.8 0.0 collective-permute-start.5
  11.8 0.3 collective-permute-done
  12.1 0.2 collective-permute-start.4
  12.3 0.0 collective-permute-done.3
  12.4 1.1 %collective-permute-done.4 = bf16[8,8192]{1,0:T(8,128)(2,1)S(1)} collective-permute-done((bf16[8,8192]{1,0:T(8,128)(2,1)S(1)}, bf16[8,8192]{1,0:T(8,128)(2,1)S(1)}, u32[]{:S(2)}, u32[]{:S(2)}) %collective-permute-start.4) | collective-permute-done | bytes 131104 | tf_op jit(solution)/shard_map/ppermute | solution.py:35
  13.4 0.0 collective-permute-done.5
  13.5 0.0 collective-permute-done.6
  13.5 3.1 %encode.1 = (bf16[64,256]{1,0:T(8,128)(2,1)S(1)}, f32[32,8192]{1,0:T(8,128)S(1)}, bf16[32,8192]{1,0:T(8,128)(2,1)S(1)}) custom-call(s32[1]{0:T(128)} %bitcast.place_ref, s32[2,2]{1,0:T(2,128)S(1)} %bitcast.9, bf16[64,8192]{1,0:T(8,128)(2,1)S(1)} %constant_dynamic-update-slice_fusion.x_ref, bf16[1,8192,256]{2,1,0:T(8,128)(2,1)S(1)} %get-tuple-element.13.enc_ref, ...), custom_call_target="tpu_custom_call" | custom-call | flops 536870912 | bytes 8388608 | tf_op jit(solution)/shard_map/encode/pallas_call | solution.py:148
  16.7 0.3 collective-permute-start.10
  16.9 2.8 %decode_own.1 = (f32[32,8192]{1,0:T(8,128)S(1)}, bf16[32,8192]{1,0:T(8,128)(2,1)S(1)}) custom-call(bf16[64,256]{1,0:T(8,128)(2,1)S(1)} %get-tuple-element.15.codes_ref, bf16[1,2,256,8192]{3,2,1,0:T(8,128)(2,1)} %dec_hbm.5), custom_call_target="tpu_custom_call" | custom-call | flops 268435456 | bytes 4194304 | tf_op jit(solution)/shard_map/decode_own/pallas_call | solution.py:163
  19.8 0.4 collective-permute-start.7
  20.1 0.0 collective-permute-done.10
  20.1 0.1 fusion.10
  20.3 1.7 %collective-permute-start.11 = (bf16[8,8192]{1,0:T(8,128)(2,1)S(1)}, bf16[8,8192]{1,0:T(8,128)(2,1)S(1)}, u32[]{:S(2)}, u32[]{:S(2)}) collective-permute-start(bf16[8,8192]{1,0:T(8,128)(2,1)S(1)} %get-tuple-element.32), channel_id=1, source_target_pairs={{0,8},{1,9},{2,10},{3,11},{4,12},{5,13},{6,14},{7,15},{8,16},{9,17... | collective-permute-start | bytes 393224 | tf_op jit(solution)/shard_map/ppermute | solution.py:40
  22.0 1.5 %collective-permute-start.14 = (bf16[8,8192]{1,0:T(8,128)(2,1)S(1)}, bf16[8,8192]{1,0:T(8,128)(2,1)S(1)}, u32[]{:S(2)}, u32[]{:S(2)}) collective-permute-start(bf16[8,8192]{1,0:T(8,128)(2,1)S(1)} %get-tuple-element.33), channel_id=1, source_target_pairs={{0,4},{1,3},{2,6},{3,1},{4,0},{5,7},{6,2},{7,5},{8,12},{9,11},{10,... | collective-permute-start | bytes 393224 | tf_op jit(solution)/shard_map/ppermute | solution.py:31
  23.5 1.5 %collective-permute-start.13 = (bf16[8,8192]{1,0:T(8,128)(2,1)S(1)}, bf16[8,8192]{1,0:T(8,128)(2,1)S(1)}, u32[]{:S(2)}, u32[]{:S(2)}) collective-permute-start(bf16[8,8192]{1,0:T(8,128)(2,1)S(1)} %get-tuple-element.34), channel_id=1, source_target_pairs={{0,2},{1,5},{2,0},{3,7},{4,6},{5,1},{6,4},{7,3},{8,10},{9,13},{10,... | collective-permute-start | bytes 393224 | tf_op jit(solution)/shard_map/ppermute | solution.py:31
  25.0 0.0 collective-permute-done.7
  25.0 0.1 fusion.9
  25.1 0.6 %collective-permute-start.8 = (bf16[8,8192]{1,0:T(8,128)(2,1)S(1)}, bf16[8,8192]{1,0:T(8,128)(2,1)S(1)}, u32[]{:S(2)}, u32[]{:S(2)}) collective-permute-start(bf16[8,8192]{1,0:T(8,128)(2,1)S(1)} %get-tuple-element.30), channel_id=1, source_target_pairs={{0,2},{1,5},{2,0},{3,7},{4,6},{5,1},{6,4},{7,3},{8,10},{9,13},{10,... | collective-permute-start | bytes 393224 | tf_op jit(solution)/shard_map/ppermute | solution.py:31
  25.8 0.5 collective-permute-start.9
  26.3 1.9 %collective-permute-done.14 = bf16[8,8192]{1,0:T(8,128)(2,1)S(1)} collective-permute-done((bf16[8,8192]{1,0:T(8,128)(2,1)S(1)}, bf16[8,8192]{1,0:T(8,128)(2,1)S(1)}, u32[]{:S(2)}, u32[]{:S(2)}) %collective-permute-start.14) | collective-permute-done | bytes 131104 | tf_op jit(solution)/shard_map/ppermute | solution.py:31
  28.1 1.4 %collective-permute-done.13 = bf16[8,8192]{1,0:T(8,128)(2,1)S(1)} collective-permute-done((bf16[8,8192]{1,0:T(8,128)(2,1)S(1)}, bf16[8,8192]{1,0:T(8,128)(2,1)S(1)}, u32[]{:S(2)}, u32[]{:S(2)}) %collective-permute-start.13) | collective-permute-done | bytes 131104 | tf_op jit(solution)/shard_map/ppermute | solution.py:31
  29.6 1.6 %collective-permute-start.15 = (bf16[8,8192]{1,0:T(8,128)(2,1)S(1)}, bf16[8,8192]{1,0:T(8,128)(2,1)S(1)}, u32[]{:S(2)}, u32[]{:S(2)}) collective-permute-start(bf16[8,8192]{1,0:T(8,128)(2,1)S(1)} %fusion.1), channel_id=1, source_target_pairs={{0,8},{1,9},{2,10},{3,11},{4,12},{5,13},{6,14},{7,15},{8,16},{9,17... | collective-permute-start | bytes 393224 | tf_op jit(solution)/shard_map/ppermute | solution.py:40
  31.2 0.0 collective-permute-done.11
  31.3 1.3 %collective-permute-start.12 = (bf16[8,8192]{1,0:T(8,128)(2,1)S(1)}, bf16[8,8192]{1,0:T(8,128)(2,1)S(1)}, u32[]{:S(2)}, u32[]{:S(2)}) collective-permute-start(bf16[8,8192]{1,0:T(8,128)(2,1)S(1)} %fusion.2), channel_id=1, source_target_pairs={{0,6},{1,7},{2,4},{3,5},{4,2},{5,3},{6,0},{7,1},{8,14},{9,15},{10,... | collective-permute-start | bytes 393224 | tf_op jit(solution)/shard_map/ppermute | solution.py:31
  32.6 0.0 collective-permute-done.8
  32.6 0.0 collective-permute-done.9
  32.6 3.8 %collective-permute-done.15 = bf16[8,8192]{1,0:T(8,128)(2,1)S(1)} collective-permute-done((bf16[8,8192]{1,0:T(8,128)(2,1)S(1)}, bf16[8,8192]{1,0:T(8,128)(2,1)S(1)}, u32[]{:S(2)}, u32[]{:S(2)}) %collective-permute-start.15) | collective-permute-done | bytes 131104 | tf_op jit(solution)/shard_map/ppermute | solution.py:40
  36.4 0.8 %collective-permute-done.12 = bf16[8,8192]{1,0:T(8,128)(2,1)S(1)} collective-permute-done((bf16[8,8192]{1,0:T(8,128)(2,1)S(1)}, bf16[8,8192]{1,0:T(8,128)(2,1)S(1)}, u32[]{:S(2)}, u32[]{:S(2)}) %collective-permute-start.12) | collective-permute-done | bytes 131104 | tf_op jit(solution)/shard_map/ppermute | solution.py:31
  37.2 0.1 constant_dynamic-update-slice_fusion.12
  37.3 0.0 copy-start.2
  37.3 2.3 %collective-permute-start.16 = (bf16[8,8192]{1,0:T(8,128)(2,1)S(1)}, bf16[8,8192]{1,0:T(8,128)(2,1)S(1)}, u32[]{:S(2)}, u32[]{:S(2)}) collective-permute-start(bf16[8,8192]{1,0:T(8,128)(2,1)S(1)} %get-tuple-element.25), channel_id=1, source_target_pairs={{8,0},{9,1},{10,2},{11,3},{12,4},{13,5},{14,6},{15,7},{16,8},{17,9... | collective-permute-start | bytes 393224 | tf_op jit(solution)/shard_map/ppermute | solution.py:46
  39.6 1.2 %collective-permute-start.21 = (bf16[8,8192]{1,0:T(8,128)(2,1)S(1)}, bf16[8,8192]{1,0:T(8,128)(2,1)S(1)}, u32[]{:S(2)}, u32[]{:S(2)}) collective-permute-start(bf16[8,8192]{1,0:T(8,128)(2,1)S(1)} %get-tuple-element.25), channel_id=1, source_target_pairs={{0,6},{1,7},{2,4},{3,5},{4,2},{5,3},{6,0},{7,1},{8,14},{9,15},{10,... | collective-permute-start | bytes 393224 | tf_op jit(solution)/shard_map/ppermute | solution.py:31
  40.9 1.5 %collective-permute-start.20 = (bf16[8,8192]{1,0:T(8,128)(2,1)S(1)}, bf16[8,8192]{1,0:T(8,128)(2,1)S(1)}, u32[]{:S(2)}, u32[]{:S(2)}) collective-permute-start(bf16[8,8192]{1,0:T(8,128)(2,1)S(1)} %get-tuple-element.25), channel_id=1, source_target_pairs={{0,4},{1,3},{2,6},{3,1},{4,0},{5,7},{6,2},{7,5},{8,12},{9,11},{10,... | collective-permute-start | bytes 393224 | tf_op jit(solution)/shard_map/ppermute | solution.py:31
  42.4 0.7 %collective-permute-start.19 = (bf16[8,8192]{1,0:T(8,128)(2,1)S(1)}, bf16[8,8192]{1,0:T(8,128)(2,1)S(1)}, u32[]{:S(2)}, u32[]{:S(2)}) collective-permute-start(bf16[8,8192]{1,0:T(8,128)(2,1)S(1)} %get-tuple-element.25), channel_id=1, source_target_pairs={{0,2},{1,5},{2,0},{3,7},{4,6},{5,1},{6,4},{7,3},{8,10},{9,13},{10,... | collective-permute-start | bytes 393224 | tf_op jit(solution)/shard_map/ppermute | solution.py:31
  43.1 0.0 collective-permute-done.16
  43.1 0.7 %collective-permute-start.18 = (bf16[8,8192]{1,0:T(8,128)(2,1)S(1)}, bf16[8,8192]{1,0:T(8,128)(2,1)S(1)}, u32[]{:S(2)}, u32[]{:S(2)}) collective-permute-start(bf16[8,8192]{1,0:T(8,128)(2,1)S(1)} %broadcast_select_fusion.1), channel_id=1, source_target_pairs={{0,4},{1,3},{2,6},{3,1},{4,0},{5,7},{6,2},{7,5},{8,12},{9,11},{10,... | collective-permute-start | bytes 393224 | tf_op jit(solution)/shard_map/ppermute | solution.py:31
  43.8 1.2 %collective-permute-start.17 = (bf16[8,8192]{1,0:T(8,128)(2,1)S(1)}, bf16[8,8192]{1,0:T(8,128)(2,1)S(1)}, u32[]{:S(2)}, u32[]{:S(2)}) collective-permute-start(bf16[8,8192]{1,0:T(8,128)(2,1)S(1)} %broadcast_select_fusion.1), channel_id=1, source_target_pairs={{0,2},{1,5},{2,0},{3,7},{4,6},{5,1},{6,4},{7,3},{8,10},{9,13},{10,... | collective-permute-start | bytes 393224 | tf_op jit(solution)/shard_map/ppermute | solution.py:31
  45.0 1.8 %collective-permute-done.21 = bf16[8,8192]{1,0:T(8,128)(2,1)S(1)} collective-permute-done((bf16[8,8192]{1,0:T(8,128)(2,1)S(1)}, bf16[8,8192]{1,0:T(8,128)(2,1)S(1)}, u32[]{:S(2)}, u32[]{:S(2)}) %collective-permute-start.21) | collective-permute-done | bytes 131104 | tf_op jit(solution)/shard_map/ppermute | solution.py:31
  46.9 1.4 %collective-permute-start.23 = (bf16[8,8192]{1,0:T(8,128)(2,1)S(1)}, bf16[8,8192]{1,0:T(8,128)(2,1)S(1)}, u32[]{:S(2)}, u32[]{:S(2)}) collective-permute-start(bf16[8,8192]{1,0:T(8,128)(2,1)S(1)} %collective-permute-done.21), channel_id=1, source_target_pairs={{8,0},{9,1},{10,2},{11,3},{12,4},{13,5},{14,6},{15,7},{16,8},{17,9... | collective-permute-start | bytes 393224 | tf_op jit(solution)/shard_map/ppermute | solution.py:46
  48.3 0.0 collective-permute-done.20
  48.3 0.0 collective-permute-done.19
  48.3 0.1 pad_maximum_fusion.1
  48.3 0.1 collective-permute-start.22
  48.5 3.3 %collective-permute-done.23 = bf16[8,8192]{1,0:T(8,128)(2,1)S(1)} collective-permute-done((bf16[8,8192]{1,0:T(8,128)(2,1)S(1)}, bf16[8,8192]{1,0:T(8,128)(2,1)S(1)}, u32[]{:S(2)}, u32[]{:S(2)}) %collective-permute-start.23) | collective-permute-done | bytes 131104 | tf_op jit(solution)/shard_map/ppermute | solution.py:46
  51.8 0.1 collective-permute-start.25
  51.9 0.0 collective-permute-done.18
  52.0 0.0 collective-permute-done.22
  52.0 0.5 collective-permute-start.24
  52.6 3.9 %grad_own.1 = (f32[64,256]{1,0:T(8,128)S(1)}, bf16[256,8192]{1,0:T(8,128)(2,1)S(1)}) custom-call(bf16[64,8192]{1,0:T(8,128)(2,1)S(1)} %constant_dynamic-update-slice_fusion.8.rows_ref, bf16[1,2,256,8192]{3,2,1,0:T(8,128)(2,1)} %dec_hbm.5), custom_call_target="tpu_custom_call" | custom-call | flops 268435456 | bytes 8388608 | tf_op jit(solution)/shard_map/grad_own/pallas_call | solution.py:211
  56.5 0.0 collective-permute-done.24
  56.5 0.1 pad_maximum_fusion.rows_ref
  56.5 2.0 %grad_all.1 = f32[1,64,256]{2,1,0:T(8,128)} custom-call(s32[1]{0:T(128)} %bitcast.place_ref, bf16[64,8192]{1,0:T(8,128)(2,1)S(1)} %pad_maximum_fusion.rows_ref, bf16[256,8192]{1,0:T(8,128)(2,1)S(1)} %get-tuple-element.22.dec_ref, f32[64,256]{1,0:T(8,128)S(1)} %get-tuple-element.23.own_ref), custom_call_target="tpu_custom_call" | custom-call | flops 268435456 | bytes 4194304 | tf_op jit(solution)/shard_map/grad_all/pallas_call | solution.py:228
  (25 shorter events, 0.3 us)
Async XLA Ops:
  0.6 11.7 %collective-permute-start.3 = (bf16[8,8192]{1,0:T(8,128)(2,1)}, bf16[8,8192]{1,0:T(8,128)(2,1)S(1)}, u32[]{:S(2)}, u32[]{:S(2)}) collective-permute-start(bf16[8,8192]{1,0:T(8,128)(2,1)} %bitcast.11), channel_id=1, source_target_pairs={{0,1},{1,0},{2,3},{3,2},{4,5},{5,4},{6,7},{7,6},{8,9},{9,8},{10,11... | collective-permute-start | bytes 393224 | tf_op jit(solution)/shard_map/ppermute | solution.py:35
  1.1 8.7 %collective-permute-start.2 = (bf16[8,8192]{1,0:T(8,128)(2,1)}, bf16[8,8192]{1,0:T(8,128)(2,1)S(1)}, u32[]{:S(2)}, u32[]{:S(2)}) collective-permute-start(bf16[8,8192]{1,0:T(8,128)(2,1)} %bitcast.12), channel_id=1, source_target_pairs={{0,6},{1,7},{2,4},{3,5},{4,2},{5,3},{6,0},{7,1},{8,14},{9,15},{10,... | collective-permute-start | bytes 393224 | tf_op jit(solution)/shard_map/ppermute | solution.py:31
  4.7 7.1 %collective-permute-start.1 = (bf16[8,8192]{1,0:T(8,128)(2,1)}, bf16[8,8192]{1,0:T(8,128)(2,1)S(1)}, u32[]{:S(2)}, u32[]{:S(2)}) collective-permute-start(bf16[8,8192]{1,0:T(8,128)(2,1)} %bitcast.13), channel_id=1, source_target_pairs={{0,4},{1,3},{2,6},{3,1},{4,0},{5,7},{6,2},{7,5},{8,12},{9,11},{10,... | collective-permute-start | bytes 393224 | tf_op jit(solution)/shard_map/ppermute | solution.py:31
  5.2 6.9 %collective-permute-start = (bf16[8,8192]{1,0:T(8,128)(2,1)}, bf16[8,8192]{1,0:T(8,128)(2,1)S(1)}, u32[]{:S(2)}, u32[]{:S(2)}) collective-permute-start(bf16[8,8192]{1,0:T(8,128)(2,1)} %bitcast.14), channel_id=1, source_target_pairs={{0,2},{1,5},{2,0},{3,7},{4,6},{5,1},{6,4},{7,3},{8,10},{9,13},{10,... | collective-permute-start | bytes 393224 | tf_op jit(solution)/shard_map/ppermute | solution.py:31
  6.3 7.2 %copy-start = (s32[1,2,2]{2,1,0:T(2,128)S(1)}, s32[1,2,2]{2,1,0:T(2,128)}, u32[]{:S(2)}) copy-start(s32[1,2,2]{2,1,0:T(2,128)} %param.9) | copy-start | bytes 52
  6.3 7.2 %copy-start.1 = (bf16[1,256]{1,0:T(2,128)(2,1)S(1)}, bf16[1,256]{1,0:T(2,128)(2,1)}, u32[]{:S(2)}) copy-start(bf16[1,256]{1,0:T(2,128)(2,1)} %bias_ref.1) | copy-start | bytes 1540
  9.8 3.7 %collective-permute-start.6 = (bf16[8,8192]{1,0:T(8,128)(2,1)S(1)}, bf16[8,8192]{1,0:T(8,128)(2,1)S(1)}, u32[]{:S(2)}, u32[]{:S(2)}) collective-permute-start(bf16[8,8192]{1,0:T(8,128)(2,1)S(1)} %collective-permute-done.2), channel_id=1, source_target_pairs={{0,1},{1,0},{2,3},{3,2},{4,5},{5,4},{6,7},{7,6},{8,9},{9,8},{10,11... | collective-permute-start | bytes 393224 | tf_op jit(solution)/shard_map/ppermute | solution.py:35
  11.8 1.7 %collective-permute-start.5 = (bf16[8,8192]{1,0:T(8,128)(2,1)S(1)}, bf16[8,8192]{1,0:T(8,128)(2,1)S(1)}, u32[]{:S(2)}, u32[]{:S(2)}) collective-permute-start(bf16[8,8192]{1,0:T(8,128)(2,1)S(1)} %collective-permute-done.1), channel_id=1, source_target_pairs={{0,1},{1,0},{2,3},{3,2},{4,5},{5,4},{6,7},{7,6},{8,9},{9,8},{10,11... | collective-permute-start | bytes 393224 | tf_op jit(solution)/shard_map/ppermute | solution.py:35
  12.1 1.3 %collective-permute-start.4 = (bf16[8,8192]{1,0:T(8,128)(2,1)S(1)}, bf16[8,8192]{1,0:T(8,128)(2,1)S(1)}, u32[]{:S(2)}, u32[]{:S(2)}) collective-permute-start(bf16[8,8192]{1,0:T(8,128)(2,1)S(1)} %collective-permute-done), channel_id=1, source_target_pairs={{0,1},{1,0},{2,3},{3,2},{4,5},{5,4},{6,7},{7,6},{8,9},{9,8},{10,11... | collective-permute-start | bytes 393224 | tf_op jit(solution)/shard_map/ppermute | solution.py:35
  16.7 3.5 %collective-permute-start.10 = (bf16[32,8192]{1,0:T(8,128)(2,1)S(1)}, bf16[32,8192]{1,0:T(8,128)(2,1)S(1)}, u32[]{:S(2)}, u32[]{:S(2)}) collective-permute-start(bf16[32,8192]{1,0:T(8,128)(2,1)S(1)} %get-tuple-element.19), channel_id=1, source_target_pairs={{0,1},{1,0},{2,3},{3,2},{4,5},{5,4},{6,7},{7,6},{8,9},{9,8},{10,11... | collective-permute-start | bytes 1572872 | tf_op jit(solution)/shard_map/ppermute | solution.py:35
  19.8 5.2 %collective-permute-start.7 = (bf16[32,8192]{1,0:T(8,128)(2,1)S(1)}, bf16[32,8192]{1,0:T(8,128)(2,1)S(1)}, u32[]{:S(2)}, u32[]{:S(2)}) collective-permute-start(bf16[32,8192]{1,0:T(8,128)(2,1)S(1)} %get-tuple-element.17), channel_id=1, source_target_pairs={{0,1},{1,0},{2,3},{3,2},{4,5},{5,4},{6,7},{7,6},{8,9},{9,8},{10,11... | collective-permute-start | bytes 1572872 | tf_op jit(solution)/shard_map/ppermute | solution.py:35
  20.3 11.0 %collective-permute-start.11 = (bf16[8,8192]{1,0:T(8,128)(2,1)S(1)}, bf16[8,8192]{1,0:T(8,128)(2,1)S(1)}, u32[]{:S(2)}, u32[]{:S(2)}) collective-permute-start(bf16[8,8192]{1,0:T(8,128)(2,1)S(1)} %get-tuple-element.32), channel_id=1, source_target_pairs={{0,8},{1,9},{2,10},{3,11},{4,12},{5,13},{6,14},{7,15},{8,16},{9,17... | collective-permute-start | bytes 393224 | tf_op jit(solution)/shard_map/ppermute | solution.py:40
  22.0 6.1 %collective-permute-start.14 = (bf16[8,8192]{1,0:T(8,128)(2,1)S(1)}, bf16[8,8192]{1,0:T(8,128)(2,1)S(1)}, u32[]{:S(2)}, u32[]{:S(2)}) collective-permute-start(bf16[8,8192]{1,0:T(8,128)(2,1)S(1)} %get-tuple-element.33), channel_id=1, source_target_pairs={{0,4},{1,3},{2,6},{3,1},{4,0},{5,7},{6,2},{7,5},{8,12},{9,11},{10,... | collective-permute-start | bytes 393224 | tf_op jit(solution)/shard_map/ppermute | solution.py:31
  23.5 6.0 %collective-permute-start.13 = (bf16[8,8192]{1,0:T(8,128)(2,1)S(1)}, bf16[8,8192]{1,0:T(8,128)(2,1)S(1)}, u32[]{:S(2)}, u32[]{:S(2)}) collective-permute-start(bf16[8,8192]{1,0:T(8,128)(2,1)S(1)} %get-tuple-element.34), channel_id=1, source_target_pairs={{0,2},{1,5},{2,0},{3,7},{4,6},{5,1},{6,4},{7,3},{8,10},{9,13},{10,... | collective-permute-start | bytes 393224 | tf_op jit(solution)/shard_map/ppermute | solution.py:31
  25.0 12.2 %copy-start.3 = (bf16[1,8,8192]{2,1,0:T(8,128)(2,1)S(1)}, bf16[1,8,8192]{2,1,0:T(8,128)(2,1)}, u32[]{:S(2)}) copy-start(bf16[1,8,8192]{2,1,0:T(8,128)(2,1)} %param.11) | copy-start | bytes 393220
  25.1 7.5 %collective-permute-start.8 = (bf16[8,8192]{1,0:T(8,128)(2,1)S(1)}, bf16[8,8192]{1,0:T(8,128)(2,1)S(1)}, u32[]{:S(2)}, u32[]{:S(2)}) collective-permute-start(bf16[8,8192]{1,0:T(8,128)(2,1)S(1)} %get-tuple-element.30), channel_id=1, source_target_pairs={{0,2},{1,5},{2,0},{3,7},{4,6},{5,1},{6,4},{7,3},{8,10},{9,13},{10,... | collective-permute-start | bytes 393224 | tf_op jit(solution)/shard_map/ppermute | solution.py:31
  25.8 6.8 %collective-permute-start.9 = (bf16[8,8192]{1,0:T(8,128)(2,1)S(1)}, bf16[8,8192]{1,0:T(8,128)(2,1)S(1)}, u32[]{:S(2)}, u32[]{:S(2)}) collective-permute-start(bf16[8,8192]{1,0:T(8,128)(2,1)S(1)} %get-tuple-element.31), channel_id=1, source_target_pairs={{0,4},{1,3},{2,6},{3,1},{4,0},{5,7},{6,2},{7,5},{8,12},{9,11},{10,... | collective-permute-start | bytes 393224 | tf_op jit(solution)/shard_map/ppermute | solution.py:31
  29.6 6.8 %collective-permute-start.15 = (bf16[8,8192]{1,0:T(8,128)(2,1)S(1)}, bf16[8,8192]{1,0:T(8,128)(2,1)S(1)}, u32[]{:S(2)}, u32[]{:S(2)}) collective-permute-start(bf16[8,8192]{1,0:T(8,128)(2,1)S(1)} %fusion.1), channel_id=1, source_target_pairs={{0,8},{1,9},{2,10},{3,11},{4,12},{5,13},{6,14},{7,15},{8,16},{9,17... | collective-permute-start | bytes 393224 | tf_op jit(solution)/shard_map/ppermute | solution.py:40
  31.3 5.9 %collective-permute-start.12 = (bf16[8,8192]{1,0:T(8,128)(2,1)S(1)}, bf16[8,8192]{1,0:T(8,128)(2,1)S(1)}, u32[]{:S(2)}, u32[]{:S(2)}) collective-permute-start(bf16[8,8192]{1,0:T(8,128)(2,1)S(1)} %fusion.2), channel_id=1, source_target_pairs={{0,6},{1,7},{2,4},{3,5},{4,2},{5,3},{6,0},{7,1},{8,14},{9,15},{10,... | collective-permute-start | bytes 393224 | tf_op jit(solution)/shard_map/ppermute | solution.py:31
  37.3 15.3 %copy-start.2 = (bf16[8,8192]{1,0:T(8,128)(2,1)}, bf16[8,8192]{1,0:T(8,128)(2,1)S(1)}, u32[]{:S(2)}) copy-start(bf16[8,8192]{1,0:T(8,128)(2,1)S(1)} %get-tuple-element.25) | copy-start | bytes 393220
  37.3 5.8 %collective-permute-start.16 = (bf16[8,8192]{1,0:T(8,128)(2,1)S(1)}, bf16[8,8192]{1,0:T(8,128)(2,1)S(1)}, u32[]{:S(2)}, u32[]{:S(2)}) collective-permute-start(bf16[8,8192]{1,0:T(8,128)(2,1)S(1)} %get-tuple-element.25), channel_id=1, source_target_pairs={{8,0},{9,1},{10,2},{11,3},{12,4},{13,5},{14,6},{15,7},{16,8},{17,9... | collective-permute-start | bytes 393224 | tf_op jit(solution)/shard_map/ppermute | solution.py:46
  39.6 7.2 %collective-permute-start.21 = (bf16[8,8192]{1,0:T(8,128)(2,1)S(1)}, bf16[8,8192]{1,0:T(8,128)(2,1)S(1)}, u32[]{:S(2)}, u32[]{:S(2)}) collective-permute-start(bf16[8,8192]{1,0:T(8,128)(2,1)S(1)} %get-tuple-element.25), channel_id=1, source_target_pairs={{0,6},{1,7},{2,4},{3,5},{4,2},{5,3},{6,0},{7,1},{8,14},{9,15},{10,... | collective-permute-start | bytes 393224 | tf_op jit(solution)/shard_map/ppermute | solution.py:31
  40.9 7.4 %collective-permute-start.20 = (bf16[8,8192]{1,0:T(8,128)(2,1)S(1)}, bf16[8,8192]{1,0:T(8,128)(2,1)S(1)}, u32[]{:S(2)}, u32[]{:S(2)}) collective-permute-start(bf16[8,8192]{1,0:T(8,128)(2,1)S(1)} %get-tuple-element.25), channel_id=1, source_target_pairs={{0,4},{1,3},{2,6},{3,1},{4,0},{5,7},{6,2},{7,5},{8,12},{9,11},{10,... | collective-permute-start | bytes 393224 | tf_op jit(solution)/shard_map/ppermute | solution.py:31
  42.4 5.9 %collective-permute-start.19 = (bf16[8,8192]{1,0:T(8,128)(2,1)S(1)}, bf16[8,8192]{1,0:T(8,128)(2,1)S(1)}, u32[]{:S(2)}, u32[]{:S(2)}) collective-permute-start(bf16[8,8192]{1,0:T(8,128)(2,1)S(1)} %get-tuple-element.25), channel_id=1, source_target_pairs={{0,2},{1,5},{2,0},{3,7},{4,6},{5,1},{6,4},{7,3},{8,10},{9,13},{10,... | collective-permute-start | bytes 393224 | tf_op jit(solution)/shard_map/ppermute | solution.py:31
  43.1 8.8 %collective-permute-start.18 = (bf16[8,8192]{1,0:T(8,128)(2,1)S(1)}, bf16[8,8192]{1,0:T(8,128)(2,1)S(1)}, u32[]{:S(2)}, u32[]{:S(2)}) collective-permute-start(bf16[8,8192]{1,0:T(8,128)(2,1)S(1)} %broadcast_select_fusion.1), channel_id=1, source_target_pairs={{0,4},{1,3},{2,6},{3,1},{4,0},{5,7},{6,2},{7,5},{8,12},{9,11},{10,... | collective-permute-start | bytes 393224 | tf_op jit(solution)/shard_map/ppermute | solution.py:31
  43.8 8.1 %collective-permute-start.17 = (bf16[8,8192]{1,0:T(8,128)(2,1)S(1)}, bf16[8,8192]{1,0:T(8,128)(2,1)S(1)}, u32[]{:S(2)}, u32[]{:S(2)}) collective-permute-start(bf16[8,8192]{1,0:T(8,128)(2,1)S(1)} %broadcast_select_fusion.1), channel_id=1, source_target_pairs={{0,2},{1,5},{2,0},{3,7},{4,6},{5,1},{6,4},{7,3},{8,10},{9,13},{10,... | collective-permute-start | bytes 393224 | tf_op jit(solution)/shard_map/ppermute | solution.py:31
  46.9 5.0 %collective-permute-start.23 = (bf16[8,8192]{1,0:T(8,128)(2,1)S(1)}, bf16[8,8192]{1,0:T(8,128)(2,1)S(1)}, u32[]{:S(2)}, u32[]{:S(2)}) collective-permute-start(bf16[8,8192]{1,0:T(8,128)(2,1)S(1)} %collective-permute-done.21), channel_id=1, source_target_pairs={{8,0},{9,1},{10,2},{11,3},{12,4},{13,5},{14,6},{15,7},{16,8},{17,9... | collective-permute-start | bytes 393224 | tf_op jit(solution)/shard_map/ppermute | solution.py:46
  48.3 3.6 %collective-permute-start.22 = (bf16[32,8192]{1,0:T(8,128)(2,1)S(1)}, bf16[32,8192]{1,0:T(8,128)(2,1)S(1)}, u32[]{:S(2)}, u32[]{:S(2)}) collective-permute-start(bf16[32,8192]{1,0:T(8,128)(2,1)S(1)} %pad_maximum_fusion.1), channel_id=1, source_target_pairs={{0,1},{1,0},{2,3},{3,2},{4,5},{5,4},{6,7},{7,6},{8,9},{9,8},{10,11... | collective-permute-start | bytes 1572872 | tf_op jit(solution)/shard_map/ppermute | solution.py:35
  51.8 4.6 %collective-permute-start.25 = (bf16[8,8192]{1,0:T(8,128)(2,1)S(1)}, bf16[8,8192]{1,0:T(8,128)(2,1)S(1)}, u32[]{:S(2)}, u32[]{:S(2)}) collective-permute-start(bf16[8,8192]{1,0:T(8,128)(2,1)S(1)} %broadcast_select_fusion), channel_id=1, source_target_pairs={{0,1},{1,0},{2,3},{3,2},{4,5},{5,4},{6,7},{7,6},{8,9},{9,8},{10,11... | collective-permute-start | bytes 393224 | tf_op jit(solution)/shard_map/ppermute | solution.py:35
  52.0 4.5 %collective-permute-start.24 = (bf16[24,8192]{1,0:T(8,128)(2,1)S(1)}, bf16[24,8192]{1,0:T(8,128)(2,1)S(1)}, u32[]{:S(2)}, u32[]{:S(2)}) collective-permute-start(bf16[24,8192]{1,0:T(8,128)(2,1)S(1)} %pad_maximum_fusion.2), channel_id=1, source_target_pairs={{0,1},{1,0},{2,3},{3,2},{4,5},{5,4},{6,7},{7,6},{8,9},{9,8},{10,11... | collective-permute-start | bytes 1179656 | tf_op jit(solution)/shard_map/ppermute | solution.py:35

commit v10 on v9

v10 whole, which is shorter than its diff:
```python
import functools

import jax
import jax.numpy as jnp
from jax import lax
from jax.experimental import pallas as pl
from jax.experimental.pallas import tpu as pltpu
from jax.sharding import PartitionSpec as P

BLOCK = 128
LAYERS = 4
TILE = 32
CORES = 2
CHUNK = 1024
LIMIT = 4 << 20
AXIS = "layer"

ANY_SPEC = pl.BlockSpec(memory_space=pl.ANY)
VMEM_SPEC = pl.BlockSpec(memory_space=pltpu.VMEM)
SMEM_SPEC = pl.BlockSpec(memory_space=pltpu.SMEM)


def turned(chip, chips):
    bits = chips.bit_length() - 1
    return sum(((chip >> bit) & 1) << (bits - 1 - bit) for bit in range(bits))


def across(value, chip, chips):
    masks = (CORES * chip, CORES * turned(chip, chips))
    pairs = [(i, i ^ masks[i % CORES]) for i in range(lax.axis_size(AXIS))]
    return lax.ppermute(value, AXIS, pairs)


def other_core(value):
    return lax.ppermute(value, AXIS, [(i, i ^ 1) for i in range(lax.axis_size(AXIS))])


def raised(value, layer, group):
    size = lax.axis_size(AXIS)
    came = lax.ppermute(value, AXIS, [(i, (i + group) % size) for i in range(size)])
    return jnp.where(layer == 0, jnp.zeros_like(came), came)


def lowered(value, layer, group):
    size = lax.axis_size(AXIS)
    came = lax.ppermute(value, AXIS, [((i + group) % size, i) for i in range(size)])
    return jnp.where(layer == LAYERS - 1, jnp.zeros_like(came), came)


def after(values, done):
    return lax.optimization_barrier((values, done))[0]


def slab_of(place, block, chips):
    far, chip = block // chips, block % chips
    odd = (place & 1) ^ far
    return place ^ (far + CORES * (chip * (1 - odd) + turned(chip, chips) * odd))


def in_vmem(*arrays):
    return [pltpu.with_memory_space_constraint(a, pltpu.VMEM) for a in arrays]


def in_hbm(*arrays):
    return [pltpu.with_memory_space_constraint(a, pltpu.HBM) for a in arrays]


def kernel_params(limit=LIMIT):
    return pltpu.CompilerParams(vmem_limit_bytes=limit)


def load_kernel(tokens, place_ref, active_ref, enc_hbm, dec_hbm, gate_ref, enc_ref, next_ref, own_ref, sems):
    pieces = [(enc_hbm.at[0], enc_ref), (dec_hbm.at[0, 1], next_ref), (dec_hbm.at[0, 0], own_ref)]
    copies = [pltpu.make_async_copy(source, target, sems.at[i]) for i, (source, target) in enumerate(pieces)]
    for copy in copies:
        copy.start()
    group = gate_ref.shape[0] // tokens
    for block in range(group):
        tile = (slab_of(place_ref[0], block, group // CORES) * tokens) // TILE
        for part in range(active_ref.shape[1]):
            live = active_ref[tile, part].astype(jnp.float32)
            gate_ref[pl.ds(block * tokens, tokens), pl.ds(part * BLOCK, BLOCK)] = jnp.full((tokens, BLOCK), live)
    for copy in copies:
        copy.wait()


def loaded(place, active, enc, dec, rows, tokens):
    _, depth, features = enc.shape
    block = pltpu.VMEM(dec.shape[2:], dec.dtype)
    return pl.pallas_call(
        functools.partial(load_kernel, tokens),
        out_shape=[pltpu.VMEM((rows, features), jnp.float32), pltpu.VMEM((depth, features), enc.dtype), block, block],
        in_specs=[SMEM_SPEC] * 2 + [ANY_SPEC] * 2,
        out_specs=[VMEM_SPEC] * 4,
        scratch_shapes=[pltpu.SemaphoreType.DMA((3,))],
        compiler_params=kernel_params(1 << 20),
        cost_estimate=pl.CostEstimate(flops=0, bytes_accessed=4 * (enc.size + dec.size), transcendentals=0),
        name="load_weights",
    )(place, active, *in_hbm(enc, dec))


def reload_kernel(dec_hbm, done_hbm, own_ref, next_ref, sems):
    del done_hbm
    pieces = [(dec_hbm.at[0, 0], own_ref), (dec_hbm.at[0, 1], next_ref)]
    copies = [pltpu.make_async_copy(source, target, sems.at[i]) for i, (source, target) in enumerate(pieces)]
    for copy in copies:
        copy.start()
    for copy in copies:
        copy.wait()


def reloaded(dec, done):
    return pl.pallas_call(
        reload_kernel,
        out_shape=[pltpu.VMEM(dec.shape[2:], dec.dtype)] * 2,
        in_specs=[ANY_SPEC] * 2,
        out_specs=[VMEM_SPEC] * 2,
        scratch_shapes=[pltpu.SemaphoreType.DMA((2,))],
        compiler_params=kernel_params(1 << 20),
        cost_estimate=pl.CostEstimate(flops=0, bytes_accessed=4 * dec.size, transcendentals=0),
        name="reload_decoder",
    )(*in_hbm(dec), done)


def decode_kernel(codes_ref, dec_ref, near_ref, far_ref):
    half, width = near_ref.shape
    for step in range(width // CHUNK):
        columns = pl.ds(step * CHUNK, CHUNK)
        part = jnp.dot(codes_ref[...], dec_ref[:, columns], preferred_element_type=jnp.float32)
        near_ref[:, columns] = part[:half]
        far_ref[:, columns] = part[half:].astype(jnp.bfloat16)


def decoded(codes, dec):
    rows, features = codes.shape
    width = dec.shape[1]
    half = (rows // CORES, width)
    return pl.pallas_call(
        decode_kernel,
        out_shape=[pltpu.VMEM(half, jnp.float32), pltpu.VMEM(half, jnp.bfloat16)],
        in_specs=[VMEM_SPEC] * 2,
        out_specs=[VMEM_SPEC] * 2,
        compiler_params=kernel_params(),
        cost_estimate=pl.CostEstimate(flops=2 * rows * width * features, bytes_accessed=2 * width * features, transcendentals=0),
        name="decode",
    )(*in_vmem(codes, dec))


def back(rows_ref, dec_ref):
    half = rows_ref.shape[1] // 2
    return sum(
        lax.dot_general(
            rows_ref[:, part], dec_ref[:, part], (((1,), (1,)), ((), ())), preferred_element_type=jnp.float32
        )
        for part in (pl.ds(0, half), pl.ds(half, half))
    )


def grad_own_kernel(rows_ref, dec_ref, out_ref, _):
    out_ref[...] = back(rows_ref, dec_ref)


def grad_all_kernel(tokens, place_ref, rows_ref, dec_ref, own_ref, out_ref):
    total = own_ref[...] + back(rows_ref, dec_ref)
    group = total.shape[0] // tokens
    for block in range(group):
        slab = slab_of(place_ref[0], block, group // CORES)
        where = pl.ds(pl.multiple_of(slab * tokens, tokens), tokens)
        out_ref[0, where, :] = total[block * tokens : (block + 1) * tokens]


def grad_own(rows, dec):
    features = dec.shape[0]
    return pl.pallas_call(
        grad_own_kernel,
        out_shape=[pltpu.VMEM((rows.shape[0], features), jnp.float32), pltpu.VMEM((8, 128), jnp.float32)],
        in_specs=[VMEM_SPEC] * 2,
        out_specs=[VMEM_SPEC] * 2,
        compiler_params=kernel_params(),
        cost_estimate=pl.CostEstimate(flops=2 * rows.size * features, bytes_accessed=2 * dec.size, transcendentals=0),
        name="grad_own",
    )(*in_vmem(rows, dec))[0]


def grad_all(place, rows, dec, own, tokens):
    return pl.pallas_call(
        functools.partial(grad_all_kernel, tokens),
        out_shape=jax.ShapeDtypeStruct((1,) + own.shape, jnp.float32),
        in_specs=[SMEM_SPEC] + [VMEM_SPEC] * 3,
        out_specs=VMEM_SPEC,
        compiler_params=kernel_params(),
        cost_estimate=pl.CostEstimate(flops=2 * rows.size * own.shape[1], bytes_accessed=2 * dec.size, transcendentals=0),
        name="grad_all",
    )(place, *in_vmem(rows, dec, own))


def blocks_of(near, far, chips):
    rows = near.shape[0] // chips
    total = near + other_core(far).astype(jnp.float32)
    return [total[chip * rows : (chip + 1) * rows] for chip in range(chips)]


def summed(blocks, sent):
    total = blocks[0]
    for came in [across(blocks[chip].astype(jnp.bfloat16), chip, len(blocks)) for chip in sent]:
        total = total + came.astype(jnp.float32)
    return total


def on_device(resid, enc_weight, enc_bias, active, dec_weight, target):
    group = lax.axis_size(AXIS) // LAYERS
    chips = group // CORES
    index = lax.axis_index(AXIS)
    layer = index // group
    place = (index % group).astype(jnp.int32).reshape(1)
    tokens = resid.shape[1]
    gate, enc, next_dec, own_dec = loaded(place, active[0], enc_weight, dec_weight, group * tokens, tokens)
    slab = resid[0]
    most, last = [across(slab, chip, chips) for chip in range(1, chips - 1)], across(slab, chips - 1, chips)
    early, late = jnp.concatenate([slab, last], axis=0), jnp.concatenate(most, axis=0)
    early_far, late_far = other_core(early), other_core(late)
    x = jnp.concatenate(
        [slab, late, last, early_far[:tokens], late_far, early_far[tokens:]], axis=0
    )
    pre = jnp.dot(x, enc, preferred_element_type=jnp.float32) + enc_bias.astype(jnp.float32)
    codes = (jax.nn.relu(pre) * gate).astype(jnp.bfloat16)
    next_near, next_far = decoded(codes, next_dec)
    own_near, own_far = decoded(codes, own_dec)

    nexts = blocks_of(next_near, next_far, chips)
    owns = blocks_of(own_near, own_far, chips)
    risen = raised(nexts[-1].astype(jnp.bfloat16), layer, group)
    owns[-1] = owns[-1] + risen.astype(jnp.float32)
    next_sum = after(summed(nexts, range(1, chips - 1)).astype(jnp.bfloat16), owns[-1])
    from_before = raised(next_sum, layer, group).astype(jnp.float32)
    crossed = across(owns[-1].astype(jnp.bfloat16), chips - 1, chips)
    own_sum = summed(owns, range(1, chips - 1))
    own_dec, next_dec = reloaded(dec_weight, own_sum)
    own_sum = after(own_sum, own_dec) + crossed.astype(jnp.float32)
    error = (own_sum + from_before - target[0].astype(jnp.float32)).astype(jnp.bfloat16)

    later = lowered(error, layer, group)
    heres = [error] + [across(error, chip, chips) for chip in range(1, chips)]
    afters = [later] + [across(later, chip, chips) for chip in range(1, chips - 1)]
    last = lowered(after(heres[-1], later), layer, group)
    here_near = jnp.concatenate(heres, axis=0)
    here_far = other_core(here_near)
    here_rows = jnp.concatenate([here_near, here_far], axis=0)
    most = after(jnp.concatenate(afters, axis=0), here_far)
    after_rows = jnp.concatenate([most, last, other_core(most), other_core(last)], axis=0)
    grad = grad_all(place, after_rows, next_dec, grad_own(here_rows, own_dec), tokens)
    return (error[None], grad)


def solution(mesh):
    return jax.shard_map(
        on_device,
        mesh=mesh,
        in_specs=(
            P("layer", "groups", None),
            P("layer", None, None),
            P("layer", None),
            P("layer", "groups", None),
            P("layer", None, None, None),
            P("layer", "groups", None),
        ),
        out_specs=(P("layer", "groups", None), P("layer", "groups", None)),
        check_vma=False,
    )
```

time: 58.7 us -> 60.7 us (1.034)
  waiting for transfers between devices: 16.4 us -> 6.74 us
  local copies, waits for them, and re-layouts: 1.16 us -> 10.1 us
  starting transfers between devices: 24.1 us -> 26.5 us
  Pallas kernels: 15.3 us -> 13.9 us
  matrix products: 0 us -> 0.81 us
  other arithmetic: 0.57 us -> 1.32 us
    unnamed x18 -> x29, local copies, waits for them, and re-layouts: 1.07 us -> 9.97 us
    ppermute x13, waiting for transfers between devices: 8.14 us -> 2.15 us  [across(): return lax.ppermute(value, AXIS, pairs)]
    pallas_call x1, Pallas kernels: 3.85 us -> 1.4 us  [grad_own(): pl.pallas_call(grad_own_kernel, out_shape=[pltpu.VMEM((rows.shape[0], fea...]
    ppermute x2, waiting for transfers between devices: 3.84 us -> 1.66 us  [raised(): lax.ppermute(value, AXIS, [(i, (i + group) % size) for i in range(size)])]
    ppermute x2, waiting for transfers between devices: 3.34 us -> 1.46 us  [lowered(): lax.ppermute(value, AXIS, [((i + group) % size, i) for i in range(size)])]
    ppermute x13, starting transfers between devices: 14.9 us -> 16.7 us  [across(): return lax.ppermute(value, AXIS, pairs)]
    ppermute x2, starting transfers between devices: 3.73 us -> 5.31 us  [lowered(): lax.ppermute(value, AXIS, [((i + group) % size, i) for i in range(size)])]
    pallas_call x3 -> x4, Pallas kernels: 9.43 us -> 10.4 us  [the longest x1 5.23 us: loaded(): pl.pallas_call(functools.partial(load_kernel, tokens), out_shape=[pltpu.V...]
  transfers between devices with their start and end apart: 26 -> 24, of which waited for: 9 -> 9; matrix products, arithmetic and copies ran while one was open for 3% -> 4% of each run, Pallas kernels for 17% -> 18%
where the time goes in v10:
time: 60.7 us; the launch traced here: 60.3 us
  starting transfers between devices  26.5 us (44%)
  Pallas kernels  13.9 us (23%)
  local copies, waits for them, and re-layouts  10.1 us (17%)
  waiting for transfers between devices  6.74 us (11%)
  other arithmetic  1.32 us (2%)
  between operations  0.98 us (2%)
  matrix products  0.81 us (1%)
    ppermute x13, starting transfers between devices, across(): return lax.ppermute(value, AXIS, pairs)  16.7 us
    unnamed x29, local copies, waits for them, and re-layouts  9.97 us
    ppermute x2, starting transfers between devices, lowered(): lax.ppermute(value, AXIS, [((i + group) % size, i) for i in range(size)])  5.31 us
    pallas_call x1, Pallas kernels, loaded(): pl.pallas_call(functools.partial(load_kernel, tokens), out_shape=[pltpu.V...  5.23 us
    pallas_call x1, Pallas kernels, reloaded(): pl.pallas_call(reload_kernel, out_shape=[pltpu.VMEM(dec.shape[2:], dec.dt...  3.51 us
    ppermute x2, starting transfers between devices, raised(): lax.ppermute(value, AXIS, [(i, (i + group) % size) for i in range(size)])  2.81 us
    ppermute x13, waiting for transfers between devices, across(): return lax.ppermute(value, AXIS, pairs)  2.15 us
    pallas_call x1, Pallas kernels, grad_all(): pl.pallas_call(functools.partial(grad_all_kernel, tokens), out_shape=jax....  2.03 us
  transfers between devices with their start and end apart: 24, of which 9 were waited for; matrix products, arithmetic and copies ran while one was open for 4% of the time, Pallas kernels for 18%

profile of v10, /device:TPU:0, one launch (start us, length us, event | category | flops | bytes accessed | tf_op | source)
XLA Modules:
  0.0 60.3 jit_solution(17668196427427104491)
XLA Ops:
  0.6 4.0 %collective-permute-start.2 = (bf16[8,8192]{1,0:T(8,128)(2,1)}, bf16[8,8192]{1,0:T(8,128)(2,1)S(1)}, u32[]{:S(2)}, u32[]{:S(2)}) collective-permute-start(bf16[8,8192]{1,0:T(8,128)(2,1)} %bitcast.13), channel_id=1, source_target_pairs={{0,6},{1,7},{2,4},{3,5},{4,2},{5,3},{6,0},{7,1},{8,14},{9,15},{10,... | collective-permute-start | bytes 393224 | tf_op jit(solution)/shard_map/ppermute | solution.py:31
  4.6 0.5 collective-permute-start.1
  5.1 0.1 collective-permute-start
  5.2 0.9 %constant_dynamic-update-slice_fusion.4 = bf16[64,8192]{1,0:T(8,128)(2,1)S(1)} fusion(bf16[1,8,8192]{2,1,0:T(8,128)(2,1)} %param.6), kind=kLoop, calls=%fused_computation.27 | loop fusion | bytes 262144
  6.2 0.7 %add.59 = f32[1,256]{1,0:T(1,128)S(1)} convert(bf16[1,256]{1,0:T(2,128)(2,1)} %param.8) | non-fusion elementwise | flops 256 | bytes 1536 | tf_op jit(solution)/shard_map/add | solution.py:225
  6.9 0.7 %copy-done.6 = s32[1,2,2]{2,1,0:T(2,128)S(1)} copy-done((s32[1,2,2]{2,1,0:T(2,128)S(1)}, s32[1,2,2]{2,1,0:T(2,128)}, u32[]{:S(2)}) %copy-start.6) | copy-done | bytes 40
  7.6 5.2 %load_weights.1 = (f32[64,256]{1,0:T(8,128)S(1)}, bf16[8192,256]{1,0:T(8,128)(2,1)S(1)}, bf16[256,8192]{1,0:T(8,128)(2,1)S(1)}, bf16[256,8192]{1,0:T(8,128)(2,1)S(1)}) custom-call(s32[1]{0:T(128)} %bitcast.1.place_ref, s32[2,2]{1,0:T(2,128)S(1)} %bitcast.12, bf16[1,8192,256]{2,1,0:T(8,128)(2,1)} %enc_hbm.1, bf16[1,2,256,8192]{3,2,1,0:T(8,128)(2,1)} %dec_hbm.3), custom_call_target="tpu_custom_call" | custom-call | bytes 25165824 | tf_op jit(solution)/shard_map/load_weights/pallas_call | solution.py:90
  12.8 2.0 %copy-done.4 = bf16[256,8192]{1,0:T(8,128)(2,1)} copy-done((bf16[256,8192]{1,0:T(8,128)(2,1)}, bf16[256,8192]{1,0:T(8,128)(2,1)S(1)}, u32[]{:S(2)}) %copy-start.4) | copy-done | bytes 4194328
  14.8 0.0 collective-permute-done.2
  14.8 0.1 collective-permute-start.3
  14.9 0.0 collective-permute-done
  14.9 0.5 collective-permute-start.4
  15.5 0.9 %collective-permute-done.3 = bf16[16,8192]{1,0:T(8,128)(2,1)S(1)} collective-permute-done((bf16[16,8192]{1,0:T(8,128)(2,1)S(1)}, bf16[16,8192]{1,0:T(8,128)(2,1)S(1)}, u32[]{:S(2)}, u32[]{:S(2)}) %collective-permute-start.3) | collective-permute-done | bytes 262176 | tf_op jit(solution)/shard_map/ppermute | solution.py:35
  16.4 0.4 collective-permute-done.4
  16.8 0.8 %fusion.2.codes_ref = bf16[64,256]{1,0:T(8,128)(2,1)S(1)} fusion(f32[64,256]{1,0:T(8,128)S(1)} %get-tuple-element.18, bf16[64,8192]{1,0:T(8,128)(2,1)S(1)} %slice_dynamic-update-slice_fusion, bf16[8192,256]{1,0:T(8,128)(2,1)S(1)} %get-tuple-element.17, f32[256]{0:T(256)S(1)} %bitcast.18), kind=kOutput, calls=%fused_computation.3 | convolution fusion | flops 268500992 | bytes 5342208 | tf_op jit(solution)/shard_map/dot_general | solution.py:225
  17.6 0.9 %decode.3 = (f32[32,8192]{1,0:T(8,128)S(1)}, bf16[32,8192]{1,0:T(8,128)(2,1)S(1)}) custom-call(bf16[64,256]{1,0:T(8,128)(2,1)S(1)} %fusion.2.codes_ref, bf16[256,8192]{1,0:T(8,128)(2,1)S(1)} %get-tuple-element.24.dec_ref), custom_call_target="tpu_custom_call" | custom-call | flops 268435456 | bytes 4194304 | tf_op jit(solution)/shard_map/decode/pallas_call | solution.py:138
  18.5 0.3 collective-permute-start.8
  18.8 2.2 %copy-done.5 = bf16[256,8192]{1,0:T(8,128)(2,1)S(1)} copy-done((bf16[256,8192]{1,0:T(8,128)(2,1)S(1)}, bf16[256,8192]{1,0:T(8,128)(2,1)}, u32[]{:S(2)}) %copy-start.5) | copy-done | bytes 4194328
  21.0 0.8 %decode.2 = (f32[32,8192]{1,0:T(8,128)S(1)}, bf16[32,8192]{1,0:T(8,128)(2,1)S(1)}) custom-call(bf16[64,256]{1,0:T(8,128)(2,1)S(1)} %fusion.2.codes_ref, bf16[256,8192]{1,0:T(8,128)(2,1)S(1)} %copy-done.5), custom_call_target="tpu_custom_call" | custom-call | flops 268435456 | bytes 4194304 | tf_op jit(solution)/shard_map/decode/pallas_call | solution.py:138
  21.8 0.3 collective-permute-start.5
  22.2 0.0 collective-permute-done.8
  22.2 0.1 fusion.8
  22.3 2.0 %collective-permute-start.9 = (bf16[8,8192]{1,0:T(8,128)(2,1)S(1)}, bf16[8,8192]{1,0:T(8,128)(2,1)S(1)}, u32[]{:S(2)}, u32[]{:S(2)}) collective-permute-start(bf16[8,8192]{1,0:T(8,128)(2,1)S(1)} %get-tuple-element.40), channel_id=1, source_target_pairs={{0,8},{1,9},{2,10},{3,11},{4,12},{5,13},{6,14},{7,15},{8,16},{9,17... | collective-permute-start | bytes 393224 | tf_op jit(solution)/shard_map/ppermute | solution.py:40
  24.4 1.5 %collective-permute-start.12 = (bf16[8,8192]{1,0:T(8,128)(2,1)S(1)}, bf16[8,8192]{1,0:T(8,128)(2,1)S(1)}, u32[]{:S(2)}, u32[]{:S(2)}) collective-permute-start(bf16[8,8192]{1,0:T(8,128)(2,1)S(1)} %get-tuple-element.41), channel_id=1, source_target_pairs={{0,4},{1,3},{2,6},{3,1},{4,0},{5,7},{6,2},{7,5},{8,12},{9,11},{10,... | collective-permute-start | bytes 393224 | tf_op jit(solution)/shard_map/ppermute | solution.py:31
  25.9 1.5 %collective-permute-start.11 = (bf16[8,8192]{1,0:T(8,128)(2,1)S(1)}, bf16[8,8192]{1,0:T(8,128)(2,1)S(1)}, u32[]{:S(2)}, u32[]{:S(2)}) collective-permute-start(bf16[8,8192]{1,0:T(8,128)(2,1)S(1)} %get-tuple-element.42), channel_id=1, source_target_pairs={{0,2},{1,5},{2,0},{3,7},{4,6},{5,1},{6,4},{7,3},{8,10},{9,13},{10,... | collective-permute-start | bytes 393224 | tf_op jit(solution)/shard_map/ppermute | solution.py:31
  27.4 0.0 collective-permute-done.5
  27.4 0.1 fusion.9
  27.5 0.6 collective-permute-start.6
  28.1 0.5 collective-permute-start.7
  28.6 1.7 %collective-permute-done.9 = bf16[8,8192]{1,0:T(8,128)(2,1)S(1)} collective-permute-done((bf16[8,8192]{1,0:T(8,128)(2,1)S(1)}, bf16[8,8192]{1,0:T(8,128)(2,1)S(1)}, u32[]{:S(2)}, u32[]{:S(2)}) %collective-permute-start.9) | collective-permute-done | bytes 131104 | tf_op jit(solution)/shard_map/ppermute | solution.py:40
  30.3 2.5 %collective-permute-start.10 = (bf16[8,8192]{1,0:T(8,128)(2,1)S(1)}, bf16[8,8192]{1,0:T(8,128)(2,1)S(1)}, u32[]{:S(2)}, u32[]{:S(2)}) collective-permute-start(bf16[8,8192]{1,0:T(8,128)(2,1)S(1)} %slice_add_fusion.1), channel_id=1, source_target_pairs={{0,6},{1,7},{2,4},{3,5},{4,2},{5,3},{6,0},{7,1},{8,14},{9,15},{10,... | collective-permute-start | bytes 393224 | tf_op jit(solution)/shard_map/ppermute | solution.py:31
  32.9 0.8 %collective-permute-start.13 = (bf16[8,8192]{1,0:T(8,128)(2,1)S(1)}, bf16[8,8192]{1,0:T(8,128)(2,1)S(1)}, u32[]{:S(2)}, u32[]{:S(2)}) collective-permute-start(bf16[8,8192]{1,0:T(8,128)(2,1)S(1)} %fusion.4), channel_id=1, source_target_pairs={{0,8},{1,9},{2,10},{3,11},{4,12},{5,13},{6,14},{7,15},{8,16},{9,17... | collective-permute-start | bytes 393224 | tf_op jit(solution)/shard_map/ppermute | solution.py:40
  33.7 0.2 collective-permute-done.6
  33.9 0.0 copy-start.9
  33.9 3.5 %reload_decoder.1 = (bf16[256,8192]{1,0:T(8,128)(2,1)S(1)}, bf16[256,8192]{1,0:T(8,128)(2,1)S(1)}) custom-call(bf16[1,2,256,8192]{3,2,1,0:T(8,128)(2,1)} %dec_hbm.3, f32[8,8192]{1,0:T(8,128)S(1)} %fusion.5.done_hbm), custom_call_target="tpu_custom_call" | custom-call | bytes 16777216 | tf_op jit(solution)/shard_map/reload_decoder/pallas_call | solution.py:113
  37.4 2.0 %copy-done = bf16[256,8192]{1,0:T(8,128)(2,1)} copy-done((bf16[256,8192]{1,0:T(8,128)(2,1)}, bf16[256,8192]{1,0:T(8,128)(2,1)S(1)}, u32[]{:S(2)}) %copy-start) | copy-done | bytes 4194328
  39.4 2.0 %copy-done.2 = bf16[256,8192]{1,0:T(8,128)(2,1)} copy-done((bf16[256,8192]{1,0:T(8,128)(2,1)}, bf16[256,8192]{1,0:T(8,128)(2,1)S(1)}, u32[]{:S(2)}) %copy-start.2) | copy-done | bytes 4194328
  41.4 0.0 collective-permute-done.13
  41.4 0.0 collective-permute-done.10
  41.4 0.1 constant_dynamic-update-slice_fusion.9
  41.5 0.0 copy-start.8
  41.5 3.0 %collective-permute-start.14 = (bf16[8,8192]{1,0:T(8,128)(2,1)S(1)}, bf16[8,8192]{1,0:T(8,128)(2,1)S(1)}, u32[]{:S(2)}, u32[]{:S(2)}) collective-permute-start(bf16[8,8192]{1,0:T(8,128)(2,1)S(1)} %get-tuple-element.33), channel_id=1, source_target_pairs={{8,0},{9,1},{10,2},{11,3},{12,4},{13,5},{14,6},{15,7},{16,8},{17,9... | collective-permute-start | bytes 393224 | tf_op jit(solution)/shard_map/ppermute | solution.py:46
  44.5 1.4 %collective-permute-start.19 = (bf16[8,8192]{1,0:T(8,128)(2,1)S(1)}, bf16[8,8192]{1,0:T(8,128)(2,1)S(1)}, u32[]{:S(2)}, u32[]{:S(2)}) collective-permute-start(bf16[8,8192]{1,0:T(8,128)(2,1)S(1)} %get-tuple-element.33), channel_id=1, source_target_pairs={{0,6},{1,7},{2,4},{3,5},{4,2},{5,3},{6,0},{7,1},{8,14},{9,15},{10,... | collective-permute-start | bytes 393224 | tf_op jit(solution)/shard_map/ppermute | solution.py:31
  45.9 1.5 %collective-permute-start.18 = (bf16[8,8192]{1,0:T(8,128)(2,1)S(1)}, bf16[8,8192]{1,0:T(8,128)(2,1)S(1)}, u32[]{:S(2)}, u32[]{:S(2)}) collective-permute-start(bf16[8,8192]{1,0:T(8,128)(2,1)S(1)} %get-tuple-element.33), channel_id=1, source_target_pairs={{0,4},{1,3},{2,6},{3,1},{4,0},{5,7},{6,2},{7,5},{8,12},{9,11},{10,... | collective-permute-start | bytes 393224 | tf_op jit(solution)/shard_map/ppermute | solution.py:31
  47.4 0.7 %collective-permute-start.17 = (bf16[8,8192]{1,0:T(8,128)(2,1)S(1)}, bf16[8,8192]{1,0:T(8,128)(2,1)S(1)}, u32[]{:S(2)}, u32[]{:S(2)}) collective-permute-start(bf16[8,8192]{1,0:T(8,128)(2,1)S(1)} %get-tuple-element.33), channel_id=1, source_target_pairs={{0,2},{1,5},{2,0},{3,7},{4,6},{5,1},{6,4},{7,3},{8,10},{9,13},{10,... | collective-permute-start | bytes 393224 | tf_op jit(solution)/shard_map/ppermute | solution.py:31
  48.0 1.3 %collective-permute-start.16 = (bf16[8,8192]{1,0:T(8,128)(2,1)S(1)}, bf16[8,8192]{1,0:T(8,128)(2,1)S(1)}, u32[]{:S(2)}, u32[]{:S(2)}) collective-permute-start(bf16[8,8192]{1,0:T(8,128)(2,1)S(1)} %broadcast_select_fusion.1), channel_id=1, source_target_pairs={{0,4},{1,3},{2,6},{3,1},{4,0},{5,7},{6,2},{7,5},{8,12},{9,11},{10,... | collective-permute-start | bytes 393224 | tf_op jit(solution)/shard_map/ppermute | solution.py:31
  49.3 0.7 %collective-permute-start.15 = (bf16[8,8192]{1,0:T(8,128)(2,1)S(1)}, bf16[8,8192]{1,0:T(8,128)(2,1)S(1)}, u32[]{:S(2)}, u32[]{:S(2)}) collective-permute-start(bf16[8,8192]{1,0:T(8,128)(2,1)S(1)} %broadcast_select_fusion.1), channel_id=1, source_target_pairs={{0,2},{1,5},{2,0},{3,7},{4,6},{5,1},{6,4},{7,3},{8,10},{9,13},{10,... | collective-permute-start | bytes 393224 | tf_op jit(solution)/shard_map/ppermute | solution.py:31
  50.0 1.0 %collective-permute-done.19 = bf16[8,8192]{1,0:T(8,128)(2,1)S(1)} collective-permute-done((bf16[8,8192]{1,0:T(8,128)(2,1)S(1)}, bf16[8,8192]{1,0:T(8,128)(2,1)S(1)}, u32[]{:S(2)}, u32[]{:S(2)}) %collective-permute-start.19) | collective-permute-done | bytes 131104 | tf_op jit(solution)/shard_map/ppermute | solution.py:31
  51.0 2.3 %collective-permute-start.21 = (bf16[8,8192]{1,0:T(8,128)(2,1)S(1)}, bf16[8,8192]{1,0:T(8,128)(2,1)S(1)}, u32[]{:S(2)}, u32[]{:S(2)}) collective-permute-start(bf16[8,8192]{1,0:T(8,128)(2,1)S(1)} %collective-permute-done.19), channel_id=1, source_target_pairs={{8,0},{9,1},{10,2},{11,3},{12,4},{13,5},{14,6},{15,7},{16,8},{17,9... | collective-permute-start | bytes 393224 | tf_op jit(solution)/shard_map/ppermute | solution.py:46
  53.3 0.1 collective-permute-done.18
  53.4 0.9 %collective-permute-done.17 = bf16[8,8192]{1,0:T(8,128)(2,1)S(1)} collective-permute-done((bf16[8,8192]{1,0:T(8,128)(2,1)S(1)}, bf16[8,8192]{1,0:T(8,128)(2,1)S(1)}, u32[]{:S(2)}, u32[]{:S(2)}) %collective-permute-start.17) | collective-permute-done | bytes 131104 | tf_op jit(solution)/shard_map/ppermute | solution.py:31
  54.3 0.1 pad_maximum_fusion.1
  54.4 0.1 collective-permute-start.20
  54.5 1.5 %collective-permute-done.21 = bf16[8,8192]{1,0:T(8,128)(2,1)S(1)} collective-permute-done((bf16[8,8192]{1,0:T(8,128)(2,1)S(1)}, bf16[8,8192]{1,0:T(8,128)(2,1)S(1)}, u32[]{:S(2)}, u32[]{:S(2)}) %collective-permute-start.21) | collective-permute-done | bytes 131104 | tf_op jit(solution)/shard_map/ppermute | solution.py:46
  56.0 0.1 collective-permute-start.23
  56.0 0.0 collective-permute-done.16
  56.1 0.0 collective-permute-done.15
  56.1 0.2 collective-permute-done.20
  56.3 0.3 collective-permute-start.22
  56.7 1.4 %grad_own.1 = (f32[64,256]{1,0:T(8,128)S(1)}, f32[8,128]{1,0:T(8,128)}) custom-call(bf16[64,8192]{1,0:T(8,128)(2,1)S(1)} %constant_dynamic-update-slice_fusion.5.rows_ref, bf16[256,8192]{1,0:T(8,128)(2,1)S(1)} %copy-done.1), custom_call_target="tpu_custom_call" | custom-call | flops 268435456 | bytes 4194304 | tf_op jit(solution)/shard_map/grad_own/pallas_call | solution.py:174
  58.1 0.0 collective-permute-done.23
  58.2 0.1 pad_maximum_fusion.rows_ref
  58.2 0.1 copy-done.3
  58.3 2.0 %grad_all.1 = f32[1,64,256]{2,1,0:T(8,128)} custom-call(s32[1]{0:T(128)} %bitcast.1.place_ref, bf16[64,8192]{1,0:T(8,128)(2,1)S(1)} %pad_maximum_fusion.rows_ref, bf16[256,8192]{1,0:T(8,128)(2,1)S(1)} %copy-done.3, f32[64,256]{1,0:T(8,128)S(1)} %get-tuple-element.31.own_ref), custom_call_target="tpu_custom_call" | custom-call | flops 268435456 | bytes 4194304 | tf_op jit(solution)/shard_map/grad_all/pallas_call | solution.py:186
  (38 shorter events, 0.4 us)
Async XLA Ops:
  0.6 14.2 %collective-permute-start.2 = (bf16[8,8192]{1,0:T(8,128)(2,1)}, bf16[8,8192]{1,0:T(8,128)(2,1)S(1)}, u32[]{:S(2)}, u32[]{:S(2)}) collective-permute-start(bf16[8,8192]{1,0:T(8,128)(2,1)} %bitcast.13), channel_id=1, source_target_pairs={{0,6},{1,7},{2,4},{3,5},{4,2},{5,3},{6,0},{7,1},{8,14},{9,15},{10,... | collective-permute-start | bytes 393224 | tf_op jit(solution)/shard_map/ppermute | solution.py:31
  4.6 10.3 %collective-permute-start.1 = (bf16[8,8192]{1,0:T(8,128)(2,1)}, bf16[8,8192]{1,0:T(8,128)(2,1)S(1)}, u32[]{:S(2)}, u32[]{:S(2)}) collective-permute-start(bf16[8,8192]{1,0:T(8,128)(2,1)} %bitcast.14), channel_id=1, source_target_pairs={{0,4},{1,3},{2,6},{3,1},{4,0},{5,7},{6,2},{7,5},{8,12},{9,11},{10,... | collective-permute-start | bytes 393224 | tf_op jit(solution)/shard_map/ppermute | solution.py:31
  5.1 9.8 %collective-permute-start = (bf16[8,8192]{1,0:T(8,128)(2,1)}, bf16[8,8192]{1,0:T(8,128)(2,1)S(1)}, u32[]{:S(2)}, u32[]{:S(2)}) collective-permute-start(bf16[8,8192]{1,0:T(8,128)(2,1)} %bitcast.15), channel_id=1, source_target_pairs={{0,2},{1,5},{2,0},{3,7},{4,6},{5,1},{6,4},{7,3},{8,10},{9,13},{10,... | collective-permute-start | bytes 393224 | tf_op jit(solution)/shard_map/ppermute | solution.py:31
  6.9 0.7 %copy-start.6 = (s32[1,2,2]{2,1,0:T(2,128)S(1)}, s32[1,2,2]{2,1,0:T(2,128)}, u32[]{:S(2)}) copy-start(s32[1,2,2]{2,1,0:T(2,128)} %param.9) | copy-start | bytes 52
  7.6 7.2 %copy-start.7 = (bf16[1,8,8192]{2,1,0:T(8,128)(2,1)S(1)}, bf16[1,8,8192]{2,1,0:T(8,128)(2,1)}, u32[]{:S(2)}) copy-start(bf16[1,8,8192]{2,1,0:T(8,128)(2,1)} %param.6) | copy-start | bytes 393220
  12.8 2.0 %copy-start.4 = (bf16[256,8192]{1,0:T(8,128)(2,1)}, bf16[256,8192]{1,0:T(8,128)(2,1)S(1)}, u32[]{:S(2)}) copy-start(bf16[256,8192]{1,0:T(8,128)(2,1)S(1)} %get-tuple-element.19.dec_ref) | copy-start | bytes 12582916
  14.8 1.6 %collective-permute-start.3 = (bf16[16,8192]{1,0:T(8,128)(2,1)S(1)}, bf16[16,8192]{1,0:T(8,128)(2,1)S(1)}, u32[]{:S(2)}, u32[]{:S(2)}) collective-permute-start(bf16[16,8192]{1,0:T(8,128)(2,1)S(1)} %pad_maximum_fusion.3), channel_id=1, source_target_pairs={{0,1},{1,0},{2,3},{3,2},{4,5},{5,4},{6,7},{7,6},{8,9},{9,8},{10,11... | collective-permute-start | bytes 786440 | tf_op jit(solution)/shard_map/ppermute | solution.py:35
  14.9 1.8 %collective-permute-start.4 = (bf16[16,8192]{1,0:T(8,128)(2,1)S(1)}, bf16[16,8192]{1,0:T(8,128)(2,1)S(1)}, u32[]{:S(2)}, u32[]{:S(2)}) collective-permute-start(bf16[16,8192]{1,0:T(8,128)(2,1)S(1)} %pad_maximum_fusion.4), channel_id=1, source_target_pairs={{0,1},{1,0},{2,3},{3,2},{4,5},{5,4},{6,7},{7,6},{8,9},{9,8},{10,11... | collective-permute-start | bytes 786440 | tf_op jit(solution)/shard_map/ppermute | solution.py:35
  18.5 3.7 %collective-permute-start.8 = (bf16[32,8192]{1,0:T(8,128)(2,1)S(1)}, bf16[32,8192]{1,0:T(8,128)(2,1)S(1)}, u32[]{:S(2)}, u32[]{:S(2)}) collective-permute-start(bf16[32,8192]{1,0:T(8,128)(2,1)S(1)} %get-tuple-element.26), channel_id=1, source_target_pairs={{0,1},{1,0},{2,3},{3,2},{4,5},{5,4},{6,7},{7,6},{8,9},{9,8},{10,11... | collective-permute-start | bytes 1572872 | tf_op jit(solution)/shard_map/ppermute | solution.py:35
  18.8 2.2 %copy-start.5 = (bf16[256,8192]{1,0:T(8,128)(2,1)S(1)}, bf16[256,8192]{1,0:T(8,128)(2,1)}, u32[]{:S(2)}) copy-start(bf16[256,8192]{1,0:T(8,128)(2,1)} %copy-done.4) | copy-start | bytes 12582916
  21.8 5.6 %collective-permute-start.5 = (bf16[32,8192]{1,0:T(8,128)(2,1)S(1)}, bf16[32,8192]{1,0:T(8,128)(2,1)S(1)}, u32[]{:S(2)}, u32[]{:S(2)}) collective-permute-start(bf16[32,8192]{1,0:T(8,128)(2,1)S(1)} %get-tuple-element.21), channel_id=1, source_target_pairs={{0,1},{1,0},{2,3},{3,2},{4,5},{5,4},{6,7},{7,6},{8,9},{9,8},{10,11... | collective-permute-start | bytes 1572872 | tf_op jit(solution)/shard_map/ppermute | solution.py:35
  22.3 7.9 %collective-permute-start.9 = (bf16[8,8192]{1,0:T(8,128)(2,1)S(1)}, bf16[8,8192]{1,0:T(8,128)(2,1)S(1)}, u32[]{:S(2)}, u32[]{:S(2)}) collective-permute-start(bf16[8,8192]{1,0:T(8,128)(2,1)S(1)} %get-tuple-element.40), channel_id=1, source_target_pairs={{0,8},{1,9},{2,10},{3,11},{4,12},{5,13},{6,14},{7,15},{8,16},{9,17... | collective-permute-start | bytes 393224 | tf_op jit(solution)/shard_map/ppermute | solution.py:40
  24.4 8.5 %collective-permute-start.12 = (bf16[8,8192]{1,0:T(8,128)(2,1)S(1)}, bf16[8,8192]{1,0:T(8,128)(2,1)S(1)}, u32[]{:S(2)}, u32[]{:S(2)}) collective-permute-start(bf16[8,8192]{1,0:T(8,128)(2,1)S(1)} %get-tuple-element.41), channel_id=1, source_target_pairs={{0,4},{1,3},{2,6},{3,1},{4,0},{5,7},{6,2},{7,5},{8,12},{9,11},{10,... | collective-permute-start | bytes 393224 | tf_op jit(solution)/shard_map/ppermute | solution.py:31
  25.9 7.0 %collective-permute-start.11 = (bf16[8,8192]{1,0:T(8,128)(2,1)S(1)}, bf16[8,8192]{1,0:T(8,128)(2,1)S(1)}, u32[]{:S(2)}, u32[]{:S(2)}) collective-permute-start(bf16[8,8192]{1,0:T(8,128)(2,1)S(1)} %get-tuple-element.42), channel_id=1, source_target_pairs={{0,2},{1,5},{2,0},{3,7},{4,6},{5,1},{6,4},{7,3},{8,10},{9,13},{10,... | collective-permute-start | bytes 393224 | tf_op jit(solution)/shard_map/ppermute | solution.py:31
  27.5 6.3 %collective-permute-start.6 = (bf16[8,8192]{1,0:T(8,128)(2,1)S(1)}, bf16[8,8192]{1,0:T(8,128)(2,1)S(1)}, u32[]{:S(2)}, u32[]{:S(2)}) collective-permute-start(bf16[8,8192]{1,0:T(8,128)(2,1)S(1)} %get-tuple-element.38), channel_id=1, source_target_pairs={{0,2},{1,5},{2,0},{3,7},{4,6},{5,1},{6,4},{7,3},{8,10},{9,13},{10,... | collective-permute-start | bytes 393224 | tf_op jit(solution)/shard_map/ppermute | solution.py:31
  28.1 5.7 %collective-permute-start.7 = (bf16[8,8192]{1,0:T(8,128)(2,1)S(1)}, bf16[8,8192]{1,0:T(8,128)(2,1)S(1)}, u32[]{:S(2)}, u32[]{:S(2)}) collective-permute-start(bf16[8,8192]{1,0:T(8,128)(2,1)S(1)} %get-tuple-element.39), channel_id=1, source_target_pairs={{0,4},{1,3},{2,6},{3,1},{4,0},{5,7},{6,2},{7,5},{8,12},{9,11},{10,... | collective-permute-start | bytes 393224 | tf_op jit(solution)/shard_map/ppermute | solution.py:31
  30.3 11.1 %collective-permute-start.10 = (bf16[8,8192]{1,0:T(8,128)(2,1)S(1)}, bf16[8,8192]{1,0:T(8,128)(2,1)S(1)}, u32[]{:S(2)}, u32[]{:S(2)}) collective-permute-start(bf16[8,8192]{1,0:T(8,128)(2,1)S(1)} %slice_add_fusion.1), channel_id=1, source_target_pairs={{0,6},{1,7},{2,4},{3,5},{4,2},{5,3},{6,0},{7,1},{8,14},{9,15},{10,... | collective-permute-start | bytes 393224 | tf_op jit(solution)/shard_map/ppermute | solution.py:31
  32.9 8.5 %collective-permute-start.13 = (bf16[8,8192]{1,0:T(8,128)(2,1)S(1)}, bf16[8,8192]{1,0:T(8,128)(2,1)S(1)}, u32[]{:S(2)}, u32[]{:S(2)}) collective-permute-start(bf16[8,8192]{1,0:T(8,128)(2,1)S(1)} %fusion.4), channel_id=1, source_target_pairs={{0,8},{1,9},{2,10},{3,11},{4,12},{5,13},{6,14},{7,15},{8,16},{9,17... | collective-permute-start | bytes 393224 | tf_op jit(solution)/shard_map/ppermute | solution.py:40
  33.9 7.6 %copy-start.9 = (bf16[1,8,8192]{2,1,0:T(8,128)(2,1)S(1)}, bf16[1,8,8192]{2,1,0:T(8,128)(2,1)}, u32[]{:S(2)}) copy-start(bf16[1,8,8192]{2,1,0:T(8,128)(2,1)} %param.11) | copy-start | bytes 393220
  37.4 2.0 %copy-start = (bf16[256,8192]{1,0:T(8,128)(2,1)}, bf16[256,8192]{1,0:T(8,128)(2,1)S(1)}, u32[]{:S(2)}) copy-start(bf16[256,8192]{1,0:T(8,128)(2,1)S(1)} %get-tuple-element.22.dec_ref) | copy-start | bytes 12582916
  39.4 2.0 %copy-start.2 = (bf16[256,8192]{1,0:T(8,128)(2,1)}, bf16[256,8192]{1,0:T(8,128)(2,1)S(1)}, u32[]{:S(2)}) copy-start(bf16[256,8192]{1,0:T(8,128)(2,1)S(1)} %get-tuple-element.30.dec_ref) | copy-start | bytes 12582916
  41.5 16.6 %copy-start.8 = (bf16[8,8192]{1,0:T(8,128)(2,1)}, bf16[8,8192]{1,0:T(8,128)(2,1)S(1)}, u32[]{:S(2)}) copy-start(bf16[8,8192]{1,0:T(8,128)(2,1)S(1)} %get-tuple-element.33) | copy-start | bytes 393220
  41.5 6.5 %collective-permute-start.14 = (bf16[8,8192]{1,0:T(8,128)(2,1)S(1)}, bf16[8,8192]{1,0:T(8,128)(2,1)S(1)}, u32[]{:S(2)}, u32[]{:S(2)}) collective-permute-start(bf16[8,8192]{1,0:T(8,128)(2,1)S(1)} %get-tuple-element.33), channel_id=1, source_target_pairs={{8,0},{9,1},{10,2},{11,3},{12,4},{13,5},{14,6},{15,7},{16,8},{17,9... | collective-permute-start | bytes 393224 | tf_op jit(solution)/shard_map/ppermute | solution.py:46
  44.5 12.2 %copy-start.1 = (bf16[256,8192]{1,0:T(8,128)(2,1)S(1)}, bf16[256,8192]{1,0:T(8,128)(2,1)}, u32[]{:S(2)}) copy-start(bf16[256,8192]{1,0:T(8,128)(2,1)} %copy-done) | copy-start | bytes 12582916
  44.5 6.5 %collective-permute-start.19 = (bf16[8,8192]{1,0:T(8,128)(2,1)S(1)}, bf16[8,8192]{1,0:T(8,128)(2,1)S(1)}, u32[]{:S(2)}, u32[]{:S(2)}) collective-permute-start(bf16[8,8192]{1,0:T(8,128)(2,1)S(1)} %get-tuple-element.33), channel_id=1, source_target_pairs={{0,6},{1,7},{2,4},{3,5},{4,2},{5,3},{6,0},{7,1},{8,14},{9,15},{10,... | collective-permute-start | bytes 393224 | tf_op jit(solution)/shard_map/ppermute | solution.py:31
  45.9 7.5 %collective-permute-start.18 = (bf16[8,8192]{1,0:T(8,128)(2,1)S(1)}, bf16[8,8192]{1,0:T(8,128)(2,1)S(1)}, u32[]{:S(2)}, u32[]{:S(2)}) collective-permute-start(bf16[8,8192]{1,0:T(8,128)(2,1)S(1)} %get-tuple-element.33), channel_id=1, source_target_pairs={{0,4},{1,3},{2,6},{3,1},{4,0},{5,7},{6,2},{7,5},{8,12},{9,11},{10,... | collective-permute-start | bytes 393224 | tf_op jit(solution)/shard_map/ppermute | solution.py:31
  47.4 6.9 %collective-permute-start.17 = (bf16[8,8192]{1,0:T(8,128)(2,1)S(1)}, bf16[8,8192]{1,0:T(8,128)(2,1)S(1)}, u32[]{:S(2)}, u32[]{:S(2)}) collective-permute-start(bf16[8,8192]{1,0:T(8,128)(2,1)S(1)} %get-tuple-element.33), channel_id=1, source_target_pairs={{0,2},{1,5},{2,0},{3,7},{4,6},{5,1},{6,4},{7,3},{8,10},{9,13},{10,... | collective-permute-start | bytes 393224 | tf_op jit(solution)/shard_map/ppermute | solution.py:31
  48.0 8.0 %collective-permute-start.16 = (bf16[8,8192]{1,0:T(8,128)(2,1)S(1)}, bf16[8,8192]{1,0:T(8,128)(2,1)S(1)}, u32[]{:S(2)}, u32[]{:S(2)}) collective-permute-start(bf16[8,8192]{1,0:T(8,128)(2,1)S(1)} %broadcast_select_fusion.1), channel_id=1, source_target_pairs={{0,4},{1,3},{2,6},{3,1},{4,0},{5,7},{6,2},{7,5},{8,12},{9,11},{10,... | collective-permute-start | bytes 393224 | tf_op jit(solution)/shard_map/ppermute | solution.py:31
  49.3 6.7 %collective-permute-start.15 = (bf16[8,8192]{1,0:T(8,128)(2,1)S(1)}, bf16[8,8192]{1,0:T(8,128)(2,1)S(1)}, u32[]{:S(2)}, u32[]{:S(2)}) collective-permute-start(bf16[8,8192]{1,0:T(8,128)(2,1)S(1)} %broadcast_select_fusion.1), channel_id=1, source_target_pairs={{0,2},{1,5},{2,0},{3,7},{4,6},{5,1},{6,4},{7,3},{8,10},{9,13},{10,... | collective-permute-start | bytes 393224 | tf_op jit(solution)/shard_map/ppermute | solution.py:31
  51.0 5.0 %collective-permute-start.21 = (bf16[8,8192]{1,0:T(8,128)(2,1)S(1)}, bf16[8,8192]{1,0:T(8,128)(2,1)S(1)}, u32[]{:S(2)}, u32[]{:S(2)}) collective-permute-start(bf16[8,8192]{1,0:T(8,128)(2,1)S(1)} %collective-permute-done.19), channel_id=1, source_target_pairs={{8,0},{9,1},{10,2},{11,3},{12,4},{13,5},{14,6},{15,7},{16,8},{17,9... | collective-permute-start | bytes 393224 | tf_op jit(solution)/shard_map/ppermute | solution.py:46
  54.4 2.0 %collective-permute-start.20 = (bf16[32,8192]{1,0:T(8,128)(2,1)S(1)}, bf16[32,8192]{1,0:T(8,128)(2,1)S(1)}, u32[]{:S(2)}, u32[]{:S(2)}) collective-permute-start(bf16[32,8192]{1,0:T(8,128)(2,1)S(1)} %pad_maximum_fusion.1), channel_id=1, source_target_pairs={{0,1},{1,0},{2,3},{3,2},{4,5},{5,4},{6,7},{7,6},{8,9},{9,8},{10,11... | collective-permute-start | bytes 1572872 | tf_op jit(solution)/shard_map/ppermute | solution.py:35
  56.0 2.2 %collective-permute-start.23 = (bf16[8,8192]{1,0:T(8,128)(2,1)S(1)}, bf16[8,8192]{1,0:T(8,128)(2,1)S(1)}, u32[]{:S(2)}, u32[]{:S(2)}) collective-permute-start(bf16[8,8192]{1,0:T(8,128)(2,1)S(1)} %broadcast_select_fusion), channel_id=1, source_target_pairs={{0,1},{1,0},{2,3},{3,2},{4,5},{5,4},{6,7},{7,6},{8,9},{9,8},{10,11... | collective-permute-start | bytes 393224 | tf_op jit(solution)/shard_map/ppermute | solution.py:35
  56.1 2.2 %copy-start.3 = (bf16[256,8192]{1,0:T(8,128)(2,1)S(1)}, bf16[256,8192]{1,0:T(8,128)(2,1)}, u32[]{:S(2)}) copy-start(bf16[256,8192]{1,0:T(8,128)(2,1)} %copy-done.2) | copy-start | bytes 12582916
  56.3 1.8 %collective-permute-start.22 = (bf16[24,8192]{1,0:T(8,128)(2,1)S(1)}, bf16[24,8192]{1,0:T(8,128)(2,1)S(1)}, u32[]{:S(2)}, u32[]{:S(2)}) collective-permute-start(bf16[24,8192]{1,0:T(8,128)(2,1)S(1)} %pad_maximum_fusion.2), channel_id=1, source_target_pairs={{0,1},{1,0},{2,3},{3,2},{4,5},{5,4},{6,7},{7,6},{8,9},{9,8},{10,11... | collective-permute-start | bytes 1179656 | tf_op jit(solution)/shard_map/ppermute | solution.py:35

commit v11 on v10

--- a/solution.py
+++ b/solution.py
@@ -13,6 +13,7 @@
 CORES = 2
 CHUNK = 1024
 LIMIT = 4 << 20
+HIGH = 28 << 20
 AXIS = "layer"
 
 ANY_SPEC = pl.BlockSpec(memory_space=pl.ANY)
@@ -69,39 +70,8 @@
     return pltpu.CompilerParams(vmem_limit_bytes=limit)
 
 
-def load_kernel(tokens, place_ref, active_ref, enc_hbm, dec_hbm, gate_ref, enc_ref, next_ref, own_ref, sems):
+def load_kernel(enc_hbm, dec_hbm, enc_ref, own_ref, next_ref, sems):
     pieces = [(enc_hbm.at[0], enc_ref), (dec_hbm.at[0, 1], next_ref), (dec_hbm.at[0, 0], own_ref)]
-    copies = [pltpu.make_async_copy(source, target, sems.at[i]) for i, (source, target) in enumerate(pieces)]
-    for copy in copies:
-        copy.start()
-    group = gate_ref.shape[0] // tokens
-    for block in range(group):
-        tile = (slab_of(place_ref[0], block, group // CORES) * tokens) // TILE
-        for part in range(active_ref.shape[1]):
-            live = active_ref[tile, part].astype(jnp.float32)
-            gate_ref[pl.ds(block * tokens, tokens), pl.ds(part * BLOCK, BLOCK)] = jnp.full((tokens, BLOCK), live)
-    for copy in copies:
-        copy.wait()
-
-
-def loaded(place, active, enc, dec, rows, tokens):
-    _, depth, features = enc.shape
-    block = pltpu.VMEM(dec.shape[2:], dec.dtype)
-    return pl.pallas_call(
-        functools.partial(load_kernel, tokens),
-        out_shape=[pltpu.VMEM((rows, features), jnp.float32), pltpu.VMEM((depth, features), enc.dtype), block, block],
-        in_specs=[SMEM_SPEC] * 2 + [ANY_SPEC] * 2,
-        out_specs=[VMEM_SPEC] * 4,
-        scratch_shapes=[pltpu.SemaphoreType.DMA((3,))],
-        compiler_params=kernel_params(1 << 20),
-        cost_estimate=pl.CostEstimate(flops=0, bytes_accessed=4 * (enc.size + dec.size), transcendentals=0),
-        name="load_weights",
-    )(place, active, *in_hbm(enc, dec))
-
-
-def reload_kernel(dec_hbm, done_hbm, own_ref, next_ref, sems):
-    del done_hbm
-    pieces = [(dec_hbm.at[0, 0], own_ref), (dec_hbm.at[0, 1], next_ref)]
     copies = [pltpu.make_async_copy(source, target, sems.at[i]) for i, (source, target) in enumerate(pieces)]
     for copy in copies:
         copy.start()
@@ -109,40 +79,87 @@
         copy.wait()
 
 
-def reloaded(dec, done):
-    return pl.pallas_call(
-        reload_kernel,
-        out_shape=[pltpu.VMEM(dec.shape[2:], dec.dtype)] * 2,
+def loaded(enc, dec):
+    block = pltpu.VMEM(dec.shape[2:], dec.dtype)
+    return pl.pallas_call(
+        load_kernel,
+        out_shape=[pltpu.VMEM(enc.shape[1:], enc.dtype), block, block],
         in_specs=[ANY_SPEC] * 2,
-        out_specs=[VMEM_SPEC] * 2,
-        scratch_shapes=[pltpu.SemaphoreType.DMA((2,))],
-        compiler_params=kernel_params(1 << 20),
-        cost_estimate=pl.CostEstimate(flops=0, bytes_accessed=4 * dec.size, transcendentals=0),
-        name="reload_decoder",
-    )(*in_hbm(dec), done)
-
-
-def decode_kernel(codes_ref, dec_ref, near_ref, far_ref):
+        out_specs=[VMEM_SPEC] * 3,
+        scratch_shapes=[pltpu.SemaphoreType.DMA((3,))],
+        compiler_params=kernel_params(HIGH),
+        cost_estimate=pl.CostEstimate(flops=0, bytes_accessed=4 * (enc.size + dec.size), transcendentals=0),
+        name="load_weights",
+    )(*in_hbm(enc, dec))
+
+
+def decode(codes, dec_ref, near_ref, far_ref):
     half, width = near_ref.shape
     for step in range(width // CHUNK):
         columns = pl.ds(step * CHUNK, CHUNK)
-        part = jnp.dot(codes_ref[...], dec_ref[:, columns], preferred_element_type=jnp.float32)
+        part = jnp.dot(codes, dec_ref[:, columns], preferred_element_type=jnp.float32)
         near_ref[:, columns] = part[:half]
         far_ref[:, columns] = part[half:].astype(jnp.bfloat16)
+
+
+def gate_of(place, active_ref, rows, tokens):
+    group = rows // tokens
+    block = lax.broadcasted_iota(jnp.int32, (rows, BLOCK), 0) // tokens
+    tile = (slab_of(place, block, group // CORES) * tokens) // TILE
+    parts = []
+    for part in range(active_ref.shape[1]):
+        live = jnp.zeros((rows, BLOCK), jnp.int32)
+        for i in range(active_ref.shape[0]):
+            live = jnp.where(tile == i, active_ref[i, part], live)
+        parts.append(live.astype(jnp.float32))
+    return jnp.concatenate(parts, axis=1)
+
+
+def encode_kernel(tokens, place_ref, active_ref, x_ref, enc_ref, bias_ref, dec_ref, codes_ref, near_ref, far_ref):
+    rows, depth = x_ref.shape
+    half = depth // 2
+    pre = bias_ref[...].astype(jnp.float32) + sum(
+        jnp.dot(x_ref[:, part], enc_ref[part, :], preferred_element_type=jnp.float32)
+        for part in (pl.ds(0, half), pl.ds(half, half))
+    )
+    codes = jnp.maximum(pre, 0.0) * gate_of(place_ref[0], active_ref, rows, tokens)
+    codes_ref[...] = codes.astype(jnp.bfloat16)
+    decode(codes_ref[...], dec_ref, near_ref, far_ref)
+
+
+def decode_kernel(codes_ref, dec_ref, near_ref, far_ref):
+    decode(codes_ref[...], dec_ref, near_ref, far_ref)
+
+
+def halves_of(rows, width):
+    return [pltpu.VMEM((rows // CORES, width), jnp.float32), pltpu.VMEM((rows // CORES, width), jnp.bfloat16)]
+
+
+def encoded(place, active, x, enc, bias, dec, tokens):
+    rows, depth = x.shape
+    features = enc.shape[1]
+    return pl.pallas_call(
+        functools.partial(encode_kernel, tokens),
+        out_shape=[pltpu.VMEM((rows, features), jnp.bfloat16)] + halves_of(rows, depth),
+        in_specs=[SMEM_SPEC, SMEM_SPEC] + [VMEM_SPEC] * 4,
+        out_specs=[VMEM_SPEC] * 3,
+        compiler_params=kernel_params(),
+        cost_estimate=pl.CostEstimate(flops=4 * rows * depth * features, bytes_accessed=4 * depth * features, transcendentals=0),
+        name="encode",
+    )(place, active, *in_vmem(x, enc, bias, dec))
 
 
 def decoded(codes, dec):
     rows, features = codes.shape
     width = dec.shape[1]
-    half = (rows // CORES, width)
     return pl.pallas_call(
         decode_kernel,
-        out_shape=[pltpu.VMEM(half, jnp.float32), pltpu.VMEM(half, jnp.bfloat16)],
+        out_shape=halves_of(rows, width),
         in_specs=[VMEM_SPEC] * 2,
         out_specs=[VMEM_SPEC] * 2,
         compiler_params=kernel_params(),
         cost_estimate=pl.CostEstimate(flops=2 * rows * width * features, bytes_accessed=2 * width * features, transcendentals=0),
-        name="decode",
+        name="decode_own",
     )(*in_vmem(codes, dec))
 
 
@@ -214,7 +231,7 @@
     layer = index // group
     place = (index % group).astype(jnp.int32).reshape(1)
     tokens = resid.shape[1]
-    gate, enc, next_dec, own_dec = loaded(place, active[0], enc_weight, dec_weight, group * tokens, tokens)
+    enc, own_dec, next_dec = loaded(enc_weight, dec_weight)
     slab = resid[0]
     most, last = [across(slab, chip, chips) for chip in range(1, chips - 1)], across(slab, chips - 1, chips)
     early, late = jnp.concatenate([slab, last], axis=0), jnp.concatenate(most, axis=0)
@@ -222,9 +239,7 @@
     x = jnp.concatenate(
         [slab, late, last, early_far[:tokens], late_far, early_far[tokens:]], axis=0
     )
-    pre = jnp.dot(x, enc, preferred_element_type=jnp.float32) + enc_bias.astype(jnp.float32)
-    codes = (jax.nn.relu(pre) * gate).astype(jnp.bfloat16)
-    next_near, next_far = decoded(codes, next_dec)
+    codes, next_near, next_far = encoded(place, active[0], x, enc, enc_bias, next_dec, tokens)
     own_near, own_far = decoded(codes, own_dec)
 
     nexts = blocks_of(next_near, next_far, chips)
@@ -233,10 +248,7 @@
     owns[-1] = owns[-1] + risen.astype(jnp.float32)
     next_sum = after(summed(nexts, range(1, chips - 1)).astype(jnp.bfloat16), owns[-1])
     from_before = raised(next_sum, layer, group).astype(jnp.float32)
-    crossed = across(owns[-1].astype(jnp.bfloat16), chips - 1, chips)
-    own_sum = summed(owns, range(1, chips - 1))
-    own_dec, next_dec = reloaded(dec_weight, own_sum)
-    own_sum = after(own_sum, own_dec) + crossed.astype(jnp.float32)
+    own_sum = summed(owns, range(1, chips))
     error = (own_sum + from_before - target[0].astype(jnp.float32)).astype(jnp.bfloat16)
 
     later = lowered(error, layer, group)

time: 60.7 us -> 57 us (0.939)
  waiting for transfers between devices: 6.74 us -> 14.1 us
  local copies, waits for them, and re-layouts: 10.1 us -> 4.04 us
  Pallas kernels: 13.9 us -> 12.1 us
  starting transfers between devices: 26.5 us -> 24.9 us
  matrix products: 0.81 us -> 0 us
  other arithmetic: 1.32 us -> 0.61 us
    unnamed x29, local copies, waits for them, and re-layouts: 9.97 us -> 3.95 us
    ppermute x13, waiting for transfers between devices: 2.15 us -> 5.9 us  [across(): return lax.ppermute(value, AXIS, pairs)]
    ppermute x2, waiting for transfers between devices: 1.66 us -> 3.82 us  [raised(): lax.ppermute(value, AXIS, [(i, (i + group) % size) for i in range(size)])]
    pallas_call x4 -> x3, Pallas kernels: 10.4 us -> 8.69 us  [the longest x1 4.72 us: loaded(): pl.pallas_call(load_kernel, out_shape=[pltpu.VMEM(enc.shape[1:], enc.dtyp...]
    ppermute x2, waiting for transfers between devices: 1.46 us -> 3.1 us  [lowered(): lax.ppermute(value, AXIS, [((i + group) % size, i) for i in range(size)])]
    ppermute x2, starting transfers between devices: 5.31 us -> 3.97 us  [lowered(): lax.ppermute(value, AXIS, [((i + group) % size, i) for i in range(size)])]
    ppermute x13, starting transfers between devices: 16.7 us -> 15.6 us  [across(): return lax.ppermute(value, AXIS, pairs)]
    ppermute x2, starting transfers between devices: 2.81 us -> 3.66 us  [raised(): lax.ppermute(value, AXIS, [(i, (i + group) % size) for i in range(size)])]
  transfers between devices with their start and end apart: 24 -> 24, of which waited for: 9 -> 9; matrix products, arithmetic and copies ran while one was open for 4% -> 3% of each run, Pallas kernels for 18% -> 12%
where the time goes in v11:
time: 57 us; the launch traced here: 56.8 us
  starting transfers between devices  24.9 us (44%)
  waiting for transfers between devices  14.1 us (25%)
  Pallas kernels  12.1 us (21%)
  local copies, waits for them, and re-layouts  4.04 us (7%)
  between operations  1.03 us (2%)
  other arithmetic  0.61 us (1%)
    ppermute x13, starting transfers between devices, across(): return lax.ppermute(value, AXIS, pairs)  15.6 us
    ppermute x13, waiting for transfers between devices, across(): return lax.ppermute(value, AXIS, pairs)  5.9 us
    pallas_call x1, Pallas kernels, loaded(): pl.pallas_call(load_kernel, out_shape=[pltpu.VMEM(enc.shape[1:], enc.dtyp...  4.72 us
    ppermute x2, starting transfers between devices, lowered(): lax.ppermute(value, AXIS, [((i + group) % size, i) for i in range(size)])  3.97 us
    unnamed x29, local copies, waits for them, and re-layouts  3.95 us
    ppermute x2, waiting for transfers between devices, raised(): lax.ppermute(value, AXIS, [(i, (i + group) % size) for i in range(size)])  3.82 us
    ppermute x2, starting transfers between devices, raised(): lax.ppermute(value, AXIS, [(i, (i + group) % size) for i in range(size)])  3.66 us
    pallas_call x1, Pallas kernels, encoded(): pl.pallas_call(functools.partial(encode_kernel, tokens), out_shape=[pltpu...  3.14 us
  transfers between devices with their start and end apart: 24, of which 9 were waited for; matrix products, arithmetic and copies ran while one was open for 3% of the time, Pallas kernels for 12%

profile of v11, /device:TPU:0, one launch (start us, length us, event | category | flops | bytes accessed | tf_op | source)
XLA Modules:
  0.0 56.8 jit_solution(6560295449014146427)
XLA Ops:
  0.6 4.0 %collective-permute-start.2 = (bf16[8,8192]{1,0:T(8,128)(2,1)}, bf16[8,8192]{1,0:T(8,128)(2,1)S(1)}, u32[]{:S(2)}, u32[]{:S(2)}) collective-permute-start(bf16[8,8192]{1,0:T(8,128)(2,1)} %bitcast.10), channel_id=1, source_target_pairs={{0,6},{1,7},{2,4},{3,5},{4,2},{5,3},{6,0},{7,1},{8,14},{9,15},{10,... | collective-permute-start | bytes 393224 | tf_op jit(solution)/shard_map/ppermute | solution.py:32
  4.6 0.5 collective-permute-start.1
  5.1 0.1 collective-permute-start
  5.2 0.9 %constant_dynamic-update-slice_fusion.4 = bf16[64,8192]{1,0:T(8,128)(2,1)S(1)} fusion(bf16[1,8,8192]{2,1,0:T(8,128)(2,1)} %param.6), kind=kLoop, calls=%fused_computation.25 | loop fusion | bytes 262144
  6.2 0.0 copy-start.7
  6.2 4.7 %load_weights.1 = (bf16[8192,256]{1,0:T(8,128)(2,1)S(1)}, bf16[256,8192]{1,0:T(8,128)(2,1)S(1)}, bf16[256,8192]{1,0:T(8,128)(2,1)S(1)}) custom-call(bf16[1,8192,256]{2,1,0:T(8,128)(2,1)} %enc_hbm.1, bf16[1,2,256,8192]{3,2,1,0:T(8,128)(2,1)} %dec_hbm.1), custom_call_target="tpu_custom_call" | custom-call | bytes 25165824 | tf_op jit(solution)/shard_map/load_weights/pallas_call | solution.py:84
  11.0 0.0 copy-start.5
  11.0 0.0 copy-start.6
  11.0 0.0 collective-permute-done.2
  11.0 0.1 collective-permute-start.3
  11.1 0.0 collective-permute-done.1
  11.1 0.2 collective-permute-done
  11.4 0.3 collective-permute-start.4
  11.7 0.9 %collective-permute-done.3 = bf16[16,8192]{1,0:T(8,128)(2,1)S(1)} collective-permute-done((bf16[16,8192]{1,0:T(8,128)(2,1)S(1)}, bf16[16,8192]{1,0:T(8,128)(2,1)S(1)}, u32[]{:S(2)}, u32[]{:S(2)}) %collective-permute-start.3) | collective-permute-done | bytes 262176 | tf_op jit(solution)/shard_map/ppermute | solution.py:36
  12.6 0.4 collective-permute-done.4
  13.1 3.1 %encode.1 = (bf16[64,256]{1,0:T(8,128)(2,1)S(1)}, f32[32,8192]{1,0:T(8,128)S(1)}, bf16[32,8192]{1,0:T(8,128)(2,1)S(1)}) custom-call(s32[1]{0:T(128)} %bitcast.place_ref, s32[2,2]{1,0:T(2,128)S(1)} %bitcast.9, bf16[64,8192]{1,0:T(8,128)(2,1)S(1)} %slice_dynamic-update-slice_fusion.x_ref, bf16[8192,256]{1,0:T(8,128)(2,1)S(1)} %get-tuple-element.14.enc_ref, ...), custom_call_target="tpu_custom_call" | custom-call | flops 536870912 | bytes 8388608 | tf_op jit(solution)/shard_map/encode/pallas_call | solution.py:141
  16.2 0.3 collective-permute-start.8
  16.5 2.2 %copy-done.1 = bf16[256,8192]{1,0:T(8,128)(2,1)S(1)} copy-done((bf16[256,8192]{1,0:T(8,128)(2,1)S(1)}, bf16[256,8192]{1,0:T(8,128)(2,1)}, u32[]{:S(2)}) %copy-start.1) | copy-done | bytes 4194328
  18.7 0.8 %decode_own.1 = (f32[32,8192]{1,0:T(8,128)S(1)}, bf16[32,8192]{1,0:T(8,128)(2,1)S(1)}) custom-call(bf16[64,256]{1,0:T(8,128)(2,1)S(1)} %get-tuple-element.16.codes_ref, bf16[256,8192]{1,0:T(8,128)(2,1)S(1)} %copy-done.1), custom_call_target="tpu_custom_call" | custom-call | flops 268435456 | bytes 4194304 | tf_op jit(solution)/shard_map/decode_own/pallas_call | solution.py:155
  19.6 0.3 collective-permute-start.5
  19.9 0.0 collective-permute-done.8
  19.9 0.1 fusion.9
  20.1 2.0 %collective-permute-start.9 = (bf16[8,8192]{1,0:T(8,128)(2,1)S(1)}, bf16[8,8192]{1,0:T(8,128)(2,1)S(1)}, u32[]{:S(2)}, u32[]{:S(2)}) collective-permute-start(bf16[8,8192]{1,0:T(8,128)(2,1)S(1)} %get-tuple-element.34), channel_id=1, source_target_pairs={{0,8},{1,9},{2,10},{3,11},{4,12},{5,13},{6,14},{7,15},{8,16},{9,17... | collective-permute-start | bytes 393224 | tf_op jit(solution)/shard_map/ppermute | solution.py:41
  22.1 1.5 %collective-permute-start.12 = (bf16[8,8192]{1,0:T(8,128)(2,1)S(1)}, bf16[8,8192]{1,0:T(8,128)(2,1)S(1)}, u32[]{:S(2)}, u32[]{:S(2)}) collective-permute-start(bf16[8,8192]{1,0:T(8,128)(2,1)S(1)} %get-tuple-element.35), channel_id=1, source_target_pairs={{0,4},{1,3},{2,6},{3,1},{4,0},{5,7},{6,2},{7,5},{8,12},{9,11},{10,... | collective-permute-start | bytes 393224 | tf_op jit(solution)/shard_map/ppermute | solution.py:32
  23.6 1.5 %collective-permute-start.11 = (bf16[8,8192]{1,0:T(8,128)(2,1)S(1)}, bf16[8,8192]{1,0:T(8,128)(2,1)S(1)}, u32[]{:S(2)}, u32[]{:S(2)}) collective-permute-start(bf16[8,8192]{1,0:T(8,128)(2,1)S(1)} %get-tuple-element.36), channel_id=1, source_target_pairs={{0,2},{1,5},{2,0},{3,7},{4,6},{5,1},{6,4},{7,3},{8,10},{9,13},{10,... | collective-permute-start | bytes 393224 | tf_op jit(solution)/shard_map/ppermute | solution.py:32
  25.1 0.0 collective-permute-done.5
  25.1 0.1 fusion.8
  25.3 0.6 %collective-permute-start.6 = (bf16[8,8192]{1,0:T(8,128)(2,1)S(1)}, bf16[8,8192]{1,0:T(8,128)(2,1)S(1)}, u32[]{:S(2)}, u32[]{:S(2)}) collective-permute-start(bf16[8,8192]{1,0:T(8,128)(2,1)S(1)} %get-tuple-element.32), channel_id=1, source_target_pairs={{0,2},{1,5},{2,0},{3,7},{4,6},{5,1},{6,4},{7,3},{8,10},{9,13},{10,... | collective-permute-start | bytes 393224 | tf_op jit(solution)/shard_map/ppermute | solution.py:32
  25.8 0.5 collective-permute-start.7
  26.4 1.9 %collective-permute-done.12 = bf16[8,8192]{1,0:T(8,128)(2,1)S(1)} collective-permute-done((bf16[8,8192]{1,0:T(8,128)(2,1)S(1)}, bf16[8,8192]{1,0:T(8,128)(2,1)S(1)}, u32[]{:S(2)}, u32[]{:S(2)}) %collective-permute-start.12) | collective-permute-done | bytes 131104 | tf_op jit(solution)/shard_map/ppermute | solution.py:32
  28.3 1.4 %collective-permute-done.11 = bf16[8,8192]{1,0:T(8,128)(2,1)S(1)} collective-permute-done((bf16[8,8192]{1,0:T(8,128)(2,1)S(1)}, bf16[8,8192]{1,0:T(8,128)(2,1)S(1)}, u32[]{:S(2)}, u32[]{:S(2)}) %collective-permute-start.11) | collective-permute-done | bytes 131104 | tf_op jit(solution)/shard_map/ppermute | solution.py:32
  29.8 0.0 collective-permute-done.9
  29.8 1.6 %collective-permute-start.13 = (bf16[8,8192]{1,0:T(8,128)(2,1)S(1)}, bf16[8,8192]{1,0:T(8,128)(2,1)S(1)}, u32[]{:S(2)}, u32[]{:S(2)}) collective-permute-start(bf16[8,8192]{1,0:T(8,128)(2,1)S(1)} %fusion.1), channel_id=1, source_target_pairs={{0,8},{1,9},{2,10},{3,11},{4,12},{5,13},{6,14},{7,15},{8,16},{9,17... | collective-permute-start | bytes 393224 | tf_op jit(solution)/shard_map/ppermute | solution.py:41
  31.4 1.4 %collective-permute-start.10 = (bf16[8,8192]{1,0:T(8,128)(2,1)S(1)}, bf16[8,8192]{1,0:T(8,128)(2,1)S(1)}, u32[]{:S(2)}, u32[]{:S(2)}) collective-permute-start(bf16[8,8192]{1,0:T(8,128)(2,1)S(1)} %slice_add_fusion.1), channel_id=1, source_target_pairs={{0,6},{1,7},{2,4},{3,5},{4,2},{5,3},{6,0},{7,1},{8,14},{9,15},{10,... | collective-permute-start | bytes 393224 | tf_op jit(solution)/shard_map/ppermute | solution.py:32
  32.8 0.0 collective-permute-done.6
  32.8 0.0 collective-permute-done.7
  32.8 3.8 %collective-permute-done.13 = bf16[8,8192]{1,0:T(8,128)(2,1)S(1)} collective-permute-done((bf16[8,8192]{1,0:T(8,128)(2,1)S(1)}, bf16[8,8192]{1,0:T(8,128)(2,1)S(1)}, u32[]{:S(2)}, u32[]{:S(2)}) %collective-permute-start.13) | collective-permute-done | bytes 131104 | tf_op jit(solution)/shard_map/ppermute | solution.py:41
  36.6 0.7 %collective-permute-done.10 = bf16[8,8192]{1,0:T(8,128)(2,1)S(1)} collective-permute-done((bf16[8,8192]{1,0:T(8,128)(2,1)S(1)}, bf16[8,8192]{1,0:T(8,128)(2,1)S(1)}, u32[]{:S(2)}, u32[]{:S(2)}) %collective-permute-start.10) | collective-permute-done | bytes 131104 | tf_op jit(solution)/shard_map/ppermute | solution.py:32
  37.3 0.1 constant_dynamic-update-slice_fusion.9
  37.4 0.0 copy-start.8
  37.4 2.3 %collective-permute-start.14 = (bf16[8,8192]{1,0:T(8,128)(2,1)S(1)}, bf16[8,8192]{1,0:T(8,128)(2,1)S(1)}, u32[]{:S(2)}, u32[]{:S(2)}) collective-permute-start(bf16[8,8192]{1,0:T(8,128)(2,1)S(1)} %get-tuple-element.27), channel_id=1, source_target_pairs={{8,0},{9,1},{10,2},{11,3},{12,4},{13,5},{14,6},{15,7},{16,8},{17,9... | collective-permute-start | bytes 393224 | tf_op jit(solution)/shard_map/ppermute | solution.py:47
  39.7 1.4 %collective-permute-start.19 = (bf16[8,8192]{1,0:T(8,128)(2,1)S(1)}, bf16[8,8192]{1,0:T(8,128)(2,1)S(1)}, u32[]{:S(2)}, u32[]{:S(2)}) collective-permute-start(bf16[8,8192]{1,0:T(8,128)(2,1)S(1)} %get-tuple-element.27), channel_id=1, source_target_pairs={{0,6},{1,7},{2,4},{3,5},{4,2},{5,3},{6,0},{7,1},{8,14},{9,15},{10,... | collective-permute-start | bytes 393224 | tf_op jit(solution)/shard_map/ppermute | solution.py:32
  41.1 1.2 %collective-permute-start.18 = (bf16[8,8192]{1,0:T(8,128)(2,1)S(1)}, bf16[8,8192]{1,0:T(8,128)(2,1)S(1)}, u32[]{:S(2)}, u32[]{:S(2)}) collective-permute-start(bf16[8,8192]{1,0:T(8,128)(2,1)S(1)} %get-tuple-element.27), channel_id=1, source_target_pairs={{0,4},{1,3},{2,6},{3,1},{4,0},{5,7},{6,2},{7,5},{8,12},{9,11},{10,... | collective-permute-start | bytes 393224 | tf_op jit(solution)/shard_map/ppermute | solution.py:32
  42.3 0.9 %collective-permute-start.17 = (bf16[8,8192]{1,0:T(8,128)(2,1)S(1)}, bf16[8,8192]{1,0:T(8,128)(2,1)S(1)}, u32[]{:S(2)}, u32[]{:S(2)}) collective-permute-start(bf16[8,8192]{1,0:T(8,128)(2,1)S(1)} %get-tuple-element.27), channel_id=1, source_target_pairs={{0,2},{1,5},{2,0},{3,7},{4,6},{5,1},{6,4},{7,3},{8,10},{9,13},{10,... | collective-permute-start | bytes 393224 | tf_op jit(solution)/shard_map/ppermute | solution.py:32
  43.2 0.0 collective-permute-done.14
  43.2 0.6 %collective-permute-start.16 = (bf16[8,8192]{1,0:T(8,128)(2,1)S(1)}, bf16[8,8192]{1,0:T(8,128)(2,1)S(1)}, u32[]{:S(2)}, u32[]{:S(2)}) collective-permute-start(bf16[8,8192]{1,0:T(8,128)(2,1)S(1)} %broadcast_select_fusion.1), channel_id=1, source_target_pairs={{0,4},{1,3},{2,6},{3,1},{4,0},{5,7},{6,2},{7,5},{8,12},{9,11},{10,... | collective-permute-start | bytes 393224 | tf_op jit(solution)/shard_map/ppermute | solution.py:32
  43.8 1.4 %collective-permute-start.15 = (bf16[8,8192]{1,0:T(8,128)(2,1)S(1)}, bf16[8,8192]{1,0:T(8,128)(2,1)S(1)}, u32[]{:S(2)}, u32[]{:S(2)}) collective-permute-start(bf16[8,8192]{1,0:T(8,128)(2,1)S(1)} %broadcast_select_fusion.1), channel_id=1, source_target_pairs={{0,2},{1,5},{2,0},{3,7},{4,6},{5,1},{6,4},{7,3},{8,10},{9,13},{10,... | collective-permute-start | bytes 393224 | tf_op jit(solution)/shard_map/ppermute | solution.py:32
  45.2 1.6 %collective-permute-done.19 = bf16[8,8192]{1,0:T(8,128)(2,1)S(1)} collective-permute-done((bf16[8,8192]{1,0:T(8,128)(2,1)S(1)}, bf16[8,8192]{1,0:T(8,128)(2,1)S(1)}, u32[]{:S(2)}, u32[]{:S(2)}) %collective-permute-start.19) | collective-permute-done | bytes 131104 | tf_op jit(solution)/shard_map/ppermute | solution.py:32
  46.8 1.7 %collective-permute-start.21 = (bf16[8,8192]{1,0:T(8,128)(2,1)S(1)}, bf16[8,8192]{1,0:T(8,128)(2,1)S(1)}, u32[]{:S(2)}, u32[]{:S(2)}) collective-permute-start(bf16[8,8192]{1,0:T(8,128)(2,1)S(1)} %collective-permute-done.19), channel_id=1, source_target_pairs={{8,0},{9,1},{10,2},{11,3},{12,4},{13,5},{14,6},{15,7},{16,8},{17,9... | collective-permute-start | bytes 393224 | tf_op jit(solution)/shard_map/ppermute | solution.py:47
  48.5 0.0 collective-permute-done.18
  48.5 0.0 collective-permute-done.17
  48.5 0.1 pad_maximum_fusion.1
  48.6 0.1 collective-permute-start.20
  48.7 3.1 %collective-permute-done.21 = bf16[8,8192]{1,0:T(8,128)(2,1)S(1)} collective-permute-done((bf16[8,8192]{1,0:T(8,128)(2,1)S(1)}, bf16[8,8192]{1,0:T(8,128)(2,1)S(1)}, u32[]{:S(2)}, u32[]{:S(2)}) %collective-permute-start.21) | collective-permute-done | bytes 131104 | tf_op jit(solution)/shard_map/ppermute | solution.py:47
  51.8 0.1 collective-permute-start.23
  51.9 0.0 collective-permute-done.16
  51.9 0.0 collective-permute-done.15
  52.0 0.0 collective-permute-done.20
  52.0 0.5 collective-permute-start.22
  52.6 1.4 %grad_own.1 = (f32[64,256]{1,0:T(8,128)S(1)}, f32[8,128]{1,0:T(8,128)}) custom-call(bf16[64,8192]{1,0:T(8,128)(2,1)S(1)} %constant_dynamic-update-slice_fusion.5.rows_ref, bf16[256,8192]{1,0:T(8,128)(2,1)S(1)} %copy-done.2), custom_call_target="tpu_custom_call" | custom-call | flops 268435456 | bytes 4194304 | tf_op jit(solution)/shard_map/grad_own/pallas_call | solution.py:191
  54.0 0.0 collective-permute-done.23
  54.0 0.1 pad_maximum_fusion.rows_ref
  54.1 0.7 %copy-done.4 = bf16[256,8192]{1,0:T(8,128)(2,1)S(1)} copy-done((bf16[256,8192]{1,0:T(8,128)(2,1)S(1)}, bf16[256,8192]{1,0:T(8,128)(2,1)}, u32[]{:S(2)}) %copy-start.4) | copy-done | bytes 4194328
  54.8 2.0 %grad_all.1 = f32[1,64,256]{2,1,0:T(8,128)} custom-call(s32[1]{0:T(128)} %bitcast.place_ref, bf16[64,8192]{1,0:T(8,128)(2,1)S(1)} %pad_maximum_fusion.rows_ref, bf16[256,8192]{1,0:T(8,128)(2,1)S(1)} %copy-done.4, f32[64,256]{1,0:T(8,128)S(1)} %get-tuple-element.25.own_ref), custom_call_target="tpu_custom_call" | custom-call | flops 268435456 | bytes 4194304 | tf_op jit(solution)/shard_map/grad_all/pallas_call | solution.py:203
  (34 shorter events, 0.4 us)
Async XLA Ops:
  0.6 10.4 %collective-permute-start.2 = (bf16[8,8192]{1,0:T(8,128)(2,1)}, bf16[8,8192]{1,0:T(8,128)(2,1)S(1)}, u32[]{:S(2)}, u32[]{:S(2)}) collective-permute-start(bf16[8,8192]{1,0:T(8,128)(2,1)} %bitcast.10), channel_id=1, source_target_pairs={{0,6},{1,7},{2,4},{3,5},{4,2},{5,3},{6,0},{7,1},{8,14},{9,15},{10,... | collective-permute-start | bytes 393224 | tf_op jit(solution)/shard_map/ppermute | solution.py:32
  4.6 6.5 %collective-permute-start.1 = (bf16[8,8192]{1,0:T(8,128)(2,1)}, bf16[8,8192]{1,0:T(8,128)(2,1)S(1)}, u32[]{:S(2)}, u32[]{:S(2)}) collective-permute-start(bf16[8,8192]{1,0:T(8,128)(2,1)} %bitcast.11), channel_id=1, source_target_pairs={{0,4},{1,3},{2,6},{3,1},{4,0},{5,7},{6,2},{7,5},{8,12},{9,11},{10,... | collective-permute-start | bytes 393224 | tf_op jit(solution)/shard_map/ppermute | solution.py:32
  5.1 6.3 %collective-permute-start = (bf16[8,8192]{1,0:T(8,128)(2,1)}, bf16[8,8192]{1,0:T(8,128)(2,1)S(1)}, u32[]{:S(2)}, u32[]{:S(2)}) collective-permute-start(bf16[8,8192]{1,0:T(8,128)(2,1)} %bitcast.12), channel_id=1, source_target_pairs={{0,2},{1,5},{2,0},{3,7},{4,6},{5,1},{6,4},{7,3},{8,10},{9,13},{10,... | collective-permute-start | bytes 393224 | tf_op jit(solution)/shard_map/ppermute | solution.py:32
  6.2 4.8 %copy-start.7 = (bf16[1,8,8192]{2,1,0:T(8,128)(2,1)S(1)}, bf16[1,8,8192]{2,1,0:T(8,128)(2,1)}, u32[]{:S(2)}) copy-start(bf16[1,8,8192]{2,1,0:T(8,128)(2,1)} %param.6) | copy-start | bytes 393220
  10.9 5.3 %copy-start = (bf16[256,8192]{1,0:T(8,128)(2,1)}, bf16[256,8192]{1,0:T(8,128)(2,1)S(1)}, u32[]{:S(2)}) copy-start(bf16[256,8192]{1,0:T(8,128)(2,1)S(1)} %get-tuple-element.17.dec_ref) | copy-start | bytes 12582916
  10.9 5.3 %copy-start.3 = (bf16[256,8192]{1,0:T(8,128)(2,1)}, bf16[256,8192]{1,0:T(8,128)(2,1)S(1)}, u32[]{:S(2)}) copy-start(bf16[256,8192]{1,0:T(8,128)(2,1)S(1)} %get-tuple-element.15.dec_ref) | copy-start | bytes 12582916
  11.0 2.1 %copy-start.5 = (s32[1,2,2]{2,1,0:T(2,128)S(1)}, s32[1,2,2]{2,1,0:T(2,128)}, u32[]{:S(2)}) copy-start(s32[1,2,2]{2,1,0:T(2,128)} %param.9) | copy-start | bytes 52
  11.0 2.1 %copy-start.6 = (bf16[1,256]{1,0:T(2,128)(2,1)S(1)}, bf16[1,256]{1,0:T(2,128)(2,1)}, u32[]{:S(2)}) copy-start(bf16[1,256]{1,0:T(2,128)(2,1)} %bias_ref.1) | copy-start | bytes 1540
  11.0 1.6 %collective-permute-start.3 = (bf16[16,8192]{1,0:T(8,128)(2,1)S(1)}, bf16[16,8192]{1,0:T(8,128)(2,1)S(1)}, u32[]{:S(2)}, u32[]{:S(2)}) collective-permute-start(bf16[16,8192]{1,0:T(8,128)(2,1)S(1)} %pad_maximum_fusion.3), channel_id=1, source_target_pairs={{0,1},{1,0},{2,3},{3,2},{4,5},{5,4},{6,7},{7,6},{8,9},{9,8},{10,11... | collective-permute-start | bytes 786440 | tf_op jit(solution)/shard_map/ppermute | solution.py:36
  11.4 1.6 %collective-permute-start.4 = (bf16[16,8192]{1,0:T(8,128)(2,1)S(1)}, bf16[16,8192]{1,0:T(8,128)(2,1)S(1)}, u32[]{:S(2)}, u32[]{:S(2)}) collective-permute-start(bf16[16,8192]{1,0:T(8,128)(2,1)S(1)} %pad_maximum_fusion.4), channel_id=1, source_target_pairs={{0,1},{1,0},{2,3},{3,2},{4,5},{5,4},{6,7},{7,6},{8,9},{9,8},{10,11... | collective-permute-start | bytes 786440 | tf_op jit(solution)/shard_map/ppermute | solution.py:36
  16.2 3.7 %collective-permute-start.8 = (bf16[32,8192]{1,0:T(8,128)(2,1)S(1)}, bf16[32,8192]{1,0:T(8,128)(2,1)S(1)}, u32[]{:S(2)}, u32[]{:S(2)}) collective-permute-start(bf16[32,8192]{1,0:T(8,128)(2,1)S(1)} %get-tuple-element.21), channel_id=1, source_target_pairs={{0,1},{1,0},{2,3},{3,2},{4,5},{5,4},{6,7},{7,6},{8,9},{9,8},{10,11... | collective-permute-start | bytes 1572872 | tf_op jit(solution)/shard_map/ppermute | solution.py:36
  16.5 2.2 %copy-start.1 = (bf16[256,8192]{1,0:T(8,128)(2,1)S(1)}, bf16[256,8192]{1,0:T(8,128)(2,1)}, u32[]{:S(2)}) copy-start(bf16[256,8192]{1,0:T(8,128)(2,1)} %copy-done) | copy-start | bytes 12582916
  19.6 5.6 %collective-permute-start.5 = (bf16[32,8192]{1,0:T(8,128)(2,1)S(1)}, bf16[32,8192]{1,0:T(8,128)(2,1)S(1)}, u32[]{:S(2)}, u32[]{:S(2)}) collective-permute-start(bf16[32,8192]{1,0:T(8,128)(2,1)S(1)} %get-tuple-element.19), channel_id=1, source_target_pairs={{0,1},{1,0},{2,3},{3,2},{4,5},{5,4},{6,7},{7,6},{8,9},{9,8},{10,11... | collective-permute-start | bytes 1572872 | tf_op jit(solution)/shard_map/ppermute | solution.py:36
  20.1 9.7 %collective-permute-start.9 = (bf16[8,8192]{1,0:T(8,128)(2,1)S(1)}, bf16[8,8192]{1,0:T(8,128)(2,1)S(1)}, u32[]{:S(2)}, u32[]{:S(2)}) collective-permute-start(bf16[8,8192]{1,0:T(8,128)(2,1)S(1)} %get-tuple-element.34), channel_id=1, source_target_pairs={{0,8},{1,9},{2,10},{3,11},{4,12},{5,13},{6,14},{7,15},{8,16},{9,17... | collective-permute-start | bytes 393224 | tf_op jit(solution)/shard_map/ppermute | solution.py:41
  22.1 6.2 %collective-permute-start.12 = (bf16[8,8192]{1,0:T(8,128)(2,1)S(1)}, bf16[8,8192]{1,0:T(8,128)(2,1)S(1)}, u32[]{:S(2)}, u32[]{:S(2)}) collective-permute-start(bf16[8,8192]{1,0:T(8,128)(2,1)S(1)} %get-tuple-element.35), channel_id=1, source_target_pairs={{0,4},{1,3},{2,6},{3,1},{4,0},{5,7},{6,2},{7,5},{8,12},{9,11},{10,... | collective-permute-start | bytes 393224 | tf_op jit(solution)/shard_map/ppermute | solution.py:32
  23.6 6.1 %collective-permute-start.11 = (bf16[8,8192]{1,0:T(8,128)(2,1)S(1)}, bf16[8,8192]{1,0:T(8,128)(2,1)S(1)}, u32[]{:S(2)}, u32[]{:S(2)}) collective-permute-start(bf16[8,8192]{1,0:T(8,128)(2,1)S(1)} %get-tuple-element.36), channel_id=1, source_target_pairs={{0,2},{1,5},{2,0},{3,7},{4,6},{5,1},{6,4},{7,3},{8,10},{9,13},{10,... | collective-permute-start | bytes 393224 | tf_op jit(solution)/shard_map/ppermute | solution.py:32
  25.1 12.2 %copy-start.9 = (bf16[1,8,8192]{2,1,0:T(8,128)(2,1)S(1)}, bf16[1,8,8192]{2,1,0:T(8,128)(2,1)}, u32[]{:S(2)}) copy-start(bf16[1,8,8192]{2,1,0:T(8,128)(2,1)} %param.11) | copy-start | bytes 393220
  25.3 7.6 %collective-permute-start.6 = (bf16[8,8192]{1,0:T(8,128)(2,1)S(1)}, bf16[8,8192]{1,0:T(8,128)(2,1)S(1)}, u32[]{:S(2)}, u32[]{:S(2)}) collective-permute-start(bf16[8,8192]{1,0:T(8,128)(2,1)S(1)} %get-tuple-element.32), channel_id=1, source_target_pairs={{0,2},{1,5},{2,0},{3,7},{4,6},{5,1},{6,4},{7,3},{8,10},{9,13},{10,... | collective-permute-start | bytes 393224 | tf_op jit(solution)/shard_map/ppermute | solution.py:32
  25.8 7.0 %collective-permute-start.7 = (bf16[8,8192]{1,0:T(8,128)(2,1)S(1)}, bf16[8,8192]{1,0:T(8,128)(2,1)S(1)}, u32[]{:S(2)}, u32[]{:S(2)}) collective-permute-start(bf16[8,8192]{1,0:T(8,128)(2,1)S(1)} %get-tuple-element.33), channel_id=1, source_target_pairs={{0,4},{1,3},{2,6},{3,1},{4,0},{5,7},{6,2},{7,5},{8,12},{9,11},{10,... | collective-permute-start | bytes 393224 | tf_op jit(solution)/shard_map/ppermute | solution.py:32
  29.8 6.8 %collective-permute-start.13 = (bf16[8,8192]{1,0:T(8,128)(2,1)S(1)}, bf16[8,8192]{1,0:T(8,128)(2,1)S(1)}, u32[]{:S(2)}, u32[]{:S(2)}) collective-permute-start(bf16[8,8192]{1,0:T(8,128)(2,1)S(1)} %fusion.1), channel_id=1, source_target_pairs={{0,8},{1,9},{2,10},{3,11},{4,12},{5,13},{6,14},{7,15},{8,16},{9,17... | collective-permute-start | bytes 393224 | tf_op jit(solution)/shard_map/ppermute | solution.py:41
  31.4 5.9 %collective-permute-start.10 = (bf16[8,8192]{1,0:T(8,128)(2,1)S(1)}, bf16[8,8192]{1,0:T(8,128)(2,1)S(1)}, u32[]{:S(2)}, u32[]{:S(2)}) collective-permute-start(bf16[8,8192]{1,0:T(8,128)(2,1)S(1)} %slice_add_fusion.1), channel_id=1, source_target_pairs={{0,6},{1,7},{2,4},{3,5},{4,2},{5,3},{6,0},{7,1},{8,14},{9,15},{10,... | collective-permute-start | bytes 393224 | tf_op jit(solution)/shard_map/ppermute | solution.py:32
  37.4 15.1 %copy-start.8 = (bf16[8,8192]{1,0:T(8,128)(2,1)}, bf16[8,8192]{1,0:T(8,128)(2,1)S(1)}, u32[]{:S(2)}) copy-start(bf16[8,8192]{1,0:T(8,128)(2,1)S(1)} %get-tuple-element.27) | copy-start | bytes 393220
  37.4 5.8 %collective-permute-start.14 = (bf16[8,8192]{1,0:T(8,128)(2,1)S(1)}, bf16[8,8192]{1,0:T(8,128)(2,1)S(1)}, u32[]{:S(2)}, u32[]{:S(2)}) collective-permute-start(bf16[8,8192]{1,0:T(8,128)(2,1)S(1)} %get-tuple-element.27), channel_id=1, source_target_pairs={{8,0},{9,1},{10,2},{11,3},{12,4},{13,5},{14,6},{15,7},{16,8},{17,9... | collective-permute-start | bytes 393224 | tf_op jit(solution)/shard_map/ppermute | solution.py:47
  39.7 12.8 %copy-start.2 = (bf16[256,8192]{1,0:T(8,128)(2,1)S(1)}, bf16[256,8192]{1,0:T(8,128)(2,1)}, u32[]{:S(2)}) copy-start(bf16[256,8192]{1,0:T(8,128)(2,1)} %copy-done) | copy-start | bytes 12582916
  39.7 7.1 %collective-permute-start.19 = (bf16[8,8192]{1,0:T(8,128)(2,1)S(1)}, bf16[8,8192]{1,0:T(8,128)(2,1)S(1)}, u32[]{:S(2)}, u32[]{:S(2)}) collective-permute-start(bf16[8,8192]{1,0:T(8,128)(2,1)S(1)} %get-tuple-element.27), channel_id=1, source_target_pairs={{0,6},{1,7},{2,4},{3,5},{4,2},{5,3},{6,0},{7,1},{8,14},{9,15},{10,... | collective-permute-start | bytes 393224 | tf_op jit(solution)/shard_map/ppermute | solution.py:32
  41.1 7.4 %collective-permute-start.18 = (bf16[8,8192]{1,0:T(8,128)(2,1)S(1)}, bf16[8,8192]{1,0:T(8,128)(2,1)S(1)}, u32[]{:S(2)}, u32[]{:S(2)}) collective-permute-start(bf16[8,8192]{1,0:T(8,128)(2,1)S(1)} %get-tuple-element.27), channel_id=1, source_target_pairs={{0,4},{1,3},{2,6},{3,1},{4,0},{5,7},{6,2},{7,5},{8,12},{9,11},{10,... | collective-permute-start | bytes 393224 | tf_op jit(solution)/shard_map/ppermute | solution.py:32
  42.3 6.2 %collective-permute-start.17 = (bf16[8,8192]{1,0:T(8,128)(2,1)S(1)}, bf16[8,8192]{1,0:T(8,128)(2,1)S(1)}, u32[]{:S(2)}, u32[]{:S(2)}) collective-permute-start(bf16[8,8192]{1,0:T(8,128)(2,1)S(1)} %get-tuple-element.27), channel_id=1, source_target_pairs={{0,2},{1,5},{2,0},{3,7},{4,6},{5,1},{6,4},{7,3},{8,10},{9,13},{10,... | collective-permute-start | bytes 393224 | tf_op jit(solution)/shard_map/ppermute | solution.py:32
  43.2 8.7 %collective-permute-start.16 = (bf16[8,8192]{1,0:T(8,128)(2,1)S(1)}, bf16[8,8192]{1,0:T(8,128)(2,1)S(1)}, u32[]{:S(2)}, u32[]{:S(2)}) collective-permute-start(bf16[8,8192]{1,0:T(8,128)(2,1)S(1)} %broadcast_select_fusion.1), channel_id=1, source_target_pairs={{0,4},{1,3},{2,6},{3,1},{4,0},{5,7},{6,2},{7,5},{8,12},{9,11},{10,... | collective-permute-start | bytes 393224 | tf_op jit(solution)/shard_map/ppermute | solution.py:32
  43.8 8.1 %collective-permute-start.15 = (bf16[8,8192]{1,0:T(8,128)(2,1)S(1)}, bf16[8,8192]{1,0:T(8,128)(2,1)S(1)}, u32[]{:S(2)}, u32[]{:S(2)}) collective-permute-start(bf16[8,8192]{1,0:T(8,128)(2,1)S(1)} %broadcast_select_fusion.1), channel_id=1, source_target_pairs={{0,2},{1,5},{2,0},{3,7},{4,6},{5,1},{6,4},{7,3},{8,10},{9,13},{10,... | collective-permute-start | bytes 393224 | tf_op jit(solution)/shard_map/ppermute | solution.py:32
  46.8 5.0 %collective-permute-start.21 = (bf16[8,8192]{1,0:T(8,128)(2,1)S(1)}, bf16[8,8192]{1,0:T(8,128)(2,1)S(1)}, u32[]{:S(2)}, u32[]{:S(2)}) collective-permute-start(bf16[8,8192]{1,0:T(8,128)(2,1)S(1)} %collective-permute-done.19), channel_id=1, source_target_pairs={{8,0},{9,1},{10,2},{11,3},{12,4},{13,5},{14,6},{15,7},{16,8},{17,9... | collective-permute-start | bytes 393224 | tf_op jit(solution)/shard_map/ppermute | solution.py:47
  48.6 3.4 %collective-permute-start.20 = (bf16[32,8192]{1,0:T(8,128)(2,1)S(1)}, bf16[32,8192]{1,0:T(8,128)(2,1)S(1)}, u32[]{:S(2)}, u32[]{:S(2)}) collective-permute-start(bf16[32,8192]{1,0:T(8,128)(2,1)S(1)} %pad_maximum_fusion.1), channel_id=1, source_target_pairs={{0,1},{1,0},{2,3},{3,2},{4,5},{5,4},{6,7},{7,6},{8,9},{9,8},{10,11... | collective-permute-start | bytes 1572872 | tf_op jit(solution)/shard_map/ppermute | solution.py:36
  51.8 2.2 %collective-permute-start.23 = (bf16[8,8192]{1,0:T(8,128)(2,1)S(1)}, bf16[8,8192]{1,0:T(8,128)(2,1)S(1)}, u32[]{:S(2)}, u32[]{:S(2)}) collective-permute-start(bf16[8,8192]{1,0:T(8,128)(2,1)S(1)} %broadcast_select_fusion), channel_id=1, source_target_pairs={{0,1},{1,0},{2,3},{3,2},{4,5},{5,4},{6,7},{7,6},{8,9},{9,8},{10,11... | collective-permute-start | bytes 393224 | tf_op jit(solution)/shard_map/ppermute | solution.py:36
  52.0 2.0 %collective-permute-start.22 = (bf16[24,8192]{1,0:T(8,128)(2,1)S(1)}, bf16[24,8192]{1,0:T(8,128)(2,1)S(1)}, u32[]{:S(2)}, u32[]{:S(2)}) collective-permute-start(bf16[24,8192]{1,0:T(8,128)(2,1)S(1)} %pad_maximum_fusion.2), channel_id=1, source_target_pairs={{0,1},{1,0},{2,3},{3,2},{4,5},{5,4},{6,7},{7,6},{8,9},{9,8},{10,11... | collective-permute-start | bytes 1179656 | tf_op jit(solution)/shard_map/ppermute | solution.py:36
  52.6 2.2 %copy-start.4 = (bf16[256,8192]{1,0:T(8,128)(2,1)S(1)}, bf16[256,8192]{1,0:T(8,128)(2,1)}, u32[]{:S(2)}) copy-start(bf16[256,8192]{1,0:T(8,128)(2,1)} %copy-done.3) | copy-start | bytes 12582916

commit v12 on v11

--- a/solution.py
+++ b/solution.py
@@ -13,12 +13,10 @@
 CORES = 2
 CHUNK = 1024
 LIMIT = 4 << 20
-HIGH = 28 << 20
 AXIS = "layer"
 
 ANY_SPEC = pl.BlockSpec(memory_space=pl.ANY)
 VMEM_SPEC = pl.BlockSpec(memory_space=pltpu.VMEM)
-SMEM_SPEC = pl.BlockSpec(memory_space=pltpu.SMEM)
 
 
 def turned(chip, chips):
@@ -36,16 +34,16 @@
     return lax.ppermute(value, AXIS, [(i, i ^ 1) for i in range(lax.axis_size(AXIS))])
 
 
-def raised(value, layer, group):
+def raised(value, first, group):
     size = lax.axis_size(AXIS)
     came = lax.ppermute(value, AXIS, [(i, (i + group) % size) for i in range(size)])
-    return jnp.where(layer == 0, jnp.zeros_like(came), came)
-
-
-def lowered(value, layer, group):
+    return jnp.where(first, jnp.zeros_like(came), came)
+
+
+def lowered(value, final, group):
     size = lax.axis_size(AXIS)
     came = lax.ppermute(value, AXIS, [((i + group) % size, i) for i in range(size)])
-    return jnp.where(layer == LAYERS - 1, jnp.zeros_like(came), came)
+    return jnp.where(final, jnp.zeros_like(came), came)
 
 
 def after(values, done):
@@ -87,7 +85,7 @@
         in_specs=[ANY_SPEC] * 2,
         out_specs=[VMEM_SPEC] * 3,
         scratch_shapes=[pltpu.SemaphoreType.DMA((3,))],
-        compiler_params=kernel_params(HIGH),
+        compiler_params=kernel_params(1 << 20),
         cost_estimate=pl.CostEstimate(flops=0, bytes_accessed=4 * (enc.size + dec.size), transcendentals=0),
         name="load_weights",
     )(*in_hbm(enc, dec))
@@ -102,27 +100,38 @@
         far_ref[:, columns] = part[half:].astype(jnp.bfloat16)
 
 
-def gate_of(place, active_ref, rows, tokens):
+def place_in(group):
+    return lax.axis_index(AXIS) & (group - 1)
+
+
+def summed_over(depth, product):
+    sums = [None, None]
+    for step in range(depth // CHUNK):
+        part = product(pl.ds(step * CHUNK, CHUNK))
+        so_far = sums[step % 2]
+        sums[step % 2] = part if so_far is None else so_far + part
+    return sums[0] + sums[1]
+
+
+def gate_of(active_ref, rows, tokens):
     group = rows // tokens
     block = lax.broadcasted_iota(jnp.int32, (rows, BLOCK), 0) // tokens
-    tile = (slab_of(place, block, group // CORES) * tokens) // TILE
+    tile = (slab_of(place_in(group), block, group // CORES) * tokens) // TILE
     parts = []
     for part in range(active_ref.shape[1]):
         live = jnp.zeros((rows, BLOCK), jnp.int32)
         for i in range(active_ref.shape[0]):
-            live = jnp.where(tile == i, active_ref[i, part], live)
+            live = jnp.where(tile == i, active_ref[pl.ds(i, 1), pl.ds(part, 1)], live)
         parts.append(live.astype(jnp.float32))
     return jnp.concatenate(parts, axis=1)
 
 
-def encode_kernel(tokens, place_ref, active_ref, x_ref, enc_ref, bias_ref, dec_ref, codes_ref, near_ref, far_ref):
+def encode_kernel(tokens, active_ref, x_ref, enc_ref, bias_ref, dec_ref, codes_ref, near_ref, far_ref):
     rows, depth = x_ref.shape
-    half = depth // 2
-    pre = bias_ref[...].astype(jnp.float32) + sum(
-        jnp.dot(x_ref[:, part], enc_ref[part, :], preferred_element_type=jnp.float32)
-        for part in (pl.ds(0, half), pl.ds(half, half))
-    )
-    codes = jnp.maximum(pre, 0.0) * gate_of(place_ref[0], active_ref, rows, tokens)
+    pre = bias_ref[...].astype(jnp.float32) + summed_over(
+        depth, lambda part: jnp.dot(x_ref[:, part], enc_ref[part, :], preferred_element_type=jnp.float32)
+    )
+    codes = jnp.maximum(pre, 0.0) * gate_of(active_ref, rows, tokens)
     codes_ref[...] = codes.astype(jnp.bfloat16)
     decode(codes_ref[...], dec_ref, near_ref, far_ref)
 
@@ -135,18 +144,18 @@
     return [pltpu.VMEM((rows // CORES, width), jnp.float32), pltpu.VMEM((rows // CORES, width), jnp.bfloat16)]
 
 
-def encoded(place, active, x, enc, bias, dec, tokens):
+def encoded(active, x, enc, bias, dec, tokens):
     rows, depth = x.shape
     features = enc.shape[1]
     return pl.pallas_call(
         functools.partial(encode_kernel, tokens),
         out_shape=[pltpu.VMEM((rows, features), jnp.bfloat16)] + halves_of(rows, depth),
-        in_specs=[SMEM_SPEC, SMEM_SPEC] + [VMEM_SPEC] * 4,
+        in_specs=[VMEM_SPEC] * 5,
         out_specs=[VMEM_SPEC] * 3,
         compiler_params=kernel_params(),
         cost_estimate=pl.CostEstimate(flops=4 * rows * depth * features, bytes_accessed=4 * depth * features, transcendentals=0),
         name="encode",
-    )(place, active, *in_vmem(x, enc, bias, dec))
+    )(*in_vmem(active, x, enc, bias, dec))
 
 
 def decoded(codes, dec):
@@ -164,12 +173,11 @@
 
 
 def back(rows_ref, dec_ref):
-    half = rows_ref.shape[1] // 2
-    return sum(
-        lax.dot_general(
+    return summed_over(
+        rows_ref.shape[1],
+        lambda part: lax.dot_general(
             rows_ref[:, part], dec_ref[:, part], (((1,), (1,)), ((), ())), preferred_element_type=jnp.float32
-        )
-        for part in (pl.ds(0, half), pl.ds(half, half))
+        ),
     )
 
 
@@ -177,11 +185,11 @@
     out_ref[...] = back(rows_ref, dec_ref)
 
 
-def grad_all_kernel(tokens, place_ref, rows_ref, dec_ref, own_ref, out_ref):
+def grad_all_kernel(tokens, rows_ref, dec_ref, own_ref, out_ref):
     total = own_ref[...] + back(rows_ref, dec_ref)
     group = total.shape[0] // tokens
     for block in range(group):
-        slab = slab_of(place_ref[0], block, group // CORES)
+        slab = slab_of(place_in(group), block, group // CORES)
         where = pl.ds(pl.multiple_of(slab * tokens, tokens), tokens)
         out_ref[0, where, :] = total[block * tokens : (block + 1) * tokens]
 
@@ -199,16 +207,16 @@
     )(*in_vmem(rows, dec))[0]
 
 
-def grad_all(place, rows, dec, own, tokens):
+def grad_all(rows, dec, own, tokens):
     return pl.pallas_call(
         functools.partial(grad_all_kernel, tokens),
         out_shape=jax.ShapeDtypeStruct((1,) + own.shape, jnp.float32),
-        in_specs=[SMEM_SPEC] + [VMEM_SPEC] * 3,
+        in_specs=[VMEM_SPEC] * 3,
         out_specs=VMEM_SPEC,
         compiler_params=kernel_params(),
         cost_estimate=pl.CostEstimate(flops=2 * rows.size * own.shape[1], bytes_accessed=2 * dec.size, transcendentals=0),
         name="grad_all",
-    )(place, *in_vmem(rows, dec, own))
+    )(*in_vmem(rows, dec, own))
 
 
 def blocks_of(near, far, chips):
@@ -228,39 +236,37 @@
     group = lax.axis_size(AXIS) // LAYERS
     chips = group // CORES
     index = lax.axis_index(AXIS)
-    layer = index // group
-    place = (index % group).astype(jnp.int32).reshape(1)
+    slab, first, final = lax.optimization_barrier((resid[0], index < group, index >= (LAYERS - 1) * group))
     tokens = resid.shape[1]
     enc, own_dec, next_dec = loaded(enc_weight, dec_weight)
-    slab = resid[0]
     most, last = [across(slab, chip, chips) for chip in range(1, chips - 1)], across(slab, chips - 1, chips)
     early, late = jnp.concatenate([slab, last], axis=0), jnp.concatenate(most, axis=0)
     early_far, late_far = other_core(early), other_core(late)
     x = jnp.concatenate(
         [slab, late, last, early_far[:tokens], late_far, early_far[tokens:]], axis=0
     )
-    codes, next_near, next_far = encoded(place, active[0], x, enc, enc_bias, next_dec, tokens)
+    codes, next_near, next_far = encoded(active[0], x, enc, enc_bias, next_dec, tokens)
     own_near, own_far = decoded(codes, own_dec)
 
     nexts = blocks_of(next_near, next_far, chips)
     owns = blocks_of(own_near, own_far, chips)
-    risen = raised(nexts[-1].astype(jnp.bfloat16), layer, group)
+    risen = raised(nexts[-1].astype(jnp.bfloat16), first, group)
     owns[-1] = owns[-1] + risen.astype(jnp.float32)
     next_sum = after(summed(nexts, range(1, chips - 1)).astype(jnp.bfloat16), owns[-1])
-    from_before = raised(next_sum, layer, group).astype(jnp.float32)
+    from_before = raised(next_sum, first, group).astype(jnp.float32)
     own_sum = summed(owns, range(1, chips))
     error = (own_sum + from_before - target[0].astype(jnp.float32)).astype(jnp.bfloat16)
 
-    later = lowered(error, layer, group)
+    later = lowered(error, final, group)
     heres = [error] + [across(error, chip, chips) for chip in range(1, chips)]
     afters = [later] + [across(later, chip, chips) for chip in range(1, chips - 1)]
-    last = lowered(after(heres[-1], later), layer, group)
+    last = lowered(after(heres[-1], later), final, group)
     here_near = jnp.concatenate(heres, axis=0)
     here_far = other_core(here_near)
     here_rows = jnp.concatenate([here_near, here_far], axis=0)
     most = after(jnp.concatenate(afters, axis=0), here_far)
     after_rows = jnp.concatenate([most, last, other_core(most), other_core(last)], axis=0)
-    grad = grad_all(place, after_rows, next_dec, grad_own(here_rows, own_dec), tokens)
+    grad = grad_all(after_rows, next_dec, grad_own(here_rows, own_dec), tokens)
     return (error[None], grad)
 
 

time: 57 us -> 54 us (0.947)
  local copies, waits for them, and re-layouts: 4.04 us -> 1.16 us
    unnamed x29 -> x19, local copies, waits for them, and re-layouts: 3.95 us -> 1.07 us
  transfers between devices with their start and end apart: 24 -> 24, of which waited for: 9 -> 10; matrix products, arithmetic and copies ran while one was open for 3% -> 3% of each run, Pallas kernels for 12% -> 13%
where the time goes in v12:
time: 54 us; the launch traced here: 53.8 us
  starting transfers between devices  24.8 us (46%)
  waiting for transfers between devices  14.6 us (27%)
  Pallas kernels  11.6 us (21%)
  local copies, waits for them, and re-layouts  1.16 us (2%)
  between operations  0.97 us (2%)
  other arithmetic  0.62 us (1%)
    ppermute x13, starting transfers between devices, across(): return lax.ppermute(value, AXIS, pairs)  15.6 us
    ppermute x13, waiting for transfers between devices, across(): return lax.ppermute(value, AXIS, pairs)  5.92 us
    pallas_call x1, Pallas kernels, loaded(): pl.pallas_call(load_kernel, out_shape=[pltpu.VMEM(enc.shape[1:], enc.dtyp...  4.72 us
    ppermute x2, starting transfers between devices, lowered(): lax.ppermute(value, AXIS, [((i + group) % size, i) for i in range(size)])  3.95 us
    ppermute x2, waiting for transfers between devices, raised(): lax.ppermute(value, AXIS, [(i, (i + group) % size) for i in range(size)])  3.82 us
    ppermute x2, starting transfers between devices, raised(): lax.ppermute(value, AXIS, [(i, (i + group) % size) for i in range(size)])  3.64 us
    ppermute x2, waiting for transfers between devices, lowered(): lax.ppermute(value, AXIS, [((i + group) % size, i) for i in range(size)])  3.14 us
    pallas_call x1, Pallas kernels, encoded(): pl.pallas_call(functools.partial(encode_kernel, tokens), out_shape=[pltpu...  2.6 us
  transfers between devices with their start and end apart: 24, of which 10 were waited for; matrix products, arithmetic and copies ran while one was open for 3% of the time, Pallas kernels for 13%

profile of v12, /device:TPU:0, one launch (start us, length us, event | category | flops | bytes accessed | tf_op | source)
XLA Modules:
  0.0 53.8 jit_solution(1654830419143482496)
XLA Ops:
  0.6 4.0 %collective-permute-start.2 = (bf16[8,8192]{1,0:T(8,128)(2,1)}, bf16[8,8192]{1,0:T(8,128)(2,1)S(1)}, u32[]{:S(2)}, u32[]{:S(2)}) collective-permute-start(bf16[8,8192]{1,0:T(8,128)(2,1)} %bitcast.8), channel_id=1, source_target_pairs={{0,6},{1,7},{2,4},{3,5},{4,2},{5,3},{6,0},{7,1},{8,14},{9,15},{10,... | collective-permute-start | bytes 393224 | tf_op jit(solution)/shard_map/ppermute | solution.py:30
  4.6 0.5 collective-permute-start.1
  5.1 0.1 collective-permute-start
  5.2 0.9 %constant_dynamic-update-slice_fusion.4 = bf16[64,8192]{1,0:T(8,128)(2,1)S(1)} fusion(bf16[8,8192]{1,0:T(8,128)(2,1)} %bitcast.11), kind=kLoop, calls=%fused_computation.25 | loop fusion | bytes 262144
  6.2 0.0 copy-start.2
  6.2 4.7 %load_weights.1 = (bf16[8192,256]{1,0:T(8,128)(2,1)S(1)}, bf16[256,8192]{1,0:T(8,128)(2,1)S(1)}, bf16[256,8192]{1,0:T(8,128)(2,1)S(1)}) custom-call(bf16[1,8192,256]{2,1,0:T(8,128)(2,1)} %enc_hbm.1, bf16[1,2,256,8192]{3,2,1,0:T(8,128)(2,1)} %dec_hbm.1), custom_call_target="tpu_custom_call" | custom-call | bytes 25165824 | tf_op jit(solution)/shard_map/load_weights/pallas_call | solution.py:82
  10.9 0.0 copy-start
  10.9 0.0 copy-start.1
  11.0 0.0 collective-permute-done.2
  11.0 0.0 copy-done.2
  11.0 0.1 collective-permute-start.3
  11.1 0.0 collective-permute-done.1
  11.1 0.2 collective-permute-done
  11.4 0.3 collective-permute-start.4
  11.7 0.9 %collective-permute-done.3 = bf16[16,8192]{1,0:T(8,128)(2,1)S(1)} collective-permute-done((bf16[16,8192]{1,0:T(8,128)(2,1)S(1)}, bf16[16,8192]{1,0:T(8,128)(2,1)S(1)}, u32[]{:S(2)}, u32[]{:S(2)}) %collective-permute-start.3) | collective-permute-done | bytes 262176 | tf_op jit(solution)/shard_map/ppermute | solution.py:34
  12.6 0.4 collective-permute-done.4
  13.0 0.0 copy-done
  13.0 2.6 %encode.1 = (bf16[64,256]{1,0:T(8,128)(2,1)S(1)}, f32[32,8192]{1,0:T(8,128)S(1)}, bf16[32,8192]{1,0:T(8,128)(2,1)S(1)}) custom-call(s32[2,2]{1,0:T(2,128)S(1)} %bitcast.7, bf16[64,8192]{1,0:T(8,128)(2,1)S(1)} %slice_dynamic-update-slice_fusion.x_ref, bf16[8192,256]{1,0:T(8,128)(2,1)S(1)} %get-tuple-element.18.enc_ref, bf16[1,256]{1,0:T(2,128)(2,1)S(1)} %copy-done.1, ...), custom_call_target="tpu_custom_call" | custom-call | flops 536870912 | bytes 8388608 | tf_op jit(solution)/shard_map/encode/pallas_call | solution.py:150
  15.7 0.3 collective-permute-start.8
  15.9 0.9 %decode_own.1 = (f32[32,8192]{1,0:T(8,128)S(1)}, bf16[32,8192]{1,0:T(8,128)(2,1)S(1)}) custom-call(bf16[64,256]{1,0:T(8,128)(2,1)S(1)} %get-tuple-element.20.codes_ref, bf16[256,8192]{1,0:T(8,128)(2,1)S(1)} %get-tuple-element.21.dec_ref), custom_call_target="tpu_custom_call" | custom-call | flops 268435456 | bytes 4194304 | tf_op jit(solution)/shard_map/decode_own/pallas_call | solution.py:164
  16.8 0.4 collective-permute-start.5
  17.2 0.5 collective-permute-done.8
  17.6 0.1 fusion.9
  17.8 2.0 %collective-permute-start.9 = (bf16[8,8192]{1,0:T(8,128)(2,1)S(1)}, bf16[8,8192]{1,0:T(8,128)(2,1)S(1)}, u32[]{:S(2)}, u32[]{:S(2)}) collective-permute-start(bf16[8,8192]{1,0:T(8,128)(2,1)S(1)} %get-tuple-element.40), channel_id=1, source_target_pairs={{0,8},{1,9},{2,10},{3,11},{4,12},{5,13},{6,14},{7,15},{8,16},{9,17... | collective-permute-start | bytes 393224 | tf_op jit(solution)/shard_map/ppermute | solution.py:39
  19.8 1.5 %collective-permute-start.12 = (bf16[8,8192]{1,0:T(8,128)(2,1)S(1)}, bf16[8,8192]{1,0:T(8,128)(2,1)S(1)}, u32[]{:S(2)}, u32[]{:S(2)}) collective-permute-start(bf16[8,8192]{1,0:T(8,128)(2,1)S(1)} %get-tuple-element.41), channel_id=1, source_target_pairs={{0,4},{1,3},{2,6},{3,1},{4,0},{5,7},{6,2},{7,5},{8,12},{9,11},{10,... | collective-permute-start | bytes 393224 | tf_op jit(solution)/shard_map/ppermute | solution.py:30
  21.3 1.5 %collective-permute-start.11 = (bf16[8,8192]{1,0:T(8,128)(2,1)S(1)}, bf16[8,8192]{1,0:T(8,128)(2,1)S(1)}, u32[]{:S(2)}, u32[]{:S(2)}) collective-permute-start(bf16[8,8192]{1,0:T(8,128)(2,1)S(1)} %get-tuple-element.42), channel_id=1, source_target_pairs={{0,2},{1,5},{2,0},{3,7},{4,6},{5,1},{6,4},{7,3},{8,10},{9,13},{10,... | collective-permute-start | bytes 393224 | tf_op jit(solution)/shard_map/ppermute | solution.py:30
  22.8 0.0 collective-permute-done.5
  22.8 0.1 fusion.8
  23.0 0.6 %collective-permute-start.6 = (bf16[8,8192]{1,0:T(8,128)(2,1)S(1)}, bf16[8,8192]{1,0:T(8,128)(2,1)S(1)}, u32[]{:S(2)}, u32[]{:S(2)}) collective-permute-start(bf16[8,8192]{1,0:T(8,128)(2,1)S(1)} %get-tuple-element.38), channel_id=1, source_target_pairs={{0,2},{1,5},{2,0},{3,7},{4,6},{5,1},{6,4},{7,3},{8,10},{9,13},{10,... | collective-permute-start | bytes 393224 | tf_op jit(solution)/shard_map/ppermute | solution.py:30
  23.6 0.5 collective-permute-start.7
  24.1 1.9 %collective-permute-done.12 = bf16[8,8192]{1,0:T(8,128)(2,1)S(1)} collective-permute-done((bf16[8,8192]{1,0:T(8,128)(2,1)S(1)}, bf16[8,8192]{1,0:T(8,128)(2,1)S(1)}, u32[]{:S(2)}, u32[]{:S(2)}) %collective-permute-start.12) | collective-permute-done | bytes 131104 | tf_op jit(solution)/shard_map/ppermute | solution.py:30
  26.0 1.4 %collective-permute-done.11 = bf16[8,8192]{1,0:T(8,128)(2,1)S(1)} collective-permute-done((bf16[8,8192]{1,0:T(8,128)(2,1)S(1)}, bf16[8,8192]{1,0:T(8,128)(2,1)S(1)}, u32[]{:S(2)}, u32[]{:S(2)}) %collective-permute-start.11) | collective-permute-done | bytes 131104 | tf_op jit(solution)/shard_map/ppermute | solution.py:30
  27.5 0.0 collective-permute-done.9
  27.5 1.6 %collective-permute-start.13 = (bf16[8,8192]{1,0:T(8,128)(2,1)S(1)}, bf16[8,8192]{1,0:T(8,128)(2,1)S(1)}, u32[]{:S(2)}, u32[]{:S(2)}) collective-permute-start(bf16[8,8192]{1,0:T(8,128)(2,1)S(1)} %fusion.1), channel_id=1, source_target_pairs={{0,8},{1,9},{2,10},{3,11},{4,12},{5,13},{6,14},{7,15},{8,16},{9,17... | collective-permute-start | bytes 393224 | tf_op jit(solution)/shard_map/ppermute | solution.py:39
  29.1 1.4 %collective-permute-start.10 = (bf16[8,8192]{1,0:T(8,128)(2,1)S(1)}, bf16[8,8192]{1,0:T(8,128)(2,1)S(1)}, u32[]{:S(2)}, u32[]{:S(2)}) collective-permute-start(bf16[8,8192]{1,0:T(8,128)(2,1)S(1)} %slice_add_fusion.1), channel_id=1, source_target_pairs={{0,6},{1,7},{2,4},{3,5},{4,2},{5,3},{6,0},{7,1},{8,14},{9,15},{10,... | collective-permute-start | bytes 393224 | tf_op jit(solution)/shard_map/ppermute | solution.py:30
  30.5 0.0 collective-permute-done.6
  30.5 0.0 collective-permute-done.7
  30.5 3.8 %collective-permute-done.13 = bf16[8,8192]{1,0:T(8,128)(2,1)S(1)} collective-permute-done((bf16[8,8192]{1,0:T(8,128)(2,1)S(1)}, bf16[8,8192]{1,0:T(8,128)(2,1)S(1)}, u32[]{:S(2)}, u32[]{:S(2)}) %collective-permute-start.13) | collective-permute-done | bytes 131104 | tf_op jit(solution)/shard_map/ppermute | solution.py:39
  34.3 0.7 %collective-permute-done.10 = bf16[8,8192]{1,0:T(8,128)(2,1)S(1)} collective-permute-done((bf16[8,8192]{1,0:T(8,128)(2,1)S(1)}, bf16[8,8192]{1,0:T(8,128)(2,1)S(1)}, u32[]{:S(2)}, u32[]{:S(2)}) %collective-permute-start.10) | collective-permute-done | bytes 131104 | tf_op jit(solution)/shard_map/ppermute | solution.py:30
  35.0 0.1 constant_dynamic-update-slice_fusion.9
  35.1 0.0 copy-start.3
  35.1 2.3 %collective-permute-start.14 = (bf16[8,8192]{1,0:T(8,128)(2,1)S(1)}, bf16[8,8192]{1,0:T(8,128)(2,1)S(1)}, u32[]{:S(2)}, u32[]{:S(2)}) collective-permute-start(bf16[8,8192]{1,0:T(8,128)(2,1)S(1)} %get-tuple-element.33), channel_id=1, source_target_pairs={{8,0},{9,1},{10,2},{11,3},{12,4},{13,5},{14,6},{15,7},{16,8},{17,9... | collective-permute-start | bytes 393224 | tf_op jit(solution)/shard_map/ppermute | solution.py:45
  37.4 1.4 %collective-permute-start.19 = (bf16[8,8192]{1,0:T(8,128)(2,1)S(1)}, bf16[8,8192]{1,0:T(8,128)(2,1)S(1)}, u32[]{:S(2)}, u32[]{:S(2)}) collective-permute-start(bf16[8,8192]{1,0:T(8,128)(2,1)S(1)} %get-tuple-element.33), channel_id=1, source_target_pairs={{0,6},{1,7},{2,4},{3,5},{4,2},{5,3},{6,0},{7,1},{8,14},{9,15},{10,... | collective-permute-start | bytes 393224 | tf_op jit(solution)/shard_map/ppermute | solution.py:30
  38.8 1.3 %collective-permute-start.18 = (bf16[8,8192]{1,0:T(8,128)(2,1)S(1)}, bf16[8,8192]{1,0:T(8,128)(2,1)S(1)}, u32[]{:S(2)}, u32[]{:S(2)}) collective-permute-start(bf16[8,8192]{1,0:T(8,128)(2,1)S(1)} %get-tuple-element.33), channel_id=1, source_target_pairs={{0,4},{1,3},{2,6},{3,1},{4,0},{5,7},{6,2},{7,5},{8,12},{9,11},{10,... | collective-permute-start | bytes 393224 | tf_op jit(solution)/shard_map/ppermute | solution.py:30
  40.1 0.8 %collective-permute-start.17 = (bf16[8,8192]{1,0:T(8,128)(2,1)S(1)}, bf16[8,8192]{1,0:T(8,128)(2,1)S(1)}, u32[]{:S(2)}, u32[]{:S(2)}) collective-permute-start(bf16[8,8192]{1,0:T(8,128)(2,1)S(1)} %get-tuple-element.33), channel_id=1, source_target_pairs={{0,2},{1,5},{2,0},{3,7},{4,6},{5,1},{6,4},{7,3},{8,10},{9,13},{10,... | collective-permute-start | bytes 393224 | tf_op jit(solution)/shard_map/ppermute | solution.py:30
  40.9 0.0 collective-permute-done.14
  40.9 0.6 %collective-permute-start.16 = (bf16[8,8192]{1,0:T(8,128)(2,1)S(1)}, bf16[8,8192]{1,0:T(8,128)(2,1)S(1)}, u32[]{:S(2)}, u32[]{:S(2)}) collective-permute-start(bf16[8,8192]{1,0:T(8,128)(2,1)S(1)} %broadcast_select_fusion.1), channel_id=1, source_target_pairs={{0,4},{1,3},{2,6},{3,1},{4,0},{5,7},{6,2},{7,5},{8,12},{9,11},{10,... | collective-permute-start | bytes 393224 | tf_op jit(solution)/shard_map/ppermute | solution.py:30
  41.6 1.4 %collective-permute-start.15 = (bf16[8,8192]{1,0:T(8,128)(2,1)S(1)}, bf16[8,8192]{1,0:T(8,128)(2,1)S(1)}, u32[]{:S(2)}, u32[]{:S(2)}) collective-permute-start(bf16[8,8192]{1,0:T(8,128)(2,1)S(1)} %broadcast_select_fusion.1), channel_id=1, source_target_pairs={{0,2},{1,5},{2,0},{3,7},{4,6},{5,1},{6,4},{7,3},{8,10},{9,13},{10,... | collective-permute-start | bytes 393224 | tf_op jit(solution)/shard_map/ppermute | solution.py:30
  42.9 1.6 %collective-permute-done.19 = bf16[8,8192]{1,0:T(8,128)(2,1)S(1)} collective-permute-done((bf16[8,8192]{1,0:T(8,128)(2,1)S(1)}, bf16[8,8192]{1,0:T(8,128)(2,1)S(1)}, u32[]{:S(2)}, u32[]{:S(2)}) %collective-permute-start.19) | collective-permute-done | bytes 131104 | tf_op jit(solution)/shard_map/ppermute | solution.py:30
  44.6 1.6 %collective-permute-start.21 = (bf16[8,8192]{1,0:T(8,128)(2,1)S(1)}, bf16[8,8192]{1,0:T(8,128)(2,1)S(1)}, u32[]{:S(2)}, u32[]{:S(2)}) collective-permute-start(bf16[8,8192]{1,0:T(8,128)(2,1)S(1)} %collective-permute-done.19), channel_id=1, source_target_pairs={{8,0},{9,1},{10,2},{11,3},{12,4},{13,5},{14,6},{15,7},{16,8},{17,9... | collective-permute-start | bytes 393224 | tf_op jit(solution)/shard_map/ppermute | solution.py:45
  46.2 0.0 collective-permute-done.18
  46.2 0.0 collective-permute-done.17
  46.3 0.1 collective-permute-start.20
  46.4 3.1 %collective-permute-done.21 = bf16[8,8192]{1,0:T(8,128)(2,1)S(1)} collective-permute-done((bf16[8,8192]{1,0:T(8,128)(2,1)S(1)}, bf16[8,8192]{1,0:T(8,128)(2,1)S(1)}, u32[]{:S(2)}, u32[]{:S(2)}) %collective-permute-start.21) | collective-permute-done | bytes 131104 | tf_op jit(solution)/shard_map/ppermute | solution.py:45
  49.5 0.1 collective-permute-start.23
  49.6 0.0 collective-permute-done.16
  49.6 0.0 collective-permute-done.15
  49.7 0.0 collective-permute-done.20
  49.7 0.5 %collective-permute-start.22 = (bf16[24,8192]{1,0:T(8,128)(2,1)S(1)}, bf16[24,8192]{1,0:T(8,128)(2,1)S(1)}, u32[]{:S(2)}, u32[]{:S(2)}) collective-permute-start(bf16[24,8192]{1,0:T(8,128)(2,1)S(1)} %pad_maximum_fusion.2), channel_id=1, source_target_pairs={{0,1},{1,0},{2,3},{3,2},{4,5},{5,4},{6,7},{7,6},{8,9},{9,8},{10,11... | collective-permute-start | bytes 1179656 | tf_op jit(solution)/shard_map/ppermute | solution.py:34
  50.3 1.4 %grad_own.1 = (f32[64,256]{1,0:T(8,128)S(1)}, f32[8,128]{1,0:T(8,128)}) custom-call(bf16[64,8192]{1,0:T(8,128)(2,1)S(1)} %constant_dynamic-update-slice_fusion.5.rows_ref, bf16[256,8192]{1,0:T(8,128)(2,1)S(1)} %get-tuple-element.21.dec_ref), custom_call_target="tpu_custom_call" | custom-call | flops 268435456 | bytes 4194304 | tf_op jit(solution)/shard_map/grad_own/pallas_call | solution.py:199
  51.7 0.0 collective-permute-done.23
  51.7 0.0 collective-permute-done.22
  51.7 0.1 pad_maximum_fusion.rows_ref
  51.8 2.0 %grad_all.1 = f32[1,64,256]{2,1,0:T(8,128)} custom-call(bf16[64,8192]{1,0:T(8,128)(2,1)S(1)} %pad_maximum_fusion.rows_ref, bf16[256,8192]{1,0:T(8,128)(2,1)S(1)} %get-tuple-element.19.dec_ref, f32[64,256]{1,0:T(8,128)S(1)} %get-tuple-element.31.own_ref), custom_call_target="tpu_custom_call" | custom-call | flops 268435456 | bytes 4194304 | tf_op jit(solution)/shard_map/grad_all/pallas_call | solution.py:211
  (24 shorter events, 0.4 us)
Async XLA Ops:
  0.6 10.3 %collective-permute-start.2 = (bf16[8,8192]{1,0:T(8,128)(2,1)}, bf16[8,8192]{1,0:T(8,128)(2,1)S(1)}, u32[]{:S(2)}, u32[]{:S(2)}) collective-permute-start(bf16[8,8192]{1,0:T(8,128)(2,1)} %bitcast.8), channel_id=1, source_target_pairs={{0,6},{1,7},{2,4},{3,5},{4,2},{5,3},{6,0},{7,1},{8,14},{9,15},{10,... | collective-permute-start | bytes 393224 | tf_op jit(solution)/shard_map/ppermute | solution.py:30
  4.6 6.5 %collective-permute-start.1 = (bf16[8,8192]{1,0:T(8,128)(2,1)}, bf16[8,8192]{1,0:T(8,128)(2,1)S(1)}, u32[]{:S(2)}, u32[]{:S(2)}) collective-permute-start(bf16[8,8192]{1,0:T(8,128)(2,1)} %bitcast.9), channel_id=1, source_target_pairs={{0,4},{1,3},{2,6},{3,1},{4,0},{5,7},{6,2},{7,5},{8,12},{9,11},{10,... | collective-permute-start | bytes 393224 | tf_op jit(solution)/shard_map/ppermute | solution.py:30
  5.1 6.3 %collective-permute-start = (bf16[8,8192]{1,0:T(8,128)(2,1)}, bf16[8,8192]{1,0:T(8,128)(2,1)S(1)}, u32[]{:S(2)}, u32[]{:S(2)}) collective-permute-start(bf16[8,8192]{1,0:T(8,128)(2,1)} %bitcast.10), channel_id=1, source_target_pairs={{0,2},{1,5},{2,0},{3,7},{4,6},{5,1},{6,4},{7,3},{8,10},{9,13},{10,... | collective-permute-start | bytes 393224 | tf_op jit(solution)/shard_map/ppermute | solution.py:30
  6.2 4.8 %copy-start.2 = (bf16[1,8,8192]{2,1,0:T(8,128)(2,1)S(1)}, bf16[1,8,8192]{2,1,0:T(8,128)(2,1)}, u32[]{:S(2)}) copy-start(bf16[1,8,8192]{2,1,0:T(8,128)(2,1)} %param.6) | copy-start | bytes 393220
  10.9 2.1 %copy-start = (s32[1,2,2]{2,1,0:T(2,128)S(1)}, s32[1,2,2]{2,1,0:T(2,128)}, u32[]{:S(2)}) copy-start(s32[1,2,2]{2,1,0:T(2,128)} %param.9) | copy-start | bytes 52
  10.9 2.1 %copy-start.1 = (bf16[1,256]{1,0:T(2,128)(2,1)S(1)}, bf16[1,256]{1,0:T(2,128)(2,1)}, u32[]{:S(2)}) copy-start(bf16[1,256]{1,0:T(2,128)(2,1)} %bias_ref.1) | copy-start | bytes 1540
  11.0 1.6 %collective-permute-start.3 = (bf16[16,8192]{1,0:T(8,128)(2,1)S(1)}, bf16[16,8192]{1,0:T(8,128)(2,1)S(1)}, u32[]{:S(2)}, u32[]{:S(2)}) collective-permute-start(bf16[16,8192]{1,0:T(8,128)(2,1)S(1)} %pad_maximum_fusion.3), channel_id=1, source_target_pairs={{0,1},{1,0},{2,3},{3,2},{4,5},{5,4},{6,7},{7,6},{8,9},{9,8},{10,11... | collective-permute-start | bytes 786440 | tf_op jit(solution)/shard_map/ppermute | solution.py:34
  11.4 1.6 %collective-permute-start.4 = (bf16[16,8192]{1,0:T(8,128)(2,1)S(1)}, bf16[16,8192]{1,0:T(8,128)(2,1)S(1)}, u32[]{:S(2)}, u32[]{:S(2)}) collective-permute-start(bf16[16,8192]{1,0:T(8,128)(2,1)S(1)} %pad_maximum_fusion.4), channel_id=1, source_target_pairs={{0,1},{1,0},{2,3},{3,2},{4,5},{5,4},{6,7},{7,6},{8,9},{9,8},{10,11... | collective-permute-start | bytes 786440 | tf_op jit(solution)/shard_map/ppermute | solution.py:34
  15.7 2.0 %collective-permute-start.8 = (bf16[32,8192]{1,0:T(8,128)(2,1)S(1)}, bf16[32,8192]{1,0:T(8,128)(2,1)S(1)}, u32[]{:S(2)}, u32[]{:S(2)}) collective-permute-start(bf16[32,8192]{1,0:T(8,128)(2,1)S(1)} %get-tuple-element.26), channel_id=1, source_target_pairs={{0,1},{1,0},{2,3},{3,2},{4,5},{5,4},{6,7},{7,6},{8,9},{9,8},{10,11... | collective-permute-start | bytes 1572872 | tf_op jit(solution)/shard_map/ppermute | solution.py:34
  16.8 6.0 %collective-permute-start.5 = (bf16[32,8192]{1,0:T(8,128)(2,1)S(1)}, bf16[32,8192]{1,0:T(8,128)(2,1)S(1)}, u32[]{:S(2)}, u32[]{:S(2)}) collective-permute-start(bf16[32,8192]{1,0:T(8,128)(2,1)S(1)} %get-tuple-element.23), channel_id=1, source_target_pairs={{0,1},{1,0},{2,3},{3,2},{4,5},{5,4},{6,7},{7,6},{8,9},{9,8},{10,11... | collective-permute-start | bytes 1572872 | tf_op jit(solution)/shard_map/ppermute | solution.py:34
  17.8 9.7 %collective-permute-start.9 = (bf16[8,8192]{1,0:T(8,128)(2,1)S(1)}, bf16[8,8192]{1,0:T(8,128)(2,1)S(1)}, u32[]{:S(2)}, u32[]{:S(2)}) collective-permute-start(bf16[8,8192]{1,0:T(8,128)(2,1)S(1)} %get-tuple-element.40), channel_id=1, source_target_pairs={{0,8},{1,9},{2,10},{3,11},{4,12},{5,13},{6,14},{7,15},{8,16},{9,17... | collective-permute-start | bytes 393224 | tf_op jit(solution)/shard_map/ppermute | solution.py:39
  19.8 6.2 %collective-permute-start.12 = (bf16[8,8192]{1,0:T(8,128)(2,1)S(1)}, bf16[8,8192]{1,0:T(8,128)(2,1)S(1)}, u32[]{:S(2)}, u32[]{:S(2)}) collective-permute-start(bf16[8,8192]{1,0:T(8,128)(2,1)S(1)} %get-tuple-element.41), channel_id=1, source_target_pairs={{0,4},{1,3},{2,6},{3,1},{4,0},{5,7},{6,2},{7,5},{8,12},{9,11},{10,... | collective-permute-start | bytes 393224 | tf_op jit(solution)/shard_map/ppermute | solution.py:30
  21.3 6.1 %collective-permute-start.11 = (bf16[8,8192]{1,0:T(8,128)(2,1)S(1)}, bf16[8,8192]{1,0:T(8,128)(2,1)S(1)}, u32[]{:S(2)}, u32[]{:S(2)}) collective-permute-start(bf16[8,8192]{1,0:T(8,128)(2,1)S(1)} %get-tuple-element.42), channel_id=1, source_target_pairs={{0,2},{1,5},{2,0},{3,7},{4,6},{5,1},{6,4},{7,3},{8,10},{9,13},{10,... | collective-permute-start | bytes 393224 | tf_op jit(solution)/shard_map/ppermute | solution.py:30
  22.8 12.2 %copy-start.4 = (bf16[1,8,8192]{2,1,0:T(8,128)(2,1)S(1)}, bf16[1,8,8192]{2,1,0:T(8,128)(2,1)}, u32[]{:S(2)}) copy-start(bf16[1,8,8192]{2,1,0:T(8,128)(2,1)} %param.11) | copy-start | bytes 393220
  23.0 7.5 %collective-permute-start.6 = (bf16[8,8192]{1,0:T(8,128)(2,1)S(1)}, bf16[8,8192]{1,0:T(8,128)(2,1)S(1)}, u32[]{:S(2)}, u32[]{:S(2)}) collective-permute-start(bf16[8,8192]{1,0:T(8,128)(2,1)S(1)} %get-tuple-element.38), channel_id=1, source_target_pairs={{0,2},{1,5},{2,0},{3,7},{4,6},{5,1},{6,4},{7,3},{8,10},{9,13},{10,... | collective-permute-start | bytes 393224 | tf_op jit(solution)/shard_map/ppermute | solution.py:30
  23.6 6.9 %collective-permute-start.7 = (bf16[8,8192]{1,0:T(8,128)(2,1)S(1)}, bf16[8,8192]{1,0:T(8,128)(2,1)S(1)}, u32[]{:S(2)}, u32[]{:S(2)}) collective-permute-start(bf16[8,8192]{1,0:T(8,128)(2,1)S(1)} %get-tuple-element.39), channel_id=1, source_target_pairs={{0,4},{1,3},{2,6},{3,1},{4,0},{5,7},{6,2},{7,5},{8,12},{9,11},{10,... | collective-permute-start | bytes 393224 | tf_op jit(solution)/shard_map/ppermute | solution.py:30
  27.5 6.8 %collective-permute-start.13 = (bf16[8,8192]{1,0:T(8,128)(2,1)S(1)}, bf16[8,8192]{1,0:T(8,128)(2,1)S(1)}, u32[]{:S(2)}, u32[]{:S(2)}) collective-permute-start(bf16[8,8192]{1,0:T(8,128)(2,1)S(1)} %fusion.1), channel_id=1, source_target_pairs={{0,8},{1,9},{2,10},{3,11},{4,12},{5,13},{6,14},{7,15},{8,16},{9,17... | collective-permute-start | bytes 393224 | tf_op jit(solution)/shard_map/ppermute | solution.py:39
  29.1 5.9 %collective-permute-start.10 = (bf16[8,8192]{1,0:T(8,128)(2,1)S(1)}, bf16[8,8192]{1,0:T(8,128)(2,1)S(1)}, u32[]{:S(2)}, u32[]{:S(2)}) collective-permute-start(bf16[8,8192]{1,0:T(8,128)(2,1)S(1)} %slice_add_fusion.1), channel_id=1, source_target_pairs={{0,6},{1,7},{2,4},{3,5},{4,2},{5,3},{6,0},{7,1},{8,14},{9,15},{10,... | collective-permute-start | bytes 393224 | tf_op jit(solution)/shard_map/ppermute | solution.py:30
  35.1 15.2 %copy-start.3 = (bf16[8,8192]{1,0:T(8,128)(2,1)}, bf16[8,8192]{1,0:T(8,128)(2,1)S(1)}, u32[]{:S(2)}) copy-start(bf16[8,8192]{1,0:T(8,128)(2,1)S(1)} %get-tuple-element.33) | copy-start | bytes 393220
  35.1 5.8 %collective-permute-start.14 = (bf16[8,8192]{1,0:T(8,128)(2,1)S(1)}, bf16[8,8192]{1,0:T(8,128)(2,1)S(1)}, u32[]{:S(2)}, u32[]{:S(2)}) collective-permute-start(bf16[8,8192]{1,0:T(8,128)(2,1)S(1)} %get-tuple-element.33), channel_id=1, source_target_pairs={{8,0},{9,1},{10,2},{11,3},{12,4},{13,5},{14,6},{15,7},{16,8},{17,9... | collective-permute-start | bytes 393224 | tf_op jit(solution)/shard_map/ppermute | solution.py:45
  37.4 7.1 %collective-permute-start.19 = (bf16[8,8192]{1,0:T(8,128)(2,1)S(1)}, bf16[8,8192]{1,0:T(8,128)(2,1)S(1)}, u32[]{:S(2)}, u32[]{:S(2)}) collective-permute-start(bf16[8,8192]{1,0:T(8,128)(2,1)S(1)} %get-tuple-element.33), channel_id=1, source_target_pairs={{0,6},{1,7},{2,4},{3,5},{4,2},{5,3},{6,0},{7,1},{8,14},{9,15},{10,... | collective-permute-start | bytes 393224 | tf_op jit(solution)/shard_map/ppermute | solution.py:30
  38.8 7.4 %collective-permute-start.18 = (bf16[8,8192]{1,0:T(8,128)(2,1)S(1)}, bf16[8,8192]{1,0:T(8,128)(2,1)S(1)}, u32[]{:S(2)}, u32[]{:S(2)}) collective-permute-start(bf16[8,8192]{1,0:T(8,128)(2,1)S(1)} %get-tuple-element.33), channel_id=1, source_target_pairs={{0,4},{1,3},{2,6},{3,1},{4,0},{5,7},{6,2},{7,5},{8,12},{9,11},{10,... | collective-permute-start | bytes 393224 | tf_op jit(solution)/shard_map/ppermute | solution.py:30
  40.1 6.1 %collective-permute-start.17 = (bf16[8,8192]{1,0:T(8,128)(2,1)S(1)}, bf16[8,8192]{1,0:T(8,128)(2,1)S(1)}, u32[]{:S(2)}, u32[]{:S(2)}) collective-permute-start(bf16[8,8192]{1,0:T(8,128)(2,1)S(1)} %get-tuple-element.33), channel_id=1, source_target_pairs={{0,2},{1,5},{2,0},{3,7},{4,6},{5,1},{6,4},{7,3},{8,10},{9,13},{10,... | collective-permute-start | bytes 393224 | tf_op jit(solution)/shard_map/ppermute | solution.py:30
  40.9 8.7 %collective-permute-start.16 = (bf16[8,8192]{1,0:T(8,128)(2,1)S(1)}, bf16[8,8192]{1,0:T(8,128)(2,1)S(1)}, u32[]{:S(2)}, u32[]{:S(2)}) collective-permute-start(bf16[8,8192]{1,0:T(8,128)(2,1)S(1)} %broadcast_select_fusion.1), channel_id=1, source_target_pairs={{0,4},{1,3},{2,6},{3,1},{4,0},{5,7},{6,2},{7,5},{8,12},{9,11},{10,... | collective-permute-start | bytes 393224 | tf_op jit(solution)/shard_map/ppermute | solution.py:30
  41.6 8.1 %collective-permute-start.15 = (bf16[8,8192]{1,0:T(8,128)(2,1)S(1)}, bf16[8,8192]{1,0:T(8,128)(2,1)S(1)}, u32[]{:S(2)}, u32[]{:S(2)}) collective-permute-start(bf16[8,8192]{1,0:T(8,128)(2,1)S(1)} %broadcast_select_fusion.1), channel_id=1, source_target_pairs={{0,2},{1,5},{2,0},{3,7},{4,6},{5,1},{6,4},{7,3},{8,10},{9,13},{10,... | collective-permute-start | bytes 393224 | tf_op jit(solution)/shard_map/ppermute | solution.py:30
  44.6 5.0 %collective-permute-start.21 = (bf16[8,8192]{1,0:T(8,128)(2,1)S(1)}, bf16[8,8192]{1,0:T(8,128)(2,1)S(1)}, u32[]{:S(2)}, u32[]{:S(2)}) collective-permute-start(bf16[8,8192]{1,0:T(8,128)(2,1)S(1)} %collective-permute-done.19), channel_id=1, source_target_pairs={{8,0},{9,1},{10,2},{11,3},{12,4},{13,5},{14,6},{15,7},{16,8},{17,9... | collective-permute-start | bytes 393224 | tf_op jit(solution)/shard_map/ppermute | solution.py:45
  46.3 3.4 %collective-permute-start.20 = (bf16[32,8192]{1,0:T(8,128)(2,1)S(1)}, bf16[32,8192]{1,0:T(8,128)(2,1)S(1)}, u32[]{:S(2)}, u32[]{:S(2)}) collective-permute-start(bf16[32,8192]{1,0:T(8,128)(2,1)S(1)} %pad_maximum_fusion.1), channel_id=1, source_target_pairs={{0,1},{1,0},{2,3},{3,2},{4,5},{5,4},{6,7},{7,6},{8,9},{9,8},{10,11... | collective-permute-start | bytes 1572872 | tf_op jit(solution)/shard_map/ppermute | solution.py:34
  49.5 2.1 %collective-permute-start.23 = (bf16[8,8192]{1,0:T(8,128)(2,1)S(1)}, bf16[8,8192]{1,0:T(8,128)(2,1)S(1)}, u32[]{:S(2)}, u32[]{:S(2)}) collective-permute-start(bf16[8,8192]{1,0:T(8,128)(2,1)S(1)} %broadcast_select_fusion), channel_id=1, source_target_pairs={{0,1},{1,0},{2,3},{3,2},{4,5},{5,4},{6,7},{7,6},{8,9},{9,8},{10,11... | collective-permute-start | bytes 393224 | tf_op jit(solution)/shard_map/ppermute | solution.py:34
  49.7 2.0 %collective-permute-start.22 = (bf16[24,8192]{1,0:T(8,128)(2,1)S(1)}, bf16[24,8192]{1,0:T(8,128)(2,1)S(1)}, u32[]{:S(2)}, u32[]{:S(2)}) collective-permute-start(bf16[24,8192]{1,0:T(8,128)(2,1)S(1)} %pad_maximum_fusion.2), channel_id=1, source_target_pairs={{0,1},{1,0},{2,3},{3,2},{4,5},{5,4},{6,7},{7,6},{8,9},{9,8},{10,11... | collective-permute-start | bytes 1179656 | tf_op jit(solution)/shard_map/ppermute | solution.py:34

commit v13 on v12

--- a/solution.py
+++ b/solution.py
@@ -126,14 +126,23 @@
     return jnp.concatenate(parts, axis=1)
 
 
-def encode_kernel(tokens, active_ref, x_ref, enc_ref, bias_ref, dec_ref, codes_ref, near_ref, far_ref):
-    rows, depth = x_ref.shape
-    pre = bias_ref[...].astype(jnp.float32) + summed_over(
-        depth, lambda part: jnp.dot(x_ref[:, part], enc_ref[part, :], preferred_element_type=jnp.float32)
-    )
-    codes = jnp.maximum(pre, 0.0) * gate_of(active_ref, rows, tokens)
-    codes_ref[...] = codes.astype(jnp.bfloat16)
-    decode(codes_ref[...], dec_ref, near_ref, far_ref)
+def gate_kernel(tokens, active_ref, bias_ref, gate_ref, shift_ref):
+    rows = gate_ref.shape[0]
+    gate_ref[...] = gate_of(active_ref, rows, tokens)
+    shift_ref[...] = jnp.broadcast_to(bias_ref[...].astype(jnp.float32), shift_ref.shape)
+
+
+def gated(active, bias, rows, tokens):
+    shape = (rows, bias.shape[1])
+    return pl.pallas_call(
+        functools.partial(gate_kernel, tokens),
+        out_shape=[pltpu.VMEM(shape, jnp.float32)] * 2,
+        in_specs=[VMEM_SPEC] * 2,
+        out_specs=[VMEM_SPEC] * 2,
+        compiler_params=kernel_params(),
+        cost_estimate=pl.CostEstimate(flops=8 * rows * shape[1], bytes_accessed=8 * rows * shape[1], transcendentals=0),
+        name="gate",
+    )(*in_vmem(active, bias))
 
 
 def decode_kernel(codes_ref, dec_ref, near_ref, far_ref):
@@ -142,20 +151,6 @@
 
 def halves_of(rows, width):
     return [pltpu.VMEM((rows // CORES, width), jnp.float32), pltpu.VMEM((rows // CORES, width), jnp.bfloat16)]
-
-
-def encoded(active, x, enc, bias, dec, tokens):
-    rows, depth = x.shape
-    features = enc.shape[1]
-    return pl.pallas_call(
-        functools.partial(encode_kernel, tokens),
-        out_shape=[pltpu.VMEM((rows, features), jnp.bfloat16)] + halves_of(rows, depth),
-        in_specs=[VMEM_SPEC] * 5,
-        out_specs=[VMEM_SPEC] * 3,
-        compiler_params=kernel_params(),
-        cost_estimate=pl.CostEstimate(flops=4 * rows * depth * features, bytes_accessed=4 * depth * features, transcendentals=0),
-        name="encode",
-    )(*in_vmem(active, x, enc, bias, dec))
 
 
 def decoded(codes, dec):
@@ -168,7 +163,7 @@
         out_specs=[VMEM_SPEC] * 2,
         compiler_params=kernel_params(),
         cost_estimate=pl.CostEstimate(flops=2 * rows * width * features, bytes_accessed=2 * width * features, transcendentals=0),
-        name="decode_own",
+        name="decode",
     )(*in_vmem(codes, dec))
 
 
@@ -245,19 +240,25 @@
     x = jnp.concatenate(
         [slab, late, last, early_far[:tokens], late_far, early_far[tokens:]], axis=0
     )
-    codes, next_near, next_far = encoded(active[0], x, enc, enc_bias, next_dec, tokens)
+    gate, bias = gated(*after((active[0], enc_bias), enc), group * tokens, tokens)
+    pre = jnp.dot(x, enc, preferred_element_type=jnp.float32) + bias
+    codes = (jax.nn.relu(pre) * gate).astype(jnp.bfloat16)
+    next_near, next_far = decoded(codes, next_dec)
     own_near, own_far = decoded(codes, own_dec)
 
     nexts = blocks_of(next_near, next_far, chips)
     owns = blocks_of(own_near, own_far, chips)
     risen = raised(nexts[-1].astype(jnp.bfloat16), first, group)
     owns[-1] = owns[-1] + risen.astype(jnp.float32)
-    next_sum = after(summed(nexts, range(1, chips - 1)).astype(jnp.bfloat16), owns[-1])
-    from_before = raised(next_sum, first, group).astype(jnp.float32)
-    own_sum = summed(owns, range(1, chips))
-    error = (own_sum + from_before - target[0].astype(jnp.float32)).astype(jnp.bfloat16)
-
-    later = lowered(error, final, group)
+    crossed = across(owns[-1].astype(jnp.bfloat16), chips - 1, chips).astype(jnp.float32)
+    next_sum = after(summed(nexts, range(1, chips - 1)), owns[-1])
+    own_less = summed(owns, range(1, chips - 1)) - target[0].astype(jnp.float32) + crossed
+
+    below = raised(next_sum.astype(jnp.bfloat16), first, group).astype(jnp.float32)
+    above = lowered(own_less.astype(jnp.bfloat16), final, group).astype(jnp.float32)
+    error = (own_less + below).astype(jnp.bfloat16)
+    later = jnp.where(final, 0.0, next_sum + after(above, error)).astype(jnp.bfloat16)
+
     heres = [error] + [across(error, chip, chips) for chip in range(1, chips)]
     afters = [later] + [across(later, chip, chips) for chip in range(1, chips - 1)]
     last = lowered(after(heres[-1], later), final, group)

time: 54 us -> 51.3 us (0.950)
  waiting for transfers between devices: 14.6 us -> 12.4 us
  Pallas kernels: 11.6 us -> 9.92 us
  matrix products: 0 us -> 0.8 us
    pallas_call x1, Pallas kernels: 2.6 us -> 0.11 us  [gated(): pl.pallas_call(functools.partial(gate_kernel, tokens), out_shape=[pltpu.V...]
    ppermute x2, waiting for transfers between devices: 3.82 us -> 2.55 us  [raised(): lax.ppermute(value, AXIS, [(i, (i + group) % size) for i in range(size)])]
    ppermute x13, starting transfers between devices: 15.6 us -> 16.8 us  [across(): return lax.ppermute(value, AXIS, pairs)]
    ppermute x13, waiting for transfers between devices: 5.92 us -> 4.95 us  [across(): return lax.ppermute(value, AXIS, pairs)]
    ppermute x2, starting transfers between devices: 3.64 us -> 2.78 us  [raised(): lax.ppermute(value, AXIS, [(i, (i + group) % size) for i in range(size)])]
    pallas_call x1 -> x2, Pallas kernels: 0.85 us -> 1.67 us  [decoded(): pl.pallas_call(decode_kernel, out_shape=halves_of(rows, width), in_specs=...]
    dot_general x0 -> x1, matrix products: none -> 0.8 us  [on_device(): pre = jnp.dot(x, enc, preferred_element_type=jnp.float32) + bias]
  transfers between devices with their start and end apart: 24 -> 24, of which waited for: 10 -> 11; matrix products, arithmetic and copies ran while one was open for 3% -> 3% of each run, Pallas kernels for 13% -> 14%
where the time goes in v13:
time: 51.3 us; the launch traced here: 51.2 us
  starting transfers between devices  25.1 us (49%)
  waiting for transfers between devices  12.4 us (24%)
  Pallas kernels  9.92 us (19%)
  local copies, waits for them, and re-layouts  1.16 us (2%)
  between operations  1 us (2%)
  matrix products  0.8 us (2%)
  other arithmetic  0.74 us (1%)
    ppermute x13, starting transfers between devices, across(): return lax.ppermute(value, AXIS, pairs)  16.8 us
    ppermute x13, waiting for transfers between devices, across(): return lax.ppermute(value, AXIS, pairs)  4.95 us
    pallas_call x1, Pallas kernels, loaded(): pl.pallas_call(load_kernel, out_shape=[pltpu.VMEM(enc.shape[1:], enc.dtyp...  4.72 us
    ppermute x2, starting transfers between devices, lowered(): lax.ppermute(value, AXIS, [((i + group) % size, i) for i in range(size)])  3.73 us
    ppermute x2, waiting for transfers between devices, lowered(): lax.ppermute(value, AXIS, [((i + group) % size, i) for i in range(size)])  3.19 us
    ppermute x2, starting transfers between devices, raised(): lax.ppermute(value, AXIS, [(i, (i + group) % size) for i in range(size)])  2.78 us
    ppermute x2, waiting for transfers between devices, raised(): lax.ppermute(value, AXIS, [(i, (i + group) % size) for i in range(size)])  2.55 us
    pallas_call x1, Pallas kernels, grad_all(): pl.pallas_call(functools.partial(grad_all_kernel, tokens), out_shape=jax....  2.03 us
  transfers between devices with their start and end apart: 24, of which 11 were waited for; matrix products, arithmetic and copies ran while one was open for 3% of the time, Pallas kernels for 14%

profile of v13, /device:TPU:0, one launch (start us, length us, event | category | flops | bytes accessed | tf_op | source)
XLA Modules:
  0.0 51.2 jit_solution(14409358332755796315)
XLA Ops:
  0.6 4.0 %collective-permute-start.2 = (bf16[8,8192]{1,0:T(8,128)(2,1)}, bf16[8,8192]{1,0:T(8,128)(2,1)S(1)}, u32[]{:S(2)}, u32[]{:S(2)}) collective-permute-start(bf16[8,8192]{1,0:T(8,128)(2,1)} %bitcast.14), channel_id=1, source_target_pairs={{0,6},{1,7},{2,4},{3,5},{4,2},{5,3},{6,0},{7,1},{8,14},{9,15},{10,... | collective-permute-start | bytes 393224 | tf_op jit(solution)/shard_map/ppermute | solution.py:30
  4.6 0.5 collective-permute-start.1
  5.1 0.1 collective-permute-start
  5.2 0.9 %constant_dynamic-update-slice_fusion.4 = bf16[64,8192]{1,0:T(8,128)(2,1)S(1)} fusion(bf16[8,8192]{1,0:T(8,128)(2,1)} %bitcast.17), kind=kLoop, calls=%fused_computation.28 | loop fusion | bytes 262144
  6.2 0.0 copy-start
  6.2 0.0 copy-start.1
  6.2 0.0 copy-start.3
  6.2 4.7 %load_weights.1 = (bf16[8192,256]{1,0:T(8,128)(2,1)S(1)}, bf16[256,8192]{1,0:T(8,128)(2,1)S(1)}, bf16[256,8192]{1,0:T(8,128)(2,1)S(1)}) custom-call(bf16[1,8192,256]{2,1,0:T(8,128)(2,1)} %enc_hbm.1, bf16[1,2,256,8192]{3,2,1,0:T(8,128)(2,1)} %dec_hbm.1), custom_call_target="tpu_custom_call" | custom-call | bytes 25165824 | tf_op jit(solution)/shard_map/load_weights/pallas_call | solution.py:82
  11.0 0.1 gate.1
  11.1 0.0 collective-permute-done.2
  11.1 0.1 collective-permute-start.3
  11.2 0.0 collective-permute-done.1
  11.2 0.1 collective-permute-done
  11.4 0.4 collective-permute-start.4
  11.9 0.9 %collective-permute-done.3 = bf16[16,8192]{1,0:T(8,128)(2,1)S(1)} collective-permute-done((bf16[16,8192]{1,0:T(8,128)(2,1)S(1)}, bf16[16,8192]{1,0:T(8,128)(2,1)S(1)}, u32[]{:S(2)}, u32[]{:S(2)}) %collective-permute-start.3) | collective-permute-done | bytes 262176 | tf_op jit(solution)/shard_map/ppermute | solution.py:34
  12.8 0.4 collective-permute-done.4
  13.2 0.8 %fusion.2.codes_ref = bf16[64,256]{1,0:T(8,128)(2,1)S(1)} fusion(f32[64,256]{1,0:T(8,128)S(1)} %get-tuple-element.26, f32[64,256]{1,0:T(8,128)S(1)} %get-tuple-element.25, bf16[64,8192]{1,0:T(8,128)(2,1)S(1)} %slice_dynamic-update-slice_fusion, bf16[8192,256]{1,0:T(8,128)(2,1)S(1)} %get-tuple-element.22), kind=kOutput, calls=%fused_computation.3 | convolution fusion | flops 268500992 | bytes 5406720 | tf_op jit(solution)/shard_map/dot_general | solution.py:244
  14.0 0.8 %decode.3 = (f32[32,8192]{1,0:T(8,128)S(1)}, bf16[32,8192]{1,0:T(8,128)(2,1)S(1)}) custom-call(bf16[64,256]{1,0:T(8,128)(2,1)S(1)} %fusion.2.codes_ref, bf16[256,8192]{1,0:T(8,128)(2,1)S(1)} %get-tuple-element.31.dec_ref), custom_call_target="tpu_custom_call" | custom-call | flops 268435456 | bytes 4194304 | tf_op jit(solution)/shard_map/decode/pallas_call | solution.py:159
  14.8 0.3 collective-permute-start.8
  15.1 0.8 %decode.2 = (f32[32,8192]{1,0:T(8,128)S(1)}, bf16[32,8192]{1,0:T(8,128)(2,1)S(1)}) custom-call(bf16[64,256]{1,0:T(8,128)(2,1)S(1)} %fusion.2.codes_ref, bf16[256,8192]{1,0:T(8,128)(2,1)S(1)} %get-tuple-element.27.dec_ref), custom_call_target="tpu_custom_call" | custom-call | flops 268435456 | bytes 4194304 | tf_op jit(solution)/shard_map/decode/pallas_call | solution.py:159
  15.9 0.3 collective-permute-start.5
  16.3 0.5 collective-permute-done.8
  16.8 0.1 fusion.9
  16.9 2.0 %collective-permute-start.9 = (bf16[8,8192]{1,0:T(8,128)(2,1)S(1)}, bf16[8,8192]{1,0:T(8,128)(2,1)S(1)}, u32[]{:S(2)}, u32[]{:S(2)}) collective-permute-start(bf16[8,8192]{1,0:T(8,128)(2,1)S(1)} %get-tuple-element.48), channel_id=1, source_target_pairs={{0,8},{1,9},{2,10},{3,11},{4,12},{5,13},{6,14},{7,15},{8,16},{9,17... | collective-permute-start | bytes 393224 | tf_op jit(solution)/shard_map/ppermute | solution.py:39
  19.0 1.5 %collective-permute-start.12 = (bf16[8,8192]{1,0:T(8,128)(2,1)S(1)}, bf16[8,8192]{1,0:T(8,128)(2,1)S(1)}, u32[]{:S(2)}, u32[]{:S(2)}) collective-permute-start(bf16[8,8192]{1,0:T(8,128)(2,1)S(1)} %get-tuple-element.49), channel_id=1, source_target_pairs={{0,4},{1,3},{2,6},{3,1},{4,0},{5,7},{6,2},{7,5},{8,12},{9,11},{10,... | collective-permute-start | bytes 393224 | tf_op jit(solution)/shard_map/ppermute | solution.py:30
  20.5 1.5 %collective-permute-start.11 = (bf16[8,8192]{1,0:T(8,128)(2,1)S(1)}, bf16[8,8192]{1,0:T(8,128)(2,1)S(1)}, u32[]{:S(2)}, u32[]{:S(2)}) collective-permute-start(bf16[8,8192]{1,0:T(8,128)(2,1)S(1)} %get-tuple-element.50), channel_id=1, source_target_pairs={{0,2},{1,5},{2,0},{3,7},{4,6},{5,1},{6,4},{7,3},{8,10},{9,13},{10,... | collective-permute-start | bytes 393224 | tf_op jit(solution)/shard_map/ppermute | solution.py:30
  22.0 0.0 collective-permute-done.5
  22.0 0.1 fusion.8
  22.2 0.6 %collective-permute-start.6 = (bf16[8,8192]{1,0:T(8,128)(2,1)S(1)}, bf16[8,8192]{1,0:T(8,128)(2,1)S(1)}, u32[]{:S(2)}, u32[]{:S(2)}) collective-permute-start(bf16[8,8192]{1,0:T(8,128)(2,1)S(1)} %get-tuple-element.46), channel_id=1, source_target_pairs={{0,2},{1,5},{2,0},{3,7},{4,6},{5,1},{6,4},{7,3},{8,10},{9,13},{10,... | collective-permute-start | bytes 393224 | tf_op jit(solution)/shard_map/ppermute | solution.py:30
  22.7 0.5 collective-permute-start.7
  23.2 1.6 %collective-permute-done.9 = bf16[8,8192]{1,0:T(8,128)(2,1)S(1)} collective-permute-done((bf16[8,8192]{1,0:T(8,128)(2,1)S(1)}, bf16[8,8192]{1,0:T(8,128)(2,1)S(1)}, u32[]{:S(2)}, u32[]{:S(2)}) %collective-permute-start.9) | collective-permute-done | bytes 131104 | tf_op jit(solution)/shard_map/ppermute | solution.py:39
  24.9 2.5 %collective-permute-start.10 = (bf16[8,8192]{1,0:T(8,128)(2,1)S(1)}, bf16[8,8192]{1,0:T(8,128)(2,1)S(1)}, u32[]{:S(2)}, u32[]{:S(2)}) collective-permute-start(bf16[8,8192]{1,0:T(8,128)(2,1)S(1)} %slice_add_fusion.1), channel_id=1, source_target_pairs={{0,6},{1,7},{2,4},{3,5},{4,2},{5,3},{6,0},{7,1},{8,14},{9,15},{10,... | collective-permute-start | bytes 393224 | tf_op jit(solution)/shard_map/ppermute | solution.py:30
  27.4 0.0 collective-permute-done.12
  27.4 0.0 collective-permute-done.11
  27.5 0.8 %collective-permute-start.13 = (bf16[8,8192]{1,0:T(8,128)(2,1)S(1)}, bf16[8,8192]{1,0:T(8,128)(2,1)S(1)}, u32[]{:S(2)}, u32[]{:S(2)}) collective-permute-start(bf16[8,8192]{1,0:T(8,128)(2,1)S(1)} %convert_element_type.71), channel_id=1, source_target_pairs={{0,8},{1,9},{2,10},{3,11},{4,12},{5,13},{6,14},{7,15},{8,16},{9,17... | collective-permute-start | bytes 393224 | tf_op jit(solution)/shard_map/ppermute | solution.py:39
  28.3 0.2 collective-permute-done.6
  28.4 0.0 collective-permute-done.7
  28.4 2.6 %collective-permute-done.10 = bf16[8,8192]{1,0:T(8,128)(2,1)S(1)} collective-permute-done((bf16[8,8192]{1,0:T(8,128)(2,1)S(1)}, bf16[8,8192]{1,0:T(8,128)(2,1)S(1)}, u32[]{:S(2)}, u32[]{:S(2)}) %collective-permute-start.10) | collective-permute-done | bytes 131104 | tf_op jit(solution)/shard_map/ppermute | solution.py:30
  31.0 0.1 fusion.7
  31.1 2.4 %collective-permute-start.14 = (bf16[8,8192]{1,0:T(8,128)(2,1)S(1)}, bf16[8,8192]{1,0:T(8,128)(2,1)S(1)}, u32[]{:S(2)}, u32[]{:S(2)}) collective-permute-start(bf16[8,8192]{1,0:T(8,128)(2,1)S(1)} %fusion.7), channel_id=1, source_target_pairs={{8,0},{9,1},{10,2},{11,3},{12,4},{13,5},{14,6},{15,7},{16,8},{17,9... | collective-permute-start | bytes 393224 | tf_op jit(solution)/shard_map/ppermute | solution.py:45
  33.5 0.9 %collective-permute-done.13 = bf16[8,8192]{1,0:T(8,128)(2,1)S(1)} collective-permute-done((bf16[8,8192]{1,0:T(8,128)(2,1)S(1)}, bf16[8,8192]{1,0:T(8,128)(2,1)S(1)}, u32[]{:S(2)}, u32[]{:S(2)}) %collective-permute-start.13) | collective-permute-done | bytes 131104 | tf_op jit(solution)/shard_map/ppermute | solution.py:39
  34.4 0.1 constant_dynamic-update-slice_fusion.9
  34.5 0.0 copy-start.4
  34.5 1.5 %collective-permute-start.19 = (bf16[8,8192]{1,0:T(8,128)(2,1)S(1)}, bf16[8,8192]{1,0:T(8,128)(2,1)S(1)}, u32[]{:S(2)}, u32[]{:S(2)}) collective-permute-start(bf16[8,8192]{1,0:T(8,128)(2,1)S(1)} %get-tuple-element.41), channel_id=1, source_target_pairs={{0,6},{1,7},{2,4},{3,5},{4,2},{5,3},{6,0},{7,1},{8,14},{9,15},{10,... | collective-permute-start | bytes 393224 | tf_op jit(solution)/shard_map/ppermute | solution.py:30
  36.0 0.6 %collective-permute-start.18 = (bf16[8,8192]{1,0:T(8,128)(2,1)S(1)}, bf16[8,8192]{1,0:T(8,128)(2,1)S(1)}, u32[]{:S(2)}, u32[]{:S(2)}) collective-permute-start(bf16[8,8192]{1,0:T(8,128)(2,1)S(1)} %get-tuple-element.41), channel_id=1, source_target_pairs={{0,4},{1,3},{2,6},{3,1},{4,0},{5,7},{6,2},{7,5},{8,12},{9,11},{10,... | collective-permute-start | bytes 393224 | tf_op jit(solution)/shard_map/ppermute | solution.py:30
  36.6 1.5 %collective-permute-start.17 = (bf16[8,8192]{1,0:T(8,128)(2,1)S(1)}, bf16[8,8192]{1,0:T(8,128)(2,1)S(1)}, u32[]{:S(2)}, u32[]{:S(2)}) collective-permute-start(bf16[8,8192]{1,0:T(8,128)(2,1)S(1)} %get-tuple-element.41), channel_id=1, source_target_pairs={{0,2},{1,5},{2,0},{3,7},{4,6},{5,1},{6,4},{7,3},{8,10},{9,13},{10,... | collective-permute-start | bytes 393224 | tf_op jit(solution)/shard_map/ppermute | solution.py:30
  38.1 0.0 collective-permute-done.14
  38.2 0.6 %collective-permute-start.16 = (bf16[8,8192]{1,0:T(8,128)(2,1)S(1)}, bf16[8,8192]{1,0:T(8,128)(2,1)S(1)}, u32[]{:S(2)}, u32[]{:S(2)}) collective-permute-start(bf16[8,8192]{1,0:T(8,128)(2,1)S(1)} %select_convert_fusion), channel_id=1, source_target_pairs={{0,4},{1,3},{2,6},{3,1},{4,0},{5,7},{6,2},{7,5},{8,12},{9,11},{10,... | collective-permute-start | bytes 393224 | tf_op jit(solution)/shard_map/ppermute | solution.py:30
  38.7 1.5 %collective-permute-start.15 = (bf16[8,8192]{1,0:T(8,128)(2,1)S(1)}, bf16[8,8192]{1,0:T(8,128)(2,1)S(1)}, u32[]{:S(2)}, u32[]{:S(2)}) collective-permute-start(bf16[8,8192]{1,0:T(8,128)(2,1)S(1)} %select_convert_fusion), channel_id=1, source_target_pairs={{0,2},{1,5},{2,0},{3,7},{4,6},{5,1},{6,4},{7,3},{8,10},{9,13},{10,... | collective-permute-start | bytes 393224 | tf_op jit(solution)/shard_map/ppermute | solution.py:30
  40.2 1.8 %collective-permute-done.19 = bf16[8,8192]{1,0:T(8,128)(2,1)S(1)} collective-permute-done((bf16[8,8192]{1,0:T(8,128)(2,1)S(1)}, bf16[8,8192]{1,0:T(8,128)(2,1)S(1)}, u32[]{:S(2)}, u32[]{:S(2)}) %collective-permute-start.19) | collective-permute-done | bytes 131104 | tf_op jit(solution)/shard_map/ppermute | solution.py:30
  41.9 1.3 %collective-permute-start.21 = (bf16[8,8192]{1,0:T(8,128)(2,1)S(1)}, bf16[8,8192]{1,0:T(8,128)(2,1)S(1)}, u32[]{:S(2)}, u32[]{:S(2)}) collective-permute-start(bf16[8,8192]{1,0:T(8,128)(2,1)S(1)} %collective-permute-done.19), channel_id=1, source_target_pairs={{8,0},{9,1},{10,2},{11,3},{12,4},{13,5},{14,6},{15,7},{16,8},{17,9... | collective-permute-start | bytes 393224 | tf_op jit(solution)/shard_map/ppermute | solution.py:45
  43.3 0.3 collective-permute-done.18
  43.5 0.0 collective-permute-done.17
  43.6 0.1 collective-permute-start.20
  43.7 3.2 %collective-permute-done.21 = bf16[8,8192]{1,0:T(8,128)(2,1)S(1)} collective-permute-done((bf16[8,8192]{1,0:T(8,128)(2,1)S(1)}, bf16[8,8192]{1,0:T(8,128)(2,1)S(1)}, u32[]{:S(2)}, u32[]{:S(2)}) %collective-permute-start.21) | collective-permute-done | bytes 131104 | tf_op jit(solution)/shard_map/ppermute | solution.py:45
  46.9 0.1 collective-permute-start.23
  47.0 0.0 collective-permute-done.16
  47.0 0.0 collective-permute-done.15
  47.1 0.0 collective-permute-done.20
  47.1 0.5 %collective-permute-start.22 = (bf16[24,8192]{1,0:T(8,128)(2,1)S(1)}, bf16[24,8192]{1,0:T(8,128)(2,1)S(1)}, u32[]{:S(2)}, u32[]{:S(2)}) collective-permute-start(bf16[24,8192]{1,0:T(8,128)(2,1)S(1)} %pad_maximum_fusion.2), channel_id=1, source_target_pairs={{0,1},{1,0},{2,3},{3,2},{4,5},{5,4},{6,7},{7,6},{8,9},{9,8},{10,11... | collective-permute-start | bytes 1179656 | tf_op jit(solution)/shard_map/ppermute | solution.py:34
  47.7 1.4 %grad_own.1 = (f32[64,256]{1,0:T(8,128)S(1)}, f32[8,128]{1,0:T(8,128)}) custom-call(bf16[64,8192]{1,0:T(8,128)(2,1)S(1)} %constant_dynamic-update-slice_fusion.5.rows_ref, bf16[256,8192]{1,0:T(8,128)(2,1)S(1)} %get-tuple-element.27.dec_ref), custom_call_target="tpu_custom_call" | custom-call | flops 268435456 | bytes 4194304 | tf_op jit(solution)/shard_map/grad_own/pallas_call | solution.py:194
  49.1 0.0 collective-permute-done.22
  49.1 0.1 pad_maximum_fusion.rows_ref
  49.2 2.0 %grad_all.1 = f32[1,64,256]{2,1,0:T(8,128)} custom-call(bf16[64,8192]{1,0:T(8,128)(2,1)S(1)} %pad_maximum_fusion.rows_ref, bf16[256,8192]{1,0:T(8,128)(2,1)S(1)} %get-tuple-element.31.dec_ref, f32[64,256]{1,0:T(8,128)S(1)} %get-tuple-element.39.own_ref), custom_call_target="tpu_custom_call" | custom-call | flops 268435456 | bytes 4194304 | tf_op jit(solution)/shard_map/grad_all/pallas_call | solution.py:206
  (29 shorter events, 0.5 us)
Async XLA Ops:
  0.6 10.5 %collective-permute-start.2 = (bf16[8,8192]{1,0:T(8,128)(2,1)}, bf16[8,8192]{1,0:T(8,128)(2,1)S(1)}, u32[]{:S(2)}, u32[]{:S(2)}) collective-permute-start(bf16[8,8192]{1,0:T(8,128)(2,1)} %bitcast.14), channel_id=1, source_target_pairs={{0,6},{1,7},{2,4},{3,5},{4,2},{5,3},{6,0},{7,1},{8,14},{9,15},{10,... | collective-permute-start | bytes 393224 | tf_op jit(solution)/shard_map/ppermute | solution.py:30
  4.6 6.6 %collective-permute-start.1 = (bf16[8,8192]{1,0:T(8,128)(2,1)}, bf16[8,8192]{1,0:T(8,128)(2,1)S(1)}, u32[]{:S(2)}, u32[]{:S(2)}) collective-permute-start(bf16[8,8192]{1,0:T(8,128)(2,1)} %bitcast.15), channel_id=1, source_target_pairs={{0,4},{1,3},{2,6},{3,1},{4,0},{5,7},{6,2},{7,5},{8,12},{9,11},{10,... | collective-permute-start | bytes 393224 | tf_op jit(solution)/shard_map/ppermute | solution.py:30
  5.1 6.3 %collective-permute-start = (bf16[8,8192]{1,0:T(8,128)(2,1)}, bf16[8,8192]{1,0:T(8,128)(2,1)S(1)}, u32[]{:S(2)}, u32[]{:S(2)}) collective-permute-start(bf16[8,8192]{1,0:T(8,128)(2,1)} %bitcast.16), channel_id=1, source_target_pairs={{0,2},{1,5},{2,0},{3,7},{4,6},{5,1},{6,4},{7,3},{8,10},{9,13},{10,... | collective-permute-start | bytes 393224 | tf_op jit(solution)/shard_map/ppermute | solution.py:30
  6.2 4.8 %copy-start = (s32[1,2,2]{2,1,0:T(2,128)S(1)}, s32[1,2,2]{2,1,0:T(2,128)}, u32[]{:S(2)}) copy-start(s32[1,2,2]{2,1,0:T(2,128)} %param.9) | copy-start | bytes 52
  6.2 4.8 %copy-start.1 = (bf16[1,256]{1,0:T(2,128)(2,1)S(1)}, bf16[1,256]{1,0:T(2,128)(2,1)}, u32[]{:S(2)}) copy-start(bf16[1,256]{1,0:T(2,128)(2,1)} %bias_ref) | copy-start | bytes 1540
  6.2 4.9 %copy-start.3 = (bf16[1,8,8192]{2,1,0:T(8,128)(2,1)S(1)}, bf16[1,8,8192]{2,1,0:T(8,128)(2,1)}, u32[]{:S(2)}) copy-start(bf16[1,8,8192]{2,1,0:T(8,128)(2,1)} %param.6) | copy-start | bytes 393220
  11.1 1.6 %collective-permute-start.3 = (bf16[16,8192]{1,0:T(8,128)(2,1)S(1)}, bf16[16,8192]{1,0:T(8,128)(2,1)S(1)}, u32[]{:S(2)}, u32[]{:S(2)}) collective-permute-start(bf16[16,8192]{1,0:T(8,128)(2,1)S(1)} %pad_maximum_fusion.3), channel_id=1, source_target_pairs={{0,1},{1,0},{2,3},{3,2},{4,5},{5,4},{6,7},{7,6},{8,9},{9,8},{10,11... | collective-permute-start | bytes 786440 | tf_op jit(solution)/shard_map/ppermute | solution.py:34
  11.4 1.7 %collective-permute-start.4 = (bf16[16,8192]{1,0:T(8,128)(2,1)S(1)}, bf16[16,8192]{1,0:T(8,128)(2,1)S(1)}, u32[]{:S(2)}, u32[]{:S(2)}) collective-permute-start(bf16[16,8192]{1,0:T(8,128)(2,1)S(1)} %pad_maximum_fusion.4), channel_id=1, source_target_pairs={{0,1},{1,0},{2,3},{3,2},{4,5},{5,4},{6,7},{7,6},{8,9},{9,8},{10,11... | collective-permute-start | bytes 786440 | tf_op jit(solution)/shard_map/ppermute | solution.py:34
  14.8 2.0 %collective-permute-start.8 = (bf16[32,8192]{1,0:T(8,128)(2,1)S(1)}, bf16[32,8192]{1,0:T(8,128)(2,1)S(1)}, u32[]{:S(2)}, u32[]{:S(2)}) collective-permute-start(bf16[32,8192]{1,0:T(8,128)(2,1)S(1)} %get-tuple-element.33), channel_id=1, source_target_pairs={{0,1},{1,0},{2,3},{3,2},{4,5},{5,4},{6,7},{7,6},{8,9},{9,8},{10,11... | collective-permute-start | bytes 1572872 | tf_op jit(solution)/shard_map/ppermute | solution.py:34
  15.9 6.1 %collective-permute-start.5 = (bf16[32,8192]{1,0:T(8,128)(2,1)S(1)}, bf16[32,8192]{1,0:T(8,128)(2,1)S(1)}, u32[]{:S(2)}, u32[]{:S(2)}) collective-permute-start(bf16[32,8192]{1,0:T(8,128)(2,1)S(1)} %get-tuple-element.29), channel_id=1, source_target_pairs={{0,1},{1,0},{2,3},{3,2},{4,5},{5,4},{6,7},{7,6},{8,9},{9,8},{10,11... | collective-permute-start | bytes 1572872 | tf_op jit(solution)/shard_map/ppermute | solution.py:34
  16.8 14.2 %copy-start.2 = (bf16[1,8,8192]{2,1,0:T(8,128)(2,1)S(1)}, bf16[1,8,8192]{2,1,0:T(8,128)(2,1)}, u32[]{:S(2)}) copy-start(bf16[1,8,8192]{2,1,0:T(8,128)(2,1)} %param.11) | copy-start | bytes 393220
  16.9 8.0 %collective-permute-start.9 = (bf16[8,8192]{1,0:T(8,128)(2,1)S(1)}, bf16[8,8192]{1,0:T(8,128)(2,1)S(1)}, u32[]{:S(2)}, u32[]{:S(2)}) collective-permute-start(bf16[8,8192]{1,0:T(8,128)(2,1)S(1)} %get-tuple-element.48), channel_id=1, source_target_pairs={{0,8},{1,9},{2,10},{3,11},{4,12},{5,13},{6,14},{7,15},{8,16},{9,17... | collective-permute-start | bytes 393224 | tf_op jit(solution)/shard_map/ppermute | solution.py:39
  19.0 8.5 %collective-permute-start.12 = (bf16[8,8192]{1,0:T(8,128)(2,1)S(1)}, bf16[8,8192]{1,0:T(8,128)(2,1)S(1)}, u32[]{:S(2)}, u32[]{:S(2)}) collective-permute-start(bf16[8,8192]{1,0:T(8,128)(2,1)S(1)} %get-tuple-element.49), channel_id=1, source_target_pairs={{0,4},{1,3},{2,6},{3,1},{4,0},{5,7},{6,2},{7,5},{8,12},{9,11},{10,... | collective-permute-start | bytes 393224 | tf_op jit(solution)/shard_map/ppermute | solution.py:30
  20.5 7.0 %collective-permute-start.11 = (bf16[8,8192]{1,0:T(8,128)(2,1)S(1)}, bf16[8,8192]{1,0:T(8,128)(2,1)S(1)}, u32[]{:S(2)}, u32[]{:S(2)}) collective-permute-start(bf16[8,8192]{1,0:T(8,128)(2,1)S(1)} %get-tuple-element.50), channel_id=1, source_target_pairs={{0,2},{1,5},{2,0},{3,7},{4,6},{5,1},{6,4},{7,3},{8,10},{9,13},{10,... | collective-permute-start | bytes 393224 | tf_op jit(solution)/shard_map/ppermute | solution.py:30
  22.2 6.3 %collective-permute-start.6 = (bf16[8,8192]{1,0:T(8,128)(2,1)S(1)}, bf16[8,8192]{1,0:T(8,128)(2,1)S(1)}, u32[]{:S(2)}, u32[]{:S(2)}) collective-permute-start(bf16[8,8192]{1,0:T(8,128)(2,1)S(1)} %get-tuple-element.46), channel_id=1, source_target_pairs={{0,2},{1,5},{2,0},{3,7},{4,6},{5,1},{6,4},{7,3},{8,10},{9,13},{10,... | collective-permute-start | bytes 393224 | tf_op jit(solution)/shard_map/ppermute | solution.py:30
  22.7 5.7 %collective-permute-start.7 = (bf16[8,8192]{1,0:T(8,128)(2,1)S(1)}, bf16[8,8192]{1,0:T(8,128)(2,1)S(1)}, u32[]{:S(2)}, u32[]{:S(2)}) collective-permute-start(bf16[8,8192]{1,0:T(8,128)(2,1)S(1)} %get-tuple-element.47), channel_id=1, source_target_pairs={{0,4},{1,3},{2,6},{3,1},{4,0},{5,7},{6,2},{7,5},{8,12},{9,11},{10,... | collective-permute-start | bytes 393224 | tf_op jit(solution)/shard_map/ppermute | solution.py:30
  24.9 6.1 %collective-permute-start.10 = (bf16[8,8192]{1,0:T(8,128)(2,1)S(1)}, bf16[8,8192]{1,0:T(8,128)(2,1)S(1)}, u32[]{:S(2)}, u32[]{:S(2)}) collective-permute-start(bf16[8,8192]{1,0:T(8,128)(2,1)S(1)} %slice_add_fusion.1), channel_id=1, source_target_pairs={{0,6},{1,7},{2,4},{3,5},{4,2},{5,3},{6,0},{7,1},{8,14},{9,15},{10,... | collective-permute-start | bytes 393224 | tf_op jit(solution)/shard_map/ppermute | solution.py:30
  27.5 6.9 %collective-permute-start.13 = (bf16[8,8192]{1,0:T(8,128)(2,1)S(1)}, bf16[8,8192]{1,0:T(8,128)(2,1)S(1)}, u32[]{:S(2)}, u32[]{:S(2)}) collective-permute-start(bf16[8,8192]{1,0:T(8,128)(2,1)S(1)} %convert_element_type.71), channel_id=1, source_target_pairs={{0,8},{1,9},{2,10},{3,11},{4,12},{5,13},{6,14},{7,15},{8,16},{9,17... | collective-permute-start | bytes 393224 | tf_op jit(solution)/shard_map/ppermute | solution.py:39
  31.1 7.0 %collective-permute-start.14 = (bf16[8,8192]{1,0:T(8,128)(2,1)S(1)}, bf16[8,8192]{1,0:T(8,128)(2,1)S(1)}, u32[]{:S(2)}, u32[]{:S(2)}) collective-permute-start(bf16[8,8192]{1,0:T(8,128)(2,1)S(1)} %fusion.7), channel_id=1, source_target_pairs={{8,0},{9,1},{10,2},{11,3},{12,4},{13,5},{14,6},{15,7},{16,8},{17,9... | collective-permute-start | bytes 393224 | tf_op jit(solution)/shard_map/ppermute | solution.py:45
  34.5 14.5 %copy-start.4 = (bf16[8,8192]{1,0:T(8,128)(2,1)}, bf16[8,8192]{1,0:T(8,128)(2,1)S(1)}, u32[]{:S(2)}) copy-start(bf16[8,8192]{1,0:T(8,128)(2,1)S(1)} %get-tuple-element.41) | copy-start | bytes 393220
  34.5 7.4 %collective-permute-start.19 = (bf16[8,8192]{1,0:T(8,128)(2,1)S(1)}, bf16[8,8192]{1,0:T(8,128)(2,1)S(1)}, u32[]{:S(2)}, u32[]{:S(2)}) collective-permute-start(bf16[8,8192]{1,0:T(8,128)(2,1)S(1)} %get-tuple-element.41), channel_id=1, source_target_pairs={{0,6},{1,7},{2,4},{3,5},{4,2},{5,3},{6,0},{7,1},{8,14},{9,15},{10,... | collective-permute-start | bytes 393224 | tf_op jit(solution)/shard_map/ppermute | solution.py:30
  36.0 7.5 %collective-permute-start.18 = (bf16[8,8192]{1,0:T(8,128)(2,1)S(1)}, bf16[8,8192]{1,0:T(8,128)(2,1)S(1)}, u32[]{:S(2)}, u32[]{:S(2)}) collective-permute-start(bf16[8,8192]{1,0:T(8,128)(2,1)S(1)} %get-tuple-element.41), channel_id=1, source_target_pairs={{0,4},{1,3},{2,6},{3,1},{4,0},{5,7},{6,2},{7,5},{8,12},{9,11},{10,... | collective-permute-start | bytes 393224 | tf_op jit(solution)/shard_map/ppermute | solution.py:30
  36.6 7.0 %collective-permute-start.17 = (bf16[8,8192]{1,0:T(8,128)(2,1)S(1)}, bf16[8,8192]{1,0:T(8,128)(2,1)S(1)}, u32[]{:S(2)}, u32[]{:S(2)}) collective-permute-start(bf16[8,8192]{1,0:T(8,128)(2,1)S(1)} %get-tuple-element.41), channel_id=1, source_target_pairs={{0,2},{1,5},{2,0},{3,7},{4,6},{5,1},{6,4},{7,3},{8,10},{9,13},{10,... | collective-permute-start | bytes 393224 | tf_op jit(solution)/shard_map/ppermute | solution.py:30
  38.2 8.8 %collective-permute-start.16 = (bf16[8,8192]{1,0:T(8,128)(2,1)S(1)}, bf16[8,8192]{1,0:T(8,128)(2,1)S(1)}, u32[]{:S(2)}, u32[]{:S(2)}) collective-permute-start(bf16[8,8192]{1,0:T(8,128)(2,1)S(1)} %select_convert_fusion), channel_id=1, source_target_pairs={{0,4},{1,3},{2,6},{3,1},{4,0},{5,7},{6,2},{7,5},{8,12},{9,11},{10,... | collective-permute-start | bytes 393224 | tf_op jit(solution)/shard_map/ppermute | solution.py:30
  38.7 8.3 %collective-permute-start.15 = (bf16[8,8192]{1,0:T(8,128)(2,1)S(1)}, bf16[8,8192]{1,0:T(8,128)(2,1)S(1)}, u32[]{:S(2)}, u32[]{:S(2)}) collective-permute-start(bf16[8,8192]{1,0:T(8,128)(2,1)S(1)} %select_convert_fusion), channel_id=1, source_target_pairs={{0,2},{1,5},{2,0},{3,7},{4,6},{5,1},{6,4},{7,3},{8,10},{9,13},{10,... | collective-permute-start | bytes 393224 | tf_op jit(solution)/shard_map/ppermute | solution.py:30
  41.9 5.0 %collective-permute-start.21 = (bf16[8,8192]{1,0:T(8,128)(2,1)S(1)}, bf16[8,8192]{1,0:T(8,128)(2,1)S(1)}, u32[]{:S(2)}, u32[]{:S(2)}) collective-permute-start(bf16[8,8192]{1,0:T(8,128)(2,1)S(1)} %collective-permute-done.19), channel_id=1, source_target_pairs={{8,0},{9,1},{10,2},{11,3},{12,4},{13,5},{14,6},{15,7},{16,8},{17,9... | collective-permute-start | bytes 393224 | tf_op jit(solution)/shard_map/ppermute | solution.py:45
  43.6 3.5 %collective-permute-start.20 = (bf16[32,8192]{1,0:T(8,128)(2,1)S(1)}, bf16[32,8192]{1,0:T(8,128)(2,1)S(1)}, u32[]{:S(2)}, u32[]{:S(2)}) collective-permute-start(bf16[32,8192]{1,0:T(8,128)(2,1)S(1)} %pad_maximum_fusion.1), channel_id=1, source_target_pairs={{0,1},{1,0},{2,3},{3,2},{4,5},{5,4},{6,7},{7,6},{8,9},{9,8},{10,11... | collective-permute-start | bytes 1572872 | tf_op jit(solution)/shard_map/ppermute | solution.py:34
  46.9 2.1 %collective-permute-start.23 = (bf16[8,8192]{1,0:T(8,128)(2,1)S(1)}, bf16[8,8192]{1,0:T(8,128)(2,1)S(1)}, u32[]{:S(2)}, u32[]{:S(2)}) collective-permute-start(bf16[8,8192]{1,0:T(8,128)(2,1)S(1)} %broadcast_select_fusion), channel_id=1, source_target_pairs={{0,1},{1,0},{2,3},{3,2},{4,5},{5,4},{6,7},{7,6},{8,9},{9,8},{10,11... | collective-permute-start | bytes 393224 | tf_op jit(solution)/shard_map/ppermute | solution.py:34
  47.1 2.0 %collective-permute-start.22 = (bf16[24,8192]{1,0:T(8,128)(2,1)S(1)}, bf16[24,8192]{1,0:T(8,128)(2,1)S(1)}, u32[]{:S(2)}, u32[]{:S(2)}) collective-permute-start(bf16[24,8192]{1,0:T(8,128)(2,1)S(1)} %pad_maximum_fusion.2), channel_id=1, source_target_pairs={{0,1},{1,0},{2,3},{3,2},{4,5},{5,4},{6,7},{7,6},{8,9},{9,8},{10,11... | collective-permute-start | bytes 1179656 | tf_op jit(solution)/shard_map/ppermute | solution.py:34

commit v14 on v13

--- a/solution.py
+++ b/solution.py
@@ -38,6 +38,11 @@
     size = lax.axis_size(AXIS)
     came = lax.ppermute(value, AXIS, [(i, (i + group) % size) for i in range(size)])
     return jnp.where(first, jnp.zeros_like(came), came)
+
+
+def shifted(value, group):
+    size = lax.axis_size(AXIS)
+    return lax.ppermute(value, AXIS, [(i, i + group) for i in range(size - group)])
 
 
 def lowered(value, final, group):
@@ -238,7 +243,7 @@
     early, late = jnp.concatenate([slab, last], axis=0), jnp.concatenate(most, axis=0)
     early_far, late_far = other_core(early), other_core(late)
     x = jnp.concatenate(
-        [slab, late, last, early_far[:tokens], late_far, early_far[tokens:]], axis=0
+        [after(slab, late), late, last, early_far[:tokens], late_far, early_far[tokens:]], axis=0
     )
     gate, bias = gated(*after((active[0], enc_bias), enc), group * tokens, tokens)
     pre = jnp.dot(x, enc, preferred_element_type=jnp.float32) + bias
@@ -254,7 +259,7 @@
     next_sum = after(summed(nexts, range(1, chips - 1)), owns[-1])
     own_less = summed(owns, range(1, chips - 1)) - target[0].astype(jnp.float32) + crossed
 
-    below = raised(next_sum.astype(jnp.bfloat16), first, group).astype(jnp.float32)
+    below = shifted(next_sum.astype(jnp.bfloat16), group).astype(jnp.float32)
     above = lowered(own_less.astype(jnp.bfloat16), final, group).astype(jnp.float32)
     error = (own_less + below).astype(jnp.bfloat16)
     later = jnp.where(final, 0.0, next_sum + after(above, error)).astype(jnp.bfloat16)

time: 51.3 us -> 50.9 us (level)
  local copies, waits for them, and re-layouts: 1.16 us -> 0.24 us
  starting transfers between devices: 25.1 us -> 25.7 us
    ppermute x0 -> x1, starting transfers between devices: none -> 2.05 us  [shifted(): lax.ppermute(value, AXIS, [(i, i + group) for i in range(size - group)])]
    ppermute x2 -> x1, starting transfers between devices: 2.78 us -> 1.63 us  [raised(): lax.ppermute(value, AXIS, [(i, (i + group) % size) for i in range(size)])]
    ppermute x13, waiting for transfers between devices: 4.95 us -> 6.02 us  [across(): return lax.ppermute(value, AXIS, pairs)]
    ppermute x2 -> x1, waiting for transfers between devices: 2.55 us -> 1.54 us  [raised(): lax.ppermute(value, AXIS, [(i, (i + group) % size) for i in range(size)])]
    unnamed x19 -> x20, local copies, waits for them, and re-layouts: 1.07 us -> 0.14 us
    ppermute x2, starting transfers between devices: 3.73 us -> 4.25 us  [lowered(): lax.ppermute(value, AXIS, [((i + group) % size, i) for i in range(size)])]
  transfers between devices with their start and end apart: 24 -> 24, of which waited for: 11 -> 8; matrix products, arithmetic and copies ran while one was open for 3% -> 2% of each run, Pallas kernels for 14% -> 14%
where the time goes in v14:
time: 50.9 us; the launch traced here: 50.8 us
  starting transfers between devices  25.7 us (50%)
  waiting for transfers between devices  12.4 us (24%)
  Pallas kernels  9.89 us (19%)
  between operations  1.04 us (2%)
  matrix products  0.8 us (2%)
  other arithmetic  0.71 us (1%)
    ppermute x13, starting transfers between devices, across(): return lax.ppermute(value, AXIS, pairs)  16.3 us
    ppermute x13, waiting for transfers between devices, across(): return lax.ppermute(value, AXIS, pairs)  6.02 us
    pallas_call x1, Pallas kernels, loaded(): pl.pallas_call(load_kernel, out_shape=[pltpu.VMEM(enc.shape[1:], enc.dtyp...  4.68 us
    ppermute x2, starting transfers between devices, lowered(): lax.ppermute(value, AXIS, [((i + group) % size, i) for i in range(size)])  4.25 us
    ppermute x2, waiting for transfers between devices, lowered(): lax.ppermute(value, AXIS, [((i + group) % size, i) for i in range(size)])  2.84 us
    ppermute x1, starting transfers between devices, shifted(): lax.ppermute(value, AXIS, [(i, i + group) for i in range(size - group)])  2.05 us
    pallas_call x1, Pallas kernels, grad_all(): pl.pallas_call(functools.partial(grad_all_kernel, tokens), out_shape=jax....  2.03 us
    ppermute x7, waiting for transfers between devices, other_core(): lax.ppermute(value, AXIS, [(i, i ^ 1) for i in range(lax.axis_size(AXIS))])  1.95 us
  transfers between devices with their start and end apart: 24, of which 8 were waited for; matrix products, arithmetic and copies ran while one was open for 2% of the time, Pallas kernels for 14%

profile of v14, /device:TPU:0, one launch (start us, length us, event | category | flops | bytes accessed | tf_op | source)
XLA Modules:
  0.0 50.8 jit_solution(12405682491663541109)
XLA Ops:
  0.7 3.0 %collective-permute-start = (bf16[8,8192]{1,0:T(8,128)(2,1)}, bf16[8,8192]{1,0:T(8,128)(2,1)S(1)}, u32[]{:S(2)}, u32[]{:S(2)}) collective-permute-start(bf16[8,8192]{1,0:T(8,128)(2,1)} %bitcast.14), channel_id=1, source_target_pairs={{0,2},{1,5},{2,0},{3,7},{4,6},{5,1},{6,4},{7,3},{8,10},{9,13},{10,... | collective-permute-start | bytes 393224 | tf_op jit(solution)/shard_map/ppermute | solution.py:30
  3.7 1.5 %collective-permute-start.2 = (bf16[8,8192]{1,0:T(8,128)(2,1)}, bf16[8,8192]{1,0:T(8,128)(2,1)S(1)}, u32[]{:S(2)}, u32[]{:S(2)}) collective-permute-start(bf16[8,8192]{1,0:T(8,128)(2,1)} %bitcast.15), channel_id=1, source_target_pairs={{0,6},{1,7},{2,4},{3,5},{4,2},{5,3},{6,0},{7,1},{8,14},{9,15},{10,... | collective-permute-start | bytes 393224 | tf_op jit(solution)/shard_map/ppermute | solution.py:30
  5.2 0.0 collective-permute-start.1
  5.2 4.7 %load_weights.1 = (bf16[8192,256]{1,0:T(8,128)(2,1)S(1)}, bf16[256,8192]{1,0:T(8,128)(2,1)S(1)}, bf16[256,8192]{1,0:T(8,128)(2,1)S(1)}) custom-call(bf16[1,8192,256]{2,1,0:T(8,128)(2,1)} %enc_hbm.1, bf16[1,2,256,8192]{3,2,1,0:T(8,128)(2,1)} %dec_hbm.1), custom_call_target="tpu_custom_call" | custom-call | bytes 25165824 | tf_op jit(solution)/shard_map/load_weights/pallas_call | solution.py:87
  9.9 0.0 copy-done
  9.9 0.0 copy-done.1
  9.9 0.1 gate.1
  10.0 0.0 collective-permute-done
  10.1 1.8 %collective-permute-done.1 = bf16[8,8192]{1,0:T(8,128)(2,1)S(1)} collective-permute-done((bf16[8,8192]{1,0:T(8,128)(2,1)}, bf16[8,8192]{1,0:T(8,128)(2,1)S(1)}, u32[]{:S(2)}, u32[]{:S(2)}) %collective-permute-start.1) | collective-permute-done | bytes 131104 | tf_op jit(solution)/shard_map/ppermute | solution.py:30
  11.9 0.1 collective-permute-start.4
  11.9 0.5 %collective-permute-done.2 = bf16[8,8192]{1,0:T(8,128)(2,1)S(1)} collective-permute-done((bf16[8,8192]{1,0:T(8,128)(2,1)}, bf16[8,8192]{1,0:T(8,128)(2,1)S(1)}, u32[]{:S(2)}, u32[]{:S(2)}) %collective-permute-start.2) | collective-permute-done | bytes 131104 | tf_op jit(solution)/shard_map/ppermute | solution.py:30
  12.5 0.1 collective-permute-start.3
  12.7 1.4 %collective-permute-done.3 = bf16[16,8192]{1,0:T(8,128)(2,1)S(1)} collective-permute-done((bf16[16,8192]{1,0:T(8,128)(2,1)S(1)}, bf16[16,8192]{1,0:T(8,128)(2,1)S(1)}, u32[]{:S(2)}, u32[]{:S(2)}) %collective-permute-start.3) | collective-permute-done | bytes 262176 | tf_op jit(solution)/shard_map/ppermute | solution.py:34
  14.1 0.0 collective-permute-done.4
  14.2 0.8 %fusion.2.codes_ref = bf16[64,256]{1,0:T(8,128)(2,1)S(1)} fusion(f32[64,256]{1,0:T(8,128)S(1)} %get-tuple-element.28, f32[64,256]{1,0:T(8,128)S(1)} %get-tuple-element.27, bf16[64,8192]{1,0:T(8,128)(2,1)S(1)} %slice_dynamic-update-slice_fusion, bf16[8192,256]{1,0:T(8,128)(2,1)S(1)} %get-tuple-element.24), kind=kOutput, calls=%fused_computation.3 | convolution fusion | flops 268500992 | bytes 5406720 | tf_op jit(solution)/shard_map/dot_general | solution.py:249
  15.0 0.8 %decode.3 = (f32[32,8192]{1,0:T(8,128)S(1)}, bf16[32,8192]{1,0:T(8,128)(2,1)S(1)}) custom-call(bf16[64,256]{1,0:T(8,128)(2,1)S(1)} %fusion.2.codes_ref, bf16[256,8192]{1,0:T(8,128)(2,1)S(1)} %get-tuple-element.33.dec_ref), custom_call_target="tpu_custom_call" | custom-call | flops 268435456 | bytes 4194304 | tf_op jit(solution)/shard_map/decode/pallas_call | solution.py:164
  15.8 0.2 collective-permute-start.8
  16.0 0.8 %decode.2 = (f32[32,8192]{1,0:T(8,128)S(1)}, bf16[32,8192]{1,0:T(8,128)(2,1)S(1)}) custom-call(bf16[64,256]{1,0:T(8,128)(2,1)S(1)} %fusion.2.codes_ref, bf16[256,8192]{1,0:T(8,128)(2,1)S(1)} %get-tuple-element.29.dec_ref), custom_call_target="tpu_custom_call" | custom-call | flops 268435456 | bytes 4194304 | tf_op jit(solution)/shard_map/decode/pallas_call | solution.py:164
  16.9 0.4 collective-permute-start.5
  17.3 0.5 collective-permute-done.8
  17.8 0.1 fusion.9
  18.0 1.6 %collective-permute-start.9 = (bf16[8,8192]{1,0:T(8,128)(2,1)S(1)}, bf16[8,8192]{1,0:T(8,128)(2,1)S(1)}, u32[]{:S(2)}, u32[]{:S(2)}) collective-permute-start(bf16[8,8192]{1,0:T(8,128)(2,1)S(1)} %get-tuple-element.50), channel_id=1, source_target_pairs={{0,8},{1,9},{2,10},{3,11},{4,12},{5,13},{6,14},{7,15},{8,16},{9,17... | collective-permute-start | bytes 393224 | tf_op jit(solution)/shard_map/ppermute | solution.py:39
  19.6 0.7 %collective-permute-start.12 = (bf16[8,8192]{1,0:T(8,128)(2,1)S(1)}, bf16[8,8192]{1,0:T(8,128)(2,1)S(1)}, u32[]{:S(2)}, u32[]{:S(2)}) collective-permute-start(bf16[8,8192]{1,0:T(8,128)(2,1)S(1)} %get-tuple-element.51), channel_id=1, source_target_pairs={{0,4},{1,3},{2,6},{3,1},{4,0},{5,7},{6,2},{7,5},{8,12},{9,11},{10,... | collective-permute-start | bytes 393224 | tf_op jit(solution)/shard_map/ppermute | solution.py:30
  20.3 1.5 %collective-permute-start.11 = (bf16[8,8192]{1,0:T(8,128)(2,1)S(1)}, bf16[8,8192]{1,0:T(8,128)(2,1)S(1)}, u32[]{:S(2)}, u32[]{:S(2)}) collective-permute-start(bf16[8,8192]{1,0:T(8,128)(2,1)S(1)} %get-tuple-element.52), channel_id=1, source_target_pairs={{0,2},{1,5},{2,0},{3,7},{4,6},{5,1},{6,4},{7,3},{8,10},{9,13},{10,... | collective-permute-start | bytes 393224 | tf_op jit(solution)/shard_map/ppermute | solution.py:30
  21.8 0.0 collective-permute-done.5
  21.8 0.1 fusion.8
  22.0 0.6 %collective-permute-start.6 = (bf16[8,8192]{1,0:T(8,128)(2,1)S(1)}, bf16[8,8192]{1,0:T(8,128)(2,1)S(1)}, u32[]{:S(2)}, u32[]{:S(2)}) collective-permute-start(bf16[8,8192]{1,0:T(8,128)(2,1)S(1)} %get-tuple-element.48), channel_id=1, source_target_pairs={{0,2},{1,5},{2,0},{3,7},{4,6},{5,1},{6,4},{7,3},{8,10},{9,13},{10,... | collective-permute-start | bytes 393224 | tf_op jit(solution)/shard_map/ppermute | solution.py:30
  22.6 1.3 %collective-permute-start.7 = (bf16[8,8192]{1,0:T(8,128)(2,1)S(1)}, bf16[8,8192]{1,0:T(8,128)(2,1)S(1)}, u32[]{:S(2)}, u32[]{:S(2)}) collective-permute-start(bf16[8,8192]{1,0:T(8,128)(2,1)S(1)} %get-tuple-element.49), channel_id=1, source_target_pairs={{0,4},{1,3},{2,6},{3,1},{4,0},{5,7},{6,2},{7,5},{8,12},{9,11},{10,... | collective-permute-start | bytes 393224 | tf_op jit(solution)/shard_map/ppermute | solution.py:30
  23.9 1.5 %collective-permute-done.9 = bf16[8,8192]{1,0:T(8,128)(2,1)S(1)} collective-permute-done((bf16[8,8192]{1,0:T(8,128)(2,1)S(1)}, bf16[8,8192]{1,0:T(8,128)(2,1)S(1)}, u32[]{:S(2)}, u32[]{:S(2)}) %collective-permute-start.9) | collective-permute-done | bytes 131104 | tf_op jit(solution)/shard_map/ppermute | solution.py:39
  25.5 1.8 %collective-permute-start.10 = (bf16[8,8192]{1,0:T(8,128)(2,1)S(1)}, bf16[8,8192]{1,0:T(8,128)(2,1)S(1)}, u32[]{:S(2)}, u32[]{:S(2)}) collective-permute-start(bf16[8,8192]{1,0:T(8,128)(2,1)S(1)} %slice_add_fusion.1), channel_id=1, source_target_pairs={{0,6},{1,7},{2,4},{3,5},{4,2},{5,3},{6,0},{7,1},{8,14},{9,15},{10,... | collective-permute-start | bytes 393224 | tf_op jit(solution)/shard_map/ppermute | solution.py:30
  27.3 0.0 collective-permute-done.12
  27.3 0.0 collective-permute-done.11
  27.4 2.0 %collective-permute-start.13 = (bf16[8,8192]{1,0:T(8,128)(2,1)S(1)}, bf16[8,8192]{1,0:T(8,128)(2,1)S(1)}, u32[]{:S(2)}, u32[]{:S(2)}) collective-permute-start(bf16[8,8192]{1,0:T(8,128)(2,1)S(1)} %convert_element_type.71), channel_id=1, source_target_pairs={{0,8},{1,9},{2,10},{3,11},{4,12},{5,13},{6,14},{7,15},{8,16},{9,17... | collective-permute-start | bytes 393224 | tf_op jit(solution)/shard_map/ppermute | solution.py:45
  29.4 0.0 collective-permute-done.6
  29.4 0.0 collective-permute-done.7
  29.4 2.2 %collective-permute-done.10 = bf16[8,8192]{1,0:T(8,128)(2,1)S(1)} collective-permute-done((bf16[8,8192]{1,0:T(8,128)(2,1)S(1)}, bf16[8,8192]{1,0:T(8,128)(2,1)S(1)}, u32[]{:S(2)}, u32[]{:S(2)}) %collective-permute-start.10) | collective-permute-done | bytes 131104 | tf_op jit(solution)/shard_map/ppermute | solution.py:30
  31.6 0.0 copy-done.2
  31.6 0.1 fusion.7
  31.7 2.3 %collective-permute-start.14 = (bf16[8,8192]{1,0:T(8,128)(2,1)S(1)}, bf16[8,8192]{1,0:T(8,128)(2,1)S(1)}, u32[]{:S(2)}, u32[]{:S(2)}) collective-permute-start(bf16[8,8192]{1,0:T(8,128)(2,1)S(1)} %fusion.7), channel_id=1, source_target_pairs={{8,0},{9,1},{10,2},{11,3},{12,4},{13,5},{14,6},{15,7},{16,8},{17,9... | collective-permute-start | bytes 393224 | tf_op jit(solution)/shard_map/ppermute | solution.py:50
  34.0 0.0 collective-permute-done.13
  34.0 0.1 constant_dynamic-update-slice_fusion.11
  34.1 0.0 copy-start.4
  34.1 1.7 %collective-permute-start.19 = (bf16[8,8192]{1,0:T(8,128)(2,1)S(1)}, bf16[8,8192]{1,0:T(8,128)(2,1)S(1)}, u32[]{:S(2)}, u32[]{:S(2)}) collective-permute-start(bf16[8,8192]{1,0:T(8,128)(2,1)S(1)} %get-tuple-element.43), channel_id=1, source_target_pairs={{0,6},{1,7},{2,4},{3,5},{4,2},{5,3},{6,0},{7,1},{8,14},{9,15},{10,... | collective-permute-start | bytes 393224 | tf_op jit(solution)/shard_map/ppermute | solution.py:30
  35.9 1.3 %collective-permute-start.18 = (bf16[8,8192]{1,0:T(8,128)(2,1)S(1)}, bf16[8,8192]{1,0:T(8,128)(2,1)S(1)}, u32[]{:S(2)}, u32[]{:S(2)}) collective-permute-start(bf16[8,8192]{1,0:T(8,128)(2,1)S(1)} %get-tuple-element.43), channel_id=1, source_target_pairs={{0,4},{1,3},{2,6},{3,1},{4,0},{5,7},{6,2},{7,5},{8,12},{9,11},{10,... | collective-permute-start | bytes 393224 | tf_op jit(solution)/shard_map/ppermute | solution.py:30
  37.1 0.6 %collective-permute-start.17 = (bf16[8,8192]{1,0:T(8,128)(2,1)S(1)}, bf16[8,8192]{1,0:T(8,128)(2,1)S(1)}, u32[]{:S(2)}, u32[]{:S(2)}) collective-permute-start(bf16[8,8192]{1,0:T(8,128)(2,1)S(1)} %get-tuple-element.43), channel_id=1, source_target_pairs={{0,2},{1,5},{2,0},{3,7},{4,6},{5,1},{6,4},{7,3},{8,10},{9,13},{10,... | collective-permute-start | bytes 393224 | tf_op jit(solution)/shard_map/ppermute | solution.py:30
  37.7 0.0 collective-permute-done.14
  37.8 0.6 %collective-permute-start.16 = (bf16[8,8192]{1,0:T(8,128)(2,1)S(1)}, bf16[8,8192]{1,0:T(8,128)(2,1)S(1)}, u32[]{:S(2)}, u32[]{:S(2)}) collective-permute-start(bf16[8,8192]{1,0:T(8,128)(2,1)S(1)} %select_convert_fusion), channel_id=1, source_target_pairs={{0,4},{1,3},{2,6},{3,1},{4,0},{5,7},{6,2},{7,5},{8,12},{9,11},{10,... | collective-permute-start | bytes 393224 | tf_op jit(solution)/shard_map/ppermute | solution.py:30
  38.4 1.7 %collective-permute-start.15 = (bf16[8,8192]{1,0:T(8,128)(2,1)S(1)}, bf16[8,8192]{1,0:T(8,128)(2,1)S(1)}, u32[]{:S(2)}, u32[]{:S(2)}) collective-permute-start(bf16[8,8192]{1,0:T(8,128)(2,1)S(1)} %select_convert_fusion), channel_id=1, source_target_pairs={{0,2},{1,5},{2,0},{3,7},{4,6},{5,1},{6,4},{7,3},{8,10},{9,13},{10,... | collective-permute-start | bytes 393224 | tf_op jit(solution)/shard_map/ppermute | solution.py:30
  40.0 1.5 %collective-permute-done.19 = bf16[8,8192]{1,0:T(8,128)(2,1)S(1)} collective-permute-done((bf16[8,8192]{1,0:T(8,128)(2,1)S(1)}, bf16[8,8192]{1,0:T(8,128)(2,1)S(1)}, u32[]{:S(2)}, u32[]{:S(2)}) %collective-permute-start.19) | collective-permute-done | bytes 131104 | tf_op jit(solution)/shard_map/ppermute | solution.py:30
  41.5 1.9 %collective-permute-start.21 = (bf16[8,8192]{1,0:T(8,128)(2,1)S(1)}, bf16[8,8192]{1,0:T(8,128)(2,1)S(1)}, u32[]{:S(2)}, u32[]{:S(2)}) collective-permute-start(bf16[8,8192]{1,0:T(8,128)(2,1)S(1)} %collective-permute-done.19), channel_id=1, source_target_pairs={{8,0},{9,1},{10,2},{11,3},{12,4},{13,5},{14,6},{15,7},{16,8},{17,9... | collective-permute-start | bytes 393224 | tf_op jit(solution)/shard_map/ppermute | solution.py:50
  43.5 0.0 collective-permute-done.18
  43.5 0.0 collective-permute-done.17
  43.5 0.1 collective-permute-start.20
  43.7 2.8 %collective-permute-done.21 = bf16[8,8192]{1,0:T(8,128)(2,1)S(1)} collective-permute-done((bf16[8,8192]{1,0:T(8,128)(2,1)S(1)}, bf16[8,8192]{1,0:T(8,128)(2,1)S(1)}, u32[]{:S(2)}, u32[]{:S(2)}) %collective-permute-start.21) | collective-permute-done | bytes 131104 | tf_op jit(solution)/shard_map/ppermute | solution.py:50
  46.5 0.1 collective-permute-start.23
  46.6 0.0 collective-permute-done.16
  46.6 0.0 collective-permute-done.15
  46.7 0.0 collective-permute-done.20
  46.7 0.5 %collective-permute-start.22 = (bf16[24,8192]{1,0:T(8,128)(2,1)S(1)}, bf16[24,8192]{1,0:T(8,128)(2,1)S(1)}, u32[]{:S(2)}, u32[]{:S(2)}) collective-permute-start(bf16[24,8192]{1,0:T(8,128)(2,1)S(1)} %pad_maximum_fusion.2), channel_id=1, source_target_pairs={{0,1},{1,0},{2,3},{3,2},{4,5},{5,4},{6,7},{7,6},{8,9},{9,8},{10,11... | collective-permute-start | bytes 1179656 | tf_op jit(solution)/shard_map/ppermute | solution.py:34
  47.2 1.4 %grad_own.1 = (f32[64,256]{1,0:T(8,128)S(1)}, f32[8,128]{1,0:T(8,128)}) custom-call(bf16[64,8192]{1,0:T(8,128)(2,1)S(1)} %constant_dynamic-update-slice_fusion.7.rows_ref, bf16[256,8192]{1,0:T(8,128)(2,1)S(1)} %get-tuple-element.29.dec_ref), custom_call_target="tpu_custom_call" | custom-call | flops 268435456 | bytes 4194304 | tf_op jit(solution)/shard_map/grad_own/pallas_call | solution.py:199
  48.6 0.0 collective-permute-done.23
  48.7 0.0 collective-permute-done.22
  48.7 0.1 pad_maximum_fusion.rows_ref
  48.7 2.0 %grad_all.1 = f32[1,64,256]{2,1,0:T(8,128)} custom-call(bf16[64,8192]{1,0:T(8,128)(2,1)S(1)} %pad_maximum_fusion.rows_ref, bf16[256,8192]{1,0:T(8,128)(2,1)S(1)} %get-tuple-element.33.dec_ref, f32[64,256]{1,0:T(8,128)S(1)} %get-tuple-element.41.own_ref), custom_call_target="tpu_custom_call" | custom-call | flops 268435456 | bytes 4194304 | tf_op jit(solution)/shard_map/grad_all/pallas_call | solution.py:211
  (30 shorter events, 0.5 us)
Async XLA Ops:
  0.6 9.3 %copy-start = (s32[1,2,2]{2,1,0:T(2,128)S(1)}, s32[1,2,2]{2,1,0:T(2,128)}, u32[]{:S(2)}) copy-start(s32[1,2,2]{2,1,0:T(2,128)} %param.9) | copy-start | bytes 52
  0.6 9.3 %copy-start.1 = (bf16[1,256]{1,0:T(2,128)(2,1)S(1)}, bf16[1,256]{1,0:T(2,128)(2,1)}, u32[]{:S(2)}) copy-start(bf16[1,256]{1,0:T(2,128)(2,1)} %bias_ref) | copy-start | bytes 1540
  0.7 11.8 %copy-start.3 = (bf16[1,8,8192]{2,1,0:T(8,128)(2,1)S(1)}, bf16[1,8,8192]{2,1,0:T(8,128)(2,1)}, u32[]{:S(2)}) copy-start(bf16[1,8,8192]{2,1,0:T(8,128)(2,1)} %param.6) | copy-start | bytes 393220
  0.7 9.4 %collective-permute-start = (bf16[8,8192]{1,0:T(8,128)(2,1)}, bf16[8,8192]{1,0:T(8,128)(2,1)S(1)}, u32[]{:S(2)}, u32[]{:S(2)}) collective-permute-start(bf16[8,8192]{1,0:T(8,128)(2,1)} %bitcast.14), channel_id=1, source_target_pairs={{0,2},{1,5},{2,0},{3,7},{4,6},{5,1},{6,4},{7,3},{8,10},{9,13},{10,... | collective-permute-start | bytes 393224 | tf_op jit(solution)/shard_map/ppermute | solution.py:30
  3.7 8.8 %collective-permute-start.2 = (bf16[8,8192]{1,0:T(8,128)(2,1)}, bf16[8,8192]{1,0:T(8,128)(2,1)S(1)}, u32[]{:S(2)}, u32[]{:S(2)}) collective-permute-start(bf16[8,8192]{1,0:T(8,128)(2,1)} %bitcast.15), channel_id=1, source_target_pairs={{0,6},{1,7},{2,4},{3,5},{4,2},{5,3},{6,0},{7,1},{8,14},{9,15},{10,... | collective-permute-start | bytes 393224 | tf_op jit(solution)/shard_map/ppermute | solution.py:30
  5.2 6.7 %collective-permute-start.1 = (bf16[8,8192]{1,0:T(8,128)(2,1)}, bf16[8,8192]{1,0:T(8,128)(2,1)S(1)}, u32[]{:S(2)}, u32[]{:S(2)}) collective-permute-start(bf16[8,8192]{1,0:T(8,128)(2,1)} %bitcast.16), channel_id=1, source_target_pairs={{0,4},{1,3},{2,6},{3,1},{4,0},{5,7},{6,2},{7,5},{8,12},{9,11},{10,... | collective-permute-start | bytes 393224 | tf_op jit(solution)/shard_map/ppermute | solution.py:30
  11.9 2.3 %collective-permute-start.4 = (bf16[16,8192]{1,0:T(8,128)(2,1)S(1)}, bf16[16,8192]{1,0:T(8,128)(2,1)S(1)}, u32[]{:S(2)}, u32[]{:S(2)}) collective-permute-start(bf16[16,8192]{1,0:T(8,128)(2,1)S(1)} %constant_dynamic-update-slice_fusion), channel_id=1, source_target_pairs={{0,1},{1,0},{2,3},{3,2},{4,5},{5,4},{6,7},{7,6},{8,9},{9,8},{10,11... | collective-permute-start | bytes 786440 | tf_op jit(solution)/shard_map/ppermute | solution.py:34
  12.5 1.6 %collective-permute-start.3 = (bf16[16,8192]{1,0:T(8,128)(2,1)S(1)}, bf16[16,8192]{1,0:T(8,128)(2,1)S(1)}, u32[]{:S(2)}, u32[]{:S(2)}) collective-permute-start(bf16[16,8192]{1,0:T(8,128)(2,1)S(1)} %pad_maximum_fusion.3), channel_id=1, source_target_pairs={{0,1},{1,0},{2,3},{3,2},{4,5},{5,4},{6,7},{7,6},{8,9},{9,8},{10,11... | collective-permute-start | bytes 786440 | tf_op jit(solution)/shard_map/ppermute | solution.py:34
  15.8 2.0 %collective-permute-start.8 = (bf16[32,8192]{1,0:T(8,128)(2,1)S(1)}, bf16[32,8192]{1,0:T(8,128)(2,1)S(1)}, u32[]{:S(2)}, u32[]{:S(2)}) collective-permute-start(bf16[32,8192]{1,0:T(8,128)(2,1)S(1)} %get-tuple-element.35), channel_id=1, source_target_pairs={{0,1},{1,0},{2,3},{3,2},{4,5},{5,4},{6,7},{7,6},{8,9},{9,8},{10,11... | collective-permute-start | bytes 1572872 | tf_op jit(solution)/shard_map/ppermute | solution.py:34
  16.9 4.9 %collective-permute-start.5 = (bf16[32,8192]{1,0:T(8,128)(2,1)S(1)}, bf16[32,8192]{1,0:T(8,128)(2,1)S(1)}, u32[]{:S(2)}, u32[]{:S(2)}) collective-permute-start(bf16[32,8192]{1,0:T(8,128)(2,1)S(1)} %get-tuple-element.31), channel_id=1, source_target_pairs={{0,1},{1,0},{2,3},{3,2},{4,5},{5,4},{6,7},{7,6},{8,9},{9,8},{10,11... | collective-permute-start | bytes 1572872 | tf_op jit(solution)/shard_map/ppermute | solution.py:34
  17.8 13.8 %copy-start.2 = (bf16[1,8,8192]{2,1,0:T(8,128)(2,1)S(1)}, bf16[1,8,8192]{2,1,0:T(8,128)(2,1)}, u32[]{:S(2)}) copy-start(bf16[1,8,8192]{2,1,0:T(8,128)(2,1)} %param.11) | copy-start | bytes 393220
  18.0 7.5 %collective-permute-start.9 = (bf16[8,8192]{1,0:T(8,128)(2,1)S(1)}, bf16[8,8192]{1,0:T(8,128)(2,1)S(1)}, u32[]{:S(2)}, u32[]{:S(2)}) collective-permute-start(bf16[8,8192]{1,0:T(8,128)(2,1)S(1)} %get-tuple-element.50), channel_id=1, source_target_pairs={{0,8},{1,9},{2,10},{3,11},{4,12},{5,13},{6,14},{7,15},{8,16},{9,17... | collective-permute-start | bytes 393224 | tf_op jit(solution)/shard_map/ppermute | solution.py:39
  19.6 7.7 %collective-permute-start.12 = (bf16[8,8192]{1,0:T(8,128)(2,1)S(1)}, bf16[8,8192]{1,0:T(8,128)(2,1)S(1)}, u32[]{:S(2)}, u32[]{:S(2)}) collective-permute-start(bf16[8,8192]{1,0:T(8,128)(2,1)S(1)} %get-tuple-element.51), channel_id=1, source_target_pairs={{0,4},{1,3},{2,6},{3,1},{4,0},{5,7},{6,2},{7,5},{8,12},{9,11},{10,... | collective-permute-start | bytes 393224 | tf_op jit(solution)/shard_map/ppermute | solution.py:30
  20.3 7.0 %collective-permute-start.11 = (bf16[8,8192]{1,0:T(8,128)(2,1)S(1)}, bf16[8,8192]{1,0:T(8,128)(2,1)S(1)}, u32[]{:S(2)}, u32[]{:S(2)}) collective-permute-start(bf16[8,8192]{1,0:T(8,128)(2,1)S(1)} %get-tuple-element.52), channel_id=1, source_target_pairs={{0,2},{1,5},{2,0},{3,7},{4,6},{5,1},{6,4},{7,3},{8,10},{9,13},{10,... | collective-permute-start | bytes 393224 | tf_op jit(solution)/shard_map/ppermute | solution.py:30
  22.0 7.5 %collective-permute-start.6 = (bf16[8,8192]{1,0:T(8,128)(2,1)S(1)}, bf16[8,8192]{1,0:T(8,128)(2,1)S(1)}, u32[]{:S(2)}, u32[]{:S(2)}) collective-permute-start(bf16[8,8192]{1,0:T(8,128)(2,1)S(1)} %get-tuple-element.48), channel_id=1, source_target_pairs={{0,2},{1,5},{2,0},{3,7},{4,6},{5,1},{6,4},{7,3},{8,10},{9,13},{10,... | collective-permute-start | bytes 393224 | tf_op jit(solution)/shard_map/ppermute | solution.py:30
  22.6 6.9 %collective-permute-start.7 = (bf16[8,8192]{1,0:T(8,128)(2,1)S(1)}, bf16[8,8192]{1,0:T(8,128)(2,1)S(1)}, u32[]{:S(2)}, u32[]{:S(2)}) collective-permute-start(bf16[8,8192]{1,0:T(8,128)(2,1)S(1)} %get-tuple-element.49), channel_id=1, source_target_pairs={{0,4},{1,3},{2,6},{3,1},{4,0},{5,7},{6,2},{7,5},{8,12},{9,11},{10,... | collective-permute-start | bytes 393224 | tf_op jit(solution)/shard_map/ppermute | solution.py:30
  25.5 6.2 %collective-permute-start.10 = (bf16[8,8192]{1,0:T(8,128)(2,1)S(1)}, bf16[8,8192]{1,0:T(8,128)(2,1)S(1)}, u32[]{:S(2)}, u32[]{:S(2)}) collective-permute-start(bf16[8,8192]{1,0:T(8,128)(2,1)S(1)} %slice_add_fusion.1), channel_id=1, source_target_pairs={{0,6},{1,7},{2,4},{3,5},{4,2},{5,3},{6,0},{7,1},{8,14},{9,15},{10,... | collective-permute-start | bytes 393224 | tf_op jit(solution)/shard_map/ppermute | solution.py:30
  27.4 6.7 %collective-permute-start.13 = (bf16[8,8192]{1,0:T(8,128)(2,1)S(1)}, bf16[8,8192]{1,0:T(8,128)(2,1)S(1)}, u32[]{:S(2)}, u32[]{:S(2)}) collective-permute-start(bf16[8,8192]{1,0:T(8,128)(2,1)S(1)} %convert_element_type.71), channel_id=1, source_target_pairs={{0,8},{1,9},{2,10},{3,11},{4,12},{5,13},{6,14},{7,15},{8,16},{9,17... | collective-permute-start | bytes 393224 | tf_op jit(solution)/shard_map/ppermute | solution.py:45
  31.7 6.0 %collective-permute-start.14 = (bf16[8,8192]{1,0:T(8,128)(2,1)S(1)}, bf16[8,8192]{1,0:T(8,128)(2,1)S(1)}, u32[]{:S(2)}, u32[]{:S(2)}) collective-permute-start(bf16[8,8192]{1,0:T(8,128)(2,1)S(1)} %fusion.7), channel_id=1, source_target_pairs={{8,0},{9,1},{10,2},{11,3},{12,4},{13,5},{14,6},{15,7},{16,8},{17,9... | collective-permute-start | bytes 393224 | tf_op jit(solution)/shard_map/ppermute | solution.py:50
  34.1 14.5 %copy-start.4 = (bf16[8,8192]{1,0:T(8,128)(2,1)}, bf16[8,8192]{1,0:T(8,128)(2,1)S(1)}, u32[]{:S(2)}) copy-start(bf16[8,8192]{1,0:T(8,128)(2,1)S(1)} %get-tuple-element.43) | copy-start | bytes 393220
  34.1 7.4 %collective-permute-start.19 = (bf16[8,8192]{1,0:T(8,128)(2,1)S(1)}, bf16[8,8192]{1,0:T(8,128)(2,1)S(1)}, u32[]{:S(2)}, u32[]{:S(2)}) collective-permute-start(bf16[8,8192]{1,0:T(8,128)(2,1)S(1)} %get-tuple-element.43), channel_id=1, source_target_pairs={{0,6},{1,7},{2,4},{3,5},{4,2},{5,3},{6,0},{7,1},{8,14},{9,15},{10,... | collective-permute-start | bytes 393224 | tf_op jit(solution)/shard_map/ppermute | solution.py:30
  35.9 7.6 %collective-permute-start.18 = (bf16[8,8192]{1,0:T(8,128)(2,1)S(1)}, bf16[8,8192]{1,0:T(8,128)(2,1)S(1)}, u32[]{:S(2)}, u32[]{:S(2)}) collective-permute-start(bf16[8,8192]{1,0:T(8,128)(2,1)S(1)} %get-tuple-element.43), channel_id=1, source_target_pairs={{0,4},{1,3},{2,6},{3,1},{4,0},{5,7},{6,2},{7,5},{8,12},{9,11},{10,... | collective-permute-start | bytes 393224 | tf_op jit(solution)/shard_map/ppermute | solution.py:30
  37.1 6.4 %collective-permute-start.17 = (bf16[8,8192]{1,0:T(8,128)(2,1)S(1)}, bf16[8,8192]{1,0:T(8,128)(2,1)S(1)}, u32[]{:S(2)}, u32[]{:S(2)}) collective-permute-start(bf16[8,8192]{1,0:T(8,128)(2,1)S(1)} %get-tuple-element.43), channel_id=1, source_target_pairs={{0,2},{1,5},{2,0},{3,7},{4,6},{5,1},{6,4},{7,3},{8,10},{9,13},{10,... | collective-permute-start | bytes 393224 | tf_op jit(solution)/shard_map/ppermute | solution.py:30
  37.8 8.8 %collective-permute-start.16 = (bf16[8,8192]{1,0:T(8,128)(2,1)S(1)}, bf16[8,8192]{1,0:T(8,128)(2,1)S(1)}, u32[]{:S(2)}, u32[]{:S(2)}) collective-permute-start(bf16[8,8192]{1,0:T(8,128)(2,1)S(1)} %select_convert_fusion), channel_id=1, source_target_pairs={{0,4},{1,3},{2,6},{3,1},{4,0},{5,7},{6,2},{7,5},{8,12},{9,11},{10,... | collective-permute-start | bytes 393224 | tf_op jit(solution)/shard_map/ppermute | solution.py:30
  38.4 8.2 %collective-permute-start.15 = (bf16[8,8192]{1,0:T(8,128)(2,1)S(1)}, bf16[8,8192]{1,0:T(8,128)(2,1)S(1)}, u32[]{:S(2)}, u32[]{:S(2)}) collective-permute-start(bf16[8,8192]{1,0:T(8,128)(2,1)S(1)} %select_convert_fusion), channel_id=1, source_target_pairs={{0,2},{1,5},{2,0},{3,7},{4,6},{5,1},{6,4},{7,3},{8,10},{9,13},{10,... | collective-permute-start | bytes 393224 | tf_op jit(solution)/shard_map/ppermute | solution.py:30
  41.5 5.0 %collective-permute-start.21 = (bf16[8,8192]{1,0:T(8,128)(2,1)S(1)}, bf16[8,8192]{1,0:T(8,128)(2,1)S(1)}, u32[]{:S(2)}, u32[]{:S(2)}) collective-permute-start(bf16[8,8192]{1,0:T(8,128)(2,1)S(1)} %collective-permute-done.19), channel_id=1, source_target_pairs={{8,0},{9,1},{10,2},{11,3},{12,4},{13,5},{14,6},{15,7},{16,8},{17,9... | collective-permute-start | bytes 393224 | tf_op jit(solution)/shard_map/ppermute | solution.py:50
  43.5 3.1 %collective-permute-start.20 = (bf16[32,8192]{1,0:T(8,128)(2,1)S(1)}, bf16[32,8192]{1,0:T(8,128)(2,1)S(1)}, u32[]{:S(2)}, u32[]{:S(2)}) collective-permute-start(bf16[32,8192]{1,0:T(8,128)(2,1)S(1)} %pad_maximum_fusion.1), channel_id=1, source_target_pairs={{0,1},{1,0},{2,3},{3,2},{4,5},{5,4},{6,7},{7,6},{8,9},{9,8},{10,11... | collective-permute-start | bytes 1572872 | tf_op jit(solution)/shard_map/ppermute | solution.py:34
  46.5 2.1 %collective-permute-start.23 = (bf16[8,8192]{1,0:T(8,128)(2,1)S(1)}, bf16[8,8192]{1,0:T(8,128)(2,1)S(1)}, u32[]{:S(2)}, u32[]{:S(2)}) collective-permute-start(bf16[8,8192]{1,0:T(8,128)(2,1)S(1)} %broadcast_select_fusion), channel_id=1, source_target_pairs={{0,1},{1,0},{2,3},{3,2},{4,5},{5,4},{6,7},{7,6},{8,9},{9,8},{10,11... | collective-permute-start | bytes 393224 | tf_op jit(solution)/shard_map/ppermute | solution.py:34
  46.7 2.0 %collective-permute-start.22 = (bf16[24,8192]{1,0:T(8,128)(2,1)S(1)}, bf16[24,8192]{1,0:T(8,128)(2,1)S(1)}, u32[]{:S(2)}, u32[]{:S(2)}) collective-permute-start(bf16[24,8192]{1,0:T(8,128)(2,1)S(1)} %pad_maximum_fusion.2), channel_id=1, source_target_pairs={{0,1},{1,0},{2,3},{3,2},{4,5},{5,4},{6,7},{7,6},{8,9},{9,8},{10,11... | collective-permute-start | bytes 1179656 | tf_op jit(solution)/shard_map/ppermute | solution.py:34

commit v15 on v13

--- a/solution.py
+++ b/solution.py
@@ -40,10 +40,9 @@
     return jnp.where(first, jnp.zeros_like(came), came)
 
 
-def lowered(value, final, group):
+def lowered(value, group):
     size = lax.axis_size(AXIS)
-    came = lax.ppermute(value, AXIS, [((i + group) % size, i) for i in range(size)])
-    return jnp.where(final, jnp.zeros_like(came), came)
+    return lax.ppermute(value, AXIS, [((i + group) % size, i) for i in range(size)])
 
 
 def after(values, done):
@@ -68,27 +67,30 @@
     return pltpu.CompilerParams(vmem_limit_bytes=limit)
 
 
-def load_kernel(enc_hbm, dec_hbm, enc_ref, own_ref, next_ref, sems):
-    pieces = [(enc_hbm.at[0], enc_ref), (dec_hbm.at[0, 1], next_ref), (dec_hbm.at[0, 0], own_ref)]
-    copies = [pltpu.make_async_copy(source, target, sems.at[i]) for i, (source, target) in enumerate(pieces)]
+def load_kernel(pieces, weight_hbm, *rest):
+    held, sems = rest[-1 - len(pieces) : -1], rest[-1]
+    copies = [
+        pltpu.make_async_copy(weight_hbm.at[piece], target, sems.at[i])
+        for i, (piece, target) in enumerate(zip(pieces, held))
+    ]
     for copy in copies:
         copy.start()
     for copy in copies:
         copy.wait()
 
 
-def loaded(enc, dec):
-    block = pltpu.VMEM(dec.shape[2:], dec.dtype)
-    return pl.pallas_call(
-        load_kernel,
-        out_shape=[pltpu.VMEM(enc.shape[1:], enc.dtype), block, block],
-        in_specs=[ANY_SPEC] * 2,
-        out_specs=[VMEM_SPEC] * 3,
-        scratch_shapes=[pltpu.SemaphoreType.DMA((3,))],
+def loaded(weight, pieces, *done):
+    shape = weight.shape[len(pieces[0]) :]
+    return pl.pallas_call(
+        functools.partial(load_kernel, pieces),
+        out_shape=[pltpu.VMEM(shape, weight.dtype)] * len(pieces),
+        in_specs=[ANY_SPEC] * (1 + len(done)),
+        out_specs=[VMEM_SPEC] * len(pieces),
+        scratch_shapes=[pltpu.SemaphoreType.DMA((len(pieces),))],
         compiler_params=kernel_params(1 << 20),
-        cost_estimate=pl.CostEstimate(flops=0, bytes_accessed=4 * (enc.size + dec.size), transcendentals=0),
+        cost_estimate=pl.CostEstimate(flops=0, bytes_accessed=4 * weight.size, transcendentals=0),
         name="load_weights",
-    )(*in_hbm(enc, dec))
+    )(*in_hbm(weight), *done)
 
 
 def decode(codes, dec_ref, near_ref, far_ref):
@@ -176,12 +178,12 @@
     )
 
 
-def grad_own_kernel(rows_ref, dec_ref, out_ref, _):
+def grad_first_kernel(rows_ref, dec_ref, out_ref, _):
     out_ref[...] = back(rows_ref, dec_ref)
 
 
-def grad_all_kernel(tokens, rows_ref, dec_ref, own_ref, out_ref):
-    total = own_ref[...] + back(rows_ref, dec_ref)
+def grad_all_kernel(tokens, rows_ref, dec_ref, first_ref, out_ref):
+    total = first_ref[...] + back(rows_ref, dec_ref)
     group = total.shape[0] // tokens
     for block in range(group):
         slab = slab_of(place_in(group), block, group // CORES)
@@ -189,16 +191,16 @@
         out_ref[0, where, :] = total[block * tokens : (block + 1) * tokens]
 
 
-def grad_own(rows, dec):
+def grad_first(rows, dec):
     features = dec.shape[0]
     return pl.pallas_call(
-        grad_own_kernel,
+        grad_first_kernel,
         out_shape=[pltpu.VMEM((rows.shape[0], features), jnp.float32), pltpu.VMEM((8, 128), jnp.float32)],
         in_specs=[VMEM_SPEC] * 2,
         out_specs=[VMEM_SPEC] * 2,
         compiler_params=kernel_params(),
         cost_estimate=pl.CostEstimate(flops=2 * rows.size * features, bytes_accessed=2 * dec.size, transcendentals=0),
-        name="grad_own",
+        name="grad_first",
     )(*in_vmem(rows, dec))[0]
 
 
@@ -214,17 +216,26 @@
     )(*in_vmem(rows, dec, own))
 
 
-def blocks_of(near, far, chips):
-    rows = near.shape[0] // chips
-    total = near + other_core(far).astype(jnp.float32)
-    return [total[chip * rows : (chip + 1) * rows] for chip in range(chips)]
-
-
-def summed(blocks, sent):
-    total = blocks[0]
-    for came in [across(blocks[chip].astype(jnp.bfloat16), chip, len(blocks)) for chip in sent]:
-        total = total + came.astype(jnp.float32)
-    return total
+def both_cores(near, far):
+    return near + other_core(far).astype(jnp.float32)
+
+
+def halved(total, bit, chips):
+    rows, width = total.shape[0] // (chips >> bit), total.shape[1]
+    pairs = total.reshape(-1, 2, rows, width)
+    came = across(pairs[:, 1].astype(jnp.bfloat16), 1 << bit, chips)
+    return (pairs[:, 0] + came.astype(jnp.float32)).reshape(-1, width)
+
+
+def gathered(slab, chips, done=None):
+    pieces = [slab]
+    for chip in range(1, chips):
+        top = 1 << (chip.bit_length() - 1)
+        piece = pieces[chip - top]
+        if chip > top and done is not None:
+            piece = after(piece, done)
+        pieces.append(across(piece, top, chips))
+    return pieces
 
 
 def on_device(resid, enc_weight, enc_bias, active, dec_weight, target):
@@ -233,41 +244,34 @@
     index = lax.axis_index(AXIS)
     slab, first, final = lax.optimization_barrier((resid[0], index < group, index >= (LAYERS - 1) * group))
     tokens = resid.shape[1]
-    enc, own_dec, next_dec = loaded(enc_weight, dec_weight)
-    most, last = [across(slab, chip, chips) for chip in range(1, chips - 1)], across(slab, chips - 1, chips)
-    early, late = jnp.concatenate([slab, last], axis=0), jnp.concatenate(most, axis=0)
-    early_far, late_far = other_core(early), other_core(late)
-    x = jnp.concatenate(
-        [slab, late, last, early_far[:tokens], late_far, early_far[tokens:]], axis=0
-    )
+    (enc,) = loaded(enc_weight, [(0,)])
+    pieces = gathered(slab, chips, enc)
+    own_dec, next_dec = loaded(dec_weight, [(0, 0), (0, 1)], pieces[1])
+    most, last = after((jnp.concatenate(pieces[:-1], axis=0), pieces[-1]), own_dec)
+    x = jnp.concatenate([most, last, other_core(most), other_core(last)], axis=0)
     gate, bias = gated(*after((active[0], enc_bias), enc), group * tokens, tokens)
     pre = jnp.dot(x, enc, preferred_element_type=jnp.float32) + bias
     codes = (jax.nn.relu(pre) * gate).astype(jnp.bfloat16)
     next_near, next_far = decoded(codes, next_dec)
     own_near, own_far = decoded(codes, own_dec)
 
-    nexts = blocks_of(next_near, next_far, chips)
-    owns = blocks_of(own_near, own_far, chips)
-    risen = raised(nexts[-1].astype(jnp.bfloat16), first, group)
-    owns[-1] = owns[-1] + risen.astype(jnp.float32)
-    crossed = across(owns[-1].astype(jnp.bfloat16), chips - 1, chips).astype(jnp.float32)
-    next_sum = after(summed(nexts, range(1, chips - 1)), owns[-1])
-    own_less = summed(owns, range(1, chips - 1)) - target[0].astype(jnp.float32) + crossed
-
+    next_sum, own_sum = both_cores(next_near, next_far), both_cores(own_near, own_far)
+    for bit in range(chips.bit_length() - 1):
+        next_sum = halved(next_sum, bit, chips)
+        own_sum = after(halved(own_sum, bit, chips), next_sum)
+    own_less = own_sum - target[0].astype(jnp.float32)
     below = raised(next_sum.astype(jnp.bfloat16), first, group).astype(jnp.float32)
-    above = lowered(own_less.astype(jnp.bfloat16), final, group).astype(jnp.float32)
+    above = lowered(own_less.astype(jnp.bfloat16), group)
     error = (own_less + below).astype(jnp.bfloat16)
-    later = jnp.where(final, 0.0, next_sum + after(above, error)).astype(jnp.bfloat16)
-
-    heres = [error] + [across(error, chip, chips) for chip in range(1, chips)]
-    afters = [later] + [across(later, chip, chips) for chip in range(1, chips - 1)]
-    last = lowered(after(heres[-1], later), final, group)
-    here_near = jnp.concatenate(heres, axis=0)
+    later = jnp.where(final, 0.0, next_sum + after(above, error).astype(jnp.float32)).astype(jnp.bfloat16)
+
+    here_near = jnp.concatenate(gathered(error, chips), axis=0)
     here_far = other_core(here_near)
     here_rows = jnp.concatenate([here_near, here_far], axis=0)
-    most = after(jnp.concatenate(afters, axis=0), here_far)
+    afters = gathered(later, chips)
+    most, last = after(jnp.concatenate(afters[:-1], axis=0), here_far), afters[-1]
     after_rows = jnp.concatenate([most, last, other_core(most), other_core(last)], axis=0)
-    grad = grad_all(after_rows, next_dec, grad_own(here_rows, own_dec), tokens)
+    grad = grad_all(after_rows, next_dec, grad_first(here_rows, own_dec), tokens)
     return (error[None], grad)
 
 

time: 51.3 us -> 61.5 us (1.20)
  waiting for transfers between devices: 12.4 us -> 21.6 us
  starting transfers between devices: 25.1 us -> 26.3 us
  Pallas kernels: 9.92 us -> 10.9 us
  local copies, waits for them, and re-layouts: 1.16 us -> 0.18 us
    ppermute x13, waiting for transfers between devices: 4.95 us -> 15.9 us  [across(): return lax.ppermute(value, AXIS, pairs)]
    ppermute x2 -> x1, waiting for transfers between devices: 2.55 us -> 0.42 us  [raised(): lax.ppermute(value, AXIS, [(i, (i + group) % size) for i in range(size)])]
    ppermute x7, waiting for transfers between devices: 1.74 us -> 3.29 us  [other_core(): lax.ppermute(value, AXIS, [(i, i ^ 1) for i in range(lax.axis_size(AXIS))])]
    ppermute x2 -> x1, waiting for transfers between devices: 3.19 us -> 2.03 us  [lowered(): lax.ppermute(value, AXIS, [((i + group) % size, i) for i in range(size)])]
    unnamed x19 -> x13, local copies, waits for them, and re-layouts: 1.07 us -> 0.06 us
    pallas_call x2 -> x3, Pallas kernels: 6.11 us -> 7.08 us  [the longest x2 5.69 us: loaded(): pl.pallas_call(functools.partial(load_kernel, pieces), out_shape=[pltpu.V...]
    ppermute x13, starting transfers between devices: 16.8 us -> 17.8 us  [across(): return lax.ppermute(value, AXIS, pairs)]
    ppermute x2 -> x1, starting transfers between devices: 3.73 us -> 4.44 us  [lowered(): lax.ppermute(value, AXIS, [((i + group) % size, i) for i in range(size)])]
  transfers between devices with their start and end apart: 24 -> 22, of which waited for: 11 -> 14; matrix products, arithmetic and copies ran while one was open for 3% -> 1% of each run, Pallas kernels for 14% -> 13%
where the time goes in v15:
time: 61.5 us; the launch traced here: 61.3 us
  starting transfers between devices  26.3 us (43%)
  waiting for transfers between devices  21.6 us (35%)
  Pallas kernels  10.9 us (18%)
  between operations  0.9 us (1%)
  matrix products  0.8 us (1%)
  other arithmetic  0.68 us (1%)
    ppermute x13, starting transfers between devices, across(): return lax.ppermute(value, AXIS, pairs)  17.8 us
    ppermute x13, waiting for transfers between devices, across(): return lax.ppermute(value, AXIS, pairs)  15.9 us
    pallas_call x2, Pallas kernels, loaded(): pl.pallas_call(functools.partial(load_kernel, pieces), out_shape=[pltpu.V...  5.69 us
    ppermute x1, starting transfers between devices, lowered(): lax.ppermute(value, AXIS, [((i + group) % size, i) for i in range(size)])  4.44 us
    ppermute x7, waiting for transfers between devices, other_core(): lax.ppermute(value, AXIS, [(i, i ^ 1) for i in range(lax.axis_size(AXIS))])  3.29 us
    ppermute x1, starting transfers between devices, raised(): lax.ppermute(value, AXIS, [(i, (i + group) % size) for i in range(size)])  2.15 us
    ppermute x1, waiting for transfers between devices, lowered(): lax.ppermute(value, AXIS, [((i + group) % size, i) for i in range(size)])  2.03 us
    pallas_call x1, Pallas kernels, grad_all(): pl.pallas_call(functools.partial(grad_all_kernel, tokens), out_shape=jax....  2.03 us
  transfers between devices with their start and end apart: 22, of which 14 were waited for; matrix products, arithmetic and copies ran while one was open for 1% of the time, Pallas kernels for 13%

profile of v15, /device:TPU:0, one launch (start us, length us, event | category | flops | bytes accessed | tf_op | source)
XLA Modules:
  0.0 61.3 jit_solution(13740285967854236009)
XLA Ops:
  0.6 3.0 %collective-permute-start = (bf16[8,8192]{1,0:T(8,128)(2,1)}, bf16[8,8192]{1,0:T(8,128)(2,1)S(1)}, u32[]{:S(2)}, u32[]{:S(2)}) collective-permute-start(bf16[8,8192]{1,0:T(8,128)(2,1)} %bitcast.64), channel_id=1, source_target_pairs={{0,2},{1,5},{2,0},{3,7},{4,6},{5,1},{6,4},{7,3},{8,10},{9,13},{10,... | collective-permute-start | bytes 393224 | tf_op jit(solution)/shard_map/ppermute | solution.py:30
  3.7 1.5 %collective-permute-start.1 = (bf16[8,8192]{1,0:T(8,128)(2,1)}, bf16[8,8192]{1,0:T(8,128)(2,1)S(1)}, u32[]{:S(2)}, u32[]{:S(2)}) collective-permute-start(bf16[8,8192]{1,0:T(8,128)(2,1)} %bitcast.65), channel_id=1, source_target_pairs={{0,4},{1,3},{2,6},{3,1},{4,0},{5,7},{6,2},{7,5},{8,12},{9,11},{10,... | collective-permute-start | bytes 393224 | tf_op jit(solution)/shard_map/ppermute | solution.py:30
  5.2 2.2 %load_weights.2 = bf16[8192,256]{1,0:T(8,128)(2,1)S(1)} custom-call(bf16[1,8192,256]{2,1,0:T(8,128)(2,1)} %weight_hbm.2), custom_call_target="tpu_custom_call" | custom-call | bytes 8388608 | tf_op jit(solution)/shard_map/load_weights/pallas_call | solution.py:84
  7.4 0.4 collective-permute-done.rest_0_
  7.7 1.5 %collective-permute-start.2 = (bf16[8,8192]{1,0:T(8,128)(2,1)S(1)}, bf16[8,8192]{1,0:T(8,128)(2,1)S(1)}, u32[]{:S(2)}, u32[]{:S(2)}) collective-permute-start(bf16[8,8192]{1,0:T(8,128)(2,1)S(1)} %collective-permute-done.rest_0_), channel_id=1, source_target_pairs={{0,4},{1,3},{2,6},{3,1},{4,0},{5,7},{6,2},{7,5},{8,12},{9,11},{10,... | collective-permute-start | bytes 393224 | tf_op jit(solution)/shard_map/ppermute | solution.py:30
  9.2 0.0 collective-permute-done.1
  9.2 0.0 copy-done.4
  9.2 0.0 copy-start
  9.3 0.0 copy-start.1
  9.3 3.5 %load_weights.3 = (bf16[256,8192]{1,0:T(8,128)(2,1)S(1)}, bf16[256,8192]{1,0:T(8,128)(2,1)S(1)}) custom-call(bf16[1,2,256,8192]{3,2,1,0:T(8,128)(2,1)} %weight_hbm.3, bf16[8,8192]{1,0:T(8,128)(2,1)S(1)} %collective-permute-done.rest_0_), custom_call_target="tpu_custom_call" | custom-call | bytes 16777216 | tf_op jit(solution)/shard_map/load_weights/pallas_call | solution.py:84
  12.8 0.0 collective-permute-done.2
  12.8 0.1 collective-permute-start.3
  12.9 0.5 collective-permute-start.4
  13.4 0.1 gate.1
  13.5 1.3 %collective-permute-done.4 = bf16[8,8192]{1,0:T(8,128)(2,1)S(1)} collective-permute-done((bf16[8,8192]{1,0:T(8,128)(2,1)S(1)}, bf16[8,8192]{1,0:T(8,128)(2,1)S(1)}, u32[]{:S(2)}, u32[]{:S(2)}) %collective-permute-start.4) | collective-permute-done | bytes 131104 | tf_op jit(solution)/shard_map/ppermute | solution.py:34
  14.8 0.0 collective-permute-done.3
  14.8 0.8 %fusion.2.codes_ref = bf16[64,256]{1,0:T(8,128)(2,1)S(1)} fusion(f32[64,256]{1,0:T(8,128)S(1)} %get-tuple-element.30, f32[64,256]{1,0:T(8,128)S(1)} %get-tuple-element.29, bf16[8192,256]{1,0:T(8,128)(2,1)S(1)} %load_weights.2, bf16[8,8192]{1,0:T(8,128)(2,1)S(1)} %collective-permute-done.4, bf16[24,8192]{1,0:T(8,128)(2,1)S(1)} %collective-permute-done.3, ...), kind=kOutput, calls=%fused_computation.3 | convolution fusion | flops 272695296 | bytes 5406720 | tf_op jit(solution)/shard_map/dot_general | solution.py:253
  15.6 0.8 %decode.3 = (f32[32,8192]{1,0:T(8,128)S(1)}, bf16[32,8192]{1,0:T(8,128)(2,1)S(1)}) custom-call(bf16[64,256]{1,0:T(8,128)(2,1)S(1)} %fusion.2.codes_ref, bf16[256,8192]{1,0:T(8,128)(2,1)S(1)} %get-tuple-element.33.dec_ref), custom_call_target="tpu_custom_call" | custom-call | flops 268435456 | bytes 4194304 | tf_op jit(solution)/shard_map/decode/pallas_call | solution.py:161
  16.4 0.2 collective-permute-start.8
  16.6 0.8 %decode.2 = (f32[32,8192]{1,0:T(8,128)S(1)}, bf16[32,8192]{1,0:T(8,128)(2,1)S(1)}) custom-call(bf16[64,256]{1,0:T(8,128)(2,1)S(1)} %fusion.2.codes_ref, bf16[256,8192]{1,0:T(8,128)(2,1)S(1)} %get-tuple-element.24.dec_ref), custom_call_target="tpu_custom_call" | custom-call | flops 268435456 | bytes 4194304 | tf_op jit(solution)/shard_map/decode/pallas_call | solution.py:161
  17.5 0.4 collective-permute-start.5
  17.9 0.5 collective-permute-done.8
  18.4 0.1 convert_add_fusion
  18.5 2.3 %collective-permute-start.9 = (bf16[2,8,8192]{2,1,0:T(8,128)(2,1)S(1)}, bf16[2,8,8192]{2,1,0:T(8,128)(2,1)S(1)}, u32[]{:S(2)}, u32[]{:S(2)}) collective-permute-start(bf16[2,8,8192]{2,1,0:T(8,128)(2,1)S(1)} %fusion.15), channel_id=1, source_target_pairs={{0,2},{1,5},{2,0},{3,7},{4,6},{5,1},{6,4},{7,3},{8,10},{9,13},{10,... | collective-permute-start | bytes 786440 | tf_op jit(solution)/shard_map/ppermute | solution.py:30
  20.9 0.0 collective-permute-done.5
  20.9 0.1 convert_add_fusion.1
  21.0 0.0 copy-start.2
  21.0 0.9 %collective-permute-start.6 = (bf16[2,8,8192]{2,1,0:T(8,128)(2,1)S(1)}, bf16[2,8,8192]{2,1,0:T(8,128)(2,1)S(1)}, u32[]{:S(2)}, u32[]{:S(2)}) collective-permute-start(bf16[2,8,8192]{2,1,0:T(8,128)(2,1)S(1)} %fusion.14), channel_id=1, source_target_pairs={{0,2},{1,5},{2,0},{3,7},{4,6},{5,1},{6,4},{7,3},{8,10},{9,13},{10,... | collective-permute-start | bytes 786440 | tf_op jit(solution)/shard_map/ppermute | solution.py:30
  21.9 3.3 %collective-permute-done.9 = bf16[2,8,8192]{2,1,0:T(8,128)(2,1)S(1)} collective-permute-done((bf16[2,8,8192]{2,1,0:T(8,128)(2,1)S(1)}, bf16[2,8,8192]{2,1,0:T(8,128)(2,1)S(1)}, u32[]{:S(2)}, u32[]{:S(2)}) %collective-permute-start.9) | collective-permute-done | bytes 262176 | tf_op jit(solution)/shard_map/ppermute | solution.py:30
  25.2 0.1 fusion.11
  25.3 1.2 %collective-permute-start.10 = (bf16[1,8,8192]{2,1,0:T(8,128)(2,1)S(1)}, bf16[1,8,8192]{2,1,0:T(8,128)(2,1)S(1)}, u32[]{:S(2)}, u32[]{:S(2)}) collective-permute-start(bf16[1,8,8192]{2,1,0:T(8,128)(2,1)S(1)} %fusion.22), channel_id=1, source_target_pairs={{0,4},{1,3},{2,6},{3,1},{4,0},{5,7},{6,2},{7,5},{8,12},{9,11},{10,... | collective-permute-start | bytes 393224 | tf_op jit(solution)/shard_map/ppermute | solution.py:30
  26.5 2.0 %collective-permute-done.6 = bf16[2,8,8192]{2,1,0:T(8,128)(2,1)S(1)} collective-permute-done((bf16[2,8,8192]{2,1,0:T(8,128)(2,1)S(1)}, bf16[2,8,8192]{2,1,0:T(8,128)(2,1)S(1)}, u32[]{:S(2)}, u32[]{:S(2)}) %collective-permute-start.6) | collective-permute-done | bytes 262176 | tf_op jit(solution)/shard_map/ppermute | solution.py:30
  28.5 0.1 fusion.13
  28.5 1.4 %collective-permute-start.7 = (bf16[1,8,8192]{2,1,0:T(8,128)(2,1)S(1)}, bf16[1,8,8192]{2,1,0:T(8,128)(2,1)S(1)}, u32[]{:S(2)}, u32[]{:S(2)}) collective-permute-start(bf16[1,8,8192]{2,1,0:T(8,128)(2,1)S(1)} %fusion.21), channel_id=1, source_target_pairs={{0,4},{1,3},{2,6},{3,1},{4,0},{5,7},{6,2},{7,5},{8,12},{9,11},{10,... | collective-permute-start | bytes 393224 | tf_op jit(solution)/shard_map/ppermute | solution.py:30
  30.0 0.4 collective-permute-done.10
  30.4 2.2 %collective-permute-start.11 = (bf16[8,8192]{1,0:T(8,128)(2,1)S(1)}, bf16[8,8192]{1,0:T(8,128)(2,1)S(1)}, u32[]{:S(2)}, u32[]{:S(2)}) collective-permute-start(bf16[8,8192]{1,0:T(8,128)(2,1)S(1)} %get-tuple-element.44), channel_id=1, source_target_pairs={{0,8},{1,9},{2,10},{3,11},{4,12},{5,13},{6,14},{7,15},{8,16},{9,17... | collective-permute-start | bytes 393224 | tf_op jit(solution)/shard_map/ppermute | solution.py:39
  32.5 1.1 %collective-permute-done.7 = bf16[1,8,8192]{2,1,0:T(8,128)(2,1)S(1)} collective-permute-done((bf16[1,8,8192]{2,1,0:T(8,128)(2,1)S(1)}, bf16[1,8,8192]{2,1,0:T(8,128)(2,1)S(1)}, u32[]{:S(2)}, u32[]{:S(2)}) %collective-permute-start.7) | collective-permute-done | bytes 131104 | tf_op jit(solution)/shard_map/ppermute | solution.py:30
  33.7 4.4 %collective-permute-start.12 = (bf16[8,8192]{1,0:T(8,128)(2,1)S(1)}, bf16[8,8192]{1,0:T(8,128)(2,1)S(1)}, u32[]{:S(2)}, u32[]{:S(2)}) collective-permute-start(bf16[8,8192]{1,0:T(8,128)(2,1)S(1)} %fusion.20), channel_id=1, source_target_pairs={{8,0},{9,1},{10,2},{11,3},{12,4},{13,5},{14,6},{15,7},{16,8},{17,9... | collective-permute-start | bytes 393224 | tf_op jit(solution)/shard_map/ppermute | solution.py:45
  38.1 0.4 collective-permute-done.11
  38.5 0.1 constant_dynamic-update-slice_fusion.4
  38.6 0.0 copy-start.3
  38.6 2.0 %collective-permute-done.12 = bf16[8,8192]{1,0:T(8,128)(2,1)S(1)} collective-permute-done((bf16[8,8192]{1,0:T(8,128)(2,1)S(1)}, bf16[8,8192]{1,0:T(8,128)(2,1)S(1)}, u32[]{:S(2)}, u32[]{:S(2)}) %collective-permute-start.12) | collective-permute-done | bytes 131104 | tf_op jit(solution)/shard_map/ppermute | solution.py:45
  40.7 1.6 %collective-permute-start.13 = (bf16[8,8192]{1,0:T(8,128)(2,1)S(1)}, bf16[8,8192]{1,0:T(8,128)(2,1)S(1)}, u32[]{:S(2)}, u32[]{:S(2)}) collective-permute-start(bf16[8,8192]{1,0:T(8,128)(2,1)S(1)} %select_convert_fusion), channel_id=1, source_target_pairs={{0,2},{1,5},{2,0},{3,7},{4,6},{5,1},{6,4},{7,3},{8,10},{9,13},{10,... | collective-permute-start | bytes 393224 | tf_op jit(solution)/shard_map/ppermute | solution.py:30
  42.2 0.7 %collective-permute-start.14 = (bf16[8,8192]{1,0:T(8,128)(2,1)S(1)}, bf16[8,8192]{1,0:T(8,128)(2,1)S(1)}, u32[]{:S(2)}, u32[]{:S(2)}) collective-permute-start(bf16[8,8192]{1,0:T(8,128)(2,1)S(1)} %select_convert_fusion), channel_id=1, source_target_pairs={{0,4},{1,3},{2,6},{3,1},{4,0},{5,7},{6,2},{7,5},{8,12},{9,11},{10,... | collective-permute-start | bytes 393224 | tf_op jit(solution)/shard_map/ppermute | solution.py:30
  42.9 1.3 %collective-permute-start.16 = (bf16[8,8192]{1,0:T(8,128)(2,1)S(1)}, bf16[8,8192]{1,0:T(8,128)(2,1)S(1)}, u32[]{:S(2)}, u32[]{:S(2)}) collective-permute-start(bf16[8,8192]{1,0:T(8,128)(2,1)S(1)} %get-tuple-element.43), channel_id=1, source_target_pairs={{0,4},{1,3},{2,6},{3,1},{4,0},{5,7},{6,2},{7,5},{8,12},{9,11},{10,... | collective-permute-start | bytes 393224 | tf_op jit(solution)/shard_map/ppermute | solution.py:30
  44.2 0.5 collective-permute-start.15
  44.8 2.1 %collective-permute-done.13 = bf16[8,8192]{1,0:T(8,128)(2,1)S(1)} collective-permute-done((bf16[8,8192]{1,0:T(8,128)(2,1)S(1)}, bf16[8,8192]{1,0:T(8,128)(2,1)S(1)}, u32[]{:S(2)}, u32[]{:S(2)}) %collective-permute-start.13) | collective-permute-done | bytes 131104 | tf_op jit(solution)/shard_map/ppermute | solution.py:30
  46.9 1.0 %collective-permute-start.19 = (bf16[8,8192]{1,0:T(8,128)(2,1)S(1)}, bf16[8,8192]{1,0:T(8,128)(2,1)S(1)}, u32[]{:S(2)}, u32[]{:S(2)}) collective-permute-start(bf16[8,8192]{1,0:T(8,128)(2,1)S(1)} %collective-permute-done.13), channel_id=1, source_target_pairs={{0,4},{1,3},{2,6},{3,1},{4,0},{5,7},{6,2},{7,5},{8,12},{9,11},{10,... | collective-permute-start | bytes 393224 | tf_op jit(solution)/shard_map/ppermute | solution.py:30
  47.9 0.0 collective-permute-done.14
  47.9 2.6 %collective-permute-done.15 = bf16[8,8192]{1,0:T(8,128)(2,1)S(1)} collective-permute-done((bf16[8,8192]{1,0:T(8,128)(2,1)S(1)}, bf16[8,8192]{1,0:T(8,128)(2,1)S(1)}, u32[]{:S(2)}, u32[]{:S(2)}) %collective-permute-start.15) | collective-permute-done | bytes 131104 | tf_op jit(solution)/shard_map/ppermute | solution.py:30
  50.5 0.9 %collective-permute-start.17 = (bf16[8,8192]{1,0:T(8,128)(2,1)S(1)}, bf16[8,8192]{1,0:T(8,128)(2,1)S(1)}, u32[]{:S(2)}, u32[]{:S(2)}) collective-permute-start(bf16[8,8192]{1,0:T(8,128)(2,1)S(1)} %collective-permute-done.15), channel_id=1, source_target_pairs={{0,4},{1,3},{2,6},{3,1},{4,0},{5,7},{6,2},{7,5},{8,12},{9,11},{10,... | collective-permute-start | bytes 393224 | tf_op jit(solution)/shard_map/ppermute | solution.py:30
  51.4 0.0 collective-permute-done.16
  51.5 4.0 %collective-permute-done.17 = bf16[8,8192]{1,0:T(8,128)(2,1)S(1)} collective-permute-done((bf16[8,8192]{1,0:T(8,128)(2,1)S(1)}, bf16[8,8192]{1,0:T(8,128)(2,1)S(1)}, u32[]{:S(2)}, u32[]{:S(2)}) %collective-permute-start.17) | collective-permute-done | bytes 131104 | tf_op jit(solution)/shard_map/ppermute | solution.py:30
  55.5 0.1 collective-permute-start.18
  55.6 0.0 collective-permute-done.19
  55.6 0.5 collective-permute-start.21
  56.1 1.4 %collective-permute-done.18 = bf16[32,8192]{1,0:T(8,128)(2,1)S(1)} collective-permute-done((bf16[32,8192]{1,0:T(8,128)(2,1)S(1)}, bf16[32,8192]{1,0:T(8,128)(2,1)S(1)}, u32[]{:S(2)}, u32[]{:S(2)}) %collective-permute-start.18) | collective-permute-done | bytes 524320 | tf_op jit(solution)/shard_map/ppermute | solution.py:34
  57.5 0.1 collective-permute-start.20
  57.7 0.0 copy-done.3
  57.7 1.4 %grad_first.1 = (f32[64,256]{1,0:T(8,128)S(1)}, f32[8,128]{1,0:T(8,128)}) custom-call(bf16[64,8192]{1,0:T(8,128)(2,1)S(1)} %constant_dynamic-update-slice_fusion.rows_ref, bf16[256,8192]{1,0:T(8,128)(2,1)S(1)} %get-tuple-element.24.dec_ref), custom_call_target="tpu_custom_call" | custom-call | flops 268435456 | bytes 4194304 | tf_op jit(solution)/shard_map/grad_first/pallas_call | solution.py:196
  59.1 0.0 collective-permute-done.21
  59.1 0.1 collective-permute-done.20
  59.2 0.1 pad_maximum_fusion.rows_ref
  59.3 2.0 %grad_all.1 = f32[1,64,256]{2,1,0:T(8,128)} custom-call(bf16[64,8192]{1,0:T(8,128)(2,1)S(1)} %pad_maximum_fusion.rows_ref, bf16[256,8192]{1,0:T(8,128)(2,1)S(1)} %get-tuple-element.33.dec_ref, f32[64,256]{1,0:T(8,128)S(1)} %get-tuple-element.41.first_ref), custom_call_target="tpu_custom_call" | custom-call | flops 268435456 | bytes 4194304 | tf_op jit(solution)/shard_map/grad_all/pallas_call | solution.py:208
  (19 shorter events, 0.4 us)
Async XLA Ops:
  0.6 8.6 %copy-start.4 = (bf16[1,8,8192]{2,1,0:T(8,128)(2,1)S(1)}, bf16[1,8,8192]{2,1,0:T(8,128)(2,1)}, u32[]{:S(2)}) copy-start(bf16[1,8,8192]{2,1,0:T(8,128)(2,1)} %param.6) | copy-start | bytes 393220
  0.6 7.1 %collective-permute-start = (bf16[8,8192]{1,0:T(8,128)(2,1)}, bf16[8,8192]{1,0:T(8,128)(2,1)S(1)}, u32[]{:S(2)}, u32[]{:S(2)}) collective-permute-start(bf16[8,8192]{1,0:T(8,128)(2,1)} %bitcast.64), channel_id=1, source_target_pairs={{0,2},{1,5},{2,0},{3,7},{4,6},{5,1},{6,4},{7,3},{8,10},{9,13},{10,... | collective-permute-start | bytes 393224 | tf_op jit(solution)/shard_map/ppermute | solution.py:30
  3.7 5.6 %collective-permute-start.1 = (bf16[8,8192]{1,0:T(8,128)(2,1)}, bf16[8,8192]{1,0:T(8,128)(2,1)S(1)}, u32[]{:S(2)}, u32[]{:S(2)}) collective-permute-start(bf16[8,8192]{1,0:T(8,128)(2,1)} %bitcast.65), channel_id=1, source_target_pairs={{0,4},{1,3},{2,6},{3,1},{4,0},{5,7},{6,2},{7,5},{8,12},{9,11},{10,... | collective-permute-start | bytes 393224 | tf_op jit(solution)/shard_map/ppermute | solution.py:30
  7.7 5.0 %collective-permute-start.2 = (bf16[8,8192]{1,0:T(8,128)(2,1)S(1)}, bf16[8,8192]{1,0:T(8,128)(2,1)S(1)}, u32[]{:S(2)}, u32[]{:S(2)}) collective-permute-start(bf16[8,8192]{1,0:T(8,128)(2,1)S(1)} %collective-permute-done.rest_0_), channel_id=1, source_target_pairs={{0,4},{1,3},{2,6},{3,1},{4,0},{5,7},{6,2},{7,5},{8,12},{9,11},{10,... | collective-permute-start | bytes 393224 | tf_op jit(solution)/shard_map/ppermute | solution.py:30
  9.2 4.1 %copy-start = (s32[1,2,2]{2,1,0:T(2,128)S(1)}, s32[1,2,2]{2,1,0:T(2,128)}, u32[]{:S(2)}) copy-start(s32[1,2,2]{2,1,0:T(2,128)} %param.9) | copy-start | bytes 52
  9.3 4.1 %copy-start.1 = (bf16[1,256]{1,0:T(2,128)(2,1)S(1)}, bf16[1,256]{1,0:T(2,128)(2,1)}, u32[]{:S(2)}) copy-start(bf16[1,256]{1,0:T(2,128)(2,1)} %bias_ref) | copy-start | bytes 1540
  12.8 2.0 %collective-permute-start.3 = (bf16[24,8192]{1,0:T(8,128)(2,1)S(1)}, bf16[24,8192]{1,0:T(8,128)(2,1)S(1)}, u32[]{:S(2)}, u32[]{:S(2)}) collective-permute-start(bf16[24,8192]{1,0:T(8,128)(2,1)S(1)} %pad_maximum_fusion.2), channel_id=1, source_target_pairs={{0,1},{1,0},{2,3},{3,2},{4,5},{5,4},{6,7},{7,6},{8,9},{9,8},{10,11... | collective-permute-start | bytes 1179656 | tf_op jit(solution)/shard_map/ppermute | solution.py:34
  12.9 1.9 %collective-permute-start.4 = (bf16[8,8192]{1,0:T(8,128)(2,1)S(1)}, bf16[8,8192]{1,0:T(8,128)(2,1)S(1)}, u32[]{:S(2)}, u32[]{:S(2)}) collective-permute-start(bf16[8,8192]{1,0:T(8,128)(2,1)S(1)} %collective-permute-done.2), channel_id=1, source_target_pairs={{0,1},{1,0},{2,3},{3,2},{4,5},{5,4},{6,7},{7,6},{8,9},{9,8},{10,11... | collective-permute-start | bytes 393224 | tf_op jit(solution)/shard_map/ppermute | solution.py:34
  16.4 2.0 %collective-permute-start.8 = (bf16[32,8192]{1,0:T(8,128)(2,1)S(1)}, bf16[32,8192]{1,0:T(8,128)(2,1)S(1)}, u32[]{:S(2)}, u32[]{:S(2)}) collective-permute-start(bf16[32,8192]{1,0:T(8,128)(2,1)S(1)} %get-tuple-element.35), channel_id=1, source_target_pairs={{0,1},{1,0},{2,3},{3,2},{4,5},{5,4},{6,7},{7,6},{8,9},{9,8},{10,11... | collective-permute-start | bytes 1572872 | tf_op jit(solution)/shard_map/ppermute | solution.py:34
  17.5 3.4 %collective-permute-start.5 = (bf16[32,8192]{1,0:T(8,128)(2,1)S(1)}, bf16[32,8192]{1,0:T(8,128)(2,1)S(1)}, u32[]{:S(2)}, u32[]{:S(2)}) collective-permute-start(bf16[32,8192]{1,0:T(8,128)(2,1)S(1)} %get-tuple-element.32), channel_id=1, source_target_pairs={{0,1},{1,0},{2,3},{3,2},{4,5},{5,4},{6,7},{7,6},{8,9},{9,8},{10,11... | collective-permute-start | bytes 1572872 | tf_op jit(solution)/shard_map/ppermute | solution.py:34
  18.5 6.7 %collective-permute-start.9 = (bf16[2,8,8192]{2,1,0:T(8,128)(2,1)S(1)}, bf16[2,8,8192]{2,1,0:T(8,128)(2,1)S(1)}, u32[]{:S(2)}, u32[]{:S(2)}) collective-permute-start(bf16[2,8,8192]{2,1,0:T(8,128)(2,1)S(1)} %fusion.15), channel_id=1, source_target_pairs={{0,2},{1,5},{2,0},{3,7},{4,6},{5,1},{6,4},{7,3},{8,10},{9,13},{10,... | collective-permute-start | bytes 786440 | tf_op jit(solution)/shard_map/ppermute | solution.py:30
  21.0 12.6 %copy-start.2 = (bf16[1,8,8192]{2,1,0:T(8,128)(2,1)S(1)}, bf16[1,8,8192]{2,1,0:T(8,128)(2,1)}, u32[]{:S(2)}) copy-start(bf16[1,8,8192]{2,1,0:T(8,128)(2,1)} %param.11) | copy-start | bytes 393220
  21.0 7.4 %collective-permute-start.6 = (bf16[2,8,8192]{2,1,0:T(8,128)(2,1)S(1)}, bf16[2,8,8192]{2,1,0:T(8,128)(2,1)S(1)}, u32[]{:S(2)}, u32[]{:S(2)}) collective-permute-start(bf16[2,8,8192]{2,1,0:T(8,128)(2,1)S(1)} %fusion.14), channel_id=1, source_target_pairs={{0,2},{1,5},{2,0},{3,7},{4,6},{5,1},{6,4},{7,3},{8,10},{9,13},{10,... | collective-permute-start | bytes 786440 | tf_op jit(solution)/shard_map/ppermute | solution.py:30
  25.3 5.0 %collective-permute-start.10 = (bf16[1,8,8192]{2,1,0:T(8,128)(2,1)S(1)}, bf16[1,8,8192]{2,1,0:T(8,128)(2,1)S(1)}, u32[]{:S(2)}, u32[]{:S(2)}) collective-permute-start(bf16[1,8,8192]{2,1,0:T(8,128)(2,1)S(1)} %fusion.22), channel_id=1, source_target_pairs={{0,4},{1,3},{2,6},{3,1},{4,0},{5,7},{6,2},{7,5},{8,12},{9,11},{10,... | collective-permute-start | bytes 393224 | tf_op jit(solution)/shard_map/ppermute | solution.py:30
  28.5 5.0 %collective-permute-start.7 = (bf16[1,8,8192]{2,1,0:T(8,128)(2,1)S(1)}, bf16[1,8,8192]{2,1,0:T(8,128)(2,1)S(1)}, u32[]{:S(2)}, u32[]{:S(2)}) collective-permute-start(bf16[1,8,8192]{2,1,0:T(8,128)(2,1)S(1)} %fusion.21), channel_id=1, source_target_pairs={{0,4},{1,3},{2,6},{3,1},{4,0},{5,7},{6,2},{7,5},{8,12},{9,11},{10,... | collective-permute-start | bytes 393224 | tf_op jit(solution)/shard_map/ppermute | solution.py:30
  30.4 8.1 %collective-permute-start.11 = (bf16[8,8192]{1,0:T(8,128)(2,1)S(1)}, bf16[8,8192]{1,0:T(8,128)(2,1)S(1)}, u32[]{:S(2)}, u32[]{:S(2)}) collective-permute-start(bf16[8,8192]{1,0:T(8,128)(2,1)S(1)} %get-tuple-element.44), channel_id=1, source_target_pairs={{0,8},{1,9},{2,10},{3,11},{4,12},{5,13},{6,14},{7,15},{8,16},{9,17... | collective-permute-start | bytes 393224 | tf_op jit(solution)/shard_map/ppermute | solution.py:39
  33.7 7.0 %collective-permute-start.12 = (bf16[8,8192]{1,0:T(8,128)(2,1)S(1)}, bf16[8,8192]{1,0:T(8,128)(2,1)S(1)}, u32[]{:S(2)}, u32[]{:S(2)}) collective-permute-start(bf16[8,8192]{1,0:T(8,128)(2,1)S(1)} %fusion.20), channel_id=1, source_target_pairs={{8,0},{9,1},{10,2},{11,3},{12,4},{13,5},{14,6},{15,7},{16,8},{17,9... | collective-permute-start | bytes 393224 | tf_op jit(solution)/shard_map/ppermute | solution.py:45
  38.6 19.1 %copy-start.3 = (bf16[8,8192]{1,0:T(8,128)(2,1)}, bf16[8,8192]{1,0:T(8,128)(2,1)S(1)}, u32[]{:S(2)}) copy-start(bf16[8,8192]{1,0:T(8,128)(2,1)S(1)} %get-tuple-element.43) | copy-start | bytes 393220
  40.7 6.3 %collective-permute-start.13 = (bf16[8,8192]{1,0:T(8,128)(2,1)S(1)}, bf16[8,8192]{1,0:T(8,128)(2,1)S(1)}, u32[]{:S(2)}, u32[]{:S(2)}) collective-permute-start(bf16[8,8192]{1,0:T(8,128)(2,1)S(1)} %select_convert_fusion), channel_id=1, source_target_pairs={{0,2},{1,5},{2,0},{3,7},{4,6},{5,1},{6,4},{7,3},{8,10},{9,13},{10,... | collective-permute-start | bytes 393224 | tf_op jit(solution)/shard_map/ppermute | solution.py:30
  42.2 5.7 %collective-permute-start.14 = (bf16[8,8192]{1,0:T(8,128)(2,1)S(1)}, bf16[8,8192]{1,0:T(8,128)(2,1)S(1)}, u32[]{:S(2)}, u32[]{:S(2)}) collective-permute-start(bf16[8,8192]{1,0:T(8,128)(2,1)S(1)} %select_convert_fusion), channel_id=1, source_target_pairs={{0,4},{1,3},{2,6},{3,1},{4,0},{5,7},{6,2},{7,5},{8,12},{9,11},{10,... | collective-permute-start | bytes 393224 | tf_op jit(solution)/shard_map/ppermute | solution.py:30
  42.9 8.5 %collective-permute-start.16 = (bf16[8,8192]{1,0:T(8,128)(2,1)S(1)}, bf16[8,8192]{1,0:T(8,128)(2,1)S(1)}, u32[]{:S(2)}, u32[]{:S(2)}) collective-permute-start(bf16[8,8192]{1,0:T(8,128)(2,1)S(1)} %get-tuple-element.43), channel_id=1, source_target_pairs={{0,4},{1,3},{2,6},{3,1},{4,0},{5,7},{6,2},{7,5},{8,12},{9,11},{10,... | collective-permute-start | bytes 393224 | tf_op jit(solution)/shard_map/ppermute | solution.py:30
  44.2 6.3 %collective-permute-start.15 = (bf16[8,8192]{1,0:T(8,128)(2,1)S(1)}, bf16[8,8192]{1,0:T(8,128)(2,1)S(1)}, u32[]{:S(2)}, u32[]{:S(2)}) collective-permute-start(bf16[8,8192]{1,0:T(8,128)(2,1)S(1)} %get-tuple-element.43), channel_id=1, source_target_pairs={{0,2},{1,5},{2,0},{3,7},{4,6},{5,1},{6,4},{7,3},{8,10},{9,13},{10,... | collective-permute-start | bytes 393224 | tf_op jit(solution)/shard_map/ppermute | solution.py:30
  46.9 8.7 %collective-permute-start.19 = (bf16[8,8192]{1,0:T(8,128)(2,1)S(1)}, bf16[8,8192]{1,0:T(8,128)(2,1)S(1)}, u32[]{:S(2)}, u32[]{:S(2)}) collective-permute-start(bf16[8,8192]{1,0:T(8,128)(2,1)S(1)} %collective-permute-done.13), channel_id=1, source_target_pairs={{0,4},{1,3},{2,6},{3,1},{4,0},{5,7},{6,2},{7,5},{8,12},{9,11},{10,... | collective-permute-start | bytes 393224 | tf_op jit(solution)/shard_map/ppermute | solution.py:30
  50.5 5.0 %collective-permute-start.17 = (bf16[8,8192]{1,0:T(8,128)(2,1)S(1)}, bf16[8,8192]{1,0:T(8,128)(2,1)S(1)}, u32[]{:S(2)}, u32[]{:S(2)}) collective-permute-start(bf16[8,8192]{1,0:T(8,128)(2,1)S(1)} %collective-permute-done.15), channel_id=1, source_target_pairs={{0,4},{1,3},{2,6},{3,1},{4,0},{5,7},{6,2},{7,5},{8,12},{9,11},{10,... | collective-permute-start | bytes 393224 | tf_op jit(solution)/shard_map/ppermute | solution.py:30
  55.5 2.0 %collective-permute-start.18 = (bf16[32,8192]{1,0:T(8,128)(2,1)S(1)}, bf16[32,8192]{1,0:T(8,128)(2,1)S(1)}, u32[]{:S(2)}, u32[]{:S(2)}) collective-permute-start(bf16[32,8192]{1,0:T(8,128)(2,1)S(1)} %pad_maximum_fusion.1), channel_id=1, source_target_pairs={{0,1},{1,0},{2,3},{3,2},{4,5},{5,4},{6,7},{7,6},{8,9},{9,8},{10,11... | collective-permute-start | bytes 1572872 | tf_op jit(solution)/shard_map/ppermute | solution.py:34
  55.6 3.5 %collective-permute-start.21 = (bf16[8,8192]{1,0:T(8,128)(2,1)S(1)}, bf16[8,8192]{1,0:T(8,128)(2,1)S(1)}, u32[]{:S(2)}, u32[]{:S(2)}) collective-permute-start(bf16[8,8192]{1,0:T(8,128)(2,1)S(1)} %collective-permute-done.19), channel_id=1, source_target_pairs={{0,1},{1,0},{2,3},{3,2},{4,5},{5,4},{6,7},{7,6},{8,9},{9,8},{10,11... | collective-permute-start | bytes 393224 | tf_op jit(solution)/shard_map/ppermute | solution.py:34
  57.5 1.7 %collective-permute-start.20 = (bf16[24,8192]{1,0:T(8,128)(2,1)S(1)}, bf16[24,8192]{1,0:T(8,128)(2,1)S(1)}, u32[]{:S(2)}, u32[]{:S(2)}) collective-permute-start(bf16[24,8192]{1,0:T(8,128)(2,1)S(1)} %pad_maximum_fusion.3), channel_id=1, source_target_pairs={{0,1},{1,0},{2,3},{3,2},{4,5},{5,4},{6,7},{7,6},{8,9},{9,8},{10,11... | collective-permute-start | bytes 1179656 | tf_op jit(solution)/shard_map/ppermute | solution.py:34

commit v16 on v13

--- a/solution.py
+++ b/solution.py
@@ -260,13 +260,12 @@
     later = jnp.where(final, 0.0, next_sum + after(above, error)).astype(jnp.bfloat16)
 
     heres = [error] + [across(error, chip, chips) for chip in range(1, chips)]
-    afters = [later] + [across(later, chip, chips) for chip in range(1, chips - 1)]
-    last = lowered(after(heres[-1], later), final, group)
+    afters = [later] + [across(later, chip, chips) for chip in range(1, chips)]
     here_near = jnp.concatenate(heres, axis=0)
     here_far = other_core(here_near)
     here_rows = jnp.concatenate([here_near, here_far], axis=0)
-    most = after(jnp.concatenate(afters, axis=0), here_far)
-    after_rows = jnp.concatenate([most, last, other_core(most), other_core(last)], axis=0)
+    after_near = after(jnp.concatenate(afters, axis=0), here_far)
+    after_rows = jnp.concatenate([after_near, other_core(after_near)], axis=0)
     grad = grad_all(after_rows, next_dec, grad_own(here_rows, own_dec), tokens)
     return (error[None], grad)
 

time: 51.3 us -> 51.8 us (level)
  waiting for transfers between devices: 12.4 us -> 13 us
    ppermute x13 -> x14, waiting for transfers between devices: 4.95 us -> 8.28 us  [across(): return lax.ppermute(value, AXIS, pairs)]
    ppermute x2 -> x1, waiting for transfers between devices: 3.19 us -> 0.01 us  [lowered(): lax.ppermute(value, AXIS, [((i + group) % size, i) for i in range(size)])]
    ppermute x13 -> x14, starting transfers between devices: 16.8 us -> 18.6 us  [across(): return lax.ppermute(value, AXIS, pairs)]
    ppermute x2 -> x1, starting transfers between devices: 3.73 us -> 2.4 us  [lowered(): lax.ppermute(value, AXIS, [((i + group) % size, i) for i in range(size)])]
    ppermute x7 -> x6, starting transfers between devices: 1.82 us -> 1.28 us  [other_core(): lax.ppermute(value, AXIS, [(i, i ^ 1) for i in range(lax.axis_size(AXIS))])]
    ppermute x7 -> x6, waiting for transfers between devices: 1.74 us -> 2.19 us  [other_core(): lax.ppermute(value, AXIS, [(i, i ^ 1) for i in range(lax.axis_size(AXIS))])]
  transfers between devices with their start and end apart: 24 -> 23, of which waited for: 11 -> 13; matrix products, arithmetic and copies ran while one was open for 3% -> 3% of each run, Pallas kernels for 14% -> 14%
where the time goes in v16:
time: 51.8 us; the launch traced here: 51.7 us
  starting transfers between devices  25.1 us (48%)
  waiting for transfers between devices  13 us (25%)
  Pallas kernels  9.92 us (19%)
  local copies, waits for them, and re-layouts  1.16 us (2%)
  between operations  0.96 us (2%)
  matrix products  0.8 us (2%)
  other arithmetic  0.73 us (1%)
    ppermute x14, starting transfers between devices, across(): return lax.ppermute(value, AXIS, pairs)  18.6 us
    ppermute x14, waiting for transfers between devices, across(): return lax.ppermute(value, AXIS, pairs)  8.28 us
    pallas_call x1, Pallas kernels, loaded(): pl.pallas_call(load_kernel, out_shape=[pltpu.VMEM(enc.shape[1:], enc.dtyp...  4.72 us
    ppermute x2, starting transfers between devices, raised(): lax.ppermute(value, AXIS, [(i, (i + group) % size) for i in range(size)])  2.78 us
    ppermute x2, waiting for transfers between devices, raised(): lax.ppermute(value, AXIS, [(i, (i + group) % size) for i in range(size)])  2.55 us
    ppermute x1, starting transfers between devices, lowered(): lax.ppermute(value, AXIS, [((i + group) % size, i) for i in range(size)])  2.4 us
    ppermute x6, waiting for transfers between devices, other_core(): lax.ppermute(value, AXIS, [(i, i ^ 1) for i in range(lax.axis_size(AXIS))])  2.19 us
    pallas_call x1, Pallas kernels, grad_all(): pl.pallas_call(functools.partial(grad_all_kernel, tokens), out_shape=jax....  2.03 us
  transfers between devices with their start and end apart: 23, of which 13 were waited for; matrix products, arithmetic and copies ran while one was open for 3% of the time, Pallas kernels for 14%

profile of v16, /device:TPU:0, one launch (start us, length us, event | category | flops | bytes accessed | tf_op | source)
XLA Modules:
  0.0 51.7 jit_solution(13243034882933583099)
XLA Ops:
  0.6 4.0 %collective-permute-start.2 = (bf16[8,8192]{1,0:T(8,128)(2,1)}, bf16[8,8192]{1,0:T(8,128)(2,1)S(1)}, u32[]{:S(2)}, u32[]{:S(2)}) collective-permute-start(bf16[8,8192]{1,0:T(8,128)(2,1)} %bitcast.14), channel_id=1, source_target_pairs={{0,6},{1,7},{2,4},{3,5},{4,2},{5,3},{6,0},{7,1},{8,14},{9,15},{10,... | collective-permute-start | bytes 393224 | tf_op jit(solution)/shard_map/ppermute | solution.py:30
  4.6 0.5 collective-permute-start.1
  5.1 0.1 collective-permute-start
  5.2 0.9 %constant_dynamic-update-slice_fusion.4 = bf16[64,8192]{1,0:T(8,128)(2,1)S(1)} fusion(bf16[8,8192]{1,0:T(8,128)(2,1)} %bitcast.17), kind=kLoop, calls=%fused_computation.27 | loop fusion | bytes 262144
  6.2 0.0 copy-start
  6.2 0.0 copy-start.1
  6.2 0.0 copy-start.3
  6.2 4.7 %load_weights.1 = (bf16[8192,256]{1,0:T(8,128)(2,1)S(1)}, bf16[256,8192]{1,0:T(8,128)(2,1)S(1)}, bf16[256,8192]{1,0:T(8,128)(2,1)S(1)}) custom-call(bf16[1,8192,256]{2,1,0:T(8,128)(2,1)} %enc_hbm.1, bf16[1,2,256,8192]{3,2,1,0:T(8,128)(2,1)} %dec_hbm.1), custom_call_target="tpu_custom_call" | custom-call | bytes 25165824 | tf_op jit(solution)/shard_map/load_weights/pallas_call | solution.py:82
  11.0 0.0 copy-done
  11.0 0.1 gate.1
  11.1 0.0 collective-permute-done.2
  11.1 0.1 collective-permute-start.3
  11.2 0.0 collective-permute-done.1
  11.2 0.1 collective-permute-done
  11.4 0.4 collective-permute-start.4
  11.9 0.9 %collective-permute-done.3 = bf16[16,8192]{1,0:T(8,128)(2,1)S(1)} collective-permute-done((bf16[16,8192]{1,0:T(8,128)(2,1)S(1)}, bf16[16,8192]{1,0:T(8,128)(2,1)S(1)}, u32[]{:S(2)}, u32[]{:S(2)}) %collective-permute-start.3) | collective-permute-done | bytes 262176 | tf_op jit(solution)/shard_map/ppermute | solution.py:34
  12.8 0.4 collective-permute-done.4
  13.2 0.8 %fusion.2.codes_ref = bf16[64,256]{1,0:T(8,128)(2,1)S(1)} fusion(f32[64,256]{1,0:T(8,128)S(1)} %get-tuple-element.25, f32[64,256]{1,0:T(8,128)S(1)} %get-tuple-element.24, bf16[64,8192]{1,0:T(8,128)(2,1)S(1)} %slice_dynamic-update-slice_fusion, bf16[8192,256]{1,0:T(8,128)(2,1)S(1)} %get-tuple-element.21), kind=kOutput, calls=%fused_computation.3 | convolution fusion | flops 268500992 | bytes 5406720 | tf_op jit(solution)/shard_map/dot_general | solution.py:244
  14.0 0.8 %decode.3 = (f32[32,8192]{1,0:T(8,128)S(1)}, bf16[32,8192]{1,0:T(8,128)(2,1)S(1)}) custom-call(bf16[64,256]{1,0:T(8,128)(2,1)S(1)} %fusion.2.codes_ref, bf16[256,8192]{1,0:T(8,128)(2,1)S(1)} %get-tuple-element.30.dec_ref), custom_call_target="tpu_custom_call" | custom-call | flops 268435456 | bytes 4194304 | tf_op jit(solution)/shard_map/decode/pallas_call | solution.py:159
  14.8 0.3 collective-permute-start.8
  15.1 0.8 %decode.2 = (f32[32,8192]{1,0:T(8,128)S(1)}, bf16[32,8192]{1,0:T(8,128)(2,1)S(1)}) custom-call(bf16[64,256]{1,0:T(8,128)(2,1)S(1)} %fusion.2.codes_ref, bf16[256,8192]{1,0:T(8,128)(2,1)S(1)} %get-tuple-element.26.dec_ref), custom_call_target="tpu_custom_call" | custom-call | flops 268435456 | bytes 4194304 | tf_op jit(solution)/shard_map/decode/pallas_call | solution.py:159
  15.9 0.3 collective-permute-start.5
  16.3 0.5 collective-permute-done.8
  16.8 0.1 fusion.9
  16.9 2.0 %collective-permute-start.9 = (bf16[8,8192]{1,0:T(8,128)(2,1)S(1)}, bf16[8,8192]{1,0:T(8,128)(2,1)S(1)}, u32[]{:S(2)}, u32[]{:S(2)}) collective-permute-start(bf16[8,8192]{1,0:T(8,128)(2,1)S(1)} %get-tuple-element.46), channel_id=1, source_target_pairs={{0,8},{1,9},{2,10},{3,11},{4,12},{5,13},{6,14},{7,15},{8,16},{9,17... | collective-permute-start | bytes 393224 | tf_op jit(solution)/shard_map/ppermute | solution.py:39
  19.0 1.5 %collective-permute-start.12 = (bf16[8,8192]{1,0:T(8,128)(2,1)S(1)}, bf16[8,8192]{1,0:T(8,128)(2,1)S(1)}, u32[]{:S(2)}, u32[]{:S(2)}) collective-permute-start(bf16[8,8192]{1,0:T(8,128)(2,1)S(1)} %get-tuple-element.47), channel_id=1, source_target_pairs={{0,4},{1,3},{2,6},{3,1},{4,0},{5,7},{6,2},{7,5},{8,12},{9,11},{10,... | collective-permute-start | bytes 393224 | tf_op jit(solution)/shard_map/ppermute | solution.py:30
  20.5 1.5 %collective-permute-start.11 = (bf16[8,8192]{1,0:T(8,128)(2,1)S(1)}, bf16[8,8192]{1,0:T(8,128)(2,1)S(1)}, u32[]{:S(2)}, u32[]{:S(2)}) collective-permute-start(bf16[8,8192]{1,0:T(8,128)(2,1)S(1)} %get-tuple-element.48), channel_id=1, source_target_pairs={{0,2},{1,5},{2,0},{3,7},{4,6},{5,1},{6,4},{7,3},{8,10},{9,13},{10,... | collective-permute-start | bytes 393224 | tf_op jit(solution)/shard_map/ppermute | solution.py:30
  22.0 0.0 collective-permute-done.5
  22.0 0.1 fusion.8
  22.2 0.6 %collective-permute-start.6 = (bf16[8,8192]{1,0:T(8,128)(2,1)S(1)}, bf16[8,8192]{1,0:T(8,128)(2,1)S(1)}, u32[]{:S(2)}, u32[]{:S(2)}) collective-permute-start(bf16[8,8192]{1,0:T(8,128)(2,1)S(1)} %get-tuple-element.44), channel_id=1, source_target_pairs={{0,2},{1,5},{2,0},{3,7},{4,6},{5,1},{6,4},{7,3},{8,10},{9,13},{10,... | collective-permute-start | bytes 393224 | tf_op jit(solution)/shard_map/ppermute | solution.py:30
  22.7 0.5 collective-permute-start.7
  23.2 1.6 %collective-permute-done.9 = bf16[8,8192]{1,0:T(8,128)(2,1)S(1)} collective-permute-done((bf16[8,8192]{1,0:T(8,128)(2,1)S(1)}, bf16[8,8192]{1,0:T(8,128)(2,1)S(1)}, u32[]{:S(2)}, u32[]{:S(2)}) %collective-permute-start.9) | collective-permute-done | bytes 131104 | tf_op jit(solution)/shard_map/ppermute | solution.py:39
  24.9 2.5 %collective-permute-start.10 = (bf16[8,8192]{1,0:T(8,128)(2,1)S(1)}, bf16[8,8192]{1,0:T(8,128)(2,1)S(1)}, u32[]{:S(2)}, u32[]{:S(2)}) collective-permute-start(bf16[8,8192]{1,0:T(8,128)(2,1)S(1)} %slice_add_fusion.1), channel_id=1, source_target_pairs={{0,6},{1,7},{2,4},{3,5},{4,2},{5,3},{6,0},{7,1},{8,14},{9,15},{10,... | collective-permute-start | bytes 393224 | tf_op jit(solution)/shard_map/ppermute | solution.py:30
  27.4 0.0 collective-permute-done.12
  27.4 0.0 collective-permute-done.11
  27.5 0.8 %collective-permute-start.13 = (bf16[8,8192]{1,0:T(8,128)(2,1)S(1)}, bf16[8,8192]{1,0:T(8,128)(2,1)S(1)}, u32[]{:S(2)}, u32[]{:S(2)}) collective-permute-start(bf16[8,8192]{1,0:T(8,128)(2,1)S(1)} %convert_element_type.71), channel_id=1, source_target_pairs={{0,8},{1,9},{2,10},{3,11},{4,12},{5,13},{6,14},{7,15},{8,16},{9,17... | collective-permute-start | bytes 393224 | tf_op jit(solution)/shard_map/ppermute | solution.py:39
  28.3 0.2 collective-permute-done.6
  28.4 0.0 collective-permute-done.7
  28.4 2.6 %collective-permute-done.10 = bf16[8,8192]{1,0:T(8,128)(2,1)S(1)} collective-permute-done((bf16[8,8192]{1,0:T(8,128)(2,1)S(1)}, bf16[8,8192]{1,0:T(8,128)(2,1)S(1)}, u32[]{:S(2)}, u32[]{:S(2)}) %collective-permute-start.10) | collective-permute-done | bytes 131104 | tf_op jit(solution)/shard_map/ppermute | solution.py:30
  31.0 0.1 fusion.7
  31.1 2.4 %collective-permute-start.14 = (bf16[8,8192]{1,0:T(8,128)(2,1)S(1)}, bf16[8,8192]{1,0:T(8,128)(2,1)S(1)}, u32[]{:S(2)}, u32[]{:S(2)}) collective-permute-start(bf16[8,8192]{1,0:T(8,128)(2,1)S(1)} %fusion.7), channel_id=1, source_target_pairs={{8,0},{9,1},{10,2},{11,3},{12,4},{13,5},{14,6},{15,7},{16,8},{17,9... | collective-permute-start | bytes 393224 | tf_op jit(solution)/shard_map/ppermute | solution.py:45
  33.5 0.9 %collective-permute-done.13 = bf16[8,8192]{1,0:T(8,128)(2,1)S(1)} collective-permute-done((bf16[8,8192]{1,0:T(8,128)(2,1)S(1)}, bf16[8,8192]{1,0:T(8,128)(2,1)S(1)}, u32[]{:S(2)}, u32[]{:S(2)}) %collective-permute-start.13) | collective-permute-done | bytes 131104 | tf_op jit(solution)/shard_map/ppermute | solution.py:39
  34.4 0.1 constant_dynamic-update-slice_fusion.9
  34.5 0.0 copy-start.4
  34.5 1.5 %collective-permute-start.20 = (bf16[8,8192]{1,0:T(8,128)(2,1)S(1)}, bf16[8,8192]{1,0:T(8,128)(2,1)S(1)}, u32[]{:S(2)}, u32[]{:S(2)}) collective-permute-start(bf16[8,8192]{1,0:T(8,128)(2,1)S(1)} %get-tuple-element.39), channel_id=1, source_target_pairs={{0,6},{1,7},{2,4},{3,5},{4,2},{5,3},{6,0},{7,1},{8,14},{9,15},{10,... | collective-permute-start | bytes 393224 | tf_op jit(solution)/shard_map/ppermute | solution.py:30
  36.0 0.6 %collective-permute-start.19 = (bf16[8,8192]{1,0:T(8,128)(2,1)S(1)}, bf16[8,8192]{1,0:T(8,128)(2,1)S(1)}, u32[]{:S(2)}, u32[]{:S(2)}) collective-permute-start(bf16[8,8192]{1,0:T(8,128)(2,1)S(1)} %get-tuple-element.39), channel_id=1, source_target_pairs={{0,4},{1,3},{2,6},{3,1},{4,0},{5,7},{6,2},{7,5},{8,12},{9,11},{10,... | collective-permute-start | bytes 393224 | tf_op jit(solution)/shard_map/ppermute | solution.py:30
  36.6 1.5 %collective-permute-start.18 = (bf16[8,8192]{1,0:T(8,128)(2,1)S(1)}, bf16[8,8192]{1,0:T(8,128)(2,1)S(1)}, u32[]{:S(2)}, u32[]{:S(2)}) collective-permute-start(bf16[8,8192]{1,0:T(8,128)(2,1)S(1)} %get-tuple-element.39), channel_id=1, source_target_pairs={{0,2},{1,5},{2,0},{3,7},{4,6},{5,1},{6,4},{7,3},{8,10},{9,13},{10,... | collective-permute-start | bytes 393224 | tf_op jit(solution)/shard_map/ppermute | solution.py:30
  38.1 0.0 collective-permute-done.14
  38.2 1.5 %collective-permute-start.17 = (bf16[8,8192]{1,0:T(8,128)(2,1)S(1)}, bf16[8,8192]{1,0:T(8,128)(2,1)S(1)}, u32[]{:S(2)}, u32[]{:S(2)}) collective-permute-start(bf16[8,8192]{1,0:T(8,128)(2,1)S(1)} %select_convert_fusion), channel_id=1, source_target_pairs={{0,6},{1,7},{2,4},{3,5},{4,2},{5,3},{6,0},{7,1},{8,14},{9,15},{10,... | collective-permute-start | bytes 393224 | tf_op jit(solution)/shard_map/ppermute | solution.py:30
  39.6 0.6 %collective-permute-start.16 = (bf16[8,8192]{1,0:T(8,128)(2,1)S(1)}, bf16[8,8192]{1,0:T(8,128)(2,1)S(1)}, u32[]{:S(2)}, u32[]{:S(2)}) collective-permute-start(bf16[8,8192]{1,0:T(8,128)(2,1)S(1)} %select_convert_fusion), channel_id=1, source_target_pairs={{0,4},{1,3},{2,6},{3,1},{4,0},{5,7},{6,2},{7,5},{8,12},{9,11},{10,... | collective-permute-start | bytes 393224 | tf_op jit(solution)/shard_map/ppermute | solution.py:30
  40.2 0.5 %collective-permute-done.20 = bf16[8,8192]{1,0:T(8,128)(2,1)S(1)} collective-permute-done((bf16[8,8192]{1,0:T(8,128)(2,1)S(1)}, bf16[8,8192]{1,0:T(8,128)(2,1)S(1)}, u32[]{:S(2)}, u32[]{:S(2)}) %collective-permute-start.20) | collective-permute-done | bytes 131104 | tf_op jit(solution)/shard_map/ppermute | solution.py:30
  40.7 1.8 %collective-permute-start.15 = (bf16[8,8192]{1,0:T(8,128)(2,1)S(1)}, bf16[8,8192]{1,0:T(8,128)(2,1)S(1)}, u32[]{:S(2)}, u32[]{:S(2)}) collective-permute-start(bf16[8,8192]{1,0:T(8,128)(2,1)S(1)} %select_convert_fusion), channel_id=1, source_target_pairs={{0,2},{1,5},{2,0},{3,7},{4,6},{5,1},{6,4},{7,3},{8,10},{9,13},{10,... | collective-permute-start | bytes 393224 | tf_op jit(solution)/shard_map/ppermute | solution.py:30
  42.6 3.0 %collective-permute-done.19 = bf16[8,8192]{1,0:T(8,128)(2,1)S(1)} collective-permute-done((bf16[8,8192]{1,0:T(8,128)(2,1)S(1)}, bf16[8,8192]{1,0:T(8,128)(2,1)S(1)}, u32[]{:S(2)}, u32[]{:S(2)}) %collective-permute-start.19) | collective-permute-done | bytes 131104 | tf_op jit(solution)/shard_map/ppermute | solution.py:30
  45.5 0.0 collective-permute-done.18
  45.6 0.1 collective-permute-start.21
  45.7 0.6 %collective-permute-done.17 = bf16[8,8192]{1,0:T(8,128)(2,1)S(1)} collective-permute-done((bf16[8,8192]{1,0:T(8,128)(2,1)S(1)}, bf16[8,8192]{1,0:T(8,128)(2,1)S(1)}, u32[]{:S(2)}, u32[]{:S(2)}) %collective-permute-start.17) | collective-permute-done | bytes 131104 | tf_op jit(solution)/shard_map/ppermute | solution.py:30
  46.3 1.3 %collective-permute-done.16 = bf16[8,8192]{1,0:T(8,128)(2,1)S(1)} collective-permute-done((bf16[8,8192]{1,0:T(8,128)(2,1)S(1)}, bf16[8,8192]{1,0:T(8,128)(2,1)S(1)}, u32[]{:S(2)}, u32[]{:S(2)}) %collective-permute-start.16) | collective-permute-done | bytes 131104 | tf_op jit(solution)/shard_map/ppermute | solution.py:30
  47.6 0.0 collective-permute-done.15
  47.6 0.0 collective-permute-done.21
  47.6 0.1 collective-permute-start.22
  47.7 1.4 %grad_own.1 = (f32[64,256]{1,0:T(8,128)S(1)}, f32[8,128]{1,0:T(8,128)}) custom-call(bf16[64,8192]{1,0:T(8,128)(2,1)S(1)} %constant_dynamic-update-slice_fusion.5.rows_ref, bf16[256,8192]{1,0:T(8,128)(2,1)S(1)} %get-tuple-element.26.dec_ref), custom_call_target="tpu_custom_call" | custom-call | flops 268435456 | bytes 4194304 | tf_op jit(solution)/shard_map/grad_own/pallas_call | solution.py:194
  49.1 0.4 collective-permute-done.22
  49.6 0.1 pad_maximum_fusion.rows_ref
  49.7 2.0 %grad_all.1 = f32[1,64,256]{2,1,0:T(8,128)} custom-call(bf16[64,8192]{1,0:T(8,128)(2,1)S(1)} %pad_maximum_fusion.rows_ref, bf16[256,8192]{1,0:T(8,128)(2,1)S(1)} %get-tuple-element.30.dec_ref, f32[64,256]{1,0:T(8,128)S(1)} %get-tuple-element.37.own_ref), custom_call_target="tpu_custom_call" | custom-call | flops 268435456 | bytes 4194304 | tf_op jit(solution)/shard_map/grad_all/pallas_call | solution.py:206
  (26 shorter events, 0.4 us)
Async XLA Ops:
  0.6 10.5 %collective-permute-start.2 = (bf16[8,8192]{1,0:T(8,128)(2,1)}, bf16[8,8192]{1,0:T(8,128)(2,1)S(1)}, u32[]{:S(2)}, u32[]{:S(2)}) collective-permute-start(bf16[8,8192]{1,0:T(8,128)(2,1)} %bitcast.14), channel_id=1, source_target_pairs={{0,6},{1,7},{2,4},{3,5},{4,2},{5,3},{6,0},{7,1},{8,14},{9,15},{10,... | collective-permute-start | bytes 393224 | tf_op jit(solution)/shard_map/ppermute | solution.py:30
  4.6 6.6 %collective-permute-start.1 = (bf16[8,8192]{1,0:T(8,128)(2,1)}, bf16[8,8192]{1,0:T(8,128)(2,1)S(1)}, u32[]{:S(2)}, u32[]{:S(2)}) collective-permute-start(bf16[8,8192]{1,0:T(8,128)(2,1)} %bitcast.15), channel_id=1, source_target_pairs={{0,4},{1,3},{2,6},{3,1},{4,0},{5,7},{6,2},{7,5},{8,12},{9,11},{10,... | collective-permute-start | bytes 393224 | tf_op jit(solution)/shard_map/ppermute | solution.py:30
  5.1 6.3 %collective-permute-start = (bf16[8,8192]{1,0:T(8,128)(2,1)}, bf16[8,8192]{1,0:T(8,128)(2,1)S(1)}, u32[]{:S(2)}, u32[]{:S(2)}) collective-permute-start(bf16[8,8192]{1,0:T(8,128)(2,1)} %bitcast.16), channel_id=1, source_target_pairs={{0,2},{1,5},{2,0},{3,7},{4,6},{5,1},{6,4},{7,3},{8,10},{9,13},{10,... | collective-permute-start | bytes 393224 | tf_op jit(solution)/shard_map/ppermute | solution.py:30
  6.2 4.8 %copy-start = (s32[1,2,2]{2,1,0:T(2,128)S(1)}, s32[1,2,2]{2,1,0:T(2,128)}, u32[]{:S(2)}) copy-start(s32[1,2,2]{2,1,0:T(2,128)} %param.9) | copy-start | bytes 52
  6.2 4.8 %copy-start.1 = (bf16[1,256]{1,0:T(2,128)(2,1)S(1)}, bf16[1,256]{1,0:T(2,128)(2,1)}, u32[]{:S(2)}) copy-start(bf16[1,256]{1,0:T(2,128)(2,1)} %bias_ref) | copy-start | bytes 1540
  6.2 4.9 %copy-start.3 = (bf16[1,8,8192]{2,1,0:T(8,128)(2,1)S(1)}, bf16[1,8,8192]{2,1,0:T(8,128)(2,1)}, u32[]{:S(2)}) copy-start(bf16[1,8,8192]{2,1,0:T(8,128)(2,1)} %param.6) | copy-start | bytes 393220
  11.1 1.6 %collective-permute-start.3 = (bf16[16,8192]{1,0:T(8,128)(2,1)S(1)}, bf16[16,8192]{1,0:T(8,128)(2,1)S(1)}, u32[]{:S(2)}, u32[]{:S(2)}) collective-permute-start(bf16[16,8192]{1,0:T(8,128)(2,1)S(1)} %pad_maximum_fusion.3), channel_id=1, source_target_pairs={{0,1},{1,0},{2,3},{3,2},{4,5},{5,4},{6,7},{7,6},{8,9},{9,8},{10,11... | collective-permute-start | bytes 786440 | tf_op jit(solution)/shard_map/ppermute | solution.py:34
  11.4 1.7 %collective-permute-start.4 = (bf16[16,8192]{1,0:T(8,128)(2,1)S(1)}, bf16[16,8192]{1,0:T(8,128)(2,1)S(1)}, u32[]{:S(2)}, u32[]{:S(2)}) collective-permute-start(bf16[16,8192]{1,0:T(8,128)(2,1)S(1)} %pad_maximum_fusion.4), channel_id=1, source_target_pairs={{0,1},{1,0},{2,3},{3,2},{4,5},{5,4},{6,7},{7,6},{8,9},{9,8},{10,11... | collective-permute-start | bytes 786440 | tf_op jit(solution)/shard_map/ppermute | solution.py:34
  14.8 2.0 %collective-permute-start.8 = (bf16[32,8192]{1,0:T(8,128)(2,1)S(1)}, bf16[32,8192]{1,0:T(8,128)(2,1)S(1)}, u32[]{:S(2)}, u32[]{:S(2)}) collective-permute-start(bf16[32,8192]{1,0:T(8,128)(2,1)S(1)} %get-tuple-element.32), channel_id=1, source_target_pairs={{0,1},{1,0},{2,3},{3,2},{4,5},{5,4},{6,7},{7,6},{8,9},{9,8},{10,11... | collective-permute-start | bytes 1572872 | tf_op jit(solution)/shard_map/ppermute | solution.py:34
  15.9 6.1 %collective-permute-start.5 = (bf16[32,8192]{1,0:T(8,128)(2,1)S(1)}, bf16[32,8192]{1,0:T(8,128)(2,1)S(1)}, u32[]{:S(2)}, u32[]{:S(2)}) collective-permute-start(bf16[32,8192]{1,0:T(8,128)(2,1)S(1)} %get-tuple-element.28), channel_id=1, source_target_pairs={{0,1},{1,0},{2,3},{3,2},{4,5},{5,4},{6,7},{7,6},{8,9},{9,8},{10,11... | collective-permute-start | bytes 1572872 | tf_op jit(solution)/shard_map/ppermute | solution.py:34
  16.8 14.2 %copy-start.2 = (bf16[1,8,8192]{2,1,0:T(8,128)(2,1)S(1)}, bf16[1,8,8192]{2,1,0:T(8,128)(2,1)}, u32[]{:S(2)}) copy-start(bf16[1,8,8192]{2,1,0:T(8,128)(2,1)} %param.11) | copy-start | bytes 393220
  16.9 8.0 %collective-permute-start.9 = (bf16[8,8192]{1,0:T(8,128)(2,1)S(1)}, bf16[8,8192]{1,0:T(8,128)(2,1)S(1)}, u32[]{:S(2)}, u32[]{:S(2)}) collective-permute-start(bf16[8,8192]{1,0:T(8,128)(2,1)S(1)} %get-tuple-element.46), channel_id=1, source_target_pairs={{0,8},{1,9},{2,10},{3,11},{4,12},{5,13},{6,14},{7,15},{8,16},{9,17... | collective-permute-start | bytes 393224 | tf_op jit(solution)/shard_map/ppermute | solution.py:39
  19.0 8.5 %collective-permute-start.12 = (bf16[8,8192]{1,0:T(8,128)(2,1)S(1)}, bf16[8,8192]{1,0:T(8,128)(2,1)S(1)}, u32[]{:S(2)}, u32[]{:S(2)}) collective-permute-start(bf16[8,8192]{1,0:T(8,128)(2,1)S(1)} %get-tuple-element.47), channel_id=1, source_target_pairs={{0,4},{1,3},{2,6},{3,1},{4,0},{5,7},{6,2},{7,5},{8,12},{9,11},{10,... | collective-permute-start | bytes 393224 | tf_op jit(solution)/shard_map/ppermute | solution.py:30
  20.5 7.0 %collective-permute-start.11 = (bf16[8,8192]{1,0:T(8,128)(2,1)S(1)}, bf16[8,8192]{1,0:T(8,128)(2,1)S(1)}, u32[]{:S(2)}, u32[]{:S(2)}) collective-permute-start(bf16[8,8192]{1,0:T(8,128)(2,1)S(1)} %get-tuple-element.48), channel_id=1, source_target_pairs={{0,2},{1,5},{2,0},{3,7},{4,6},{5,1},{6,4},{7,3},{8,10},{9,13},{10,... | collective-permute-start | bytes 393224 | tf_op jit(solution)/shard_map/ppermute | solution.py:30
  22.2 6.3 %collective-permute-start.6 = (bf16[8,8192]{1,0:T(8,128)(2,1)S(1)}, bf16[8,8192]{1,0:T(8,128)(2,1)S(1)}, u32[]{:S(2)}, u32[]{:S(2)}) collective-permute-start(bf16[8,8192]{1,0:T(8,128)(2,1)S(1)} %get-tuple-element.44), channel_id=1, source_target_pairs={{0,2},{1,5},{2,0},{3,7},{4,6},{5,1},{6,4},{7,3},{8,10},{9,13},{10,... | collective-permute-start | bytes 393224 | tf_op jit(solution)/shard_map/ppermute | solution.py:30
  22.7 5.7 %collective-permute-start.7 = (bf16[8,8192]{1,0:T(8,128)(2,1)S(1)}, bf16[8,8192]{1,0:T(8,128)(2,1)S(1)}, u32[]{:S(2)}, u32[]{:S(2)}) collective-permute-start(bf16[8,8192]{1,0:T(8,128)(2,1)S(1)} %get-tuple-element.45), channel_id=1, source_target_pairs={{0,4},{1,3},{2,6},{3,1},{4,0},{5,7},{6,2},{7,5},{8,12},{9,11},{10,... | collective-permute-start | bytes 393224 | tf_op jit(solution)/shard_map/ppermute | solution.py:30
  24.9 6.1 %collective-permute-start.10 = (bf16[8,8192]{1,0:T(8,128)(2,1)S(1)}, bf16[8,8192]{1,0:T(8,128)(2,1)S(1)}, u32[]{:S(2)}, u32[]{:S(2)}) collective-permute-start(bf16[8,8192]{1,0:T(8,128)(2,1)S(1)} %slice_add_fusion.1), channel_id=1, source_target_pairs={{0,6},{1,7},{2,4},{3,5},{4,2},{5,3},{6,0},{7,1},{8,14},{9,15},{10,... | collective-permute-start | bytes 393224 | tf_op jit(solution)/shard_map/ppermute | solution.py:30
  27.5 6.9 %collective-permute-start.13 = (bf16[8,8192]{1,0:T(8,128)(2,1)S(1)}, bf16[8,8192]{1,0:T(8,128)(2,1)S(1)}, u32[]{:S(2)}, u32[]{:S(2)}) collective-permute-start(bf16[8,8192]{1,0:T(8,128)(2,1)S(1)} %convert_element_type.71), channel_id=1, source_target_pairs={{0,8},{1,9},{2,10},{3,11},{4,12},{5,13},{6,14},{7,15},{8,16},{9,17... | collective-permute-start | bytes 393224 | tf_op jit(solution)/shard_map/ppermute | solution.py:39
  31.1 7.0 %collective-permute-start.14 = (bf16[8,8192]{1,0:T(8,128)(2,1)S(1)}, bf16[8,8192]{1,0:T(8,128)(2,1)S(1)}, u32[]{:S(2)}, u32[]{:S(2)}) collective-permute-start(bf16[8,8192]{1,0:T(8,128)(2,1)S(1)} %fusion.7), channel_id=1, source_target_pairs={{8,0},{9,1},{10,2},{11,3},{12,4},{13,5},{14,6},{15,7},{16,8},{17,9... | collective-permute-start | bytes 393224 | tf_op jit(solution)/shard_map/ppermute | solution.py:45
  34.5 14.6 %copy-start.4 = (bf16[8,8192]{1,0:T(8,128)(2,1)}, bf16[8,8192]{1,0:T(8,128)(2,1)S(1)}, u32[]{:S(2)}) copy-start(bf16[8,8192]{1,0:T(8,128)(2,1)S(1)} %get-tuple-element.39) | copy-start | bytes 393220
  34.5 6.2 %collective-permute-start.20 = (bf16[8,8192]{1,0:T(8,128)(2,1)S(1)}, bf16[8,8192]{1,0:T(8,128)(2,1)S(1)}, u32[]{:S(2)}, u32[]{:S(2)}) collective-permute-start(bf16[8,8192]{1,0:T(8,128)(2,1)S(1)} %get-tuple-element.39), channel_id=1, source_target_pairs={{0,6},{1,7},{2,4},{3,5},{4,2},{5,3},{6,0},{7,1},{8,14},{9,15},{10,... | collective-permute-start | bytes 393224 | tf_op jit(solution)/shard_map/ppermute | solution.py:30
  36.0 9.5 %collective-permute-start.19 = (bf16[8,8192]{1,0:T(8,128)(2,1)S(1)}, bf16[8,8192]{1,0:T(8,128)(2,1)S(1)}, u32[]{:S(2)}, u32[]{:S(2)}) collective-permute-start(bf16[8,8192]{1,0:T(8,128)(2,1)S(1)} %get-tuple-element.39), channel_id=1, source_target_pairs={{0,4},{1,3},{2,6},{3,1},{4,0},{5,7},{6,2},{7,5},{8,12},{9,11},{10,... | collective-permute-start | bytes 393224 | tf_op jit(solution)/shard_map/ppermute | solution.py:30
  36.6 9.0 %collective-permute-start.18 = (bf16[8,8192]{1,0:T(8,128)(2,1)S(1)}, bf16[8,8192]{1,0:T(8,128)(2,1)S(1)}, u32[]{:S(2)}, u32[]{:S(2)}) collective-permute-start(bf16[8,8192]{1,0:T(8,128)(2,1)S(1)} %get-tuple-element.39), channel_id=1, source_target_pairs={{0,2},{1,5},{2,0},{3,7},{4,6},{5,1},{6,4},{7,3},{8,10},{9,13},{10,... | collective-permute-start | bytes 393224 | tf_op jit(solution)/shard_map/ppermute | solution.py:30
  38.2 8.1 %collective-permute-start.17 = (bf16[8,8192]{1,0:T(8,128)(2,1)S(1)}, bf16[8,8192]{1,0:T(8,128)(2,1)S(1)}, u32[]{:S(2)}, u32[]{:S(2)}) collective-permute-start(bf16[8,8192]{1,0:T(8,128)(2,1)S(1)} %select_convert_fusion), channel_id=1, source_target_pairs={{0,6},{1,7},{2,4},{3,5},{4,2},{5,3},{6,0},{7,1},{8,14},{9,15},{10,... | collective-permute-start | bytes 393224 | tf_op jit(solution)/shard_map/ppermute | solution.py:30
  39.6 7.9 %collective-permute-start.16 = (bf16[8,8192]{1,0:T(8,128)(2,1)S(1)}, bf16[8,8192]{1,0:T(8,128)(2,1)S(1)}, u32[]{:S(2)}, u32[]{:S(2)}) collective-permute-start(bf16[8,8192]{1,0:T(8,128)(2,1)S(1)} %select_convert_fusion), channel_id=1, source_target_pairs={{0,4},{1,3},{2,6},{3,1},{4,0},{5,7},{6,2},{7,5},{8,12},{9,11},{10,... | collective-permute-start | bytes 393224 | tf_op jit(solution)/shard_map/ppermute | solution.py:30
  40.7 6.8 %collective-permute-start.15 = (bf16[8,8192]{1,0:T(8,128)(2,1)S(1)}, bf16[8,8192]{1,0:T(8,128)(2,1)S(1)}, u32[]{:S(2)}, u32[]{:S(2)}) collective-permute-start(bf16[8,8192]{1,0:T(8,128)(2,1)S(1)} %select_convert_fusion), channel_id=1, source_target_pairs={{0,2},{1,5},{2,0},{3,7},{4,6},{5,1},{6,4},{7,3},{8,10},{9,13},{10,... | collective-permute-start | bytes 393224 | tf_op jit(solution)/shard_map/ppermute | solution.py:30
  45.6 2.0 %collective-permute-start.21 = (bf16[32,8192]{1,0:T(8,128)(2,1)S(1)}, bf16[32,8192]{1,0:T(8,128)(2,1)S(1)}, u32[]{:S(2)}, u32[]{:S(2)}) collective-permute-start(bf16[32,8192]{1,0:T(8,128)(2,1)S(1)} %pad_maximum_fusion.2), channel_id=1, source_target_pairs={{0,1},{1,0},{2,3},{3,2},{4,5},{5,4},{6,7},{7,6},{8,9},{9,8},{10,11... | collective-permute-start | bytes 1572872 | tf_op jit(solution)/shard_map/ppermute | solution.py:34
  47.6 2.0 %collective-permute-start.22 = (bf16[32,8192]{1,0:T(8,128)(2,1)S(1)}, bf16[32,8192]{1,0:T(8,128)(2,1)S(1)}, u32[]{:S(2)}, u32[]{:S(2)}) collective-permute-start(bf16[32,8192]{1,0:T(8,128)(2,1)S(1)} %pad_maximum_fusion.1), channel_id=1, source_target_pairs={{0,1},{1,0},{2,3},{3,2},{4,5},{5,4},{6,7},{7,6},{8,9},{9,8},{10,11... | collective-permute-start | bytes 1572872 | tf_op jit(solution)/shard_map/ppermute | solution.py:34

commit v17 on v16

--- a/solution.py
+++ b/solution.py
@@ -40,10 +40,14 @@
     return jnp.where(first, jnp.zeros_like(came), came)
 
 
-def lowered(value, final, group):
+def shifted(value, group):
     size = lax.axis_size(AXIS)
-    came = lax.ppermute(value, AXIS, [((i + group) % size, i) for i in range(size)])
-    return jnp.where(final, jnp.zeros_like(came), came)
+    return lax.ppermute(value, AXIS, [(i, i + group) for i in range(size - group)])
+
+
+def lowered(value, group):
+    size = lax.axis_size(AXIS)
+    return lax.ppermute(value, AXIS, [(i + group, i) for i in range(size - group)])
 
 
 def after(values, done):
@@ -254,8 +258,8 @@
     next_sum = after(summed(nexts, range(1, chips - 1)), owns[-1])
     own_less = summed(owns, range(1, chips - 1)) - target[0].astype(jnp.float32) + crossed
 
-    below = raised(next_sum.astype(jnp.bfloat16), first, group).astype(jnp.float32)
-    above = lowered(own_less.astype(jnp.bfloat16), final, group).astype(jnp.float32)
+    below = shifted(next_sum.astype(jnp.bfloat16), group).astype(jnp.float32)
+    above = lowered(own_less.astype(jnp.bfloat16), group).astype(jnp.float32)
     error = (own_less + below).astype(jnp.bfloat16)
     later = jnp.where(final, 0.0, next_sum + after(above, error)).astype(jnp.bfloat16)
 

time: 51.8 us -> 51.1 us (0.986)
  waiting for transfers between devices: 13 us -> 11.4 us
    ppermute x14, waiting for transfers between devices: 8.28 us -> 5.64 us  [across(): return lax.ppermute(value, AXIS, pairs)]
    ppermute x1 -> x2, waiting for transfers between devices: 0.01 us -> 1.95 us  [the longest x1 1.74 us: lowered(): lax.ppermute(value, AXIS, [(i + group, i) for i in range(size - group)])]
    ppermute x1 -> x2, starting transfers between devices: 2.4 us -> 3.91 us  [the longest x1 2.61 us: shifted(): lax.ppermute(value, AXIS, [(i, i + group) for i in range(size - group)])]
    ppermute x2 -> x1, waiting for transfers between devices: 2.55 us -> 1.64 us  [raised(): lax.ppermute(value, AXIS, [(i, (i + group) % size) for i in range(size)])]
    ppermute x2 -> x1, starting transfers between devices: 2.78 us -> 2.03 us  [raised(): lax.ppermute(value, AXIS, [(i, (i + group) % size) for i in range(size)])]
  transfers between devices with their start and end apart: 23 -> 23, of which waited for: 13 -> 12; matrix products, arithmetic and copies ran while one was open for 3% -> 3% of each run, Pallas kernels for 14% -> 14%
where the time goes in v17:
time: 51.1 us; the launch traced here: 50.6 us
  starting transfers between devices  25.5 us (50%)
  waiting for transfers between devices  11.4 us (22%)
  Pallas kernels  9.93 us (19%)
  local copies, waits for them, and re-layouts  1.16 us (2%)
  between operations  0.99 us (2%)
  matrix products  0.8 us (2%)
  other arithmetic  0.72 us (1%)
    ppermute x14, starting transfers between devices, across(): return lax.ppermute(value, AXIS, pairs)  18.3 us
    ppermute x14, waiting for transfers between devices, across(): return lax.ppermute(value, AXIS, pairs)  5.64 us
    pallas_call x1, Pallas kernels, loaded(): pl.pallas_call(load_kernel, out_shape=[pltpu.VMEM(enc.shape[1:], enc.dtyp...  4.72 us
    ppermute x1, starting transfers between devices, shifted(): lax.ppermute(value, AXIS, [(i, i + group) for i in range(size - group)])  2.61 us
    ppermute x6, waiting for transfers between devices, other_core(): lax.ppermute(value, AXIS, [(i, i ^ 1) for i in range(lax.axis_size(AXIS))])  2.19 us
    pallas_call x1, Pallas kernels, grad_all(): pl.pallas_call(functools.partial(grad_all_kernel, tokens), out_shape=jax....  2.03 us
    ppermute x1, starting transfers between devices, raised(): lax.ppermute(value, AXIS, [(i, (i + group) % size) for i in range(size)])  2.03 us
    ppermute x1, waiting for transfers between devices, lowered(): lax.ppermute(value, AXIS, [(i + group, i) for i in range(size - group)])  1.74 us
  transfers between devices with their start and end apart: 23, of which 12 were waited for; matrix products, arithmetic and copies ran while one was open for 3% of the time, Pallas kernels for 14%

profile of v17, /device:TPU:0, one launch (start us, length us, event | category | flops | bytes accessed | tf_op | source)
XLA Modules:
  0.0 50.6 jit_solution(5519566737295513936)
XLA Ops:
  0.6 4.0 %collective-permute-start.2 = (bf16[8,8192]{1,0:T(8,128)(2,1)}, bf16[8,8192]{1,0:T(8,128)(2,1)S(1)}, u32[]{:S(2)}, u32[]{:S(2)}) collective-permute-start(bf16[8,8192]{1,0:T(8,128)(2,1)} %bitcast.14), channel_id=1, source_target_pairs={{0,6},{1,7},{2,4},{3,5},{4,2},{5,3},{6,0},{7,1},{8,14},{9,15},{10,... | collective-permute-start | bytes 393224 | tf_op jit(solution)/shard_map/ppermute | solution.py:30
  4.6 0.5 %collective-permute-start.1 = (bf16[8,8192]{1,0:T(8,128)(2,1)}, bf16[8,8192]{1,0:T(8,128)(2,1)S(1)}, u32[]{:S(2)}, u32[]{:S(2)}) collective-permute-start(bf16[8,8192]{1,0:T(8,128)(2,1)} %bitcast.15), channel_id=1, source_target_pairs={{0,4},{1,3},{2,6},{3,1},{4,0},{5,7},{6,2},{7,5},{8,12},{9,11},{10,... | collective-permute-start | bytes 393224 | tf_op jit(solution)/shard_map/ppermute | solution.py:30
  5.1 0.1 collective-permute-start
  5.2 0.9 %constant_dynamic-update-slice_fusion.4 = bf16[64,8192]{1,0:T(8,128)(2,1)S(1)} fusion(bf16[8,8192]{1,0:T(8,128)(2,1)} %bitcast.17), kind=kLoop, calls=%fused_computation.26 | loop fusion | bytes 262144
  6.2 0.0 copy-start
  6.2 0.0 copy-start.1
  6.2 0.0 copy-start.3
  6.2 4.7 %load_weights.1 = (bf16[8192,256]{1,0:T(8,128)(2,1)S(1)}, bf16[256,8192]{1,0:T(8,128)(2,1)S(1)}, bf16[256,8192]{1,0:T(8,128)(2,1)S(1)}) custom-call(bf16[1,8192,256]{2,1,0:T(8,128)(2,1)} %enc_hbm.1, bf16[1,2,256,8192]{3,2,1,0:T(8,128)(2,1)} %dec_hbm.1), custom_call_target="tpu_custom_call" | custom-call | bytes 25165824 | tf_op jit(solution)/shard_map/load_weights/pallas_call | solution.py:86
  11.0 0.0 copy-done
  11.0 0.1 gate.1
  11.1 0.0 collective-permute-done.2
  11.1 0.1 collective-permute-start.3
  11.2 0.0 collective-permute-done.1
  11.2 0.1 collective-permute-done
  11.4 0.4 collective-permute-start.4
  11.9 0.9 %collective-permute-done.3 = bf16[16,8192]{1,0:T(8,128)(2,1)S(1)} collective-permute-done((bf16[16,8192]{1,0:T(8,128)(2,1)S(1)}, bf16[16,8192]{1,0:T(8,128)(2,1)S(1)}, u32[]{:S(2)}, u32[]{:S(2)}) %collective-permute-start.3) | collective-permute-done | bytes 262176 | tf_op jit(solution)/shard_map/ppermute | solution.py:34
  12.8 0.4 collective-permute-done.4
  13.2 0.8 %fusion.2.codes_ref = bf16[64,256]{1,0:T(8,128)(2,1)S(1)} fusion(f32[64,256]{1,0:T(8,128)S(1)} %get-tuple-element.25, f32[64,256]{1,0:T(8,128)S(1)} %get-tuple-element.24, bf16[64,8192]{1,0:T(8,128)(2,1)S(1)} %slice_dynamic-update-slice_fusion, bf16[8192,256]{1,0:T(8,128)(2,1)S(1)} %get-tuple-element.21), kind=kOutput, calls=%fused_computation.3 | convolution fusion | flops 268500992 | bytes 5406720 | tf_op jit(solution)/shard_map/dot_general | solution.py:248
  14.0 0.8 %decode.3 = (f32[32,8192]{1,0:T(8,128)S(1)}, bf16[32,8192]{1,0:T(8,128)(2,1)S(1)}) custom-call(bf16[64,256]{1,0:T(8,128)(2,1)S(1)} %fusion.2.codes_ref, bf16[256,8192]{1,0:T(8,128)(2,1)S(1)} %get-tuple-element.30.dec_ref), custom_call_target="tpu_custom_call" | custom-call | flops 268435456 | bytes 4194304 | tf_op jit(solution)/shard_map/decode/pallas_call | solution.py:163
  14.8 0.3 collective-permute-start.8
  15.1 0.8 %decode.2 = (f32[32,8192]{1,0:T(8,128)S(1)}, bf16[32,8192]{1,0:T(8,128)(2,1)S(1)}) custom-call(bf16[64,256]{1,0:T(8,128)(2,1)S(1)} %fusion.2.codes_ref, bf16[256,8192]{1,0:T(8,128)(2,1)S(1)} %get-tuple-element.26.dec_ref), custom_call_target="tpu_custom_call" | custom-call | flops 268435456 | bytes 4194304 | tf_op jit(solution)/shard_map/decode/pallas_call | solution.py:163
  15.9 0.3 collective-permute-start.5
  16.3 0.5 collective-permute-done.8
  16.8 0.1 fusion.9
  16.9 2.0 %collective-permute-start.9 = (bf16[8,8192]{1,0:T(8,128)(2,1)S(1)}, bf16[8,8192]{1,0:T(8,128)(2,1)S(1)}, u32[]{:S(2)}, u32[]{:S(2)}) collective-permute-start(bf16[8,8192]{1,0:T(8,128)(2,1)S(1)} %get-tuple-element.46), channel_id=1, source_target_pairs={{0,8},{1,9},{2,10},{3,11},{4,12},{5,13},{6,14},{7,15},{8,16},{9,17... | collective-permute-start | bytes 393224 | tf_op jit(solution)/shard_map/ppermute | solution.py:39
  19.0 1.5 %collective-permute-start.12 = (bf16[8,8192]{1,0:T(8,128)(2,1)S(1)}, bf16[8,8192]{1,0:T(8,128)(2,1)S(1)}, u32[]{:S(2)}, u32[]{:S(2)}) collective-permute-start(bf16[8,8192]{1,0:T(8,128)(2,1)S(1)} %get-tuple-element.47), channel_id=1, source_target_pairs={{0,4},{1,3},{2,6},{3,1},{4,0},{5,7},{6,2},{7,5},{8,12},{9,11},{10,... | collective-permute-start | bytes 393224 | tf_op jit(solution)/shard_map/ppermute | solution.py:30
  20.5 1.5 %collective-permute-start.11 = (bf16[8,8192]{1,0:T(8,128)(2,1)S(1)}, bf16[8,8192]{1,0:T(8,128)(2,1)S(1)}, u32[]{:S(2)}, u32[]{:S(2)}) collective-permute-start(bf16[8,8192]{1,0:T(8,128)(2,1)S(1)} %get-tuple-element.48), channel_id=1, source_target_pairs={{0,2},{1,5},{2,0},{3,7},{4,6},{5,1},{6,4},{7,3},{8,10},{9,13},{10,... | collective-permute-start | bytes 393224 | tf_op jit(solution)/shard_map/ppermute | solution.py:30
  22.0 0.0 collective-permute-done.5
  22.0 0.1 fusion.8
  22.2 0.6 %collective-permute-start.6 = (bf16[8,8192]{1,0:T(8,128)(2,1)S(1)}, bf16[8,8192]{1,0:T(8,128)(2,1)S(1)}, u32[]{:S(2)}, u32[]{:S(2)}) collective-permute-start(bf16[8,8192]{1,0:T(8,128)(2,1)S(1)} %get-tuple-element.44), channel_id=1, source_target_pairs={{0,2},{1,5},{2,0},{3,7},{4,6},{5,1},{6,4},{7,3},{8,10},{9,13},{10,... | collective-permute-start | bytes 393224 | tf_op jit(solution)/shard_map/ppermute | solution.py:30
  22.7 0.5 collective-permute-start.7
  23.2 1.6 %collective-permute-done.9 = bf16[8,8192]{1,0:T(8,128)(2,1)S(1)} collective-permute-done((bf16[8,8192]{1,0:T(8,128)(2,1)S(1)}, bf16[8,8192]{1,0:T(8,128)(2,1)S(1)}, u32[]{:S(2)}, u32[]{:S(2)}) %collective-permute-start.9) | collective-permute-done | bytes 131104 | tf_op jit(solution)/shard_map/ppermute | solution.py:39
  24.9 2.5 %collective-permute-start.10 = (bf16[8,8192]{1,0:T(8,128)(2,1)S(1)}, bf16[8,8192]{1,0:T(8,128)(2,1)S(1)}, u32[]{:S(2)}, u32[]{:S(2)}) collective-permute-start(bf16[8,8192]{1,0:T(8,128)(2,1)S(1)} %slice_add_fusion.1), channel_id=1, source_target_pairs={{0,6},{1,7},{2,4},{3,5},{4,2},{5,3},{6,0},{7,1},{8,14},{9,15},{10,... | collective-permute-start | bytes 393224 | tf_op jit(solution)/shard_map/ppermute | solution.py:30
  27.4 0.0 collective-permute-done.12
  27.4 0.0 collective-permute-done.11
  27.5 2.6 %collective-permute-start.13 = (bf16[8,8192]{1,0:T(8,128)(2,1)S(1)}, bf16[8,8192]{1,0:T(8,128)(2,1)S(1)}, u32[]{:S(2)}, u32[]{:S(2)}) collective-permute-start(bf16[8,8192]{1,0:T(8,128)(2,1)S(1)} %convert_element_type.71), channel_id=1, source_target_pairs={{0,8},{1,9},{2,10},{3,11},{4,12},{5,13},{6,14},{7,15},{8,16},{9,17... | collective-permute-start | bytes 393224 | tf_op jit(solution)/shard_map/ppermute | solution.py:45
  30.1 0.0 collective-permute-done.6
  30.1 0.0 collective-permute-done.7
  30.1 0.9 %collective-permute-done.10 = bf16[8,8192]{1,0:T(8,128)(2,1)S(1)} collective-permute-done((bf16[8,8192]{1,0:T(8,128)(2,1)S(1)}, bf16[8,8192]{1,0:T(8,128)(2,1)S(1)}, u32[]{:S(2)}, u32[]{:S(2)}) %collective-permute-start.10) | collective-permute-done | bytes 131104 | tf_op jit(solution)/shard_map/ppermute | solution.py:30
  31.0 0.1 fusion.7
  31.1 1.3 %collective-permute-start.14 = (bf16[8,8192]{1,0:T(8,128)(2,1)S(1)}, bf16[8,8192]{1,0:T(8,128)(2,1)S(1)}, u32[]{:S(2)}, u32[]{:S(2)}) collective-permute-start(bf16[8,8192]{1,0:T(8,128)(2,1)S(1)} %fusion.7), channel_id=1, source_target_pairs={{8,0},{9,1},{10,2},{11,3},{12,4},{13,5},{14,6},{15,7},{16,8},{17,9... | collective-permute-start | bytes 393224 | tf_op jit(solution)/shard_map/ppermute | solution.py:50
  32.4 0.2 collective-permute-done.13
  32.6 0.1 constant_dynamic-update-slice_fusion.9
  32.7 0.0 copy-start.4
  32.7 2.1 %collective-permute-start.20 = (bf16[8,8192]{1,0:T(8,128)(2,1)S(1)}, bf16[8,8192]{1,0:T(8,128)(2,1)S(1)}, u32[]{:S(2)}, u32[]{:S(2)}) collective-permute-start(bf16[8,8192]{1,0:T(8,128)(2,1)S(1)} %get-tuple-element.39), channel_id=1, source_target_pairs={{0,6},{1,7},{2,4},{3,5},{4,2},{5,3},{6,0},{7,1},{8,14},{9,15},{10,... | collective-permute-start | bytes 393224 | tf_op jit(solution)/shard_map/ppermute | solution.py:30
  34.9 0.7 %collective-permute-start.19 = (bf16[8,8192]{1,0:T(8,128)(2,1)S(1)}, bf16[8,8192]{1,0:T(8,128)(2,1)S(1)}, u32[]{:S(2)}, u32[]{:S(2)}) collective-permute-start(bf16[8,8192]{1,0:T(8,128)(2,1)S(1)} %get-tuple-element.39), channel_id=1, source_target_pairs={{0,4},{1,3},{2,6},{3,1},{4,0},{5,7},{6,2},{7,5},{8,12},{9,11},{10,... | collective-permute-start | bytes 393224 | tf_op jit(solution)/shard_map/ppermute | solution.py:30
  35.6 0.7 %collective-permute-start.18 = (bf16[8,8192]{1,0:T(8,128)(2,1)S(1)}, bf16[8,8192]{1,0:T(8,128)(2,1)S(1)}, u32[]{:S(2)}, u32[]{:S(2)}) collective-permute-start(bf16[8,8192]{1,0:T(8,128)(2,1)S(1)} %get-tuple-element.39), channel_id=1, source_target_pairs={{0,2},{1,5},{2,0},{3,7},{4,6},{5,1},{6,4},{7,3},{8,10},{9,13},{10,... | collective-permute-start | bytes 393224 | tf_op jit(solution)/shard_map/ppermute | solution.py:30
  36.3 1.7 %collective-permute-done.14 = bf16[8,8192]{1,0:T(8,128)(2,1)S(1)} collective-permute-done((bf16[8,8192]{1,0:T(8,128)(2,1)S(1)}, bf16[8,8192]{1,0:T(8,128)(2,1)S(1)}, u32[]{:S(2)}, u32[]{:S(2)}) %collective-permute-start.14) | collective-permute-done | bytes 131104 | tf_op jit(solution)/shard_map/ppermute | solution.py:50
  38.1 2.3 %collective-permute-start.17 = (bf16[8,8192]{1,0:T(8,128)(2,1)S(1)}, bf16[8,8192]{1,0:T(8,128)(2,1)S(1)}, u32[]{:S(2)}, u32[]{:S(2)}) collective-permute-start(bf16[8,8192]{1,0:T(8,128)(2,1)S(1)} %select_convert_fusion), channel_id=1, source_target_pairs={{0,6},{1,7},{2,4},{3,5},{4,2},{5,3},{6,0},{7,1},{8,14},{9,15},{10,... | collective-permute-start | bytes 393224 | tf_op jit(solution)/shard_map/ppermute | solution.py:30
  40.4 0.7 %collective-permute-start.16 = (bf16[8,8192]{1,0:T(8,128)(2,1)S(1)}, bf16[8,8192]{1,0:T(8,128)(2,1)S(1)}, u32[]{:S(2)}, u32[]{:S(2)}) collective-permute-start(bf16[8,8192]{1,0:T(8,128)(2,1)S(1)} %select_convert_fusion), channel_id=1, source_target_pairs={{0,4},{1,3},{2,6},{3,1},{4,0},{5,7},{6,2},{7,5},{8,12},{9,11},{10,... | collective-permute-start | bytes 393224 | tf_op jit(solution)/shard_map/ppermute | solution.py:30
  41.0 0.0 collective-permute-done.20
  41.0 0.6 %collective-permute-start.15 = (bf16[8,8192]{1,0:T(8,128)(2,1)S(1)}, bf16[8,8192]{1,0:T(8,128)(2,1)S(1)}, u32[]{:S(2)}, u32[]{:S(2)}) collective-permute-start(bf16[8,8192]{1,0:T(8,128)(2,1)S(1)} %select_convert_fusion), channel_id=1, source_target_pairs={{0,2},{1,5},{2,0},{3,7},{4,6},{5,1},{6,4},{7,3},{8,10},{9,13},{10,... | collective-permute-start | bytes 393224 | tf_op jit(solution)/shard_map/ppermute | solution.py:30
  41.6 0.5 %collective-permute-done.19 = bf16[8,8192]{1,0:T(8,128)(2,1)S(1)} collective-permute-done((bf16[8,8192]{1,0:T(8,128)(2,1)S(1)}, bf16[8,8192]{1,0:T(8,128)(2,1)S(1)}, u32[]{:S(2)}, u32[]{:S(2)}) %collective-permute-start.19) | collective-permute-done | bytes 131104 | tf_op jit(solution)/shard_map/ppermute | solution.py:30
  42.2 0.0 collective-permute-done.18
  42.2 0.1 collective-permute-start.21
  42.4 3.1 %collective-permute-done.17 = bf16[8,8192]{1,0:T(8,128)(2,1)S(1)} collective-permute-done((bf16[8,8192]{1,0:T(8,128)(2,1)S(1)}, bf16[8,8192]{1,0:T(8,128)(2,1)S(1)}, u32[]{:S(2)}, u32[]{:S(2)}) %collective-permute-start.17) | collective-permute-done | bytes 131104 | tf_op jit(solution)/shard_map/ppermute | solution.py:30
  45.5 0.9 %collective-permute-done.16 = bf16[8,8192]{1,0:T(8,128)(2,1)S(1)} collective-permute-done((bf16[8,8192]{1,0:T(8,128)(2,1)S(1)}, bf16[8,8192]{1,0:T(8,128)(2,1)S(1)}, u32[]{:S(2)}, u32[]{:S(2)}) %collective-permute-start.16) | collective-permute-done | bytes 131104 | tf_op jit(solution)/shard_map/ppermute | solution.py:30
  46.4 0.0 collective-permute-done.15
  46.5 0.0 collective-permute-done.21
  46.5 0.1 collective-permute-start.22
  46.6 1.4 %grad_own.1 = (f32[64,256]{1,0:T(8,128)S(1)}, f32[8,128]{1,0:T(8,128)}) custom-call(bf16[64,8192]{1,0:T(8,128)(2,1)S(1)} %constant_dynamic-update-slice_fusion.5.rows_ref, bf16[256,8192]{1,0:T(8,128)(2,1)S(1)} %get-tuple-element.26.dec_ref), custom_call_target="tpu_custom_call" | custom-call | flops 268435456 | bytes 4194304 | tf_op jit(solution)/shard_map/grad_own/pallas_call | solution.py:198
  48.0 0.4 collective-permute-done.22
  48.5 0.1 pad_maximum_fusion.rows_ref
  48.5 2.0 %grad_all.1 = f32[1,64,256]{2,1,0:T(8,128)} custom-call(bf16[64,8192]{1,0:T(8,128)(2,1)S(1)} %pad_maximum_fusion.rows_ref, bf16[256,8192]{1,0:T(8,128)(2,1)S(1)} %get-tuple-element.30.dec_ref, f32[64,256]{1,0:T(8,128)S(1)} %get-tuple-element.37.own_ref), custom_call_target="tpu_custom_call" | custom-call | flops 268435456 | bytes 4194304 | tf_op jit(solution)/shard_map/grad_all/pallas_call | solution.py:210
  (26 shorter events, 0.4 us)
Async XLA Ops:
  0.6 10.5 %collective-permute-start.2 = (bf16[8,8192]{1,0:T(8,128)(2,1)}, bf16[8,8192]{1,0:T(8,128)(2,1)S(1)}, u32[]{:S(2)}, u32[]{:S(2)}) collective-permute-start(bf16[8,8192]{1,0:T(8,128)(2,1)} %bitcast.14), channel_id=1, source_target_pairs={{0,6},{1,7},{2,4},{3,5},{4,2},{5,3},{6,0},{7,1},{8,14},{9,15},{10,... | collective-permute-start | bytes 393224 | tf_op jit(solution)/shard_map/ppermute | solution.py:30
  4.6 6.6 %collective-permute-start.1 = (bf16[8,8192]{1,0:T(8,128)(2,1)}, bf16[8,8192]{1,0:T(8,128)(2,1)S(1)}, u32[]{:S(2)}, u32[]{:S(2)}) collective-permute-start(bf16[8,8192]{1,0:T(8,128)(2,1)} %bitcast.15), channel_id=1, source_target_pairs={{0,4},{1,3},{2,6},{3,1},{4,0},{5,7},{6,2},{7,5},{8,12},{9,11},{10,... | collective-permute-start | bytes 393224 | tf_op jit(solution)/shard_map/ppermute | solution.py:30
  5.1 6.3 %collective-permute-start = (bf16[8,8192]{1,0:T(8,128)(2,1)}, bf16[8,8192]{1,0:T(8,128)(2,1)S(1)}, u32[]{:S(2)}, u32[]{:S(2)}) collective-permute-start(bf16[8,8192]{1,0:T(8,128)(2,1)} %bitcast.16), channel_id=1, source_target_pairs={{0,2},{1,5},{2,0},{3,7},{4,6},{5,1},{6,4},{7,3},{8,10},{9,13},{10,... | collective-permute-start | bytes 393224 | tf_op jit(solution)/shard_map/ppermute | solution.py:30
  6.2 4.8 %copy-start = (s32[1,2,2]{2,1,0:T(2,128)S(1)}, s32[1,2,2]{2,1,0:T(2,128)}, u32[]{:S(2)}) copy-start(s32[1,2,2]{2,1,0:T(2,128)} %param.9) | copy-start | bytes 52
  6.2 4.8 %copy-start.1 = (bf16[1,256]{1,0:T(2,128)(2,1)S(1)}, bf16[1,256]{1,0:T(2,128)(2,1)}, u32[]{:S(2)}) copy-start(bf16[1,256]{1,0:T(2,128)(2,1)} %bias_ref) | copy-start | bytes 1540
  6.2 4.9 %copy-start.3 = (bf16[1,8,8192]{2,1,0:T(8,128)(2,1)S(1)}, bf16[1,8,8192]{2,1,0:T(8,128)(2,1)}, u32[]{:S(2)}) copy-start(bf16[1,8,8192]{2,1,0:T(8,128)(2,1)} %param.6) | copy-start | bytes 393220
  11.1 1.6 %collective-permute-start.3 = (bf16[16,8192]{1,0:T(8,128)(2,1)S(1)}, bf16[16,8192]{1,0:T(8,128)(2,1)S(1)}, u32[]{:S(2)}, u32[]{:S(2)}) collective-permute-start(bf16[16,8192]{1,0:T(8,128)(2,1)S(1)} %pad_maximum_fusion.3), channel_id=1, source_target_pairs={{0,1},{1,0},{2,3},{3,2},{4,5},{5,4},{6,7},{7,6},{8,9},{9,8},{10,11... | collective-permute-start | bytes 786440 | tf_op jit(solution)/shard_map/ppermute | solution.py:34
  11.4 1.7 %collective-permute-start.4 = (bf16[16,8192]{1,0:T(8,128)(2,1)S(1)}, bf16[16,8192]{1,0:T(8,128)(2,1)S(1)}, u32[]{:S(2)}, u32[]{:S(2)}) collective-permute-start(bf16[16,8192]{1,0:T(8,128)(2,1)S(1)} %pad_maximum_fusion.4), channel_id=1, source_target_pairs={{0,1},{1,0},{2,3},{3,2},{4,5},{5,4},{6,7},{7,6},{8,9},{9,8},{10,11... | collective-permute-start | bytes 786440 | tf_op jit(solution)/shard_map/ppermute | solution.py:34
  14.8 2.0 %collective-permute-start.8 = (bf16[32,8192]{1,0:T(8,128)(2,1)S(1)}, bf16[32,8192]{1,0:T(8,128)(2,1)S(1)}, u32[]{:S(2)}, u32[]{:S(2)}) collective-permute-start(bf16[32,8192]{1,0:T(8,128)(2,1)S(1)} %get-tuple-element.32), channel_id=1, source_target_pairs={{0,1},{1,0},{2,3},{3,2},{4,5},{5,4},{6,7},{7,6},{8,9},{9,8},{10,11... | collective-permute-start | bytes 1572872 | tf_op jit(solution)/shard_map/ppermute | solution.py:34
  15.9 6.1 %collective-permute-start.5 = (bf16[32,8192]{1,0:T(8,128)(2,1)S(1)}, bf16[32,8192]{1,0:T(8,128)(2,1)S(1)}, u32[]{:S(2)}, u32[]{:S(2)}) collective-permute-start(bf16[32,8192]{1,0:T(8,128)(2,1)S(1)} %get-tuple-element.28), channel_id=1, source_target_pairs={{0,1},{1,0},{2,3},{3,2},{4,5},{5,4},{6,7},{7,6},{8,9},{9,8},{10,11... | collective-permute-start | bytes 1572872 | tf_op jit(solution)/shard_map/ppermute | solution.py:34
  16.8 14.2 %copy-start.2 = (bf16[1,8,8192]{2,1,0:T(8,128)(2,1)S(1)}, bf16[1,8,8192]{2,1,0:T(8,128)(2,1)}, u32[]{:S(2)}) copy-start(bf16[1,8,8192]{2,1,0:T(8,128)(2,1)} %param.11) | copy-start | bytes 393220
  16.9 8.0 %collective-permute-start.9 = (bf16[8,8192]{1,0:T(8,128)(2,1)S(1)}, bf16[8,8192]{1,0:T(8,128)(2,1)S(1)}, u32[]{:S(2)}, u32[]{:S(2)}) collective-permute-start(bf16[8,8192]{1,0:T(8,128)(2,1)S(1)} %get-tuple-element.46), channel_id=1, source_target_pairs={{0,8},{1,9},{2,10},{3,11},{4,12},{5,13},{6,14},{7,15},{8,16},{9,17... | collective-permute-start | bytes 393224 | tf_op jit(solution)/shard_map/ppermute | solution.py:39
  19.0 8.5 %collective-permute-start.12 = (bf16[8,8192]{1,0:T(8,128)(2,1)S(1)}, bf16[8,8192]{1,0:T(8,128)(2,1)S(1)}, u32[]{:S(2)}, u32[]{:S(2)}) collective-permute-start(bf16[8,8192]{1,0:T(8,128)(2,1)S(1)} %get-tuple-element.47), channel_id=1, source_target_pairs={{0,4},{1,3},{2,6},{3,1},{4,0},{5,7},{6,2},{7,5},{8,12},{9,11},{10,... | collective-permute-start | bytes 393224 | tf_op jit(solution)/shard_map/ppermute | solution.py:30
  20.5 7.0 %collective-permute-start.11 = (bf16[8,8192]{1,0:T(8,128)(2,1)S(1)}, bf16[8,8192]{1,0:T(8,128)(2,1)S(1)}, u32[]{:S(2)}, u32[]{:S(2)}) collective-permute-start(bf16[8,8192]{1,0:T(8,128)(2,1)S(1)} %get-tuple-element.48), channel_id=1, source_target_pairs={{0,2},{1,5},{2,0},{3,7},{4,6},{5,1},{6,4},{7,3},{8,10},{9,13},{10,... | collective-permute-start | bytes 393224 | tf_op jit(solution)/shard_map/ppermute | solution.py:30
  22.2 8.0 %collective-permute-start.6 = (bf16[8,8192]{1,0:T(8,128)(2,1)S(1)}, bf16[8,8192]{1,0:T(8,128)(2,1)S(1)}, u32[]{:S(2)}, u32[]{:S(2)}) collective-permute-start(bf16[8,8192]{1,0:T(8,128)(2,1)S(1)} %get-tuple-element.44), channel_id=1, source_target_pairs={{0,2},{1,5},{2,0},{3,7},{4,6},{5,1},{6,4},{7,3},{8,10},{9,13},{10,... | collective-permute-start | bytes 393224 | tf_op jit(solution)/shard_map/ppermute | solution.py:30
  22.7 7.4 %collective-permute-start.7 = (bf16[8,8192]{1,0:T(8,128)(2,1)S(1)}, bf16[8,8192]{1,0:T(8,128)(2,1)S(1)}, u32[]{:S(2)}, u32[]{:S(2)}) collective-permute-start(bf16[8,8192]{1,0:T(8,128)(2,1)S(1)} %get-tuple-element.45), channel_id=1, source_target_pairs={{0,4},{1,3},{2,6},{3,1},{4,0},{5,7},{6,2},{7,5},{8,12},{9,11},{10,... | collective-permute-start | bytes 393224 | tf_op jit(solution)/shard_map/ppermute | solution.py:30
  24.9 6.1 %collective-permute-start.10 = (bf16[8,8192]{1,0:T(8,128)(2,1)S(1)}, bf16[8,8192]{1,0:T(8,128)(2,1)S(1)}, u32[]{:S(2)}, u32[]{:S(2)}) collective-permute-start(bf16[8,8192]{1,0:T(8,128)(2,1)S(1)} %slice_add_fusion.1), channel_id=1, source_target_pairs={{0,6},{1,7},{2,4},{3,5},{4,2},{5,3},{6,0},{7,1},{8,14},{9,15},{10,... | collective-permute-start | bytes 393224 | tf_op jit(solution)/shard_map/ppermute | solution.py:30
  27.5 5.1 %collective-permute-start.13 = (bf16[8,8192]{1,0:T(8,128)(2,1)S(1)}, bf16[8,8192]{1,0:T(8,128)(2,1)S(1)}, u32[]{:S(2)}, u32[]{:S(2)}) collective-permute-start(bf16[8,8192]{1,0:T(8,128)(2,1)S(1)} %convert_element_type.71), channel_id=1, source_target_pairs={{0,8},{1,9},{2,10},{3,11},{4,12},{5,13},{6,14},{7,15},{8,16},{9,17... | collective-permute-start | bytes 393224 | tf_op jit(solution)/shard_map/ppermute | solution.py:45
  31.1 6.9 %collective-permute-start.14 = (bf16[8,8192]{1,0:T(8,128)(2,1)S(1)}, bf16[8,8192]{1,0:T(8,128)(2,1)S(1)}, u32[]{:S(2)}, u32[]{:S(2)}) collective-permute-start(bf16[8,8192]{1,0:T(8,128)(2,1)S(1)} %fusion.7), channel_id=1, source_target_pairs={{8,0},{9,1},{10,2},{11,3},{12,4},{13,5},{14,6},{15,7},{16,8},{17,9... | collective-permute-start | bytes 393224 | tf_op jit(solution)/shard_map/ppermute | solution.py:50
  32.7 15.3 %copy-start.4 = (bf16[8,8192]{1,0:T(8,128)(2,1)}, bf16[8,8192]{1,0:T(8,128)(2,1)S(1)}, u32[]{:S(2)}) copy-start(bf16[8,8192]{1,0:T(8,128)(2,1)S(1)} %get-tuple-element.39) | copy-start | bytes 393220
  32.7 8.3 %collective-permute-start.20 = (bf16[8,8192]{1,0:T(8,128)(2,1)S(1)}, bf16[8,8192]{1,0:T(8,128)(2,1)S(1)}, u32[]{:S(2)}, u32[]{:S(2)}) collective-permute-start(bf16[8,8192]{1,0:T(8,128)(2,1)S(1)} %get-tuple-element.39), channel_id=1, source_target_pairs={{0,6},{1,7},{2,4},{3,5},{4,2},{5,3},{6,0},{7,1},{8,14},{9,15},{10,... | collective-permute-start | bytes 393224 | tf_op jit(solution)/shard_map/ppermute | solution.py:30
  34.9 7.3 %collective-permute-start.19 = (bf16[8,8192]{1,0:T(8,128)(2,1)S(1)}, bf16[8,8192]{1,0:T(8,128)(2,1)S(1)}, u32[]{:S(2)}, u32[]{:S(2)}) collective-permute-start(bf16[8,8192]{1,0:T(8,128)(2,1)S(1)} %get-tuple-element.39), channel_id=1, source_target_pairs={{0,4},{1,3},{2,6},{3,1},{4,0},{5,7},{6,2},{7,5},{8,12},{9,11},{10,... | collective-permute-start | bytes 393224 | tf_op jit(solution)/shard_map/ppermute | solution.py:30
  35.6 6.6 %collective-permute-start.18 = (bf16[8,8192]{1,0:T(8,128)(2,1)S(1)}, bf16[8,8192]{1,0:T(8,128)(2,1)S(1)}, u32[]{:S(2)}, u32[]{:S(2)}) collective-permute-start(bf16[8,8192]{1,0:T(8,128)(2,1)S(1)} %get-tuple-element.39), channel_id=1, source_target_pairs={{0,2},{1,5},{2,0},{3,7},{4,6},{5,1},{6,4},{7,3},{8,10},{9,13},{10,... | collective-permute-start | bytes 393224 | tf_op jit(solution)/shard_map/ppermute | solution.py:30
  38.1 7.4 %collective-permute-start.17 = (bf16[8,8192]{1,0:T(8,128)(2,1)S(1)}, bf16[8,8192]{1,0:T(8,128)(2,1)S(1)}, u32[]{:S(2)}, u32[]{:S(2)}) collective-permute-start(bf16[8,8192]{1,0:T(8,128)(2,1)S(1)} %select_convert_fusion), channel_id=1, source_target_pairs={{0,6},{1,7},{2,4},{3,5},{4,2},{5,3},{6,0},{7,1},{8,14},{9,15},{10,... | collective-permute-start | bytes 393224 | tf_op jit(solution)/shard_map/ppermute | solution.py:30
  40.4 6.1 %collective-permute-start.16 = (bf16[8,8192]{1,0:T(8,128)(2,1)S(1)}, bf16[8,8192]{1,0:T(8,128)(2,1)S(1)}, u32[]{:S(2)}, u32[]{:S(2)}) collective-permute-start(bf16[8,8192]{1,0:T(8,128)(2,1)S(1)} %select_convert_fusion), channel_id=1, source_target_pairs={{0,4},{1,3},{2,6},{3,1},{4,0},{5,7},{6,2},{7,5},{8,12},{9,11},{10,... | collective-permute-start | bytes 393224 | tf_op jit(solution)/shard_map/ppermute | solution.py:30
  41.0 5.4 %collective-permute-start.15 = (bf16[8,8192]{1,0:T(8,128)(2,1)S(1)}, bf16[8,8192]{1,0:T(8,128)(2,1)S(1)}, u32[]{:S(2)}, u32[]{:S(2)}) collective-permute-start(bf16[8,8192]{1,0:T(8,128)(2,1)S(1)} %select_convert_fusion), channel_id=1, source_target_pairs={{0,2},{1,5},{2,0},{3,7},{4,6},{5,1},{6,4},{7,3},{8,10},{9,13},{10,... | collective-permute-start | bytes 393224 | tf_op jit(solution)/shard_map/ppermute | solution.py:30
  42.2 4.2 %collective-permute-start.21 = (bf16[32,8192]{1,0:T(8,128)(2,1)S(1)}, bf16[32,8192]{1,0:T(8,128)(2,1)S(1)}, u32[]{:S(2)}, u32[]{:S(2)}) collective-permute-start(bf16[32,8192]{1,0:T(8,128)(2,1)S(1)} %pad_maximum_fusion.2), channel_id=1, source_target_pairs={{0,1},{1,0},{2,3},{3,2},{4,5},{5,4},{6,7},{7,6},{8,9},{9,8},{10,11... | collective-permute-start | bytes 1572872 | tf_op jit(solution)/shard_map/ppermute | solution.py:34
  46.5 2.0 %collective-permute-start.22 = (bf16[32,8192]{1,0:T(8,128)(2,1)S(1)}, bf16[32,8192]{1,0:T(8,128)(2,1)S(1)}, u32[]{:S(2)}, u32[]{:S(2)}) collective-permute-start(bf16[32,8192]{1,0:T(8,128)(2,1)S(1)} %pad_maximum_fusion.1), channel_id=1, source_target_pairs={{0,1},{1,0},{2,3},{3,2},{4,5},{5,4},{6,7},{7,6},{8,9},{9,8},{10,11... | collective-permute-start | bytes 1572872 | tf_op jit(solution)/shard_map/ppermute | solution.py:34

commit v18 on v17

--- a/solution.py
+++ b/solution.py
@@ -238,12 +238,11 @@
     slab, first, final = lax.optimization_barrier((resid[0], index < group, index >= (LAYERS - 1) * group))
     tokens = resid.shape[1]
     enc, own_dec, next_dec = loaded(enc_weight, dec_weight)
-    most, last = [across(slab, chip, chips) for chip in range(1, chips - 1)], across(slab, chips - 1, chips)
-    early, late = jnp.concatenate([slab, last], axis=0), jnp.concatenate(most, axis=0)
-    early_far, late_far = other_core(early), other_core(late)
-    x = jnp.concatenate(
-        [slab, late, last, early_far[:tokens], late_far, early_far[tokens:]], axis=0
-    )
+    pieces = jnp.concatenate([across(slab, chip, chips) for chip in range(chips - 1, 0, -1)], axis=0)
+    pieces_far = other_core(pieces)
+    rows = [after(slab, pieces)] + [pieces[i * tokens : (i + 1) * tokens] for i in range(chips - 1)][::-1]
+    rows += [other_core(slab)] + [pieces_far[i * tokens : (i + 1) * tokens] for i in range(chips - 1)][::-1]
+    x = jnp.concatenate(rows, axis=0)
     gate, bias = gated(*after((active[0], enc_bias), enc), group * tokens, tokens)
     pre = jnp.dot(x, enc, preferred_element_type=jnp.float32) + bias
     codes = (jax.nn.relu(pre) * gate).astype(jnp.bfloat16)
@@ -264,12 +263,13 @@
     later = jnp.where(final, 0.0, next_sum + after(above, error)).astype(jnp.bfloat16)
 
     heres = [error] + [across(error, chip, chips) for chip in range(1, chips)]
-    afters = [later] + [across(later, chip, chips) for chip in range(1, chips)]
+    afters = [later] + [across(later, chip, chips) for chip in range(1, chips - 1)]
+    last = lowered(after(heres[-1], later), group)
     here_near = jnp.concatenate(heres, axis=0)
     here_far = other_core(here_near)
     here_rows = jnp.concatenate([here_near, here_far], axis=0)
-    after_near = after(jnp.concatenate(afters, axis=0), here_far)
-    after_rows = jnp.concatenate([after_near, other_core(after_near)], axis=0)
+    most = after(jnp.concatenate(afters, axis=0), here_far)
+    after_rows = jnp.concatenate([most, last, other_core(most), other_core(last)], axis=0)
     grad = grad_all(after_rows, next_dec, grad_own(here_rows, own_dec), tokens)
     return (error[None], grad)
 

time: 51.1 us -> 51.8 us (1.014)
  waiting for transfers between devices: 11.4 us -> 13.1 us
  local copies, waits for them, and re-layouts: 1.16 us -> 0.25 us
    ppermute x1 -> x2, waiting for transfers between devices: 1.74 us -> 7.13 us  [lowered(): lax.ppermute(value, AXIS, [(i + group, i) for i in range(size - group)])]
    ppermute x14 -> x13, waiting for transfers between devices: 5.64 us -> 2.1 us  [across(): return lax.ppermute(value, AXIS, pairs)]
    ppermute x1 -> x2, starting transfers between devices: 1.29 us -> 2.57 us  [lowered(): lax.ppermute(value, AXIS, [(i + group, i) for i in range(size - group)])]
    unnamed x19 -> x22, local copies, waits for them, and re-layouts: 1.07 us -> 0.15 us
    ppermute x14 -> x13, starting transfers between devices: 18.3 us -> 17.6 us  [across(): return lax.ppermute(value, AXIS, pairs)]
    ppermute x6 -> x7, waiting for transfers between devices: 2.19 us -> 2.1 us  [other_core(): lax.ppermute(value, AXIS, [(i, i ^ 1) for i in range(lax.axis_size(AXIS))])]
    ppermute x6 -> x7, starting transfers between devices: 1.28 us -> 1.35 us  [other_core(): lax.ppermute(value, AXIS, [(i, i ^ 1) for i in range(lax.axis_size(AXIS))])]
  transfers between devices with their start and end apart: 23 -> 24, of which waited for: 12 -> 9; matrix products, arithmetic and copies ran while one was open for 3% -> 2% of each run, Pallas kernels for 14% -> 14%
where the time goes in v18:
time: 51.8 us; the launch traced here: 51.6 us
  starting transfers between devices  25.8 us (50%)
  waiting for transfers between devices  13.1 us (25%)
  Pallas kernels  9.89 us (19%)
  between operations  1.06 us (2%)
  matrix products  0.8 us (2%)
  other arithmetic  0.68 us (1%)
    ppermute x13, starting transfers between devices, across(): return lax.ppermute(value, AXIS, pairs)  17.6 us
    ppermute x2, waiting for transfers between devices, lowered(): lax.ppermute(value, AXIS, [(i + group, i) for i in range(size - group)])  7.13 us
    pallas_call x1, Pallas kernels, loaded(): pl.pallas_call(load_kernel, out_shape=[pltpu.VMEM(enc.shape[1:], enc.dtyp...  4.68 us
    ppermute x1, starting transfers between devices, shifted(): lax.ppermute(value, AXIS, [(i, i + group) for i in range(size - group)])  2.7 us
    ppermute x2, starting transfers between devices, lowered(): lax.ppermute(value, AXIS, [(i + group, i) for i in range(size - group)])  2.57 us
    ppermute x7, waiting for transfers between devices, other_core(): lax.ppermute(value, AXIS, [(i, i ^ 1) for i in range(lax.axis_size(AXIS))])  2.1 us
    ppermute x13, waiting for transfers between devices, across(): return lax.ppermute(value, AXIS, pairs)  2.1 us
    pallas_call x1, Pallas kernels, grad_all(): pl.pallas_call(functools.partial(grad_all_kernel, tokens), out_shape=jax....  2.03 us
  transfers between devices with their start and end apart: 24, of which 9 were waited for; matrix products, arithmetic and copies ran while one was open for 2% of the time, Pallas kernels for 14%

profile of v18, /device:TPU:0, one launch (start us, length us, event | category | flops | bytes accessed | tf_op | source)
XLA Modules:
  0.0 51.6 jit_solution(16363990548286224075)
XLA Ops:
  0.6 0.0 copy-start
  0.6 0.0 copy-start.1
  0.7 0.0 copy-start.4
  0.7 4.0 %collective-permute-start = (bf16[8,8192]{1,0:T(8,128)(2,1)}, bf16[8,8192]{1,0:T(8,128)(2,1)S(1)}, u32[]{:S(2)}, u32[]{:S(2)}) collective-permute-start(bf16[8,8192]{1,0:T(8,128)(2,1)} %bitcast.15), channel_id=1, source_target_pairs={{0,6},{1,7},{2,4},{3,5},{4,2},{5,3},{6,0},{7,1},{8,14},{9,15},{10,... | collective-permute-start | bytes 393224 | tf_op jit(solution)/shard_map/ppermute | solution.py:30
  4.6 0.0 collective-permute-start.3
  4.6 0.5 %collective-permute-start.2 = (bf16[8,8192]{1,0:T(8,128)(2,1)}, bf16[8,8192]{1,0:T(8,128)(2,1)S(1)}, u32[]{:S(2)}, u32[]{:S(2)}) collective-permute-start(bf16[8,8192]{1,0:T(8,128)(2,1)} %bitcast.17), channel_id=1, source_target_pairs={{0,2},{1,5},{2,0},{3,7},{4,6},{5,1},{6,4},{7,3},{8,10},{9,13},{10,... | collective-permute-start | bytes 393224 | tf_op jit(solution)/shard_map/ppermute | solution.py:30
  5.2 0.2 collective-permute-start.1
  5.3 4.7 %load_weights.1 = (bf16[8192,256]{1,0:T(8,128)(2,1)S(1)}, bf16[256,8192]{1,0:T(8,128)(2,1)S(1)}, bf16[256,8192]{1,0:T(8,128)(2,1)S(1)}) custom-call(bf16[1,8192,256]{2,1,0:T(8,128)(2,1)} %enc_hbm.1, bf16[1,2,256,8192]{3,2,1,0:T(8,128)(2,1)} %dec_hbm.1), custom_call_target="tpu_custom_call" | custom-call | bytes 25165824 | tf_op jit(solution)/shard_map/load_weights/pallas_call | solution.py:86
  10.1 0.1 gate.1
  10.2 0.0 collective-permute-done
  10.2 0.9 %collective-permute-done.1 = bf16[8,8192]{1,0:T(8,128)(2,1)S(1)} collective-permute-done((bf16[8,8192]{1,0:T(8,128)(2,1)}, bf16[8,8192]{1,0:T(8,128)(2,1)S(1)}, u32[]{:S(2)}, u32[]{:S(2)}) %collective-permute-start.1) | collective-permute-done | bytes 131104 | tf_op jit(solution)/shard_map/ppermute | solution.py:30
  11.2 0.2 collective-permute-done.2
  11.4 0.1 collective-permute-start.4
  11.6 0.0 collective-permute-done.3
  11.6 1.6 %collective-permute-done.4 = bf16[24,8192]{1,0:T(8,128)(2,1)S(1)} collective-permute-done((bf16[24,8192]{1,0:T(8,128)(2,1)S(1)}, bf16[24,8192]{1,0:T(8,128)(2,1)S(1)}, u32[]{:S(2)}, u32[]{:S(2)}) %collective-permute-start.4) | collective-permute-done | bytes 393248 | tf_op jit(solution)/shard_map/ppermute | solution.py:34
  13.2 0.8 %fusion.2.codes_ref = bf16[64,256]{1,0:T(8,128)(2,1)S(1)} fusion(f32[64,256]{1,0:T(8,128)S(1)} %get-tuple-element.28, f32[64,256]{1,0:T(8,128)S(1)} %get-tuple-element.27, bf16[64,8192]{1,0:T(8,128)(2,1)S(1)} %slice_dynamic-update-slice_fusion, bf16[8192,256]{1,0:T(8,128)(2,1)S(1)} %get-tuple-element.24), kind=kOutput, calls=%fused_computation.3 | convolution fusion | flops 268500992 | bytes 5406720 | tf_op jit(solution)/shard_map/dot_general | solution.py:247
  14.1 0.8 %decode.3 = (f32[32,8192]{1,0:T(8,128)S(1)}, bf16[32,8192]{1,0:T(8,128)(2,1)S(1)}) custom-call(bf16[64,256]{1,0:T(8,128)(2,1)S(1)} %fusion.2.codes_ref, bf16[256,8192]{1,0:T(8,128)(2,1)S(1)} %get-tuple-element.33.dec_ref), custom_call_target="tpu_custom_call" | custom-call | flops 268435456 | bytes 4194304 | tf_op jit(solution)/shard_map/decode/pallas_call | solution.py:163
  14.9 0.2 collective-permute-start.8
  15.1 0.8 %decode.2 = (f32[32,8192]{1,0:T(8,128)S(1)}, bf16[32,8192]{1,0:T(8,128)(2,1)S(1)}) custom-call(bf16[64,256]{1,0:T(8,128)(2,1)S(1)} %fusion.2.codes_ref, bf16[256,8192]{1,0:T(8,128)(2,1)S(1)} %get-tuple-element.29.dec_ref), custom_call_target="tpu_custom_call" | custom-call | flops 268435456 | bytes 4194304 | tf_op jit(solution)/shard_map/decode/pallas_call | solution.py:163
  16.0 0.4 collective-permute-start.5
  16.4 0.5 collective-permute-done.8
  16.9 0.1 fusion.9
  17.0 1.6 %collective-permute-start.9 = (bf16[8,8192]{1,0:T(8,128)(2,1)S(1)}, bf16[8,8192]{1,0:T(8,128)(2,1)S(1)}, u32[]{:S(2)}, u32[]{:S(2)}) collective-permute-start(bf16[8,8192]{1,0:T(8,128)(2,1)S(1)} %get-tuple-element.50), channel_id=1, source_target_pairs={{0,8},{1,9},{2,10},{3,11},{4,12},{5,13},{6,14},{7,15},{8,16},{9,17... | collective-permute-start | bytes 393224 | tf_op jit(solution)/shard_map/ppermute | solution.py:39
  18.7 1.5 %collective-permute-start.12 = (bf16[8,8192]{1,0:T(8,128)(2,1)S(1)}, bf16[8,8192]{1,0:T(8,128)(2,1)S(1)}, u32[]{:S(2)}, u32[]{:S(2)}) collective-permute-start(bf16[8,8192]{1,0:T(8,128)(2,1)S(1)} %get-tuple-element.51), channel_id=1, source_target_pairs={{0,4},{1,3},{2,6},{3,1},{4,0},{5,7},{6,2},{7,5},{8,12},{9,11},{10,... | collective-permute-start | bytes 393224 | tf_op jit(solution)/shard_map/ppermute | solution.py:30
  20.2 1.5 %collective-permute-start.11 = (bf16[8,8192]{1,0:T(8,128)(2,1)S(1)}, bf16[8,8192]{1,0:T(8,128)(2,1)S(1)}, u32[]{:S(2)}, u32[]{:S(2)}) collective-permute-start(bf16[8,8192]{1,0:T(8,128)(2,1)S(1)} %get-tuple-element.52), channel_id=1, source_target_pairs={{0,2},{1,5},{2,0},{3,7},{4,6},{5,1},{6,4},{7,3},{8,10},{9,13},{10,... | collective-permute-start | bytes 393224 | tf_op jit(solution)/shard_map/ppermute | solution.py:30
  21.6 0.0 collective-permute-done.5
  21.6 0.1 fusion.8
  21.8 0.6 %collective-permute-start.6 = (bf16[8,8192]{1,0:T(8,128)(2,1)S(1)}, bf16[8,8192]{1,0:T(8,128)(2,1)S(1)}, u32[]{:S(2)}, u32[]{:S(2)}) collective-permute-start(bf16[8,8192]{1,0:T(8,128)(2,1)S(1)} %get-tuple-element.48), channel_id=1, source_target_pairs={{0,2},{1,5},{2,0},{3,7},{4,6},{5,1},{6,4},{7,3},{8,10},{9,13},{10,... | collective-permute-start | bytes 393224 | tf_op jit(solution)/shard_map/ppermute | solution.py:30
  22.4 0.5 %collective-permute-start.7 = (bf16[8,8192]{1,0:T(8,128)(2,1)S(1)}, bf16[8,8192]{1,0:T(8,128)(2,1)S(1)}, u32[]{:S(2)}, u32[]{:S(2)}) collective-permute-start(bf16[8,8192]{1,0:T(8,128)(2,1)S(1)} %get-tuple-element.49), channel_id=1, source_target_pairs={{0,4},{1,3},{2,6},{3,1},{4,0},{5,7},{6,2},{7,5},{8,12},{9,11},{10,... | collective-permute-start | bytes 393224 | tf_op jit(solution)/shard_map/ppermute | solution.py:30
  22.9 1.5 %collective-permute-done.9 = bf16[8,8192]{1,0:T(8,128)(2,1)S(1)} collective-permute-done((bf16[8,8192]{1,0:T(8,128)(2,1)S(1)}, bf16[8,8192]{1,0:T(8,128)(2,1)S(1)}, u32[]{:S(2)}, u32[]{:S(2)}) %collective-permute-start.9) | collective-permute-done | bytes 131104 | tf_op jit(solution)/shard_map/ppermute | solution.py:39
  24.5 2.5 %collective-permute-start.10 = (bf16[8,8192]{1,0:T(8,128)(2,1)S(1)}, bf16[8,8192]{1,0:T(8,128)(2,1)S(1)}, u32[]{:S(2)}, u32[]{:S(2)}) collective-permute-start(bf16[8,8192]{1,0:T(8,128)(2,1)S(1)} %slice_add_fusion.1), channel_id=1, source_target_pairs={{0,6},{1,7},{2,4},{3,5},{4,2},{5,3},{6,0},{7,1},{8,14},{9,15},{10,... | collective-permute-start | bytes 393224 | tf_op jit(solution)/shard_map/ppermute | solution.py:30
  27.0 0.0 collective-permute-done.12
  27.0 0.0 collective-permute-done.11
  27.1 2.7 %collective-permute-start.13 = (bf16[8,8192]{1,0:T(8,128)(2,1)S(1)}, bf16[8,8192]{1,0:T(8,128)(2,1)S(1)}, u32[]{:S(2)}, u32[]{:S(2)}) collective-permute-start(bf16[8,8192]{1,0:T(8,128)(2,1)S(1)} %convert_element_type.71), channel_id=1, source_target_pairs={{0,8},{1,9},{2,10},{3,11},{4,12},{5,13},{6,14},{7,15},{8,16},{9,17... | collective-permute-start | bytes 393224 | tf_op jit(solution)/shard_map/ppermute | solution.py:45
  29.8 0.0 collective-permute-done.6
  29.8 0.0 collective-permute-done.7
  29.8 0.9 %collective-permute-done.10 = bf16[8,8192]{1,0:T(8,128)(2,1)S(1)} collective-permute-done((bf16[8,8192]{1,0:T(8,128)(2,1)S(1)}, bf16[8,8192]{1,0:T(8,128)(2,1)S(1)}, u32[]{:S(2)}, u32[]{:S(2)}) %collective-permute-start.10) | collective-permute-done | bytes 131104 | tf_op jit(solution)/shard_map/ppermute | solution.py:30
  30.7 0.1 fusion.7
  30.8 1.3 %collective-permute-start.14 = (bf16[8,8192]{1,0:T(8,128)(2,1)S(1)}, bf16[8,8192]{1,0:T(8,128)(2,1)S(1)}, u32[]{:S(2)}, u32[]{:S(2)}) collective-permute-start(bf16[8,8192]{1,0:T(8,128)(2,1)S(1)} %fusion.7), channel_id=1, source_target_pairs={{8,0},{9,1},{10,2},{11,3},{12,4},{13,5},{14,6},{15,7},{16,8},{17,9... | collective-permute-start | bytes 393224 | tf_op jit(solution)/shard_map/ppermute | solution.py:50
  32.1 0.2 collective-permute-done.13
  32.3 0.1 constant_dynamic-update-slice_fusion.12
  32.4 0.0 copy-start.3
  32.4 2.1 %collective-permute-start.19 = (bf16[8,8192]{1,0:T(8,128)(2,1)S(1)}, bf16[8,8192]{1,0:T(8,128)(2,1)S(1)}, u32[]{:S(2)}, u32[]{:S(2)}) collective-permute-start(bf16[8,8192]{1,0:T(8,128)(2,1)S(1)} %get-tuple-element.43), channel_id=1, source_target_pairs={{0,6},{1,7},{2,4},{3,5},{4,2},{5,3},{6,0},{7,1},{8,14},{9,15},{10,... | collective-permute-start | bytes 393224 | tf_op jit(solution)/shard_map/ppermute | solution.py:30
  34.4 0.9 %collective-permute-start.18 = (bf16[8,8192]{1,0:T(8,128)(2,1)S(1)}, bf16[8,8192]{1,0:T(8,128)(2,1)S(1)}, u32[]{:S(2)}, u32[]{:S(2)}) collective-permute-start(bf16[8,8192]{1,0:T(8,128)(2,1)S(1)} %get-tuple-element.43), channel_id=1, source_target_pairs={{0,4},{1,3},{2,6},{3,1},{4,0},{5,7},{6,2},{7,5},{8,12},{9,11},{10,... | collective-permute-start | bytes 393224 | tf_op jit(solution)/shard_map/ppermute | solution.py:30
  35.3 0.6 %collective-permute-start.17 = (bf16[8,8192]{1,0:T(8,128)(2,1)S(1)}, bf16[8,8192]{1,0:T(8,128)(2,1)S(1)}, u32[]{:S(2)}, u32[]{:S(2)}) collective-permute-start(bf16[8,8192]{1,0:T(8,128)(2,1)S(1)} %get-tuple-element.43), channel_id=1, source_target_pairs={{0,2},{1,5},{2,0},{3,7},{4,6},{5,1},{6,4},{7,3},{8,10},{9,13},{10,... | collective-permute-start | bytes 393224 | tf_op jit(solution)/shard_map/ppermute | solution.py:30
  35.9 1.8 %collective-permute-done.14 = bf16[8,8192]{1,0:T(8,128)(2,1)S(1)} collective-permute-done((bf16[8,8192]{1,0:T(8,128)(2,1)S(1)}, bf16[8,8192]{1,0:T(8,128)(2,1)S(1)}, u32[]{:S(2)}, u32[]{:S(2)}) %collective-permute-start.14) | collective-permute-done | bytes 131104 | tf_op jit(solution)/shard_map/ppermute | solution.py:50
  37.8 1.5 %collective-permute-start.16 = (bf16[8,8192]{1,0:T(8,128)(2,1)S(1)}, bf16[8,8192]{1,0:T(8,128)(2,1)S(1)}, u32[]{:S(2)}, u32[]{:S(2)}) collective-permute-start(bf16[8,8192]{1,0:T(8,128)(2,1)S(1)} %select_convert_fusion), channel_id=1, source_target_pairs={{0,4},{1,3},{2,6},{3,1},{4,0},{5,7},{6,2},{7,5},{8,12},{9,11},{10,... | collective-permute-start | bytes 393224 | tf_op jit(solution)/shard_map/ppermute | solution.py:30
  39.3 1.2 %collective-permute-start.15 = (bf16[8,8192]{1,0:T(8,128)(2,1)S(1)}, bf16[8,8192]{1,0:T(8,128)(2,1)S(1)}, u32[]{:S(2)}, u32[]{:S(2)}) collective-permute-start(bf16[8,8192]{1,0:T(8,128)(2,1)S(1)} %select_convert_fusion), channel_id=1, source_target_pairs={{0,2},{1,5},{2,0},{3,7},{4,6},{5,1},{6,4},{7,3},{8,10},{9,13},{10,... | collective-permute-start | bytes 393224 | tf_op jit(solution)/shard_map/ppermute | solution.py:30
  40.5 0.0 collective-permute-done.19
  40.5 1.3 %collective-permute-start.21 = (bf16[8,8192]{1,0:T(8,128)(2,1)S(1)}, bf16[8,8192]{1,0:T(8,128)(2,1)S(1)}, u32[]{:S(2)}, u32[]{:S(2)}) collective-permute-start(bf16[8,8192]{1,0:T(8,128)(2,1)S(1)} %collective-permute-done.19), channel_id=1, source_target_pairs={{8,0},{9,1},{10,2},{11,3},{12,4},{13,5},{14,6},{15,7},{16,8},{17,9... | collective-permute-start | bytes 393224 | tf_op jit(solution)/shard_map/ppermute | solution.py:50
  41.8 0.0 collective-permute-done.18
  41.8 0.0 collective-permute-done.17
  41.9 0.1 collective-permute-start.20
  42.0 5.4 %collective-permute-done.21 = bf16[8,8192]{1,0:T(8,128)(2,1)S(1)} collective-permute-done((bf16[8,8192]{1,0:T(8,128)(2,1)S(1)}, bf16[8,8192]{1,0:T(8,128)(2,1)S(1)}, u32[]{:S(2)}, u32[]{:S(2)}) %collective-permute-start.21) | collective-permute-done | bytes 131104 | tf_op jit(solution)/shard_map/ppermute | solution.py:50
  47.4 0.0 collective-permute-start.23
  47.4 0.0 collective-permute-done.16
  47.4 0.0 collective-permute-done.15
  47.4 0.0 collective-permute-done.20
  47.4 0.6 %collective-permute-start.22 = (bf16[24,8192]{1,0:T(8,128)(2,1)S(1)}, bf16[24,8192]{1,0:T(8,128)(2,1)S(1)}, u32[]{:S(2)}, u32[]{:S(2)}) collective-permute-start(bf16[24,8192]{1,0:T(8,128)(2,1)S(1)} %pad_maximum_fusion.2), channel_id=1, source_target_pairs={{0,1},{1,0},{2,3},{3,2},{4,5},{5,4},{6,7},{7,6},{8,9},{9,8},{10,11... | collective-permute-start | bytes 1179656 | tf_op jit(solution)/shard_map/ppermute | solution.py:34
  48.0 1.4 %grad_own.1 = (f32[64,256]{1,0:T(8,128)S(1)}, f32[8,128]{1,0:T(8,128)}) custom-call(bf16[64,8192]{1,0:T(8,128)(2,1)S(1)} %constant_dynamic-update-slice_fusion.8.rows_ref, bf16[256,8192]{1,0:T(8,128)(2,1)S(1)} %get-tuple-element.29.dec_ref), custom_call_target="tpu_custom_call" | custom-call | flops 268435456 | bytes 4194304 | tf_op jit(solution)/shard_map/grad_own/pallas_call | solution.py:198
  49.4 0.0 collective-permute-done.23
  49.4 0.0 collective-permute-done.22
  49.4 0.1 pad_maximum_fusion.rows_ref
  49.5 2.0 %grad_all.1 = f32[1,64,256]{2,1,0:T(8,128)} custom-call(bf16[64,8192]{1,0:T(8,128)(2,1)S(1)} %pad_maximum_fusion.rows_ref, bf16[256,8192]{1,0:T(8,128)(2,1)S(1)} %get-tuple-element.33.dec_ref, f32[64,256]{1,0:T(8,128)S(1)} %get-tuple-element.41.own_ref), custom_call_target="tpu_custom_call" | custom-call | flops 268435456 | bytes 4194304 | tf_op jit(solution)/shard_map/grad_all/pallas_call | solution.py:210
  (30 shorter events, 0.4 us)
Async XLA Ops:
  0.6 9.4 %copy-start = (s32[1,2,2]{2,1,0:T(2,128)S(1)}, s32[1,2,2]{2,1,0:T(2,128)}, u32[]{:S(2)}) copy-start(s32[1,2,2]{2,1,0:T(2,128)} %param.9) | copy-start | bytes 52
  0.6 9.4 %copy-start.1 = (bf16[1,256]{1,0:T(2,128)(2,1)S(1)}, bf16[1,256]{1,0:T(2,128)(2,1)}, u32[]{:S(2)}) copy-start(bf16[1,256]{1,0:T(2,128)(2,1)} %bias_ref) | copy-start | bytes 1540
  0.7 10.8 %copy-start.4 = (bf16[1,8,8192]{2,1,0:T(8,128)(2,1)S(1)}, bf16[1,8,8192]{2,1,0:T(8,128)(2,1)}, u32[]{:S(2)}) copy-start(bf16[1,8,8192]{2,1,0:T(8,128)(2,1)} %param.6) | copy-start | bytes 393220
  0.7 9.5 %collective-permute-start = (bf16[8,8192]{1,0:T(8,128)(2,1)}, bf16[8,8192]{1,0:T(8,128)(2,1)S(1)}, u32[]{:S(2)}, u32[]{:S(2)}) collective-permute-start(bf16[8,8192]{1,0:T(8,128)(2,1)} %bitcast.15), channel_id=1, source_target_pairs={{0,6},{1,7},{2,4},{3,5},{4,2},{5,3},{6,0},{7,1},{8,14},{9,15},{10,... | collective-permute-start | bytes 393224 | tf_op jit(solution)/shard_map/ppermute | solution.py:30
  4.6 6.9 %collective-permute-start.3 = (bf16[8,8192]{1,0:T(8,128)(2,1)}, bf16[8,8192]{1,0:T(8,128)(2,1)S(1)}, u32[]{:S(2)}, u32[]{:S(2)}) collective-permute-start(bf16[8,8192]{1,0:T(8,128)(2,1)} %bitcast.16), channel_id=1, source_target_pairs={{0,1},{1,0},{2,3},{3,2},{4,5},{5,4},{6,7},{7,6},{8,9},{9,8},{10,11... | collective-permute-start | bytes 393224 | tf_op jit(solution)/shard_map/ppermute | solution.py:34
  4.6 6.8 %collective-permute-start.2 = (bf16[8,8192]{1,0:T(8,128)(2,1)}, bf16[8,8192]{1,0:T(8,128)(2,1)S(1)}, u32[]{:S(2)}, u32[]{:S(2)}) collective-permute-start(bf16[8,8192]{1,0:T(8,128)(2,1)} %bitcast.17), channel_id=1, source_target_pairs={{0,2},{1,5},{2,0},{3,7},{4,6},{5,1},{6,4},{7,3},{8,10},{9,13},{10,... | collective-permute-start | bytes 393224 | tf_op jit(solution)/shard_map/ppermute | solution.py:30
  5.2 6.0 %collective-permute-start.1 = (bf16[8,8192]{1,0:T(8,128)(2,1)}, bf16[8,8192]{1,0:T(8,128)(2,1)S(1)}, u32[]{:S(2)}, u32[]{:S(2)}) collective-permute-start(bf16[8,8192]{1,0:T(8,128)(2,1)} %bitcast.18), channel_id=1, source_target_pairs={{0,4},{1,3},{2,6},{3,1},{4,0},{5,7},{6,2},{7,5},{8,12},{9,11},{10,... | collective-permute-start | bytes 393224 | tf_op jit(solution)/shard_map/ppermute | solution.py:30
  11.4 1.8 %collective-permute-start.4 = (bf16[24,8192]{1,0:T(8,128)(2,1)S(1)}, bf16[24,8192]{1,0:T(8,128)(2,1)S(1)}, u32[]{:S(2)}, u32[]{:S(2)}) collective-permute-start(bf16[24,8192]{1,0:T(8,128)(2,1)S(1)} %constant_dynamic-update-slice_fusion), channel_id=1, source_target_pairs={{0,1},{1,0},{2,3},{3,2},{4,5},{5,4},{6,7},{7,6},{8,9},{9,8},{10,11... | collective-permute-start | bytes 1179656 | tf_op jit(solution)/shard_map/ppermute | solution.py:34
  14.9 2.0 %collective-permute-start.8 = (bf16[32,8192]{1,0:T(8,128)(2,1)S(1)}, bf16[32,8192]{1,0:T(8,128)(2,1)S(1)}, u32[]{:S(2)}, u32[]{:S(2)}) collective-permute-start(bf16[32,8192]{1,0:T(8,128)(2,1)S(1)} %get-tuple-element.35), channel_id=1, source_target_pairs={{0,1},{1,0},{2,3},{3,2},{4,5},{5,4},{6,7},{7,6},{8,9},{9,8},{10,11... | collective-permute-start | bytes 1572872 | tf_op jit(solution)/shard_map/ppermute | solution.py:34
  16.0 5.7 %collective-permute-start.5 = (bf16[32,8192]{1,0:T(8,128)(2,1)S(1)}, bf16[32,8192]{1,0:T(8,128)(2,1)S(1)}, u32[]{:S(2)}, u32[]{:S(2)}) collective-permute-start(bf16[32,8192]{1,0:T(8,128)(2,1)S(1)} %get-tuple-element.31), channel_id=1, source_target_pairs={{0,1},{1,0},{2,3},{3,2},{4,5},{5,4},{6,7},{7,6},{8,9},{9,8},{10,11... | collective-permute-start | bytes 1572872 | tf_op jit(solution)/shard_map/ppermute | solution.py:34
  16.9 13.8 %copy-start.2 = (bf16[1,8,8192]{2,1,0:T(8,128)(2,1)S(1)}, bf16[1,8,8192]{2,1,0:T(8,128)(2,1)}, u32[]{:S(2)}) copy-start(bf16[1,8,8192]{2,1,0:T(8,128)(2,1)} %param.11) | copy-start | bytes 393220
  17.0 7.5 %collective-permute-start.9 = (bf16[8,8192]{1,0:T(8,128)(2,1)S(1)}, bf16[8,8192]{1,0:T(8,128)(2,1)S(1)}, u32[]{:S(2)}, u32[]{:S(2)}) collective-permute-start(bf16[8,8192]{1,0:T(8,128)(2,1)S(1)} %get-tuple-element.50), channel_id=1, source_target_pairs={{0,8},{1,9},{2,10},{3,11},{4,12},{5,13},{6,14},{7,15},{8,16},{9,17... | collective-permute-start | bytes 393224 | tf_op jit(solution)/shard_map/ppermute | solution.py:39
  18.7 8.3 %collective-permute-start.12 = (bf16[8,8192]{1,0:T(8,128)(2,1)S(1)}, bf16[8,8192]{1,0:T(8,128)(2,1)S(1)}, u32[]{:S(2)}, u32[]{:S(2)}) collective-permute-start(bf16[8,8192]{1,0:T(8,128)(2,1)S(1)} %get-tuple-element.51), channel_id=1, source_target_pairs={{0,4},{1,3},{2,6},{3,1},{4,0},{5,7},{6,2},{7,5},{8,12},{9,11},{10,... | collective-permute-start | bytes 393224 | tf_op jit(solution)/shard_map/ppermute | solution.py:30
  20.2 6.9 %collective-permute-start.11 = (bf16[8,8192]{1,0:T(8,128)(2,1)S(1)}, bf16[8,8192]{1,0:T(8,128)(2,1)S(1)}, u32[]{:S(2)}, u32[]{:S(2)}) collective-permute-start(bf16[8,8192]{1,0:T(8,128)(2,1)S(1)} %get-tuple-element.52), channel_id=1, source_target_pairs={{0,2},{1,5},{2,0},{3,7},{4,6},{5,1},{6,4},{7,3},{8,10},{9,13},{10,... | collective-permute-start | bytes 393224 | tf_op jit(solution)/shard_map/ppermute | solution.py:30
  21.8 8.0 %collective-permute-start.6 = (bf16[8,8192]{1,0:T(8,128)(2,1)S(1)}, bf16[8,8192]{1,0:T(8,128)(2,1)S(1)}, u32[]{:S(2)}, u32[]{:S(2)}) collective-permute-start(bf16[8,8192]{1,0:T(8,128)(2,1)S(1)} %get-tuple-element.48), channel_id=1, source_target_pairs={{0,2},{1,5},{2,0},{3,7},{4,6},{5,1},{6,4},{7,3},{8,10},{9,13},{10,... | collective-permute-start | bytes 393224 | tf_op jit(solution)/shard_map/ppermute | solution.py:30
  22.4 7.4 %collective-permute-start.7 = (bf16[8,8192]{1,0:T(8,128)(2,1)S(1)}, bf16[8,8192]{1,0:T(8,128)(2,1)S(1)}, u32[]{:S(2)}, u32[]{:S(2)}) collective-permute-start(bf16[8,8192]{1,0:T(8,128)(2,1)S(1)} %get-tuple-element.49), channel_id=1, source_target_pairs={{0,4},{1,3},{2,6},{3,1},{4,0},{5,7},{6,2},{7,5},{8,12},{9,11},{10,... | collective-permute-start | bytes 393224 | tf_op jit(solution)/shard_map/ppermute | solution.py:30
  24.5 6.2 %collective-permute-start.10 = (bf16[8,8192]{1,0:T(8,128)(2,1)S(1)}, bf16[8,8192]{1,0:T(8,128)(2,1)S(1)}, u32[]{:S(2)}, u32[]{:S(2)}) collective-permute-start(bf16[8,8192]{1,0:T(8,128)(2,1)S(1)} %slice_add_fusion.1), channel_id=1, source_target_pairs={{0,6},{1,7},{2,4},{3,5},{4,2},{5,3},{6,0},{7,1},{8,14},{9,15},{10,... | collective-permute-start | bytes 393224 | tf_op jit(solution)/shard_map/ppermute | solution.py:30
  27.1 5.2 %collective-permute-start.13 = (bf16[8,8192]{1,0:T(8,128)(2,1)S(1)}, bf16[8,8192]{1,0:T(8,128)(2,1)S(1)}, u32[]{:S(2)}, u32[]{:S(2)}) collective-permute-start(bf16[8,8192]{1,0:T(8,128)(2,1)S(1)} %convert_element_type.71), channel_id=1, source_target_pairs={{0,8},{1,9},{2,10},{3,11},{4,12},{5,13},{6,14},{7,15},{8,16},{9,17... | collective-permute-start | bytes 393224 | tf_op jit(solution)/shard_map/ppermute | solution.py:45
  30.8 6.9 %collective-permute-start.14 = (bf16[8,8192]{1,0:T(8,128)(2,1)S(1)}, bf16[8,8192]{1,0:T(8,128)(2,1)S(1)}, u32[]{:S(2)}, u32[]{:S(2)}) collective-permute-start(bf16[8,8192]{1,0:T(8,128)(2,1)S(1)} %fusion.7), channel_id=1, source_target_pairs={{8,0},{9,1},{10,2},{11,3},{12,4},{13,5},{14,6},{15,7},{16,8},{17,9... | collective-permute-start | bytes 393224 | tf_op jit(solution)/shard_map/ppermute | solution.py:50
  32.4 17.0 %copy-start.3 = (bf16[8,8192]{1,0:T(8,128)(2,1)}, bf16[8,8192]{1,0:T(8,128)(2,1)S(1)}, u32[]{:S(2)}) copy-start(bf16[8,8192]{1,0:T(8,128)(2,1)S(1)} %get-tuple-element.43) | copy-start | bytes 393220
  32.4 8.1 %collective-permute-start.19 = (bf16[8,8192]{1,0:T(8,128)(2,1)S(1)}, bf16[8,8192]{1,0:T(8,128)(2,1)S(1)}, u32[]{:S(2)}, u32[]{:S(2)}) collective-permute-start(bf16[8,8192]{1,0:T(8,128)(2,1)S(1)} %get-tuple-element.43), channel_id=1, source_target_pairs={{0,6},{1,7},{2,4},{3,5},{4,2},{5,3},{6,0},{7,1},{8,14},{9,15},{10,... | collective-permute-start | bytes 393224 | tf_op jit(solution)/shard_map/ppermute | solution.py:30
  34.4 7.4 %collective-permute-start.18 = (bf16[8,8192]{1,0:T(8,128)(2,1)S(1)}, bf16[8,8192]{1,0:T(8,128)(2,1)S(1)}, u32[]{:S(2)}, u32[]{:S(2)}) collective-permute-start(bf16[8,8192]{1,0:T(8,128)(2,1)S(1)} %get-tuple-element.43), channel_id=1, source_target_pairs={{0,4},{1,3},{2,6},{3,1},{4,0},{5,7},{6,2},{7,5},{8,12},{9,11},{10,... | collective-permute-start | bytes 393224 | tf_op jit(solution)/shard_map/ppermute | solution.py:30
  35.3 6.5 %collective-permute-start.17 = (bf16[8,8192]{1,0:T(8,128)(2,1)S(1)}, bf16[8,8192]{1,0:T(8,128)(2,1)S(1)}, u32[]{:S(2)}, u32[]{:S(2)}) collective-permute-start(bf16[8,8192]{1,0:T(8,128)(2,1)S(1)} %get-tuple-element.43), channel_id=1, source_target_pairs={{0,2},{1,5},{2,0},{3,7},{4,6},{5,1},{6,4},{7,3},{8,10},{9,13},{10,... | collective-permute-start | bytes 393224 | tf_op jit(solution)/shard_map/ppermute | solution.py:30
  37.8 9.6 %collective-permute-start.16 = (bf16[8,8192]{1,0:T(8,128)(2,1)S(1)}, bf16[8,8192]{1,0:T(8,128)(2,1)S(1)}, u32[]{:S(2)}, u32[]{:S(2)}) collective-permute-start(bf16[8,8192]{1,0:T(8,128)(2,1)S(1)} %select_convert_fusion), channel_id=1, source_target_pairs={{0,4},{1,3},{2,6},{3,1},{4,0},{5,7},{6,2},{7,5},{8,12},{9,11},{10,... | collective-permute-start | bytes 393224 | tf_op jit(solution)/shard_map/ppermute | solution.py:30
  39.3 8.1 %collective-permute-start.15 = (bf16[8,8192]{1,0:T(8,128)(2,1)S(1)}, bf16[8,8192]{1,0:T(8,128)(2,1)S(1)}, u32[]{:S(2)}, u32[]{:S(2)}) collective-permute-start(bf16[8,8192]{1,0:T(8,128)(2,1)S(1)} %select_convert_fusion), channel_id=1, source_target_pairs={{0,2},{1,5},{2,0},{3,7},{4,6},{5,1},{6,4},{7,3},{8,10},{9,13},{10,... | collective-permute-start | bytes 393224 | tf_op jit(solution)/shard_map/ppermute | solution.py:30
  40.5 6.9 %collective-permute-start.21 = (bf16[8,8192]{1,0:T(8,128)(2,1)S(1)}, bf16[8,8192]{1,0:T(8,128)(2,1)S(1)}, u32[]{:S(2)}, u32[]{:S(2)}) collective-permute-start(bf16[8,8192]{1,0:T(8,128)(2,1)S(1)} %collective-permute-done.19), channel_id=1, source_target_pairs={{8,0},{9,1},{10,2},{11,3},{12,4},{13,5},{14,6},{15,7},{16,8},{17,9... | collective-permute-start | bytes 393224 | tf_op jit(solution)/shard_map/ppermute | solution.py:50
  41.9 5.5 %collective-permute-start.20 = (bf16[32,8192]{1,0:T(8,128)(2,1)S(1)}, bf16[32,8192]{1,0:T(8,128)(2,1)S(1)}, u32[]{:S(2)}, u32[]{:S(2)}) collective-permute-start(bf16[32,8192]{1,0:T(8,128)(2,1)S(1)} %pad_maximum_fusion.1), channel_id=1, source_target_pairs={{0,1},{1,0},{2,3},{3,2},{4,5},{5,4},{6,7},{7,6},{8,9},{9,8},{10,11... | collective-permute-start | bytes 1572872 | tf_op jit(solution)/shard_map/ppermute | solution.py:34
  47.4 2.1 %collective-permute-start.23 = (bf16[8,8192]{1,0:T(8,128)(2,1)S(1)}, bf16[8,8192]{1,0:T(8,128)(2,1)S(1)}, u32[]{:S(2)}, u32[]{:S(2)}) collective-permute-start(bf16[8,8192]{1,0:T(8,128)(2,1)S(1)} %collective-permute-done.21), channel_id=1, source_target_pairs={{0,1},{1,0},{2,3},{3,2},{4,5},{5,4},{6,7},{7,6},{8,9},{9,8},{10,11... | collective-permute-start | bytes 393224 | tf_op jit(solution)/shard_map/ppermute | solution.py:34
  47.4 2.0 %collective-permute-start.22 = (bf16[24,8192]{1,0:T(8,128)(2,1)S(1)}, bf16[24,8192]{1,0:T(8,128)(2,1)S(1)}, u32[]{:S(2)}, u32[]{:S(2)}) collective-permute-start(bf16[24,8192]{1,0:T(8,128)(2,1)S(1)} %pad_maximum_fusion.2), channel_id=1, source_target_pairs={{0,1},{1,0},{2,3},{3,2},{4,5},{5,4},{6,7},{7,6},{8,9},{9,8},{10,11... | collective-permute-start | bytes 1179656 | tf_op jit(solution)/shard_map/ppermute | solution.py:34

commit v19 on v18

--- a/solution.py
+++ b/solution.py
@@ -48,6 +48,12 @@
 def lowered(value, group):
     size = lax.axis_size(AXIS)
     return lax.ppermute(value, AXIS, [(i + group, i) for i in range(size - group)])
+
+
+def rotated_down(value, final, group):
+    size = lax.axis_size(AXIS)
+    came = lax.ppermute(value, AXIS, [((i + group) % size, i) for i in range(size)])
+    return jnp.where(final, jnp.zeros_like(came), came)
 
 
 def after(values, done):
@@ -188,7 +194,9 @@
     total = own_ref[...] + back(rows_ref, dec_ref)
     group = total.shape[0] // tokens
     for block in range(group):
-        slab = slab_of(place_in(group), block, group // CORES)
+        chips = group // CORES
+        label = (chips - block % chips) % chips
+        slab = slab_of(place_in(group), block // chips * chips + label, chips)
         where = pl.ds(pl.multiple_of(slab * tokens, tokens), tokens)
         out_ref[0, where, :] = total[block * tokens : (block + 1) * tokens]
 
@@ -262,14 +270,14 @@
     error = (own_less + below).astype(jnp.bfloat16)
     later = jnp.where(final, 0.0, next_sum + after(above, error)).astype(jnp.bfloat16)
 
-    heres = [error] + [across(error, chip, chips) for chip in range(1, chips)]
-    afters = [later] + [across(later, chip, chips) for chip in range(1, chips - 1)]
-    last = lowered(after(heres[-1], later), group)
+    heres = [error] + [across(error, chip, chips) for chip in range(chips - 1, 0, -1)]
+    passed = rotated_down(after(heres[-1], later), final, group)
     here_near = jnp.concatenate(heres, axis=0)
     here_far = other_core(here_near)
     here_rows = jnp.concatenate([here_near, here_far], axis=0)
-    most = after(jnp.concatenate(afters, axis=0), here_far)
-    after_rows = jnp.concatenate([most, last, other_core(most), other_core(last)], axis=0)
+    straight = [across(later, chip, chips) for chip in range(chips - 1, 1, -1)]
+    most = after(jnp.concatenate([later] + straight, axis=0), here_far)
+    after_rows = jnp.concatenate([most, passed, other_core(most), other_core(passed)], axis=0)
     grad = grad_all(after_rows, next_dec, grad_own(here_rows, own_dec), tokens)
     return (error[None], grad)
 

time: 51.8 us -> 50.5 us (0.975)
  waiting for transfers between devices: 13.1 us -> 10 us
  starting transfers between devices: 25.8 us -> 27.6 us
    ppermute x2 -> x1, waiting for transfers between devices: 7.13 us -> 1.77 us  [lowered(): lax.ppermute(value, AXIS, [(i + group, i) for i in range(size - group)])]
    ppermute x0 -> x1, starting transfers between devices: none -> 2.8 us  [rotated_down(): lax.ppermute(value, AXIS, [((i + group) % size, i) for i in range(size)])]
    ppermute x0 -> x1, waiting for transfers between devices: none -> 2.34 us  [rotated_down(): lax.ppermute(value, AXIS, [((i + group) % size, i) for i in range(size)])]
    ppermute x2 -> x1, starting transfers between devices: 2.57 us -> 1.29 us  [lowered(): lax.ppermute(value, AXIS, [(i + group, i) for i in range(size - group)])]
where the time goes in v19:
time: 50.5 us; the launch traced here: 50.3 us
  starting transfers between devices  27.6 us (55%)
  waiting for transfers between devices  10 us (20%)
  Pallas kernels  9.89 us (20%)
  between operations  1.05 us (2%)
  matrix products  0.8 us (2%)
  other arithmetic  0.69 us (1%)
    ppermute x13, starting transfers between devices, across(): return lax.ppermute(value, AXIS, pairs)  17.8 us
    pallas_call x1, Pallas kernels, loaded(): pl.pallas_call(load_kernel, out_shape=[pltpu.VMEM(enc.shape[1:], enc.dtyp...  4.68 us
    ppermute x1, starting transfers between devices, rotated_down(): lax.ppermute(value, AXIS, [((i + group) % size, i) for i in range(size)])  2.8 us
    ppermute x1, starting transfers between devices, shifted(): lax.ppermute(value, AXIS, [(i, i + group) for i in range(size - group)])  2.7 us
    ppermute x1, waiting for transfers between devices, rotated_down(): lax.ppermute(value, AXIS, [((i + group) % size, i) for i in range(size)])  2.34 us
    ppermute x13, waiting for transfers between devices, across(): return lax.ppermute(value, AXIS, pairs)  2.1 us
    ppermute x7, waiting for transfers between devices, other_core(): lax.ppermute(value, AXIS, [(i, i ^ 1) for i in range(lax.axis_size(AXIS))])  2.1 us
    pallas_call x1, Pallas kernels, grad_all(): pl.pallas_call(functools.partial(grad_all_kernel, tokens), out_shape=jax....  2.03 us
  transfers between devices with their start and end apart: 24, of which 9 were waited for; matrix products, arithmetic and copies ran while one was open for 2% of the time, Pallas kernels for 14%

profile of v19, /device:TPU:0, one launch (start us, length us, event | category | flops | bytes accessed | tf_op | source)
XLA Modules:
  0.0 50.3 jit_solution(13726934076839151572)
XLA Ops:
  0.6 0.0 copy-start
  0.6 0.0 copy-start.1
  0.7 0.0 copy-start.4
  0.7 4.0 %collective-permute-start = (bf16[8,8192]{1,0:T(8,128)(2,1)}, bf16[8,8192]{1,0:T(8,128)(2,1)S(1)}, u32[]{:S(2)}, u32[]{:S(2)}) collective-permute-start(bf16[8,8192]{1,0:T(8,128)(2,1)} %bitcast.15), channel_id=1, source_target_pairs={{0,6},{1,7},{2,4},{3,5},{4,2},{5,3},{6,0},{7,1},{8,14},{9,15},{10,... | collective-permute-start | bytes 393224 | tf_op jit(solution)/shard_map/ppermute | solution.py:30
  4.6 0.0 collective-permute-start.3
  4.6 0.5 %collective-permute-start.2 = (bf16[8,8192]{1,0:T(8,128)(2,1)}, bf16[8,8192]{1,0:T(8,128)(2,1)S(1)}, u32[]{:S(2)}, u32[]{:S(2)}) collective-permute-start(bf16[8,8192]{1,0:T(8,128)(2,1)} %bitcast.17), channel_id=1, source_target_pairs={{0,2},{1,5},{2,0},{3,7},{4,6},{5,1},{6,4},{7,3},{8,10},{9,13},{10,... | collective-permute-start | bytes 393224 | tf_op jit(solution)/shard_map/ppermute | solution.py:30
  5.2 0.2 collective-permute-start.1
  5.3 4.7 %load_weights.1 = (bf16[8192,256]{1,0:T(8,128)(2,1)S(1)}, bf16[256,8192]{1,0:T(8,128)(2,1)S(1)}, bf16[256,8192]{1,0:T(8,128)(2,1)S(1)}) custom-call(bf16[1,8192,256]{2,1,0:T(8,128)(2,1)} %enc_hbm.1, bf16[1,2,256,8192]{3,2,1,0:T(8,128)(2,1)} %dec_hbm.1), custom_call_target="tpu_custom_call" | custom-call | bytes 25165824 | tf_op jit(solution)/shard_map/load_weights/pallas_call | solution.py:92
  10.1 0.1 gate.1
  10.2 0.0 collective-permute-done
  10.2 0.9 %collective-permute-done.1 = bf16[8,8192]{1,0:T(8,128)(2,1)S(1)} collective-permute-done((bf16[8,8192]{1,0:T(8,128)(2,1)}, bf16[8,8192]{1,0:T(8,128)(2,1)S(1)}, u32[]{:S(2)}, u32[]{:S(2)}) %collective-permute-start.1) | collective-permute-done | bytes 131104 | tf_op jit(solution)/shard_map/ppermute | solution.py:30
  11.2 0.2 collective-permute-done.2
  11.4 0.1 collective-permute-start.4
  11.6 0.0 collective-permute-done.3
  11.6 1.6 %collective-permute-done.4 = bf16[24,8192]{1,0:T(8,128)(2,1)S(1)} collective-permute-done((bf16[24,8192]{1,0:T(8,128)(2,1)S(1)}, bf16[24,8192]{1,0:T(8,128)(2,1)S(1)}, u32[]{:S(2)}, u32[]{:S(2)}) %collective-permute-start.4) | collective-permute-done | bytes 393248 | tf_op jit(solution)/shard_map/ppermute | solution.py:34
  13.2 0.8 %fusion.2.codes_ref = bf16[64,256]{1,0:T(8,128)(2,1)S(1)} fusion(f32[64,256]{1,0:T(8,128)S(1)} %get-tuple-element.28, f32[64,256]{1,0:T(8,128)S(1)} %get-tuple-element.27, bf16[64,8192]{1,0:T(8,128)(2,1)S(1)} %slice_dynamic-update-slice_fusion, bf16[8192,256]{1,0:T(8,128)(2,1)S(1)} %get-tuple-element.24), kind=kOutput, calls=%fused_computation.3 | convolution fusion | flops 268500992 | bytes 5406720 | tf_op jit(solution)/shard_map/dot_general | solution.py:255
  14.1 0.8 %decode.3 = (f32[32,8192]{1,0:T(8,128)S(1)}, bf16[32,8192]{1,0:T(8,128)(2,1)S(1)}) custom-call(bf16[64,256]{1,0:T(8,128)(2,1)S(1)} %fusion.2.codes_ref, bf16[256,8192]{1,0:T(8,128)(2,1)S(1)} %get-tuple-element.33.dec_ref), custom_call_target="tpu_custom_call" | custom-call | flops 268435456 | bytes 4194304 | tf_op jit(solution)/shard_map/decode/pallas_call | solution.py:169
  14.9 0.2 collective-permute-start.8
  15.1 0.8 %decode.2 = (f32[32,8192]{1,0:T(8,128)S(1)}, bf16[32,8192]{1,0:T(8,128)(2,1)S(1)}) custom-call(bf16[64,256]{1,0:T(8,128)(2,1)S(1)} %fusion.2.codes_ref, bf16[256,8192]{1,0:T(8,128)(2,1)S(1)} %get-tuple-element.29.dec_ref), custom_call_target="tpu_custom_call" | custom-call | flops 268435456 | bytes 4194304 | tf_op jit(solution)/shard_map/decode/pallas_call | solution.py:169
  16.0 0.4 collective-permute-start.5
  16.4 0.5 collective-permute-done.8
  16.9 0.1 fusion.9
  17.0 1.6 %collective-permute-start.9 = (bf16[8,8192]{1,0:T(8,128)(2,1)S(1)}, bf16[8,8192]{1,0:T(8,128)(2,1)S(1)}, u32[]{:S(2)}, u32[]{:S(2)}) collective-permute-start(bf16[8,8192]{1,0:T(8,128)(2,1)S(1)} %get-tuple-element.50), channel_id=1, source_target_pairs={{0,8},{1,9},{2,10},{3,11},{4,12},{5,13},{6,14},{7,15},{8,16},{9,17... | collective-permute-start | bytes 393224 | tf_op jit(solution)/shard_map/ppermute | solution.py:39
  18.7 1.5 %collective-permute-start.12 = (bf16[8,8192]{1,0:T(8,128)(2,1)S(1)}, bf16[8,8192]{1,0:T(8,128)(2,1)S(1)}, u32[]{:S(2)}, u32[]{:S(2)}) collective-permute-start(bf16[8,8192]{1,0:T(8,128)(2,1)S(1)} %get-tuple-element.51), channel_id=1, source_target_pairs={{0,4},{1,3},{2,6},{3,1},{4,0},{5,7},{6,2},{7,5},{8,12},{9,11},{10,... | collective-permute-start | bytes 393224 | tf_op jit(solution)/shard_map/ppermute | solution.py:30
  20.2 1.5 %collective-permute-start.11 = (bf16[8,8192]{1,0:T(8,128)(2,1)S(1)}, bf16[8,8192]{1,0:T(8,128)(2,1)S(1)}, u32[]{:S(2)}, u32[]{:S(2)}) collective-permute-start(bf16[8,8192]{1,0:T(8,128)(2,1)S(1)} %get-tuple-element.52), channel_id=1, source_target_pairs={{0,2},{1,5},{2,0},{3,7},{4,6},{5,1},{6,4},{7,3},{8,10},{9,13},{10,... | collective-permute-start | bytes 393224 | tf_op jit(solution)/shard_map/ppermute | solution.py:30
  21.6 0.0 collective-permute-done.5
  21.6 0.1 fusion.8
  21.8 0.6 %collective-permute-start.6 = (bf16[8,8192]{1,0:T(8,128)(2,1)S(1)}, bf16[8,8192]{1,0:T(8,128)(2,1)S(1)}, u32[]{:S(2)}, u32[]{:S(2)}) collective-permute-start(bf16[8,8192]{1,0:T(8,128)(2,1)S(1)} %get-tuple-element.48), channel_id=1, source_target_pairs={{0,2},{1,5},{2,0},{3,7},{4,6},{5,1},{6,4},{7,3},{8,10},{9,13},{10,... | collective-permute-start | bytes 393224 | tf_op jit(solution)/shard_map/ppermute | solution.py:30
  22.4 0.5 %collective-permute-start.7 = (bf16[8,8192]{1,0:T(8,128)(2,1)S(1)}, bf16[8,8192]{1,0:T(8,128)(2,1)S(1)}, u32[]{:S(2)}, u32[]{:S(2)}) collective-permute-start(bf16[8,8192]{1,0:T(8,128)(2,1)S(1)} %get-tuple-element.49), channel_id=1, source_target_pairs={{0,4},{1,3},{2,6},{3,1},{4,0},{5,7},{6,2},{7,5},{8,12},{9,11},{10,... | collective-permute-start | bytes 393224 | tf_op jit(solution)/shard_map/ppermute | solution.py:30
  22.9 1.5 %collective-permute-done.9 = bf16[8,8192]{1,0:T(8,128)(2,1)S(1)} collective-permute-done((bf16[8,8192]{1,0:T(8,128)(2,1)S(1)}, bf16[8,8192]{1,0:T(8,128)(2,1)S(1)}, u32[]{:S(2)}, u32[]{:S(2)}) %collective-permute-start.9) | collective-permute-done | bytes 131104 | tf_op jit(solution)/shard_map/ppermute | solution.py:39
  24.5 2.5 %collective-permute-start.10 = (bf16[8,8192]{1,0:T(8,128)(2,1)S(1)}, bf16[8,8192]{1,0:T(8,128)(2,1)S(1)}, u32[]{:S(2)}, u32[]{:S(2)}) collective-permute-start(bf16[8,8192]{1,0:T(8,128)(2,1)S(1)} %slice_add_fusion.1), channel_id=1, source_target_pairs={{0,6},{1,7},{2,4},{3,5},{4,2},{5,3},{6,0},{7,1},{8,14},{9,15},{10,... | collective-permute-start | bytes 393224 | tf_op jit(solution)/shard_map/ppermute | solution.py:30
  27.0 0.0 collective-permute-done.12
  27.0 0.0 collective-permute-done.11
  27.1 2.7 %collective-permute-start.13 = (bf16[8,8192]{1,0:T(8,128)(2,1)S(1)}, bf16[8,8192]{1,0:T(8,128)(2,1)S(1)}, u32[]{:S(2)}, u32[]{:S(2)}) collective-permute-start(bf16[8,8192]{1,0:T(8,128)(2,1)S(1)} %convert_element_type.71), channel_id=1, source_target_pairs={{0,8},{1,9},{2,10},{3,11},{4,12},{5,13},{6,14},{7,15},{8,16},{9,17... | collective-permute-start | bytes 393224 | tf_op jit(solution)/shard_map/ppermute | solution.py:45
  29.8 0.0 collective-permute-done.6
  29.8 0.0 collective-permute-done.7
  29.8 0.9 %collective-permute-done.10 = bf16[8,8192]{1,0:T(8,128)(2,1)S(1)} collective-permute-done((bf16[8,8192]{1,0:T(8,128)(2,1)S(1)}, bf16[8,8192]{1,0:T(8,128)(2,1)S(1)}, u32[]{:S(2)}, u32[]{:S(2)}) %collective-permute-start.10) | collective-permute-done | bytes 131104 | tf_op jit(solution)/shard_map/ppermute | solution.py:30
  30.7 0.1 fusion.7
  30.8 1.3 %collective-permute-start.14 = (bf16[8,8192]{1,0:T(8,128)(2,1)S(1)}, bf16[8,8192]{1,0:T(8,128)(2,1)S(1)}, u32[]{:S(2)}, u32[]{:S(2)}) collective-permute-start(bf16[8,8192]{1,0:T(8,128)(2,1)S(1)} %fusion.7), channel_id=1, source_target_pairs={{8,0},{9,1},{10,2},{11,3},{12,4},{13,5},{14,6},{15,7},{16,8},{17,9... | collective-permute-start | bytes 393224 | tf_op jit(solution)/shard_map/ppermute | solution.py:50
  32.1 0.2 collective-permute-done.13
  32.3 0.1 constant_dynamic-update-slice_fusion.12
  32.4 0.0 copy-start.3
  32.4 1.4 %collective-permute-start.19 = (bf16[8,8192]{1,0:T(8,128)(2,1)S(1)}, bf16[8,8192]{1,0:T(8,128)(2,1)S(1)}, u32[]{:S(2)}, u32[]{:S(2)}) collective-permute-start(bf16[8,8192]{1,0:T(8,128)(2,1)S(1)} %get-tuple-element.43), channel_id=1, source_target_pairs={{0,2},{1,5},{2,0},{3,7},{4,6},{5,1},{6,4},{7,3},{8,10},{9,13},{10,... | collective-permute-start | bytes 393224 | tf_op jit(solution)/shard_map/ppermute | solution.py:30
  33.8 1.2 %collective-permute-start.18 = (bf16[8,8192]{1,0:T(8,128)(2,1)S(1)}, bf16[8,8192]{1,0:T(8,128)(2,1)S(1)}, u32[]{:S(2)}, u32[]{:S(2)}) collective-permute-start(bf16[8,8192]{1,0:T(8,128)(2,1)S(1)} %get-tuple-element.43), channel_id=1, source_target_pairs={{0,4},{1,3},{2,6},{3,1},{4,0},{5,7},{6,2},{7,5},{8,12},{9,11},{10,... | collective-permute-start | bytes 393224 | tf_op jit(solution)/shard_map/ppermute | solution.py:30
  35.0 0.9 %collective-permute-start.17 = (bf16[8,8192]{1,0:T(8,128)(2,1)S(1)}, bf16[8,8192]{1,0:T(8,128)(2,1)S(1)}, u32[]{:S(2)}, u32[]{:S(2)}) collective-permute-start(bf16[8,8192]{1,0:T(8,128)(2,1)S(1)} %get-tuple-element.43), channel_id=1, source_target_pairs={{0,6},{1,7},{2,4},{3,5},{4,2},{5,3},{6,0},{7,1},{8,14},{9,15},{10,... | collective-permute-start | bytes 393224 | tf_op jit(solution)/shard_map/ppermute | solution.py:30
  35.9 1.8 %collective-permute-done.14 = bf16[8,8192]{1,0:T(8,128)(2,1)S(1)} collective-permute-done((bf16[8,8192]{1,0:T(8,128)(2,1)S(1)}, bf16[8,8192]{1,0:T(8,128)(2,1)S(1)}, u32[]{:S(2)}, u32[]{:S(2)}) %collective-permute-start.14) | collective-permute-done | bytes 131104 | tf_op jit(solution)/shard_map/ppermute | solution.py:50
  37.8 1.5 %collective-permute-start.16 = (bf16[8,8192]{1,0:T(8,128)(2,1)S(1)}, bf16[8,8192]{1,0:T(8,128)(2,1)S(1)}, u32[]{:S(2)}, u32[]{:S(2)}) collective-permute-start(bf16[8,8192]{1,0:T(8,128)(2,1)S(1)} %select_convert_fusion), channel_id=1, source_target_pairs={{0,4},{1,3},{2,6},{3,1},{4,0},{5,7},{6,2},{7,5},{8,12},{9,11},{10,... | collective-permute-start | bytes 393224 | tf_op jit(solution)/shard_map/ppermute | solution.py:30
  39.3 1.5 %collective-permute-start.15 = (bf16[8,8192]{1,0:T(8,128)(2,1)S(1)}, bf16[8,8192]{1,0:T(8,128)(2,1)S(1)}, u32[]{:S(2)}, u32[]{:S(2)}) collective-permute-start(bf16[8,8192]{1,0:T(8,128)(2,1)S(1)} %select_convert_fusion), channel_id=1, source_target_pairs={{0,6},{1,7},{2,4},{3,5},{4,2},{5,3},{6,0},{7,1},{8,14},{9,15},{10,... | collective-permute-start | bytes 393224 | tf_op jit(solution)/shard_map/ppermute | solution.py:30
  40.7 0.0 collective-permute-done.19
  40.7 2.8 %collective-permute-start.21 = (bf16[8,8192]{1,0:T(8,128)(2,1)S(1)}, bf16[8,8192]{1,0:T(8,128)(2,1)S(1)}, u32[]{:S(2)}, u32[]{:S(2)}) collective-permute-start(bf16[8,8192]{1,0:T(8,128)(2,1)S(1)} %collective-permute-done.19), channel_id=1, source_target_pairs={{8,0},{9,1},{10,2},{11,3},{12,4},{13,5},{14,6},{15,7},{16,8},{17,9... | collective-permute-start | bytes 393224 | tf_op jit(solution)/shard_map/ppermute | solution.py:55
  43.5 0.0 collective-permute-done.18
  43.5 0.0 collective-permute-done.17
  43.6 0.1 collective-permute-start.20
  43.7 2.3 %collective-permute-done.21 = bf16[8,8192]{1,0:T(8,128)(2,1)S(1)} collective-permute-done((bf16[8,8192]{1,0:T(8,128)(2,1)S(1)}, bf16[8,8192]{1,0:T(8,128)(2,1)S(1)}, u32[]{:S(2)}, u32[]{:S(2)}) %collective-permute-start.21) | collective-permute-done | bytes 131104 | tf_op jit(solution)/shard_map/ppermute | solution.py:55
  46.1 0.1 collective-permute-start.23
  46.1 0.0 collective-permute-done.16
  46.2 0.0 collective-permute-done.15
  46.2 0.0 collective-permute-done.20
  46.2 0.5 %collective-permute-start.22 = (bf16[24,8192]{1,0:T(8,128)(2,1)S(1)}, bf16[24,8192]{1,0:T(8,128)(2,1)S(1)}, u32[]{:S(2)}, u32[]{:S(2)}) collective-permute-start(bf16[24,8192]{1,0:T(8,128)(2,1)S(1)} %pad_maximum_fusion.2), channel_id=1, source_target_pairs={{0,1},{1,0},{2,3},{3,2},{4,5},{5,4},{6,7},{7,6},{8,9},{9,8},{10,11... | collective-permute-start | bytes 1179656 | tf_op jit(solution)/shard_map/ppermute | solution.py:34
  46.8 1.4 %grad_own.1 = (f32[64,256]{1,0:T(8,128)S(1)}, f32[8,128]{1,0:T(8,128)}) custom-call(bf16[64,8192]{1,0:T(8,128)(2,1)S(1)} %constant_dynamic-update-slice_fusion.8.rows_ref, bf16[256,8192]{1,0:T(8,128)(2,1)S(1)} %get-tuple-element.29.dec_ref), custom_call_target="tpu_custom_call" | custom-call | flops 268435456 | bytes 4194304 | tf_op jit(solution)/shard_map/grad_own/pallas_call | solution.py:206
  48.2 0.0 collective-permute-done.23
  48.2 0.0 collective-permute-done.22
  48.2 0.1 pad_maximum_fusion.rows_ref
  48.3 2.0 %grad_all.1 = f32[1,64,256]{2,1,0:T(8,128)} custom-call(bf16[64,8192]{1,0:T(8,128)(2,1)S(1)} %pad_maximum_fusion.rows_ref, bf16[256,8192]{1,0:T(8,128)(2,1)S(1)} %get-tuple-element.33.dec_ref, f32[64,256]{1,0:T(8,128)S(1)} %get-tuple-element.41.own_ref), custom_call_target="tpu_custom_call" | custom-call | flops 268435456 | bytes 4194304 | tf_op jit(solution)/shard_map/grad_all/pallas_call | solution.py:218
  (31 shorter events, 0.5 us)
Async XLA Ops:
  0.6 9.4 %copy-start = (s32[1,2,2]{2,1,0:T(2,128)S(1)}, s32[1,2,2]{2,1,0:T(2,128)}, u32[]{:S(2)}) copy-start(s32[1,2,2]{2,1,0:T(2,128)} %param.9) | copy-start | bytes 52
  0.6 9.4 %copy-start.1 = (bf16[1,256]{1,0:T(2,128)(2,1)S(1)}, bf16[1,256]{1,0:T(2,128)(2,1)}, u32[]{:S(2)}) copy-start(bf16[1,256]{1,0:T(2,128)(2,1)} %bias_ref) | copy-start | bytes 1540
  0.7 10.8 %copy-start.4 = (bf16[1,8,8192]{2,1,0:T(8,128)(2,1)S(1)}, bf16[1,8,8192]{2,1,0:T(8,128)(2,1)}, u32[]{:S(2)}) copy-start(bf16[1,8,8192]{2,1,0:T(8,128)(2,1)} %param.6) | copy-start | bytes 393220
  0.7 9.5 %collective-permute-start = (bf16[8,8192]{1,0:T(8,128)(2,1)}, bf16[8,8192]{1,0:T(8,128)(2,1)S(1)}, u32[]{:S(2)}, u32[]{:S(2)}) collective-permute-start(bf16[8,8192]{1,0:T(8,128)(2,1)} %bitcast.15), channel_id=1, source_target_pairs={{0,6},{1,7},{2,4},{3,5},{4,2},{5,3},{6,0},{7,1},{8,14},{9,15},{10,... | collective-permute-start | bytes 393224 | tf_op jit(solution)/shard_map/ppermute | solution.py:30
  4.6 6.9 %collective-permute-start.3 = (bf16[8,8192]{1,0:T(8,128)(2,1)}, bf16[8,8192]{1,0:T(8,128)(2,1)S(1)}, u32[]{:S(2)}, u32[]{:S(2)}) collective-permute-start(bf16[8,8192]{1,0:T(8,128)(2,1)} %bitcast.16), channel_id=1, source_target_pairs={{0,1},{1,0},{2,3},{3,2},{4,5},{5,4},{6,7},{7,6},{8,9},{9,8},{10,11... | collective-permute-start | bytes 393224 | tf_op jit(solution)/shard_map/ppermute | solution.py:34
  4.6 6.8 %collective-permute-start.2 = (bf16[8,8192]{1,0:T(8,128)(2,1)}, bf16[8,8192]{1,0:T(8,128)(2,1)S(1)}, u32[]{:S(2)}, u32[]{:S(2)}) collective-permute-start(bf16[8,8192]{1,0:T(8,128)(2,1)} %bitcast.17), channel_id=1, source_target_pairs={{0,2},{1,5},{2,0},{3,7},{4,6},{5,1},{6,4},{7,3},{8,10},{9,13},{10,... | collective-permute-start | bytes 393224 | tf_op jit(solution)/shard_map/ppermute | solution.py:30
  5.2 6.0 %collective-permute-start.1 = (bf16[8,8192]{1,0:T(8,128)(2,1)}, bf16[8,8192]{1,0:T(8,128)(2,1)S(1)}, u32[]{:S(2)}, u32[]{:S(2)}) collective-permute-start(bf16[8,8192]{1,0:T(8,128)(2,1)} %bitcast.18), channel_id=1, source_target_pairs={{0,4},{1,3},{2,6},{3,1},{4,0},{5,7},{6,2},{7,5},{8,12},{9,11},{10,... | collective-permute-start | bytes 393224 | tf_op jit(solution)/shard_map/ppermute | solution.py:30
  11.4 1.8 %collective-permute-start.4 = (bf16[24,8192]{1,0:T(8,128)(2,1)S(1)}, bf16[24,8192]{1,0:T(8,128)(2,1)S(1)}, u32[]{:S(2)}, u32[]{:S(2)}) collective-permute-start(bf16[24,8192]{1,0:T(8,128)(2,1)S(1)} %constant_dynamic-update-slice_fusion), channel_id=1, source_target_pairs={{0,1},{1,0},{2,3},{3,2},{4,5},{5,4},{6,7},{7,6},{8,9},{9,8},{10,11... | collective-permute-start | bytes 1179656 | tf_op jit(solution)/shard_map/ppermute | solution.py:34
  14.9 2.0 %collective-permute-start.8 = (bf16[32,8192]{1,0:T(8,128)(2,1)S(1)}, bf16[32,8192]{1,0:T(8,128)(2,1)S(1)}, u32[]{:S(2)}, u32[]{:S(2)}) collective-permute-start(bf16[32,8192]{1,0:T(8,128)(2,1)S(1)} %get-tuple-element.35), channel_id=1, source_target_pairs={{0,1},{1,0},{2,3},{3,2},{4,5},{5,4},{6,7},{7,6},{8,9},{9,8},{10,11... | collective-permute-start | bytes 1572872 | tf_op jit(solution)/shard_map/ppermute | solution.py:34
  16.0 5.7 %collective-permute-start.5 = (bf16[32,8192]{1,0:T(8,128)(2,1)S(1)}, bf16[32,8192]{1,0:T(8,128)(2,1)S(1)}, u32[]{:S(2)}, u32[]{:S(2)}) collective-permute-start(bf16[32,8192]{1,0:T(8,128)(2,1)S(1)} %get-tuple-element.31), channel_id=1, source_target_pairs={{0,1},{1,0},{2,3},{3,2},{4,5},{5,4},{6,7},{7,6},{8,9},{9,8},{10,11... | collective-permute-start | bytes 1572872 | tf_op jit(solution)/shard_map/ppermute | solution.py:34
  16.9 13.8 %copy-start.2 = (bf16[1,8,8192]{2,1,0:T(8,128)(2,1)S(1)}, bf16[1,8,8192]{2,1,0:T(8,128)(2,1)}, u32[]{:S(2)}) copy-start(bf16[1,8,8192]{2,1,0:T(8,128)(2,1)} %param.11) | copy-start | bytes 393220
  17.0 7.5 %collective-permute-start.9 = (bf16[8,8192]{1,0:T(8,128)(2,1)S(1)}, bf16[8,8192]{1,0:T(8,128)(2,1)S(1)}, u32[]{:S(2)}, u32[]{:S(2)}) collective-permute-start(bf16[8,8192]{1,0:T(8,128)(2,1)S(1)} %get-tuple-element.50), channel_id=1, source_target_pairs={{0,8},{1,9},{2,10},{3,11},{4,12},{5,13},{6,14},{7,15},{8,16},{9,17... | collective-permute-start | bytes 393224 | tf_op jit(solution)/shard_map/ppermute | solution.py:39
  18.7 8.3 %collective-permute-start.12 = (bf16[8,8192]{1,0:T(8,128)(2,1)S(1)}, bf16[8,8192]{1,0:T(8,128)(2,1)S(1)}, u32[]{:S(2)}, u32[]{:S(2)}) collective-permute-start(bf16[8,8192]{1,0:T(8,128)(2,1)S(1)} %get-tuple-element.51), channel_id=1, source_target_pairs={{0,4},{1,3},{2,6},{3,1},{4,0},{5,7},{6,2},{7,5},{8,12},{9,11},{10,... | collective-permute-start | bytes 393224 | tf_op jit(solution)/shard_map/ppermute | solution.py:30
  20.2 6.9 %collective-permute-start.11 = (bf16[8,8192]{1,0:T(8,128)(2,1)S(1)}, bf16[8,8192]{1,0:T(8,128)(2,1)S(1)}, u32[]{:S(2)}, u32[]{:S(2)}) collective-permute-start(bf16[8,8192]{1,0:T(8,128)(2,1)S(1)} %get-tuple-element.52), channel_id=1, source_target_pairs={{0,2},{1,5},{2,0},{3,7},{4,6},{5,1},{6,4},{7,3},{8,10},{9,13},{10,... | collective-permute-start | bytes 393224 | tf_op jit(solution)/shard_map/ppermute | solution.py:30
  21.8 8.0 %collective-permute-start.6 = (bf16[8,8192]{1,0:T(8,128)(2,1)S(1)}, bf16[8,8192]{1,0:T(8,128)(2,1)S(1)}, u32[]{:S(2)}, u32[]{:S(2)}) collective-permute-start(bf16[8,8192]{1,0:T(8,128)(2,1)S(1)} %get-tuple-element.48), channel_id=1, source_target_pairs={{0,2},{1,5},{2,0},{3,7},{4,6},{5,1},{6,4},{7,3},{8,10},{9,13},{10,... | collective-permute-start | bytes 393224 | tf_op jit(solution)/shard_map/ppermute | solution.py:30
  22.4 7.4 %collective-permute-start.7 = (bf16[8,8192]{1,0:T(8,128)(2,1)S(1)}, bf16[8,8192]{1,0:T(8,128)(2,1)S(1)}, u32[]{:S(2)}, u32[]{:S(2)}) collective-permute-start(bf16[8,8192]{1,0:T(8,128)(2,1)S(1)} %get-tuple-element.49), channel_id=1, source_target_pairs={{0,4},{1,3},{2,6},{3,1},{4,0},{5,7},{6,2},{7,5},{8,12},{9,11},{10,... | collective-permute-start | bytes 393224 | tf_op jit(solution)/shard_map/ppermute | solution.py:30
  24.5 6.2 %collective-permute-start.10 = (bf16[8,8192]{1,0:T(8,128)(2,1)S(1)}, bf16[8,8192]{1,0:T(8,128)(2,1)S(1)}, u32[]{:S(2)}, u32[]{:S(2)}) collective-permute-start(bf16[8,8192]{1,0:T(8,128)(2,1)S(1)} %slice_add_fusion.1), channel_id=1, source_target_pairs={{0,6},{1,7},{2,4},{3,5},{4,2},{5,3},{6,0},{7,1},{8,14},{9,15},{10,... | collective-permute-start | bytes 393224 | tf_op jit(solution)/shard_map/ppermute | solution.py:30
  27.1 5.2 %collective-permute-start.13 = (bf16[8,8192]{1,0:T(8,128)(2,1)S(1)}, bf16[8,8192]{1,0:T(8,128)(2,1)S(1)}, u32[]{:S(2)}, u32[]{:S(2)}) collective-permute-start(bf16[8,8192]{1,0:T(8,128)(2,1)S(1)} %convert_element_type.71), channel_id=1, source_target_pairs={{0,8},{1,9},{2,10},{3,11},{4,12},{5,13},{6,14},{7,15},{8,16},{9,17... | collective-permute-start | bytes 393224 | tf_op jit(solution)/shard_map/ppermute | solution.py:45
  30.8 6.9 %collective-permute-start.14 = (bf16[8,8192]{1,0:T(8,128)(2,1)S(1)}, bf16[8,8192]{1,0:T(8,128)(2,1)S(1)}, u32[]{:S(2)}, u32[]{:S(2)}) collective-permute-start(bf16[8,8192]{1,0:T(8,128)(2,1)S(1)} %fusion.7), channel_id=1, source_target_pairs={{8,0},{9,1},{10,2},{11,3},{12,4},{13,5},{14,6},{15,7},{16,8},{17,9... | collective-permute-start | bytes 393224 | tf_op jit(solution)/shard_map/ppermute | solution.py:50
  32.4 15.8 %copy-start.3 = (bf16[8,8192]{1,0:T(8,128)(2,1)}, bf16[8,8192]{1,0:T(8,128)(2,1)S(1)}, u32[]{:S(2)}) copy-start(bf16[8,8192]{1,0:T(8,128)(2,1)S(1)} %get-tuple-element.43) | copy-start | bytes 393220
  32.4 8.3 %collective-permute-start.19 = (bf16[8,8192]{1,0:T(8,128)(2,1)S(1)}, bf16[8,8192]{1,0:T(8,128)(2,1)S(1)}, u32[]{:S(2)}, u32[]{:S(2)}) collective-permute-start(bf16[8,8192]{1,0:T(8,128)(2,1)S(1)} %get-tuple-element.43), channel_id=1, source_target_pairs={{0,2},{1,5},{2,0},{3,7},{4,6},{5,1},{6,4},{7,3},{8,10},{9,13},{10,... | collective-permute-start | bytes 393224 | tf_op jit(solution)/shard_map/ppermute | solution.py:30
  33.8 9.7 %collective-permute-start.18 = (bf16[8,8192]{1,0:T(8,128)(2,1)S(1)}, bf16[8,8192]{1,0:T(8,128)(2,1)S(1)}, u32[]{:S(2)}, u32[]{:S(2)}) collective-permute-start(bf16[8,8192]{1,0:T(8,128)(2,1)S(1)} %get-tuple-element.43), channel_id=1, source_target_pairs={{0,4},{1,3},{2,6},{3,1},{4,0},{5,7},{6,2},{7,5},{8,12},{9,11},{10,... | collective-permute-start | bytes 393224 | tf_op jit(solution)/shard_map/ppermute | solution.py:30
  35.0 8.5 %collective-permute-start.17 = (bf16[8,8192]{1,0:T(8,128)(2,1)S(1)}, bf16[8,8192]{1,0:T(8,128)(2,1)S(1)}, u32[]{:S(2)}, u32[]{:S(2)}) collective-permute-start(bf16[8,8192]{1,0:T(8,128)(2,1)S(1)} %get-tuple-element.43), channel_id=1, source_target_pairs={{0,6},{1,7},{2,4},{3,5},{4,2},{5,3},{6,0},{7,1},{8,14},{9,15},{10,... | collective-permute-start | bytes 393224 | tf_op jit(solution)/shard_map/ppermute | solution.py:30
  37.8 8.4 %collective-permute-start.16 = (bf16[8,8192]{1,0:T(8,128)(2,1)S(1)}, bf16[8,8192]{1,0:T(8,128)(2,1)S(1)}, u32[]{:S(2)}, u32[]{:S(2)}) collective-permute-start(bf16[8,8192]{1,0:T(8,128)(2,1)S(1)} %select_convert_fusion), channel_id=1, source_target_pairs={{0,4},{1,3},{2,6},{3,1},{4,0},{5,7},{6,2},{7,5},{8,12},{9,11},{10,... | collective-permute-start | bytes 393224 | tf_op jit(solution)/shard_map/ppermute | solution.py:30
  39.3 6.9 %collective-permute-start.15 = (bf16[8,8192]{1,0:T(8,128)(2,1)S(1)}, bf16[8,8192]{1,0:T(8,128)(2,1)S(1)}, u32[]{:S(2)}, u32[]{:S(2)}) collective-permute-start(bf16[8,8192]{1,0:T(8,128)(2,1)S(1)} %select_convert_fusion), channel_id=1, source_target_pairs={{0,6},{1,7},{2,4},{3,5},{4,2},{5,3},{6,0},{7,1},{8,14},{9,15},{10,... | collective-permute-start | bytes 393224 | tf_op jit(solution)/shard_map/ppermute | solution.py:30
  40.7 5.3 %collective-permute-start.21 = (bf16[8,8192]{1,0:T(8,128)(2,1)S(1)}, bf16[8,8192]{1,0:T(8,128)(2,1)S(1)}, u32[]{:S(2)}, u32[]{:S(2)}) collective-permute-start(bf16[8,8192]{1,0:T(8,128)(2,1)S(1)} %collective-permute-done.19), channel_id=1, source_target_pairs={{8,0},{9,1},{10,2},{11,3},{12,4},{13,5},{14,6},{15,7},{16,8},{17,9... | collective-permute-start | bytes 393224 | tf_op jit(solution)/shard_map/ppermute | solution.py:55
  43.6 2.6 %collective-permute-start.20 = (bf16[32,8192]{1,0:T(8,128)(2,1)S(1)}, bf16[32,8192]{1,0:T(8,128)(2,1)S(1)}, u32[]{:S(2)}, u32[]{:S(2)}) collective-permute-start(bf16[32,8192]{1,0:T(8,128)(2,1)S(1)} %pad_maximum_fusion.1), channel_id=1, source_target_pairs={{0,1},{1,0},{2,3},{3,2},{4,5},{5,4},{6,7},{7,6},{8,9},{9,8},{10,11... | collective-permute-start | bytes 1572872 | tf_op jit(solution)/shard_map/ppermute | solution.py:34
  46.1 2.1 %collective-permute-start.23 = (bf16[8,8192]{1,0:T(8,128)(2,1)S(1)}, bf16[8,8192]{1,0:T(8,128)(2,1)S(1)}, u32[]{:S(2)}, u32[]{:S(2)}) collective-permute-start(bf16[8,8192]{1,0:T(8,128)(2,1)S(1)} %broadcast_select_fusion), channel_id=1, source_target_pairs={{0,1},{1,0},{2,3},{3,2},{4,5},{5,4},{6,7},{7,6},{8,9},{9,8},{10,11... | collective-permute-start | bytes 393224 | tf_op jit(solution)/shard_map/ppermute | solution.py:34
  46.2 2.0 %collective-permute-start.22 = (bf16[24,8192]{1,0:T(8,128)(2,1)S(1)}, bf16[24,8192]{1,0:T(8,128)(2,1)S(1)}, u32[]{:S(2)}, u32[]{:S(2)}) collective-permute-start(bf16[24,8192]{1,0:T(8,128)(2,1)S(1)} %pad_maximum_fusion.2), channel_id=1, source_target_pairs={{0,1},{1,0},{2,3},{3,2},{4,5},{5,4},{6,7},{7,6},{8,9},{9,8},{10,11... | collective-permute-start | bytes 1179656 | tf_op jit(solution)/shard_map/ppermute | solution.py:34

commit v20 on v19

--- a/solution.py
+++ b/solution.py
@@ -195,7 +195,8 @@
     group = total.shape[0] // tokens
     for block in range(group):
         chips = group // CORES
-        label = (chips - block % chips) % chips
+        row = block % chips
+        label = row % (chips - 1) + 1 if row else 0
         slab = slab_of(place_in(group), block // chips * chips + label, chips)
         where = pl.ds(pl.multiple_of(slab * tokens, tokens), tokens)
         out_ref[0, where, :] = total[block * tokens : (block + 1) * tokens]
@@ -259,23 +260,23 @@
 
     nexts = blocks_of(next_near, next_far, chips)
     owns = blocks_of(own_near, own_far, chips)
-    risen = raised(nexts[-1].astype(jnp.bfloat16), first, group)
-    owns[-1] = owns[-1] + risen.astype(jnp.float32)
-    crossed = across(owns[-1].astype(jnp.bfloat16), chips - 1, chips).astype(jnp.float32)
-    next_sum = after(summed(nexts, range(1, chips - 1)), owns[-1])
-    own_less = summed(owns, range(1, chips - 1)) - target[0].astype(jnp.float32) + crossed
+    risen = raised(nexts[1].astype(jnp.bfloat16), first, group)
+    owns[1] = owns[1] + risen.astype(jnp.float32)
+    crossed = across(owns[1].astype(jnp.bfloat16), 1, chips).astype(jnp.float32)
+    next_sum = after(summed(nexts, range(2, chips)), owns[1])
+    own_less = summed(owns, range(2, chips)) - target[0].astype(jnp.float32) + crossed
 
     below = shifted(next_sum.astype(jnp.bfloat16), group).astype(jnp.float32)
     above = lowered(own_less.astype(jnp.bfloat16), group).astype(jnp.float32)
     error = (own_less + below).astype(jnp.bfloat16)
     later = jnp.where(final, 0.0, next_sum + after(above, error)).astype(jnp.bfloat16)
 
-    heres = [error] + [across(error, chip, chips) for chip in range(chips - 1, 0, -1)]
+    heres = [error] + [across(error, chip, chips) for chip in [*range(2, chips), 1]]
     passed = rotated_down(after(heres[-1], later), final, group)
     here_near = jnp.concatenate(heres, axis=0)
     here_far = other_core(here_near)
     here_rows = jnp.concatenate([here_near, here_far], axis=0)
-    straight = [across(later, chip, chips) for chip in range(chips - 1, 1, -1)]
+    straight = [across(later, chip, chips) for chip in range(2, chips)]
     most = after(jnp.concatenate([later] + straight, axis=0), here_far)
     after_rows = jnp.concatenate([most, passed, other_core(most), other_core(passed)], axis=0)
     grad = grad_all(after_rows, next_dec, grad_own(here_rows, own_dec), tokens)

time: 50.5 us -> 53.1 us (1.051)
  starting transfers between devices: 27.6 us -> 31.4 us
  waiting for transfers between devices: 10 us -> 8.84 us
    ppermute x1, starting transfers between devices: 2.7 us -> 7.32 us  [shifted(): lax.ppermute(value, AXIS, [(i, i + group) for i in range(size - group)])]
    ppermute x13, starting transfers between devices: 17.8 us -> 15.8 us  [across(): return lax.ppermute(value, AXIS, pairs)]
    ppermute x1, starting transfers between devices: 2.8 us -> 4 us  [rotated_down(): lax.ppermute(value, AXIS, [((i + group) % size, i) for i in range(size)])]
    ppermute x1, waiting for transfers between devices: 1.77 us -> 0.83 us  [lowered(): lax.ppermute(value, AXIS, [(i + group, i) for i in range(size - group)])]
    ppermute x1, waiting for transfers between devices: 1.54 us -> 0.64 us  [raised(): lax.ppermute(value, AXIS, [(i, (i + group) % size) for i in range(size)])]
    ppermute x1, waiting for transfers between devices: 0.19 us -> 1.07 us  [shifted(): lax.ppermute(value, AXIS, [(i, i + group) for i in range(size - group)])]
  transfers between devices with their start and end apart: 24 -> 24, of which waited for: 9 -> 10; matrix products, arithmetic and copies ran while one was open for 2% -> 2% of each run, Pallas kernels for 14% -> 13%
where the time goes in v20:
time: 53.1 us; the launch traced here: 53 us
  starting transfers between devices  31.4 us (59%)
  Pallas kernels  9.89 us (19%)
  waiting for transfers between devices  8.84 us (17%)
  between operations  1.08 us (2%)
  matrix products  0.8 us (2%)
  other arithmetic  0.69 us (1%)
    ppermute x13, starting transfers between devices, across(): return lax.ppermute(value, AXIS, pairs)  15.8 us
    ppermute x1, starting transfers between devices, shifted(): lax.ppermute(value, AXIS, [(i, i + group) for i in range(size - group)])  7.32 us
    pallas_call x1, Pallas kernels, loaded(): pl.pallas_call(load_kernel, out_shape=[pltpu.VMEM(enc.shape[1:], enc.dtyp...  4.68 us
    ppermute x1, starting transfers between devices, rotated_down(): lax.ppermute(value, AXIS, [((i + group) % size, i) for i in range(size)])  4 us
    ppermute x13, waiting for transfers between devices, across(): return lax.ppermute(value, AXIS, pairs)  2.26 us
    ppermute x7, waiting for transfers between devices, other_core(): lax.ppermute(value, AXIS, [(i, i ^ 1) for i in range(lax.axis_size(AXIS))])  2.1 us
    pallas_call x1, Pallas kernels, grad_all(): pl.pallas_call(functools.partial(grad_all_kernel, tokens), out_shape=jax....  2.03 us
    ppermute x1, waiting for transfers between devices, rotated_down(): lax.ppermute(value, AXIS, [((i + group) % size, i) for i in range(size)])  1.95 us
  transfers between devices with their start and end apart: 24, of which 10 were waited for; matrix products, arithmetic and copies ran while one was open for 2% of the time, Pallas kernels for 13%

profile of v20, /device:TPU:0, one launch (start us, length us, event | category | flops | bytes accessed | tf_op | source)
XLA Modules:
  0.0 53.0 jit_solution(9173015399843649614)
XLA Ops:
  0.6 0.0 copy-start
  0.6 0.0 copy-start.1
  0.7 4.0 %collective-permute-start = (bf16[8,8192]{1,0:T(8,128)(2,1)}, bf16[8,8192]{1,0:T(8,128)(2,1)S(1)}, u32[]{:S(2)}, u32[]{:S(2)}) collective-permute-start(bf16[8,8192]{1,0:T(8,128)(2,1)} %bitcast.15), channel_id=1, source_target_pairs={{0,6},{1,7},{2,4},{3,5},{4,2},{5,3},{6,0},{7,1},{8,14},{9,15},{10,... | collective-permute-start | bytes 393224 | tf_op jit(solution)/shard_map/ppermute | solution.py:30
  4.6 0.0 collective-permute-start.3
  4.6 0.5 %collective-permute-start.2 = (bf16[8,8192]{1,0:T(8,128)(2,1)}, bf16[8,8192]{1,0:T(8,128)(2,1)S(1)}, u32[]{:S(2)}, u32[]{:S(2)}) collective-permute-start(bf16[8,8192]{1,0:T(8,128)(2,1)} %bitcast.17), channel_id=1, source_target_pairs={{0,2},{1,5},{2,0},{3,7},{4,6},{5,1},{6,4},{7,3},{8,10},{9,13},{10,... | collective-permute-start | bytes 393224 | tf_op jit(solution)/shard_map/ppermute | solution.py:30
  5.2 0.2 collective-permute-start.1
  5.3 4.7 %load_weights.1 = (bf16[8192,256]{1,0:T(8,128)(2,1)S(1)}, bf16[256,8192]{1,0:T(8,128)(2,1)S(1)}, bf16[256,8192]{1,0:T(8,128)(2,1)S(1)}) custom-call(bf16[1,8192,256]{2,1,0:T(8,128)(2,1)} %enc_hbm.1, bf16[1,2,256,8192]{3,2,1,0:T(8,128)(2,1)} %dec_hbm.1), custom_call_target="tpu_custom_call" | custom-call | bytes 25165824 | tf_op jit(solution)/shard_map/load_weights/pallas_call | solution.py:92
  10.1 0.1 gate.1
  10.2 0.0 collective-permute-done
  10.2 0.9 %collective-permute-done.1 = bf16[8,8192]{1,0:T(8,128)(2,1)S(1)} collective-permute-done((bf16[8,8192]{1,0:T(8,128)(2,1)}, bf16[8,8192]{1,0:T(8,128)(2,1)S(1)}, u32[]{:S(2)}, u32[]{:S(2)}) %collective-permute-start.1) | collective-permute-done | bytes 131104 | tf_op jit(solution)/shard_map/ppermute | solution.py:30
  11.2 0.2 collective-permute-done.2
  11.4 0.1 collective-permute-start.4
  11.6 0.0 collective-permute-done.3
  11.6 1.6 %collective-permute-done.4 = bf16[24,8192]{1,0:T(8,128)(2,1)S(1)} collective-permute-done((bf16[24,8192]{1,0:T(8,128)(2,1)S(1)}, bf16[24,8192]{1,0:T(8,128)(2,1)S(1)}, u32[]{:S(2)}, u32[]{:S(2)}) %collective-permute-start.4) | collective-permute-done | bytes 393248 | tf_op jit(solution)/shard_map/ppermute | solution.py:34
  13.2 0.8 %fusion.2.codes_ref = bf16[64,256]{1,0:T(8,128)(2,1)S(1)} fusion(f32[64,256]{1,0:T(8,128)S(1)} %get-tuple-element.28, f32[64,256]{1,0:T(8,128)S(1)} %get-tuple-element.27, bf16[64,8192]{1,0:T(8,128)(2,1)S(1)} %slice_dynamic-update-slice_fusion, bf16[8192,256]{1,0:T(8,128)(2,1)S(1)} %get-tuple-element.24), kind=kOutput, calls=%fused_computation.3 | convolution fusion | flops 268500992 | bytes 5406720 | tf_op jit(solution)/shard_map/dot_general | solution.py:256
  14.1 0.8 %decode.3 = (f32[32,8192]{1,0:T(8,128)S(1)}, bf16[32,8192]{1,0:T(8,128)(2,1)S(1)}) custom-call(bf16[64,256]{1,0:T(8,128)(2,1)S(1)} %fusion.2.codes_ref, bf16[256,8192]{1,0:T(8,128)(2,1)S(1)} %get-tuple-element.33.dec_ref), custom_call_target="tpu_custom_call" | custom-call | flops 268435456 | bytes 4194304 | tf_op jit(solution)/shard_map/decode/pallas_call | solution.py:169
  14.9 0.2 collective-permute-start.8
  15.1 0.8 %decode.2 = (f32[32,8192]{1,0:T(8,128)S(1)}, bf16[32,8192]{1,0:T(8,128)(2,1)S(1)}) custom-call(bf16[64,256]{1,0:T(8,128)(2,1)S(1)} %fusion.2.codes_ref, bf16[256,8192]{1,0:T(8,128)(2,1)S(1)} %get-tuple-element.29.dec_ref), custom_call_target="tpu_custom_call" | custom-call | flops 268435456 | bytes 4194304 | tf_op jit(solution)/shard_map/decode/pallas_call | solution.py:169
  16.0 0.4 collective-permute-start.5
  16.4 0.5 collective-permute-done.8
  16.9 0.1 fusion.9
  17.0 1.6 %collective-permute-start.9 = (bf16[8,8192]{1,0:T(8,128)(2,1)S(1)}, bf16[8,8192]{1,0:T(8,128)(2,1)S(1)}, u32[]{:S(2)}, u32[]{:S(2)}) collective-permute-start(bf16[8,8192]{1,0:T(8,128)(2,1)S(1)} %get-tuple-element.50), channel_id=1, source_target_pairs={{0,8},{1,9},{2,10},{3,11},{4,12},{5,13},{6,14},{7,15},{8,16},{9,17... | collective-permute-start | bytes 393224 | tf_op jit(solution)/shard_map/ppermute | solution.py:39
  18.7 2.4 %collective-permute-start.12 = (bf16[8,8192]{1,0:T(8,128)(2,1)S(1)}, bf16[8,8192]{1,0:T(8,128)(2,1)S(1)}, u32[]{:S(2)}, u32[]{:S(2)}) collective-permute-start(bf16[8,8192]{1,0:T(8,128)(2,1)S(1)} %get-tuple-element.51), channel_id=1, source_target_pairs={{0,6},{1,7},{2,4},{3,5},{4,2},{5,3},{6,0},{7,1},{8,14},{9,15},{10,... | collective-permute-start | bytes 393224 | tf_op jit(solution)/shard_map/ppermute | solution.py:30
  21.1 0.5 %collective-permute-start.11 = (bf16[8,8192]{1,0:T(8,128)(2,1)S(1)}, bf16[8,8192]{1,0:T(8,128)(2,1)S(1)}, u32[]{:S(2)}, u32[]{:S(2)}) collective-permute-start(bf16[8,8192]{1,0:T(8,128)(2,1)S(1)} %get-tuple-element.52), channel_id=1, source_target_pairs={{0,4},{1,3},{2,6},{3,1},{4,0},{5,7},{6,2},{7,5},{8,12},{9,11},{10,... | collective-permute-start | bytes 393224 | tf_op jit(solution)/shard_map/ppermute | solution.py:30
  21.6 0.0 collective-permute-done.5
  21.6 0.1 fusion.8
  21.8 1.6 %collective-permute-start.6 = (bf16[8,8192]{1,0:T(8,128)(2,1)S(1)}, bf16[8,8192]{1,0:T(8,128)(2,1)S(1)}, u32[]{:S(2)}, u32[]{:S(2)}) collective-permute-start(bf16[8,8192]{1,0:T(8,128)(2,1)S(1)} %get-tuple-element.48), channel_id=1, source_target_pairs={{0,4},{1,3},{2,6},{3,1},{4,0},{5,7},{6,2},{7,5},{8,12},{9,11},{10,... | collective-permute-start | bytes 393224 | tf_op jit(solution)/shard_map/ppermute | solution.py:30
  23.3 0.5 collective-permute-start.7
  23.8 0.6 %collective-permute-done.9 = bf16[8,8192]{1,0:T(8,128)(2,1)S(1)} collective-permute-done((bf16[8,8192]{1,0:T(8,128)(2,1)S(1)}, bf16[8,8192]{1,0:T(8,128)(2,1)S(1)}, u32[]{:S(2)}, u32[]{:S(2)}) %collective-permute-start.9) | collective-permute-done | bytes 131104 | tf_op jit(solution)/shard_map/ppermute | solution.py:39
  24.5 1.6 %collective-permute-start.10 = (bf16[8,8192]{1,0:T(8,128)(2,1)S(1)}, bf16[8,8192]{1,0:T(8,128)(2,1)S(1)}, u32[]{:S(2)}, u32[]{:S(2)}) collective-permute-start(bf16[8,8192]{1,0:T(8,128)(2,1)S(1)} %slice_add_fusion.1), channel_id=1, source_target_pairs={{0,2},{1,5},{2,0},{3,7},{4,6},{5,1},{6,4},{7,3},{8,10},{9,13},{10,... | collective-permute-start | bytes 393224 | tf_op jit(solution)/shard_map/ppermute | solution.py:30
  26.1 0.0 collective-permute-done.12
  26.1 0.7 %collective-permute-done.11 = bf16[8,8192]{1,0:T(8,128)(2,1)S(1)} collective-permute-done((bf16[8,8192]{1,0:T(8,128)(2,1)S(1)}, bf16[8,8192]{1,0:T(8,128)(2,1)S(1)}, u32[]{:S(2)}, u32[]{:S(2)}) %collective-permute-start.11) | collective-permute-done | bytes 131104 | tf_op jit(solution)/shard_map/ppermute | solution.py:30
  26.8 7.3 %collective-permute-start.13 = (bf16[8,8192]{1,0:T(8,128)(2,1)S(1)}, bf16[8,8192]{1,0:T(8,128)(2,1)S(1)}, u32[]{:S(2)}, u32[]{:S(2)}) collective-permute-start(bf16[8,8192]{1,0:T(8,128)(2,1)S(1)} %convert_element_type.71), channel_id=1, source_target_pairs={{0,8},{1,9},{2,10},{3,11},{4,12},{5,13},{6,14},{7,15},{8,16},{9,17... | collective-permute-start | bytes 393224 | tf_op jit(solution)/shard_map/ppermute | solution.py:45
  34.1 0.0 collective-permute-done.6
  34.2 0.0 collective-permute-done.7
  34.2 0.0 collective-permute-done.10
  34.2 0.1 fusion.7
  34.3 1.3 %collective-permute-start.14 = (bf16[8,8192]{1,0:T(8,128)(2,1)S(1)}, bf16[8,8192]{1,0:T(8,128)(2,1)S(1)}, u32[]{:S(2)}, u32[]{:S(2)}) collective-permute-start(bf16[8,8192]{1,0:T(8,128)(2,1)S(1)} %fusion.7), channel_id=1, source_target_pairs={{8,0},{9,1},{10,2},{11,3},{12,4},{13,5},{14,6},{15,7},{16,8},{17,9... | collective-permute-start | bytes 393224 | tf_op jit(solution)/shard_map/ppermute | solution.py:50
  35.6 1.1 %collective-permute-done.13 = bf16[8,8192]{1,0:T(8,128)(2,1)S(1)} collective-permute-done((bf16[8,8192]{1,0:T(8,128)(2,1)S(1)}, bf16[8,8192]{1,0:T(8,128)(2,1)S(1)}, u32[]{:S(2)}, u32[]{:S(2)}) %collective-permute-start.13) | collective-permute-done | bytes 131104 | tf_op jit(solution)/shard_map/ppermute | solution.py:45
  36.6 0.1 constant_dynamic-update-slice_fusion.12
  36.7 0.0 copy-start.3
  36.8 0.1 collective-permute-start.19
  36.8 0.1 collective-permute-start.18
  36.9 3.4 %collective-permute-start.17 = (bf16[8,8192]{1,0:T(8,128)(2,1)S(1)}, bf16[8,8192]{1,0:T(8,128)(2,1)S(1)}, u32[]{:S(2)}, u32[]{:S(2)}) collective-permute-start(bf16[8,8192]{1,0:T(8,128)(2,1)S(1)} %get-tuple-element.43), channel_id=1, source_target_pairs={{0,4},{1,3},{2,6},{3,1},{4,0},{5,7},{6,2},{7,5},{8,12},{9,11},{10,... | collective-permute-start | bytes 393224 | tf_op jit(solution)/shard_map/ppermute | solution.py:30
  40.3 0.8 %collective-permute-done.14 = bf16[8,8192]{1,0:T(8,128)(2,1)S(1)} collective-permute-done((bf16[8,8192]{1,0:T(8,128)(2,1)S(1)}, bf16[8,8192]{1,0:T(8,128)(2,1)S(1)}, u32[]{:S(2)}, u32[]{:S(2)}) %collective-permute-start.14) | collective-permute-done | bytes 131104 | tf_op jit(solution)/shard_map/ppermute | solution.py:50
  41.2 0.4 collective-permute-start.16
  41.6 0.6 %collective-permute-start.15 = (bf16[8,8192]{1,0:T(8,128)(2,1)S(1)}, bf16[8,8192]{1,0:T(8,128)(2,1)S(1)}, u32[]{:S(2)}, u32[]{:S(2)}) collective-permute-start(bf16[8,8192]{1,0:T(8,128)(2,1)S(1)} %select_convert_fusion), channel_id=1, source_target_pairs={{0,4},{1,3},{2,6},{3,1},{4,0},{5,7},{6,2},{7,5},{8,12},{9,11},{10,... | collective-permute-start | bytes 393224 | tf_op jit(solution)/shard_map/ppermute | solution.py:30
  42.2 0.0 collective-permute-done.19
  42.2 4.0 %collective-permute-start.21 = (bf16[8,8192]{1,0:T(8,128)(2,1)S(1)}, bf16[8,8192]{1,0:T(8,128)(2,1)S(1)}, u32[]{:S(2)}, u32[]{:S(2)}) collective-permute-start(bf16[8,8192]{1,0:T(8,128)(2,1)S(1)} %collective-permute-done.19), channel_id=1, source_target_pairs={{8,0},{9,1},{10,2},{11,3},{12,4},{13,5},{14,6},{15,7},{16,8},{17,9... | collective-permute-start | bytes 393224 | tf_op jit(solution)/shard_map/ppermute | solution.py:55
  46.2 0.0 collective-permute-done.18
  46.2 0.4 collective-permute-done.17
  46.6 0.1 collective-permute-start.20
  46.7 1.9 %collective-permute-done.21 = bf16[8,8192]{1,0:T(8,128)(2,1)S(1)} collective-permute-done((bf16[8,8192]{1,0:T(8,128)(2,1)S(1)}, bf16[8,8192]{1,0:T(8,128)(2,1)S(1)}, u32[]{:S(2)}, u32[]{:S(2)}) %collective-permute-start.21) | collective-permute-done | bytes 131104 | tf_op jit(solution)/shard_map/ppermute | solution.py:55
  48.7 0.1 collective-permute-start.23
  48.8 0.0 collective-permute-done.16
  48.8 0.0 collective-permute-done.15
  48.8 0.0 collective-permute-done.20
  48.8 0.5 %collective-permute-start.22 = (bf16[24,8192]{1,0:T(8,128)(2,1)S(1)}, bf16[24,8192]{1,0:T(8,128)(2,1)S(1)}, u32[]{:S(2)}, u32[]{:S(2)}) collective-permute-start(bf16[24,8192]{1,0:T(8,128)(2,1)S(1)} %pad_maximum_fusion.2), channel_id=1, source_target_pairs={{0,1},{1,0},{2,3},{3,2},{4,5},{5,4},{6,7},{7,6},{8,9},{9,8},{10,11... | collective-permute-start | bytes 1179656 | tf_op jit(solution)/shard_map/ppermute | solution.py:34
  49.4 1.4 %grad_own.1 = (f32[64,256]{1,0:T(8,128)S(1)}, f32[8,128]{1,0:T(8,128)}) custom-call(bf16[64,8192]{1,0:T(8,128)(2,1)S(1)} %constant_dynamic-update-slice_fusion.8.rows_ref, bf16[256,8192]{1,0:T(8,128)(2,1)S(1)} %get-tuple-element.29.dec_ref), custom_call_target="tpu_custom_call" | custom-call | flops 268435456 | bytes 4194304 | tf_op jit(solution)/shard_map/grad_own/pallas_call | solution.py:207
  50.8 0.0 copy-done.3
  50.8 0.0 collective-permute-done.23
  50.8 0.0 collective-permute-done.22
  50.9 0.1 pad_maximum_fusion.rows_ref
  50.9 2.0 %grad_all.1 = f32[1,64,256]{2,1,0:T(8,128)} custom-call(bf16[64,8192]{1,0:T(8,128)(2,1)S(1)} %pad_maximum_fusion.rows_ref, bf16[256,8192]{1,0:T(8,128)(2,1)S(1)} %get-tuple-element.33.dec_ref, f32[64,256]{1,0:T(8,128)S(1)} %get-tuple-element.41.own_ref), custom_call_target="tpu_custom_call" | custom-call | flops 268435456 | bytes 4194304 | tf_op jit(solution)/shard_map/grad_all/pallas_call | solution.py:219
  (31 shorter events, 0.5 us)
Async XLA Ops:
  0.6 9.4 %copy-start = (s32[1,2,2]{2,1,0:T(2,128)S(1)}, s32[1,2,2]{2,1,0:T(2,128)}, u32[]{:S(2)}) copy-start(s32[1,2,2]{2,1,0:T(2,128)} %param.9) | copy-start | bytes 52
  0.6 9.4 %copy-start.1 = (bf16[1,256]{1,0:T(2,128)(2,1)S(1)}, bf16[1,256]{1,0:T(2,128)(2,1)}, u32[]{:S(2)}) copy-start(bf16[1,256]{1,0:T(2,128)(2,1)} %bias_ref) | copy-start | bytes 1540
  0.7 10.8 %copy-start.4 = (bf16[1,8,8192]{2,1,0:T(8,128)(2,1)S(1)}, bf16[1,8,8192]{2,1,0:T(8,128)(2,1)}, u32[]{:S(2)}) copy-start(bf16[1,8,8192]{2,1,0:T(8,128)(2,1)} %param.6) | copy-start | bytes 393220
  0.7 9.5 %collective-permute-start = (bf16[8,8192]{1,0:T(8,128)(2,1)}, bf16[8,8192]{1,0:T(8,128)(2,1)S(1)}, u32[]{:S(2)}, u32[]{:S(2)}) collective-permute-start(bf16[8,8192]{1,0:T(8,128)(2,1)} %bitcast.15), channel_id=1, source_target_pairs={{0,6},{1,7},{2,4},{3,5},{4,2},{5,3},{6,0},{7,1},{8,14},{9,15},{10,... | collective-permute-start | bytes 393224 | tf_op jit(solution)/shard_map/ppermute | solution.py:30
  4.6 6.9 %collective-permute-start.3 = (bf16[8,8192]{1,0:T(8,128)(2,1)}, bf16[8,8192]{1,0:T(8,128)(2,1)S(1)}, u32[]{:S(2)}, u32[]{:S(2)}) collective-permute-start(bf16[8,8192]{1,0:T(8,128)(2,1)} %bitcast.16), channel_id=1, source_target_pairs={{0,1},{1,0},{2,3},{3,2},{4,5},{5,4},{6,7},{7,6},{8,9},{9,8},{10,11... | collective-permute-start | bytes 393224 | tf_op jit(solution)/shard_map/ppermute | solution.py:34
  4.6 6.8 %collective-permute-start.2 = (bf16[8,8192]{1,0:T(8,128)(2,1)}, bf16[8,8192]{1,0:T(8,128)(2,1)S(1)}, u32[]{:S(2)}, u32[]{:S(2)}) collective-permute-start(bf16[8,8192]{1,0:T(8,128)(2,1)} %bitcast.17), channel_id=1, source_target_pairs={{0,2},{1,5},{2,0},{3,7},{4,6},{5,1},{6,4},{7,3},{8,10},{9,13},{10,... | collective-permute-start | bytes 393224 | tf_op jit(solution)/shard_map/ppermute | solution.py:30
  5.2 6.0 %collective-permute-start.1 = (bf16[8,8192]{1,0:T(8,128)(2,1)}, bf16[8,8192]{1,0:T(8,128)(2,1)S(1)}, u32[]{:S(2)}, u32[]{:S(2)}) collective-permute-start(bf16[8,8192]{1,0:T(8,128)(2,1)} %bitcast.18), channel_id=1, source_target_pairs={{0,4},{1,3},{2,6},{3,1},{4,0},{5,7},{6,2},{7,5},{8,12},{9,11},{10,... | collective-permute-start | bytes 393224 | tf_op jit(solution)/shard_map/ppermute | solution.py:30
  11.4 1.8 %collective-permute-start.4 = (bf16[24,8192]{1,0:T(8,128)(2,1)S(1)}, bf16[24,8192]{1,0:T(8,128)(2,1)S(1)}, u32[]{:S(2)}, u32[]{:S(2)}) collective-permute-start(bf16[24,8192]{1,0:T(8,128)(2,1)S(1)} %constant_dynamic-update-slice_fusion), channel_id=1, source_target_pairs={{0,1},{1,0},{2,3},{3,2},{4,5},{5,4},{6,7},{7,6},{8,9},{9,8},{10,11... | collective-permute-start | bytes 1179656 | tf_op jit(solution)/shard_map/ppermute | solution.py:34
  14.9 2.0 %collective-permute-start.8 = (bf16[32,8192]{1,0:T(8,128)(2,1)S(1)}, bf16[32,8192]{1,0:T(8,128)(2,1)S(1)}, u32[]{:S(2)}, u32[]{:S(2)}) collective-permute-start(bf16[32,8192]{1,0:T(8,128)(2,1)S(1)} %get-tuple-element.35), channel_id=1, source_target_pairs={{0,1},{1,0},{2,3},{3,2},{4,5},{5,4},{6,7},{7,6},{8,9},{9,8},{10,11... | collective-permute-start | bytes 1572872 | tf_op jit(solution)/shard_map/ppermute | solution.py:34
  16.0 5.7 %collective-permute-start.5 = (bf16[32,8192]{1,0:T(8,128)(2,1)S(1)}, bf16[32,8192]{1,0:T(8,128)(2,1)S(1)}, u32[]{:S(2)}, u32[]{:S(2)}) collective-permute-start(bf16[32,8192]{1,0:T(8,128)(2,1)S(1)} %get-tuple-element.31), channel_id=1, source_target_pairs={{0,1},{1,0},{2,3},{3,2},{4,5},{5,4},{6,7},{7,6},{8,9},{9,8},{10,11... | collective-permute-start | bytes 1572872 | tf_op jit(solution)/shard_map/ppermute | solution.py:34
  16.9 17.3 %copy-start.2 = (bf16[1,8,8192]{2,1,0:T(8,128)(2,1)S(1)}, bf16[1,8,8192]{2,1,0:T(8,128)(2,1)}, u32[]{:S(2)}) copy-start(bf16[1,8,8192]{2,1,0:T(8,128)(2,1)} %param.11) | copy-start | bytes 393220
  17.0 7.5 %collective-permute-start.9 = (bf16[8,8192]{1,0:T(8,128)(2,1)S(1)}, bf16[8,8192]{1,0:T(8,128)(2,1)S(1)}, u32[]{:S(2)}, u32[]{:S(2)}) collective-permute-start(bf16[8,8192]{1,0:T(8,128)(2,1)S(1)} %get-tuple-element.50), channel_id=1, source_target_pairs={{0,8},{1,9},{2,10},{3,11},{4,12},{5,13},{6,14},{7,15},{8,16},{9,17... | collective-permute-start | bytes 393224 | tf_op jit(solution)/shard_map/ppermute | solution.py:39
  18.7 7.4 %collective-permute-start.12 = (bf16[8,8192]{1,0:T(8,128)(2,1)S(1)}, bf16[8,8192]{1,0:T(8,128)(2,1)S(1)}, u32[]{:S(2)}, u32[]{:S(2)}) collective-permute-start(bf16[8,8192]{1,0:T(8,128)(2,1)S(1)} %get-tuple-element.51), channel_id=1, source_target_pairs={{0,6},{1,7},{2,4},{3,5},{4,2},{5,3},{6,0},{7,1},{8,14},{9,15},{10,... | collective-permute-start | bytes 393224 | tf_op jit(solution)/shard_map/ppermute | solution.py:30
  21.1 5.7 %collective-permute-start.11 = (bf16[8,8192]{1,0:T(8,128)(2,1)S(1)}, bf16[8,8192]{1,0:T(8,128)(2,1)S(1)}, u32[]{:S(2)}, u32[]{:S(2)}) collective-permute-start(bf16[8,8192]{1,0:T(8,128)(2,1)S(1)} %get-tuple-element.52), channel_id=1, source_target_pairs={{0,4},{1,3},{2,6},{3,1},{4,0},{5,7},{6,2},{7,5},{8,12},{9,11},{10,... | collective-permute-start | bytes 393224 | tf_op jit(solution)/shard_map/ppermute | solution.py:30
  21.8 12.4 %collective-permute-start.6 = (bf16[8,8192]{1,0:T(8,128)(2,1)S(1)}, bf16[8,8192]{1,0:T(8,128)(2,1)S(1)}, u32[]{:S(2)}, u32[]{:S(2)}) collective-permute-start(bf16[8,8192]{1,0:T(8,128)(2,1)S(1)} %get-tuple-element.48), channel_id=1, source_target_pairs={{0,4},{1,3},{2,6},{3,1},{4,0},{5,7},{6,2},{7,5},{8,12},{9,11},{10,... | collective-permute-start | bytes 393224 | tf_op jit(solution)/shard_map/ppermute | solution.py:30
  23.3 10.8 %collective-permute-start.7 = (bf16[8,8192]{1,0:T(8,128)(2,1)S(1)}, bf16[8,8192]{1,0:T(8,128)(2,1)S(1)}, u32[]{:S(2)}, u32[]{:S(2)}) collective-permute-start(bf16[8,8192]{1,0:T(8,128)(2,1)S(1)} %get-tuple-element.49), channel_id=1, source_target_pairs={{0,6},{1,7},{2,4},{3,5},{4,2},{5,3},{6,0},{7,1},{8,14},{9,15},{10,... | collective-permute-start | bytes 393224 | tf_op jit(solution)/shard_map/ppermute | solution.py:30
  24.5 9.6 %collective-permute-start.10 = (bf16[8,8192]{1,0:T(8,128)(2,1)S(1)}, bf16[8,8192]{1,0:T(8,128)(2,1)S(1)}, u32[]{:S(2)}, u32[]{:S(2)}) collective-permute-start(bf16[8,8192]{1,0:T(8,128)(2,1)S(1)} %slice_add_fusion.1), channel_id=1, source_target_pairs={{0,2},{1,5},{2,0},{3,7},{4,6},{5,1},{6,4},{7,3},{8,10},{9,13},{10,... | collective-permute-start | bytes 393224 | tf_op jit(solution)/shard_map/ppermute | solution.py:30
  26.8 9.8 %collective-permute-start.13 = (bf16[8,8192]{1,0:T(8,128)(2,1)S(1)}, bf16[8,8192]{1,0:T(8,128)(2,1)S(1)}, u32[]{:S(2)}, u32[]{:S(2)}) collective-permute-start(bf16[8,8192]{1,0:T(8,128)(2,1)S(1)} %convert_element_type.71), channel_id=1, source_target_pairs={{0,8},{1,9},{2,10},{3,11},{4,12},{5,13},{6,14},{7,15},{8,16},{9,17... | collective-permute-start | bytes 393224 | tf_op jit(solution)/shard_map/ppermute | solution.py:45
  34.3 6.9 %collective-permute-start.14 = (bf16[8,8192]{1,0:T(8,128)(2,1)S(1)}, bf16[8,8192]{1,0:T(8,128)(2,1)S(1)}, u32[]{:S(2)}, u32[]{:S(2)}) collective-permute-start(bf16[8,8192]{1,0:T(8,128)(2,1)S(1)} %fusion.7), channel_id=1, source_target_pairs={{8,0},{9,1},{10,2},{11,3},{12,4},{13,5},{14,6},{15,7},{16,8},{17,9... | collective-permute-start | bytes 393224 | tf_op jit(solution)/shard_map/ppermute | solution.py:50
  36.7 14.1 %copy-start.3 = (bf16[8,8192]{1,0:T(8,128)(2,1)}, bf16[8,8192]{1,0:T(8,128)(2,1)S(1)}, u32[]{:S(2)}) copy-start(bf16[8,8192]{1,0:T(8,128)(2,1)S(1)} %get-tuple-element.43) | copy-start | bytes 393220
  36.8 5.4 %collective-permute-start.19 = (bf16[8,8192]{1,0:T(8,128)(2,1)S(1)}, bf16[8,8192]{1,0:T(8,128)(2,1)S(1)}, u32[]{:S(2)}, u32[]{:S(2)}) collective-permute-start(bf16[8,8192]{1,0:T(8,128)(2,1)S(1)} %get-tuple-element.43), channel_id=1, source_target_pairs={{0,2},{1,5},{2,0},{3,7},{4,6},{5,1},{6,4},{7,3},{8,10},{9,13},{10,... | collective-permute-start | bytes 393224 | tf_op jit(solution)/shard_map/ppermute | solution.py:30
  36.8 9.3 %collective-permute-start.18 = (bf16[8,8192]{1,0:T(8,128)(2,1)S(1)}, bf16[8,8192]{1,0:T(8,128)(2,1)S(1)}, u32[]{:S(2)}, u32[]{:S(2)}) collective-permute-start(bf16[8,8192]{1,0:T(8,128)(2,1)S(1)} %get-tuple-element.43), channel_id=1, source_target_pairs={{0,6},{1,7},{2,4},{3,5},{4,2},{5,3},{6,0},{7,1},{8,14},{9,15},{10,... | collective-permute-start | bytes 393224 | tf_op jit(solution)/shard_map/ppermute | solution.py:30
  36.9 9.7 %collective-permute-start.17 = (bf16[8,8192]{1,0:T(8,128)(2,1)S(1)}, bf16[8,8192]{1,0:T(8,128)(2,1)S(1)}, u32[]{:S(2)}, u32[]{:S(2)}) collective-permute-start(bf16[8,8192]{1,0:T(8,128)(2,1)S(1)} %get-tuple-element.43), channel_id=1, source_target_pairs={{0,4},{1,3},{2,6},{3,1},{4,0},{5,7},{6,2},{7,5},{8,12},{9,11},{10,... | collective-permute-start | bytes 393224 | tf_op jit(solution)/shard_map/ppermute | solution.py:30
  41.2 7.6 %collective-permute-start.16 = (bf16[8,8192]{1,0:T(8,128)(2,1)S(1)}, bf16[8,8192]{1,0:T(8,128)(2,1)S(1)}, u32[]{:S(2)}, u32[]{:S(2)}) collective-permute-start(bf16[8,8192]{1,0:T(8,128)(2,1)S(1)} %select_convert_fusion), channel_id=1, source_target_pairs={{0,6},{1,7},{2,4},{3,5},{4,2},{5,3},{6,0},{7,1},{8,14},{9,15},{10,... | collective-permute-start | bytes 393224 | tf_op jit(solution)/shard_map/ppermute | solution.py:30
  41.6 7.2 %collective-permute-start.15 = (bf16[8,8192]{1,0:T(8,128)(2,1)S(1)}, bf16[8,8192]{1,0:T(8,128)(2,1)S(1)}, u32[]{:S(2)}, u32[]{:S(2)}) collective-permute-start(bf16[8,8192]{1,0:T(8,128)(2,1)S(1)} %select_convert_fusion), channel_id=1, source_target_pairs={{0,4},{1,3},{2,6},{3,1},{4,0},{5,7},{6,2},{7,5},{8,12},{9,11},{10,... | collective-permute-start | bytes 393224 | tf_op jit(solution)/shard_map/ppermute | solution.py:30
  42.2 6.5 %collective-permute-start.21 = (bf16[8,8192]{1,0:T(8,128)(2,1)S(1)}, bf16[8,8192]{1,0:T(8,128)(2,1)S(1)}, u32[]{:S(2)}, u32[]{:S(2)}) collective-permute-start(bf16[8,8192]{1,0:T(8,128)(2,1)S(1)} %collective-permute-done.19), channel_id=1, source_target_pairs={{8,0},{9,1},{10,2},{11,3},{12,4},{13,5},{14,6},{15,7},{16,8},{17,9... | collective-permute-start | bytes 393224 | tf_op jit(solution)/shard_map/ppermute | solution.py:55
  46.6 2.2 %collective-permute-start.20 = (bf16[32,8192]{1,0:T(8,128)(2,1)S(1)}, bf16[32,8192]{1,0:T(8,128)(2,1)S(1)}, u32[]{:S(2)}, u32[]{:S(2)}) collective-permute-start(bf16[32,8192]{1,0:T(8,128)(2,1)S(1)} %pad_maximum_fusion.1), channel_id=1, source_target_pairs={{0,1},{1,0},{2,3},{3,2},{4,5},{5,4},{6,7},{7,6},{8,9},{9,8},{10,11... | collective-permute-start | bytes 1572872 | tf_op jit(solution)/shard_map/ppermute | solution.py:34
  48.7 2.1 %collective-permute-start.23 = (bf16[8,8192]{1,0:T(8,128)(2,1)S(1)}, bf16[8,8192]{1,0:T(8,128)(2,1)S(1)}, u32[]{:S(2)}, u32[]{:S(2)}) collective-permute-start(bf16[8,8192]{1,0:T(8,128)(2,1)S(1)} %broadcast_select_fusion), channel_id=1, source_target_pairs={{0,1},{1,0},{2,3},{3,2},{4,5},{5,4},{6,7},{7,6},{8,9},{9,8},{10,11... | collective-permute-start | bytes 393224 | tf_op jit(solution)/shard_map/ppermute | solution.py:34
  48.8 2.0 %collective-permute-start.22 = (bf16[24,8192]{1,0:T(8,128)(2,1)S(1)}, bf16[24,8192]{1,0:T(8,128)(2,1)S(1)}, u32[]{:S(2)}, u32[]{:S(2)}) collective-permute-start(bf16[24,8192]{1,0:T(8,128)(2,1)S(1)} %pad_maximum_fusion.2), channel_id=1, source_target_pairs={{0,1},{1,0},{2,3},{3,2},{4,5},{5,4},{6,7},{7,6},{8,9},{9,8},{10,11... | collective-permute-start | bytes 1179656 | tf_op jit(solution)/shard_map/ppermute | solution.py:34

commit v21 on v19

--- a/solution.py
+++ b/solution.py
@@ -195,7 +195,8 @@
     group = total.shape[0] // tokens
     for block in range(group):
         chips = group // CORES
-        label = (chips - block % chips) % chips
+        row = block % chips
+        label = row % (chips - 1) + 1 if row else 0
         slab = slab_of(place_in(group), block // chips * chips + label, chips)
         where = pl.ds(pl.multiple_of(slab * tokens, tokens), tokens)
         out_ref[0, where, :] = total[block * tokens : (block + 1) * tokens]
@@ -270,13 +271,18 @@
     error = (own_less + below).astype(jnp.bfloat16)
     later = jnp.where(final, 0.0, next_sum + after(above, error)).astype(jnp.bfloat16)
 
-    heres = [error] + [across(error, chip, chips) for chip in range(chips - 1, 0, -1)]
+    pieces = {}
+    for chip in range(1, chips):
+        top = 1 << (chip.bit_length() - 1)
+        pieces[chip] = across(pieces.get(chip - top, error), top, chips)
+    heres = [error] + [pieces[chip] for chip in [*range(2, chips), 1]]
     passed = rotated_down(after(heres[-1], later), final, group)
     here_near = jnp.concatenate(heres, axis=0)
     here_far = other_core(here_near)
     here_rows = jnp.concatenate([here_near, here_far], axis=0)
-    straight = [across(later, chip, chips) for chip in range(chips - 1, 1, -1)]
+    straight = [across(later, chip, chips) for chip in range(2, chips)]
     most = after(jnp.concatenate([later] + straight, axis=0), here_far)
+    passed = after(passed, here_near)
     after_rows = jnp.concatenate([most, passed, other_core(most), other_core(passed)], axis=0)
     grad = grad_all(after_rows, next_dec, grad_own(here_rows, own_dec), tokens)
     return (error[None], grad)

time: 50.5 us -> 54.3 us (1.075)
  waiting for transfers between devices: 10 us -> 13.4 us
    ppermute x13, waiting for transfers between devices: 2.1 us -> 5.53 us  [across(): return lax.ppermute(value, AXIS, pairs)]
    ppermute x1, waiting for transfers between devices: 2.34 us -> 0.01 us  [rotated_down(): lax.ppermute(value, AXIS, [((i + group) % size, i) for i in range(size)])]
    ppermute x7, waiting for transfers between devices: 2.1 us -> 3.45 us  [other_core(): lax.ppermute(value, AXIS, [(i, i ^ 1) for i in range(lax.axis_size(AXIS))])]
    ppermute x1, waiting for transfers between devices: 1.77 us -> 2.71 us  [lowered(): lax.ppermute(value, AXIS, [(i + group, i) for i in range(size - group)])]
    ppermute x13, starting transfers between devices: 17.8 us -> 18.4 us  [across(): return lax.ppermute(value, AXIS, pairs)]
  transfers between devices with their start and end apart: 24 -> 24, of which waited for: 9 -> 11; matrix products, arithmetic and copies ran while one was open for 2% -> 2% of each run, Pallas kernels for 14% -> 13%
where the time goes in v21:
time: 54.3 us; the launch traced here: 54.1 us
  starting transfers between devices  28 us (52%)
  waiting for transfers between devices  13.4 us (25%)
  Pallas kernels  9.89 us (18%)
  between operations  1.03 us (2%)
  matrix products  0.8 us (1%)
  other arithmetic  0.69 us (1%)
    ppermute x13, starting transfers between devices, across(): return lax.ppermute(value, AXIS, pairs)  18.4 us
    ppermute x13, waiting for transfers between devices, across(): return lax.ppermute(value, AXIS, pairs)  5.53 us
    pallas_call x1, Pallas kernels, loaded(): pl.pallas_call(load_kernel, out_shape=[pltpu.VMEM(enc.shape[1:], enc.dtyp...  4.68 us
    ppermute x7, waiting for transfers between devices, other_core(): lax.ppermute(value, AXIS, [(i, i ^ 1) for i in range(lax.axis_size(AXIS))])  3.45 us
    ppermute x1, waiting for transfers between devices, lowered(): lax.ppermute(value, AXIS, [(i + group, i) for i in range(size - group)])  2.71 us
    ppermute x1, starting transfers between devices, shifted(): lax.ppermute(value, AXIS, [(i, i + group) for i in range(size - group)])  2.7 us
    ppermute x1, starting transfers between devices, rotated_down(): lax.ppermute(value, AXIS, [((i + group) % size, i) for i in range(size)])  2.6 us
    pallas_call x1, Pallas kernels, grad_all(): pl.pallas_call(functools.partial(grad_all_kernel, tokens), out_shape=jax....  2.03 us
  transfers between devices with their start and end apart: 24, of which 11 were waited for; matrix products, arithmetic and copies ran while one was open for 2% of the time, Pallas kernels for 13%

profile of v21, /device:TPU:0, one launch (start us, length us, event | category | flops | bytes accessed | tf_op | source)
XLA Modules:
  0.0 54.1 jit_solution(16395330809712113626)
XLA Ops:
  0.6 0.0 copy-start
  0.6 0.0 copy-start.1
  0.7 4.0 %collective-permute-start = (bf16[8,8192]{1,0:T(8,128)(2,1)}, bf16[8,8192]{1,0:T(8,128)(2,1)S(1)}, u32[]{:S(2)}, u32[]{:S(2)}) collective-permute-start(bf16[8,8192]{1,0:T(8,128)(2,1)} %bitcast.15), channel_id=1, source_target_pairs={{0,6},{1,7},{2,4},{3,5},{4,2},{5,3},{6,0},{7,1},{8,14},{9,15},{10,... | collective-permute-start | bytes 393224 | tf_op jit(solution)/shard_map/ppermute | solution.py:30
  4.6 0.0 collective-permute-start.3
  4.6 0.5 collective-permute-start.2
  5.2 0.2 collective-permute-start.1
  5.3 4.7 %load_weights.1 = (bf16[8192,256]{1,0:T(8,128)(2,1)S(1)}, bf16[256,8192]{1,0:T(8,128)(2,1)S(1)}, bf16[256,8192]{1,0:T(8,128)(2,1)S(1)}) custom-call(bf16[1,8192,256]{2,1,0:T(8,128)(2,1)} %enc_hbm.1, bf16[1,2,256,8192]{3,2,1,0:T(8,128)(2,1)} %dec_hbm.1), custom_call_target="tpu_custom_call" | custom-call | bytes 25165824 | tf_op jit(solution)/shard_map/load_weights/pallas_call | solution.py:92
  10.1 0.1 gate.1
  10.2 0.0 collective-permute-done
  10.2 0.9 %collective-permute-done.1 = bf16[8,8192]{1,0:T(8,128)(2,1)S(1)} collective-permute-done((bf16[8,8192]{1,0:T(8,128)(2,1)}, bf16[8,8192]{1,0:T(8,128)(2,1)S(1)}, u32[]{:S(2)}, u32[]{:S(2)}) %collective-permute-start.1) | collective-permute-done | bytes 131104 | tf_op jit(solution)/shard_map/ppermute | solution.py:30
  11.2 0.2 collective-permute-done.2
  11.4 0.1 collective-permute-start.4
  11.5 0.0 copy-done.4
  11.6 0.0 collective-permute-done.3
  11.6 1.6 %collective-permute-done.4 = bf16[24,8192]{1,0:T(8,128)(2,1)S(1)} collective-permute-done((bf16[24,8192]{1,0:T(8,128)(2,1)S(1)}, bf16[24,8192]{1,0:T(8,128)(2,1)S(1)}, u32[]{:S(2)}, u32[]{:S(2)}) %collective-permute-start.4) | collective-permute-done | bytes 393248 | tf_op jit(solution)/shard_map/ppermute | solution.py:34
  13.2 0.8 %fusion.2.codes_ref = bf16[64,256]{1,0:T(8,128)(2,1)S(1)} fusion(f32[64,256]{1,0:T(8,128)S(1)} %get-tuple-element.29, f32[64,256]{1,0:T(8,128)S(1)} %get-tuple-element.28, bf16[64,8192]{1,0:T(8,128)(2,1)S(1)} %slice_dynamic-update-slice_fusion, bf16[8192,256]{1,0:T(8,128)(2,1)S(1)} %get-tuple-element.25), kind=kOutput, calls=%fused_computation.3 | convolution fusion | flops 268500992 | bytes 5406720 | tf_op jit(solution)/shard_map/dot_general | solution.py:256
  14.1 0.8 %decode.3 = (f32[32,8192]{1,0:T(8,128)S(1)}, bf16[32,8192]{1,0:T(8,128)(2,1)S(1)}) custom-call(bf16[64,256]{1,0:T(8,128)(2,1)S(1)} %fusion.2.codes_ref, bf16[256,8192]{1,0:T(8,128)(2,1)S(1)} %get-tuple-element.34.dec_ref), custom_call_target="tpu_custom_call" | custom-call | flops 268435456 | bytes 4194304 | tf_op jit(solution)/shard_map/decode/pallas_call | solution.py:169
  14.9 0.2 collective-permute-start.8
  15.1 0.8 %decode.2 = (f32[32,8192]{1,0:T(8,128)S(1)}, bf16[32,8192]{1,0:T(8,128)(2,1)S(1)}) custom-call(bf16[64,256]{1,0:T(8,128)(2,1)S(1)} %fusion.2.codes_ref, bf16[256,8192]{1,0:T(8,128)(2,1)S(1)} %get-tuple-element.30.dec_ref), custom_call_target="tpu_custom_call" | custom-call | flops 268435456 | bytes 4194304 | tf_op jit(solution)/shard_map/decode/pallas_call | solution.py:169
  16.0 0.4 collective-permute-start.5
  16.4 0.5 collective-permute-done.8
  16.9 0.1 fusion.9
  17.0 1.6 %collective-permute-start.9 = (bf16[8,8192]{1,0:T(8,128)(2,1)S(1)}, bf16[8,8192]{1,0:T(8,128)(2,1)S(1)}, u32[]{:S(2)}, u32[]{:S(2)}) collective-permute-start(bf16[8,8192]{1,0:T(8,128)(2,1)S(1)} %get-tuple-element.52), channel_id=1, source_target_pairs={{0,8},{1,9},{2,10},{3,11},{4,12},{5,13},{6,14},{7,15},{8,16},{9,17... | collective-permute-start | bytes 393224 | tf_op jit(solution)/shard_map/ppermute | solution.py:39
  18.7 1.5 %collective-permute-start.12 = (bf16[8,8192]{1,0:T(8,128)(2,1)S(1)}, bf16[8,8192]{1,0:T(8,128)(2,1)S(1)}, u32[]{:S(2)}, u32[]{:S(2)}) collective-permute-start(bf16[8,8192]{1,0:T(8,128)(2,1)S(1)} %get-tuple-element.53), channel_id=1, source_target_pairs={{0,4},{1,3},{2,6},{3,1},{4,0},{5,7},{6,2},{7,5},{8,12},{9,11},{10,... | collective-permute-start | bytes 393224 | tf_op jit(solution)/shard_map/ppermute | solution.py:30
  20.2 1.5 %collective-permute-start.11 = (bf16[8,8192]{1,0:T(8,128)(2,1)S(1)}, bf16[8,8192]{1,0:T(8,128)(2,1)S(1)}, u32[]{:S(2)}, u32[]{:S(2)}) collective-permute-start(bf16[8,8192]{1,0:T(8,128)(2,1)S(1)} %get-tuple-element.54), channel_id=1, source_target_pairs={{0,2},{1,5},{2,0},{3,7},{4,6},{5,1},{6,4},{7,3},{8,10},{9,13},{10,... | collective-permute-start | bytes 393224 | tf_op jit(solution)/shard_map/ppermute | solution.py:30
  21.6 0.0 collective-permute-done.5
  21.6 0.1 fusion.8
  21.8 0.6 %collective-permute-start.6 = (bf16[8,8192]{1,0:T(8,128)(2,1)S(1)}, bf16[8,8192]{1,0:T(8,128)(2,1)S(1)}, u32[]{:S(2)}, u32[]{:S(2)}) collective-permute-start(bf16[8,8192]{1,0:T(8,128)(2,1)S(1)} %get-tuple-element.50), channel_id=1, source_target_pairs={{0,2},{1,5},{2,0},{3,7},{4,6},{5,1},{6,4},{7,3},{8,10},{9,13},{10,... | collective-permute-start | bytes 393224 | tf_op jit(solution)/shard_map/ppermute | solution.py:30
  22.4 0.5 collective-permute-start.7
  22.9 1.5 %collective-permute-done.9 = bf16[8,8192]{1,0:T(8,128)(2,1)S(1)} collective-permute-done((bf16[8,8192]{1,0:T(8,128)(2,1)S(1)}, bf16[8,8192]{1,0:T(8,128)(2,1)S(1)}, u32[]{:S(2)}, u32[]{:S(2)}) %collective-permute-start.9) | collective-permute-done | bytes 131104 | tf_op jit(solution)/shard_map/ppermute | solution.py:39
  24.5 2.5 %collective-permute-start.10 = (bf16[8,8192]{1,0:T(8,128)(2,1)S(1)}, bf16[8,8192]{1,0:T(8,128)(2,1)S(1)}, u32[]{:S(2)}, u32[]{:S(2)}) collective-permute-start(bf16[8,8192]{1,0:T(8,128)(2,1)S(1)} %slice_add_fusion.1), channel_id=1, source_target_pairs={{0,6},{1,7},{2,4},{3,5},{4,2},{5,3},{6,0},{7,1},{8,14},{9,15},{10,... | collective-permute-start | bytes 393224 | tf_op jit(solution)/shard_map/ppermute | solution.py:30
  27.0 0.0 collective-permute-done.12
  27.0 0.0 collective-permute-done.11
  27.1 2.7 %collective-permute-start.13 = (bf16[8,8192]{1,0:T(8,128)(2,1)S(1)}, bf16[8,8192]{1,0:T(8,128)(2,1)S(1)}, u32[]{:S(2)}, u32[]{:S(2)}) collective-permute-start(bf16[8,8192]{1,0:T(8,128)(2,1)S(1)} %convert_element_type.71), channel_id=1, source_target_pairs={{0,8},{1,9},{2,10},{3,11},{4,12},{5,13},{6,14},{7,15},{8,16},{9,17... | collective-permute-start | bytes 393224 | tf_op jit(solution)/shard_map/ppermute | solution.py:45
  29.8 0.0 collective-permute-done.6
  29.8 0.0 collective-permute-done.7
  29.8 0.9 %collective-permute-done.10 = bf16[8,8192]{1,0:T(8,128)(2,1)S(1)} collective-permute-done((bf16[8,8192]{1,0:T(8,128)(2,1)S(1)}, bf16[8,8192]{1,0:T(8,128)(2,1)S(1)}, u32[]{:S(2)}, u32[]{:S(2)}) %collective-permute-start.10) | collective-permute-done | bytes 131104 | tf_op jit(solution)/shard_map/ppermute | solution.py:30
  30.7 0.1 fusion.7
  30.8 1.3 %collective-permute-start.14 = (bf16[8,8192]{1,0:T(8,128)(2,1)S(1)}, bf16[8,8192]{1,0:T(8,128)(2,1)S(1)}, u32[]{:S(2)}, u32[]{:S(2)}) collective-permute-start(bf16[8,8192]{1,0:T(8,128)(2,1)S(1)} %fusion.7), channel_id=1, source_target_pairs={{8,0},{9,1},{10,2},{11,3},{12,4},{13,5},{14,6},{15,7},{16,8},{17,9... | collective-permute-start | bytes 393224 | tf_op jit(solution)/shard_map/ppermute | solution.py:50
  32.1 0.2 collective-permute-done.13
  32.3 0.1 constant_dynamic-update-slice_fusion.12
  32.4 0.0 copy-start.3
  32.4 1.4 %collective-permute-start.18 = (bf16[8,8192]{1,0:T(8,128)(2,1)S(1)}, bf16[8,8192]{1,0:T(8,128)(2,1)S(1)}, u32[]{:S(2)}, u32[]{:S(2)}) collective-permute-start(bf16[8,8192]{1,0:T(8,128)(2,1)S(1)} %get-tuple-element.45), channel_id=1, source_target_pairs={{0,2},{1,5},{2,0},{3,7},{4,6},{5,1},{6,4},{7,3},{8,10},{9,13},{10,... | collective-permute-start | bytes 393224 | tf_op jit(solution)/shard_map/ppermute | solution.py:30
  33.8 1.2 %collective-permute-start.17 = (bf16[8,8192]{1,0:T(8,128)(2,1)S(1)}, bf16[8,8192]{1,0:T(8,128)(2,1)S(1)}, u32[]{:S(2)}, u32[]{:S(2)}) collective-permute-start(bf16[8,8192]{1,0:T(8,128)(2,1)S(1)} %get-tuple-element.45), channel_id=1, source_target_pairs={{0,4},{1,3},{2,6},{3,1},{4,0},{5,7},{6,2},{7,5},{8,12},{9,11},{10,... | collective-permute-start | bytes 393224 | tf_op jit(solution)/shard_map/ppermute | solution.py:30
  35.0 2.7 %collective-permute-done.14 = bf16[8,8192]{1,0:T(8,128)(2,1)S(1)} collective-permute-done((bf16[8,8192]{1,0:T(8,128)(2,1)S(1)}, bf16[8,8192]{1,0:T(8,128)(2,1)S(1)}, u32[]{:S(2)}, u32[]{:S(2)}) %collective-permute-start.14) | collective-permute-done | bytes 131104 | tf_op jit(solution)/shard_map/ppermute | solution.py:50
  37.8 2.2 %collective-permute-start.16 = (bf16[8,8192]{1,0:T(8,128)(2,1)S(1)}, bf16[8,8192]{1,0:T(8,128)(2,1)S(1)}, u32[]{:S(2)}, u32[]{:S(2)}) collective-permute-start(bf16[8,8192]{1,0:T(8,128)(2,1)S(1)} %select_convert_fusion), channel_id=1, source_target_pairs={{0,6},{1,7},{2,4},{3,5},{4,2},{5,3},{6,0},{7,1},{8,14},{9,15},{10,... | collective-permute-start | bytes 393224 | tf_op jit(solution)/shard_map/ppermute | solution.py:30
  39.9 0.8 %collective-permute-start.15 = (bf16[8,8192]{1,0:T(8,128)(2,1)S(1)}, bf16[8,8192]{1,0:T(8,128)(2,1)S(1)}, u32[]{:S(2)}, u32[]{:S(2)}) collective-permute-start(bf16[8,8192]{1,0:T(8,128)(2,1)S(1)} %select_convert_fusion), channel_id=1, source_target_pairs={{0,4},{1,3},{2,6},{3,1},{4,0},{5,7},{6,2},{7,5},{8,12},{9,11},{10,... | collective-permute-start | bytes 393224 | tf_op jit(solution)/shard_map/ppermute | solution.py:30
  40.7 0.0 collective-permute-done.18
  40.7 2.6 %collective-permute-start.21 = (bf16[8,8192]{1,0:T(8,128)(2,1)S(1)}, bf16[8,8192]{1,0:T(8,128)(2,1)S(1)}, u32[]{:S(2)}, u32[]{:S(2)}) collective-permute-start(bf16[8,8192]{1,0:T(8,128)(2,1)S(1)} %collective-permute-done.18), channel_id=1, source_target_pairs={{8,0},{9,1},{10,2},{11,3},{12,4},{13,5},{14,6},{15,7},{16,8},{17,9... | collective-permute-start | bytes 393224 | tf_op jit(solution)/shard_map/ppermute | solution.py:55
  43.3 1.5 %collective-permute-start.19 = (bf16[8,8192]{1,0:T(8,128)(2,1)S(1)}, bf16[8,8192]{1,0:T(8,128)(2,1)S(1)}, u32[]{:S(2)}, u32[]{:S(2)}) collective-permute-start(bf16[8,8192]{1,0:T(8,128)(2,1)S(1)} %collective-permute-done.18), channel_id=1, source_target_pairs={{0,4},{1,3},{2,6},{3,1},{4,0},{5,7},{6,2},{7,5},{8,12},{9,11},{10,... | collective-permute-start | bytes 393224 | tf_op jit(solution)/shard_map/ppermute | solution.py:30
  44.9 0.0 collective-permute-done.17
  44.9 3.4 %collective-permute-done.19 = bf16[8,8192]{1,0:T(8,128)(2,1)S(1)} collective-permute-done((bf16[8,8192]{1,0:T(8,128)(2,1)S(1)}, bf16[8,8192]{1,0:T(8,128)(2,1)S(1)}, u32[]{:S(2)}, u32[]{:S(2)}) %collective-permute-start.19) | collective-permute-done | bytes 131104 | tf_op jit(solution)/shard_map/ppermute | solution.py:30
  48.3 0.1 collective-permute-start.20
  48.4 0.0 collective-permute-done.21
  48.4 0.5 %collective-permute-start.23 = (bf16[8,8192]{1,0:T(8,128)(2,1)S(1)}, bf16[8,8192]{1,0:T(8,128)(2,1)S(1)}, u32[]{:S(2)}, u32[]{:S(2)}) collective-permute-start(bf16[8,8192]{1,0:T(8,128)(2,1)S(1)} %broadcast_select_fusion), channel_id=1, source_target_pairs={{0,1},{1,0},{2,3},{3,2},{4,5},{5,4},{6,7},{7,6},{8,9},{9,8},{10,11... | collective-permute-start | bytes 393224 | tf_op jit(solution)/shard_map/ppermute | solution.py:34
  49.0 0.0 collective-permute-done.16
  49.0 0.0 collective-permute-done.15
  49.1 1.2 %collective-permute-done.20 = bf16[32,8192]{1,0:T(8,128)(2,1)S(1)} collective-permute-done((bf16[32,8192]{1,0:T(8,128)(2,1)S(1)}, bf16[32,8192]{1,0:T(8,128)(2,1)S(1)}, u32[]{:S(2)}, u32[]{:S(2)}) %collective-permute-start.20) | collective-permute-done | bytes 524320 | tf_op jit(solution)/shard_map/ppermute | solution.py:34
  50.3 0.1 collective-permute-start.22
  50.5 1.4 %grad_own.1 = (f32[64,256]{1,0:T(8,128)S(1)}, f32[8,128]{1,0:T(8,128)}) custom-call(bf16[64,8192]{1,0:T(8,128)(2,1)S(1)} %constant_dynamic-update-slice_fusion.8.rows_ref, bf16[256,8192]{1,0:T(8,128)(2,1)S(1)} %get-tuple-element.30.dec_ref), custom_call_target="tpu_custom_call" | custom-call | flops 268435456 | bytes 4194304 | tf_op jit(solution)/shard_map/grad_own/pallas_call | solution.py:207
  51.9 0.0 collective-permute-done.23
  51.9 0.1 collective-permute-done.22
  52.0 0.1 pad_maximum_fusion.rows_ref
  52.1 2.0 %grad_all.1 = f32[1,64,256]{2,1,0:T(8,128)} custom-call(bf16[64,8192]{1,0:T(8,128)(2,1)S(1)} %pad_maximum_fusion.rows_ref, bf16[256,8192]{1,0:T(8,128)(2,1)S(1)} %get-tuple-element.34.dec_ref, f32[64,256]{1,0:T(8,128)S(1)} %get-tuple-element.43.own_ref), custom_call_target="tpu_custom_call" | custom-call | flops 268435456 | bytes 4194304 | tf_op jit(solution)/shard_map/grad_all/pallas_call | solution.py:219
  (31 shorter events, 0.5 us)
Async XLA Ops:
  0.6 9.4 %copy-start = (s32[1,2,2]{2,1,0:T(2,128)S(1)}, s32[1,2,2]{2,1,0:T(2,128)}, u32[]{:S(2)}) copy-start(s32[1,2,2]{2,1,0:T(2,128)} %param.9) | copy-start | bytes 52
  0.6 9.4 %copy-start.1 = (bf16[1,256]{1,0:T(2,128)(2,1)S(1)}, bf16[1,256]{1,0:T(2,128)(2,1)}, u32[]{:S(2)}) copy-start(bf16[1,256]{1,0:T(2,128)(2,1)} %bias_ref) | copy-start | bytes 1540
  0.7 10.8 %copy-start.4 = (bf16[1,8,8192]{2,1,0:T(8,128)(2,1)S(1)}, bf16[1,8,8192]{2,1,0:T(8,128)(2,1)}, u32[]{:S(2)}) copy-start(bf16[1,8,8192]{2,1,0:T(8,128)(2,1)} %param.6) | copy-start | bytes 393220
  0.7 9.5 %collective-permute-start = (bf16[8,8192]{1,0:T(8,128)(2,1)}, bf16[8,8192]{1,0:T(8,128)(2,1)S(1)}, u32[]{:S(2)}, u32[]{:S(2)}) collective-permute-start(bf16[8,8192]{1,0:T(8,128)(2,1)} %bitcast.15), channel_id=1, source_target_pairs={{0,6},{1,7},{2,4},{3,5},{4,2},{5,3},{6,0},{7,1},{8,14},{9,15},{10,... | collective-permute-start | bytes 393224 | tf_op jit(solution)/shard_map/ppermute | solution.py:30
  4.6 6.9 %collective-permute-start.3 = (bf16[8,8192]{1,0:T(8,128)(2,1)}, bf16[8,8192]{1,0:T(8,128)(2,1)S(1)}, u32[]{:S(2)}, u32[]{:S(2)}) collective-permute-start(bf16[8,8192]{1,0:T(8,128)(2,1)} %bitcast.16), channel_id=1, source_target_pairs={{0,1},{1,0},{2,3},{3,2},{4,5},{5,4},{6,7},{7,6},{8,9},{9,8},{10,11... | collective-permute-start | bytes 393224 | tf_op jit(solution)/shard_map/ppermute | solution.py:34
  4.6 6.8 %collective-permute-start.2 = (bf16[8,8192]{1,0:T(8,128)(2,1)}, bf16[8,8192]{1,0:T(8,128)(2,1)S(1)}, u32[]{:S(2)}, u32[]{:S(2)}) collective-permute-start(bf16[8,8192]{1,0:T(8,128)(2,1)} %bitcast.17), channel_id=1, source_target_pairs={{0,2},{1,5},{2,0},{3,7},{4,6},{5,1},{6,4},{7,3},{8,10},{9,13},{10,... | collective-permute-start | bytes 393224 | tf_op jit(solution)/shard_map/ppermute | solution.py:30
  5.2 6.0 %collective-permute-start.1 = (bf16[8,8192]{1,0:T(8,128)(2,1)}, bf16[8,8192]{1,0:T(8,128)(2,1)S(1)}, u32[]{:S(2)}, u32[]{:S(2)}) collective-permute-start(bf16[8,8192]{1,0:T(8,128)(2,1)} %bitcast.18), channel_id=1, source_target_pairs={{0,4},{1,3},{2,6},{3,1},{4,0},{5,7},{6,2},{7,5},{8,12},{9,11},{10,... | collective-permute-start | bytes 393224 | tf_op jit(solution)/shard_map/ppermute | solution.py:30
  11.4 1.8 %collective-permute-start.4 = (bf16[24,8192]{1,0:T(8,128)(2,1)S(1)}, bf16[24,8192]{1,0:T(8,128)(2,1)S(1)}, u32[]{:S(2)}, u32[]{:S(2)}) collective-permute-start(bf16[24,8192]{1,0:T(8,128)(2,1)S(1)} %constant_dynamic-update-slice_fusion), channel_id=1, source_target_pairs={{0,1},{1,0},{2,3},{3,2},{4,5},{5,4},{6,7},{7,6},{8,9},{9,8},{10,11... | collective-permute-start | bytes 1179656 | tf_op jit(solution)/shard_map/ppermute | solution.py:34
  14.9 2.0 %collective-permute-start.8 = (bf16[32,8192]{1,0:T(8,128)(2,1)S(1)}, bf16[32,8192]{1,0:T(8,128)(2,1)S(1)}, u32[]{:S(2)}, u32[]{:S(2)}) collective-permute-start(bf16[32,8192]{1,0:T(8,128)(2,1)S(1)} %get-tuple-element.36), channel_id=1, source_target_pairs={{0,1},{1,0},{2,3},{3,2},{4,5},{5,4},{6,7},{7,6},{8,9},{9,8},{10,11... | collective-permute-start | bytes 1572872 | tf_op jit(solution)/shard_map/ppermute | solution.py:34
  16.0 5.7 %collective-permute-start.5 = (bf16[32,8192]{1,0:T(8,128)(2,1)S(1)}, bf16[32,8192]{1,0:T(8,128)(2,1)S(1)}, u32[]{:S(2)}, u32[]{:S(2)}) collective-permute-start(bf16[32,8192]{1,0:T(8,128)(2,1)S(1)} %get-tuple-element.32), channel_id=1, source_target_pairs={{0,1},{1,0},{2,3},{3,2},{4,5},{5,4},{6,7},{7,6},{8,9},{9,8},{10,11... | collective-permute-start | bytes 1572872 | tf_op jit(solution)/shard_map/ppermute | solution.py:34
  16.9 13.8 %copy-start.2 = (bf16[1,8,8192]{2,1,0:T(8,128)(2,1)S(1)}, bf16[1,8,8192]{2,1,0:T(8,128)(2,1)}, u32[]{:S(2)}) copy-start(bf16[1,8,8192]{2,1,0:T(8,128)(2,1)} %param.11) | copy-start | bytes 393220
  17.0 7.5 %collective-permute-start.9 = (bf16[8,8192]{1,0:T(8,128)(2,1)S(1)}, bf16[8,8192]{1,0:T(8,128)(2,1)S(1)}, u32[]{:S(2)}, u32[]{:S(2)}) collective-permute-start(bf16[8,8192]{1,0:T(8,128)(2,1)S(1)} %get-tuple-element.52), channel_id=1, source_target_pairs={{0,8},{1,9},{2,10},{3,11},{4,12},{5,13},{6,14},{7,15},{8,16},{9,17... | collective-permute-start | bytes 393224 | tf_op jit(solution)/shard_map/ppermute | solution.py:39
  18.7 8.3 %collective-permute-start.12 = (bf16[8,8192]{1,0:T(8,128)(2,1)S(1)}, bf16[8,8192]{1,0:T(8,128)(2,1)S(1)}, u32[]{:S(2)}, u32[]{:S(2)}) collective-permute-start(bf16[8,8192]{1,0:T(8,128)(2,1)S(1)} %get-tuple-element.53), channel_id=1, source_target_pairs={{0,4},{1,3},{2,6},{3,1},{4,0},{5,7},{6,2},{7,5},{8,12},{9,11},{10,... | collective-permute-start | bytes 393224 | tf_op jit(solution)/shard_map/ppermute | solution.py:30
  20.2 6.9 %collective-permute-start.11 = (bf16[8,8192]{1,0:T(8,128)(2,1)S(1)}, bf16[8,8192]{1,0:T(8,128)(2,1)S(1)}, u32[]{:S(2)}, u32[]{:S(2)}) collective-permute-start(bf16[8,8192]{1,0:T(8,128)(2,1)S(1)} %get-tuple-element.54), channel_id=1, source_target_pairs={{0,2},{1,5},{2,0},{3,7},{4,6},{5,1},{6,4},{7,3},{8,10},{9,13},{10,... | collective-permute-start | bytes 393224 | tf_op jit(solution)/shard_map/ppermute | solution.py:30
  21.8 8.0 %collective-permute-start.6 = (bf16[8,8192]{1,0:T(8,128)(2,1)S(1)}, bf16[8,8192]{1,0:T(8,128)(2,1)S(1)}, u32[]{:S(2)}, u32[]{:S(2)}) collective-permute-start(bf16[8,8192]{1,0:T(8,128)(2,1)S(1)} %get-tuple-element.50), channel_id=1, source_target_pairs={{0,2},{1,5},{2,0},{3,7},{4,6},{5,1},{6,4},{7,3},{8,10},{9,13},{10,... | collective-permute-start | bytes 393224 | tf_op jit(solution)/shard_map/ppermute | solution.py:30
  22.4 7.4 %collective-permute-start.7 = (bf16[8,8192]{1,0:T(8,128)(2,1)S(1)}, bf16[8,8192]{1,0:T(8,128)(2,1)S(1)}, u32[]{:S(2)}, u32[]{:S(2)}) collective-permute-start(bf16[8,8192]{1,0:T(8,128)(2,1)S(1)} %get-tuple-element.51), channel_id=1, source_target_pairs={{0,4},{1,3},{2,6},{3,1},{4,0},{5,7},{6,2},{7,5},{8,12},{9,11},{10,... | collective-permute-start | bytes 393224 | tf_op jit(solution)/shard_map/ppermute | solution.py:30
  24.5 6.2 %collective-permute-start.10 = (bf16[8,8192]{1,0:T(8,128)(2,1)S(1)}, bf16[8,8192]{1,0:T(8,128)(2,1)S(1)}, u32[]{:S(2)}, u32[]{:S(2)}) collective-permute-start(bf16[8,8192]{1,0:T(8,128)(2,1)S(1)} %slice_add_fusion.1), channel_id=1, source_target_pairs={{0,6},{1,7},{2,4},{3,5},{4,2},{5,3},{6,0},{7,1},{8,14},{9,15},{10,... | collective-permute-start | bytes 393224 | tf_op jit(solution)/shard_map/ppermute | solution.py:30
  27.1 5.2 %collective-permute-start.13 = (bf16[8,8192]{1,0:T(8,128)(2,1)S(1)}, bf16[8,8192]{1,0:T(8,128)(2,1)S(1)}, u32[]{:S(2)}, u32[]{:S(2)}) collective-permute-start(bf16[8,8192]{1,0:T(8,128)(2,1)S(1)} %convert_element_type.71), channel_id=1, source_target_pairs={{0,8},{1,9},{2,10},{3,11},{4,12},{5,13},{6,14},{7,15},{8,16},{9,17... | collective-permute-start | bytes 393224 | tf_op jit(solution)/shard_map/ppermute | solution.py:45
  30.8 6.9 %collective-permute-start.14 = (bf16[8,8192]{1,0:T(8,128)(2,1)S(1)}, bf16[8,8192]{1,0:T(8,128)(2,1)S(1)}, u32[]{:S(2)}, u32[]{:S(2)}) collective-permute-start(bf16[8,8192]{1,0:T(8,128)(2,1)S(1)} %fusion.7), channel_id=1, source_target_pairs={{8,0},{9,1},{10,2},{11,3},{12,4},{13,5},{14,6},{15,7},{16,8},{17,9... | collective-permute-start | bytes 393224 | tf_op jit(solution)/shard_map/ppermute | solution.py:50
  32.4 19.5 %copy-start.3 = (bf16[8,8192]{1,0:T(8,128)(2,1)}, bf16[8,8192]{1,0:T(8,128)(2,1)S(1)}, u32[]{:S(2)}) copy-start(bf16[8,8192]{1,0:T(8,128)(2,1)S(1)} %get-tuple-element.45) | copy-start | bytes 393220
  32.4 8.3 %collective-permute-start.18 = (bf16[8,8192]{1,0:T(8,128)(2,1)S(1)}, bf16[8,8192]{1,0:T(8,128)(2,1)S(1)}, u32[]{:S(2)}, u32[]{:S(2)}) collective-permute-start(bf16[8,8192]{1,0:T(8,128)(2,1)S(1)} %get-tuple-element.45), channel_id=1, source_target_pairs={{0,2},{1,5},{2,0},{3,7},{4,6},{5,1},{6,4},{7,3},{8,10},{9,13},{10,... | collective-permute-start | bytes 393224 | tf_op jit(solution)/shard_map/ppermute | solution.py:30
  33.8 11.0 %collective-permute-start.17 = (bf16[8,8192]{1,0:T(8,128)(2,1)S(1)}, bf16[8,8192]{1,0:T(8,128)(2,1)S(1)}, u32[]{:S(2)}, u32[]{:S(2)}) collective-permute-start(bf16[8,8192]{1,0:T(8,128)(2,1)S(1)} %get-tuple-element.45), channel_id=1, source_target_pairs={{0,4},{1,3},{2,6},{3,1},{4,0},{5,7},{6,2},{7,5},{8,12},{9,11},{10,... | collective-permute-start | bytes 393224 | tf_op jit(solution)/shard_map/ppermute | solution.py:30
  37.8 11.2 %collective-permute-start.16 = (bf16[8,8192]{1,0:T(8,128)(2,1)S(1)}, bf16[8,8192]{1,0:T(8,128)(2,1)S(1)}, u32[]{:S(2)}, u32[]{:S(2)}) collective-permute-start(bf16[8,8192]{1,0:T(8,128)(2,1)S(1)} %select_convert_fusion), channel_id=1, source_target_pairs={{0,6},{1,7},{2,4},{3,5},{4,2},{5,3},{6,0},{7,1},{8,14},{9,15},{10,... | collective-permute-start | bytes 393224 | tf_op jit(solution)/shard_map/ppermute | solution.py:30
  39.9 9.1 %collective-permute-start.15 = (bf16[8,8192]{1,0:T(8,128)(2,1)S(1)}, bf16[8,8192]{1,0:T(8,128)(2,1)S(1)}, u32[]{:S(2)}, u32[]{:S(2)}) collective-permute-start(bf16[8,8192]{1,0:T(8,128)(2,1)S(1)} %select_convert_fusion), channel_id=1, source_target_pairs={{0,4},{1,3},{2,6},{3,1},{4,0},{5,7},{6,2},{7,5},{8,12},{9,11},{10,... | collective-permute-start | bytes 393224 | tf_op jit(solution)/shard_map/ppermute | solution.py:30
  40.7 7.7 %collective-permute-start.21 = (bf16[8,8192]{1,0:T(8,128)(2,1)S(1)}, bf16[8,8192]{1,0:T(8,128)(2,1)S(1)}, u32[]{:S(2)}, u32[]{:S(2)}) collective-permute-start(bf16[8,8192]{1,0:T(8,128)(2,1)S(1)} %collective-permute-done.18), channel_id=1, source_target_pairs={{8,0},{9,1},{10,2},{11,3},{12,4},{13,5},{14,6},{15,7},{16,8},{17,9... | collective-permute-start | bytes 393224 | tf_op jit(solution)/shard_map/ppermute | solution.py:55
  43.3 5.0 %collective-permute-start.19 = (bf16[8,8192]{1,0:T(8,128)(2,1)S(1)}, bf16[8,8192]{1,0:T(8,128)(2,1)S(1)}, u32[]{:S(2)}, u32[]{:S(2)}) collective-permute-start(bf16[8,8192]{1,0:T(8,128)(2,1)S(1)} %collective-permute-done.18), channel_id=1, source_target_pairs={{0,4},{1,3},{2,6},{3,1},{4,0},{5,7},{6,2},{7,5},{8,12},{9,11},{10,... | collective-permute-start | bytes 393224 | tf_op jit(solution)/shard_map/ppermute | solution.py:30
  48.3 2.0 %collective-permute-start.20 = (bf16[32,8192]{1,0:T(8,128)(2,1)S(1)}, bf16[32,8192]{1,0:T(8,128)(2,1)S(1)}, u32[]{:S(2)}, u32[]{:S(2)}) collective-permute-start(bf16[32,8192]{1,0:T(8,128)(2,1)S(1)} %pad_maximum_fusion.1), channel_id=1, source_target_pairs={{0,1},{1,0},{2,3},{3,2},{4,5},{5,4},{6,7},{7,6},{8,9},{9,8},{10,11... | collective-permute-start | bytes 1572872 | tf_op jit(solution)/shard_map/ppermute | solution.py:34
  48.4 3.4 %collective-permute-start.23 = (bf16[8,8192]{1,0:T(8,128)(2,1)S(1)}, bf16[8,8192]{1,0:T(8,128)(2,1)S(1)}, u32[]{:S(2)}, u32[]{:S(2)}) collective-permute-start(bf16[8,8192]{1,0:T(8,128)(2,1)S(1)} %broadcast_select_fusion), channel_id=1, source_target_pairs={{0,1},{1,0},{2,3},{3,2},{4,5},{5,4},{6,7},{7,6},{8,9},{9,8},{10,11... | collective-permute-start | bytes 393224 | tf_op jit(solution)/shard_map/ppermute | solution.py:34
  50.3 1.7 %collective-permute-start.22 = (bf16[24,8192]{1,0:T(8,128)(2,1)S(1)}, bf16[24,8192]{1,0:T(8,128)(2,1)S(1)}, u32[]{:S(2)}, u32[]{:S(2)}) collective-permute-start(bf16[24,8192]{1,0:T(8,128)(2,1)S(1)} %pad_maximum_fusion.2), channel_id=1, source_target_pairs={{0,1},{1,0},{2,3},{3,2},{4,5},{5,4},{6,7},{7,6},{8,9},{9,8},{10,11... | collective-permute-start | bytes 1179656 | tf_op jit(solution)/shard_map/ppermute | solution.py:34

commit v22 on v21

--- a/solution.py
+++ b/solution.py
@@ -50,10 +50,9 @@
     return lax.ppermute(value, AXIS, [(i + group, i) for i in range(size - group)])
 
 
-def rotated_down(value, final, group):
+def rotated_down(value, group):
     size = lax.axis_size(AXIS)
-    came = lax.ppermute(value, AXIS, [((i + group) % size, i) for i in range(size)])
-    return jnp.where(final, jnp.zeros_like(came), came)
+    return lax.ppermute(value, AXIS, [((i + group) % size, i) for i in range(size)])
 
 
 def after(values, done):
@@ -271,20 +270,18 @@
     error = (own_less + below).astype(jnp.bfloat16)
     later = jnp.where(final, 0.0, next_sum + after(above, error)).astype(jnp.bfloat16)
 
-    pieces = {}
-    for chip in range(1, chips):
-        top = 1 << (chip.bit_length() - 1)
-        pieces[chip] = across(pieces.get(chip - top, error), top, chips)
-    heres = [error] + [pieces[chip] for chip in [*range(2, chips), 1]]
-    passed = rotated_down(after(heres[-1], later), final, group)
+    heres = [error] + [across(error, chip, chips) for chip in [*range(2, chips), 1]]
+    passed = rotated_down(after(heres[-1], later), group)
     here_near = jnp.concatenate(heres, axis=0)
     here_far = other_core(here_near)
     here_rows = jnp.concatenate([here_near, here_far], axis=0)
     straight = [across(later, chip, chips) for chip in range(2, chips)]
     most = after(jnp.concatenate([later] + straight, axis=0), here_far)
-    passed = after(passed, here_near)
-    after_rows = jnp.concatenate([most, passed, other_core(most), other_core(passed)], axis=0)
-    grad = grad_all(after_rows, next_dec, grad_own(here_rows, own_dec), tokens)
+    own_grad = grad_own(here_rows, own_dec)
+    most_far = other_core(most)
+    passed = jnp.where(final, jnp.zeros_like(passed), after(passed, (own_grad, most_far)))
+    after_rows = jnp.concatenate([most, passed, most_far, other_core(passed)], axis=0)
+    grad = grad_all(after_rows, next_dec, own_grad, tokens)
     return (error[None], grad)
 
 

time: 54.3 us -> 51.4 us (0.947)
  waiting for transfers between devices: 13.4 us -> 11.2 us
  starting transfers between devices: 28 us -> 27.4 us
    ppermute x13, waiting for transfers between devices: 5.53 us -> 4.22 us  [across(): return lax.ppermute(value, AXIS, pairs)]
    ppermute x1, waiting for transfers between devices: 2.71 us -> 1.77 us  [lowered(): lax.ppermute(value, AXIS, [(i + group, i) for i in range(size - group)])]
    ppermute x13, starting transfers between devices: 18.4 us -> 17.8 us  [across(): return lax.ppermute(value, AXIS, pairs)]
  transfers between devices with their start and end apart: 24 -> 24, of which waited for: 11 -> 13; matrix products, arithmetic and copies ran while one was open for 2% -> 2% of each run, Pallas kernels for 13% -> 14%
where the time goes in v22:
time: 51.4 us; the launch traced here: 51.2 us
  starting transfers between devices  27.4 us (53%)
  waiting for transfers between devices  11.2 us (22%)
  Pallas kernels  9.89 us (19%)
  between operations  1.03 us (2%)
  matrix products  0.8 us (2%)
  other arithmetic  0.69 us (1%)
    ppermute x13, starting transfers between devices, across(): return lax.ppermute(value, AXIS, pairs)  17.8 us
    pallas_call x1, Pallas kernels, loaded(): pl.pallas_call(load_kernel, out_shape=[pltpu.VMEM(enc.shape[1:], enc.dtyp...  4.68 us
    ppermute x13, waiting for transfers between devices, across(): return lax.ppermute(value, AXIS, pairs)  4.22 us
    ppermute x7, waiting for transfers between devices, other_core(): lax.ppermute(value, AXIS, [(i, i ^ 1) for i in range(lax.axis_size(AXIS))])  3.44 us
    ppermute x1, starting transfers between devices, rotated_down(): lax.ppermute(value, AXIS, [((i + group) % size, i) for i in range(size)])  2.8 us
    ppermute x1, starting transfers between devices, shifted(): lax.ppermute(value, AXIS, [(i, i + group) for i in range(size - group)])  2.7 us
    pallas_call x1, Pallas kernels, grad_all(): pl.pallas_call(functools.partial(grad_all_kernel, tokens), out_shape=jax....  2.03 us
    ppermute x1, waiting for transfers between devices, lowered(): lax.ppermute(value, AXIS, [(i + group, i) for i in range(size - group)])  1.77 us
  transfers between devices with their start and end apart: 24, of which 13 were waited for; matrix products, arithmetic and copies ran while one was open for 2% of the time, Pallas kernels for 14%

profile of v22, /device:TPU:0, one launch (start us, length us, event | category | flops | bytes accessed | tf_op | source)
XLA Modules:
  0.0 51.2 jit_solution(8572955839712240050)
XLA Ops:
  0.6 0.0 copy-start
  0.6 0.0 copy-start.1
  0.7 0.0 copy-start.4
  0.7 4.0 %collective-permute-start = (bf16[8,8192]{1,0:T(8,128)(2,1)}, bf16[8,8192]{1,0:T(8,128)(2,1)S(1)}, u32[]{:S(2)}, u32[]{:S(2)}) collective-permute-start(bf16[8,8192]{1,0:T(8,128)(2,1)} %bitcast.15), channel_id=1, source_target_pairs={{0,6},{1,7},{2,4},{3,5},{4,2},{5,3},{6,0},{7,1},{8,14},{9,15},{10,... | collective-permute-start | bytes 393224 | tf_op jit(solution)/shard_map/ppermute | solution.py:30
  4.6 0.0 collective-permute-start.3
  4.6 0.5 %collective-permute-start.2 = (bf16[8,8192]{1,0:T(8,128)(2,1)}, bf16[8,8192]{1,0:T(8,128)(2,1)S(1)}, u32[]{:S(2)}, u32[]{:S(2)}) collective-permute-start(bf16[8,8192]{1,0:T(8,128)(2,1)} %bitcast.17), channel_id=1, source_target_pairs={{0,2},{1,5},{2,0},{3,7},{4,6},{5,1},{6,4},{7,3},{8,10},{9,13},{10,... | collective-permute-start | bytes 393224 | tf_op jit(solution)/shard_map/ppermute | solution.py:30
  5.2 0.2 collective-permute-start.1
  5.3 4.7 %load_weights.1 = (bf16[8192,256]{1,0:T(8,128)(2,1)S(1)}, bf16[256,8192]{1,0:T(8,128)(2,1)S(1)}, bf16[256,8192]{1,0:T(8,128)(2,1)S(1)}) custom-call(bf16[1,8192,256]{2,1,0:T(8,128)(2,1)} %enc_hbm.1, bf16[1,2,256,8192]{3,2,1,0:T(8,128)(2,1)} %dec_hbm.1), custom_call_target="tpu_custom_call" | custom-call | bytes 25165824 | tf_op jit(solution)/shard_map/load_weights/pallas_call | solution.py:91
  10.1 0.1 gate.1
  10.2 0.0 collective-permute-done
  10.2 0.9 %collective-permute-done.1 = bf16[8,8192]{1,0:T(8,128)(2,1)S(1)} collective-permute-done((bf16[8,8192]{1,0:T(8,128)(2,1)}, bf16[8,8192]{1,0:T(8,128)(2,1)S(1)}, u32[]{:S(2)}, u32[]{:S(2)}) %collective-permute-start.1) | collective-permute-done | bytes 131104 | tf_op jit(solution)/shard_map/ppermute | solution.py:30
  11.2 0.2 collective-permute-done.2
  11.4 0.1 collective-permute-start.4
  11.6 0.0 collective-permute-done.3
  11.6 1.6 %collective-permute-done.4 = bf16[24,8192]{1,0:T(8,128)(2,1)S(1)} collective-permute-done((bf16[24,8192]{1,0:T(8,128)(2,1)S(1)}, bf16[24,8192]{1,0:T(8,128)(2,1)S(1)}, u32[]{:S(2)}, u32[]{:S(2)}) %collective-permute-start.4) | collective-permute-done | bytes 393248 | tf_op jit(solution)/shard_map/ppermute | solution.py:34
  13.2 0.8 %fusion.2.codes_ref = bf16[64,256]{1,0:T(8,128)(2,1)S(1)} fusion(f32[64,256]{1,0:T(8,128)S(1)} %get-tuple-element.29, f32[64,256]{1,0:T(8,128)S(1)} %get-tuple-element.28, bf16[64,8192]{1,0:T(8,128)(2,1)S(1)} %slice_dynamic-update-slice_fusion, bf16[8192,256]{1,0:T(8,128)(2,1)S(1)} %get-tuple-element.25), kind=kOutput, calls=%fused_computation.3 | convolution fusion | flops 268500992 | bytes 5406720 | tf_op jit(solution)/shard_map/dot_general | solution.py:255
  14.1 0.8 %decode.3 = (f32[32,8192]{1,0:T(8,128)S(1)}, bf16[32,8192]{1,0:T(8,128)(2,1)S(1)}) custom-call(bf16[64,256]{1,0:T(8,128)(2,1)S(1)} %fusion.2.codes_ref, bf16[256,8192]{1,0:T(8,128)(2,1)S(1)} %get-tuple-element.34.dec_ref), custom_call_target="tpu_custom_call" | custom-call | flops 268435456 | bytes 4194304 | tf_op jit(solution)/shard_map/decode/pallas_call | solution.py:168
  14.9 0.2 collective-permute-start.8
  15.1 0.8 %decode.2 = (f32[32,8192]{1,0:T(8,128)S(1)}, bf16[32,8192]{1,0:T(8,128)(2,1)S(1)}) custom-call(bf16[64,256]{1,0:T(8,128)(2,1)S(1)} %fusion.2.codes_ref, bf16[256,8192]{1,0:T(8,128)(2,1)S(1)} %get-tuple-element.30.dec_ref), custom_call_target="tpu_custom_call" | custom-call | flops 268435456 | bytes 4194304 | tf_op jit(solution)/shard_map/decode/pallas_call | solution.py:168
  16.0 0.4 collective-permute-start.5
  16.4 0.5 collective-permute-done.8
  16.9 0.1 fusion.9
  17.0 1.6 %collective-permute-start.9 = (bf16[8,8192]{1,0:T(8,128)(2,1)S(1)}, bf16[8,8192]{1,0:T(8,128)(2,1)S(1)}, u32[]{:S(2)}, u32[]{:S(2)}) collective-permute-start(bf16[8,8192]{1,0:T(8,128)(2,1)S(1)} %get-tuple-element.52), channel_id=1, source_target_pairs={{0,8},{1,9},{2,10},{3,11},{4,12},{5,13},{6,14},{7,15},{8,16},{9,17... | collective-permute-start | bytes 393224 | tf_op jit(solution)/shard_map/ppermute | solution.py:39
  18.7 1.5 %collective-permute-start.12 = (bf16[8,8192]{1,0:T(8,128)(2,1)S(1)}, bf16[8,8192]{1,0:T(8,128)(2,1)S(1)}, u32[]{:S(2)}, u32[]{:S(2)}) collective-permute-start(bf16[8,8192]{1,0:T(8,128)(2,1)S(1)} %get-tuple-element.53), channel_id=1, source_target_pairs={{0,4},{1,3},{2,6},{3,1},{4,0},{5,7},{6,2},{7,5},{8,12},{9,11},{10,... | collective-permute-start | bytes 393224 | tf_op jit(solution)/shard_map/ppermute | solution.py:30
  20.2 1.5 %collective-permute-start.11 = (bf16[8,8192]{1,0:T(8,128)(2,1)S(1)}, bf16[8,8192]{1,0:T(8,128)(2,1)S(1)}, u32[]{:S(2)}, u32[]{:S(2)}) collective-permute-start(bf16[8,8192]{1,0:T(8,128)(2,1)S(1)} %get-tuple-element.54), channel_id=1, source_target_pairs={{0,2},{1,5},{2,0},{3,7},{4,6},{5,1},{6,4},{7,3},{8,10},{9,13},{10,... | collective-permute-start | bytes 393224 | tf_op jit(solution)/shard_map/ppermute | solution.py:30
  21.6 0.0 collective-permute-done.5
  21.6 0.1 fusion.8
  21.8 0.6 %collective-permute-start.6 = (bf16[8,8192]{1,0:T(8,128)(2,1)S(1)}, bf16[8,8192]{1,0:T(8,128)(2,1)S(1)}, u32[]{:S(2)}, u32[]{:S(2)}) collective-permute-start(bf16[8,8192]{1,0:T(8,128)(2,1)S(1)} %get-tuple-element.50), channel_id=1, source_target_pairs={{0,2},{1,5},{2,0},{3,7},{4,6},{5,1},{6,4},{7,3},{8,10},{9,13},{10,... | collective-permute-start | bytes 393224 | tf_op jit(solution)/shard_map/ppermute | solution.py:30
  22.4 0.5 %collective-permute-start.7 = (bf16[8,8192]{1,0:T(8,128)(2,1)S(1)}, bf16[8,8192]{1,0:T(8,128)(2,1)S(1)}, u32[]{:S(2)}, u32[]{:S(2)}) collective-permute-start(bf16[8,8192]{1,0:T(8,128)(2,1)S(1)} %get-tuple-element.51), channel_id=1, source_target_pairs={{0,4},{1,3},{2,6},{3,1},{4,0},{5,7},{6,2},{7,5},{8,12},{9,11},{10,... | collective-permute-start | bytes 393224 | tf_op jit(solution)/shard_map/ppermute | solution.py:30
  22.9 1.5 %collective-permute-done.9 = bf16[8,8192]{1,0:T(8,128)(2,1)S(1)} collective-permute-done((bf16[8,8192]{1,0:T(8,128)(2,1)S(1)}, bf16[8,8192]{1,0:T(8,128)(2,1)S(1)}, u32[]{:S(2)}, u32[]{:S(2)}) %collective-permute-start.9) | collective-permute-done | bytes 131104 | tf_op jit(solution)/shard_map/ppermute | solution.py:39
  24.5 2.5 %collective-permute-start.10 = (bf16[8,8192]{1,0:T(8,128)(2,1)S(1)}, bf16[8,8192]{1,0:T(8,128)(2,1)S(1)}, u32[]{:S(2)}, u32[]{:S(2)}) collective-permute-start(bf16[8,8192]{1,0:T(8,128)(2,1)S(1)} %slice_add_fusion.1), channel_id=1, source_target_pairs={{0,6},{1,7},{2,4},{3,5},{4,2},{5,3},{6,0},{7,1},{8,14},{9,15},{10,... | collective-permute-start | bytes 393224 | tf_op jit(solution)/shard_map/ppermute | solution.py:30
  27.0 0.0 collective-permute-done.12
  27.0 0.0 collective-permute-done.11
  27.1 2.7 %collective-permute-start.13 = (bf16[8,8192]{1,0:T(8,128)(2,1)S(1)}, bf16[8,8192]{1,0:T(8,128)(2,1)S(1)}, u32[]{:S(2)}, u32[]{:S(2)}) collective-permute-start(bf16[8,8192]{1,0:T(8,128)(2,1)S(1)} %convert_element_type.71), channel_id=1, source_target_pairs={{0,8},{1,9},{2,10},{3,11},{4,12},{5,13},{6,14},{7,15},{8,16},{9,17... | collective-permute-start | bytes 393224 | tf_op jit(solution)/shard_map/ppermute | solution.py:45
  29.8 0.0 collective-permute-done.6
  29.8 0.0 collective-permute-done.7
  29.8 0.9 %collective-permute-done.10 = bf16[8,8192]{1,0:T(8,128)(2,1)S(1)} collective-permute-done((bf16[8,8192]{1,0:T(8,128)(2,1)S(1)}, bf16[8,8192]{1,0:T(8,128)(2,1)S(1)}, u32[]{:S(2)}, u32[]{:S(2)}) %collective-permute-start.10) | collective-permute-done | bytes 131104 | tf_op jit(solution)/shard_map/ppermute | solution.py:30
  30.7 0.1 fusion.7
  30.8 1.3 %collective-permute-start.14 = (bf16[8,8192]{1,0:T(8,128)(2,1)S(1)}, bf16[8,8192]{1,0:T(8,128)(2,1)S(1)}, u32[]{:S(2)}, u32[]{:S(2)}) collective-permute-start(bf16[8,8192]{1,0:T(8,128)(2,1)S(1)} %fusion.7), channel_id=1, source_target_pairs={{8,0},{9,1},{10,2},{11,3},{12,4},{13,5},{14,6},{15,7},{16,8},{17,9... | collective-permute-start | bytes 393224 | tf_op jit(solution)/shard_map/ppermute | solution.py:50
  32.1 0.2 collective-permute-done.13
  32.3 0.1 constant_dynamic-update-slice_fusion.12
  32.4 0.0 copy-start.3
  32.4 1.4 %collective-permute-start.19 = (bf16[8,8192]{1,0:T(8,128)(2,1)S(1)}, bf16[8,8192]{1,0:T(8,128)(2,1)S(1)}, u32[]{:S(2)}, u32[]{:S(2)}) collective-permute-start(bf16[8,8192]{1,0:T(8,128)(2,1)S(1)} %get-tuple-element.45), channel_id=1, source_target_pairs={{0,2},{1,5},{2,0},{3,7},{4,6},{5,1},{6,4},{7,3},{8,10},{9,13},{10,... | collective-permute-start | bytes 393224 | tf_op jit(solution)/shard_map/ppermute | solution.py:30
  33.8 1.4 %collective-permute-start.18 = (bf16[8,8192]{1,0:T(8,128)(2,1)S(1)}, bf16[8,8192]{1,0:T(8,128)(2,1)S(1)}, u32[]{:S(2)}, u32[]{:S(2)}) collective-permute-start(bf16[8,8192]{1,0:T(8,128)(2,1)S(1)} %get-tuple-element.45), channel_id=1, source_target_pairs={{0,6},{1,7},{2,4},{3,5},{4,2},{5,3},{6,0},{7,1},{8,14},{9,15},{10,... | collective-permute-start | bytes 393224 | tf_op jit(solution)/shard_map/ppermute | solution.py:30
  35.3 0.7 %collective-permute-start.17 = (bf16[8,8192]{1,0:T(8,128)(2,1)S(1)}, bf16[8,8192]{1,0:T(8,128)(2,1)S(1)}, u32[]{:S(2)}, u32[]{:S(2)}) collective-permute-start(bf16[8,8192]{1,0:T(8,128)(2,1)S(1)} %get-tuple-element.45), channel_id=1, source_target_pairs={{0,4},{1,3},{2,6},{3,1},{4,0},{5,7},{6,2},{7,5},{8,12},{9,11},{10,... | collective-permute-start | bytes 393224 | tf_op jit(solution)/shard_map/ppermute | solution.py:30
  35.9 1.8 %collective-permute-done.14 = bf16[8,8192]{1,0:T(8,128)(2,1)S(1)} collective-permute-done((bf16[8,8192]{1,0:T(8,128)(2,1)S(1)}, bf16[8,8192]{1,0:T(8,128)(2,1)S(1)}, u32[]{:S(2)}, u32[]{:S(2)}) %collective-permute-start.14) | collective-permute-done | bytes 131104 | tf_op jit(solution)/shard_map/ppermute | solution.py:50
  37.8 2.2 %collective-permute-start.16 = (bf16[8,8192]{1,0:T(8,128)(2,1)S(1)}, bf16[8,8192]{1,0:T(8,128)(2,1)S(1)}, u32[]{:S(2)}, u32[]{:S(2)}) collective-permute-start(bf16[8,8192]{1,0:T(8,128)(2,1)S(1)} %select_convert_fusion), channel_id=1, source_target_pairs={{0,6},{1,7},{2,4},{3,5},{4,2},{5,3},{6,0},{7,1},{8,14},{9,15},{10,... | collective-permute-start | bytes 393224 | tf_op jit(solution)/shard_map/ppermute | solution.py:30
  39.9 0.8 %collective-permute-start.15 = (bf16[8,8192]{1,0:T(8,128)(2,1)S(1)}, bf16[8,8192]{1,0:T(8,128)(2,1)S(1)}, u32[]{:S(2)}, u32[]{:S(2)}) collective-permute-start(bf16[8,8192]{1,0:T(8,128)(2,1)S(1)} %select_convert_fusion), channel_id=1, source_target_pairs={{0,4},{1,3},{2,6},{3,1},{4,0},{5,7},{6,2},{7,5},{8,12},{9,11},{10,... | collective-permute-start | bytes 393224 | tf_op jit(solution)/shard_map/ppermute | solution.py:30
  40.7 0.0 collective-permute-done.19
  40.7 2.8 %collective-permute-start.21 = (bf16[8,8192]{1,0:T(8,128)(2,1)S(1)}, bf16[8,8192]{1,0:T(8,128)(2,1)S(1)}, u32[]{:S(2)}, u32[]{:S(2)}) collective-permute-start(bf16[8,8192]{1,0:T(8,128)(2,1)S(1)} %collective-permute-done.19), channel_id=1, source_target_pairs={{8,0},{9,1},{10,2},{11,3},{12,4},{13,5},{14,6},{15,7},{16,8},{17,9... | collective-permute-start | bytes 393224 | tf_op jit(solution)/shard_map/ppermute | solution.py:55
  43.5 0.0 collective-permute-done.18
  43.5 0.1 collective-permute-done.17
  43.7 0.1 collective-permute-start.20
  43.8 1.5 %collective-permute-done.16 = bf16[8,8192]{1,0:T(8,128)(2,1)S(1)} collective-permute-done((bf16[8,8192]{1,0:T(8,128)(2,1)S(1)}, bf16[8,8192]{1,0:T(8,128)(2,1)S(1)}, u32[]{:S(2)}, u32[]{:S(2)}) %collective-permute-start.16) | collective-permute-done | bytes 131104 | tf_op jit(solution)/shard_map/ppermute | solution.py:30
  45.2 0.6 %collective-permute-done.15 = bf16[8,8192]{1,0:T(8,128)(2,1)S(1)} collective-permute-done((bf16[8,8192]{1,0:T(8,128)(2,1)S(1)}, bf16[8,8192]{1,0:T(8,128)(2,1)S(1)}, u32[]{:S(2)}, u32[]{:S(2)}) %collective-permute-start.15) | collective-permute-done | bytes 131104 | tf_op jit(solution)/shard_map/ppermute | solution.py:30
  45.9 0.0 collective-permute-done.20
  45.9 0.1 collective-permute-start.22
  46.0 1.4 %grad_own.1 = (f32[64,256]{1,0:T(8,128)S(1)}, f32[8,128]{1,0:T(8,128)}) custom-call(bf16[64,8192]{1,0:T(8,128)(2,1)S(1)} %constant_dynamic-update-slice_fusion.8.rows_ref, bf16[256,8192]{1,0:T(8,128)(2,1)S(1)} %get-tuple-element.30.dec_ref), custom_call_target="tpu_custom_call" | custom-call | flops 268435456 | bytes 4194304 | tf_op jit(solution)/shard_map/grad_own/pallas_call | solution.py:206
  47.4 0.0 collective-permute-done.21
  47.4 0.3 collective-permute-done.22
  47.7 0.3 collective-permute-start.23
  48.0 1.1 %collective-permute-done.23 = bf16[8,8192]{1,0:T(8,128)(2,1)S(1)} collective-permute-done((bf16[8,8192]{1,0:T(8,128)(2,1)S(1)}, bf16[8,8192]{1,0:T(8,128)(2,1)S(1)}, u32[]{:S(2)}, u32[]{:S(2)}) %collective-permute-start.23) | collective-permute-done | bytes 131104 | tf_op jit(solution)/shard_map/ppermute | solution.py:34
  49.1 0.1 pad_maximum_fusion.rows_ref
  49.2 2.0 %grad_all.1 = f32[1,64,256]{2,1,0:T(8,128)} custom-call(bf16[64,8192]{1,0:T(8,128)(2,1)S(1)} %pad_maximum_fusion.rows_ref, bf16[256,8192]{1,0:T(8,128)(2,1)S(1)} %get-tuple-element.34.dec_ref, f32[64,256]{1,0:T(8,128)S(1)} %get-tuple-element.42.own_ref), custom_call_target="tpu_custom_call" | custom-call | flops 268435456 | bytes 4194304 | tf_op jit(solution)/shard_map/grad_all/pallas_call | solution.py:218
  (31 shorter events, 0.5 us)
Async XLA Ops:
  0.6 9.4 %copy-start = (s32[1,2,2]{2,1,0:T(2,128)S(1)}, s32[1,2,2]{2,1,0:T(2,128)}, u32[]{:S(2)}) copy-start(s32[1,2,2]{2,1,0:T(2,128)} %param.9) | copy-start | bytes 52
  0.6 9.4 %copy-start.1 = (bf16[1,256]{1,0:T(2,128)(2,1)S(1)}, bf16[1,256]{1,0:T(2,128)(2,1)}, u32[]{:S(2)}) copy-start(bf16[1,256]{1,0:T(2,128)(2,1)} %bias_ref) | copy-start | bytes 1540
  0.7 10.8 %copy-start.4 = (bf16[1,8,8192]{2,1,0:T(8,128)(2,1)S(1)}, bf16[1,8,8192]{2,1,0:T(8,128)(2,1)}, u32[]{:S(2)}) copy-start(bf16[1,8,8192]{2,1,0:T(8,128)(2,1)} %param.6) | copy-start | bytes 393220
  0.7 9.5 %collective-permute-start = (bf16[8,8192]{1,0:T(8,128)(2,1)}, bf16[8,8192]{1,0:T(8,128)(2,1)S(1)}, u32[]{:S(2)}, u32[]{:S(2)}) collective-permute-start(bf16[8,8192]{1,0:T(8,128)(2,1)} %bitcast.15), channel_id=1, source_target_pairs={{0,6},{1,7},{2,4},{3,5},{4,2},{5,3},{6,0},{7,1},{8,14},{9,15},{10,... | collective-permute-start | bytes 393224 | tf_op jit(solution)/shard_map/ppermute | solution.py:30
  4.6 6.9 %collective-permute-start.3 = (bf16[8,8192]{1,0:T(8,128)(2,1)}, bf16[8,8192]{1,0:T(8,128)(2,1)S(1)}, u32[]{:S(2)}, u32[]{:S(2)}) collective-permute-start(bf16[8,8192]{1,0:T(8,128)(2,1)} %bitcast.16), channel_id=1, source_target_pairs={{0,1},{1,0},{2,3},{3,2},{4,5},{5,4},{6,7},{7,6},{8,9},{9,8},{10,11... | collective-permute-start | bytes 393224 | tf_op jit(solution)/shard_map/ppermute | solution.py:34
  4.6 6.8 %collective-permute-start.2 = (bf16[8,8192]{1,0:T(8,128)(2,1)}, bf16[8,8192]{1,0:T(8,128)(2,1)S(1)}, u32[]{:S(2)}, u32[]{:S(2)}) collective-permute-start(bf16[8,8192]{1,0:T(8,128)(2,1)} %bitcast.17), channel_id=1, source_target_pairs={{0,2},{1,5},{2,0},{3,7},{4,6},{5,1},{6,4},{7,3},{8,10},{9,13},{10,... | collective-permute-start | bytes 393224 | tf_op jit(solution)/shard_map/ppermute | solution.py:30
  5.2 6.0 %collective-permute-start.1 = (bf16[8,8192]{1,0:T(8,128)(2,1)}, bf16[8,8192]{1,0:T(8,128)(2,1)S(1)}, u32[]{:S(2)}, u32[]{:S(2)}) collective-permute-start(bf16[8,8192]{1,0:T(8,128)(2,1)} %bitcast.18), channel_id=1, source_target_pairs={{0,4},{1,3},{2,6},{3,1},{4,0},{5,7},{6,2},{7,5},{8,12},{9,11},{10,... | collective-permute-start | bytes 393224 | tf_op jit(solution)/shard_map/ppermute | solution.py:30
  11.4 1.8 %collective-permute-start.4 = (bf16[24,8192]{1,0:T(8,128)(2,1)S(1)}, bf16[24,8192]{1,0:T(8,128)(2,1)S(1)}, u32[]{:S(2)}, u32[]{:S(2)}) collective-permute-start(bf16[24,8192]{1,0:T(8,128)(2,1)S(1)} %constant_dynamic-update-slice_fusion), channel_id=1, source_target_pairs={{0,1},{1,0},{2,3},{3,2},{4,5},{5,4},{6,7},{7,6},{8,9},{9,8},{10,11... | collective-permute-start | bytes 1179656 | tf_op jit(solution)/shard_map/ppermute | solution.py:34
  14.9 2.0 %collective-permute-start.8 = (bf16[32,8192]{1,0:T(8,128)(2,1)S(1)}, bf16[32,8192]{1,0:T(8,128)(2,1)S(1)}, u32[]{:S(2)}, u32[]{:S(2)}) collective-permute-start(bf16[32,8192]{1,0:T(8,128)(2,1)S(1)} %get-tuple-element.36), channel_id=1, source_target_pairs={{0,1},{1,0},{2,3},{3,2},{4,5},{5,4},{6,7},{7,6},{8,9},{9,8},{10,11... | collective-permute-start | bytes 1572872 | tf_op jit(solution)/shard_map/ppermute | solution.py:34
  16.0 5.7 %collective-permute-start.5 = (bf16[32,8192]{1,0:T(8,128)(2,1)S(1)}, bf16[32,8192]{1,0:T(8,128)(2,1)S(1)}, u32[]{:S(2)}, u32[]{:S(2)}) collective-permute-start(bf16[32,8192]{1,0:T(8,128)(2,1)S(1)} %get-tuple-element.32), channel_id=1, source_target_pairs={{0,1},{1,0},{2,3},{3,2},{4,5},{5,4},{6,7},{7,6},{8,9},{9,8},{10,11... | collective-permute-start | bytes 1572872 | tf_op jit(solution)/shard_map/ppermute | solution.py:34
  16.9 13.8 %copy-start.2 = (bf16[1,8,8192]{2,1,0:T(8,128)(2,1)S(1)}, bf16[1,8,8192]{2,1,0:T(8,128)(2,1)}, u32[]{:S(2)}) copy-start(bf16[1,8,8192]{2,1,0:T(8,128)(2,1)} %param.11) | copy-start | bytes 393220
  17.0 7.5 %collective-permute-start.9 = (bf16[8,8192]{1,0:T(8,128)(2,1)S(1)}, bf16[8,8192]{1,0:T(8,128)(2,1)S(1)}, u32[]{:S(2)}, u32[]{:S(2)}) collective-permute-start(bf16[8,8192]{1,0:T(8,128)(2,1)S(1)} %get-tuple-element.52), channel_id=1, source_target_pairs={{0,8},{1,9},{2,10},{3,11},{4,12},{5,13},{6,14},{7,15},{8,16},{9,17... | collective-permute-start | bytes 393224 | tf_op jit(solution)/shard_map/ppermute | solution.py:39
  18.7 8.3 %collective-permute-start.12 = (bf16[8,8192]{1,0:T(8,128)(2,1)S(1)}, bf16[8,8192]{1,0:T(8,128)(2,1)S(1)}, u32[]{:S(2)}, u32[]{:S(2)}) collective-permute-start(bf16[8,8192]{1,0:T(8,128)(2,1)S(1)} %get-tuple-element.53), channel_id=1, source_target_pairs={{0,4},{1,3},{2,6},{3,1},{4,0},{5,7},{6,2},{7,5},{8,12},{9,11},{10,... | collective-permute-start | bytes 393224 | tf_op jit(solution)/shard_map/ppermute | solution.py:30
  20.2 6.9 %collective-permute-start.11 = (bf16[8,8192]{1,0:T(8,128)(2,1)S(1)}, bf16[8,8192]{1,0:T(8,128)(2,1)S(1)}, u32[]{:S(2)}, u32[]{:S(2)}) collective-permute-start(bf16[8,8192]{1,0:T(8,128)(2,1)S(1)} %get-tuple-element.54), channel_id=1, source_target_pairs={{0,2},{1,5},{2,0},{3,7},{4,6},{5,1},{6,4},{7,3},{8,10},{9,13},{10,... | collective-permute-start | bytes 393224 | tf_op jit(solution)/shard_map/ppermute | solution.py:30
  21.8 8.0 %collective-permute-start.6 = (bf16[8,8192]{1,0:T(8,128)(2,1)S(1)}, bf16[8,8192]{1,0:T(8,128)(2,1)S(1)}, u32[]{:S(2)}, u32[]{:S(2)}) collective-permute-start(bf16[8,8192]{1,0:T(8,128)(2,1)S(1)} %get-tuple-element.50), channel_id=1, source_target_pairs={{0,2},{1,5},{2,0},{3,7},{4,6},{5,1},{6,4},{7,3},{8,10},{9,13},{10,... | collective-permute-start | bytes 393224 | tf_op jit(solution)/shard_map/ppermute | solution.py:30
  22.4 7.4 %collective-permute-start.7 = (bf16[8,8192]{1,0:T(8,128)(2,1)S(1)}, bf16[8,8192]{1,0:T(8,128)(2,1)S(1)}, u32[]{:S(2)}, u32[]{:S(2)}) collective-permute-start(bf16[8,8192]{1,0:T(8,128)(2,1)S(1)} %get-tuple-element.51), channel_id=1, source_target_pairs={{0,4},{1,3},{2,6},{3,1},{4,0},{5,7},{6,2},{7,5},{8,12},{9,11},{10,... | collective-permute-start | bytes 393224 | tf_op jit(solution)/shard_map/ppermute | solution.py:30
  24.5 6.2 %collective-permute-start.10 = (bf16[8,8192]{1,0:T(8,128)(2,1)S(1)}, bf16[8,8192]{1,0:T(8,128)(2,1)S(1)}, u32[]{:S(2)}, u32[]{:S(2)}) collective-permute-start(bf16[8,8192]{1,0:T(8,128)(2,1)S(1)} %slice_add_fusion.1), channel_id=1, source_target_pairs={{0,6},{1,7},{2,4},{3,5},{4,2},{5,3},{6,0},{7,1},{8,14},{9,15},{10,... | collective-permute-start | bytes 393224 | tf_op jit(solution)/shard_map/ppermute | solution.py:30
  27.1 5.2 %collective-permute-start.13 = (bf16[8,8192]{1,0:T(8,128)(2,1)S(1)}, bf16[8,8192]{1,0:T(8,128)(2,1)S(1)}, u32[]{:S(2)}, u32[]{:S(2)}) collective-permute-start(bf16[8,8192]{1,0:T(8,128)(2,1)S(1)} %convert_element_type.71), channel_id=1, source_target_pairs={{0,8},{1,9},{2,10},{3,11},{4,12},{5,13},{6,14},{7,15},{8,16},{9,17... | collective-permute-start | bytes 393224 | tf_op jit(solution)/shard_map/ppermute | solution.py:45
  30.8 6.9 %collective-permute-start.14 = (bf16[8,8192]{1,0:T(8,128)(2,1)S(1)}, bf16[8,8192]{1,0:T(8,128)(2,1)S(1)}, u32[]{:S(2)}, u32[]{:S(2)}) collective-permute-start(bf16[8,8192]{1,0:T(8,128)(2,1)S(1)} %fusion.7), channel_id=1, source_target_pairs={{8,0},{9,1},{10,2},{11,3},{12,4},{13,5},{14,6},{15,7},{16,8},{17,9... | collective-permute-start | bytes 393224 | tf_op jit(solution)/shard_map/ppermute | solution.py:50
  32.4 15.0 %copy-start.3 = (bf16[8,8192]{1,0:T(8,128)(2,1)}, bf16[8,8192]{1,0:T(8,128)(2,1)S(1)}, u32[]{:S(2)}) copy-start(bf16[8,8192]{1,0:T(8,128)(2,1)S(1)} %get-tuple-element.45) | copy-start | bytes 393220
  32.4 8.3 %collective-permute-start.19 = (bf16[8,8192]{1,0:T(8,128)(2,1)S(1)}, bf16[8,8192]{1,0:T(8,128)(2,1)S(1)}, u32[]{:S(2)}, u32[]{:S(2)}) collective-permute-start(bf16[8,8192]{1,0:T(8,128)(2,1)S(1)} %get-tuple-element.45), channel_id=1, source_target_pairs={{0,2},{1,5},{2,0},{3,7},{4,6},{5,1},{6,4},{7,3},{8,10},{9,13},{10,... | collective-permute-start | bytes 393224 | tf_op jit(solution)/shard_map/ppermute | solution.py:30
  33.8 9.7 %collective-permute-start.18 = (bf16[8,8192]{1,0:T(8,128)(2,1)S(1)}, bf16[8,8192]{1,0:T(8,128)(2,1)S(1)}, u32[]{:S(2)}, u32[]{:S(2)}) collective-permute-start(bf16[8,8192]{1,0:T(8,128)(2,1)S(1)} %get-tuple-element.45), channel_id=1, source_target_pairs={{0,6},{1,7},{2,4},{3,5},{4,2},{5,3},{6,0},{7,1},{8,14},{9,15},{10,... | collective-permute-start | bytes 393224 | tf_op jit(solution)/shard_map/ppermute | solution.py:30
  35.3 8.4 %collective-permute-start.17 = (bf16[8,8192]{1,0:T(8,128)(2,1)S(1)}, bf16[8,8192]{1,0:T(8,128)(2,1)S(1)}, u32[]{:S(2)}, u32[]{:S(2)}) collective-permute-start(bf16[8,8192]{1,0:T(8,128)(2,1)S(1)} %get-tuple-element.45), channel_id=1, source_target_pairs={{0,4},{1,3},{2,6},{3,1},{4,0},{5,7},{6,2},{7,5},{8,12},{9,11},{10,... | collective-permute-start | bytes 393224 | tf_op jit(solution)/shard_map/ppermute | solution.py:30
  37.8 7.5 %collective-permute-start.16 = (bf16[8,8192]{1,0:T(8,128)(2,1)S(1)}, bf16[8,8192]{1,0:T(8,128)(2,1)S(1)}, u32[]{:S(2)}, u32[]{:S(2)}) collective-permute-start(bf16[8,8192]{1,0:T(8,128)(2,1)S(1)} %select_convert_fusion), channel_id=1, source_target_pairs={{0,6},{1,7},{2,4},{3,5},{4,2},{5,3},{6,0},{7,1},{8,14},{9,15},{10,... | collective-permute-start | bytes 393224 | tf_op jit(solution)/shard_map/ppermute | solution.py:30
  39.9 5.9 %collective-permute-start.15 = (bf16[8,8192]{1,0:T(8,128)(2,1)S(1)}, bf16[8,8192]{1,0:T(8,128)(2,1)S(1)}, u32[]{:S(2)}, u32[]{:S(2)}) collective-permute-start(bf16[8,8192]{1,0:T(8,128)(2,1)S(1)} %select_convert_fusion), channel_id=1, source_target_pairs={{0,4},{1,3},{2,6},{3,1},{4,0},{5,7},{6,2},{7,5},{8,12},{9,11},{10,... | collective-permute-start | bytes 393224 | tf_op jit(solution)/shard_map/ppermute | solution.py:30
  40.7 6.7 %collective-permute-start.21 = (bf16[8,8192]{1,0:T(8,128)(2,1)S(1)}, bf16[8,8192]{1,0:T(8,128)(2,1)S(1)}, u32[]{:S(2)}, u32[]{:S(2)}) collective-permute-start(bf16[8,8192]{1,0:T(8,128)(2,1)S(1)} %collective-permute-done.19), channel_id=1, source_target_pairs={{8,0},{9,1},{10,2},{11,3},{12,4},{13,5},{14,6},{15,7},{16,8},{17,9... | collective-permute-start | bytes 393224 | tf_op jit(solution)/shard_map/ppermute | solution.py:55
  43.7 2.2 %collective-permute-start.20 = (bf16[32,8192]{1,0:T(8,128)(2,1)S(1)}, bf16[32,8192]{1,0:T(8,128)(2,1)S(1)}, u32[]{:S(2)}, u32[]{:S(2)}) collective-permute-start(bf16[32,8192]{1,0:T(8,128)(2,1)S(1)} %pad_maximum_fusion.1), channel_id=1, source_target_pairs={{0,1},{1,0},{2,3},{3,2},{4,5},{5,4},{6,7},{7,6},{8,9},{9,8},{10,11... | collective-permute-start | bytes 1572872 | tf_op jit(solution)/shard_map/ppermute | solution.py:34
  45.9 1.8 %collective-permute-start.22 = (bf16[24,8192]{1,0:T(8,128)(2,1)S(1)}, bf16[24,8192]{1,0:T(8,128)(2,1)S(1)}, u32[]{:S(2)}, u32[]{:S(2)}) collective-permute-start(bf16[24,8192]{1,0:T(8,128)(2,1)S(1)} %pad_maximum_fusion.2), channel_id=1, source_target_pairs={{0,1},{1,0},{2,3},{3,2},{4,5},{5,4},{6,7},{7,6},{8,9},{9,8},{10,11... | collective-permute-start | bytes 1179656 | tf_op jit(solution)/shard_map/ppermute | solution.py:34
  47.7 1.4 %collective-permute-start.23 = (bf16[8,8192]{1,0:T(8,128)(2,1)S(1)}, bf16[8,8192]{1,0:T(8,128)(2,1)S(1)}, u32[]{:S(2)}, u32[]{:S(2)}) collective-permute-start(bf16[8,8192]{1,0:T(8,128)(2,1)S(1)} %broadcast_select_fusion), channel_id=1, source_target_pairs={{0,1},{1,0},{2,3},{3,2},{4,5},{5,4},{6,7},{7,6},{8,9},{9,8},{10,11... | collective-permute-start | bytes 393224 | tf_op jit(solution)/shard_map/ppermute | solution.py:34

commit v23 on v19

--- a/solution.py
+++ b/solution.py
@@ -45,9 +45,10 @@
     return lax.ppermute(value, AXIS, [(i, i + group) for i in range(size - group)])
 
 
-def lowered(value, group):
+def lowered(value, final, group):
     size = lax.axis_size(AXIS)
-    return lax.ppermute(value, AXIS, [(i + group, i) for i in range(size - group)])
+    came = lax.ppermute(value, AXIS, [((i + group) % size, i) for i in range(size)])
+    return jnp.where(final, jnp.zeros_like(came), came)
 
 
 def rotated_down(value, final, group):
@@ -266,7 +267,7 @@
     own_less = summed(owns, range(1, chips - 1)) - target[0].astype(jnp.float32) + crossed
 
     below = shifted(next_sum.astype(jnp.bfloat16), group).astype(jnp.float32)
-    above = lowered(own_less.astype(jnp.bfloat16), group).astype(jnp.float32)
+    above = lowered(own_less.astype(jnp.bfloat16), final, group).astype(jnp.float32)
     error = (own_less + below).astype(jnp.bfloat16)
     later = jnp.where(final, 0.0, next_sum + after(above, error)).astype(jnp.bfloat16)
 

time: 50.5 us -> 50.7 us (level)
  starting transfers between devices: 27.6 us -> 28.5 us
  waiting for transfers between devices: 10 us -> 9.39 us
    ppermute x1, waiting for transfers between devices: 1.77 us -> 0.01 us  [lowered(): lax.ppermute(value, AXIS, [((i + group) % size, i) for i in range(size)])]
    ppermute x13, waiting for transfers between devices: 2.1 us -> 3.78 us  [across(): return lax.ppermute(value, AXIS, pairs)]
    ppermute x1, starting transfers between devices: 1.29 us -> 2.3 us  [lowered(): lax.ppermute(value, AXIS, [((i + group) % size, i) for i in range(size)])]
    ppermute x1, waiting for transfers between devices: 2.34 us -> 1.71 us  [rotated_down(): lax.ppermute(value, AXIS, [((i + group) % size, i) for i in range(size)])]
  transfers between devices with their start and end apart: 24 -> 24, of which waited for: 9 -> 10; matrix products, arithmetic and copies ran while one was open for 2% -> 2% of each run, Pallas kernels for 14% -> 14%
where the time goes in v23:
time: 50.7 us; the launch traced here: 50.6 us
  starting transfers between devices  28.5 us (56%)
  Pallas kernels  9.89 us (20%)
  waiting for transfers between devices  9.39 us (19%)
  between operations  1.03 us (2%)
  matrix products  0.8 us (2%)
  other arithmetic  0.69 us (1%)
    ppermute x13, starting transfers between devices, across(): return lax.ppermute(value, AXIS, pairs)  17.9 us
    pallas_call x1, Pallas kernels, loaded(): pl.pallas_call(load_kernel, out_shape=[pltpu.VMEM(enc.shape[1:], enc.dtyp...  4.68 us
    ppermute x13, waiting for transfers between devices, across(): return lax.ppermute(value, AXIS, pairs)  3.78 us
    ppermute x1, starting transfers between devices, rotated_down(): lax.ppermute(value, AXIS, [((i + group) % size, i) for i in range(size)])  3.09 us
    ppermute x1, starting transfers between devices, shifted(): lax.ppermute(value, AXIS, [(i, i + group) for i in range(size - group)])  2.7 us
    ppermute x7, waiting for transfers between devices, other_core(): lax.ppermute(value, AXIS, [(i, i ^ 1) for i in range(lax.axis_size(AXIS))])  2.35 us
    ppermute x1, starting transfers between devices, lowered(): lax.ppermute(value, AXIS, [((i + group) % size, i) for i in range(size)])  2.3 us
    pallas_call x1, Pallas kernels, grad_all(): pl.pallas_call(functools.partial(grad_all_kernel, tokens), out_shape=jax....  2.03 us
  transfers between devices with their start and end apart: 24, of which 10 were waited for; matrix products, arithmetic and copies ran while one was open for 2% of the time, Pallas kernels for 14%

profile of v23, /device:TPU:0, one launch (start us, length us, event | category | flops | bytes accessed | tf_op | source)
XLA Modules:
  0.0 50.6 jit_solution(9378813215908457474)
XLA Ops:
  0.6 0.0 copy-start
  0.6 0.0 copy-start.1
  0.7 4.0 %collective-permute-start = (bf16[8,8192]{1,0:T(8,128)(2,1)}, bf16[8,8192]{1,0:T(8,128)(2,1)S(1)}, u32[]{:S(2)}, u32[]{:S(2)}) collective-permute-start(bf16[8,8192]{1,0:T(8,128)(2,1)} %bitcast.15), channel_id=1, source_target_pairs={{0,6},{1,7},{2,4},{3,5},{4,2},{5,3},{6,0},{7,1},{8,14},{9,15},{10,... | collective-permute-start | bytes 393224 | tf_op jit(solution)/shard_map/ppermute | solution.py:30
  4.6 0.0 collective-permute-start.3
  4.6 0.5 %collective-permute-start.2 = (bf16[8,8192]{1,0:T(8,128)(2,1)}, bf16[8,8192]{1,0:T(8,128)(2,1)S(1)}, u32[]{:S(2)}, u32[]{:S(2)}) collective-permute-start(bf16[8,8192]{1,0:T(8,128)(2,1)} %bitcast.17), channel_id=1, source_target_pairs={{0,2},{1,5},{2,0},{3,7},{4,6},{5,1},{6,4},{7,3},{8,10},{9,13},{10,... | collective-permute-start | bytes 393224 | tf_op jit(solution)/shard_map/ppermute | solution.py:30
  5.2 0.2 collective-permute-start.1
  5.3 4.7 %load_weights.1 = (bf16[8192,256]{1,0:T(8,128)(2,1)S(1)}, bf16[256,8192]{1,0:T(8,128)(2,1)S(1)}, bf16[256,8192]{1,0:T(8,128)(2,1)S(1)}) custom-call(bf16[1,8192,256]{2,1,0:T(8,128)(2,1)} %enc_hbm.1, bf16[1,2,256,8192]{3,2,1,0:T(8,128)(2,1)} %dec_hbm.1), custom_call_target="tpu_custom_call" | custom-call | bytes 25165824 | tf_op jit(solution)/shard_map/load_weights/pallas_call | solution.py:93
  10.1 0.1 gate.1
  10.2 0.0 collective-permute-done
  10.2 0.9 %collective-permute-done.1 = bf16[8,8192]{1,0:T(8,128)(2,1)S(1)} collective-permute-done((bf16[8,8192]{1,0:T(8,128)(2,1)}, bf16[8,8192]{1,0:T(8,128)(2,1)S(1)}, u32[]{:S(2)}, u32[]{:S(2)}) %collective-permute-start.1) | collective-permute-done | bytes 131104 | tf_op jit(solution)/shard_map/ppermute | solution.py:30
  11.2 0.2 collective-permute-done.2
  11.4 0.1 collective-permute-start.4
  11.5 0.0 copy-done.4
  11.6 0.0 collective-permute-done.3
  11.6 1.6 %collective-permute-done.4 = bf16[24,8192]{1,0:T(8,128)(2,1)S(1)} collective-permute-done((bf16[24,8192]{1,0:T(8,128)(2,1)S(1)}, bf16[24,8192]{1,0:T(8,128)(2,1)S(1)}, u32[]{:S(2)}, u32[]{:S(2)}) %collective-permute-start.4) | collective-permute-done | bytes 393248 | tf_op jit(solution)/shard_map/ppermute | solution.py:34
  13.2 0.8 %fusion.2.codes_ref = bf16[64,256]{1,0:T(8,128)(2,1)S(1)} fusion(f32[64,256]{1,0:T(8,128)S(1)} %get-tuple-element.28, f32[64,256]{1,0:T(8,128)S(1)} %get-tuple-element.27, bf16[64,8192]{1,0:T(8,128)(2,1)S(1)} %slice_dynamic-update-slice_fusion, bf16[8192,256]{1,0:T(8,128)(2,1)S(1)} %get-tuple-element.24), kind=kOutput, calls=%fused_computation.3 | convolution fusion | flops 268500992 | bytes 5406720 | tf_op jit(solution)/shard_map/dot_general | solution.py:256
  14.1 0.8 %decode.3 = (f32[32,8192]{1,0:T(8,128)S(1)}, bf16[32,8192]{1,0:T(8,128)(2,1)S(1)}) custom-call(bf16[64,256]{1,0:T(8,128)(2,1)S(1)} %fusion.2.codes_ref, bf16[256,8192]{1,0:T(8,128)(2,1)S(1)} %get-tuple-element.33.dec_ref), custom_call_target="tpu_custom_call" | custom-call | flops 268435456 | bytes 4194304 | tf_op jit(solution)/shard_map/decode/pallas_call | solution.py:170
  14.9 0.2 collective-permute-start.8
  15.1 0.8 %decode.2 = (f32[32,8192]{1,0:T(8,128)S(1)}, bf16[32,8192]{1,0:T(8,128)(2,1)S(1)}) custom-call(bf16[64,256]{1,0:T(8,128)(2,1)S(1)} %fusion.2.codes_ref, bf16[256,8192]{1,0:T(8,128)(2,1)S(1)} %get-tuple-element.29.dec_ref), custom_call_target="tpu_custom_call" | custom-call | flops 268435456 | bytes 4194304 | tf_op jit(solution)/shard_map/decode/pallas_call | solution.py:170
  16.0 0.4 collective-permute-start.5
  16.4 0.5 collective-permute-done.8
  16.9 0.1 fusion.9
  17.0 1.6 %collective-permute-start.9 = (bf16[8,8192]{1,0:T(8,128)(2,1)S(1)}, bf16[8,8192]{1,0:T(8,128)(2,1)S(1)}, u32[]{:S(2)}, u32[]{:S(2)}) collective-permute-start(bf16[8,8192]{1,0:T(8,128)(2,1)S(1)} %get-tuple-element.50), channel_id=1, source_target_pairs={{0,8},{1,9},{2,10},{3,11},{4,12},{5,13},{6,14},{7,15},{8,16},{9,17... | collective-permute-start | bytes 393224 | tf_op jit(solution)/shard_map/ppermute | solution.py:39
  18.7 1.5 %collective-permute-start.12 = (bf16[8,8192]{1,0:T(8,128)(2,1)S(1)}, bf16[8,8192]{1,0:T(8,128)(2,1)S(1)}, u32[]{:S(2)}, u32[]{:S(2)}) collective-permute-start(bf16[8,8192]{1,0:T(8,128)(2,1)S(1)} %get-tuple-element.51), channel_id=1, source_target_pairs={{0,4},{1,3},{2,6},{3,1},{4,0},{5,7},{6,2},{7,5},{8,12},{9,11},{10,... | collective-permute-start | bytes 393224 | tf_op jit(solution)/shard_map/ppermute | solution.py:30
  20.2 1.5 %collective-permute-start.11 = (bf16[8,8192]{1,0:T(8,128)(2,1)S(1)}, bf16[8,8192]{1,0:T(8,128)(2,1)S(1)}, u32[]{:S(2)}, u32[]{:S(2)}) collective-permute-start(bf16[8,8192]{1,0:T(8,128)(2,1)S(1)} %get-tuple-element.52), channel_id=1, source_target_pairs={{0,2},{1,5},{2,0},{3,7},{4,6},{5,1},{6,4},{7,3},{8,10},{9,13},{10,... | collective-permute-start | bytes 393224 | tf_op jit(solution)/shard_map/ppermute | solution.py:30
  21.6 0.0 collective-permute-done.5
  21.6 0.1 fusion.8
  21.8 0.6 %collective-permute-start.6 = (bf16[8,8192]{1,0:T(8,128)(2,1)S(1)}, bf16[8,8192]{1,0:T(8,128)(2,1)S(1)}, u32[]{:S(2)}, u32[]{:S(2)}) collective-permute-start(bf16[8,8192]{1,0:T(8,128)(2,1)S(1)} %get-tuple-element.48), channel_id=1, source_target_pairs={{0,2},{1,5},{2,0},{3,7},{4,6},{5,1},{6,4},{7,3},{8,10},{9,13},{10,... | collective-permute-start | bytes 393224 | tf_op jit(solution)/shard_map/ppermute | solution.py:30
  22.4 0.5 %collective-permute-start.7 = (bf16[8,8192]{1,0:T(8,128)(2,1)S(1)}, bf16[8,8192]{1,0:T(8,128)(2,1)S(1)}, u32[]{:S(2)}, u32[]{:S(2)}) collective-permute-start(bf16[8,8192]{1,0:T(8,128)(2,1)S(1)} %get-tuple-element.49), channel_id=1, source_target_pairs={{0,4},{1,3},{2,6},{3,1},{4,0},{5,7},{6,2},{7,5},{8,12},{9,11},{10,... | collective-permute-start | bytes 393224 | tf_op jit(solution)/shard_map/ppermute | solution.py:30
  22.9 1.5 %collective-permute-done.9 = bf16[8,8192]{1,0:T(8,128)(2,1)S(1)} collective-permute-done((bf16[8,8192]{1,0:T(8,128)(2,1)S(1)}, bf16[8,8192]{1,0:T(8,128)(2,1)S(1)}, u32[]{:S(2)}, u32[]{:S(2)}) %collective-permute-start.9) | collective-permute-done | bytes 131104 | tf_op jit(solution)/shard_map/ppermute | solution.py:39
  24.5 2.5 %collective-permute-start.10 = (bf16[8,8192]{1,0:T(8,128)(2,1)S(1)}, bf16[8,8192]{1,0:T(8,128)(2,1)S(1)}, u32[]{:S(2)}, u32[]{:S(2)}) collective-permute-start(bf16[8,8192]{1,0:T(8,128)(2,1)S(1)} %slice_add_fusion.1), channel_id=1, source_target_pairs={{0,6},{1,7},{2,4},{3,5},{4,2},{5,3},{6,0},{7,1},{8,14},{9,15},{10,... | collective-permute-start | bytes 393224 | tf_op jit(solution)/shard_map/ppermute | solution.py:30
  27.0 0.0 collective-permute-done.12
  27.0 0.0 collective-permute-done.11
  27.1 2.7 %collective-permute-start.13 = (bf16[8,8192]{1,0:T(8,128)(2,1)S(1)}, bf16[8,8192]{1,0:T(8,128)(2,1)S(1)}, u32[]{:S(2)}, u32[]{:S(2)}) collective-permute-start(bf16[8,8192]{1,0:T(8,128)(2,1)S(1)} %convert_element_type.71), channel_id=1, source_target_pairs={{0,8},{1,9},{2,10},{3,11},{4,12},{5,13},{6,14},{7,15},{8,16},{9,17... | collective-permute-start | bytes 393224 | tf_op jit(solution)/shard_map/ppermute | solution.py:45
  29.8 0.0 collective-permute-done.6
  29.8 0.0 collective-permute-done.7
  29.8 0.9 %collective-permute-done.10 = bf16[8,8192]{1,0:T(8,128)(2,1)S(1)} collective-permute-done((bf16[8,8192]{1,0:T(8,128)(2,1)S(1)}, bf16[8,8192]{1,0:T(8,128)(2,1)S(1)}, u32[]{:S(2)}, u32[]{:S(2)}) %collective-permute-start.10) | collective-permute-done | bytes 131104 | tf_op jit(solution)/shard_map/ppermute | solution.py:30
  30.7 0.1 fusion.7
  30.8 2.3 %collective-permute-start.14 = (bf16[8,8192]{1,0:T(8,128)(2,1)S(1)}, bf16[8,8192]{1,0:T(8,128)(2,1)S(1)}, u32[]{:S(2)}, u32[]{:S(2)}) collective-permute-start(bf16[8,8192]{1,0:T(8,128)(2,1)S(1)} %fusion.7), channel_id=1, source_target_pairs={{8,0},{9,1},{10,2},{11,3},{12,4},{13,5},{14,6},{15,7},{16,8},{17,9... | collective-permute-start | bytes 393224 | tf_op jit(solution)/shard_map/ppermute | solution.py:50
  33.1 0.0 collective-permute-done.13
  33.1 0.1 constant_dynamic-update-slice_fusion.12
  33.2 0.0 copy-start.3
  33.2 1.6 %collective-permute-start.19 = (bf16[8,8192]{1,0:T(8,128)(2,1)S(1)}, bf16[8,8192]{1,0:T(8,128)(2,1)S(1)}, u32[]{:S(2)}, u32[]{:S(2)}) collective-permute-start(bf16[8,8192]{1,0:T(8,128)(2,1)S(1)} %get-tuple-element.43), channel_id=1, source_target_pairs={{0,2},{1,5},{2,0},{3,7},{4,6},{5,1},{6,4},{7,3},{8,10},{9,13},{10,... | collective-permute-start | bytes 393224 | tf_op jit(solution)/shard_map/ppermute | solution.py:30
  34.8 1.4 %collective-permute-start.18 = (bf16[8,8192]{1,0:T(8,128)(2,1)S(1)}, bf16[8,8192]{1,0:T(8,128)(2,1)S(1)}, u32[]{:S(2)}, u32[]{:S(2)}) collective-permute-start(bf16[8,8192]{1,0:T(8,128)(2,1)S(1)} %get-tuple-element.43), channel_id=1, source_target_pairs={{0,4},{1,3},{2,6},{3,1},{4,0},{5,7},{6,2},{7,5},{8,12},{9,11},{10,... | collective-permute-start | bytes 393224 | tf_op jit(solution)/shard_map/ppermute | solution.py:30
  36.2 0.5 %collective-permute-start.17 = (bf16[8,8192]{1,0:T(8,128)(2,1)S(1)}, bf16[8,8192]{1,0:T(8,128)(2,1)S(1)}, u32[]{:S(2)}, u32[]{:S(2)}) collective-permute-start(bf16[8,8192]{1,0:T(8,128)(2,1)S(1)} %get-tuple-element.43), channel_id=1, source_target_pairs={{0,6},{1,7},{2,4},{3,5},{4,2},{5,3},{6,0},{7,1},{8,14},{9,15},{10,... | collective-permute-start | bytes 393224 | tf_op jit(solution)/shard_map/ppermute | solution.py:30
  36.8 0.0 collective-permute-done.14
  36.8 1.6 %collective-permute-start.16 = (bf16[8,8192]{1,0:T(8,128)(2,1)S(1)}, bf16[8,8192]{1,0:T(8,128)(2,1)S(1)}, u32[]{:S(2)}, u32[]{:S(2)}) collective-permute-start(bf16[8,8192]{1,0:T(8,128)(2,1)S(1)} %select_convert_fusion), channel_id=1, source_target_pairs={{0,4},{1,3},{2,6},{3,1},{4,0},{5,7},{6,2},{7,5},{8,12},{9,11},{10,... | collective-permute-start | bytes 393224 | tf_op jit(solution)/shard_map/ppermute | solution.py:30
  38.4 1.5 %collective-permute-start.15 = (bf16[8,8192]{1,0:T(8,128)(2,1)S(1)}, bf16[8,8192]{1,0:T(8,128)(2,1)S(1)}, u32[]{:S(2)}, u32[]{:S(2)}) collective-permute-start(bf16[8,8192]{1,0:T(8,128)(2,1)S(1)} %select_convert_fusion), channel_id=1, source_target_pairs={{0,6},{1,7},{2,4},{3,5},{4,2},{5,3},{6,0},{7,1},{8,14},{9,15},{10,... | collective-permute-start | bytes 393224 | tf_op jit(solution)/shard_map/ppermute | solution.py:30
  39.9 0.0 collective-permute-done.19
  39.9 3.1 %collective-permute-start.21 = (bf16[8,8192]{1,0:T(8,128)(2,1)S(1)}, bf16[8,8192]{1,0:T(8,128)(2,1)S(1)}, u32[]{:S(2)}, u32[]{:S(2)}) collective-permute-start(bf16[8,8192]{1,0:T(8,128)(2,1)S(1)} %collective-permute-done.19), channel_id=1, source_target_pairs={{8,0},{9,1},{10,2},{11,3},{12,4},{13,5},{14,6},{15,7},{16,8},{17,9... | collective-permute-start | bytes 393224 | tf_op jit(solution)/shard_map/ppermute | solution.py:56
  43.0 0.0 collective-permute-done.18
  43.0 0.6 %collective-permute-done.17 = bf16[8,8192]{1,0:T(8,128)(2,1)S(1)} collective-permute-done((bf16[8,8192]{1,0:T(8,128)(2,1)S(1)}, bf16[8,8192]{1,0:T(8,128)(2,1)S(1)}, u32[]{:S(2)}, u32[]{:S(2)}) %collective-permute-start.17) | collective-permute-done | bytes 131104 | tf_op jit(solution)/shard_map/ppermute | solution.py:30
  43.6 0.1 collective-permute-start.20
  43.8 1.7 %collective-permute-done.21 = bf16[8,8192]{1,0:T(8,128)(2,1)S(1)} collective-permute-done((bf16[8,8192]{1,0:T(8,128)(2,1)S(1)}, bf16[8,8192]{1,0:T(8,128)(2,1)S(1)}, u32[]{:S(2)}, u32[]{:S(2)}) %collective-permute-start.21) | collective-permute-done | bytes 131104 | tf_op jit(solution)/shard_map/ppermute | solution.py:56
  45.5 0.1 collective-permute-start.23
  45.6 1.1 %collective-permute-done.16 = bf16[8,8192]{1,0:T(8,128)(2,1)S(1)} collective-permute-done((bf16[8,8192]{1,0:T(8,128)(2,1)S(1)}, bf16[8,8192]{1,0:T(8,128)(2,1)S(1)}, u32[]{:S(2)}, u32[]{:S(2)}) %collective-permute-start.16) | collective-permute-done | bytes 131104 | tf_op jit(solution)/shard_map/ppermute | solution.py:30
  46.6 0.0 collective-permute-done.15
  46.7 0.0 collective-permute-done.20
  46.7 0.1 collective-permute-start.22
  46.8 1.4 %grad_own.1 = (f32[64,256]{1,0:T(8,128)S(1)}, f32[8,128]{1,0:T(8,128)}) custom-call(bf16[64,8192]{1,0:T(8,128)(2,1)S(1)} %constant_dynamic-update-slice_fusion.8.rows_ref, bf16[256,8192]{1,0:T(8,128)(2,1)S(1)} %get-tuple-element.29.dec_ref), custom_call_target="tpu_custom_call" | custom-call | flops 268435456 | bytes 4194304 | tf_op jit(solution)/shard_map/grad_own/pallas_call | solution.py:207
  48.2 0.0 collective-permute-done.23
  48.2 0.3 collective-permute-done.22
  48.5 0.1 pad_maximum_fusion.rows_ref
  48.5 2.0 %grad_all.1 = f32[1,64,256]{2,1,0:T(8,128)} custom-call(bf16[64,8192]{1,0:T(8,128)(2,1)S(1)} %pad_maximum_fusion.rows_ref, bf16[256,8192]{1,0:T(8,128)(2,1)S(1)} %get-tuple-element.33.dec_ref, f32[64,256]{1,0:T(8,128)S(1)} %get-tuple-element.41.own_ref), custom_call_target="tpu_custom_call" | custom-call | flops 268435456 | bytes 4194304 | tf_op jit(solution)/shard_map/grad_all/pallas_call | solution.py:219
  (31 shorter events, 0.5 us)
Async XLA Ops:
  0.6 9.4 %copy-start = (s32[1,2,2]{2,1,0:T(2,128)S(1)}, s32[1,2,2]{2,1,0:T(2,128)}, u32[]{:S(2)}) copy-start(s32[1,2,2]{2,1,0:T(2,128)} %param.9) | copy-start | bytes 52
  0.6 9.4 %copy-start.1 = (bf16[1,256]{1,0:T(2,128)(2,1)S(1)}, bf16[1,256]{1,0:T(2,128)(2,1)}, u32[]{:S(2)}) copy-start(bf16[1,256]{1,0:T(2,128)(2,1)} %bias_ref) | copy-start | bytes 1540
  0.7 10.8 %copy-start.4 = (bf16[1,8,8192]{2,1,0:T(8,128)(2,1)S(1)}, bf16[1,8,8192]{2,1,0:T(8,128)(2,1)}, u32[]{:S(2)}) copy-start(bf16[1,8,8192]{2,1,0:T(8,128)(2,1)} %param.6) | copy-start | bytes 393220
  0.7 9.5 %collective-permute-start = (bf16[8,8192]{1,0:T(8,128)(2,1)}, bf16[8,8192]{1,0:T(8,128)(2,1)S(1)}, u32[]{:S(2)}, u32[]{:S(2)}) collective-permute-start(bf16[8,8192]{1,0:T(8,128)(2,1)} %bitcast.15), channel_id=1, source_target_pairs={{0,6},{1,7},{2,4},{3,5},{4,2},{5,3},{6,0},{7,1},{8,14},{9,15},{10,... | collective-permute-start | bytes 393224 | tf_op jit(solution)/shard_map/ppermute | solution.py:30
  4.6 6.9 %collective-permute-start.3 = (bf16[8,8192]{1,0:T(8,128)(2,1)}, bf16[8,8192]{1,0:T(8,128)(2,1)S(1)}, u32[]{:S(2)}, u32[]{:S(2)}) collective-permute-start(bf16[8,8192]{1,0:T(8,128)(2,1)} %bitcast.16), channel_id=1, source_target_pairs={{0,1},{1,0},{2,3},{3,2},{4,5},{5,4},{6,7},{7,6},{8,9},{9,8},{10,11... | collective-permute-start | bytes 393224 | tf_op jit(solution)/shard_map/ppermute | solution.py:34
  4.6 6.8 %collective-permute-start.2 = (bf16[8,8192]{1,0:T(8,128)(2,1)}, bf16[8,8192]{1,0:T(8,128)(2,1)S(1)}, u32[]{:S(2)}, u32[]{:S(2)}) collective-permute-start(bf16[8,8192]{1,0:T(8,128)(2,1)} %bitcast.17), channel_id=1, source_target_pairs={{0,2},{1,5},{2,0},{3,7},{4,6},{5,1},{6,4},{7,3},{8,10},{9,13},{10,... | collective-permute-start | bytes 393224 | tf_op jit(solution)/shard_map/ppermute | solution.py:30
  5.2 6.0 %collective-permute-start.1 = (bf16[8,8192]{1,0:T(8,128)(2,1)}, bf16[8,8192]{1,0:T(8,128)(2,1)S(1)}, u32[]{:S(2)}, u32[]{:S(2)}) collective-permute-start(bf16[8,8192]{1,0:T(8,128)(2,1)} %bitcast.18), channel_id=1, source_target_pairs={{0,4},{1,3},{2,6},{3,1},{4,0},{5,7},{6,2},{7,5},{8,12},{9,11},{10,... | collective-permute-start | bytes 393224 | tf_op jit(solution)/shard_map/ppermute | solution.py:30
  11.4 1.8 %collective-permute-start.4 = (bf16[24,8192]{1,0:T(8,128)(2,1)S(1)}, bf16[24,8192]{1,0:T(8,128)(2,1)S(1)}, u32[]{:S(2)}, u32[]{:S(2)}) collective-permute-start(bf16[24,8192]{1,0:T(8,128)(2,1)S(1)} %constant_dynamic-update-slice_fusion), channel_id=1, source_target_pairs={{0,1},{1,0},{2,3},{3,2},{4,5},{5,4},{6,7},{7,6},{8,9},{9,8},{10,11... | collective-permute-start | bytes 1179656 | tf_op jit(solution)/shard_map/ppermute | solution.py:34
  14.9 2.0 %collective-permute-start.8 = (bf16[32,8192]{1,0:T(8,128)(2,1)S(1)}, bf16[32,8192]{1,0:T(8,128)(2,1)S(1)}, u32[]{:S(2)}, u32[]{:S(2)}) collective-permute-start(bf16[32,8192]{1,0:T(8,128)(2,1)S(1)} %get-tuple-element.35), channel_id=1, source_target_pairs={{0,1},{1,0},{2,3},{3,2},{4,5},{5,4},{6,7},{7,6},{8,9},{9,8},{10,11... | collective-permute-start | bytes 1572872 | tf_op jit(solution)/shard_map/ppermute | solution.py:34
  16.0 5.7 %collective-permute-start.5 = (bf16[32,8192]{1,0:T(8,128)(2,1)S(1)}, bf16[32,8192]{1,0:T(8,128)(2,1)S(1)}, u32[]{:S(2)}, u32[]{:S(2)}) collective-permute-start(bf16[32,8192]{1,0:T(8,128)(2,1)S(1)} %get-tuple-element.31), channel_id=1, source_target_pairs={{0,1},{1,0},{2,3},{3,2},{4,5},{5,4},{6,7},{7,6},{8,9},{9,8},{10,11... | collective-permute-start | bytes 1572872 | tf_op jit(solution)/shard_map/ppermute | solution.py:34
  16.9 13.8 %copy-start.2 = (bf16[1,8,8192]{2,1,0:T(8,128)(2,1)S(1)}, bf16[1,8,8192]{2,1,0:T(8,128)(2,1)}, u32[]{:S(2)}) copy-start(bf16[1,8,8192]{2,1,0:T(8,128)(2,1)} %param.11) | copy-start | bytes 393220
  17.0 7.5 %collective-permute-start.9 = (bf16[8,8192]{1,0:T(8,128)(2,1)S(1)}, bf16[8,8192]{1,0:T(8,128)(2,1)S(1)}, u32[]{:S(2)}, u32[]{:S(2)}) collective-permute-start(bf16[8,8192]{1,0:T(8,128)(2,1)S(1)} %get-tuple-element.50), channel_id=1, source_target_pairs={{0,8},{1,9},{2,10},{3,11},{4,12},{5,13},{6,14},{7,15},{8,16},{9,17... | collective-permute-start | bytes 393224 | tf_op jit(solution)/shard_map/ppermute | solution.py:39
  18.7 8.3 %collective-permute-start.12 = (bf16[8,8192]{1,0:T(8,128)(2,1)S(1)}, bf16[8,8192]{1,0:T(8,128)(2,1)S(1)}, u32[]{:S(2)}, u32[]{:S(2)}) collective-permute-start(bf16[8,8192]{1,0:T(8,128)(2,1)S(1)} %get-tuple-element.51), channel_id=1, source_target_pairs={{0,4},{1,3},{2,6},{3,1},{4,0},{5,7},{6,2},{7,5},{8,12},{9,11},{10,... | collective-permute-start | bytes 393224 | tf_op jit(solution)/shard_map/ppermute | solution.py:30
  20.2 6.9 %collective-permute-start.11 = (bf16[8,8192]{1,0:T(8,128)(2,1)S(1)}, bf16[8,8192]{1,0:T(8,128)(2,1)S(1)}, u32[]{:S(2)}, u32[]{:S(2)}) collective-permute-start(bf16[8,8192]{1,0:T(8,128)(2,1)S(1)} %get-tuple-element.52), channel_id=1, source_target_pairs={{0,2},{1,5},{2,0},{3,7},{4,6},{5,1},{6,4},{7,3},{8,10},{9,13},{10,... | collective-permute-start | bytes 393224 | tf_op jit(solution)/shard_map/ppermute | solution.py:30
  21.8 8.0 %collective-permute-start.6 = (bf16[8,8192]{1,0:T(8,128)(2,1)S(1)}, bf16[8,8192]{1,0:T(8,128)(2,1)S(1)}, u32[]{:S(2)}, u32[]{:S(2)}) collective-permute-start(bf16[8,8192]{1,0:T(8,128)(2,1)S(1)} %get-tuple-element.48), channel_id=1, source_target_pairs={{0,2},{1,5},{2,0},{3,7},{4,6},{5,1},{6,4},{7,3},{8,10},{9,13},{10,... | collective-permute-start | bytes 393224 | tf_op jit(solution)/shard_map/ppermute | solution.py:30
  22.4 7.4 %collective-permute-start.7 = (bf16[8,8192]{1,0:T(8,128)(2,1)S(1)}, bf16[8,8192]{1,0:T(8,128)(2,1)S(1)}, u32[]{:S(2)}, u32[]{:S(2)}) collective-permute-start(bf16[8,8192]{1,0:T(8,128)(2,1)S(1)} %get-tuple-element.49), channel_id=1, source_target_pairs={{0,4},{1,3},{2,6},{3,1},{4,0},{5,7},{6,2},{7,5},{8,12},{9,11},{10,... | collective-permute-start | bytes 393224 | tf_op jit(solution)/shard_map/ppermute | solution.py:30
  24.5 6.2 %collective-permute-start.10 = (bf16[8,8192]{1,0:T(8,128)(2,1)S(1)}, bf16[8,8192]{1,0:T(8,128)(2,1)S(1)}, u32[]{:S(2)}, u32[]{:S(2)}) collective-permute-start(bf16[8,8192]{1,0:T(8,128)(2,1)S(1)} %slice_add_fusion.1), channel_id=1, source_target_pairs={{0,6},{1,7},{2,4},{3,5},{4,2},{5,3},{6,0},{7,1},{8,14},{9,15},{10,... | collective-permute-start | bytes 393224 | tf_op jit(solution)/shard_map/ppermute | solution.py:30
  27.1 6.0 %collective-permute-start.13 = (bf16[8,8192]{1,0:T(8,128)(2,1)S(1)}, bf16[8,8192]{1,0:T(8,128)(2,1)S(1)}, u32[]{:S(2)}, u32[]{:S(2)}) collective-permute-start(bf16[8,8192]{1,0:T(8,128)(2,1)S(1)} %convert_element_type.71), channel_id=1, source_target_pairs={{0,8},{1,9},{2,10},{3,11},{4,12},{5,13},{6,14},{7,15},{8,16},{9,17... | collective-permute-start | bytes 393224 | tf_op jit(solution)/shard_map/ppermute | solution.py:45
  30.8 6.0 %collective-permute-start.14 = (bf16[8,8192]{1,0:T(8,128)(2,1)S(1)}, bf16[8,8192]{1,0:T(8,128)(2,1)S(1)}, u32[]{:S(2)}, u32[]{:S(2)}) collective-permute-start(bf16[8,8192]{1,0:T(8,128)(2,1)S(1)} %fusion.7), channel_id=1, source_target_pairs={{8,0},{9,1},{10,2},{11,3},{12,4},{13,5},{14,6},{15,7},{16,8},{17,9... | collective-permute-start | bytes 393224 | tf_op jit(solution)/shard_map/ppermute | solution.py:50
  33.2 15.0 %copy-start.3 = (bf16[8,8192]{1,0:T(8,128)(2,1)}, bf16[8,8192]{1,0:T(8,128)(2,1)S(1)}, u32[]{:S(2)}) copy-start(bf16[8,8192]{1,0:T(8,128)(2,1)S(1)} %get-tuple-element.43) | copy-start | bytes 393220
  33.2 6.7 %collective-permute-start.19 = (bf16[8,8192]{1,0:T(8,128)(2,1)S(1)}, bf16[8,8192]{1,0:T(8,128)(2,1)S(1)}, u32[]{:S(2)}, u32[]{:S(2)}) collective-permute-start(bf16[8,8192]{1,0:T(8,128)(2,1)S(1)} %get-tuple-element.43), channel_id=1, source_target_pairs={{0,2},{1,5},{2,0},{3,7},{4,6},{5,1},{6,4},{7,3},{8,10},{9,13},{10,... | collective-permute-start | bytes 393224 | tf_op jit(solution)/shard_map/ppermute | solution.py:30
  34.8 8.2 %collective-permute-start.18 = (bf16[8,8192]{1,0:T(8,128)(2,1)S(1)}, bf16[8,8192]{1,0:T(8,128)(2,1)S(1)}, u32[]{:S(2)}, u32[]{:S(2)}) collective-permute-start(bf16[8,8192]{1,0:T(8,128)(2,1)S(1)} %get-tuple-element.43), channel_id=1, source_target_pairs={{0,4},{1,3},{2,6},{3,1},{4,0},{5,7},{6,2},{7,5},{8,12},{9,11},{10,... | collective-permute-start | bytes 393224 | tf_op jit(solution)/shard_map/ppermute | solution.py:30
  36.2 7.4 %collective-permute-start.17 = (bf16[8,8192]{1,0:T(8,128)(2,1)S(1)}, bf16[8,8192]{1,0:T(8,128)(2,1)S(1)}, u32[]{:S(2)}, u32[]{:S(2)}) collective-permute-start(bf16[8,8192]{1,0:T(8,128)(2,1)S(1)} %get-tuple-element.43), channel_id=1, source_target_pairs={{0,6},{1,7},{2,4},{3,5},{4,2},{5,3},{6,0},{7,1},{8,14},{9,15},{10,... | collective-permute-start | bytes 393224 | tf_op jit(solution)/shard_map/ppermute | solution.py:30
  36.8 9.8 %collective-permute-start.16 = (bf16[8,8192]{1,0:T(8,128)(2,1)S(1)}, bf16[8,8192]{1,0:T(8,128)(2,1)S(1)}, u32[]{:S(2)}, u32[]{:S(2)}) collective-permute-start(bf16[8,8192]{1,0:T(8,128)(2,1)S(1)} %select_convert_fusion), channel_id=1, source_target_pairs={{0,4},{1,3},{2,6},{3,1},{4,0},{5,7},{6,2},{7,5},{8,12},{9,11},{10,... | collective-permute-start | bytes 393224 | tf_op jit(solution)/shard_map/ppermute | solution.py:30
  38.4 8.2 %collective-permute-start.15 = (bf16[8,8192]{1,0:T(8,128)(2,1)S(1)}, bf16[8,8192]{1,0:T(8,128)(2,1)S(1)}, u32[]{:S(2)}, u32[]{:S(2)}) collective-permute-start(bf16[8,8192]{1,0:T(8,128)(2,1)S(1)} %select_convert_fusion), channel_id=1, source_target_pairs={{0,6},{1,7},{2,4},{3,5},{4,2},{5,3},{6,0},{7,1},{8,14},{9,15},{10,... | collective-permute-start | bytes 393224 | tf_op jit(solution)/shard_map/ppermute | solution.py:30
  39.9 5.6 %collective-permute-start.21 = (bf16[8,8192]{1,0:T(8,128)(2,1)S(1)}, bf16[8,8192]{1,0:T(8,128)(2,1)S(1)}, u32[]{:S(2)}, u32[]{:S(2)}) collective-permute-start(bf16[8,8192]{1,0:T(8,128)(2,1)S(1)} %collective-permute-done.19), channel_id=1, source_target_pairs={{8,0},{9,1},{10,2},{11,3},{12,4},{13,5},{14,6},{15,7},{16,8},{17,9... | collective-permute-start | bytes 393224 | tf_op jit(solution)/shard_map/ppermute | solution.py:56
  43.6 3.0 %collective-permute-start.20 = (bf16[32,8192]{1,0:T(8,128)(2,1)S(1)}, bf16[32,8192]{1,0:T(8,128)(2,1)S(1)}, u32[]{:S(2)}, u32[]{:S(2)}) collective-permute-start(bf16[32,8192]{1,0:T(8,128)(2,1)S(1)} %pad_maximum_fusion.1), channel_id=1, source_target_pairs={{0,1},{1,0},{2,3},{3,2},{4,5},{5,4},{6,7},{7,6},{8,9},{9,8},{10,11... | collective-permute-start | bytes 1572872 | tf_op jit(solution)/shard_map/ppermute | solution.py:34
  45.5 2.7 %collective-permute-start.23 = (bf16[8,8192]{1,0:T(8,128)(2,1)S(1)}, bf16[8,8192]{1,0:T(8,128)(2,1)S(1)}, u32[]{:S(2)}, u32[]{:S(2)}) collective-permute-start(bf16[8,8192]{1,0:T(8,128)(2,1)S(1)} %broadcast_select_fusion), channel_id=1, source_target_pairs={{0,1},{1,0},{2,3},{3,2},{4,5},{5,4},{6,7},{7,6},{8,9},{9,8},{10,11... | collective-permute-start | bytes 393224 | tf_op jit(solution)/shard_map/ppermute | solution.py:34
  46.7 1.8 %collective-permute-start.22 = (bf16[24,8192]{1,0:T(8,128)(2,1)S(1)}, bf16[24,8192]{1,0:T(8,128)(2,1)S(1)}, u32[]{:S(2)}, u32[]{:S(2)}) collective-permute-start(bf16[24,8192]{1,0:T(8,128)(2,1)S(1)} %pad_maximum_fusion.2), channel_id=1, source_target_pairs={{0,1},{1,0},{2,3},{3,2},{4,5},{5,4},{6,7},{7,6},{8,9},{9,8},{10,11... | collective-permute-start | bytes 1179656 | tf_op jit(solution)/shard_map/ppermute | solution.py:34

commit v24 on v23

--- a/solution.py
+++ b/solution.py
@@ -196,7 +196,8 @@
     group = total.shape[0] // tokens
     for block in range(group):
         chips = group // CORES
-        label = (chips - block % chips) % chips
+        row = block % chips
+        label = row % (chips - 1) + 1 if row else 0
         slab = slab_of(place_in(group), block // chips * chips + label, chips)
         where = pl.ds(pl.multiple_of(slab * tokens, tokens), tokens)
         out_ref[0, where, :] = total[block * tokens : (block + 1) * tokens]
@@ -271,12 +272,12 @@
     error = (own_less + below).astype(jnp.bfloat16)
     later = jnp.where(final, 0.0, next_sum + after(above, error)).astype(jnp.bfloat16)
 
-    heres = [error] + [across(error, chip, chips) for chip in range(chips - 1, 0, -1)]
+    heres = [error] + [across(error, chip, chips) for chip in [*range(2, chips), 1]]
     passed = rotated_down(after(heres[-1], later), final, group)
     here_near = jnp.concatenate(heres, axis=0)
     here_far = other_core(here_near)
     here_rows = jnp.concatenate([here_near, here_far], axis=0)
-    straight = [across(later, chip, chips) for chip in range(chips - 1, 1, -1)]
+    straight = [across(later, chip, chips) for chip in range(2, chips)]
     most = after(jnp.concatenate([later] + straight, axis=0), here_far)
     after_rows = jnp.concatenate([most, passed, other_core(most), other_core(passed)], axis=0)
     grad = grad_all(after_rows, next_dec, grad_own(here_rows, own_dec), tokens)

time: 50.7 us -> 50.9 us (level)
    ppermute x13, waiting for transfers between devices: 3.78 us -> 4.95 us  [across(): return lax.ppermute(value, AXIS, pairs)]
    ppermute x1, waiting for transfers between devices: 1.71 us -> 0.72 us  [rotated_down(): lax.ppermute(value, AXIS, [((i + group) % size, i) for i in range(size)])]
  transfers between devices with their start and end apart: 24 -> 24, of which waited for: 10 -> 12; matrix products, arithmetic and copies ran while one was open for 2% -> 2% of each run, Pallas kernels for 14% -> 14%
where the time goes in v24:
time: 50.9 us; the launch traced here: 50.7 us
  starting transfers between devices  28.5 us (56%)
  Pallas kernels  9.89 us (19%)
  waiting for transfers between devices  9.56 us (19%)
  between operations  1.03 us (2%)
  matrix products  0.8 us (2%)
  other arithmetic  0.69 us (1%)
    ppermute x13, starting transfers between devices, across(): return lax.ppermute(value, AXIS, pairs)  17.9 us
    ppermute x13, waiting for transfers between devices, across(): return lax.ppermute(value, AXIS, pairs)  4.95 us
    pallas_call x1, Pallas kernels, loaded(): pl.pallas_call(load_kernel, out_shape=[pltpu.VMEM(enc.shape[1:], enc.dtyp...  4.68 us
    ppermute x1, starting transfers between devices, rotated_down(): lax.ppermute(value, AXIS, [((i + group) % size, i) for i in range(size)])  3.06 us
    ppermute x1, starting transfers between devices, shifted(): lax.ppermute(value, AXIS, [(i, i + group) for i in range(size - group)])  2.7 us
    ppermute x7, waiting for transfers between devices, other_core(): lax.ppermute(value, AXIS, [(i, i ^ 1) for i in range(lax.axis_size(AXIS))])  2.35 us
    ppermute x1, starting transfers between devices, lowered(): lax.ppermute(value, AXIS, [((i + group) % size, i) for i in range(size)])  2.3 us
    pallas_call x1, Pallas kernels, grad_all(): pl.pallas_call(functools.partial(grad_all_kernel, tokens), out_shape=jax....  2.03 us
  transfers between devices with their start and end apart: 24, of which 12 were waited for; matrix products, arithmetic and copies ran while one was open for 2% of the time, Pallas kernels for 14%

profile of v24, /device:TPU:0, one launch (start us, length us, event | category | flops | bytes accessed | tf_op | source)
XLA Modules:
  0.0 50.7 jit_solution(11112476083822236152)
XLA Ops:
  0.6 0.0 copy-start
  0.6 0.0 copy-start.1
  0.7 4.0 %collective-permute-start = (bf16[8,8192]{1,0:T(8,128)(2,1)}, bf16[8,8192]{1,0:T(8,128)(2,1)S(1)}, u32[]{:S(2)}, u32[]{:S(2)}) collective-permute-start(bf16[8,8192]{1,0:T(8,128)(2,1)} %bitcast.15), channel_id=1, source_target_pairs={{0,6},{1,7},{2,4},{3,5},{4,2},{5,3},{6,0},{7,1},{8,14},{9,15},{10,... | collective-permute-start | bytes 393224 | tf_op jit(solution)/shard_map/ppermute | solution.py:30
  4.6 0.0 collective-permute-start.3
  4.6 0.5 %collective-permute-start.2 = (bf16[8,8192]{1,0:T(8,128)(2,1)}, bf16[8,8192]{1,0:T(8,128)(2,1)S(1)}, u32[]{:S(2)}, u32[]{:S(2)}) collective-permute-start(bf16[8,8192]{1,0:T(8,128)(2,1)} %bitcast.17), channel_id=1, source_target_pairs={{0,2},{1,5},{2,0},{3,7},{4,6},{5,1},{6,4},{7,3},{8,10},{9,13},{10,... | collective-permute-start | bytes 393224 | tf_op jit(solution)/shard_map/ppermute | solution.py:30
  5.2 0.2 collective-permute-start.1
  5.3 4.7 %load_weights.1 = (bf16[8192,256]{1,0:T(8,128)(2,1)S(1)}, bf16[256,8192]{1,0:T(8,128)(2,1)S(1)}, bf16[256,8192]{1,0:T(8,128)(2,1)S(1)}) custom-call(bf16[1,8192,256]{2,1,0:T(8,128)(2,1)} %enc_hbm.1, bf16[1,2,256,8192]{3,2,1,0:T(8,128)(2,1)} %dec_hbm.1), custom_call_target="tpu_custom_call" | custom-call | bytes 25165824 | tf_op jit(solution)/shard_map/load_weights/pallas_call | solution.py:93
  10.1 0.1 gate.1
  10.2 0.0 collective-permute-done
  10.2 0.9 %collective-permute-done.1 = bf16[8,8192]{1,0:T(8,128)(2,1)S(1)} collective-permute-done((bf16[8,8192]{1,0:T(8,128)(2,1)}, bf16[8,8192]{1,0:T(8,128)(2,1)S(1)}, u32[]{:S(2)}, u32[]{:S(2)}) %collective-permute-start.1) | collective-permute-done | bytes 131104 | tf_op jit(solution)/shard_map/ppermute | solution.py:30
  11.2 0.2 collective-permute-done.2
  11.4 0.1 collective-permute-start.4
  11.5 0.0 copy-done.4
  11.6 0.0 collective-permute-done.3
  11.6 1.6 %collective-permute-done.4 = bf16[24,8192]{1,0:T(8,128)(2,1)S(1)} collective-permute-done((bf16[24,8192]{1,0:T(8,128)(2,1)S(1)}, bf16[24,8192]{1,0:T(8,128)(2,1)S(1)}, u32[]{:S(2)}, u32[]{:S(2)}) %collective-permute-start.4) | collective-permute-done | bytes 393248 | tf_op jit(solution)/shard_map/ppermute | solution.py:34
  13.2 0.8 %fusion.2.codes_ref = bf16[64,256]{1,0:T(8,128)(2,1)S(1)} fusion(f32[64,256]{1,0:T(8,128)S(1)} %get-tuple-element.28, f32[64,256]{1,0:T(8,128)S(1)} %get-tuple-element.27, bf16[64,8192]{1,0:T(8,128)(2,1)S(1)} %slice_dynamic-update-slice_fusion, bf16[8192,256]{1,0:T(8,128)(2,1)S(1)} %get-tuple-element.24), kind=kOutput, calls=%fused_computation.3 | convolution fusion | flops 268500992 | bytes 5406720 | tf_op jit(solution)/shard_map/dot_general | solution.py:257
  14.1 0.8 %decode.3 = (f32[32,8192]{1,0:T(8,128)S(1)}, bf16[32,8192]{1,0:T(8,128)(2,1)S(1)}) custom-call(bf16[64,256]{1,0:T(8,128)(2,1)S(1)} %fusion.2.codes_ref, bf16[256,8192]{1,0:T(8,128)(2,1)S(1)} %get-tuple-element.33.dec_ref), custom_call_target="tpu_custom_call" | custom-call | flops 268435456 | bytes 4194304 | tf_op jit(solution)/shard_map/decode/pallas_call | solution.py:170
  14.9 0.2 collective-permute-start.8
  15.1 0.8 %decode.2 = (f32[32,8192]{1,0:T(8,128)S(1)}, bf16[32,8192]{1,0:T(8,128)(2,1)S(1)}) custom-call(bf16[64,256]{1,0:T(8,128)(2,1)S(1)} %fusion.2.codes_ref, bf16[256,8192]{1,0:T(8,128)(2,1)S(1)} %get-tuple-element.29.dec_ref), custom_call_target="tpu_custom_call" | custom-call | flops 268435456 | bytes 4194304 | tf_op jit(solution)/shard_map/decode/pallas_call | solution.py:170
  16.0 0.4 collective-permute-start.5
  16.4 0.5 collective-permute-done.8
  16.9 0.1 fusion.9
  17.0 1.6 %collective-permute-start.9 = (bf16[8,8192]{1,0:T(8,128)(2,1)S(1)}, bf16[8,8192]{1,0:T(8,128)(2,1)S(1)}, u32[]{:S(2)}, u32[]{:S(2)}) collective-permute-start(bf16[8,8192]{1,0:T(8,128)(2,1)S(1)} %get-tuple-element.50), channel_id=1, source_target_pairs={{0,8},{1,9},{2,10},{3,11},{4,12},{5,13},{6,14},{7,15},{8,16},{9,17... | collective-permute-start | bytes 393224 | tf_op jit(solution)/shard_map/ppermute | solution.py:39
  18.7 1.5 %collective-permute-start.12 = (bf16[8,8192]{1,0:T(8,128)(2,1)S(1)}, bf16[8,8192]{1,0:T(8,128)(2,1)S(1)}, u32[]{:S(2)}, u32[]{:S(2)}) collective-permute-start(bf16[8,8192]{1,0:T(8,128)(2,1)S(1)} %get-tuple-element.51), channel_id=1, source_target_pairs={{0,4},{1,3},{2,6},{3,1},{4,0},{5,7},{6,2},{7,5},{8,12},{9,11},{10,... | collective-permute-start | bytes 393224 | tf_op jit(solution)/shard_map/ppermute | solution.py:30
  20.2 1.5 %collective-permute-start.11 = (bf16[8,8192]{1,0:T(8,128)(2,1)S(1)}, bf16[8,8192]{1,0:T(8,128)(2,1)S(1)}, u32[]{:S(2)}, u32[]{:S(2)}) collective-permute-start(bf16[8,8192]{1,0:T(8,128)(2,1)S(1)} %get-tuple-element.52), channel_id=1, source_target_pairs={{0,2},{1,5},{2,0},{3,7},{4,6},{5,1},{6,4},{7,3},{8,10},{9,13},{10,... | collective-permute-start | bytes 393224 | tf_op jit(solution)/shard_map/ppermute | solution.py:30
  21.6 0.0 collective-permute-done.5
  21.6 0.1 fusion.8
  21.8 0.6 %collective-permute-start.6 = (bf16[8,8192]{1,0:T(8,128)(2,1)S(1)}, bf16[8,8192]{1,0:T(8,128)(2,1)S(1)}, u32[]{:S(2)}, u32[]{:S(2)}) collective-permute-start(bf16[8,8192]{1,0:T(8,128)(2,1)S(1)} %get-tuple-element.48), channel_id=1, source_target_pairs={{0,2},{1,5},{2,0},{3,7},{4,6},{5,1},{6,4},{7,3},{8,10},{9,13},{10,... | collective-permute-start | bytes 393224 | tf_op jit(solution)/shard_map/ppermute | solution.py:30
  22.4 0.5 %collective-permute-start.7 = (bf16[8,8192]{1,0:T(8,128)(2,1)S(1)}, bf16[8,8192]{1,0:T(8,128)(2,1)S(1)}, u32[]{:S(2)}, u32[]{:S(2)}) collective-permute-start(bf16[8,8192]{1,0:T(8,128)(2,1)S(1)} %get-tuple-element.49), channel_id=1, source_target_pairs={{0,4},{1,3},{2,6},{3,1},{4,0},{5,7},{6,2},{7,5},{8,12},{9,11},{10,... | collective-permute-start | bytes 393224 | tf_op jit(solution)/shard_map/ppermute | solution.py:30
  22.9 1.5 %collective-permute-done.9 = bf16[8,8192]{1,0:T(8,128)(2,1)S(1)} collective-permute-done((bf16[8,8192]{1,0:T(8,128)(2,1)S(1)}, bf16[8,8192]{1,0:T(8,128)(2,1)S(1)}, u32[]{:S(2)}, u32[]{:S(2)}) %collective-permute-start.9) | collective-permute-done | bytes 131104 | tf_op jit(solution)/shard_map/ppermute | solution.py:39
  24.5 2.5 %collective-permute-start.10 = (bf16[8,8192]{1,0:T(8,128)(2,1)S(1)}, bf16[8,8192]{1,0:T(8,128)(2,1)S(1)}, u32[]{:S(2)}, u32[]{:S(2)}) collective-permute-start(bf16[8,8192]{1,0:T(8,128)(2,1)S(1)} %slice_add_fusion.1), channel_id=1, source_target_pairs={{0,6},{1,7},{2,4},{3,5},{4,2},{5,3},{6,0},{7,1},{8,14},{9,15},{10,... | collective-permute-start | bytes 393224 | tf_op jit(solution)/shard_map/ppermute | solution.py:30
  27.0 0.0 collective-permute-done.12
  27.0 0.0 collective-permute-done.11
  27.1 2.7 %collective-permute-start.13 = (bf16[8,8192]{1,0:T(8,128)(2,1)S(1)}, bf16[8,8192]{1,0:T(8,128)(2,1)S(1)}, u32[]{:S(2)}, u32[]{:S(2)}) collective-permute-start(bf16[8,8192]{1,0:T(8,128)(2,1)S(1)} %convert_element_type.71), channel_id=1, source_target_pairs={{0,8},{1,9},{2,10},{3,11},{4,12},{5,13},{6,14},{7,15},{8,16},{9,17... | collective-permute-start | bytes 393224 | tf_op jit(solution)/shard_map/ppermute | solution.py:45
  29.8 0.0 collective-permute-done.6
  29.8 0.0 collective-permute-done.7
  29.8 0.9 %collective-permute-done.10 = bf16[8,8192]{1,0:T(8,128)(2,1)S(1)} collective-permute-done((bf16[8,8192]{1,0:T(8,128)(2,1)S(1)}, bf16[8,8192]{1,0:T(8,128)(2,1)S(1)}, u32[]{:S(2)}, u32[]{:S(2)}) %collective-permute-start.10) | collective-permute-done | bytes 131104 | tf_op jit(solution)/shard_map/ppermute | solution.py:30
  30.7 0.1 fusion.7
  30.8 2.3 %collective-permute-start.14 = (bf16[8,8192]{1,0:T(8,128)(2,1)S(1)}, bf16[8,8192]{1,0:T(8,128)(2,1)S(1)}, u32[]{:S(2)}, u32[]{:S(2)}) collective-permute-start(bf16[8,8192]{1,0:T(8,128)(2,1)S(1)} %fusion.7), channel_id=1, source_target_pairs={{8,0},{9,1},{10,2},{11,3},{12,4},{13,5},{14,6},{15,7},{16,8},{17,9... | collective-permute-start | bytes 393224 | tf_op jit(solution)/shard_map/ppermute | solution.py:50
  33.1 0.0 collective-permute-done.13
  33.1 0.1 constant_dynamic-update-slice_fusion.12
  33.2 0.0 copy-start.3
  33.2 1.6 %collective-permute-start.19 = (bf16[8,8192]{1,0:T(8,128)(2,1)S(1)}, bf16[8,8192]{1,0:T(8,128)(2,1)S(1)}, u32[]{:S(2)}, u32[]{:S(2)}) collective-permute-start(bf16[8,8192]{1,0:T(8,128)(2,1)S(1)} %get-tuple-element.43), channel_id=1, source_target_pairs={{0,2},{1,5},{2,0},{3,7},{4,6},{5,1},{6,4},{7,3},{8,10},{9,13},{10,... | collective-permute-start | bytes 393224 | tf_op jit(solution)/shard_map/ppermute | solution.py:30
  34.8 1.4 %collective-permute-start.18 = (bf16[8,8192]{1,0:T(8,128)(2,1)S(1)}, bf16[8,8192]{1,0:T(8,128)(2,1)S(1)}, u32[]{:S(2)}, u32[]{:S(2)}) collective-permute-start(bf16[8,8192]{1,0:T(8,128)(2,1)S(1)} %get-tuple-element.43), channel_id=1, source_target_pairs={{0,6},{1,7},{2,4},{3,5},{4,2},{5,3},{6,0},{7,1},{8,14},{9,15},{10,... | collective-permute-start | bytes 393224 | tf_op jit(solution)/shard_map/ppermute | solution.py:30
  36.2 0.5 %collective-permute-start.17 = (bf16[8,8192]{1,0:T(8,128)(2,1)S(1)}, bf16[8,8192]{1,0:T(8,128)(2,1)S(1)}, u32[]{:S(2)}, u32[]{:S(2)}) collective-permute-start(bf16[8,8192]{1,0:T(8,128)(2,1)S(1)} %get-tuple-element.43), channel_id=1, source_target_pairs={{0,4},{1,3},{2,6},{3,1},{4,0},{5,7},{6,2},{7,5},{8,12},{9,11},{10,... | collective-permute-start | bytes 393224 | tf_op jit(solution)/shard_map/ppermute | solution.py:30
  36.8 0.0 collective-permute-done.14
  36.8 2.5 %collective-permute-start.16 = (bf16[8,8192]{1,0:T(8,128)(2,1)S(1)}, bf16[8,8192]{1,0:T(8,128)(2,1)S(1)}, u32[]{:S(2)}, u32[]{:S(2)}) collective-permute-start(bf16[8,8192]{1,0:T(8,128)(2,1)S(1)} %select_convert_fusion), channel_id=1, source_target_pairs={{0,6},{1,7},{2,4},{3,5},{4,2},{5,3},{6,0},{7,1},{8,14},{9,15},{10,... | collective-permute-start | bytes 393224 | tf_op jit(solution)/shard_map/ppermute | solution.py:30
  39.3 0.6 %collective-permute-start.15 = (bf16[8,8192]{1,0:T(8,128)(2,1)S(1)}, bf16[8,8192]{1,0:T(8,128)(2,1)S(1)}, u32[]{:S(2)}, u32[]{:S(2)}) collective-permute-start(bf16[8,8192]{1,0:T(8,128)(2,1)S(1)} %select_convert_fusion), channel_id=1, source_target_pairs={{0,4},{1,3},{2,6},{3,1},{4,0},{5,7},{6,2},{7,5},{8,12},{9,11},{10,... | collective-permute-start | bytes 393224 | tf_op jit(solution)/shard_map/ppermute | solution.py:30
  39.9 0.0 collective-permute-done.19
  39.9 3.1 %collective-permute-start.21 = (bf16[8,8192]{1,0:T(8,128)(2,1)S(1)}, bf16[8,8192]{1,0:T(8,128)(2,1)S(1)}, u32[]{:S(2)}, u32[]{:S(2)}) collective-permute-start(bf16[8,8192]{1,0:T(8,128)(2,1)S(1)} %collective-permute-done.19), channel_id=1, source_target_pairs={{8,0},{9,1},{10,2},{11,3},{12,4},{13,5},{14,6},{15,7},{16,8},{17,9... | collective-permute-start | bytes 393224 | tf_op jit(solution)/shard_map/ppermute | solution.py:56
  43.0 0.5 collective-permute-done.18
  43.5 1.1 %collective-permute-done.17 = bf16[8,8192]{1,0:T(8,128)(2,1)S(1)} collective-permute-done((bf16[8,8192]{1,0:T(8,128)(2,1)S(1)}, bf16[8,8192]{1,0:T(8,128)(2,1)S(1)}, u32[]{:S(2)}, u32[]{:S(2)}) %collective-permute-start.17) | collective-permute-done | bytes 131104 | tf_op jit(solution)/shard_map/ppermute | solution.py:30
  44.6 0.1 collective-permute-start.20
  44.8 0.7 %collective-permute-done.21 = bf16[8,8192]{1,0:T(8,128)(2,1)S(1)} collective-permute-done((bf16[8,8192]{1,0:T(8,128)(2,1)S(1)}, bf16[8,8192]{1,0:T(8,128)(2,1)S(1)}, u32[]{:S(2)}, u32[]{:S(2)}) %collective-permute-start.21) | collective-permute-done | bytes 131104 | tf_op jit(solution)/shard_map/ppermute | solution.py:56
  45.5 0.1 collective-permute-start.23
  45.6 0.6 %collective-permute-done.16 = bf16[8,8192]{1,0:T(8,128)(2,1)S(1)} collective-permute-done((bf16[8,8192]{1,0:T(8,128)(2,1)S(1)}, bf16[8,8192]{1,0:T(8,128)(2,1)S(1)}, u32[]{:S(2)}, u32[]{:S(2)}) %collective-permute-start.16) | collective-permute-done | bytes 131104 | tf_op jit(solution)/shard_map/ppermute | solution.py:30
  46.2 0.6 %collective-permute-done.15 = bf16[8,8192]{1,0:T(8,128)(2,1)S(1)} collective-permute-done((bf16[8,8192]{1,0:T(8,128)(2,1)S(1)}, bf16[8,8192]{1,0:T(8,128)(2,1)S(1)}, u32[]{:S(2)}, u32[]{:S(2)}) %collective-permute-start.15) | collective-permute-done | bytes 131104 | tf_op jit(solution)/shard_map/ppermute | solution.py:30
  46.8 0.0 collective-permute-done.20
  46.9 0.1 collective-permute-start.22
  47.0 1.4 %grad_own.1 = (f32[64,256]{1,0:T(8,128)S(1)}, f32[8,128]{1,0:T(8,128)}) custom-call(bf16[64,8192]{1,0:T(8,128)(2,1)S(1)} %constant_dynamic-update-slice_fusion.8.rows_ref, bf16[256,8192]{1,0:T(8,128)(2,1)S(1)} %get-tuple-element.29.dec_ref), custom_call_target="tpu_custom_call" | custom-call | flops 268435456 | bytes 4194304 | tf_op jit(solution)/shard_map/grad_own/pallas_call | solution.py:208
  48.4 0.0 collective-permute-done.23
  48.4 0.2 collective-permute-done.22
  48.6 0.1 pad_maximum_fusion.rows_ref
  48.7 2.0 %grad_all.1 = f32[1,64,256]{2,1,0:T(8,128)} custom-call(bf16[64,8192]{1,0:T(8,128)(2,1)S(1)} %pad_maximum_fusion.rows_ref, bf16[256,8192]{1,0:T(8,128)(2,1)S(1)} %get-tuple-element.33.dec_ref, f32[64,256]{1,0:T(8,128)S(1)} %get-tuple-element.41.own_ref), custom_call_target="tpu_custom_call" | custom-call | flops 268435456 | bytes 4194304 | tf_op jit(solution)/shard_map/grad_all/pallas_call | solution.py:220
  (31 shorter events, 0.5 us)
Async XLA Ops:
  0.6 9.4 %copy-start = (s32[1,2,2]{2,1,0:T(2,128)S(1)}, s32[1,2,2]{2,1,0:T(2,128)}, u32[]{:S(2)}) copy-start(s32[1,2,2]{2,1,0:T(2,128)} %param.9) | copy-start | bytes 52
  0.6 9.4 %copy-start.1 = (bf16[1,256]{1,0:T(2,128)(2,1)S(1)}, bf16[1,256]{1,0:T(2,128)(2,1)}, u32[]{:S(2)}) copy-start(bf16[1,256]{1,0:T(2,128)(2,1)} %bias_ref) | copy-start | bytes 1540
  0.7 10.8 %copy-start.4 = (bf16[1,8,8192]{2,1,0:T(8,128)(2,1)S(1)}, bf16[1,8,8192]{2,1,0:T(8,128)(2,1)}, u32[]{:S(2)}) copy-start(bf16[1,8,8192]{2,1,0:T(8,128)(2,1)} %param.6) | copy-start | bytes 393220
  0.7 9.5 %collective-permute-start = (bf16[8,8192]{1,0:T(8,128)(2,1)}, bf16[8,8192]{1,0:T(8,128)(2,1)S(1)}, u32[]{:S(2)}, u32[]{:S(2)}) collective-permute-start(bf16[8,8192]{1,0:T(8,128)(2,1)} %bitcast.15), channel_id=1, source_target_pairs={{0,6},{1,7},{2,4},{3,5},{4,2},{5,3},{6,0},{7,1},{8,14},{9,15},{10,... | collective-permute-start | bytes 393224 | tf_op jit(solution)/shard_map/ppermute | solution.py:30
  4.6 6.9 %collective-permute-start.3 = (bf16[8,8192]{1,0:T(8,128)(2,1)}, bf16[8,8192]{1,0:T(8,128)(2,1)S(1)}, u32[]{:S(2)}, u32[]{:S(2)}) collective-permute-start(bf16[8,8192]{1,0:T(8,128)(2,1)} %bitcast.16), channel_id=1, source_target_pairs={{0,1},{1,0},{2,3},{3,2},{4,5},{5,4},{6,7},{7,6},{8,9},{9,8},{10,11... | collective-permute-start | bytes 393224 | tf_op jit(solution)/shard_map/ppermute | solution.py:34
  4.6 6.8 %collective-permute-start.2 = (bf16[8,8192]{1,0:T(8,128)(2,1)}, bf16[8,8192]{1,0:T(8,128)(2,1)S(1)}, u32[]{:S(2)}, u32[]{:S(2)}) collective-permute-start(bf16[8,8192]{1,0:T(8,128)(2,1)} %bitcast.17), channel_id=1, source_target_pairs={{0,2},{1,5},{2,0},{3,7},{4,6},{5,1},{6,4},{7,3},{8,10},{9,13},{10,... | collective-permute-start | bytes 393224 | tf_op jit(solution)/shard_map/ppermute | solution.py:30
  5.2 6.0 %collective-permute-start.1 = (bf16[8,8192]{1,0:T(8,128)(2,1)}, bf16[8,8192]{1,0:T(8,128)(2,1)S(1)}, u32[]{:S(2)}, u32[]{:S(2)}) collective-permute-start(bf16[8,8192]{1,0:T(8,128)(2,1)} %bitcast.18), channel_id=1, source_target_pairs={{0,4},{1,3},{2,6},{3,1},{4,0},{5,7},{6,2},{7,5},{8,12},{9,11},{10,... | collective-permute-start | bytes 393224 | tf_op jit(solution)/shard_map/ppermute | solution.py:30
  11.4 1.8 %collective-permute-start.4 = (bf16[24,8192]{1,0:T(8,128)(2,1)S(1)}, bf16[24,8192]{1,0:T(8,128)(2,1)S(1)}, u32[]{:S(2)}, u32[]{:S(2)}) collective-permute-start(bf16[24,8192]{1,0:T(8,128)(2,1)S(1)} %constant_dynamic-update-slice_fusion), channel_id=1, source_target_pairs={{0,1},{1,0},{2,3},{3,2},{4,5},{5,4},{6,7},{7,6},{8,9},{9,8},{10,11... | collective-permute-start | bytes 1179656 | tf_op jit(solution)/shard_map/ppermute | solution.py:34
  14.9 2.0 %collective-permute-start.8 = (bf16[32,8192]{1,0:T(8,128)(2,1)S(1)}, bf16[32,8192]{1,0:T(8,128)(2,1)S(1)}, u32[]{:S(2)}, u32[]{:S(2)}) collective-permute-start(bf16[32,8192]{1,0:T(8,128)(2,1)S(1)} %get-tuple-element.35), channel_id=1, source_target_pairs={{0,1},{1,0},{2,3},{3,2},{4,5},{5,4},{6,7},{7,6},{8,9},{9,8},{10,11... | collective-permute-start | bytes 1572872 | tf_op jit(solution)/shard_map/ppermute | solution.py:34
  16.0 5.7 %collective-permute-start.5 = (bf16[32,8192]{1,0:T(8,128)(2,1)S(1)}, bf16[32,8192]{1,0:T(8,128)(2,1)S(1)}, u32[]{:S(2)}, u32[]{:S(2)}) collective-permute-start(bf16[32,8192]{1,0:T(8,128)(2,1)S(1)} %get-tuple-element.31), channel_id=1, source_target_pairs={{0,1},{1,0},{2,3},{3,2},{4,5},{5,4},{6,7},{7,6},{8,9},{9,8},{10,11... | collective-permute-start | bytes 1572872 | tf_op jit(solution)/shard_map/ppermute | solution.py:34
  16.9 13.8 %copy-start.2 = (bf16[1,8,8192]{2,1,0:T(8,128)(2,1)S(1)}, bf16[1,8,8192]{2,1,0:T(8,128)(2,1)}, u32[]{:S(2)}) copy-start(bf16[1,8,8192]{2,1,0:T(8,128)(2,1)} %param.11) | copy-start | bytes 393220
  17.0 7.5 %collective-permute-start.9 = (bf16[8,8192]{1,0:T(8,128)(2,1)S(1)}, bf16[8,8192]{1,0:T(8,128)(2,1)S(1)}, u32[]{:S(2)}, u32[]{:S(2)}) collective-permute-start(bf16[8,8192]{1,0:T(8,128)(2,1)S(1)} %get-tuple-element.50), channel_id=1, source_target_pairs={{0,8},{1,9},{2,10},{3,11},{4,12},{5,13},{6,14},{7,15},{8,16},{9,17... | collective-permute-start | bytes 393224 | tf_op jit(solution)/shard_map/ppermute | solution.py:39
  18.7 8.3 %collective-permute-start.12 = (bf16[8,8192]{1,0:T(8,128)(2,1)S(1)}, bf16[8,8192]{1,0:T(8,128)(2,1)S(1)}, u32[]{:S(2)}, u32[]{:S(2)}) collective-permute-start(bf16[8,8192]{1,0:T(8,128)(2,1)S(1)} %get-tuple-element.51), channel_id=1, source_target_pairs={{0,4},{1,3},{2,6},{3,1},{4,0},{5,7},{6,2},{7,5},{8,12},{9,11},{10,... | collective-permute-start | bytes 393224 | tf_op jit(solution)/shard_map/ppermute | solution.py:30
  20.2 6.9 %collective-permute-start.11 = (bf16[8,8192]{1,0:T(8,128)(2,1)S(1)}, bf16[8,8192]{1,0:T(8,128)(2,1)S(1)}, u32[]{:S(2)}, u32[]{:S(2)}) collective-permute-start(bf16[8,8192]{1,0:T(8,128)(2,1)S(1)} %get-tuple-element.52), channel_id=1, source_target_pairs={{0,2},{1,5},{2,0},{3,7},{4,6},{5,1},{6,4},{7,3},{8,10},{9,13},{10,... | collective-permute-start | bytes 393224 | tf_op jit(solution)/shard_map/ppermute | solution.py:30
  21.8 8.0 %collective-permute-start.6 = (bf16[8,8192]{1,0:T(8,128)(2,1)S(1)}, bf16[8,8192]{1,0:T(8,128)(2,1)S(1)}, u32[]{:S(2)}, u32[]{:S(2)}) collective-permute-start(bf16[8,8192]{1,0:T(8,128)(2,1)S(1)} %get-tuple-element.48), channel_id=1, source_target_pairs={{0,2},{1,5},{2,0},{3,7},{4,6},{5,1},{6,4},{7,3},{8,10},{9,13},{10,... | collective-permute-start | bytes 393224 | tf_op jit(solution)/shard_map/ppermute | solution.py:30
  22.4 7.4 %collective-permute-start.7 = (bf16[8,8192]{1,0:T(8,128)(2,1)S(1)}, bf16[8,8192]{1,0:T(8,128)(2,1)S(1)}, u32[]{:S(2)}, u32[]{:S(2)}) collective-permute-start(bf16[8,8192]{1,0:T(8,128)(2,1)S(1)} %get-tuple-element.49), channel_id=1, source_target_pairs={{0,4},{1,3},{2,6},{3,1},{4,0},{5,7},{6,2},{7,5},{8,12},{9,11},{10,... | collective-permute-start | bytes 393224 | tf_op jit(solution)/shard_map/ppermute | solution.py:30
  24.5 6.2 %collective-permute-start.10 = (bf16[8,8192]{1,0:T(8,128)(2,1)S(1)}, bf16[8,8192]{1,0:T(8,128)(2,1)S(1)}, u32[]{:S(2)}, u32[]{:S(2)}) collective-permute-start(bf16[8,8192]{1,0:T(8,128)(2,1)S(1)} %slice_add_fusion.1), channel_id=1, source_target_pairs={{0,6},{1,7},{2,4},{3,5},{4,2},{5,3},{6,0},{7,1},{8,14},{9,15},{10,... | collective-permute-start | bytes 393224 | tf_op jit(solution)/shard_map/ppermute | solution.py:30
  27.1 6.0 %collective-permute-start.13 = (bf16[8,8192]{1,0:T(8,128)(2,1)S(1)}, bf16[8,8192]{1,0:T(8,128)(2,1)S(1)}, u32[]{:S(2)}, u32[]{:S(2)}) collective-permute-start(bf16[8,8192]{1,0:T(8,128)(2,1)S(1)} %convert_element_type.71), channel_id=1, source_target_pairs={{0,8},{1,9},{2,10},{3,11},{4,12},{5,13},{6,14},{7,15},{8,16},{9,17... | collective-permute-start | bytes 393224 | tf_op jit(solution)/shard_map/ppermute | solution.py:45
  30.8 6.0 %collective-permute-start.14 = (bf16[8,8192]{1,0:T(8,128)(2,1)S(1)}, bf16[8,8192]{1,0:T(8,128)(2,1)S(1)}, u32[]{:S(2)}, u32[]{:S(2)}) collective-permute-start(bf16[8,8192]{1,0:T(8,128)(2,1)S(1)} %fusion.7), channel_id=1, source_target_pairs={{8,0},{9,1},{10,2},{11,3},{12,4},{13,5},{14,6},{15,7},{16,8},{17,9... | collective-permute-start | bytes 393224 | tf_op jit(solution)/shard_map/ppermute | solution.py:50
  33.2 15.2 %copy-start.3 = (bf16[8,8192]{1,0:T(8,128)(2,1)}, bf16[8,8192]{1,0:T(8,128)(2,1)S(1)}, u32[]{:S(2)}) copy-start(bf16[8,8192]{1,0:T(8,128)(2,1)S(1)} %get-tuple-element.43) | copy-start | bytes 393220
  33.2 6.7 %collective-permute-start.19 = (bf16[8,8192]{1,0:T(8,128)(2,1)S(1)}, bf16[8,8192]{1,0:T(8,128)(2,1)S(1)}, u32[]{:S(2)}, u32[]{:S(2)}) collective-permute-start(bf16[8,8192]{1,0:T(8,128)(2,1)S(1)} %get-tuple-element.43), channel_id=1, source_target_pairs={{0,2},{1,5},{2,0},{3,7},{4,6},{5,1},{6,4},{7,3},{8,10},{9,13},{10,... | collective-permute-start | bytes 393224 | tf_op jit(solution)/shard_map/ppermute | solution.py:30
  34.8 8.7 %collective-permute-start.18 = (bf16[8,8192]{1,0:T(8,128)(2,1)S(1)}, bf16[8,8192]{1,0:T(8,128)(2,1)S(1)}, u32[]{:S(2)}, u32[]{:S(2)}) collective-permute-start(bf16[8,8192]{1,0:T(8,128)(2,1)S(1)} %get-tuple-element.43), channel_id=1, source_target_pairs={{0,6},{1,7},{2,4},{3,5},{4,2},{5,3},{6,0},{7,1},{8,14},{9,15},{10,... | collective-permute-start | bytes 393224 | tf_op jit(solution)/shard_map/ppermute | solution.py:30
  36.2 8.4 %collective-permute-start.17 = (bf16[8,8192]{1,0:T(8,128)(2,1)S(1)}, bf16[8,8192]{1,0:T(8,128)(2,1)S(1)}, u32[]{:S(2)}, u32[]{:S(2)}) collective-permute-start(bf16[8,8192]{1,0:T(8,128)(2,1)S(1)} %get-tuple-element.43), channel_id=1, source_target_pairs={{0,4},{1,3},{2,6},{3,1},{4,0},{5,7},{6,2},{7,5},{8,12},{9,11},{10,... | collective-permute-start | bytes 393224 | tf_op jit(solution)/shard_map/ppermute | solution.py:30
  36.8 9.4 %collective-permute-start.16 = (bf16[8,8192]{1,0:T(8,128)(2,1)S(1)}, bf16[8,8192]{1,0:T(8,128)(2,1)S(1)}, u32[]{:S(2)}, u32[]{:S(2)}) collective-permute-start(bf16[8,8192]{1,0:T(8,128)(2,1)S(1)} %select_convert_fusion), channel_id=1, source_target_pairs={{0,6},{1,7},{2,4},{3,5},{4,2},{5,3},{6,0},{7,1},{8,14},{9,15},{10,... | collective-permute-start | bytes 393224 | tf_op jit(solution)/shard_map/ppermute | solution.py:30
  39.3 7.5 %collective-permute-start.15 = (bf16[8,8192]{1,0:T(8,128)(2,1)S(1)}, bf16[8,8192]{1,0:T(8,128)(2,1)S(1)}, u32[]{:S(2)}, u32[]{:S(2)}) collective-permute-start(bf16[8,8192]{1,0:T(8,128)(2,1)S(1)} %select_convert_fusion), channel_id=1, source_target_pairs={{0,4},{1,3},{2,6},{3,1},{4,0},{5,7},{6,2},{7,5},{8,12},{9,11},{10,... | collective-permute-start | bytes 393224 | tf_op jit(solution)/shard_map/ppermute | solution.py:30
  39.9 5.6 %collective-permute-start.21 = (bf16[8,8192]{1,0:T(8,128)(2,1)S(1)}, bf16[8,8192]{1,0:T(8,128)(2,1)S(1)}, u32[]{:S(2)}, u32[]{:S(2)}) collective-permute-start(bf16[8,8192]{1,0:T(8,128)(2,1)S(1)} %collective-permute-done.19), channel_id=1, source_target_pairs={{8,0},{9,1},{10,2},{11,3},{12,4},{13,5},{14,6},{15,7},{16,8},{17,9... | collective-permute-start | bytes 393224 | tf_op jit(solution)/shard_map/ppermute | solution.py:56
  44.6 2.2 %collective-permute-start.20 = (bf16[32,8192]{1,0:T(8,128)(2,1)S(1)}, bf16[32,8192]{1,0:T(8,128)(2,1)S(1)}, u32[]{:S(2)}, u32[]{:S(2)}) collective-permute-start(bf16[32,8192]{1,0:T(8,128)(2,1)S(1)} %pad_maximum_fusion.1), channel_id=1, source_target_pairs={{0,1},{1,0},{2,3},{3,2},{4,5},{5,4},{6,7},{7,6},{8,9},{9,8},{10,11... | collective-permute-start | bytes 1572872 | tf_op jit(solution)/shard_map/ppermute | solution.py:34
  45.5 2.9 %collective-permute-start.23 = (bf16[8,8192]{1,0:T(8,128)(2,1)S(1)}, bf16[8,8192]{1,0:T(8,128)(2,1)S(1)}, u32[]{:S(2)}, u32[]{:S(2)}) collective-permute-start(bf16[8,8192]{1,0:T(8,128)(2,1)S(1)} %broadcast_select_fusion), channel_id=1, source_target_pairs={{0,1},{1,0},{2,3},{3,2},{4,5},{5,4},{6,7},{7,6},{8,9},{9,8},{10,11... | collective-permute-start | bytes 393224 | tf_op jit(solution)/shard_map/ppermute | solution.py:34
  46.9 1.8 %collective-permute-start.22 = (bf16[24,8192]{1,0:T(8,128)(2,1)S(1)}, bf16[24,8192]{1,0:T(8,128)(2,1)S(1)}, u32[]{:S(2)}, u32[]{:S(2)}) collective-permute-start(bf16[24,8192]{1,0:T(8,128)(2,1)S(1)} %pad_maximum_fusion.2), channel_id=1, source_target_pairs={{0,1},{1,0},{2,3},{3,2},{4,5},{5,4},{6,7},{7,6},{8,9},{9,8},{10,11... | collective-permute-start | bytes 1179656 | tf_op jit(solution)/shard_map/ppermute | solution.py:34

commit v25 on v19

--- a/solution.py
+++ b/solution.py
@@ -246,11 +246,10 @@
     slab, first, final = lax.optimization_barrier((resid[0], index < group, index >= (LAYERS - 1) * group))
     tokens = resid.shape[1]
     enc, own_dec, next_dec = loaded(enc_weight, dec_weight)
-    pieces = jnp.concatenate([across(slab, chip, chips) for chip in range(chips - 1, 0, -1)], axis=0)
-    pieces_far = other_core(pieces)
-    rows = [after(slab, pieces)] + [pieces[i * tokens : (i + 1) * tokens] for i in range(chips - 1)][::-1]
-    rows += [other_core(slab)] + [pieces_far[i * tokens : (i + 1) * tokens] for i in range(chips - 1)][::-1]
-    x = jnp.concatenate(rows, axis=0)
+    last = across(slab, chips - 1, chips)
+    last_far = other_core(after(last, enc))
+    most = jnp.concatenate(after([across(slab, chip, chips) for chip in range(1, chips - 1)], last_far), axis=0)
+    x = jnp.concatenate([after(slab, most), most, last, other_core(slab), other_core(most), last_far], axis=0)
     gate, bias = gated(*after((active[0], enc_bias), enc), group * tokens, tokens)
     pre = jnp.dot(x, enc, preferred_element_type=jnp.float32) + bias
     codes = (jax.nn.relu(pre) * gate).astype(jnp.bfloat16)

time: 50.5 us -> 55.3 us (1.095)
  starting transfers between devices: 27.6 us -> 32.1 us
    ppermute x1, starting transfers between devices: 2.8 us -> 6.07 us  [rotated_down(): lax.ppermute(value, AXIS, [((i + group) % size, i) for i in range(size)])]
    ppermute x1, waiting for transfers between devices: 2.34 us -> 3.31 us  [rotated_down(): lax.ppermute(value, AXIS, [((i + group) % size, i) for i in range(size)])]
    ppermute x7 -> x8, starting transfers between devices: 1.4 us -> 2.09 us  [other_core(): lax.ppermute(value, AXIS, [(i, i ^ 1) for i in range(lax.axis_size(AXIS))])]
    ppermute x7 -> x8, waiting for transfers between devices: 2.1 us -> 1.81 us  [other_core(): lax.ppermute(value, AXIS, [(i, i ^ 1) for i in range(lax.axis_size(AXIS))])]
  transfers between devices with their start and end apart: 24 -> 25, of which waited for: 9 -> 9; matrix products, arithmetic and copies ran while one was open for 2% -> 1% of each run, Pallas kernels for 14% -> 13%
where the time goes in v25:
time: 55.3 us; the launch traced here: 55.1 us
  starting transfers between devices  32.1 us (58%)
  waiting for transfers between devices  10.3 us (19%)
  Pallas kernels  9.89 us (18%)
  between operations  1.02 us (2%)
  matrix products  0.8 us (1%)
  other arithmetic  0.69 us (1%)
    ppermute x13, starting transfers between devices, across(): return lax.ppermute(value, AXIS, pairs)  17.7 us
    ppermute x1, starting transfers between devices, rotated_down(): lax.ppermute(value, AXIS, [((i + group) % size, i) for i in range(size)])  6.07 us
    pallas_call x1, Pallas kernels, loaded(): pl.pallas_call(load_kernel, out_shape=[pltpu.VMEM(enc.shape[1:], enc.dtyp...  4.68 us
    ppermute x1, waiting for transfers between devices, rotated_down(): lax.ppermute(value, AXIS, [((i + group) % size, i) for i in range(size)])  3.31 us
    ppermute x1, starting transfers between devices, shifted(): lax.ppermute(value, AXIS, [(i, i + group) for i in range(size - group)])  2.87 us
    ppermute x8, starting transfers between devices, other_core(): lax.ppermute(value, AXIS, [(i, i ^ 1) for i in range(lax.axis_size(AXIS))])  2.09 us
    pallas_call x1, Pallas kernels, grad_all(): pl.pallas_call(functools.partial(grad_all_kernel, tokens), out_shape=jax....  2.03 us
    ppermute x1, starting transfers between devices, raised(): lax.ppermute(value, AXIS, [(i, (i + group) % size) for i in range(size)])  2.02 us
  transfers between devices with their start and end apart: 25, of which 9 were waited for; matrix products, arithmetic and copies ran while one was open for 1% of the time, Pallas kernels for 13%

profile of v25, /device:TPU:0, one launch (start us, length us, event | category | flops | bytes accessed | tf_op | source)
XLA Modules:
  0.0 55.1 jit_solution(16652538917010387602)
XLA Ops:
  0.7 4.0 %collective-permute-start.2 = (bf16[8,8192]{1,0:T(8,128)(2,1)}, bf16[8,8192]{1,0:T(8,128)(2,1)S(1)}, u32[]{:S(2)}, u32[]{:S(2)}) collective-permute-start(bf16[8,8192]{1,0:T(8,128)(2,1)} %bitcast.15), channel_id=1, source_target_pairs={{0,6},{1,7},{2,4},{3,5},{4,2},{5,3},{6,0},{7,1},{8,14},{9,15},{10,... | collective-permute-start | bytes 393224 | tf_op jit(solution)/shard_map/ppermute | solution.py:30
  4.6 0.5 collective-permute-start
  5.2 0.1 collective-permute-start.1
  5.3 4.7 %load_weights.1 = (bf16[8192,256]{1,0:T(8,128)(2,1)S(1)}, bf16[256,8192]{1,0:T(8,128)(2,1)S(1)}, bf16[256,8192]{1,0:T(8,128)(2,1)S(1)}) custom-call(bf16[1,8192,256]{2,1,0:T(8,128)(2,1)} %enc_hbm.1, bf16[1,2,256,8192]{3,2,1,0:T(8,128)(2,1)} %dec_hbm.1), custom_call_target="tpu_custom_call" | custom-call | bytes 25165824 | tf_op jit(solution)/shard_map/load_weights/pallas_call | solution.py:92
  10.0 0.0 collective-permute-done.2
  10.0 0.1 collective-permute-start.3
  10.1 0.5 collective-permute-start.4
  10.6 0.0 copy-done.1
  10.6 0.1 gate.1
  10.7 0.7 %collective-permute-done = bf16[8,8192]{1,0:T(8,128)(2,1)S(1)} collective-permute-done((bf16[8,8192]{1,0:T(8,128)(2,1)}, bf16[8,8192]{1,0:T(8,128)(2,1)S(1)}, u32[]{:S(2)}, u32[]{:S(2)}) %collective-permute-start) | collective-permute-done | bytes 131104 | tf_op jit(solution)/shard_map/ppermute | solution.py:30
  11.4 0.0 collective-permute-done.1
  11.4 0.0 collective-permute-done.3
  11.4 0.2 collective-permute-start.5
  11.7 0.0 collective-permute-done.4
  11.7 1.3 %collective-permute-done.5 = bf16[16,8192]{1,0:T(8,128)(2,1)S(1)} collective-permute-done((bf16[16,8192]{1,0:T(8,128)(2,1)S(1)}, bf16[16,8192]{1,0:T(8,128)(2,1)S(1)}, u32[]{:S(2)}, u32[]{:S(2)}) %collective-permute-start.5) | collective-permute-done | bytes 262176 | tf_op jit(solution)/shard_map/ppermute | solution.py:34
  13.1 0.8 %fusion.2.codes_ref = bf16[64,256]{1,0:T(8,128)(2,1)S(1)} fusion(f32[64,256]{1,0:T(8,128)S(1)} %get-tuple-element.34, f32[64,256]{1,0:T(8,128)S(1)} %get-tuple-element.33, bf16[64,8192]{1,0:T(8,128)(2,1)S(1)} %constant_dynamic-update-slice_fusion.2, bf16[8192,256]{1,0:T(8,128)(2,1)S(1)} %get-tuple-element.26), kind=kOutput, calls=%fused_computation.3 | convolution fusion | flops 268500992 | bytes 5406720 | tf_op jit(solution)/shard_map/dot_general | solution.py:254
  13.9 0.8 %decode.3 = (f32[32,8192]{1,0:T(8,128)S(1)}, bf16[32,8192]{1,0:T(8,128)(2,1)S(1)}) custom-call(bf16[64,256]{1,0:T(8,128)(2,1)S(1)} %fusion.2.codes_ref, bf16[256,8192]{1,0:T(8,128)(2,1)S(1)} %get-tuple-element.39.dec_ref), custom_call_target="tpu_custom_call" | custom-call | flops 268435456 | bytes 4194304 | tf_op jit(solution)/shard_map/decode/pallas_call | solution.py:169
  14.7 0.2 collective-permute-start.9
  14.9 0.8 %decode.2 = (f32[32,8192]{1,0:T(8,128)S(1)}, bf16[32,8192]{1,0:T(8,128)(2,1)S(1)}) custom-call(bf16[64,256]{1,0:T(8,128)(2,1)S(1)} %fusion.2.codes_ref, bf16[256,8192]{1,0:T(8,128)(2,1)S(1)} %get-tuple-element.35.dec_ref), custom_call_target="tpu_custom_call" | custom-call | flops 268435456 | bytes 4194304 | tf_op jit(solution)/shard_map/decode/pallas_call | solution.py:169
  15.8 0.4 collective-permute-start.6
  16.2 0.5 collective-permute-done.9
  16.7 0.1 fusion.9
  16.9 2.0 %collective-permute-start.10 = (bf16[8,8192]{1,0:T(8,128)(2,1)S(1)}, bf16[8,8192]{1,0:T(8,128)(2,1)S(1)}, u32[]{:S(2)}, u32[]{:S(2)}) collective-permute-start(bf16[8,8192]{1,0:T(8,128)(2,1)S(1)} %get-tuple-element.56), channel_id=1, source_target_pairs={{0,8},{1,9},{2,10},{3,11},{4,12},{5,13},{6,14},{7,15},{8,16},{9,17... | collective-permute-start | bytes 393224 | tf_op jit(solution)/shard_map/ppermute | solution.py:39
  18.9 1.5 %collective-permute-start.12 = (bf16[8,8192]{1,0:T(8,128)(2,1)S(1)}, bf16[8,8192]{1,0:T(8,128)(2,1)S(1)}, u32[]{:S(2)}, u32[]{:S(2)}) collective-permute-start(bf16[8,8192]{1,0:T(8,128)(2,1)S(1)} %get-tuple-element.58), channel_id=1, source_target_pairs={{0,2},{1,5},{2,0},{3,7},{4,6},{5,1},{6,4},{7,3},{8,10},{9,13},{10,... | collective-permute-start | bytes 393224 | tf_op jit(solution)/shard_map/ppermute | solution.py:30
  20.4 1.5 %collective-permute-start.13 = (bf16[8,8192]{1,0:T(8,128)(2,1)S(1)}, bf16[8,8192]{1,0:T(8,128)(2,1)S(1)}, u32[]{:S(2)}, u32[]{:S(2)}) collective-permute-start(bf16[8,8192]{1,0:T(8,128)(2,1)S(1)} %get-tuple-element.57), channel_id=1, source_target_pairs={{0,4},{1,3},{2,6},{3,1},{4,0},{5,7},{6,2},{7,5},{8,12},{9,11},{10,... | collective-permute-start | bytes 393224 | tf_op jit(solution)/shard_map/ppermute | solution.py:30
  21.9 0.0 collective-permute-done.6
  21.9 0.1 fusion.8
  22.1 0.6 %collective-permute-start.7 = (bf16[8,8192]{1,0:T(8,128)(2,1)S(1)}, bf16[8,8192]{1,0:T(8,128)(2,1)S(1)}, u32[]{:S(2)}, u32[]{:S(2)}) collective-permute-start(bf16[8,8192]{1,0:T(8,128)(2,1)S(1)} %get-tuple-element.54), channel_id=1, source_target_pairs={{0,2},{1,5},{2,0},{3,7},{4,6},{5,1},{6,4},{7,3},{8,10},{9,13},{10,... | collective-permute-start | bytes 393224 | tf_op jit(solution)/shard_map/ppermute | solution.py:30
  22.7 0.5 collective-permute-start.8
  23.2 1.5 %collective-permute-done.10 = bf16[8,8192]{1,0:T(8,128)(2,1)S(1)} collective-permute-done((bf16[8,8192]{1,0:T(8,128)(2,1)S(1)}, bf16[8,8192]{1,0:T(8,128)(2,1)S(1)}, u32[]{:S(2)}, u32[]{:S(2)}) %collective-permute-start.10) | collective-permute-done | bytes 131104 | tf_op jit(solution)/shard_map/ppermute | solution.py:39
  24.7 2.5 %collective-permute-start.11 = (bf16[8,8192]{1,0:T(8,128)(2,1)S(1)}, bf16[8,8192]{1,0:T(8,128)(2,1)S(1)}, u32[]{:S(2)}, u32[]{:S(2)}) collective-permute-start(bf16[8,8192]{1,0:T(8,128)(2,1)S(1)} %slice_add_fusion.1), channel_id=1, source_target_pairs={{0,6},{1,7},{2,4},{3,5},{4,2},{5,3},{6,0},{7,1},{8,14},{9,15},{10,... | collective-permute-start | bytes 393224 | tf_op jit(solution)/shard_map/ppermute | solution.py:30
  27.3 0.0 collective-permute-done.12
  27.3 0.0 collective-permute-done.13
  27.3 2.9 %collective-permute-start.14 = (bf16[8,8192]{1,0:T(8,128)(2,1)S(1)}, bf16[8,8192]{1,0:T(8,128)(2,1)S(1)}, u32[]{:S(2)}, u32[]{:S(2)}) collective-permute-start(bf16[8,8192]{1,0:T(8,128)(2,1)S(1)} %convert_element_type.71), channel_id=1, source_target_pairs={{0,8},{1,9},{2,10},{3,11},{4,12},{5,13},{6,14},{7,15},{8,16},{9,17... | collective-permute-start | bytes 393224 | tf_op jit(solution)/shard_map/ppermute | solution.py:45
  30.2 0.0 collective-permute-done.7
  30.2 0.0 collective-permute-done.8
  30.2 0.7 %collective-permute-done.11 = bf16[8,8192]{1,0:T(8,128)(2,1)S(1)} collective-permute-done((bf16[8,8192]{1,0:T(8,128)(2,1)S(1)}, bf16[8,8192]{1,0:T(8,128)(2,1)S(1)}, u32[]{:S(2)}, u32[]{:S(2)}) %collective-permute-start.11) | collective-permute-done | bytes 131104 | tf_op jit(solution)/shard_map/ppermute | solution.py:30
  31.0 0.1 fusion.7
  31.0 1.3 %collective-permute-start.15 = (bf16[8,8192]{1,0:T(8,128)(2,1)S(1)}, bf16[8,8192]{1,0:T(8,128)(2,1)S(1)}, u32[]{:S(2)}, u32[]{:S(2)}) collective-permute-start(bf16[8,8192]{1,0:T(8,128)(2,1)S(1)} %fusion.7), channel_id=1, source_target_pairs={{8,0},{9,1},{10,2},{11,3},{12,4},{13,5},{14,6},{15,7},{16,8},{17,9... | collective-permute-start | bytes 393224 | tf_op jit(solution)/shard_map/ppermute | solution.py:50
  32.3 0.4 collective-permute-done.14
  32.7 0.1 constant_dynamic-update-slice_fusion.13
  32.8 0.0 copy-start.3
  32.8 2.0 %collective-permute-start.18 = (bf16[8,8192]{1,0:T(8,128)(2,1)S(1)}, bf16[8,8192]{1,0:T(8,128)(2,1)S(1)}, u32[]{:S(2)}, u32[]{:S(2)}) collective-permute-start(bf16[8,8192]{1,0:T(8,128)(2,1)S(1)} %get-tuple-element.49), channel_id=1, source_target_pairs={{0,6},{1,7},{2,4},{3,5},{4,2},{5,3},{6,0},{7,1},{8,14},{9,15},{10,... | collective-permute-start | bytes 393224 | tf_op jit(solution)/shard_map/ppermute | solution.py:30
  34.8 0.6 %collective-permute-start.19 = (bf16[8,8192]{1,0:T(8,128)(2,1)S(1)}, bf16[8,8192]{1,0:T(8,128)(2,1)S(1)}, u32[]{:S(2)}, u32[]{:S(2)}) collective-permute-start(bf16[8,8192]{1,0:T(8,128)(2,1)S(1)} %get-tuple-element.49), channel_id=1, source_target_pairs={{0,4},{1,3},{2,6},{3,1},{4,0},{5,7},{6,2},{7,5},{8,12},{9,11},{10,... | collective-permute-start | bytes 393224 | tf_op jit(solution)/shard_map/ppermute | solution.py:30
  35.5 0.9 %collective-permute-start.20 = (bf16[8,8192]{1,0:T(8,128)(2,1)S(1)}, bf16[8,8192]{1,0:T(8,128)(2,1)S(1)}, u32[]{:S(2)}, u32[]{:S(2)}) collective-permute-start(bf16[8,8192]{1,0:T(8,128)(2,1)S(1)} %get-tuple-element.49), channel_id=1, source_target_pairs={{0,2},{1,5},{2,0},{3,7},{4,6},{5,1},{6,4},{7,3},{8,10},{9,13},{10,... | collective-permute-start | bytes 393224 | tf_op jit(solution)/shard_map/ppermute | solution.py:30
  36.4 1.6 %collective-permute-done.15 = bf16[8,8192]{1,0:T(8,128)(2,1)S(1)} collective-permute-done((bf16[8,8192]{1,0:T(8,128)(2,1)S(1)}, bf16[8,8192]{1,0:T(8,128)(2,1)S(1)}, u32[]{:S(2)}, u32[]{:S(2)}) %collective-permute-start.15) | collective-permute-done | bytes 131104 | tf_op jit(solution)/shard_map/ppermute | solution.py:50
  38.0 2.6 %collective-permute-start.16 = (bf16[8,8192]{1,0:T(8,128)(2,1)S(1)}, bf16[8,8192]{1,0:T(8,128)(2,1)S(1)}, u32[]{:S(2)}, u32[]{:S(2)}) collective-permute-start(bf16[8,8192]{1,0:T(8,128)(2,1)S(1)} %select_convert_fusion), channel_id=1, source_target_pairs={{0,6},{1,7},{2,4},{3,5},{4,2},{5,3},{6,0},{7,1},{8,14},{9,15},{10,... | collective-permute-start | bytes 393224 | tf_op jit(solution)/shard_map/ppermute | solution.py:30
  40.6 0.4 collective-permute-start.17
  41.0 0.0 collective-permute-done.18
  41.0 0.0 collective-permute-done.19
  41.0 0.2 collective-permute-done.20
  41.3 0.1 collective-permute-start.21
  41.3 6.1 %collective-permute-start.22 = (bf16[8,8192]{1,0:T(8,128)(2,1)S(1)}, bf16[8,8192]{1,0:T(8,128)(2,1)S(1)}, u32[]{:S(2)}, u32[]{:S(2)}) collective-permute-start(bf16[8,8192]{1,0:T(8,128)(2,1)S(1)} %collective-permute-done.20), channel_id=1, source_target_pairs={{8,0},{9,1},{10,2},{11,3},{12,4},{13,5},{14,6},{15,7},{16,8},{17,9... | collective-permute-start | bytes 393224 | tf_op jit(solution)/shard_map/ppermute | solution.py:55
  47.5 3.3 %collective-permute-done.22 = bf16[8,8192]{1,0:T(8,128)(2,1)S(1)} collective-permute-done((bf16[8,8192]{1,0:T(8,128)(2,1)S(1)}, bf16[8,8192]{1,0:T(8,128)(2,1)S(1)}, u32[]{:S(2)}, u32[]{:S(2)}) %collective-permute-start.22) | collective-permute-done | bytes 131104 | tf_op jit(solution)/shard_map/ppermute | solution.py:55
  50.8 0.1 collective-permute-start.24
  50.9 0.0 collective-permute-done.16
  50.9 0.0 collective-permute-done.17
  50.9 0.0 collective-permute-done.21
  50.9 0.5 collective-permute-start.23
  51.5 1.4 %grad_own.1 = (f32[64,256]{1,0:T(8,128)S(1)}, f32[8,128]{1,0:T(8,128)}) custom-call(bf16[64,8192]{1,0:T(8,128)(2,1)S(1)} %constant_dynamic-update-slice_fusion.9.rows_ref, bf16[256,8192]{1,0:T(8,128)(2,1)S(1)} %get-tuple-element.35.dec_ref), custom_call_target="tpu_custom_call" | custom-call | flops 268435456 | bytes 4194304 | tf_op jit(solution)/shard_map/grad_own/pallas_call | solution.py:206
  52.9 0.0 collective-permute-done.24
  52.9 0.0 collective-permute-done.23
  52.9 0.1 pad_maximum_fusion.rows_ref
  53.0 2.0 %grad_all.1 = f32[1,64,256]{2,1,0:T(8,128)} custom-call(bf16[64,8192]{1,0:T(8,128)(2,1)S(1)} %pad_maximum_fusion.rows_ref, bf16[256,8192]{1,0:T(8,128)(2,1)S(1)} %get-tuple-element.39.dec_ref, f32[64,256]{1,0:T(8,128)S(1)} %get-tuple-element.47.own_ref), custom_call_target="tpu_custom_call" | custom-call | flops 268435456 | bytes 4194304 | tf_op jit(solution)/shard_map/grad_all/pallas_call | solution.py:218
  (31 shorter events, 0.4 us)
Async XLA Ops:
  0.6 9.4 %copy-start.4 = (bf16[1,8,8192]{2,1,0:T(8,128)(2,1)S(1)}, bf16[1,8,8192]{2,1,0:T(8,128)(2,1)}, u32[]{:S(2)}) copy-start(bf16[1,8,8192]{2,1,0:T(8,128)(2,1)} %param.6) | copy-start | bytes 393220
  0.6 9.9 %copy-start = (s32[1,2,2]{2,1,0:T(2,128)S(1)}, s32[1,2,2]{2,1,0:T(2,128)}, u32[]{:S(2)}) copy-start(s32[1,2,2]{2,1,0:T(2,128)} %param.9) | copy-start | bytes 52
  0.7 9.9 %copy-start.1 = (bf16[1,256]{1,0:T(2,128)(2,1)S(1)}, bf16[1,256]{1,0:T(2,128)(2,1)}, u32[]{:S(2)}) copy-start(bf16[1,256]{1,0:T(2,128)(2,1)} %bias_ref) | copy-start | bytes 1540
  0.7 9.3 %collective-permute-start.2 = (bf16[8,8192]{1,0:T(8,128)(2,1)}, bf16[8,8192]{1,0:T(8,128)(2,1)S(1)}, u32[]{:S(2)}, u32[]{:S(2)}) collective-permute-start(bf16[8,8192]{1,0:T(8,128)(2,1)} %bitcast.15), channel_id=1, source_target_pairs={{0,6},{1,7},{2,4},{3,5},{4,2},{5,3},{6,0},{7,1},{8,14},{9,15},{10,... | collective-permute-start | bytes 393224 | tf_op jit(solution)/shard_map/ppermute | solution.py:30
  4.6 6.8 %collective-permute-start = (bf16[8,8192]{1,0:T(8,128)(2,1)}, bf16[8,8192]{1,0:T(8,128)(2,1)S(1)}, u32[]{:S(2)}, u32[]{:S(2)}) collective-permute-start(bf16[8,8192]{1,0:T(8,128)(2,1)} %bitcast.16), channel_id=1, source_target_pairs={{0,2},{1,5},{2,0},{3,7},{4,6},{5,1},{6,4},{7,3},{8,10},{9,13},{10,... | collective-permute-start | bytes 393224 | tf_op jit(solution)/shard_map/ppermute | solution.py:30
  5.2 6.2 %collective-permute-start.1 = (bf16[8,8192]{1,0:T(8,128)(2,1)}, bf16[8,8192]{1,0:T(8,128)(2,1)S(1)}, u32[]{:S(2)}, u32[]{:S(2)}) collective-permute-start(bf16[8,8192]{1,0:T(8,128)(2,1)} %bitcast.17), channel_id=1, source_target_pairs={{0,4},{1,3},{2,6},{3,1},{4,0},{5,7},{6,2},{7,5},{8,12},{9,11},{10,... | collective-permute-start | bytes 393224 | tf_op jit(solution)/shard_map/ppermute | solution.py:30
  10.0 1.4 %collective-permute-start.3 = (bf16[8,8192]{1,0:T(8,128)(2,1)S(1)}, bf16[8,8192]{1,0:T(8,128)(2,1)S(1)}, u32[]{:S(2)}, u32[]{:S(2)}) collective-permute-start(bf16[8,8192]{1,0:T(8,128)(2,1)S(1)} %collective-permute-done.2), channel_id=1, source_target_pairs={{0,1},{1,0},{2,3},{3,2},{4,5},{5,4},{6,7},{7,6},{8,9},{9,8},{10,11... | collective-permute-start | bytes 393224 | tf_op jit(solution)/shard_map/ppermute | solution.py:34
  10.1 1.6 %collective-permute-start.4 = (bf16[8,8192]{1,0:T(8,128)(2,1)S(1)}, bf16[8,8192]{1,0:T(8,128)(2,1)S(1)}, u32[]{:S(2)}, u32[]{:S(2)}) collective-permute-start(bf16[8,8192]{1,0:T(8,128)(2,1)S(1)} %bitcast.18), channel_id=1, source_target_pairs={{0,1},{1,0},{2,3},{3,2},{4,5},{5,4},{6,7},{7,6},{8,9},{9,8},{10,11... | collective-permute-start | bytes 393224 | tf_op jit(solution)/shard_map/ppermute | solution.py:34
  11.4 1.6 %collective-permute-start.5 = (bf16[16,8192]{1,0:T(8,128)(2,1)S(1)}, bf16[16,8192]{1,0:T(8,128)(2,1)S(1)}, u32[]{:S(2)}, u32[]{:S(2)}) collective-permute-start(bf16[16,8192]{1,0:T(8,128)(2,1)S(1)} %constant_dynamic-update-slice_fusion), channel_id=1, source_target_pairs={{0,1},{1,0},{2,3},{3,2},{4,5},{5,4},{6,7},{7,6},{8,9},{9,8},{10,11... | collective-permute-start | bytes 786440 | tf_op jit(solution)/shard_map/ppermute | solution.py:34
  14.7 2.0 %collective-permute-start.9 = (bf16[32,8192]{1,0:T(8,128)(2,1)S(1)}, bf16[32,8192]{1,0:T(8,128)(2,1)S(1)}, u32[]{:S(2)}, u32[]{:S(2)}) collective-permute-start(bf16[32,8192]{1,0:T(8,128)(2,1)S(1)} %get-tuple-element.41), channel_id=1, source_target_pairs={{0,1},{1,0},{2,3},{3,2},{4,5},{5,4},{6,7},{7,6},{8,9},{9,8},{10,11... | collective-permute-start | bytes 1572872 | tf_op jit(solution)/shard_map/ppermute | solution.py:34
  15.8 6.1 %collective-permute-start.6 = (bf16[32,8192]{1,0:T(8,128)(2,1)S(1)}, bf16[32,8192]{1,0:T(8,128)(2,1)S(1)}, u32[]{:S(2)}, u32[]{:S(2)}) collective-permute-start(bf16[32,8192]{1,0:T(8,128)(2,1)S(1)} %get-tuple-element.37), channel_id=1, source_target_pairs={{0,1},{1,0},{2,3},{3,2},{4,5},{5,4},{6,7},{7,6},{8,9},{9,8},{10,11... | collective-permute-start | bytes 1572872 | tf_op jit(solution)/shard_map/ppermute | solution.py:34
  16.7 14.3 %copy-start.2 = (bf16[1,8,8192]{2,1,0:T(8,128)(2,1)S(1)}, bf16[1,8,8192]{2,1,0:T(8,128)(2,1)}, u32[]{:S(2)}) copy-start(bf16[1,8,8192]{2,1,0:T(8,128)(2,1)} %param.11) | copy-start | bytes 393220
  16.9 7.8 %collective-permute-start.10 = (bf16[8,8192]{1,0:T(8,128)(2,1)S(1)}, bf16[8,8192]{1,0:T(8,128)(2,1)S(1)}, u32[]{:S(2)}, u32[]{:S(2)}) collective-permute-start(bf16[8,8192]{1,0:T(8,128)(2,1)S(1)} %get-tuple-element.56), channel_id=1, source_target_pairs={{0,8},{1,9},{2,10},{3,11},{4,12},{5,13},{6,14},{7,15},{8,16},{9,17... | collective-permute-start | bytes 393224 | tf_op jit(solution)/shard_map/ppermute | solution.py:39
  18.9 8.4 %collective-permute-start.12 = (bf16[8,8192]{1,0:T(8,128)(2,1)S(1)}, bf16[8,8192]{1,0:T(8,128)(2,1)S(1)}, u32[]{:S(2)}, u32[]{:S(2)}) collective-permute-start(bf16[8,8192]{1,0:T(8,128)(2,1)S(1)} %get-tuple-element.58), channel_id=1, source_target_pairs={{0,2},{1,5},{2,0},{3,7},{4,6},{5,1},{6,4},{7,3},{8,10},{9,13},{10,... | collective-permute-start | bytes 393224 | tf_op jit(solution)/shard_map/ppermute | solution.py:30
  20.4 6.9 %collective-permute-start.13 = (bf16[8,8192]{1,0:T(8,128)(2,1)S(1)}, bf16[8,8192]{1,0:T(8,128)(2,1)S(1)}, u32[]{:S(2)}, u32[]{:S(2)}) collective-permute-start(bf16[8,8192]{1,0:T(8,128)(2,1)S(1)} %get-tuple-element.57), channel_id=1, source_target_pairs={{0,4},{1,3},{2,6},{3,1},{4,0},{5,7},{6,2},{7,5},{8,12},{9,11},{10,... | collective-permute-start | bytes 393224 | tf_op jit(solution)/shard_map/ppermute | solution.py:30
  22.1 8.2 %collective-permute-start.7 = (bf16[8,8192]{1,0:T(8,128)(2,1)S(1)}, bf16[8,8192]{1,0:T(8,128)(2,1)S(1)}, u32[]{:S(2)}, u32[]{:S(2)}) collective-permute-start(bf16[8,8192]{1,0:T(8,128)(2,1)S(1)} %get-tuple-element.54), channel_id=1, source_target_pairs={{0,2},{1,5},{2,0},{3,7},{4,6},{5,1},{6,4},{7,3},{8,10},{9,13},{10,... | collective-permute-start | bytes 393224 | tf_op jit(solution)/shard_map/ppermute | solution.py:30
  22.7 7.6 %collective-permute-start.8 = (bf16[8,8192]{1,0:T(8,128)(2,1)S(1)}, bf16[8,8192]{1,0:T(8,128)(2,1)S(1)}, u32[]{:S(2)}, u32[]{:S(2)}) collective-permute-start(bf16[8,8192]{1,0:T(8,128)(2,1)S(1)} %get-tuple-element.55), channel_id=1, source_target_pairs={{0,4},{1,3},{2,6},{3,1},{4,0},{5,7},{6,2},{7,5},{8,12},{9,11},{10,... | collective-permute-start | bytes 393224 | tf_op jit(solution)/shard_map/ppermute | solution.py:30
  24.7 6.2 %collective-permute-start.11 = (bf16[8,8192]{1,0:T(8,128)(2,1)S(1)}, bf16[8,8192]{1,0:T(8,128)(2,1)S(1)}, u32[]{:S(2)}, u32[]{:S(2)}) collective-permute-start(bf16[8,8192]{1,0:T(8,128)(2,1)S(1)} %slice_add_fusion.1), channel_id=1, source_target_pairs={{0,6},{1,7},{2,4},{3,5},{4,2},{5,3},{6,0},{7,1},{8,14},{9,15},{10,... | collective-permute-start | bytes 393224 | tf_op jit(solution)/shard_map/ppermute | solution.py:30
  27.3 5.4 %collective-permute-start.14 = (bf16[8,8192]{1,0:T(8,128)(2,1)S(1)}, bf16[8,8192]{1,0:T(8,128)(2,1)S(1)}, u32[]{:S(2)}, u32[]{:S(2)}) collective-permute-start(bf16[8,8192]{1,0:T(8,128)(2,1)S(1)} %convert_element_type.71), channel_id=1, source_target_pairs={{0,8},{1,9},{2,10},{3,11},{4,12},{5,13},{6,14},{7,15},{8,16},{9,17... | collective-permute-start | bytes 393224 | tf_op jit(solution)/shard_map/ppermute | solution.py:45
  31.0 6.9 %collective-permute-start.15 = (bf16[8,8192]{1,0:T(8,128)(2,1)S(1)}, bf16[8,8192]{1,0:T(8,128)(2,1)S(1)}, u32[]{:S(2)}, u32[]{:S(2)}) collective-permute-start(bf16[8,8192]{1,0:T(8,128)(2,1)S(1)} %fusion.7), channel_id=1, source_target_pairs={{8,0},{9,1},{10,2},{11,3},{12,4},{13,5},{14,6},{15,7},{16,8},{17,9... | collective-permute-start | bytes 393224 | tf_op jit(solution)/shard_map/ppermute | solution.py:50
  32.8 20.1 %copy-start.3 = (bf16[8,8192]{1,0:T(8,128)(2,1)}, bf16[8,8192]{1,0:T(8,128)(2,1)S(1)}, u32[]{:S(2)}) copy-start(bf16[8,8192]{1,0:T(8,128)(2,1)S(1)} %get-tuple-element.49) | copy-start | bytes 393220
  32.8 8.2 %collective-permute-start.18 = (bf16[8,8192]{1,0:T(8,128)(2,1)S(1)}, bf16[8,8192]{1,0:T(8,128)(2,1)S(1)}, u32[]{:S(2)}, u32[]{:S(2)}) collective-permute-start(bf16[8,8192]{1,0:T(8,128)(2,1)S(1)} %get-tuple-element.49), channel_id=1, source_target_pairs={{0,6},{1,7},{2,4},{3,5},{4,2},{5,3},{6,0},{7,1},{8,14},{9,15},{10,... | collective-permute-start | bytes 393224 | tf_op jit(solution)/shard_map/ppermute | solution.py:30
  34.8 6.1 %collective-permute-start.19 = (bf16[8,8192]{1,0:T(8,128)(2,1)S(1)}, bf16[8,8192]{1,0:T(8,128)(2,1)S(1)}, u32[]{:S(2)}, u32[]{:S(2)}) collective-permute-start(bf16[8,8192]{1,0:T(8,128)(2,1)S(1)} %get-tuple-element.49), channel_id=1, source_target_pairs={{0,4},{1,3},{2,6},{3,1},{4,0},{5,7},{6,2},{7,5},{8,12},{9,11},{10,... | collective-permute-start | bytes 393224 | tf_op jit(solution)/shard_map/ppermute | solution.py:30
  35.5 5.7 %collective-permute-start.20 = (bf16[8,8192]{1,0:T(8,128)(2,1)S(1)}, bf16[8,8192]{1,0:T(8,128)(2,1)S(1)}, u32[]{:S(2)}, u32[]{:S(2)}) collective-permute-start(bf16[8,8192]{1,0:T(8,128)(2,1)S(1)} %get-tuple-element.49), channel_id=1, source_target_pairs={{0,2},{1,5},{2,0},{3,7},{4,6},{5,1},{6,4},{7,3},{8,10},{9,13},{10,... | collective-permute-start | bytes 393224 | tf_op jit(solution)/shard_map/ppermute | solution.py:30
  38.0 12.8 %collective-permute-start.16 = (bf16[8,8192]{1,0:T(8,128)(2,1)S(1)}, bf16[8,8192]{1,0:T(8,128)(2,1)S(1)}, u32[]{:S(2)}, u32[]{:S(2)}) collective-permute-start(bf16[8,8192]{1,0:T(8,128)(2,1)S(1)} %select_convert_fusion), channel_id=1, source_target_pairs={{0,6},{1,7},{2,4},{3,5},{4,2},{5,3},{6,0},{7,1},{8,14},{9,15},{10,... | collective-permute-start | bytes 393224 | tf_op jit(solution)/shard_map/ppermute | solution.py:30
  40.6 10.3 %collective-permute-start.17 = (bf16[8,8192]{1,0:T(8,128)(2,1)S(1)}, bf16[8,8192]{1,0:T(8,128)(2,1)S(1)}, u32[]{:S(2)}, u32[]{:S(2)}) collective-permute-start(bf16[8,8192]{1,0:T(8,128)(2,1)S(1)} %select_convert_fusion), channel_id=1, source_target_pairs={{0,4},{1,3},{2,6},{3,1},{4,0},{5,7},{6,2},{7,5},{8,12},{9,11},{10,... | collective-permute-start | bytes 393224 | tf_op jit(solution)/shard_map/ppermute | solution.py:30
  41.3 9.7 %collective-permute-start.21 = (bf16[32,8192]{1,0:T(8,128)(2,1)S(1)}, bf16[32,8192]{1,0:T(8,128)(2,1)S(1)}, u32[]{:S(2)}, u32[]{:S(2)}) collective-permute-start(bf16[32,8192]{1,0:T(8,128)(2,1)S(1)} %pad_maximum_fusion.1), channel_id=1, source_target_pairs={{0,1},{1,0},{2,3},{3,2},{4,5},{5,4},{6,7},{7,6},{8,9},{9,8},{10,11... | collective-permute-start | bytes 1572872 | tf_op jit(solution)/shard_map/ppermute | solution.py:34
  41.3 9.4 %collective-permute-start.22 = (bf16[8,8192]{1,0:T(8,128)(2,1)S(1)}, bf16[8,8192]{1,0:T(8,128)(2,1)S(1)}, u32[]{:S(2)}, u32[]{:S(2)}) collective-permute-start(bf16[8,8192]{1,0:T(8,128)(2,1)S(1)} %collective-permute-done.20), channel_id=1, source_target_pairs={{8,0},{9,1},{10,2},{11,3},{12,4},{13,5},{14,6},{15,7},{16,8},{17,9... | collective-permute-start | bytes 393224 | tf_op jit(solution)/shard_map/ppermute | solution.py:55
  50.8 2.1 %collective-permute-start.24 = (bf16[8,8192]{1,0:T(8,128)(2,1)S(1)}, bf16[8,8192]{1,0:T(8,128)(2,1)S(1)}, u32[]{:S(2)}, u32[]{:S(2)}) collective-permute-start(bf16[8,8192]{1,0:T(8,128)(2,1)S(1)} %broadcast_select_fusion), channel_id=1, source_target_pairs={{0,1},{1,0},{2,3},{3,2},{4,5},{5,4},{6,7},{7,6},{8,9},{9,8},{10,11... | collective-permute-start | bytes 393224 | tf_op jit(solution)/shard_map/ppermute | solution.py:34
  50.9 2.0 %collective-permute-start.23 = (bf16[24,8192]{1,0:T(8,128)(2,1)S(1)}, bf16[24,8192]{1,0:T(8,128)(2,1)S(1)}, u32[]{:S(2)}, u32[]{:S(2)}) collective-permute-start(bf16[24,8192]{1,0:T(8,128)(2,1)S(1)} %pad_maximum_fusion.2), channel_id=1, source_target_pairs={{0,1},{1,0},{2,3},{3,2},{4,5},{5,4},{6,7},{7,6},{8,9},{9,8},{10,11... | collective-permute-start | bytes 1179656 | tf_op jit(solution)/shard_map/ppermute | solution.py:34

commit v26 on v19

--- a/solution.py
+++ b/solution.py
@@ -178,12 +178,13 @@
 
 
 def back(rows_ref, dec_ref):
-    return summed_over(
+    turned_round = summed_over(
         rows_ref.shape[1],
         lambda part: lax.dot_general(
-            rows_ref[:, part], dec_ref[:, part], (((1,), (1,)), ((), ())), preferred_element_type=jnp.float32
+            dec_ref[:, part], rows_ref[:, part], (((1,), (1,)), ((), ())), preferred_element_type=jnp.float32
         ),
     )
+    return turned_round.T
 
 
 def grad_own_kernel(rows_ref, dec_ref, out_ref, _):

time: 50.5 us -> 50.6 us (level)
  no operation moved by 1% of the time
where the time goes in v26:
time: 50.6 us; the launch traced here: 50.4 us
  starting transfers between devices  27.6 us (55%)
  Pallas kernels  10 us (20%)
  waiting for transfers between devices  10 us (20%)
  between operations  1.04 us (2%)
  matrix products  0.8 us (2%)
  other arithmetic  0.69 us (1%)
    ppermute x13, starting transfers between devices, across(): return lax.ppermute(value, AXIS, pairs)  17.8 us
    pallas_call x1, Pallas kernels, loaded(): pl.pallas_call(load_kernel, out_shape=[pltpu.VMEM(enc.shape[1:], enc.dtyp...  4.68 us
    ppermute x1, starting transfers between devices, rotated_down(): lax.ppermute(value, AXIS, [((i + group) % size, i) for i in range(size)])  2.8 us
    ppermute x1, starting transfers between devices, shifted(): lax.ppermute(value, AXIS, [(i, i + group) for i in range(size - group)])  2.7 us
    ppermute x1, waiting for transfers between devices, rotated_down(): lax.ppermute(value, AXIS, [((i + group) % size, i) for i in range(size)])  2.34 us
    ppermute x7, waiting for transfers between devices, other_core(): lax.ppermute(value, AXIS, [(i, i ^ 1) for i in range(lax.axis_size(AXIS))])  2.1 us
    ppermute x13, waiting for transfers between devices, across(): return lax.ppermute(value, AXIS, pairs)  2.1 us
    pallas_call x1, Pallas kernels, grad_all(): pl.pallas_call(functools.partial(grad_all_kernel, tokens), out_shape=jax....  1.91 us
  transfers between devices with their start and end apart: 24, of which 9 were waited for; matrix products, arithmetic and copies ran while one was open for 2% of the time, Pallas kernels for 14%

profile of v26, /device:TPU:0, one launch (start us, length us, event | category | flops | bytes accessed | tf_op | source)
XLA Modules:
  0.0 50.4 jit_solution(16838783929239089024)
XLA Ops:
  0.6 0.0 copy-start
  0.6 0.0 copy-start.1
  0.7 0.0 copy-start.4
  0.7 4.0 %collective-permute-start = (bf16[8,8192]{1,0:T(8,128)(2,1)}, bf16[8,8192]{1,0:T(8,128)(2,1)S(1)}, u32[]{:S(2)}, u32[]{:S(2)}) collective-permute-start(bf16[8,8192]{1,0:T(8,128)(2,1)} %bitcast.15), channel_id=1, source_target_pairs={{0,6},{1,7},{2,4},{3,5},{4,2},{5,3},{6,0},{7,1},{8,14},{9,15},{10,... | collective-permute-start | bytes 393224 | tf_op jit(solution)/shard_map/ppermute | solution.py:30
  4.6 0.0 collective-permute-start.3
  4.6 0.5 %collective-permute-start.2 = (bf16[8,8192]{1,0:T(8,128)(2,1)}, bf16[8,8192]{1,0:T(8,128)(2,1)S(1)}, u32[]{:S(2)}, u32[]{:S(2)}) collective-permute-start(bf16[8,8192]{1,0:T(8,128)(2,1)} %bitcast.17), channel_id=1, source_target_pairs={{0,2},{1,5},{2,0},{3,7},{4,6},{5,1},{6,4},{7,3},{8,10},{9,13},{10,... | collective-permute-start | bytes 393224 | tf_op jit(solution)/shard_map/ppermute | solution.py:30
  5.2 0.2 collective-permute-start.1
  5.3 4.7 %load_weights.1 = (bf16[8192,256]{1,0:T(8,128)(2,1)S(1)}, bf16[256,8192]{1,0:T(8,128)(2,1)S(1)}, bf16[256,8192]{1,0:T(8,128)(2,1)S(1)}) custom-call(bf16[1,8192,256]{2,1,0:T(8,128)(2,1)} %enc_hbm.1, bf16[1,2,256,8192]{3,2,1,0:T(8,128)(2,1)} %dec_hbm.1), custom_call_target="tpu_custom_call" | custom-call | bytes 25165824 | tf_op jit(solution)/shard_map/load_weights/pallas_call | solution.py:92
  10.1 0.1 gate.1
  10.2 0.0 collective-permute-done
  10.2 0.9 %collective-permute-done.1 = bf16[8,8192]{1,0:T(8,128)(2,1)S(1)} collective-permute-done((bf16[8,8192]{1,0:T(8,128)(2,1)}, bf16[8,8192]{1,0:T(8,128)(2,1)S(1)}, u32[]{:S(2)}, u32[]{:S(2)}) %collective-permute-start.1) | collective-permute-done | bytes 131104 | tf_op jit(solution)/shard_map/ppermute | solution.py:30
  11.2 0.2 collective-permute-done.2
  11.4 0.1 collective-permute-start.4
  11.6 0.0 collective-permute-done.3
  11.6 1.6 %collective-permute-done.4 = bf16[24,8192]{1,0:T(8,128)(2,1)S(1)} collective-permute-done((bf16[24,8192]{1,0:T(8,128)(2,1)S(1)}, bf16[24,8192]{1,0:T(8,128)(2,1)S(1)}, u32[]{:S(2)}, u32[]{:S(2)}) %collective-permute-start.4) | collective-permute-done | bytes 393248 | tf_op jit(solution)/shard_map/ppermute | solution.py:34
  13.2 0.8 %fusion.2.codes_ref = bf16[64,256]{1,0:T(8,128)(2,1)S(1)} fusion(f32[64,256]{1,0:T(8,128)S(1)} %get-tuple-element.28, f32[64,256]{1,0:T(8,128)S(1)} %get-tuple-element.27, bf16[64,8192]{1,0:T(8,128)(2,1)S(1)} %slice_dynamic-update-slice_fusion, bf16[8192,256]{1,0:T(8,128)(2,1)S(1)} %get-tuple-element.24), kind=kOutput, calls=%fused_computation.3 | convolution fusion | flops 268500992 | bytes 5406720 | tf_op jit(solution)/shard_map/dot_general | solution.py:256
  14.1 0.8 %decode.3 = (f32[32,8192]{1,0:T(8,128)S(1)}, bf16[32,8192]{1,0:T(8,128)(2,1)S(1)}) custom-call(bf16[64,256]{1,0:T(8,128)(2,1)S(1)} %fusion.2.codes_ref, bf16[256,8192]{1,0:T(8,128)(2,1)S(1)} %get-tuple-element.33.dec_ref), custom_call_target="tpu_custom_call" | custom-call | flops 268435456 | bytes 4194304 | tf_op jit(solution)/shard_map/decode/pallas_call | solution.py:169
  14.9 0.2 collective-permute-start.8
  15.1 0.8 %decode.2 = (f32[32,8192]{1,0:T(8,128)S(1)}, bf16[32,8192]{1,0:T(8,128)(2,1)S(1)}) custom-call(bf16[64,256]{1,0:T(8,128)(2,1)S(1)} %fusion.2.codes_ref, bf16[256,8192]{1,0:T(8,128)(2,1)S(1)} %get-tuple-element.29.dec_ref), custom_call_target="tpu_custom_call" | custom-call | flops 268435456 | bytes 4194304 | tf_op jit(solution)/shard_map/decode/pallas_call | solution.py:169
  16.0 0.4 collective-permute-start.5
  16.4 0.5 collective-permute-done.8
  16.9 0.1 fusion.9
  17.0 1.6 %collective-permute-start.9 = (bf16[8,8192]{1,0:T(8,128)(2,1)S(1)}, bf16[8,8192]{1,0:T(8,128)(2,1)S(1)}, u32[]{:S(2)}, u32[]{:S(2)}) collective-permute-start(bf16[8,8192]{1,0:T(8,128)(2,1)S(1)} %get-tuple-element.50), channel_id=1, source_target_pairs={{0,8},{1,9},{2,10},{3,11},{4,12},{5,13},{6,14},{7,15},{8,16},{9,17... | collective-permute-start | bytes 393224 | tf_op jit(solution)/shard_map/ppermute | solution.py:39
  18.7 1.5 %collective-permute-start.12 = (bf16[8,8192]{1,0:T(8,128)(2,1)S(1)}, bf16[8,8192]{1,0:T(8,128)(2,1)S(1)}, u32[]{:S(2)}, u32[]{:S(2)}) collective-permute-start(bf16[8,8192]{1,0:T(8,128)(2,1)S(1)} %get-tuple-element.51), channel_id=1, source_target_pairs={{0,4},{1,3},{2,6},{3,1},{4,0},{5,7},{6,2},{7,5},{8,12},{9,11},{10,... | collective-permute-start | bytes 393224 | tf_op jit(solution)/shard_map/ppermute | solution.py:30
  20.2 1.5 %collective-permute-start.11 = (bf16[8,8192]{1,0:T(8,128)(2,1)S(1)}, bf16[8,8192]{1,0:T(8,128)(2,1)S(1)}, u32[]{:S(2)}, u32[]{:S(2)}) collective-permute-start(bf16[8,8192]{1,0:T(8,128)(2,1)S(1)} %get-tuple-element.52), channel_id=1, source_target_pairs={{0,2},{1,5},{2,0},{3,7},{4,6},{5,1},{6,4},{7,3},{8,10},{9,13},{10,... | collective-permute-start | bytes 393224 | tf_op jit(solution)/shard_map/ppermute | solution.py:30
  21.6 0.0 collective-permute-done.5
  21.6 0.1 fusion.8
  21.8 0.6 %collective-permute-start.6 = (bf16[8,8192]{1,0:T(8,128)(2,1)S(1)}, bf16[8,8192]{1,0:T(8,128)(2,1)S(1)}, u32[]{:S(2)}, u32[]{:S(2)}) collective-permute-start(bf16[8,8192]{1,0:T(8,128)(2,1)S(1)} %get-tuple-element.48), channel_id=1, source_target_pairs={{0,2},{1,5},{2,0},{3,7},{4,6},{5,1},{6,4},{7,3},{8,10},{9,13},{10,... | collective-permute-start | bytes 393224 | tf_op jit(solution)/shard_map/ppermute | solution.py:30
  22.4 0.5 %collective-permute-start.7 = (bf16[8,8192]{1,0:T(8,128)(2,1)S(1)}, bf16[8,8192]{1,0:T(8,128)(2,1)S(1)}, u32[]{:S(2)}, u32[]{:S(2)}) collective-permute-start(bf16[8,8192]{1,0:T(8,128)(2,1)S(1)} %get-tuple-element.49), channel_id=1, source_target_pairs={{0,4},{1,3},{2,6},{3,1},{4,0},{5,7},{6,2},{7,5},{8,12},{9,11},{10,... | collective-permute-start | bytes 393224 | tf_op jit(solution)/shard_map/ppermute | solution.py:30
  22.9 1.5 %collective-permute-done.9 = bf16[8,8192]{1,0:T(8,128)(2,1)S(1)} collective-permute-done((bf16[8,8192]{1,0:T(8,128)(2,1)S(1)}, bf16[8,8192]{1,0:T(8,128)(2,1)S(1)}, u32[]{:S(2)}, u32[]{:S(2)}) %collective-permute-start.9) | collective-permute-done | bytes 131104 | tf_op jit(solution)/shard_map/ppermute | solution.py:39
  24.5 2.5 %collective-permute-start.10 = (bf16[8,8192]{1,0:T(8,128)(2,1)S(1)}, bf16[8,8192]{1,0:T(8,128)(2,1)S(1)}, u32[]{:S(2)}, u32[]{:S(2)}) collective-permute-start(bf16[8,8192]{1,0:T(8,128)(2,1)S(1)} %slice_add_fusion.1), channel_id=1, source_target_pairs={{0,6},{1,7},{2,4},{3,5},{4,2},{5,3},{6,0},{7,1},{8,14},{9,15},{10,... | collective-permute-start | bytes 393224 | tf_op jit(solution)/shard_map/ppermute | solution.py:30
  27.0 0.0 collective-permute-done.12
  27.0 0.0 collective-permute-done.11
  27.1 2.7 %collective-permute-start.13 = (bf16[8,8192]{1,0:T(8,128)(2,1)S(1)}, bf16[8,8192]{1,0:T(8,128)(2,1)S(1)}, u32[]{:S(2)}, u32[]{:S(2)}) collective-permute-start(bf16[8,8192]{1,0:T(8,128)(2,1)S(1)} %convert_element_type.71), channel_id=1, source_target_pairs={{0,8},{1,9},{2,10},{3,11},{4,12},{5,13},{6,14},{7,15},{8,16},{9,17... | collective-permute-start | bytes 393224 | tf_op jit(solution)/shard_map/ppermute | solution.py:45
  29.8 0.0 collective-permute-done.6
  29.8 0.0 collective-permute-done.7
  29.8 0.9 %collective-permute-done.10 = bf16[8,8192]{1,0:T(8,128)(2,1)S(1)} collective-permute-done((bf16[8,8192]{1,0:T(8,128)(2,1)S(1)}, bf16[8,8192]{1,0:T(8,128)(2,1)S(1)}, u32[]{:S(2)}, u32[]{:S(2)}) %collective-permute-start.10) | collective-permute-done | bytes 131104 | tf_op jit(solution)/shard_map/ppermute | solution.py:30
  30.7 0.1 fusion.7
  30.8 1.3 %collective-permute-start.14 = (bf16[8,8192]{1,0:T(8,128)(2,1)S(1)}, bf16[8,8192]{1,0:T(8,128)(2,1)S(1)}, u32[]{:S(2)}, u32[]{:S(2)}) collective-permute-start(bf16[8,8192]{1,0:T(8,128)(2,1)S(1)} %fusion.7), channel_id=1, source_target_pairs={{8,0},{9,1},{10,2},{11,3},{12,4},{13,5},{14,6},{15,7},{16,8},{17,9... | collective-permute-start | bytes 393224 | tf_op jit(solution)/shard_map/ppermute | solution.py:50
  32.1 0.2 collective-permute-done.13
  32.3 0.1 constant_dynamic-update-slice_fusion.12
  32.4 0.0 copy-start.3
  32.4 1.4 %collective-permute-start.19 = (bf16[8,8192]{1,0:T(8,128)(2,1)S(1)}, bf16[8,8192]{1,0:T(8,128)(2,1)S(1)}, u32[]{:S(2)}, u32[]{:S(2)}) collective-permute-start(bf16[8,8192]{1,0:T(8,128)(2,1)S(1)} %get-tuple-element.43), channel_id=1, source_target_pairs={{0,2},{1,5},{2,0},{3,7},{4,6},{5,1},{6,4},{7,3},{8,10},{9,13},{10,... | collective-permute-start | bytes 393224 | tf_op jit(solution)/shard_map/ppermute | solution.py:30
  33.8 1.2 %collective-permute-start.18 = (bf16[8,8192]{1,0:T(8,128)(2,1)S(1)}, bf16[8,8192]{1,0:T(8,128)(2,1)S(1)}, u32[]{:S(2)}, u32[]{:S(2)}) collective-permute-start(bf16[8,8192]{1,0:T(8,128)(2,1)S(1)} %get-tuple-element.43), channel_id=1, source_target_pairs={{0,4},{1,3},{2,6},{3,1},{4,0},{5,7},{6,2},{7,5},{8,12},{9,11},{10,... | collective-permute-start | bytes 393224 | tf_op jit(solution)/shard_map/ppermute | solution.py:30
  35.0 0.9 %collective-permute-start.17 = (bf16[8,8192]{1,0:T(8,128)(2,1)S(1)}, bf16[8,8192]{1,0:T(8,128)(2,1)S(1)}, u32[]{:S(2)}, u32[]{:S(2)}) collective-permute-start(bf16[8,8192]{1,0:T(8,128)(2,1)S(1)} %get-tuple-element.43), channel_id=1, source_target_pairs={{0,6},{1,7},{2,4},{3,5},{4,2},{5,3},{6,0},{7,1},{8,14},{9,15},{10,... | collective-permute-start | bytes 393224 | tf_op jit(solution)/shard_map/ppermute | solution.py:30
  35.9 1.8 %collective-permute-done.14 = bf16[8,8192]{1,0:T(8,128)(2,1)S(1)} collective-permute-done((bf16[8,8192]{1,0:T(8,128)(2,1)S(1)}, bf16[8,8192]{1,0:T(8,128)(2,1)S(1)}, u32[]{:S(2)}, u32[]{:S(2)}) %collective-permute-start.14) | collective-permute-done | bytes 131104 | tf_op jit(solution)/shard_map/ppermute | solution.py:50
  37.8 1.5 %collective-permute-start.16 = (bf16[8,8192]{1,0:T(8,128)(2,1)S(1)}, bf16[8,8192]{1,0:T(8,128)(2,1)S(1)}, u32[]{:S(2)}, u32[]{:S(2)}) collective-permute-start(bf16[8,8192]{1,0:T(8,128)(2,1)S(1)} %select_convert_fusion), channel_id=1, source_target_pairs={{0,4},{1,3},{2,6},{3,1},{4,0},{5,7},{6,2},{7,5},{8,12},{9,11},{10,... | collective-permute-start | bytes 393224 | tf_op jit(solution)/shard_map/ppermute | solution.py:30
  39.3 1.5 %collective-permute-start.15 = (bf16[8,8192]{1,0:T(8,128)(2,1)S(1)}, bf16[8,8192]{1,0:T(8,128)(2,1)S(1)}, u32[]{:S(2)}, u32[]{:S(2)}) collective-permute-start(bf16[8,8192]{1,0:T(8,128)(2,1)S(1)} %select_convert_fusion), channel_id=1, source_target_pairs={{0,6},{1,7},{2,4},{3,5},{4,2},{5,3},{6,0},{7,1},{8,14},{9,15},{10,... | collective-permute-start | bytes 393224 | tf_op jit(solution)/shard_map/ppermute | solution.py:30
  40.7 0.0 collective-permute-done.19
  40.7 2.8 %collective-permute-start.21 = (bf16[8,8192]{1,0:T(8,128)(2,1)S(1)}, bf16[8,8192]{1,0:T(8,128)(2,1)S(1)}, u32[]{:S(2)}, u32[]{:S(2)}) collective-permute-start(bf16[8,8192]{1,0:T(8,128)(2,1)S(1)} %collective-permute-done.19), channel_id=1, source_target_pairs={{8,0},{9,1},{10,2},{11,3},{12,4},{13,5},{14,6},{15,7},{16,8},{17,9... | collective-permute-start | bytes 393224 | tf_op jit(solution)/shard_map/ppermute | solution.py:55
  43.5 0.0 collective-permute-done.18
  43.5 0.0 collective-permute-done.17
  43.6 0.1 collective-permute-start.20
  43.7 2.3 %collective-permute-done.21 = bf16[8,8192]{1,0:T(8,128)(2,1)S(1)} collective-permute-done((bf16[8,8192]{1,0:T(8,128)(2,1)S(1)}, bf16[8,8192]{1,0:T(8,128)(2,1)S(1)}, u32[]{:S(2)}, u32[]{:S(2)}) %collective-permute-start.21) | collective-permute-done | bytes 131104 | tf_op jit(solution)/shard_map/ppermute | solution.py:55
  46.1 0.1 collective-permute-start.23
  46.1 0.0 collective-permute-done.16
  46.2 0.0 collective-permute-done.15
  46.2 0.0 collective-permute-done.20
  46.2 0.5 %collective-permute-start.22 = (bf16[24,8192]{1,0:T(8,128)(2,1)S(1)}, bf16[24,8192]{1,0:T(8,128)(2,1)S(1)}, u32[]{:S(2)}, u32[]{:S(2)}) collective-permute-start(bf16[24,8192]{1,0:T(8,128)(2,1)S(1)} %pad_maximum_fusion.2), channel_id=1, source_target_pairs={{0,1},{1,0},{2,3},{3,2},{4,5},{5,4},{6,7},{7,6},{8,9},{9,8},{10,11... | collective-permute-start | bytes 1179656 | tf_op jit(solution)/shard_map/ppermute | solution.py:34
  46.8 1.6 %grad_own.1 = (f32[64,256]{1,0:T(8,128)S(1)}, f32[8,128]{1,0:T(8,128)}) custom-call(bf16[64,8192]{1,0:T(8,128)(2,1)S(1)} %constant_dynamic-update-slice_fusion.8.rows_ref, bf16[256,8192]{1,0:T(8,128)(2,1)S(1)} %get-tuple-element.29.dec_ref), custom_call_target="tpu_custom_call" | custom-call | flops 268435456 | bytes 4194304 | tf_op jit(solution)/shard_map/grad_own/pallas_call | solution.py:207
  48.4 0.0 collective-permute-done.23
  48.5 0.0 collective-permute-done.22
  48.5 0.1 pad_maximum_fusion.rows_ref
  48.5 1.9 %grad_all.1 = f32[1,64,256]{2,1,0:T(8,128)} custom-call(bf16[64,8192]{1,0:T(8,128)(2,1)S(1)} %pad_maximum_fusion.rows_ref, bf16[256,8192]{1,0:T(8,128)(2,1)S(1)} %get-tuple-element.33.dec_ref, f32[64,256]{1,0:T(8,128)S(1)} %get-tuple-element.41.own_ref), custom_call_target="tpu_custom_call" | custom-call | flops 268435456 | bytes 4194304 | tf_op jit(solution)/shard_map/grad_all/pallas_call | solution.py:219
  (31 shorter events, 0.5 us)
Async XLA Ops:
  0.6 9.4 %copy-start = (s32[1,2,2]{2,1,0:T(2,128)S(1)}, s32[1,2,2]{2,1,0:T(2,128)}, u32[]{:S(2)}) copy-start(s32[1,2,2]{2,1,0:T(2,128)} %param.9) | copy-start | bytes 52
  0.6 9.4 %copy-start.1 = (bf16[1,256]{1,0:T(2,128)(2,1)S(1)}, bf16[1,256]{1,0:T(2,128)(2,1)}, u32[]{:S(2)}) copy-start(bf16[1,256]{1,0:T(2,128)(2,1)} %bias_ref) | copy-start | bytes 1540
  0.7 10.8 %copy-start.4 = (bf16[1,8,8192]{2,1,0:T(8,128)(2,1)S(1)}, bf16[1,8,8192]{2,1,0:T(8,128)(2,1)}, u32[]{:S(2)}) copy-start(bf16[1,8,8192]{2,1,0:T(8,128)(2,1)} %param.6) | copy-start | bytes 393220
  0.7 9.5 %collective-permute-start = (bf16[8,8192]{1,0:T(8,128)(2,1)}, bf16[8,8192]{1,0:T(8,128)(2,1)S(1)}, u32[]{:S(2)}, u32[]{:S(2)}) collective-permute-start(bf16[8,8192]{1,0:T(8,128)(2,1)} %bitcast.15), channel_id=1, source_target_pairs={{0,6},{1,7},{2,4},{3,5},{4,2},{5,3},{6,0},{7,1},{8,14},{9,15},{10,... | collective-permute-start | bytes 393224 | tf_op jit(solution)/shard_map/ppermute | solution.py:30
  4.6 6.9 %collective-permute-start.3 = (bf16[8,8192]{1,0:T(8,128)(2,1)}, bf16[8,8192]{1,0:T(8,128)(2,1)S(1)}, u32[]{:S(2)}, u32[]{:S(2)}) collective-permute-start(bf16[8,8192]{1,0:T(8,128)(2,1)} %bitcast.16), channel_id=1, source_target_pairs={{0,1},{1,0},{2,3},{3,2},{4,5},{5,4},{6,7},{7,6},{8,9},{9,8},{10,11... | collective-permute-start | bytes 393224 | tf_op jit(solution)/shard_map/ppermute | solution.py:34
  4.6 6.8 %collective-permute-start.2 = (bf16[8,8192]{1,0:T(8,128)(2,1)}, bf16[8,8192]{1,0:T(8,128)(2,1)S(1)}, u32[]{:S(2)}, u32[]{:S(2)}) collective-permute-start(bf16[8,8192]{1,0:T(8,128)(2,1)} %bitcast.17), channel_id=1, source_target_pairs={{0,2},{1,5},{2,0},{3,7},{4,6},{5,1},{6,4},{7,3},{8,10},{9,13},{10,... | collective-permute-start | bytes 393224 | tf_op jit(solution)/shard_map/ppermute | solution.py:30
  5.2 6.0 %collective-permute-start.1 = (bf16[8,8192]{1,0:T(8,128)(2,1)}, bf16[8,8192]{1,0:T(8,128)(2,1)S(1)}, u32[]{:S(2)}, u32[]{:S(2)}) collective-permute-start(bf16[8,8192]{1,0:T(8,128)(2,1)} %bitcast.18), channel_id=1, source_target_pairs={{0,4},{1,3},{2,6},{3,1},{4,0},{5,7},{6,2},{7,5},{8,12},{9,11},{10,... | collective-permute-start | bytes 393224 | tf_op jit(solution)/shard_map/ppermute | solution.py:30
  11.4 1.8 %collective-permute-start.4 = (bf16[24,8192]{1,0:T(8,128)(2,1)S(1)}, bf16[24,8192]{1,0:T(8,128)(2,1)S(1)}, u32[]{:S(2)}, u32[]{:S(2)}) collective-permute-start(bf16[24,8192]{1,0:T(8,128)(2,1)S(1)} %constant_dynamic-update-slice_fusion), channel_id=1, source_target_pairs={{0,1},{1,0},{2,3},{3,2},{4,5},{5,4},{6,7},{7,6},{8,9},{9,8},{10,11... | collective-permute-start | bytes 1179656 | tf_op jit(solution)/shard_map/ppermute | solution.py:34
  14.9 2.0 %collective-permute-start.8 = (bf16[32,8192]{1,0:T(8,128)(2,1)S(1)}, bf16[32,8192]{1,0:T(8,128)(2,1)S(1)}, u32[]{:S(2)}, u32[]{:S(2)}) collective-permute-start(bf16[32,8192]{1,0:T(8,128)(2,1)S(1)} %get-tuple-element.35), channel_id=1, source_target_pairs={{0,1},{1,0},{2,3},{3,2},{4,5},{5,4},{6,7},{7,6},{8,9},{9,8},{10,11... | collective-permute-start | bytes 1572872 | tf_op jit(solution)/shard_map/ppermute | solution.py:34
  16.0 5.7 %collective-permute-start.5 = (bf16[32,8192]{1,0:T(8,128)(2,1)S(1)}, bf16[32,8192]{1,0:T(8,128)(2,1)S(1)}, u32[]{:S(2)}, u32[]{:S(2)}) collective-permute-start(bf16[32,8192]{1,0:T(8,128)(2,1)S(1)} %get-tuple-element.31), channel_id=1, source_target_pairs={{0,1},{1,0},{2,3},{3,2},{4,5},{5,4},{6,7},{7,6},{8,9},{9,8},{10,11... | collective-permute-start | bytes 1572872 | tf_op jit(solution)/shard_map/ppermute | solution.py:34
  16.9 13.8 %copy-start.2 = (bf16[1,8,8192]{2,1,0:T(8,128)(2,1)S(1)}, bf16[1,8,8192]{2,1,0:T(8,128)(2,1)}, u32[]{:S(2)}) copy-start(bf16[1,8,8192]{2,1,0:T(8,128)(2,1)} %param.11) | copy-start | bytes 393220
  17.0 7.5 %collective-permute-start.9 = (bf16[8,8192]{1,0:T(8,128)(2,1)S(1)}, bf16[8,8192]{1,0:T(8,128)(2,1)S(1)}, u32[]{:S(2)}, u32[]{:S(2)}) collective-permute-start(bf16[8,8192]{1,0:T(8,128)(2,1)S(1)} %get-tuple-element.50), channel_id=1, source_target_pairs={{0,8},{1,9},{2,10},{3,11},{4,12},{5,13},{6,14},{7,15},{8,16},{9,17... | collective-permute-start | bytes 393224 | tf_op jit(solution)/shard_map/ppermute | solution.py:39
  18.7 8.3 %collective-permute-start.12 = (bf16[8,8192]{1,0:T(8,128)(2,1)S(1)}, bf16[8,8192]{1,0:T(8,128)(2,1)S(1)}, u32[]{:S(2)}, u32[]{:S(2)}) collective-permute-start(bf16[8,8192]{1,0:T(8,128)(2,1)S(1)} %get-tuple-element.51), channel_id=1, source_target_pairs={{0,4},{1,3},{2,6},{3,1},{4,0},{5,7},{6,2},{7,5},{8,12},{9,11},{10,... | collective-permute-start | bytes 393224 | tf_op jit(solution)/shard_map/ppermute | solution.py:30
  20.2 6.9 %collective-permute-start.11 = (bf16[8,8192]{1,0:T(8,128)(2,1)S(1)}, bf16[8,8192]{1,0:T(8,128)(2,1)S(1)}, u32[]{:S(2)}, u32[]{:S(2)}) collective-permute-start(bf16[8,8192]{1,0:T(8,128)(2,1)S(1)} %get-tuple-element.52), channel_id=1, source_target_pairs={{0,2},{1,5},{2,0},{3,7},{4,6},{5,1},{6,4},{7,3},{8,10},{9,13},{10,... | collective-permute-start | bytes 393224 | tf_op jit(solution)/shard_map/ppermute | solution.py:30
  21.8 8.0 %collective-permute-start.6 = (bf16[8,8192]{1,0:T(8,128)(2,1)S(1)}, bf16[8,8192]{1,0:T(8,128)(2,1)S(1)}, u32[]{:S(2)}, u32[]{:S(2)}) collective-permute-start(bf16[8,8192]{1,0:T(8,128)(2,1)S(1)} %get-tuple-element.48), channel_id=1, source_target_pairs={{0,2},{1,5},{2,0},{3,7},{4,6},{5,1},{6,4},{7,3},{8,10},{9,13},{10,... | collective-permute-start | bytes 393224 | tf_op jit(solution)/shard_map/ppermute | solution.py:30
  22.4 7.4 %collective-permute-start.7 = (bf16[8,8192]{1,0:T(8,128)(2,1)S(1)}, bf16[8,8192]{1,0:T(8,128)(2,1)S(1)}, u32[]{:S(2)}, u32[]{:S(2)}) collective-permute-start(bf16[8,8192]{1,0:T(8,128)(2,1)S(1)} %get-tuple-element.49), channel_id=1, source_target_pairs={{0,4},{1,3},{2,6},{3,1},{4,0},{5,7},{6,2},{7,5},{8,12},{9,11},{10,... | collective-permute-start | bytes 393224 | tf_op jit(solution)/shard_map/ppermute | solution.py:30
  24.5 6.2 %collective-permute-start.10 = (bf16[8,8192]{1,0:T(8,128)(2,1)S(1)}, bf16[8,8192]{1,0:T(8,128)(2,1)S(1)}, u32[]{:S(2)}, u32[]{:S(2)}) collective-permute-start(bf16[8,8192]{1,0:T(8,128)(2,1)S(1)} %slice_add_fusion.1), channel_id=1, source_target_pairs={{0,6},{1,7},{2,4},{3,5},{4,2},{5,3},{6,0},{7,1},{8,14},{9,15},{10,... | collective-permute-start | bytes 393224 | tf_op jit(solution)/shard_map/ppermute | solution.py:30
  27.1 5.2 %collective-permute-start.13 = (bf16[8,8192]{1,0:T(8,128)(2,1)S(1)}, bf16[8,8192]{1,0:T(8,128)(2,1)S(1)}, u32[]{:S(2)}, u32[]{:S(2)}) collective-permute-start(bf16[8,8192]{1,0:T(8,128)(2,1)S(1)} %convert_element_type.71), channel_id=1, source_target_pairs={{0,8},{1,9},{2,10},{3,11},{4,12},{5,13},{6,14},{7,15},{8,16},{9,17... | collective-permute-start | bytes 393224 | tf_op jit(solution)/shard_map/ppermute | solution.py:45
  30.8 6.9 %collective-permute-start.14 = (bf16[8,8192]{1,0:T(8,128)(2,1)S(1)}, bf16[8,8192]{1,0:T(8,128)(2,1)S(1)}, u32[]{:S(2)}, u32[]{:S(2)}) collective-permute-start(bf16[8,8192]{1,0:T(8,128)(2,1)S(1)} %fusion.7), channel_id=1, source_target_pairs={{8,0},{9,1},{10,2},{11,3},{12,4},{13,5},{14,6},{15,7},{16,8},{17,9... | collective-permute-start | bytes 393224 | tf_op jit(solution)/shard_map/ppermute | solution.py:50
  32.4 16.1 %copy-start.3 = (bf16[8,8192]{1,0:T(8,128)(2,1)}, bf16[8,8192]{1,0:T(8,128)(2,1)S(1)}, u32[]{:S(2)}) copy-start(bf16[8,8192]{1,0:T(8,128)(2,1)S(1)} %get-tuple-element.43) | copy-start | bytes 393220
  32.4 8.3 %collective-permute-start.19 = (bf16[8,8192]{1,0:T(8,128)(2,1)S(1)}, bf16[8,8192]{1,0:T(8,128)(2,1)S(1)}, u32[]{:S(2)}, u32[]{:S(2)}) collective-permute-start(bf16[8,8192]{1,0:T(8,128)(2,1)S(1)} %get-tuple-element.43), channel_id=1, source_target_pairs={{0,2},{1,5},{2,0},{3,7},{4,6},{5,1},{6,4},{7,3},{8,10},{9,13},{10,... | collective-permute-start | bytes 393224 | tf_op jit(solution)/shard_map/ppermute | solution.py:30
  33.8 9.7 %collective-permute-start.18 = (bf16[8,8192]{1,0:T(8,128)(2,1)S(1)}, bf16[8,8192]{1,0:T(8,128)(2,1)S(1)}, u32[]{:S(2)}, u32[]{:S(2)}) collective-permute-start(bf16[8,8192]{1,0:T(8,128)(2,1)S(1)} %get-tuple-element.43), channel_id=1, source_target_pairs={{0,4},{1,3},{2,6},{3,1},{4,0},{5,7},{6,2},{7,5},{8,12},{9,11},{10,... | collective-permute-start | bytes 393224 | tf_op jit(solution)/shard_map/ppermute | solution.py:30
  35.0 8.5 %collective-permute-start.17 = (bf16[8,8192]{1,0:T(8,128)(2,1)S(1)}, bf16[8,8192]{1,0:T(8,128)(2,1)S(1)}, u32[]{:S(2)}, u32[]{:S(2)}) collective-permute-start(bf16[8,8192]{1,0:T(8,128)(2,1)S(1)} %get-tuple-element.43), channel_id=1, source_target_pairs={{0,6},{1,7},{2,4},{3,5},{4,2},{5,3},{6,0},{7,1},{8,14},{9,15},{10,... | collective-permute-start | bytes 393224 | tf_op jit(solution)/shard_map/ppermute | solution.py:30
  37.8 8.4 %collective-permute-start.16 = (bf16[8,8192]{1,0:T(8,128)(2,1)S(1)}, bf16[8,8192]{1,0:T(8,128)(2,1)S(1)}, u32[]{:S(2)}, u32[]{:S(2)}) collective-permute-start(bf16[8,8192]{1,0:T(8,128)(2,1)S(1)} %select_convert_fusion), channel_id=1, source_target_pairs={{0,4},{1,3},{2,6},{3,1},{4,0},{5,7},{6,2},{7,5},{8,12},{9,11},{10,... | collective-permute-start | bytes 393224 | tf_op jit(solution)/shard_map/ppermute | solution.py:30
  39.3 6.9 %collective-permute-start.15 = (bf16[8,8192]{1,0:T(8,128)(2,1)S(1)}, bf16[8,8192]{1,0:T(8,128)(2,1)S(1)}, u32[]{:S(2)}, u32[]{:S(2)}) collective-permute-start(bf16[8,8192]{1,0:T(8,128)(2,1)S(1)} %select_convert_fusion), channel_id=1, source_target_pairs={{0,6},{1,7},{2,4},{3,5},{4,2},{5,3},{6,0},{7,1},{8,14},{9,15},{10,... | collective-permute-start | bytes 393224 | tf_op jit(solution)/shard_map/ppermute | solution.py:30
  40.7 5.3 %collective-permute-start.21 = (bf16[8,8192]{1,0:T(8,128)(2,1)S(1)}, bf16[8,8192]{1,0:T(8,128)(2,1)S(1)}, u32[]{:S(2)}, u32[]{:S(2)}) collective-permute-start(bf16[8,8192]{1,0:T(8,128)(2,1)S(1)} %collective-permute-done.19), channel_id=1, source_target_pairs={{8,0},{9,1},{10,2},{11,3},{12,4},{13,5},{14,6},{15,7},{16,8},{17,9... | collective-permute-start | bytes 393224 | tf_op jit(solution)/shard_map/ppermute | solution.py:55
  43.6 2.6 %collective-permute-start.20 = (bf16[32,8192]{1,0:T(8,128)(2,1)S(1)}, bf16[32,8192]{1,0:T(8,128)(2,1)S(1)}, u32[]{:S(2)}, u32[]{:S(2)}) collective-permute-start(bf16[32,8192]{1,0:T(8,128)(2,1)S(1)} %pad_maximum_fusion.1), channel_id=1, source_target_pairs={{0,1},{1,0},{2,3},{3,2},{4,5},{5,4},{6,7},{7,6},{8,9},{9,8},{10,11... | collective-permute-start | bytes 1572872 | tf_op jit(solution)/shard_map/ppermute | solution.py:34
  46.1 2.4 %collective-permute-start.23 = (bf16[8,8192]{1,0:T(8,128)(2,1)S(1)}, bf16[8,8192]{1,0:T(8,128)(2,1)S(1)}, u32[]{:S(2)}, u32[]{:S(2)}) collective-permute-start(bf16[8,8192]{1,0:T(8,128)(2,1)S(1)} %broadcast_select_fusion), channel_id=1, source_target_pairs={{0,1},{1,0},{2,3},{3,2},{4,5},{5,4},{6,7},{7,6},{8,9},{9,8},{10,11... | collective-permute-start | bytes 393224 | tf_op jit(solution)/shard_map/ppermute | solution.py:34
  46.2 2.2 %collective-permute-start.22 = (bf16[24,8192]{1,0:T(8,128)(2,1)S(1)}, bf16[24,8192]{1,0:T(8,128)(2,1)S(1)}, u32[]{:S(2)}, u32[]{:S(2)}) collective-permute-start(bf16[24,8192]{1,0:T(8,128)(2,1)S(1)} %pad_maximum_fusion.2), channel_id=1, source_target_pairs={{0,1},{1,0},{2,3},{3,2},{4,5},{5,4},{6,7},{7,6},{8,9},{9,8},{10,11... | collective-permute-start | bytes 1179656 | tf_op jit(solution)/shard_map/ppermute | solution.py:34

commit v27 on v26

--- a/solution.py
+++ b/solution.py
@@ -178,6 +178,15 @@
 
 
 def back(rows_ref, dec_ref):
+    return summed_over(
+        rows_ref.shape[1],
+        lambda part: lax.dot_general(
+            rows_ref[:, part], dec_ref[:, part], (((1,), (1,)), ((), ())), preferred_element_type=jnp.float32
+        ),
+    )
+
+
+def back_turned(rows_ref, dec_ref):
     turned_round = summed_over(
         rows_ref.shape[1],
         lambda part: lax.dot_general(
@@ -192,7 +201,7 @@
 
 
 def grad_all_kernel(tokens, rows_ref, dec_ref, own_ref, out_ref):
-    total = own_ref[...] + back(rows_ref, dec_ref)
+    total = own_ref[...] + back_turned(rows_ref, dec_ref)
     group = total.shape[0] // tokens
     for block in range(group):
         chips = group // CORES

time: 50.6 us -> 50.4 us (level)
  no operation moved by 1% of the time
where the time goes in v27:
time: 50.4 us; the launch traced here: 50.2 us
  starting transfers between devices  27.6 us (55%)
  waiting for transfers between devices  10 us (20%)
  Pallas kernels  9.78 us (19%)
  between operations  1.05 us (2%)
  matrix products  0.8 us (2%)
  other arithmetic  0.69 us (1%)
    ppermute x13, starting transfers between devices, across(): return lax.ppermute(value, AXIS, pairs)  17.8 us
    pallas_call x1, Pallas kernels, loaded(): pl.pallas_call(load_kernel, out_shape=[pltpu.VMEM(enc.shape[1:], enc.dtyp...  4.68 us
    ppermute x1, starting transfers between devices, rotated_down(): lax.ppermute(value, AXIS, [((i + group) % size, i) for i in range(size)])  2.8 us
    ppermute x1, starting transfers between devices, shifted(): lax.ppermute(value, AXIS, [(i, i + group) for i in range(size - group)])  2.7 us
    ppermute x1, waiting for transfers between devices, rotated_down(): lax.ppermute(value, AXIS, [((i + group) % size, i) for i in range(size)])  2.34 us
    ppermute x13, waiting for transfers between devices, across(): return lax.ppermute(value, AXIS, pairs)  2.1 us
    ppermute x7, waiting for transfers between devices, other_core(): lax.ppermute(value, AXIS, [(i, i ^ 1) for i in range(lax.axis_size(AXIS))])  2.1 us
    pallas_call x1, Pallas kernels, grad_all(): pl.pallas_call(functools.partial(grad_all_kernel, tokens), out_shape=jax....  1.91 us
  transfers between devices with their start and end apart: 24, of which 9 were waited for; matrix products, arithmetic and copies ran while one was open for 2% of the time, Pallas kernels for 14%

profile of v27, /device:TPU:0, one launch (start us, length us, event | category | flops | bytes accessed | tf_op | source)
XLA Modules:
  0.0 50.2 jit_solution(14985115998099292987)
XLA Ops:
  0.6 0.0 copy-start
  0.6 0.0 copy-start.1
  0.7 4.0 %collective-permute-start = (bf16[8,8192]{1,0:T(8,128)(2,1)}, bf16[8,8192]{1,0:T(8,128)(2,1)S(1)}, u32[]{:S(2)}, u32[]{:S(2)}) collective-permute-start(bf16[8,8192]{1,0:T(8,128)(2,1)} %bitcast.15), channel_id=1, source_target_pairs={{0,6},{1,7},{2,4},{3,5},{4,2},{5,3},{6,0},{7,1},{8,14},{9,15},{10,... | collective-permute-start | bytes 393224 | tf_op jit(solution)/shard_map/ppermute | solution.py:30
  4.6 0.0 collective-permute-start.3
  4.6 0.5 %collective-permute-start.2 = (bf16[8,8192]{1,0:T(8,128)(2,1)}, bf16[8,8192]{1,0:T(8,128)(2,1)S(1)}, u32[]{:S(2)}, u32[]{:S(2)}) collective-permute-start(bf16[8,8192]{1,0:T(8,128)(2,1)} %bitcast.17), channel_id=1, source_target_pairs={{0,2},{1,5},{2,0},{3,7},{4,6},{5,1},{6,4},{7,3},{8,10},{9,13},{10,... | collective-permute-start | bytes 393224 | tf_op jit(solution)/shard_map/ppermute | solution.py:30
  5.2 0.2 collective-permute-start.1
  5.3 4.7 %load_weights.1 = (bf16[8192,256]{1,0:T(8,128)(2,1)S(1)}, bf16[256,8192]{1,0:T(8,128)(2,1)S(1)}, bf16[256,8192]{1,0:T(8,128)(2,1)S(1)}) custom-call(bf16[1,8192,256]{2,1,0:T(8,128)(2,1)} %enc_hbm.1, bf16[1,2,256,8192]{3,2,1,0:T(8,128)(2,1)} %dec_hbm.1), custom_call_target="tpu_custom_call" | custom-call | bytes 25165824 | tf_op jit(solution)/shard_map/load_weights/pallas_call | solution.py:92
  10.1 0.1 gate.1
  10.2 0.0 collective-permute-done
  10.2 0.9 %collective-permute-done.1 = bf16[8,8192]{1,0:T(8,128)(2,1)S(1)} collective-permute-done((bf16[8,8192]{1,0:T(8,128)(2,1)}, bf16[8,8192]{1,0:T(8,128)(2,1)S(1)}, u32[]{:S(2)}, u32[]{:S(2)}) %collective-permute-start.1) | collective-permute-done | bytes 131104 | tf_op jit(solution)/shard_map/ppermute | solution.py:30
  11.2 0.2 collective-permute-done.2
  11.4 0.1 collective-permute-start.4
  11.5 0.0 copy-done.4
  11.6 0.0 collective-permute-done.3
  11.6 1.6 %collective-permute-done.4 = bf16[24,8192]{1,0:T(8,128)(2,1)S(1)} collective-permute-done((bf16[24,8192]{1,0:T(8,128)(2,1)S(1)}, bf16[24,8192]{1,0:T(8,128)(2,1)S(1)}, u32[]{:S(2)}, u32[]{:S(2)}) %collective-permute-start.4) | collective-permute-done | bytes 393248 | tf_op jit(solution)/shard_map/ppermute | solution.py:34
  13.2 0.8 %fusion.2.codes_ref = bf16[64,256]{1,0:T(8,128)(2,1)S(1)} fusion(f32[64,256]{1,0:T(8,128)S(1)} %get-tuple-element.28, f32[64,256]{1,0:T(8,128)S(1)} %get-tuple-element.27, bf16[64,8192]{1,0:T(8,128)(2,1)S(1)} %slice_dynamic-update-slice_fusion, bf16[8192,256]{1,0:T(8,128)(2,1)S(1)} %get-tuple-element.24), kind=kOutput, calls=%fused_computation.3 | convolution fusion | flops 268500992 | bytes 5406720 | tf_op jit(solution)/shard_map/dot_general | solution.py:265
  14.1 0.8 %decode.3 = (f32[32,8192]{1,0:T(8,128)S(1)}, bf16[32,8192]{1,0:T(8,128)(2,1)S(1)}) custom-call(bf16[64,256]{1,0:T(8,128)(2,1)S(1)} %fusion.2.codes_ref, bf16[256,8192]{1,0:T(8,128)(2,1)S(1)} %get-tuple-element.33.dec_ref), custom_call_target="tpu_custom_call" | custom-call | flops 268435456 | bytes 4194304 | tf_op jit(solution)/shard_map/decode/pallas_call | solution.py:169
  14.9 0.2 collective-permute-start.8
  15.1 0.8 %decode.2 = (f32[32,8192]{1,0:T(8,128)S(1)}, bf16[32,8192]{1,0:T(8,128)(2,1)S(1)}) custom-call(bf16[64,256]{1,0:T(8,128)(2,1)S(1)} %fusion.2.codes_ref, bf16[256,8192]{1,0:T(8,128)(2,1)S(1)} %get-tuple-element.29.dec_ref), custom_call_target="tpu_custom_call" | custom-call | flops 268435456 | bytes 4194304 | tf_op jit(solution)/shard_map/decode/pallas_call | solution.py:169
  16.0 0.4 collective-permute-start.5
  16.4 0.5 collective-permute-done.8
  16.9 0.1 fusion.9
  17.0 1.6 %collective-permute-start.9 = (bf16[8,8192]{1,0:T(8,128)(2,1)S(1)}, bf16[8,8192]{1,0:T(8,128)(2,1)S(1)}, u32[]{:S(2)}, u32[]{:S(2)}) collective-permute-start(bf16[8,8192]{1,0:T(8,128)(2,1)S(1)} %get-tuple-element.50), channel_id=1, source_target_pairs={{0,8},{1,9},{2,10},{3,11},{4,12},{5,13},{6,14},{7,15},{8,16},{9,17... | collective-permute-start | bytes 393224 | tf_op jit(solution)/shard_map/ppermute | solution.py:39
  18.7 1.5 %collective-permute-start.12 = (bf16[8,8192]{1,0:T(8,128)(2,1)S(1)}, bf16[8,8192]{1,0:T(8,128)(2,1)S(1)}, u32[]{:S(2)}, u32[]{:S(2)}) collective-permute-start(bf16[8,8192]{1,0:T(8,128)(2,1)S(1)} %get-tuple-element.51), channel_id=1, source_target_pairs={{0,4},{1,3},{2,6},{3,1},{4,0},{5,7},{6,2},{7,5},{8,12},{9,11},{10,... | collective-permute-start | bytes 393224 | tf_op jit(solution)/shard_map/ppermute | solution.py:30
  20.2 1.5 %collective-permute-start.11 = (bf16[8,8192]{1,0:T(8,128)(2,1)S(1)}, bf16[8,8192]{1,0:T(8,128)(2,1)S(1)}, u32[]{:S(2)}, u32[]{:S(2)}) collective-permute-start(bf16[8,8192]{1,0:T(8,128)(2,1)S(1)} %get-tuple-element.52), channel_id=1, source_target_pairs={{0,2},{1,5},{2,0},{3,7},{4,6},{5,1},{6,4},{7,3},{8,10},{9,13},{10,... | collective-permute-start | bytes 393224 | tf_op jit(solution)/shard_map/ppermute | solution.py:30
  21.6 0.0 collective-permute-done.5
  21.6 0.1 fusion.8
  21.8 0.6 %collective-permute-start.6 = (bf16[8,8192]{1,0:T(8,128)(2,1)S(1)}, bf16[8,8192]{1,0:T(8,128)(2,1)S(1)}, u32[]{:S(2)}, u32[]{:S(2)}) collective-permute-start(bf16[8,8192]{1,0:T(8,128)(2,1)S(1)} %get-tuple-element.48), channel_id=1, source_target_pairs={{0,2},{1,5},{2,0},{3,7},{4,6},{5,1},{6,4},{7,3},{8,10},{9,13},{10,... | collective-permute-start | bytes 393224 | tf_op jit(solution)/shard_map/ppermute | solution.py:30
  22.4 0.5 %collective-permute-start.7 = (bf16[8,8192]{1,0:T(8,128)(2,1)S(1)}, bf16[8,8192]{1,0:T(8,128)(2,1)S(1)}, u32[]{:S(2)}, u32[]{:S(2)}) collective-permute-start(bf16[8,8192]{1,0:T(8,128)(2,1)S(1)} %get-tuple-element.49), channel_id=1, source_target_pairs={{0,4},{1,3},{2,6},{3,1},{4,0},{5,7},{6,2},{7,5},{8,12},{9,11},{10,... | collective-permute-start | bytes 393224 | tf_op jit(solution)/shard_map/ppermute | solution.py:30
  22.9 1.5 %collective-permute-done.9 = bf16[8,8192]{1,0:T(8,128)(2,1)S(1)} collective-permute-done((bf16[8,8192]{1,0:T(8,128)(2,1)S(1)}, bf16[8,8192]{1,0:T(8,128)(2,1)S(1)}, u32[]{:S(2)}, u32[]{:S(2)}) %collective-permute-start.9) | collective-permute-done | bytes 131104 | tf_op jit(solution)/shard_map/ppermute | solution.py:39
  24.5 2.5 %collective-permute-start.10 = (bf16[8,8192]{1,0:T(8,128)(2,1)S(1)}, bf16[8,8192]{1,0:T(8,128)(2,1)S(1)}, u32[]{:S(2)}, u32[]{:S(2)}) collective-permute-start(bf16[8,8192]{1,0:T(8,128)(2,1)S(1)} %slice_add_fusion.1), channel_id=1, source_target_pairs={{0,6},{1,7},{2,4},{3,5},{4,2},{5,3},{6,0},{7,1},{8,14},{9,15},{10,... | collective-permute-start | bytes 393224 | tf_op jit(solution)/shard_map/ppermute | solution.py:30
  27.0 0.0 collective-permute-done.12
  27.0 0.0 collective-permute-done.11
  27.1 2.7 %collective-permute-start.13 = (bf16[8,8192]{1,0:T(8,128)(2,1)S(1)}, bf16[8,8192]{1,0:T(8,128)(2,1)S(1)}, u32[]{:S(2)}, u32[]{:S(2)}) collective-permute-start(bf16[8,8192]{1,0:T(8,128)(2,1)S(1)} %convert_element_type.71), channel_id=1, source_target_pairs={{0,8},{1,9},{2,10},{3,11},{4,12},{5,13},{6,14},{7,15},{8,16},{9,17... | collective-permute-start | bytes 393224 | tf_op jit(solution)/shard_map/ppermute | solution.py:45
  29.8 0.0 collective-permute-done.6
  29.8 0.0 collective-permute-done.7
  29.8 0.9 %collective-permute-done.10 = bf16[8,8192]{1,0:T(8,128)(2,1)S(1)} collective-permute-done((bf16[8,8192]{1,0:T(8,128)(2,1)S(1)}, bf16[8,8192]{1,0:T(8,128)(2,1)S(1)}, u32[]{:S(2)}, u32[]{:S(2)}) %collective-permute-start.10) | collective-permute-done | bytes 131104 | tf_op jit(solution)/shard_map/ppermute | solution.py:30
  30.7 0.1 fusion.7
  30.8 1.3 %collective-permute-start.14 = (bf16[8,8192]{1,0:T(8,128)(2,1)S(1)}, bf16[8,8192]{1,0:T(8,128)(2,1)S(1)}, u32[]{:S(2)}, u32[]{:S(2)}) collective-permute-start(bf16[8,8192]{1,0:T(8,128)(2,1)S(1)} %fusion.7), channel_id=1, source_target_pairs={{8,0},{9,1},{10,2},{11,3},{12,4},{13,5},{14,6},{15,7},{16,8},{17,9... | collective-permute-start | bytes 393224 | tf_op jit(solution)/shard_map/ppermute | solution.py:50
  32.1 0.2 collective-permute-done.13
  32.3 0.1 constant_dynamic-update-slice_fusion.12
  32.4 0.0 copy-start.3
  32.4 1.4 %collective-permute-start.19 = (bf16[8,8192]{1,0:T(8,128)(2,1)S(1)}, bf16[8,8192]{1,0:T(8,128)(2,1)S(1)}, u32[]{:S(2)}, u32[]{:S(2)}) collective-permute-start(bf16[8,8192]{1,0:T(8,128)(2,1)S(1)} %get-tuple-element.43), channel_id=1, source_target_pairs={{0,2},{1,5},{2,0},{3,7},{4,6},{5,1},{6,4},{7,3},{8,10},{9,13},{10,... | collective-permute-start | bytes 393224 | tf_op jit(solution)/shard_map/ppermute | solution.py:30
  33.8 1.2 %collective-permute-start.18 = (bf16[8,8192]{1,0:T(8,128)(2,1)S(1)}, bf16[8,8192]{1,0:T(8,128)(2,1)S(1)}, u32[]{:S(2)}, u32[]{:S(2)}) collective-permute-start(bf16[8,8192]{1,0:T(8,128)(2,1)S(1)} %get-tuple-element.43), channel_id=1, source_target_pairs={{0,4},{1,3},{2,6},{3,1},{4,0},{5,7},{6,2},{7,5},{8,12},{9,11},{10,... | collective-permute-start | bytes 393224 | tf_op jit(solution)/shard_map/ppermute | solution.py:30
  35.0 0.9 %collective-permute-start.17 = (bf16[8,8192]{1,0:T(8,128)(2,1)S(1)}, bf16[8,8192]{1,0:T(8,128)(2,1)S(1)}, u32[]{:S(2)}, u32[]{:S(2)}) collective-permute-start(bf16[8,8192]{1,0:T(8,128)(2,1)S(1)} %get-tuple-element.43), channel_id=1, source_target_pairs={{0,6},{1,7},{2,4},{3,5},{4,2},{5,3},{6,0},{7,1},{8,14},{9,15},{10,... | collective-permute-start | bytes 393224 | tf_op jit(solution)/shard_map/ppermute | solution.py:30
  35.9 1.8 %collective-permute-done.14 = bf16[8,8192]{1,0:T(8,128)(2,1)S(1)} collective-permute-done((bf16[8,8192]{1,0:T(8,128)(2,1)S(1)}, bf16[8,8192]{1,0:T(8,128)(2,1)S(1)}, u32[]{:S(2)}, u32[]{:S(2)}) %collective-permute-start.14) | collective-permute-done | bytes 131104 | tf_op jit(solution)/shard_map/ppermute | solution.py:50
  37.8 1.5 %collective-permute-start.16 = (bf16[8,8192]{1,0:T(8,128)(2,1)S(1)}, bf16[8,8192]{1,0:T(8,128)(2,1)S(1)}, u32[]{:S(2)}, u32[]{:S(2)}) collective-permute-start(bf16[8,8192]{1,0:T(8,128)(2,1)S(1)} %select_convert_fusion), channel_id=1, source_target_pairs={{0,4},{1,3},{2,6},{3,1},{4,0},{5,7},{6,2},{7,5},{8,12},{9,11},{10,... | collective-permute-start | bytes 393224 | tf_op jit(solution)/shard_map/ppermute | solution.py:30
  39.3 1.5 %collective-permute-start.15 = (bf16[8,8192]{1,0:T(8,128)(2,1)S(1)}, bf16[8,8192]{1,0:T(8,128)(2,1)S(1)}, u32[]{:S(2)}, u32[]{:S(2)}) collective-permute-start(bf16[8,8192]{1,0:T(8,128)(2,1)S(1)} %select_convert_fusion), channel_id=1, source_target_pairs={{0,6},{1,7},{2,4},{3,5},{4,2},{5,3},{6,0},{7,1},{8,14},{9,15},{10,... | collective-permute-start | bytes 393224 | tf_op jit(solution)/shard_map/ppermute | solution.py:30
  40.7 0.0 collective-permute-done.19
  40.7 2.8 %collective-permute-start.21 = (bf16[8,8192]{1,0:T(8,128)(2,1)S(1)}, bf16[8,8192]{1,0:T(8,128)(2,1)S(1)}, u32[]{:S(2)}, u32[]{:S(2)}) collective-permute-start(bf16[8,8192]{1,0:T(8,128)(2,1)S(1)} %collective-permute-done.19), channel_id=1, source_target_pairs={{8,0},{9,1},{10,2},{11,3},{12,4},{13,5},{14,6},{15,7},{16,8},{17,9... | collective-permute-start | bytes 393224 | tf_op jit(solution)/shard_map/ppermute | solution.py:55
  43.5 0.0 collective-permute-done.18
  43.5 0.0 collective-permute-done.17
  43.6 0.1 collective-permute-start.20
  43.7 2.3 %collective-permute-done.21 = bf16[8,8192]{1,0:T(8,128)(2,1)S(1)} collective-permute-done((bf16[8,8192]{1,0:T(8,128)(2,1)S(1)}, bf16[8,8192]{1,0:T(8,128)(2,1)S(1)}, u32[]{:S(2)}, u32[]{:S(2)}) %collective-permute-start.21) | collective-permute-done | bytes 131104 | tf_op jit(solution)/shard_map/ppermute | solution.py:55
  46.1 0.1 collective-permute-start.23
  46.1 0.0 collective-permute-done.16
  46.2 0.0 collective-permute-done.15
  46.2 0.0 collective-permute-done.20
  46.2 0.5 %collective-permute-start.22 = (bf16[24,8192]{1,0:T(8,128)(2,1)S(1)}, bf16[24,8192]{1,0:T(8,128)(2,1)S(1)}, u32[]{:S(2)}, u32[]{:S(2)}) collective-permute-start(bf16[24,8192]{1,0:T(8,128)(2,1)S(1)} %pad_maximum_fusion.2), channel_id=1, source_target_pairs={{0,1},{1,0},{2,3},{3,2},{4,5},{5,4},{6,7},{7,6},{8,9},{9,8},{10,11... | collective-permute-start | bytes 1179656 | tf_op jit(solution)/shard_map/ppermute | solution.py:34
  46.8 1.4 %grad_own.1 = (f32[64,256]{1,0:T(8,128)S(1)}, f32[8,128]{1,0:T(8,128)}) custom-call(bf16[64,8192]{1,0:T(8,128)(2,1)S(1)} %constant_dynamic-update-slice_fusion.8.rows_ref, bf16[256,8192]{1,0:T(8,128)(2,1)S(1)} %get-tuple-element.29.dec_ref), custom_call_target="tpu_custom_call" | custom-call | flops 268435456 | bytes 4194304 | tf_op jit(solution)/shard_map/grad_own/pallas_call | solution.py:216
  48.2 0.0 collective-permute-done.23
  48.2 0.0 collective-permute-done.22
  48.2 0.1 pad_maximum_fusion.rows_ref
  48.3 1.9 %grad_all.1 = f32[1,64,256]{2,1,0:T(8,128)} custom-call(bf16[64,8192]{1,0:T(8,128)(2,1)S(1)} %pad_maximum_fusion.rows_ref, bf16[256,8192]{1,0:T(8,128)(2,1)S(1)} %get-tuple-element.33.dec_ref, f32[64,256]{1,0:T(8,128)S(1)} %get-tuple-element.41.own_ref), custom_call_target="tpu_custom_call" | custom-call | flops 268435456 | bytes 4194304 | tf_op jit(solution)/shard_map/grad_all/pallas_call | solution.py:228
  (31 shorter events, 0.5 us)
Async XLA Ops:
  0.6 9.4 %copy-start = (s32[1,2,2]{2,1,0:T(2,128)S(1)}, s32[1,2,2]{2,1,0:T(2,128)}, u32[]{:S(2)}) copy-start(s32[1,2,2]{2,1,0:T(2,128)} %param.9) | copy-start | bytes 52
  0.6 9.4 %copy-start.1 = (bf16[1,256]{1,0:T(2,128)(2,1)S(1)}, bf16[1,256]{1,0:T(2,128)(2,1)}, u32[]{:S(2)}) copy-start(bf16[1,256]{1,0:T(2,128)(2,1)} %bias_ref) | copy-start | bytes 1540
  0.7 10.8 %copy-start.4 = (bf16[1,8,8192]{2,1,0:T(8,128)(2,1)S(1)}, bf16[1,8,8192]{2,1,0:T(8,128)(2,1)}, u32[]{:S(2)}) copy-start(bf16[1,8,8192]{2,1,0:T(8,128)(2,1)} %param.6) | copy-start | bytes 393220
  0.7 9.5 %collective-permute-start = (bf16[8,8192]{1,0:T(8,128)(2,1)}, bf16[8,8192]{1,0:T(8,128)(2,1)S(1)}, u32[]{:S(2)}, u32[]{:S(2)}) collective-permute-start(bf16[8,8192]{1,0:T(8,128)(2,1)} %bitcast.15), channel_id=1, source_target_pairs={{0,6},{1,7},{2,4},{3,5},{4,2},{5,3},{6,0},{7,1},{8,14},{9,15},{10,... | collective-permute-start | bytes 393224 | tf_op jit(solution)/shard_map/ppermute | solution.py:30
  4.6 6.9 %collective-permute-start.3 = (bf16[8,8192]{1,0:T(8,128)(2,1)}, bf16[8,8192]{1,0:T(8,128)(2,1)S(1)}, u32[]{:S(2)}, u32[]{:S(2)}) collective-permute-start(bf16[8,8192]{1,0:T(8,128)(2,1)} %bitcast.16), channel_id=1, source_target_pairs={{0,1},{1,0},{2,3},{3,2},{4,5},{5,4},{6,7},{7,6},{8,9},{9,8},{10,11... | collective-permute-start | bytes 393224 | tf_op jit(solution)/shard_map/ppermute | solution.py:34
  4.6 6.8 %collective-permute-start.2 = (bf16[8,8192]{1,0:T(8,128)(2,1)}, bf16[8,8192]{1,0:T(8,128)(2,1)S(1)}, u32[]{:S(2)}, u32[]{:S(2)}) collective-permute-start(bf16[8,8192]{1,0:T(8,128)(2,1)} %bitcast.17), channel_id=1, source_target_pairs={{0,2},{1,5},{2,0},{3,7},{4,6},{5,1},{6,4},{7,3},{8,10},{9,13},{10,... | collective-permute-start | bytes 393224 | tf_op jit(solution)/shard_map/ppermute | solution.py:30
  5.2 6.0 %collective-permute-start.1 = (bf16[8,8192]{1,0:T(8,128)(2,1)}, bf16[8,8192]{1,0:T(8,128)(2,1)S(1)}, u32[]{:S(2)}, u32[]{:S(2)}) collective-permute-start(bf16[8,8192]{1,0:T(8,128)(2,1)} %bitcast.18), channel_id=1, source_target_pairs={{0,4},{1,3},{2,6},{3,1},{4,0},{5,7},{6,2},{7,5},{8,12},{9,11},{10,... | collective-permute-start | bytes 393224 | tf_op jit(solution)/shard_map/ppermute | solution.py:30
  11.4 1.8 %collective-permute-start.4 = (bf16[24,8192]{1,0:T(8,128)(2,1)S(1)}, bf16[24,8192]{1,0:T(8,128)(2,1)S(1)}, u32[]{:S(2)}, u32[]{:S(2)}) collective-permute-start(bf16[24,8192]{1,0:T(8,128)(2,1)S(1)} %constant_dynamic-update-slice_fusion), channel_id=1, source_target_pairs={{0,1},{1,0},{2,3},{3,2},{4,5},{5,4},{6,7},{7,6},{8,9},{9,8},{10,11... | collective-permute-start | bytes 1179656 | tf_op jit(solution)/shard_map/ppermute | solution.py:34
  14.9 2.0 %collective-permute-start.8 = (bf16[32,8192]{1,0:T(8,128)(2,1)S(1)}, bf16[32,8192]{1,0:T(8,128)(2,1)S(1)}, u32[]{:S(2)}, u32[]{:S(2)}) collective-permute-start(bf16[32,8192]{1,0:T(8,128)(2,1)S(1)} %get-tuple-element.35), channel_id=1, source_target_pairs={{0,1},{1,0},{2,3},{3,2},{4,5},{5,4},{6,7},{7,6},{8,9},{9,8},{10,11... | collective-permute-start | bytes 1572872 | tf_op jit(solution)/shard_map/ppermute | solution.py:34
  16.0 5.7 %collective-permute-start.5 = (bf16[32,8192]{1,0:T(8,128)(2,1)S(1)}, bf16[32,8192]{1,0:T(8,128)(2,1)S(1)}, u32[]{:S(2)}, u32[]{:S(2)}) collective-permute-start(bf16[32,8192]{1,0:T(8,128)(2,1)S(1)} %get-tuple-element.31), channel_id=1, source_target_pairs={{0,1},{1,0},{2,3},{3,2},{4,5},{5,4},{6,7},{7,6},{8,9},{9,8},{10,11... | collective-permute-start | bytes 1572872 | tf_op jit(solution)/shard_map/ppermute | solution.py:34
  16.9 13.8 %copy-start.2 = (bf16[1,8,8192]{2,1,0:T(8,128)(2,1)S(1)}, bf16[1,8,8192]{2,1,0:T(8,128)(2,1)}, u32[]{:S(2)}) copy-start(bf16[1,8,8192]{2,1,0:T(8,128)(2,1)} %param.11) | copy-start | bytes 393220
  17.0 7.5 %collective-permute-start.9 = (bf16[8,8192]{1,0:T(8,128)(2,1)S(1)}, bf16[8,8192]{1,0:T(8,128)(2,1)S(1)}, u32[]{:S(2)}, u32[]{:S(2)}) collective-permute-start(bf16[8,8192]{1,0:T(8,128)(2,1)S(1)} %get-tuple-element.50), channel_id=1, source_target_pairs={{0,8},{1,9},{2,10},{3,11},{4,12},{5,13},{6,14},{7,15},{8,16},{9,17... | collective-permute-start | bytes 393224 | tf_op jit(solution)/shard_map/ppermute | solution.py:39
  18.7 8.3 %collective-permute-start.12 = (bf16[8,8192]{1,0:T(8,128)(2,1)S(1)}, bf16[8,8192]{1,0:T(8,128)(2,1)S(1)}, u32[]{:S(2)}, u32[]{:S(2)}) collective-permute-start(bf16[8,8192]{1,0:T(8,128)(2,1)S(1)} %get-tuple-element.51), channel_id=1, source_target_pairs={{0,4},{1,3},{2,6},{3,1},{4,0},{5,7},{6,2},{7,5},{8,12},{9,11},{10,... | collective-permute-start | bytes 393224 | tf_op jit(solution)/shard_map/ppermute | solution.py:30
  20.2 6.9 %collective-permute-start.11 = (bf16[8,8192]{1,0:T(8,128)(2,1)S(1)}, bf16[8,8192]{1,0:T(8,128)(2,1)S(1)}, u32[]{:S(2)}, u32[]{:S(2)}) collective-permute-start(bf16[8,8192]{1,0:T(8,128)(2,1)S(1)} %get-tuple-element.52), channel_id=1, source_target_pairs={{0,2},{1,5},{2,0},{3,7},{4,6},{5,1},{6,4},{7,3},{8,10},{9,13},{10,... | collective-permute-start | bytes 393224 | tf_op jit(solution)/shard_map/ppermute | solution.py:30
  21.8 8.0 %collective-permute-start.6 = (bf16[8,8192]{1,0:T(8,128)(2,1)S(1)}, bf16[8,8192]{1,0:T(8,128)(2,1)S(1)}, u32[]{:S(2)}, u32[]{:S(2)}) collective-permute-start(bf16[8,8192]{1,0:T(8,128)(2,1)S(1)} %get-tuple-element.48), channel_id=1, source_target_pairs={{0,2},{1,5},{2,0},{3,7},{4,6},{5,1},{6,4},{7,3},{8,10},{9,13},{10,... | collective-permute-start | bytes 393224 | tf_op jit(solution)/shard_map/ppermute | solution.py:30
  22.4 7.4 %collective-permute-start.7 = (bf16[8,8192]{1,0:T(8,128)(2,1)S(1)}, bf16[8,8192]{1,0:T(8,128)(2,1)S(1)}, u32[]{:S(2)}, u32[]{:S(2)}) collective-permute-start(bf16[8,8192]{1,0:T(8,128)(2,1)S(1)} %get-tuple-element.49), channel_id=1, source_target_pairs={{0,4},{1,3},{2,6},{3,1},{4,0},{5,7},{6,2},{7,5},{8,12},{9,11},{10,... | collective-permute-start | bytes 393224 | tf_op jit(solution)/shard_map/ppermute | solution.py:30
  24.5 6.2 %collective-permute-start.10 = (bf16[8,8192]{1,0:T(8,128)(2,1)S(1)}, bf16[8,8192]{1,0:T(8,128)(2,1)S(1)}, u32[]{:S(2)}, u32[]{:S(2)}) collective-permute-start(bf16[8,8192]{1,0:T(8,128)(2,1)S(1)} %slice_add_fusion.1), channel_id=1, source_target_pairs={{0,6},{1,7},{2,4},{3,5},{4,2},{5,3},{6,0},{7,1},{8,14},{9,15},{10,... | collective-permute-start | bytes 393224 | tf_op jit(solution)/shard_map/ppermute | solution.py:30
  27.1 5.2 %collective-permute-start.13 = (bf16[8,8192]{1,0:T(8,128)(2,1)S(1)}, bf16[8,8192]{1,0:T(8,128)(2,1)S(1)}, u32[]{:S(2)}, u32[]{:S(2)}) collective-permute-start(bf16[8,8192]{1,0:T(8,128)(2,1)S(1)} %convert_element_type.71), channel_id=1, source_target_pairs={{0,8},{1,9},{2,10},{3,11},{4,12},{5,13},{6,14},{7,15},{8,16},{9,17... | collective-permute-start | bytes 393224 | tf_op jit(solution)/shard_map/ppermute | solution.py:45
  30.8 6.9 %collective-permute-start.14 = (bf16[8,8192]{1,0:T(8,128)(2,1)S(1)}, bf16[8,8192]{1,0:T(8,128)(2,1)S(1)}, u32[]{:S(2)}, u32[]{:S(2)}) collective-permute-start(bf16[8,8192]{1,0:T(8,128)(2,1)S(1)} %fusion.7), channel_id=1, source_target_pairs={{8,0},{9,1},{10,2},{11,3},{12,4},{13,5},{14,6},{15,7},{16,8},{17,9... | collective-permute-start | bytes 393224 | tf_op jit(solution)/shard_map/ppermute | solution.py:50
  32.4 15.8 %copy-start.3 = (bf16[8,8192]{1,0:T(8,128)(2,1)}, bf16[8,8192]{1,0:T(8,128)(2,1)S(1)}, u32[]{:S(2)}) copy-start(bf16[8,8192]{1,0:T(8,128)(2,1)S(1)} %get-tuple-element.43) | copy-start | bytes 393220
  32.4 8.3 %collective-permute-start.19 = (bf16[8,8192]{1,0:T(8,128)(2,1)S(1)}, bf16[8,8192]{1,0:T(8,128)(2,1)S(1)}, u32[]{:S(2)}, u32[]{:S(2)}) collective-permute-start(bf16[8,8192]{1,0:T(8,128)(2,1)S(1)} %get-tuple-element.43), channel_id=1, source_target_pairs={{0,2},{1,5},{2,0},{3,7},{4,6},{5,1},{6,4},{7,3},{8,10},{9,13},{10,... | collective-permute-start | bytes 393224 | tf_op jit(solution)/shard_map/ppermute | solution.py:30
  33.8 9.7 %collective-permute-start.18 = (bf16[8,8192]{1,0:T(8,128)(2,1)S(1)}, bf16[8,8192]{1,0:T(8,128)(2,1)S(1)}, u32[]{:S(2)}, u32[]{:S(2)}) collective-permute-start(bf16[8,8192]{1,0:T(8,128)(2,1)S(1)} %get-tuple-element.43), channel_id=1, source_target_pairs={{0,4},{1,3},{2,6},{3,1},{4,0},{5,7},{6,2},{7,5},{8,12},{9,11},{10,... | collective-permute-start | bytes 393224 | tf_op jit(solution)/shard_map/ppermute | solution.py:30
  35.0 8.5 %collective-permute-start.17 = (bf16[8,8192]{1,0:T(8,128)(2,1)S(1)}, bf16[8,8192]{1,0:T(8,128)(2,1)S(1)}, u32[]{:S(2)}, u32[]{:S(2)}) collective-permute-start(bf16[8,8192]{1,0:T(8,128)(2,1)S(1)} %get-tuple-element.43), channel_id=1, source_target_pairs={{0,6},{1,7},{2,4},{3,5},{4,2},{5,3},{6,0},{7,1},{8,14},{9,15},{10,... | collective-permute-start | bytes 393224 | tf_op jit(solution)/shard_map/ppermute | solution.py:30
  37.8 8.4 %collective-permute-start.16 = (bf16[8,8192]{1,0:T(8,128)(2,1)S(1)}, bf16[8,8192]{1,0:T(8,128)(2,1)S(1)}, u32[]{:S(2)}, u32[]{:S(2)}) collective-permute-start(bf16[8,8192]{1,0:T(8,128)(2,1)S(1)} %select_convert_fusion), channel_id=1, source_target_pairs={{0,4},{1,3},{2,6},{3,1},{4,0},{5,7},{6,2},{7,5},{8,12},{9,11},{10,... | collective-permute-start | bytes 393224 | tf_op jit(solution)/shard_map/ppermute | solution.py:30
  39.3 6.9 %collective-permute-start.15 = (bf16[8,8192]{1,0:T(8,128)(2,1)S(1)}, bf16[8,8192]{1,0:T(8,128)(2,1)S(1)}, u32[]{:S(2)}, u32[]{:S(2)}) collective-permute-start(bf16[8,8192]{1,0:T(8,128)(2,1)S(1)} %select_convert_fusion), channel_id=1, source_target_pairs={{0,6},{1,7},{2,4},{3,5},{4,2},{5,3},{6,0},{7,1},{8,14},{9,15},{10,... | collective-permute-start | bytes 393224 | tf_op jit(solution)/shard_map/ppermute | solution.py:30
  40.7 5.3 %collective-permute-start.21 = (bf16[8,8192]{1,0:T(8,128)(2,1)S(1)}, bf16[8,8192]{1,0:T(8,128)(2,1)S(1)}, u32[]{:S(2)}, u32[]{:S(2)}) collective-permute-start(bf16[8,8192]{1,0:T(8,128)(2,1)S(1)} %collective-permute-done.19), channel_id=1, source_target_pairs={{8,0},{9,1},{10,2},{11,3},{12,4},{13,5},{14,6},{15,7},{16,8},{17,9... | collective-permute-start | bytes 393224 | tf_op jit(solution)/shard_map/ppermute | solution.py:55
  43.6 2.6 %collective-permute-start.20 = (bf16[32,8192]{1,0:T(8,128)(2,1)S(1)}, bf16[32,8192]{1,0:T(8,128)(2,1)S(1)}, u32[]{:S(2)}, u32[]{:S(2)}) collective-permute-start(bf16[32,8192]{1,0:T(8,128)(2,1)S(1)} %pad_maximum_fusion.1), channel_id=1, source_target_pairs={{0,1},{1,0},{2,3},{3,2},{4,5},{5,4},{6,7},{7,6},{8,9},{9,8},{10,11... | collective-permute-start | bytes 1572872 | tf_op jit(solution)/shard_map/ppermute | solution.py:34
  46.1 2.1 %collective-permute-start.23 = (bf16[8,8192]{1,0:T(8,128)(2,1)S(1)}, bf16[8,8192]{1,0:T(8,128)(2,1)S(1)}, u32[]{:S(2)}, u32[]{:S(2)}) collective-permute-start(bf16[8,8192]{1,0:T(8,128)(2,1)S(1)} %broadcast_select_fusion), channel_id=1, source_target_pairs={{0,1},{1,0},{2,3},{3,2},{4,5},{5,4},{6,7},{7,6},{8,9},{9,8},{10,11... | collective-permute-start | bytes 393224 | tf_op jit(solution)/shard_map/ppermute | solution.py:34
  46.2 2.0 %collective-permute-start.22 = (bf16[24,8192]{1,0:T(8,128)(2,1)S(1)}, bf16[24,8192]{1,0:T(8,128)(2,1)S(1)}, u32[]{:S(2)}, u32[]{:S(2)}) collective-permute-start(bf16[24,8192]{1,0:T(8,128)(2,1)S(1)} %pad_maximum_fusion.2), channel_id=1, source_target_pairs={{0,1},{1,0},{2,3},{3,2},{4,5},{5,4},{6,7},{7,6},{8,9},{9,8},{10,11... | collective-permute-start | bytes 1179656 | tf_op jit(solution)/shard_map/ppermute | solution.py:34
